TPU v7x, 32 devices: a whole 2x2x4 slice. The times are simulated.
32 devices in a mesh: space: 16 (over z, y, x), dp: 2 (over core).
Axes of the slice: x: 2, y: 2, z: 4, core: 2. Of those that a mesh axis runs over, the one named last changes fastest.
Arguments:
- coarse_latents: bfloat16 [2, 1024, 512], P('dp', 'space'), may hold values from -6 to 6
- active_blocks: int32 [2, 32], P('dp'), may hold values from 0 to 1023, as said below
- face_links: int32 [2, 32, 6], P('dp', 'space'), may hold values from -1 to 31, as said below
- cotangent: bfloat16 [2, 32, 8, 8, 256], P('dp', 'space'), may hold values from -6 to 6
- up_weight: bfloat16 [64, 2048], replicated, may hold values from -0.75 to 0.75
- conv_one: bfloat16 [27, 32, 32], replicated, may hold values from -0.21875 to 0.21875
- conv_two: bfloat16 [27, 32, 32], replicated, may hold values from -0.21875 to 0.21875
Outputs:
- fine: bfloat16 [2, 32, 8, 8, 256], P('dp', 'space')
- grad_one: float32 [27, 32, 32], replicated
- grad_two: float32 [27, 32, 32], replicated
Inputs may be any that keep to these rules, and one draw needn't show every extreme that they name: `active_blocks`: call the bricks at positions i * 2 to (i + 1) * 2 - 1 group i and the block rows i * 64 to (i + 1) * 64 - 1 range i. At most 2 bricks of one group take their blocks from one range, and in every scene every group has exactly 2 from some range. `face_links`: links are mutual: if brick h is the neighbour of g across face f, g is the neighbour of h across the opposite face. A neighbour of brick g lies at a position whose quotient by 2 differs from that of g by at most one; across a -x, -y or -z face that quotient is never larger than that of g, across a +x, +y or +z face never smaller.
All inputs are finite; a program needn't handle non-finite values.
Results may differ from a plain program's by a relative error of at most 0.0057.
Values may be sent and summed in bfloat16 or wider, within the bound.
No kernel may reach another device: no remote copies, remote signals or barrier semaphores. Data moves between devices by JAX's collectives and lax.ppermute only.
A program may use at most 128 MiB of HBM per device.

v0:
```python
import math

import jax
import jax.numpy as jnp
from jax import lax
from jax.sharding import PartitionSpec as P


def passed_along(value, axis, steps):
    count = lax.axis_size(axis)
    first, last = (max(0, -steps), min(count, count - steps))
    return lax.ppermute(value, axis, [(source, source + steps) for source in range(first, last)])


def depth_select(extent):
    inputs_z = jnp.arange(extent + 2)[None, :, None]
    outputs_z = jnp.arange(extent)[None, None, :]
    offsets_z = jnp.arange(3)[:, None, None]
    return (inputs_z == outputs_z + offsets_z).astype(jnp.float32)


def band_matrix(weights, extent):
    channels = weights.shape[1]
    cube = weights.astype(jnp.float32).reshape(3, 3, 3, channels, channels)
    banded = jnp.einsum(
        "dpq,abdio->abpiqo", depth_select(extent), cube, precision=lax.Precision.HIGHEST
    )
    return banded.reshape(3, 3, (extent + 2) * channels, extent * channels).astype(jnp.bfloat16)


def apply_band(padded, banded, extent):
    total = None
    for shift_x in range(3):
        for shift_y in range(3):
            window = padded[:, shift_x : shift_x + extent, shift_y : shift_y + extent, :]
            term = jnp.einsum(
                "nxyp,pq->nxyq",
                window,
                banded[shift_x, shift_y],
                preferred_element_type=jnp.float32,
            )
            total = term if total is None else total + term
    return total


def band_gradient(padded, gradient, extent, channels):
    select = depth_select(extent)
    pieces = []
    for shift_x in range(3):
        for shift_y in range(3):
            window = padded[:, shift_x : shift_x + extent, shift_y : shift_y + extent, :]
            outer = jnp.einsum(
                "nxyp,nxyq->pq", window, gradient, preferred_element_type=jnp.float32
            )
            outer = outer.reshape(extent + 2, channels, extent, channels)
            pieces.append(
                jnp.einsum("dpq,piqo->dio", select, outer, precision=lax.Precision.HIGHEST)
            )
    return jnp.stack(pieces).reshape(27, channels, channels)


def lift_bricks(latent_rows, up_weight, extent, channels):
    bricks_here = latent_rows.shape[0]
    blocks = latent_rows.reshape(bricks_here, 8, -1)
    cells = jnp.einsum("nci,io->nco", blocks, up_weight, preferred_element_type=jnp.float32)
    half = extent // 2
    shaped = cells.reshape(bricks_here, 2, 2, 2, half, half, half, channels)
    shaped = shaped.transpose(0, 1, 4, 2, 5, 3, 6, 7)
    return shaped.reshape(bricks_here, extent, extent, extent * channels).astype(jnp.bfloat16)


def face_planes(volume, channels):
    bricks_here, extent = (volume.shape[0], volume.shape[1])
    planes = [
        volume[:, 0],
        volume[:, extent - 1],
        volume[:, :, 0],
        volume[:, :, extent - 1],
        volume[:, :, :, 0:channels],
        volume[:, :, :, (extent - 1) * channels :],
    ]
    return jnp.stack([one_plane.reshape(bricks_here, -1) for one_plane in planes], axis=1)


def share_faces(stacked):
    from_left = passed_along(stacked, "space", 1)
    from_right = passed_along(stacked, "space", -1)
    return jnp.stack([from_left, stacked, from_right], axis=1)


def fill_padding(volume, face_pool, face_links, position, channels):
    bricks_here, extent = (volume.shape[0], volume.shape[1])
    neighbour = jnp.maximum(face_links, 0)
    source = jnp.clip(neighbour // bricks_here - position + 1, 0, 2)
    face_index = jnp.arange(6, dtype=jnp.int32)[None, :]
    row_index = (source * bricks_here + neighbour % bricks_here) * 6 + (face_index ^ 1)
    flattened = face_pool.reshape(3 * bricks_here * 6, -1)
    picked = jnp.take(flattened, row_index.reshape(-1), axis=0).reshape(bricks_here, 6, -1)
    picked = jnp.where((face_links >= 0)[:, :, None], picked, jnp.zeros((), picked.dtype))
    padded = jnp.pad(volume, ((0, 0), (1, 1), (1, 1), (channels, channels)))
    inside_range = slice(1, extent + 1)
    middle_range = slice(channels, (extent + 1) * channels)
    flat_face = (bricks_here, extent, extent * channels)
    depth_face = (bricks_here, extent, extent, channels)
    padded = padded.at[:, 0, inside_range, middle_range].set(picked[:, 0].reshape(flat_face))
    padded = padded.at[:, extent + 1, inside_range, middle_range].set(
        picked[:, 1].reshape(flat_face)
    )
    padded = padded.at[:, inside_range, 0, middle_range].set(picked[:, 2].reshape(flat_face))
    padded = padded.at[:, inside_range, extent + 1, middle_range].set(
        picked[:, 3].reshape(flat_face)
    )
    padded = padded.at[:, inside_range, inside_range, 0:channels].set(
        picked[:, 4].reshape(depth_face)
    )
    padded = padded.at[:, inside_range, inside_range, (extent + 1) * channels :].set(
        picked[:, 5].reshape(depth_face)
    )
    return padded


def body(coarse_latents, active_blocks, face_links, cotangent, up_weight, conv_one, conv_two):
    position = lax.axis_index("space")
    devices = lax.axis_size("space")
    bricks_here = face_links.shape[1]
    extent = cotangent.shape[2]
    channels = conv_one.shape[1]
    blocks_here = coarse_latents.shape[1]
    local_rows = coarse_latents[0]
    listed = active_blocks[0]
    mine = lax.dynamic_slice_in_dim(listed, position * bricks_here, bricks_here)
    owners = mine // blocks_here
    wanted = listed.reshape(devices, bricks_here)
    held = wanted // blocks_here == position
    local_index = jnp.clip(wanted - position * blocks_here, 0, blocks_here - 1)
    packed = jnp.where(
        held[:, :, None], jnp.take(local_rows, local_index, axis=0), jnp.zeros((), local_rows.dtype)
    )
    received = lax.all_to_all(packed, "space", split_axis=0, concat_axis=0, tiled=True)
    latent_rows = received[owners, jnp.arange(bricks_here)]
    lifted = lift_bricks(latent_rows, up_weight, extent, channels)
    links = face_links[0]
    upstream = cotangent[0]
    lifted_pool = share_faces(face_planes(lifted, channels)[None])[0]
    lifted_pad = fill_padding(lifted, lifted_pool, links, position, channels)
    band_one = band_matrix(conv_one, extent)
    band_two = band_matrix(conv_two, extent)
    band_back = band_matrix(jnp.flip(conv_two, axis=0).transpose(0, 2, 1), extent)
    pre = apply_band(lifted_pad, band_one, extent)
    hidden = jax.nn.silu(pre).astype(jnp.bfloat16)
    hidden_pool = share_faces(face_planes(hidden, channels)[None])[0]
    hidden_pad = fill_padding(hidden, hidden_pool, links, position, channels)
    fine = (lifted.astype(jnp.float32) + apply_band(hidden_pad, band_two, extent)).astype(
        jnp.bfloat16
    )
    scale = 1.0 / math.sqrt(lax.axis_size("dp") * devices * bricks_here * extent**3)
    second_local = band_gradient(hidden_pad, upstream, extent, channels) * scale
    upstream_pool = share_faces(face_planes(upstream, channels)[None])[0]
    upstream_pad = fill_padding(upstream, upstream_pool, links, position, channels)
    back = apply_band(upstream_pad, band_back, extent)
    sigmoid = jax.nn.sigmoid(pre)
    grad_pre = (back * sigmoid * (1.0 + pre * (1.0 - sigmoid))).astype(jnp.bfloat16)
    first_local = band_gradient(lifted_pad, grad_pre, extent, channels) * scale
    grad_one, grad_two = lax.psum((first_local, second_local), ("space", "dp"))
    return (fine[None], grad_one, grad_two)


def solution(mesh):
    return jax.shard_map(
        body,
        mesh=mesh,
        in_specs=(
            P("dp", "space", None),
            P("dp", None),
            P("dp", "space", None),
            P("dp", "space", None, None, None),
            P(),
            P(),
            P(),
        ),
        out_specs=(P("dp", "space", None, None, None), P(), P()),
        check_vma=False,
    )
```

profile of v0, /device:TPU:0, one launch (start us, length us, event | category | flops | bytes accessed | tf_op | source)
XLA Modules:
  0.0 412.8 jit_solution(16305808883196725654)
XLA Ops:
  13.7 5.4 %collective-permute-start.4 = (bf16[1,2,6,2048]{3,1,2,0:T(2,128)(2,1)}, bf16[1,2,6,2048]{3,1,2,0:T(2,128)(2,1)}, u32[]{:S(2)}, u32[]{:S(2)}) collective-permute-start(bf16[1,2,6,2048]{3,1,2,0:T(2,128)(2,1)} %bitcast.92), channel_id=1, source_target_pairs={{0,2},{2,4},{4,6},{6,8},{8,10},{10,12},{12,14},{14,16},{16,18},{18... | collective-permute-start | bytes 147464 | tf_op jit(solution)/shard_map/ppermute | solution.py:12
  25.7 8.0 %all-to-all-start = ((bf16[16,2,512]{2,1,0:T(2,128)(2,1)}), bf16[16,2,512]{2,1,0:T(2,128)(2,1)S(1)}, u32[]{:S(2)}, u32[]{:S(2)}) async-start(bf16[16,2,512]{2,1,0:T(2,128)(2,1)} %broadcast_select_fusion.7), calls=%async_computation | async-start | bytes 65536 | tf_op jit(solution)/shard_map/all_to_all | solution.py:139
  35.3 5.6 %convert_bitcast_fusion.2 = bf16[3,3,10,32,8,32]{5,2,3,1,0,4:T(8,128)(2,1)} fusion(bf16[3,3,3,32,32]{4,3,2,1,0:T(8,128)(2,1)S(1)} %bitcast.662, s32[3,8]{0,1:T(8,128)S(1)} %iota_add_fusion), kind=kOutput, calls=%fused_computation.7 | convolution fusion | flops 5161200 | bytes 1529952 | tf_op jit(solution)/shard_map/dpq,abdio->abpiqo/dot_general | solution.py:25
  40.9 5.6 %convert_bitcast_fusion = bf16[3,3,10,32,8,32]{5,2,3,1,0,4:T(8,128)(2,1)} fusion(bf16[3,3,3,32,32]{4,2,3,1,0:T(4,128)(2,1)S(1)} %copy.140, s32[3,8]{0,1:T(8,128)S(1)} %iota_add_fusion), kind=kOutput, calls=%fused_computation.5 | convolution fusion | flops 5161200 | bytes 1529952 | tf_op jit(solution)/shard_map/dpq,abdio->abpiqo/dot_general | solution.py:25
  52.5 4.4 %collective-permute-start = (bf16[1,2,6,2048]{3,1,2,0:T(2,128)(2,1)}, bf16[1,2,6,2048]{3,1,2,0:T(2,128)(2,1)}, u32[]{:S(2)}, u32[]{:S(2)}) collective-permute-start(bf16[1,2,6,2048]{3,1,2,0:T(2,128)(2,1)} %bitcast.10), channel_id=1, source_target_pairs={{0,2},{2,4},{4,6},{6,8},{8,10},{10,12},{12,14},{14,16},{16,18},{18... | collective-permute-start | bytes 147464 | tf_op jit(solution)/shard_map/ppermute | solution.py:12
  58.4 5.9 %convert_bitcast_fusion.1 = bf16[3,3,10,32,8,32]{5,2,3,1,0,4:T(8,128)(2,1)} fusion(bf16[3,3,3,32,32]{4,3,2,1,0:T(8,128)(2,1)S(1)} %bitcast.655, s32[3,8]{0,1:T(8,128)S(1)} %iota_add_fusion), kind=kOutput, calls=%fused_computation.6 | convolution fusion | flops 5161200 | bytes 1529952 | tf_op jit(solution)/shard_map/dpq,abdio->abpiqo/dot_general | solution.py:25
  65.4 6.7 %copy.127 = bf16[3,3,10,32,8,32]{5,4,3,2,1,0:T(8,128)(2,1)} copy(bf16[3,3,10,32,8,32]{5,2,3,1,0,4:T(8,128)(2,1)S(1)} %copy-done.2) | data formatting | bytes 2949120 | tf_op jit(solution)/shard_map/convert_element_type | solution.py:28
  72.2 7.2 %convert_element_type.66 = bf16[3,3,320,256]{3,2,1,0:T(8,128)(2,1)S(1)} reshape(bf16[3,3,10,32,8,32]{5,4,3,2,1,0:T(8,128)(2,1)} %copy.127) | data formatting | bytes 2949120 | tf_op jit(solution)/shard_map/convert_element_type | solution.py:28
  79.7 10.3 %copy.141 = bf16[3,3,10,32,8,32]{5,4,3,2,1,0:T(8,128)(2,1)} copy(bf16[3,3,10,32,8,32]{5,2,3,1,0,4:T(8,128)(2,1)} %convert_bitcast_fusion) | data formatting | bytes 2949120 | tf_op jit(solution)/shard_map/convert_element_type | solution.py:28
  90.0 8.3 %convert_element_type.74 = bf16[3,3,320,256]{3,2,1,0:T(8,128)(2,1)} reshape(bf16[3,3,10,32,8,32]{5,4,3,2,1,0:T(8,128)(2,1)} %copy.141) | data formatting | bytes 2949120 | tf_op jit(solution)/shard_map/convert_element_type | solution.py:28
  98.2 10.4 %copy.134 = bf16[3,3,10,32,8,32]{5,4,3,2,1,0:T(8,128)(2,1)} copy(bf16[3,3,10,32,8,32]{5,2,3,1,0,4:T(8,128)(2,1)} %convert_bitcast_fusion.1) | data formatting | bytes 2949120 | tf_op jit(solution)/shard_map/convert_element_type | solution.py:28
  108.6 7.2 %convert_element_type.70 = bf16[3,3,320,256]{3,2,1,0:T(8,128)(2,1)S(1)} reshape(bf16[3,3,10,32,8,32]{5,4,3,2,1,0:T(8,128)(2,1)} %copy.134) | data formatting | bytes 2949120 | tf_op jit(solution)/shard_map/convert_element_type | solution.py:28
  128.1 3.0 scatter.60
  131.1 2.9 scatter.61
  134.1 4.0 scatter.64
  138.0 4.0 scatter.65
  142.0 2.9 scatter.66
  145.0 5.7 %scatter.69 = bf16[2,10,10,320]{3,2,1,0:T(8,128)(2,1)} dynamic-update-slice(bf16[2,10,10,320]{3,2,1,0:T(8,128)(2,1)} %scatter.66, bf16[2,8,8,32]{3,2,1,0:T(8,128)(2,1)S(1)} %reshape.984, s32[]{:T(128)} %constant.551.clone.1, s32[]{:T(128)} %constant.550.clone.1, s32[]{:T(128)} %constant.550.clone.1, s32[]{:T(128)} %constant.564.clone.1) | dynamic-update-slice | bytes 16388 | tf_op jit(solution)/shard_map/scatter | solution.py:116
  156.4 4.5 %collective-permute-start.2 = (bf16[1,2,6,2048]{3,1,2,0:T(2,128)(2,1)S(1)}, bf16[1,2,6,2048]{3,1,2,0:T(2,128)(2,1)S(1)}, u32[]{:S(2)}, u32[]{:S(2)}) collective-permute-start(bf16[1,2,6,2048]{3,1,2,0:T(2,128)(2,1)S(1)} %bitcast.663), channel_id=1, source_target_pairs={{0,2},{2,4},{4,6},{6,8},{8,10},{10,12},{12,14},{14,16},{16,18},{18... | collective-permute-start | bytes 147464 | tf_op jit(solution)/shard_map/ppermute | solution.py:12
  170.6 2.7 scatter.84
  173.3 2.7 scatter.85
  176.8 5.0 %scatter.89 = bf16[2,10,10,320]{3,2,1,0:T(8,128)(2,1)S(1)} dynamic-update-slice(bf16[2,10,10,320]{3,2,1,0:T(8,128)(2,1)S(1)} %scatter.86, bf16[2,8,8,32]{3,2,1,0:T(8,128)(2,1)S(1)} %reshape.1000, s32[]{:T(128)} %constant.551.clone.1, s32[]{:T(128)} %constant.550.clone.1, s32[]{:T(128)} %constant.550.clone.1, s32[]{:T(128)} %constant.564.clone.1) | dynamic-update-slice | bytes 16388 | tf_op jit(solution)/shard_map/scatter | solution.py:116
  209.3 5.2 %scatter.79 = bf16[2,10,10,320]{3,2,1,0:T(8,128)(2,1)S(1)} dynamic-update-slice(bf16[2,10,10,320]{3,2,1,0:T(8,128)(2,1)S(1)} %scatter.76, bf16[2,8,8,32]{3,2,1,0:T(8,128)(2,1)S(1)} %reshape.992, s32[]{:T(128)} %constant.551.clone.1, s32[]{:T(128)} %constant.550.clone.1, s32[]{:T(128)} %constant.550.clone.1, s32[]{:T(128)} %constant.564.clone.1) | dynamic-update-slice | bytes 16388 | tf_op jit(solution)/shard_map/scatter | solution.py:116
  270.9 131.3 %all-reduce.6.cloned.1.call-done = (f32[27,32,32]{2,1,0:T(8,128)}, f32[27,32,32]{2,1,0:T(8,128)}) async-done(((f32[27,32,32]{2,1,0:T(8,128)}, f32[27,32,32]{2,1,0:T(8,128)}), (f32[27,32,32]{2,1,0:T(8,128)}, f32[27,32,32]{2,1,0:T(8,128)})) %all-reduce.6.cloned.1.call-update) | async-done | bytes 221200 | tf_op jit(solution)/shard_map/psum | solution.py:164
  (277 shorter events, 138.4 us)
Async XLA Ops:
  7.2 17.0 %copy-start = (bf16[1,64,512]{2,1,0:T(8,128)(2,1)S(1)}, bf16[1,64,512]{2,1,0:T(8,128)(2,1)}, u32[]{:S(2)}) copy-start(bf16[1,64,512]{2,1,0:T(8,128)(2,1)} %param.45) | copy-start | bytes 196612
  7.2 27.9 %copy-start.7 = (bf16[27,32,32]{2,1,0:T(8,128)(2,1)S(1)}, bf16[27,32,32]{2,1,0:T(8,128)(2,1)}, u32[]{:S(2)}) copy-start(bf16[27,32,32]{2,1,0:T(8,128)(2,1)} %param.51) | copy-start | bytes 165892
  7.2 28.1 %copy-start.9 = (bf16[27,32,32]{2,1,0:T(8,128)(2,1)S(1)}, bf16[27,32,32]{2,1,0:T(8,128)(2,1)}, u32[]{:S(2)}) copy-start(bf16[27,32,32]{2,1,0:T(8,128)(2,1)} %param.50) | copy-start | bytes 165892
  13.7 149.0 %collective-permute-start.4 = (bf16[1,2,6,2048]{3,1,2,0:T(2,128)(2,1)}, bf16[1,2,6,2048]{3,1,2,0:T(2,128)(2,1)}, u32[]{:S(2)}, u32[]{:S(2)}) collective-permute-start(bf16[1,2,6,2048]{3,1,2,0:T(2,128)(2,1)} %bitcast.92), channel_id=1, source_target_pairs={{0,2},{2,4},{4,6},{6,8},{8,10},{10,12},{12,14},{14,16},{16,18},{18... | collective-permute-start | bytes 147464 | tf_op jit(solution)/shard_map/ppermute | solution.py:12
  19.1 143.6 %collective-permute-start.5 = (bf16[1,2,6,2048]{3,1,2,0:T(2,128)(2,1)}, bf16[1,2,6,2048]{3,1,2,0:T(2,128)(2,1)}, u32[]{:S(2)}, u32[]{:S(2)}) collective-permute-start(bf16[1,2,6,2048]{3,1,2,0:T(2,128)(2,1)} %bitcast.92), channel_id=1, source_target_pairs={{2,0},{4,2},{6,4},{8,6},{10,8},{12,10},{14,12},{16,14},{18,16},{20... | collective-permute-start | bytes 147464 | tf_op jit(solution)/shard_map/ppermute | solution.py:12
  21.8 102.0 %copy-start.16 = (pred[2,6]{1,0:T(4,128)(4,1)}, pred[2,6]{1,0:T(4,128)(4,1)S(1)}, u32[]{:S(2)}) copy-start(pred[2,6]{1,0:T(4,128)(4,1)S(1)} %get-tuple-element.285) | copy-start | bytes 40
  24.2 98.1 %copy-start.14 = (pred[12]{0:T(512)(128)(4,1)}, pred[12]{0:T(512)(128)(4,1)S(1)}, u32[]{:S(2)}) copy-start(pred[12]{0:T(512)(128)(4,1)S(1)} %get-tuple-element.242) | copy-start | bytes 40
  25.7 20.9 %all-to-all-start = ((bf16[16,2,512]{2,1,0:T(2,128)(2,1)}), bf16[16,2,512]{2,1,0:T(2,128)(2,1)S(1)}, u32[]{:S(2)}, u32[]{:S(2)}) async-start(bf16[16,2,512]{2,1,0:T(2,128)(2,1)} %broadcast_select_fusion.7), calls=%async_computation | async-start | bytes 65536 | tf_op jit(solution)/shard_map/all_to_all | solution.py:139
  33.7 368.4 %all-reduce.6.cloned.1.call-start = ((), (), s32[]{:S(2)}) async-start(), calls=%async_computation.1 | async-start | bytes 1769472 | tf_op jit(solution)/shard_map/psum | solution.py:164
  40.9 5.6 %copy-start.18 = (s32[1,32]{1,0:T(1,128)S(1)}, s32[1,32]{1,0:T(1,128)}, u32[]{:S(2)}) copy-start(s32[1,32]{1,0:T(1,128)} %param.46) | copy-start | bytes 388
  48.4 67.4 %copy-start.5 = (bf16[2,8,8,256]{3,2,1,0:T(8,128)(2,1)}, bf16[2,8,8,256]{3,2,1,0:T(8,128)(2,1)S(1)}, u32[]{:S(2)}) copy-start(bf16[2,8,8,256]{3,2,1,0:T(8,128)(2,1)S(1)} %convert_element_type.62) | copy-start | bytes 196612
  52.5 64.1 %collective-permute-start = (bf16[1,2,6,2048]{3,1,2,0:T(2,128)(2,1)}, bf16[1,2,6,2048]{3,1,2,0:T(2,128)(2,1)}, u32[]{:S(2)}, u32[]{:S(2)}) collective-permute-start(bf16[1,2,6,2048]{3,1,2,0:T(2,128)(2,1)} %bitcast.10), channel_id=1, source_target_pairs={{0,2},{2,4},{4,6},{6,8},{8,10},{10,12},{12,14},{14,16},{16,18},{18... | collective-permute-start | bytes 147464 | tf_op jit(solution)/shard_map/ppermute | solution.py:12
  56.9 59.7 %collective-permute-start.1 = (bf16[1,2,6,2048]{3,1,2,0:T(2,128)(2,1)}, bf16[1,2,6,2048]{3,1,2,0:T(2,128)(2,1)}, u32[]{:S(2)}, u32[]{:S(2)}) collective-permute-start(bf16[1,2,6,2048]{3,1,2,0:T(2,128)(2,1)} %bitcast.10), channel_id=1, source_target_pairs={{2,0},{4,2},{6,4},{8,6},{10,8},{12,10},{14,12},{16,14},{18,16},{20... | collective-permute-start | bytes 147464 | tf_op jit(solution)/shard_map/ppermute | solution.py:12
  58.4 7.1 %copy-start.2 = (bf16[3,3,10,32,8,32]{5,2,3,1,0,4:T(8,128)(2,1)S(1)}, bf16[3,3,10,32,8,32]{5,2,3,1,0,4:T(8,128)(2,1)}, u32[]{:S(2)}) copy-start(bf16[3,3,10,32,8,32]{5,2,3,1,0,4:T(8,128)(2,1)} %convert_bitcast_fusion.2) | copy-start | bytes 4423684
  72.2 7.2 %copy-start.8 = (bf16[1,2,8,8,256]{4,3,2,1,0:T(8,128)(2,1)S(1)}, bf16[1,2,8,8,256]{4,3,2,1,0:T(8,128)(2,1)}, u32[]{:S(2)}) copy-start(bf16[1,2,8,8,256]{4,3,2,1,0:T(8,128)(2,1)} %param.48) | copy-start | bytes 196612
  150.6 3.4 copy-start.3
  156.4 8.2 %collective-permute-start.2 = (bf16[1,2,6,2048]{3,1,2,0:T(2,128)(2,1)S(1)}, bf16[1,2,6,2048]{3,1,2,0:T(2,128)(2,1)S(1)}, u32[]{:S(2)}, u32[]{:S(2)}) collective-permute-start(bf16[1,2,6,2048]{3,1,2,0:T(2,128)(2,1)S(1)} %bitcast.663), channel_id=1, source_target_pairs={{0,2},{2,4},{4,6},{6,8},{8,10},{10,12},{12,14},{14,16},{16,18},{18... | collective-permute-start | bytes 147464 | tf_op jit(solution)/shard_map/ppermute | solution.py:12
  161.0 6.0 %collective-permute-start.3 = (bf16[1,2,6,2048]{3,1,2,0:T(2,128)(2,1)S(1)}, bf16[1,2,6,2048]{3,1,2,0:T(2,128)(2,1)S(1)}, u32[]{:S(2)}, u32[]{:S(2)}) collective-permute-start(bf16[1,2,6,2048]{3,1,2,0:T(2,128)(2,1)S(1)} %bitcast.664), channel_id=1, source_target_pairs={{2,0},{4,2},{6,4},{8,6},{10,8},{12,10},{14,12},{16,14},{18,16},{20... | collective-permute-start | bytes 147464 | tf_op jit(solution)/shard_map/ppermute | solution.py:12
  163.8 4.1 copy-start.15
  163.9 4.2 %copy-start.17 = (pred[2,6]{1,0:T(4,128)(4,1)S(1)}, pred[2,6]{1,0:T(4,128)(4,1)}, u32[]{:S(2)}) copy-start(pred[2,6]{1,0:T(4,128)(4,1)} %copy-done.16) | copy-start | bytes 40
  184.0 6.7 %copy-start.19 = (f32[2,8,8,256]{3,2,1,0:T(8,128)S(1)}, f32[2,8,8,256]{3,2,1,0:T(8,128)}, u32[]{:S(2)}) copy-start(f32[2,8,8,256]{3,2,1,0:T(8,128)} %get-tuple-element.294) | copy-start | bytes 393220
  187.4 4.5 %copy-start.4 = (bf16[2,10,10,320]{3,2,1,0:T(8,128)(2,1)S(1)}, bf16[2,10,10,320]{3,2,1,0:T(8,128)(2,1)}, u32[]{:S(2)}) copy-start(bf16[2,10,10,320]{3,2,1,0:T(8,128)(2,1)} %scatter.69) | copy-start | bytes 384004
  238.6 1.6 copy-start.12
  270.0 135.8 %copy-start.1 = (bf16[1,64,512]{2,1,0:T(8,128)(2,1)S(1)}, bf16[1,64,512]{2,1,0:T(8,128)(2,1)}, u32[]{:S(2)}) copy-start(bf16[1,64,512]{2,1,0:T(8,128)(2,1)} %param.45) | copy-start | bytes 196612
  (4 other events, 5.6 us)
Sparse Core Ops, SparseCore 0:
  270.1 131.9 all-reduce.5
where the time goes:
time: 420 us; the launch traced here: 413 us
  local copies, waits for them, and re-layouts  149 us (35%)
  waiting for transfers between devices  134 us (32%)
  matrix products  78.4 us (19%)
  starting transfers between devices  26.9 us (6%)
  between operations  15.5 us (4%)
  other arithmetic  9.6 us (2%)
    psum x1, waiting for transfers between devices, body(): grad_one, grad_two = lax.psum((first_local, second_local), ('space', 'dp'))  131 us
    convert_element_type x6, local copies, waits for them, and re-layouts, band_matrix(): banded.reshape(3, 3, (extent + 2) * channels, extent * channels)  50 us
    dot_general x18, matrix products, band_gradient(): jnp.einsum('dpq,piqo->dio', select, outer, precision=lax.Precision.HIGHEST)  30.9 us
    ppermute x6, starting transfers between devices, passed_along(): lax.ppermute(value, axis, [(source, source + steps) for source in range(f...  18.9 us
    dot_general x27, matrix products, apply_band(): jnp.einsum('nxyp,pq->nxyq', window, banded[shift_x, shift_y], preferred_e...  17.4 us
    dot_general x3, matrix products, band_matrix(): jnp.einsum('dpq,abdio->abpiqo', depth_select(extent), cube, precision=lax...  17.1 us
    scatter x3, local copies, waits for them, and re-layouts, fill_padding(): padded.at[:, inside_range, inside_range, (extent + 1) * channels:]  15.9 us
    unnamed x81, local copies, waits for them, and re-layouts  14 us
  transfers between devices with their start and end apart: 8, of which 2 were waited for; matrix products, arithmetic and copies ran while one was open for 30% of the time, Pallas kernels for 0%

commit v1 on v0

v1 whole, which is shorter than its diff:
```python
import functools
import math

import jax
import jax.numpy as jnp
from jax import lax
from jax.experimental import pallas as pl
from jax.experimental.pallas import tpu as pltpu
from jax.sharding import PartitionSpec as P

BF16 = jnp.bfloat16
F32 = jnp.float32
EDGE = 8
CHANNELS = 32
LINE = EDGE * CHANNELS
WIDE = LINE + 128
BRICKS = 2
CUBE = EDGE * EDGE
LINES = BRICKS * CUBE
FACE = 3 * EDGE
BLOCKS = 54


def dot(left, right):
    return jnp.dot(left, right, preferred_element_type=F32)


def dot_rows(left, right):
    return lax.dot_general(left, right, (((0,), (0,)), ((), ())), preferred_element_type=F32)


def lines(halves_ref, start, count, stride=1):
    index = pl.ds(start, count, stride=stride) if stride > 1 else pl.ds(start, count)
    return jnp.concatenate([halves_ref[0, index, :], halves_ref[1, index, :]], axis=-1)


def lanes_of(shape):
    return lax.broadcasted_iota(jnp.int32, shape, len(shape) - 1)


def pick_kernel(devices, ids_ref, latents_ref, out_ref, rows_ref):
    held = latents_ref.shape[1]
    bricks = ids_ref.shape[1]
    first = lax.axis_index("space") * held
    rows = lax.broadcasted_iota(jnp.int32, (held, bricks), 0) + first
    hot = jnp.where(rows == ids_ref[...], 1.0, 0.0).astype(BF16)
    rows_ref[0:8] = jnp.zeros((8, rows_ref.shape[1]), F32)
    rows_ref[8 : 8 + bricks] = dot_rows(hot, latents_ref[0])
    rows_ref[8 + bricks : 16 + bricks] = jnp.zeros((8, rows_ref.shape[1]), F32)
    for receiver in range(devices):
        start = 8 + BRICKS * (receiver - 1)
        out_ref[receiver] = rows_ref[start : start + 8].astype(BF16)


def build_band(band_ref, rows):
    shape = (3 * CHANNELS, LINE)
    row = lax.broadcasted_iota(jnp.int32, shape, 0)
    target = CHANNELS - (row // CHANNELS) * CHANNELS + row % CHANNELS
    distance = lanes_of(shape) - target
    band_ref[:, LINE:, :] = jnp.zeros((9, 128, LINE), BF16)
    places = [(z, z * CHANNELS) for z in range(EDGE)] + [(EDGE, LINE), (-1, WIDE - CHANNELS)]
    for z, start in places:
        select = jnp.where(distance == z * CHANNELS, 1.0, 0.0).astype(BF16)
        block = dot(rows, select).astype(BF16)
        band_ref[:, start : start + CHANNELS, :] = block.reshape(9, CHANNELS, LINE)


def weight_rows(weights):
    cube = weights.reshape(9, 3, CHANNELS, CHANNELS)
    rows = jnp.concatenate([cube[:, 0], cube[:, 1], cube[:, 2]], axis=-1)
    return rows.reshape(9 * CHANNELS, 3 * CHANNELS).astype(BF16)


def flipped_rows(weights):
    cube = jnp.swapaxes(weights, 1, 2).reshape(9, 3, CHANNELS, CHANNELS)
    pieces = [jnp.concatenate([cube[8 - k, 2], cube[8 - k, 1], cube[8 - k, 0]], axis=-1) for k in range(9)]
    return jnp.concatenate(pieces, axis=0).astype(BF16)


def put_padded(pad_ref, brick, volume, x_low, x_high, y_low, y_high, z_low, z_high):
    lane = lanes_of((EDGE, EDGE, 128))
    tail = jnp.where(lane < CHANNELS, z_high, jnp.where(lane >= 128 - CHANNELS, z_low, 0.0))
    full = jnp.concatenate([volume, tail], axis=-1)
    zeros = jnp.zeros((EDGE, 128), F32)
    first = jnp.concatenate([x_low, zeros], axis=-1)[None]
    last = jnp.concatenate([x_high, zeros], axis=-1)[None]
    slabs = jnp.concatenate([first, full, last], axis=0)
    no_halo = jnp.zeros((1, WIDE), F32)
    low = jnp.concatenate([no_halo, jnp.concatenate([y_low, zeros], axis=-1), no_halo], axis=0)
    high = jnp.concatenate([no_halo, jnp.concatenate([y_high, zeros], axis=-1), no_halo], axis=0)
    row = lax.broadcasted_iota(jnp.int32, slabs.shape, 1)
    pad_ref[0, brick] = jnp.where(row == 0, low[:, None, :], pltpu.roll(slabs, 1, 1))
    pad_ref[1, brick] = slabs
    pad_ref[2, brick] = jnp.where(row == EDGE - 1, high[:, None, :], pltpu.roll(slabs, EDGE - 1, 1))


def window(pad_ref, k):
    lines = pad_ref[k % 3, :, k // 3 : k // 3 + EDGE]
    return lines.reshape(LINES, WIDE).astype(BF16)


def convolve(pad_ref, band_ref):
    total = None
    for k in range(9):
        term = dot(window(pad_ref, k), band_ref[k])
        total = term if total is None else total + term
    return total


def pack_faces(faces_ref, base, halves_ref, start, high):
    first = start + ((EDGE - 1) * EDGE if high else 0)
    faces_ref[base : base + EDGE] = lines(halves_ref, first, EDGE)
    first = start + (EDGE - 1 if high else 0)
    faces_ref[base + EDGE : base + 2 * EDGE] = lines(halves_ref, first, EDGE, EDGE)
    tile = halves_ref[1 if high else 0, start : start + CUBE, :]
    lane = lanes_of((16, 128)) // CHANNELS
    packed = jnp.zeros((16, 128), F32)
    for part in range(4):
        shift = (part + 1 if high else part) % 4 * CHANNELS
        piece = tile[part * 16 : part * 16 + 16]
        packed = jnp.where(lane == part, pltpu.roll(piece, shift, 1) if shift else piece, packed)
    faces_ref[base + 2 * EDGE : base + FACE, :128] = packed[:8]
    faces_ref[base + 2 * EDGE : base + FACE, 128:] = packed[8:]


def unpack_depth(rows, high):
    packed = jnp.concatenate([rows[:, :128], rows[:, 128:]], axis=0)
    pieces = []
    for part in range(4):
        shift = ((3 - part) if high else (4 - part)) % 4 * CHANNELS
        pieces.append(pltpu.roll(packed, shift, 1) if shift else packed)
    return jnp.concatenate(pieces, axis=0).reshape(EDGE, EDGE, 128)


def first_kernel(
    links_ref, received_ref, up_ref, one_ref, cotangent_ref,
    lifted_out, pre_out, hidden_out, pad_out, high_out, low_out,
    volumes_ref, pad_ref, band_ref, lines_ref, high_ref, low_ref,
):
    position = lax.axis_index("space")
    latents = jnp.sum(received_ref[...].astype(F32), axis=0)
    cells = [latents[:, cell * 64 : cell * 64 + 64] for cell in range(8)]
    lifted = dot(jnp.concatenate(cells, axis=0).astype(BF16), up_ref[...])
    lifted = lifted.astype(BF16).astype(F32)
    for cell in range(8):
        a, b, c = cell // 4, cell // 2 % 2, cell % 2
        for sub in range(16):
            line = (4 * a + sub // 4) * EDGE + 4 * b + sub % 4
            volumes_ref[c, pl.ds(line, 8, stride=CUBE), :] = lifted[
                cell * 8 : cell * 8 + 8, sub * 128 : sub * 128 + 128
            ]
    for brick in range(BRICKS):

        def near(face):
            link = links_ref[0, brick, face]
            index = jnp.clip(link - BRICKS * (position - 1), 0, 3 * BRICKS - 1)
            return pl.multiple_of(index * CUBE, CUBE), jnp.where(link >= 0, 1.0, 0.0).astype(F32)

        def x_face(face):
            start, present = near(face)
            offset = EDGE * (EDGE - 1) if face % 2 == 0 else 0
            return lines(volumes_ref, pl.multiple_of(start + offset, 8), EDGE) * present

        def y_face(face):
            start, present = near(face)
            offset = EDGE - 1 if face % 2 == 0 else 0
            return lines(volumes_ref, start + offset, EDGE, EDGE) * present

        def z_face(face):
            start, present = near(face)
            tile = volumes_ref[1 if face % 2 == 0 else 0, pl.ds(start, CUBE), :] * present
            return tile.reshape(EDGE, EDGE, 128)

        own = (BRICKS + brick) * CUBE
        volume = lines(volumes_ref, own, CUBE).reshape(EDGE, EDGE, LINE)
        put_padded(
            pad_ref, brick, volume, x_face(0), x_face(1), y_face(2), y_face(3), z_face(4), z_face(5)
        )
    build_band(band_ref, weight_rows(one_ref[...].astype(F32)))
    pre = convolve(pad_ref, band_ref)
    hidden = pre / (1.0 + jnp.exp(-pre))
    hidden = hidden.astype(BF16)
    lifted_out[...] = lines(volumes_ref, BRICKS * CUBE, LINES).astype(BF16)
    pre_out[...] = pre
    hidden_out[...] = hidden
    pad_out[...] = pad_ref[...].reshape(pad_out.shape).astype(BF16)
    sources = (hidden.astype(F32), cotangent_ref[...].astype(F32).reshape(LINES, LINE))
    for which, values in enumerate(sources):
        for half in range(2):
            lines_ref[half, which * LINES : which * LINES + LINES] = values[:, half * 128 : half * 128 + 128]
    for which in range(2):
        for brick in range(BRICKS):
            base = (which * BRICKS + brick) * FACE
            start = which * LINES + brick * CUBE
            pack_faces(high_ref, base, lines_ref, start, True)
            pack_faces(low_ref, base, lines_ref, start, False)
    high_out[...] = high_ref[...].astype(BF16)
    low_out[...] = low_ref[...].astype(BF16)


def fold_diagonals(outer_ref, part):
    lane = lanes_of((CHANNELS, 128)) // CHANNELS
    folded = None
    for half in range(2):
        picked = None
        for block in range(4):
            depth = 4 * half + block + part - 1
            start = depth * CHANNELS if 0 <= depth < EDGE else (LINE if depth == EDGE else WIDE - CHANNELS)
            rows = outer_ref[start : start + CHANNELS, half * 128 : half * 128 + 128]
            picked = rows if picked is None else jnp.where(lane == block, rows, picked)
        folded = picked if folded is None else folded + picked
    quarter = [folded[8 * q : 8 * q + 8] for q in range(4)]
    small = lanes_of((8, 128)) // CHANNELS
    total = None
    for turn in range(4):
        mixed = quarter[0]
        for q in range(1, 4):
            mixed = jnp.where(small == (q + turn) % 4, quarter[q], mixed)
        if turn:
            mixed = pltpu.roll(mixed, 128 - turn * CHANNELS, 1)
        total = mixed if total is None else total + mixed
    return total


def second_kernel(
    links_ref, cotangent_ref, two_ref, lifted_ref, pre_ref, hidden_ref, pad_in,
    high_own, low_own, high_left, low_right,
    fine_out, sums_out,
    high_ref, low_ref, hidden_pad, cotangent_pad, lifted_pad, band_ref, outer_ref,
):
    position = lax.axis_index("space")
    half = 2 * BRICKS * FACE
    high_ref[0:half] = high_left[...].astype(F32)
    high_ref[half:] = high_own[...].astype(F32)
    low_ref[0:half] = low_own[...].astype(F32)
    low_ref[half:] = low_right[...].astype(F32)
    lifted_pad[...] = pad_in[...].astype(F32).reshape(lifted_pad.shape)
    cotangent = cotangent_ref[...].astype(F32).reshape(LINES, LINE)
    hidden = hidden_ref[...].astype(F32)
    for which, values, pad_ref in ((0, hidden, hidden_pad), (1, cotangent, cotangent_pad)):
        for brick in range(BRICKS):

            def rows(face, axis):
                link = links_ref[0, brick, face]
                high = face % 2 == 0
                index = jnp.clip(link - BRICKS * (position - 1 if high else position), 0, 2 * BRICKS - 1)
                start = (index // BRICKS) * half + (which * BRICKS + index % BRICKS) * FACE + axis * EDGE
                pool = high_ref if high else low_ref
                present = jnp.where(link >= 0, 1.0, 0.0).astype(F32)
                return pool[pl.ds(pl.multiple_of(start, 8), EDGE), :] * present

            volume = values[brick * CUBE : brick * CUBE + CUBE].reshape(EDGE, EDGE, LINE)
            put_padded(
                pad_ref, brick, volume, rows(0, 0), rows(1, 0), rows(2, 1), rows(3, 1),
                unpack_depth(rows(4, 2), True), unpack_depth(rows(5, 2), False),
            )
    weights = two_ref[...].astype(F32)
    build_band(band_ref, weight_rows(weights))
    fine = lifted_ref[...].astype(F32) + convolve(hidden_pad, band_ref)
    fine_out[...] = fine.astype(BF16).reshape(fine_out.shape)
    build_band(band_ref, flipped_rows(weights))
    back = convolve(cotangent_pad, band_ref)
    pre = pre_ref[...]
    sigmoid = 1.0 / (1.0 + jnp.exp(-pre))
    gradient = (back * sigmoid * (1.0 + pre * (1.0 - sigmoid))).astype(BF16)
    upstream = cotangent.astype(BF16)
    sums_out[...] = jnp.zeros(sums_out.shape, F32)
    per = sums_out.shape[1] // 8
    for base, pad_ref, right in ((0, lifted_pad, gradient), (27, hidden_pad, upstream)):
        for k in range(9):
            outer_ref[...] = dot_rows(window(pad_ref, k), right)
            for part in range(3):
                index = base + 3 * k + part
                sums_out[index // per, index % per * 8 : index % per * 8 + 8] = fold_diagonals(outer_ref, part)


def sum_kernel(scale, parts_ref, out_ref):
    total = jnp.sum(parts_ref[...], axis=0) * scale
    out_ref[...] = jnp.broadcast_to(total[None], out_ref.shape)


def unpack_kernel(sums_ref, one_out, two_out):
    per = sums_ref.shape[1] // 8
    for index in range(BLOCKS):
        block = sums_ref[index // per, index % per * 8 : index % per * 8 + 8]
        out = one_out if index < 27 else two_out
        for q in range(4):
            moved = pltpu.roll(block, 128 - q * CHANNELS, 1) if q else block
            out[index % 27, 8 * q : 8 * q + 8, :] = moved[:, :CHANNELS]


def call(kernel, out_shape, scratch=(), smem_first=False, inputs=1, limit=24):
    specs = [pl.BlockSpec(memory_space=pltpu.VMEM)] * inputs
    if smem_first:
        specs[0] = pl.BlockSpec(memory_space=pltpu.SMEM)
    out_specs = jax.tree.map(lambda _: pl.BlockSpec(memory_space=pltpu.VMEM), out_shape)
    return pl.pallas_call(
        kernel,
        out_shape=out_shape,
        in_specs=specs,
        out_specs=out_specs,
        scratch_shapes=list(scratch),
        compiler_params=pltpu.CompilerParams(vmem_limit_bytes=limit * 2**20),
    )


def shape(*dims, dtype=BF16):
    return jax.ShapeDtypeStruct(dims, dtype)


def passed_along(value, axis, steps):
    count = lax.axis_size(axis)
    first, last = (max(0, -steps), min(count, count - steps))
    return lax.ppermute(value, axis, [(source, source + steps) for source in range(first, last)])


def body(coarse_latents, active_blocks, face_links, cotangent, up_weight, conv_one, conv_two):
    devices = lax.axis_size("space")
    everyone = devices * lax.axis_size("dp")
    width = coarse_latents.shape[2]
    bricks = active_blocks.shape[1]
    packed = call(
        functools.partial(pick_kernel, devices),
        shape(devices, 8, width),
        [pltpu.VMEM((bricks + 16, width), F32)],
        inputs=2,
    )(active_blocks, coarse_latents)
    received = lax.all_to_all(packed, "space", split_axis=0, concat_axis=0, tiled=True)
    pad_shape = (3, BRICKS, EDGE + 2, EDGE, WIDE)
    pad = pltpu.VMEM(pad_shape, F32)
    band = pltpu.VMEM((9, WIDE, LINE), BF16)
    packed_faces = 2 * BRICKS * FACE
    lifted, pre, hidden, lifted_pad, high, low = call(
        first_kernel,
        (
            shape(LINES, LINE),
            shape(LINES, LINE, dtype=F32),
            shape(LINES, LINE),
            shape(math.prod(pad_shape[:-1]), WIDE),
            shape(packed_faces, LINE),
            shape(packed_faces, LINE),
        ),
        [
            pltpu.VMEM((2, 8 * CUBE, 128), F32),
            pad,
            band,
            pltpu.VMEM((2, 2 * LINES, 128), F32),
            pltpu.VMEM((packed_faces, LINE), F32),
            pltpu.VMEM((packed_faces, LINE), F32),
        ],
        smem_first=True,
        inputs=5,
    )(face_links, received, up_weight, conv_one, cotangent)
    high_left = passed_along(high, "space", 1)
    low_right = passed_along(low, "space", -1)
    per = -(-BLOCKS // everyone)
    per += per % 2
    fine, sums = call(
        second_kernel,
        (shape(*cotangent.shape), shape(everyone, per * 8, 128, dtype=F32)),
        [
            pltpu.VMEM((2 * packed_faces, LINE), F32),
            pltpu.VMEM((2 * packed_faces, LINE), F32),
            pad,
            pad,
            pad,
            band,
            pltpu.VMEM((WIDE, LINE), F32),
        ],
        smem_first=True,
        inputs=11,
    )(face_links, cotangent, conv_two, lifted, pre, hidden, lifted_pad, high, low, high_left, low_right)
    axes = ("space", "dp")
    parts = lax.all_to_all(sums, axes, split_axis=0, concat_axis=0, tiled=True)
    scale = 1.0 / math.sqrt(lax.axis_size("dp") * devices * BRICKS * EDGE**3)
    total = call(functools.partial(sum_kernel, scale), shape(*sums.shape, dtype=F32))(parts)
    gathered = lax.all_to_all(total, axes, split_axis=0, concat_axis=0, tiled=True)
    grads = shape(27, CHANNELS, CHANNELS, dtype=F32)
    grad_one, grad_two = call(unpack_kernel, (grads, grads))(gathered)
    return (fine, grad_one, grad_two)


def solution(mesh):
    return jax.shard_map(
        body,
        mesh=mesh,
        in_specs=(
            P("dp", "space", None),
            P("dp", None),
            P("dp", "space", None),
            P("dp", "space", None, None, None),
            P(),
            P(),
            P(),
        ),
        out_specs=(P("dp", "space", None, None, None), P(), P()),
        check_vma=False,
    )
```

time: 420 us -> 64.5 us (0.15); the launches traced: 413 us -> 64.2 us
  local copies, waits for them, and re-layouts: 149 us -> 2.48 us
  waiting for transfers between devices: 134 us -> 4.68 us
  matrix products: 78.4 us -> 0 us
  blocking collectives: 0 us -> 43.9 us
  starting transfers between devices: 26.9 us -> 4.29 us
  between operations: 15.5 us -> 0.71 us
  other arithmetic: 9.6 us -> 0 us
  Pallas kernels: 0 us -> 8.06 us
    psum x1 -> x0, waiting for transfers between devices: 131 us -> none  [body(): grad_one, grad_two = lax.psum((first_local, second_local), ('space', 'dp'))]
    dot_general x67 -> x0, matrix products: 78.4 us -> none  [the longest x18 30.9 us: band_gradient(): jnp.einsum('dpq,piqo->dio', select, outer, precision=lax.Precision.HIGHEST)]
    convert_element_type x8 -> x0, local copies, waits for them, and re-layouts: 50.3 us -> none  [the longest x6 50 us: band_matrix(): banded.reshape(3, 3, (extent + 2) * channels, extent * channels)]
    scatter x18 -> x0, local copies, waits for them, and re-layouts: 49 us -> none  [the longest x3 15.9 us: fill_padding(): padded.at[:, inside_range, inside_range, (extent + 1) * channels:]]
    all_to_all x0 -> x3, blocking collectives: none -> 43.9 us  [the longest x1 16 us: body(): lax.all_to_all(packed, 'space', split_axis=0, concat_axis=0, tiled=True)]
    ppermute x6 -> x2, starting transfers between devices: 18.9 us -> 4.29 us  [passed_along(): lax.ppermute(value, axis, [(source, source + steps) for source in range(f...]
    reshape x13 -> x0, local copies, waits for them, and re-layouts: 12.5 us -> none  [the longest x9 11.6 us: band_gradient(): outer = outer.reshape(extent + 2, channels, extent, channels)]
    unnamed x81 -> x14, local copies, waits for them, and re-layouts: 14 us -> 2.48 us
  transfers between devices with their start and end apart: 8 -> 2, of which waited for: 2 -> 2; matrix products, arithmetic and copies ran while one was open for 30% -> 0% of each run, Pallas kernels for 0% -> 0%
where the time goes in v1:
time: 64.5 us; the launch traced here: 64.2 us
  blocking collectives  43.9 us (68%)
  Pallas kernels  8.06 us (12%)
  waiting for transfers between devices  4.68 us (7%)
  starting transfers between devices  4.29 us (7%)
  local copies, waits for them, and re-layouts  2.48 us (4%)
  between operations  0.71 us (1%)
    all_to_all x1, blocking collectives, body(): lax.all_to_all(packed, 'space', split_axis=0, concat_axis=0, tiled=True)  16 us
    all_to_all x1, blocking collectives, body(): parts = lax.all_to_all(sums, axes, split_axis=0, concat_axis=0, tiled=True)  15.1 us
    all_to_all x1, blocking collectives, body(): lax.all_to_all(total, axes, split_axis=0, concat_axis=0, tiled=True)  12.8 us
    ppermute x2, waiting for transfers between devices, passed_along(): lax.ppermute(value, axis, [(source, source + steps) for source in range(f...  4.68 us
    ppermute x2, starting transfers between devices, passed_along(): lax.ppermute(value, axis, [(source, source + steps) for source in range(f...  4.29 us
    pallas_call x1, Pallas kernels, body(): call(second_kernel, (shape(*cotangent.shape), shape(everyone, per * 8, 12...  4.04 us
    pallas_call x1, Pallas kernels, body(): call(first_kernel, (shape(LINES, LINE), shape(LINES, LINE, dtype=F32), sh...  2.67 us
    unnamed x14, local copies, waits for them, and re-layouts  2.48 us
  transfers between devices with their start and end apart: 2, of which 2 were waited for; matrix products, arithmetic and copies ran while one was open for 0% of the time, Pallas kernels for 0%

profile of v1, /device:TPU:0, one launch (start us, length us, event | category | flops | bytes accessed | tf_op | source)
XLA Modules:
  0.0 64.2 jit_solution(13259513038442289311)
XLA Ops:
  0.6 0.0 copy-start
  0.6 0.0 copy-start.4
  0.7 0.9 %copy-done.4 = bf16[1,64,512]{2,1,0:T(8,128)(2,1)S(1)} copy-done((bf16[1,64,512]{2,1,0:T(8,128)(2,1)S(1)}, bf16[1,64,512]{2,1,0:T(8,128)(2,1)}, u32[]{:S(2)}) %copy-start.4) | copy-done | bytes 65560
  1.5 0.7 %copy-done.6 = s32[1,32]{1,0:T(1,128)S(1)} copy-done((s32[1,32]{1,0:T(1,128)S(1)}, s32[1,32]{1,0:T(1,128)}, u32[]{:S(2)}) %copy-start.6) | copy-done | bytes 152
  2.2 0.2 shard_map.94
  2.4 0.0 copy-start.1
  2.4 0.0 copy-start.5
  2.4 16.0 %all_to_all.15.received_ref = bf16[16,8,512]{2,1,0:T(8,128)(2,1)S(1)} all-to-all(bf16[16,8,512]{2,1,0:T(8,128)(2,1)S(1)} %shard_map.94), channel_id=1, replica_groups=mesh['space'=16,'dp'=2] {'space'}, dimensions={0} | all-to-all | bytes 262144 | tf_op jit(solution)/shard_map/all_to_all | solution.py:328
  18.5 0.0 copy-done
  18.5 0.0 copy-done.1
  18.5 0.0 copy-done.5
  18.5 0.0 copy-start.3
  18.5 0.9 %copy-done.3 = bf16[27,32,32]{2,1,0:T(8,128)(2,1)S(1)} copy-done((bf16[27,32,32]{2,1,0:T(8,128)(2,1)S(1)}, bf16[27,32,32]{2,1,0:T(8,128)(2,1)}, u32[]{:S(2)}) %copy-start.3) | copy-done | bytes 55320
  19.4 2.7 %shard_map.95 = (bf16[128,256]{1,0:T(8,128)(2,1)S(1)}, f32[128,256]{1,0:T(8,128)S(1)}, bf16[128,256]{1,0:T(8,128)(2,1)S(1)}, bf16[480,384]{1,0:T(8,128)(2,1)S(1)...) custom-call(s32[1,2,6]{2,1,0:T(2,128)S(1)} %copy-done.5, bf16[16,8,512]{2,1,0:T(8,128)(2,1)S(1)} %all_to_all.15.received_ref, ...), custom_call_target="tpu_custom_call" | custom-call | tf_op jit(solution)/shard_map/pallas_call | solution.py:333
  22.1 3.0 %collective-permute-start = (bf16[96,256]{1,0:T(8,128)(2,1)S(1)}, bf16[96,256]{1,0:T(8,128)(2,1)S(1)}, u32[]{:S(2)}, u32[]{:S(2)}) collective-permute-start(bf16[96,256]{1,0:T(8,128)(2,1)S(1)} %get-tuple-element.17.high_own), channel_id=1, source_target_pairs={{0,2},{2,4},{4,6},{6,8},{8,10},{10,12},{12,14},{14,16},{16,18},{18... | collective-permute-start | bytes 147464 | tf_op jit(solution)/shard_map/ppermute | solution.py:314
  25.1 1.3 %collective-permute-start.1 = (bf16[96,256]{1,0:T(8,128)(2,1)S(1)}, bf16[96,256]{1,0:T(8,128)(2,1)S(1)}, u32[]{:S(2)}, u32[]{:S(2)}) collective-permute-start(bf16[96,256]{1,0:T(8,128)(2,1)S(1)} %get-tuple-element.18.low_own), channel_id=1, source_target_pairs={{2,0},{4,2},{6,4},{8,6},{10,8},{12,10},{14,12},{16,14},{18,16},{20... | collective-permute-start | bytes 147464 | tf_op jit(solution)/shard_map/ppermute | solution.py:314
  26.4 0.4 collective-permute-done.high_left
  26.8 4.3 %collective-permute-done.1.low_right = bf16[96,256]{1,0:T(8,128)(2,1)S(1)} collective-permute-done((bf16[96,256]{1,0:T(8,128)(2,1)S(1)}, bf16[96,256]{1,0:T(8,128)(2,1)S(1)}, u32[]{:S(2)}, u32[]{:S(2)}) %collective-permute-start.1) | collective-permute-done | bytes 49184 | tf_op jit(solution)/shard_map/ppermute | solution.py:314
  31.1 0.0 copy-done.2
  31.1 4.0 %shard_map.96 = (bf16[1,2,8,8,256]{4,3,2,1,0:T(8,128)(2,1)}, f32[32,16,128]{2,1,0:T(8,128)S(1)}) custom-call(s32[1,2,6]{2,1,0:T(2,128)S(1)} %copy-done.5, bf16[1,2,8,8,256]{4,3,2,1,0:T(8,128)(2,1)S(1)} %copy-done.1, bf16[27,32,32]{2,1,0:T(8,128)(2,1)S(1)} %copy-done.2, bf16[128,256]{1,0:T(8,128)(2,1)S(1)} %get-tuple-element.13.lifted_ref, ...), custom_call_target="tpu_custom_call" | custom-call | tf_op jit(solution)/shard_map/pallas_call | solution.py:358
  35.1 15.1 %all_to_all.16.parts_ref = f32[32,16,128]{2,1,0:T(8,128)S(1)} all-to-all(f32[32,16,128]{2,1,0:T(8,128)S(1)} %get-tuple-element.20), channel_id=1, replica_groups=mesh['space'=16,'dp'=2] {'space','dp'}, dimensions={0} | all-to-all | bytes 524288 | tf_op jit(solution)/shard_map/all_to_all | solution.py:374
  50.2 0.1 shard_map.97
  50.3 12.8 %all_to_all.17.sums_ref = f32[32,16,128]{2,1,0:T(8,128)S(1)} all-to-all(f32[32,16,128]{2,1,0:T(8,128)S(1)} %shard_map.97), channel_id=1, replica_groups=mesh['space'=16,'dp'=2] {'space','dp'}, dimensions={0} | all-to-all | bytes 524288 | tf_op jit(solution)/shard_map/all_to_all | solution.py:377
  63.1 1.1 %shard_map.98 = (f32[27,32,32]{2,1,0:T(8,128)}, f32[27,32,32]{2,1,0:T(8,128)}) custom-call(f32[32,16,128]{2,1,0:T(8,128)S(1)} %all_to_all.17.sums_ref), custom_call_target="tpu_custom_call" | custom-call | tf_op jit(solution)/shard_map/pallas_call | solution.py:379
  (2 shorter events, 0.0 us)
Async XLA Ops:
  0.6 17.8 %copy-start = (bf16[64,2048]{1,0:T(8,128)(2,1)S(1)}, bf16[64,2048]{1,0:T(8,128)(2,1)}, u32[]{:S(2)}) copy-start(bf16[64,2048]{1,0:T(8,128)(2,1)} %up_ref.1) | copy-start | bytes 786436
  0.6 0.9 %copy-start.4 = (bf16[1,64,512]{2,1,0:T(8,128)(2,1)S(1)}, bf16[1,64,512]{2,1,0:T(8,128)(2,1)}, u32[]{:S(2)}) copy-start(bf16[1,64,512]{2,1,0:T(8,128)(2,1)} %latents_ref.1) | copy-start | bytes 196612
  1.5 0.7 %copy-start.6 = (s32[1,32]{1,0:T(1,128)S(1)}, s32[1,32]{1,0:T(1,128)}, u32[]{:S(2)}) copy-start(s32[1,32]{1,0:T(1,128)} %ids_ref.1) | copy-start | bytes 388
  2.4 16.1 %copy-start.1 = (bf16[1,2,8,8,256]{4,3,2,1,0:T(8,128)(2,1)S(1)}, bf16[1,2,8,8,256]{4,3,2,1,0:T(8,128)(2,1)}, u32[]{:S(2)}) copy-start(bf16[1,2,8,8,256]{4,3,2,1,0:T(8,128)(2,1)} %cotangent_ref.3) | copy-start | bytes 196612
  2.4 16.1 %copy-start.5 = (s32[1,2,6]{2,1,0:T(2,128)S(1)}, s32[1,2,6]{2,1,0:T(2,128)}, u32[]{:S(2)}) copy-start(s32[1,2,6]{2,1,0:T(2,128)} %links_ref.3) | copy-start | bytes 148
  18.5 0.9 %copy-start.3 = (bf16[27,32,32]{2,1,0:T(8,128)(2,1)S(1)}, bf16[27,32,32]{2,1,0:T(8,128)(2,1)}, u32[]{:S(2)}) copy-start(bf16[27,32,32]{2,1,0:T(8,128)(2,1)} %one_ref.1) | copy-start | bytes 165892
  19.4 11.7 %copy-start.2 = (bf16[27,32,32]{2,1,0:T(8,128)(2,1)S(1)}, bf16[27,32,32]{2,1,0:T(8,128)(2,1)}, u32[]{:S(2)}) copy-start(bf16[27,32,32]{2,1,0:T(8,128)(2,1)} %two_ref.1) | copy-start | bytes 165892
  22.1 4.7 %collective-permute-start = (bf16[96,256]{1,0:T(8,128)(2,1)S(1)}, bf16[96,256]{1,0:T(8,128)(2,1)S(1)}, u32[]{:S(2)}, u32[]{:S(2)}) collective-permute-start(bf16[96,256]{1,0:T(8,128)(2,1)S(1)} %get-tuple-element.17.high_own), channel_id=1, source_target_pairs={{0,2},{2,4},{4,6},{6,8},{8,10},{10,12},{12,14},{14,16},{16,18},{18... | collective-permute-start | bytes 147464 | tf_op jit(solution)/shard_map/ppermute | solution.py:314
  25.1 6.0 %collective-permute-start.1 = (bf16[96,256]{1,0:T(8,128)(2,1)S(1)}, bf16[96,256]{1,0:T(8,128)(2,1)S(1)}, u32[]{:S(2)}, u32[]{:S(2)}) collective-permute-start(bf16[96,256]{1,0:T(8,128)(2,1)S(1)} %get-tuple-element.18.low_own), channel_id=1, source_target_pairs={{2,0},{4,2},{6,4},{8,6},{10,8},{12,10},{14,12},{16,14},{18,16},{20... | collective-permute-start | bytes 147464 | tf_op jit(solution)/shard_map/ppermute | solution.py:314

commit v2 on v1

--- a/solution.py
+++ b/solution.py
@@ -38,18 +38,29 @@
     return lax.broadcasted_iota(jnp.int32, shape, len(shape) - 1)
 
 
-def pick_kernel(devices, ids_ref, latents_ref, out_ref, rows_ref):
-    held = latents_ref.shape[1]
+def pick_kernel(devices, ids_hbm, latents_hbm, out_ref, ids_ref, latents_ref, rows_ref, sems):
+    ids_copy = pltpu.make_async_copy(ids_hbm, ids_ref, sems.at[0])
+    latents_copy = pltpu.make_async_copy(latents_hbm, latents_ref, sems.at[1])
+    ids_copy.start()
+    latents_copy.start()
+    held, width = latents_ref.shape[1:]
     bricks = ids_ref.shape[1]
+    margin = 8 * width // 128
+    tiles = width // 128
+    rows_ref[0:margin] = jnp.zeros((margin, 128), F32)
+    rows_ref[margin + bricks * tiles :] = jnp.zeros((margin, 128), F32)
     first = lax.axis_index("space") * held
     rows = lax.broadcasted_iota(jnp.int32, (held, bricks), 0) + first
+    ids_copy.wait()
     hot = jnp.where(rows == ids_ref[...], 1.0, 0.0).astype(BF16)
-    rows_ref[0:8] = jnp.zeros((8, rows_ref.shape[1]), F32)
-    rows_ref[8 : 8 + bricks] = dot_rows(hot, latents_ref[0])
-    rows_ref[8 + bricks : 16 + bricks] = jnp.zeros((8, rows_ref.shape[1]), F32)
+    latents_copy.wait()
+    picked = dot_rows(hot, latents_ref[0])
+    for tile in range(tiles):
+        rows_ref[pl.ds(margin + tile, bricks, stride=tiles), :] = picked[:, tile * 128 : tile * 128 + 128]
+    count = out_ref.shape[1]
     for receiver in range(devices):
-        start = 8 + BRICKS * (receiver - 1)
-        out_ref[receiver] = rows_ref[start : start + 8].astype(BF16)
+        start = margin + BRICKS * (receiver - 1) * tiles
+        out_ref[receiver] = rows_ref[start : start + count].astype(BF16)
 
 
 def build_band(band_ref, rows):
@@ -75,6 +86,16 @@
     cube = jnp.swapaxes(weights, 1, 2).reshape(9, 3, CHANNELS, CHANNELS)
     pieces = [jnp.concatenate([cube[8 - k, 2], cube[8 - k, 1], cube[8 - k, 0]], axis=-1) for k in range(9)]
     return jnp.concatenate(pieces, axis=0).astype(BF16)
+
+
+def band_kernel(weights_ref, band_ref):
+    build_band(band_ref, weight_rows(weights_ref[...].astype(F32)))
+
+
+def two_bands_kernel(weights_ref, band_ref, back_ref):
+    weights = weights_ref[...].astype(F32)
+    build_band(band_ref, weight_rows(weights))
+    build_band(back_ref, flipped_rows(weights))
 
 
 def put_padded(pad_ref, brick, volume, x_low, x_high, y_low, y_high, z_low, z_high):
@@ -133,13 +154,18 @@
 
 
 def first_kernel(
-    links_ref, received_ref, up_ref, one_ref, cotangent_ref,
+    links_ref, received_ref, up_ref, band_ref, cotangent_ref,
     lifted_out, pre_out, hidden_out, pad_out, high_out, low_out,
-    volumes_ref, pad_ref, band_ref, lines_ref, high_ref, low_ref,
+    volumes_ref, pad_ref, lines_ref, high_ref, low_ref, rows_ref,
 ):
     position = lax.axis_index("space")
-    latents = jnp.sum(received_ref[...].astype(F32), axis=0)
-    cells = [latents[:, cell * 64 : cell * 64 + 64] for cell in range(8)]
+    tiles = received_ref.shape[1] // (3 * BRICKS)
+    rows_ref[0 : 3 * BRICKS * tiles] = jnp.sum(received_ref[...].astype(F32), axis=0)
+    rows_ref[3 * BRICKS * tiles :] = jnp.zeros((2 * tiles, 128), F32)
+    cells = []
+    for tile in range(tiles):
+        rows = rows_ref[pl.ds(tile, 8, stride=tiles), :]
+        cells += [rows[:, :64], rows[:, 64:]]
     lifted = dot(jnp.concatenate(cells, axis=0).astype(BF16), up_ref[...])
     lifted = lifted.astype(BF16).astype(F32)
     for cell in range(8):
@@ -176,7 +202,6 @@
         put_padded(
             pad_ref, brick, volume, x_face(0), x_face(1), y_face(2), y_face(3), z_face(4), z_face(5)
         )
-    build_band(band_ref, weight_rows(one_ref[...].astype(F32)))
     pre = convolve(pad_ref, band_ref)
     hidden = pre / (1.0 + jnp.exp(-pre))
     hidden = hidden.astype(BF16)
@@ -222,85 +247,89 @@
     return total
 
 
-def second_kernel(
-    links_ref, cotangent_ref, two_ref, lifted_ref, pre_ref, hidden_ref, pad_in,
-    high_own, low_own, high_left, low_right,
-    fine_out, sums_out,
-    high_ref, low_ref, hidden_pad, cotangent_pad, lifted_pad, band_ref, outer_ref,
-):
+def padded_brick(pad_ref, brick, which, values, links_ref, high_ref, low_ref):
     position = lax.axis_index("space")
+    half = high_ref.shape[0] // 2
+
+    def rows(face, axis):
+        link = links_ref[0, brick, face]
+        high = face % 2 == 0
+        index = jnp.clip(link - BRICKS * (position - 1 if high else position), 0, 2 * BRICKS - 1)
+        start = (index // BRICKS) * half + (which * BRICKS + index % BRICKS) * FACE + axis * EDGE
+        pool = high_ref if high else low_ref
+        present = jnp.where(link >= 0, 1.0, 0.0).astype(F32)
+        return pool[pl.ds(pl.multiple_of(start, 8), EDGE), :] * present
+
+    volume = values[brick * CUBE : brick * CUBE + CUBE].reshape(EDGE, EDGE, LINE)
+    put_padded(
+        pad_ref, brick, volume, rows(0, 0), rows(1, 0), rows(2, 1), rows(3, 1),
+        unpack_depth(rows(4, 2), True), unpack_depth(rows(5, 2), False),
+    )
+
+
+def fill_pools(high_ref, low_ref, high_own, low_own, high_left, low_right):
     half = 2 * BRICKS * FACE
     high_ref[0:half] = high_left[...].astype(F32)
     high_ref[half:] = high_own[...].astype(F32)
     low_ref[0:half] = low_own[...].astype(F32)
     low_ref[half:] = low_right[...].astype(F32)
+
+
+def second_kernel(
+    links_ref, cotangent_ref, band_ref, back_ref, lifted_ref, pre_ref, hidden_ref, pad_in,
+    high_own, low_own, high_left, low_right,
+    fine_out, sums_out,
+    high_ref, low_ref, hidden_pad, cotangent_pad, lifted_pad, outer_ref, sums_ref,
+):
+    fill_pools(high_ref, low_ref, high_own, low_own, high_left, low_right)
     lifted_pad[...] = pad_in[...].astype(F32).reshape(lifted_pad.shape)
     cotangent = cotangent_ref[...].astype(F32).reshape(LINES, LINE)
     hidden = hidden_ref[...].astype(F32)
     for which, values, pad_ref in ((0, hidden, hidden_pad), (1, cotangent, cotangent_pad)):
         for brick in range(BRICKS):
-
-            def rows(face, axis):
-                link = links_ref[0, brick, face]
-                high = face % 2 == 0
-                index = jnp.clip(link - BRICKS * (position - 1 if high else position), 0, 2 * BRICKS - 1)
-                start = (index // BRICKS) * half + (which * BRICKS + index % BRICKS) * FACE + axis * EDGE
-                pool = high_ref if high else low_ref
-                present = jnp.where(link >= 0, 1.0, 0.0).astype(F32)
-                return pool[pl.ds(pl.multiple_of(start, 8), EDGE), :] * present
-
-            volume = values[brick * CUBE : brick * CUBE + CUBE].reshape(EDGE, EDGE, LINE)
-            put_padded(
-                pad_ref, brick, volume, rows(0, 0), rows(1, 0), rows(2, 1), rows(3, 1),
-                unpack_depth(rows(4, 2), True), unpack_depth(rows(5, 2), False),
-            )
-    weights = two_ref[...].astype(F32)
-    build_band(band_ref, weight_rows(weights))
+            padded_brick(pad_ref, brick, which, values, links_ref, high_ref, low_ref)
     fine = lifted_ref[...].astype(F32) + convolve(hidden_pad, band_ref)
     fine_out[...] = fine.astype(BF16).reshape(fine_out.shape)
-    build_band(band_ref, flipped_rows(weights))
-    back = convolve(cotangent_pad, band_ref)
+    back = convolve(cotangent_pad, back_ref)
     pre = pre_ref[...]
     sigmoid = 1.0 / (1.0 + jnp.exp(-pre))
     gradient = (back * sigmoid * (1.0 + pre * (1.0 - sigmoid))).astype(BF16)
     upstream = cotangent.astype(BF16)
-    sums_out[...] = jnp.zeros(sums_out.shape, F32)
-    per = sums_out.shape[1] // 8
+    sums_ref[8 * BLOCKS :] = jnp.zeros((sums_ref.shape[0] - 8 * BLOCKS, 128), F32)
     for base, pad_ref, right in ((0, lifted_pad, gradient), (27, hidden_pad, upstream)):
         for k in range(9):
             outer_ref[...] = dot_rows(window(pad_ref, k), right)
             for part in range(3):
-                index = base + 3 * k + part
-                sums_out[index // per, index % per * 8 : index % per * 8 + 8] = fold_diagonals(outer_ref, part)
+                start = 8 * (base + 3 * k + part)
+                sums_ref[start : start + 8] = fold_diagonals(outer_ref, part)
+    sums_out[...] = sums_ref[...].astype(BF16).reshape(sums_out.shape)
 
 
 def sum_kernel(scale, parts_ref, out_ref):
-    total = jnp.sum(parts_ref[...], axis=0) * scale
-    out_ref[...] = jnp.broadcast_to(total[None], out_ref.shape)
-
-
-def unpack_kernel(sums_ref, one_out, two_out):
-    per = sums_ref.shape[1] // 8
+    total = jnp.sum(parts_ref[...].astype(F32), axis=0) * scale
+    out_ref[...] = jnp.broadcast_to(total.astype(BF16)[None], out_ref.shape)
+
+
+def unpack_kernel(sums_ref, one_out, two_out, rows_ref):
+    rows_ref[...] = sums_ref[...].astype(F32).reshape(rows_ref.shape)
     for index in range(BLOCKS):
-        block = sums_ref[index // per, index % per * 8 : index % per * 8 + 8]
+        block = rows_ref[8 * index : 8 * index + 8]
         out = one_out if index < 27 else two_out
         for q in range(4):
             moved = pltpu.roll(block, 128 - q * CHANNELS, 1) if q else block
             out[index % 27, 8 * q : 8 * q + 8, :] = moved[:, :CHANNELS]
 
 
-def call(kernel, out_shape, scratch=(), smem_first=False, inputs=1, limit=24):
-    specs = [pl.BlockSpec(memory_space=pltpu.VMEM)] * inputs
-    if smem_first:
-        specs[0] = pl.BlockSpec(memory_space=pltpu.SMEM)
-    out_specs = jax.tree.map(lambda _: pl.BlockSpec(memory_space=pltpu.VMEM), out_shape)
+def call(kernel, out_shape, scratch=(), smem=(), hbm=(), inputs=1, limit=24, cost=None):
+    spaces = [pltpu.SMEM if i in smem else pltpu.HBM if i in hbm else pltpu.VMEM for i in range(inputs)]
     return pl.pallas_call(
         kernel,
         out_shape=out_shape,
-        in_specs=specs,
-        out_specs=out_specs,
+        in_specs=[pl.BlockSpec(memory_space=space) for space in spaces],
+        out_specs=jax.tree.map(lambda _: pl.BlockSpec(memory_space=pltpu.VMEM), out_shape),
         scratch_shapes=list(scratch),
         compiler_params=pltpu.CompilerParams(vmem_limit_bytes=limit * 2**20),
+        cost_estimate=cost,
     )
 
 
@@ -317,18 +346,28 @@
 def body(coarse_latents, active_blocks, face_links, cotangent, up_weight, conv_one, conv_two):
     devices = lax.axis_size("space")
     everyone = devices * lax.axis_size("dp")
-    width = coarse_latents.shape[2]
+    held, width = coarse_latents.shape[1:]
     bricks = active_blocks.shape[1]
+    tiles = width // 128
     packed = call(
         functools.partial(pick_kernel, devices),
-        shape(devices, 8, width),
-        [pltpu.VMEM((bricks + 16, width), F32)],
+        shape(devices, 3 * BRICKS * tiles, 128),
+        [
+            pltpu.VMEM((1, bricks), jnp.int32),
+            pltpu.VMEM((1, held, width), BF16),
+            pltpu.VMEM(((bricks + 16) * tiles, 128), F32),
+            pltpu.SemaphoreType.DMA((2,)),
+        ],
+        hbm=(0, 1),
         inputs=2,
     )(active_blocks, coarse_latents)
     received = lax.all_to_all(packed, "space", split_axis=0, concat_axis=0, tiled=True)
+    band = shape(9, WIDE, LINE)
+    cost = pl.CostEstimate(flops=10**9, bytes_accessed=2 * 10**6, transcendentals=0)
+    band_one = call(band_kernel, band, cost=cost)(conv_one)
+    band_two, band_back = call(two_bands_kernel, (band, band), cost=cost)(conv_two)
     pad_shape = (3, BRICKS, EDGE + 2, EDGE, WIDE)
     pad = pltpu.VMEM(pad_shape, F32)
-    band = pltpu.VMEM((9, WIDE, LINE), BF16)
     packed_faces = 2 * BRICKS * FACE
     lifted, pre, hidden, lifted_pad, high, low = call(
         first_kernel,
@@ -343,40 +382,44 @@
         [
             pltpu.VMEM((2, 8 * CUBE, 128), F32),
             pad,
-            band,
             pltpu.VMEM((2, 2 * LINES, 128), F32),
             pltpu.VMEM((packed_faces, LINE), F32),
             pltpu.VMEM((packed_faces, LINE), F32),
+            pltpu.VMEM((8 * tiles, 128), F32),
         ],
-        smem_first=True,
+        smem=(0,),
         inputs=5,
-    )(face_links, received, up_weight, conv_one, cotangent)
+    )(face_links, received, up_weight, band_one, cotangent)
     high_left = passed_along(high, "space", 1)
     low_right = passed_along(low, "space", -1)
     per = -(-BLOCKS // everyone)
     per += per % 2
     fine, sums = call(
         second_kernel,
-        (shape(*cotangent.shape), shape(everyone, per * 8, 128, dtype=F32)),
+        (shape(*cotangent.shape), shape(everyone, per * 8, 128)),
         [
             pltpu.VMEM((2 * packed_faces, LINE), F32),
             pltpu.VMEM((2 * packed_faces, LINE), F32),
             pad,
             pad,
             pad,
-            band,
             pltpu.VMEM((WIDE, LINE), F32),
+            pltpu.VMEM((everyone * per * 8, 128), F32),
         ],
-        smem_first=True,
-        inputs=11,
-    )(face_links, cotangent, conv_two, lifted, pre, hidden, lifted_pad, high, low, high_left, low_right)
+        smem=(0,),
+        inputs=12,
+    )(
+        face_links, cotangent, band_two, band_back, lifted, pre, hidden, lifted_pad,
+        high, low, high_left, low_right,
+    )
     axes = ("space", "dp")
     parts = lax.all_to_all(sums, axes, split_axis=0, concat_axis=0, tiled=True)
     scale = 1.0 / math.sqrt(lax.axis_size("dp") * devices * BRICKS * EDGE**3)
-    total = call(functools.partial(sum_kernel, scale), shape(*sums.shape, dtype=F32))(parts)
+    total = call(functools.partial(sum_kernel, scale), shape(*sums.shape))(parts)
     gathered = lax.all_to_all(total, axes, split_axis=0, concat_axis=0, tiled=True)
     grads = shape(27, CHANNELS, CHANNELS, dtype=F32)
-    grad_one, grad_two = call(unpack_kernel, (grads, grads))(gathered)
+    rows = pltpu.VMEM((everyone * per * 8, 128), F32)
+    grad_one, grad_two = call(unpack_kernel, (grads, grads), [rows])(gathered)
     return (fine, grad_one, grad_two)
 
 

time: 64.5 us -> 57.1 us (0.89)
  blocking collectives: 43.9 us -> 22.7 us
  starting transfers between devices: 4.29 us -> 12.5 us
  waiting for transfers between devices: 4.68 us -> 9.76 us
    all_to_all x1 -> x0, blocking collectives: 16 us -> none  [body(): lax.all_to_all(packed, 'space', split_axis=0, concat_axis=0, tiled=True)]
    all_to_all x0 -> x1, starting transfers between devices: none -> 8.32 us  [body(): lax.all_to_all(packed, 'space', split_axis=0, concat_axis=0, tiled=True)]
    all_to_all x0 -> x1, waiting for transfers between devices: none -> 6.1 us  [body(): lax.all_to_all(packed, 'space', split_axis=0, concat_axis=0, tiled=True)]
    all_to_all x1, blocking collectives: 12.8 us -> 10 us  [body(): lax.all_to_all(total, axes, split_axis=0, concat_axis=0, tiled=True)]
    all_to_all x1, blocking collectives: 15.1 us -> 12.7 us  [body(): parts = lax.all_to_all(sums, axes, split_axis=0, concat_axis=0, tiled=True)]
    pallas_call x3 -> x5, Pallas kernels: 1.35 us -> 3.6 us  [the longest x1 1.04 us: body(): grad_one, grad_two = call(unpack_kernel, (grads, grads), [rows])(gathered)]
    ppermute x2, waiting for transfers between devices: 4.68 us -> 3.66 us  [passed_along(): lax.ppermute(value, axis, [(source, source + steps) for source in range(f...]
    pallas_call x1, Pallas kernels: 2.67 us -> 1.79 us  [body(): call(first_kernel, (shape(LINES, LINE), shape(LINES, LINE, dtype=F32), sh...]
  transfers between devices with their start and end apart: 2 -> 3, of which waited for: 2 -> 2; matrix products, arithmetic and copies ran while one was open for 0% -> 0% of each run, Pallas kernels for 0% -> 3%
where the time goes in v2:
time: 57.1 us; the launch traced here: 56.7 us
  blocking collectives  22.7 us (40%)
  starting transfers between devices  12.5 us (22%)
  waiting for transfers between devices  9.76 us (17%)
  Pallas kernels  8.63 us (15%)
  local copies, waits for them, and re-layouts  2.44 us (4%)
  between operations  0.73 us (1%)
    all_to_all x1, blocking collectives, body(): parts = lax.all_to_all(sums, axes, split_axis=0, concat_axis=0, tiled=True)  12.7 us
    all_to_all x1, blocking collectives, body(): lax.all_to_all(total, axes, split_axis=0, concat_axis=0, tiled=True)  10 us
    all_to_all x1, starting transfers between devices, body(): lax.all_to_all(packed, 'space', split_axis=0, concat_axis=0, tiled=True)  8.32 us
    all_to_all x1, waiting for transfers between devices, body(): lax.all_to_all(packed, 'space', split_axis=0, concat_axis=0, tiled=True)  6.1 us
    ppermute x2, starting transfers between devices, passed_along(): lax.ppermute(value, axis, [(source, source + steps) for source in range(f...  4.16 us
    ppermute x2, waiting for transfers between devices, passed_along(): lax.ppermute(value, axis, [(source, source + steps) for source in range(f...  3.66 us
    pallas_call x1, Pallas kernels, body(): call(second_kernel, (shape(*cotangent.shape), shape(everyone, per * 8, 12...  3.24 us
    unnamed x14, local copies, waits for them, and re-layouts  2.44 us
  transfers between devices with their start and end apart: 3, of which 2 were waited for; matrix products, arithmetic and copies ran while one was open for 0% of the time, Pallas kernels for 3%

profile of v2, /device:TPU:0, one launch (start us, length us, event | category | flops | bytes accessed | tf_op | source)
XLA Modules:
  0.0 56.7 jit_solution(1213052270350550336)
XLA Ops:
  0.6 0.0 copy-start.2
  0.6 0.8 %copy-done.2 = bf16[1,64,512]{2,1,0:T(8,128)(2,1)S(1)} copy-done((bf16[1,64,512]{2,1,0:T(8,128)(2,1)S(1)}, bf16[1,64,512]{2,1,0:T(8,128)(2,1)}, u32[]{:S(2)}) %copy-start.2) | copy-done | bytes 65560
  1.5 0.7 %copy-done.4 = s32[1,32]{1,0:T(1,128)S(1)} copy-done((s32[1,32]{1,0:T(1,128)S(1)}, s32[1,32]{1,0:T(1,128)}, u32[]{:S(2)}) %copy-start.4) | copy-done | bytes 152
  2.1 0.9 %shard_map.95 = bf16[16,24,128]{2,1,0:T(8,128)(2,1)} custom-call(s32[1,32]{1,0:T(1,128)S(1)} %copy-done.4, bf16[1,64,512]{2,1,0:T(8,128)(2,1)S(1)} %copy-done.2), custom_call_target="tpu_custom_call" | custom-call | tf_op jit(solution)/shard_map/pallas_call | solution.py:352
  3.1 8.3 %all-to-all-start = ((bf16[16,24,128]{2,1,0:T(8,128)(2,1)}), bf16[16,24,128]{2,1,0:T(8,128)(2,1)S(1)}, u32[]{:S(2)}, u32[]{:S(2)}) async-start(bf16[16,24,128]{2,1,0:T(8,128)(2,1)} %shard_map.95), calls=%async_computation | async-start | bytes 196608 | tf_op jit(solution)/shard_map/all_to_all | solution.py:364
  11.4 0.0 copy-start.5
  11.4 0.9 %copy-done.5 = bf16[27,32,32]{2,1,0:T(8,128)(2,1)S(1)} copy-done((bf16[27,32,32]{2,1,0:T(8,128)(2,1)S(1)}, bf16[27,32,32]{2,1,0:T(8,128)(2,1)}, u32[]{:S(2)}) %copy-start.5) | copy-done | bytes 55320
  12.3 0.6 %shard_map.96.band_ref = bf16[9,384,256]{2,1,0:T(8,128)(2,1)S(1)} custom-call(bf16[27,32,32]{2,1,0:T(8,128)(2,1)S(1)} %copy-done.5), custom_call_target="tpu_custom_call" | custom-call | flops 1000000000 | bytes 2000000 | tf_op jit(solution)/shard_map/pallas_call | solution.py:367
  12.9 0.0 copy-start.6
  13.0 6.1 %all-to-all-done.received_ref = bf16[16,24,128]{2,1,0:T(8,128)(2,1)S(1)} async-done(((bf16[16,24,128]{2,1,0:T(8,128)(2,1)}), bf16[16,24,128]{2,1,0:T(8,128)(2,1)S(1)}, u32[]{:S(2)}, u32[]{:S(2)}) %all-to-all-start) | async-done | bytes 98336 | tf_op jit(solution)/shard_map/all_to_all | solution.py:364
  19.1 0.0 copy-done
  19.1 0.0 copy-done.1
  19.1 0.0 copy-done.3
  19.1 1.8 %shard_map.97 = (bf16[128,256]{1,0:T(8,128)(2,1)S(1)}, f32[128,256]{1,0:T(8,128)S(1)}, bf16[128,256]{1,0:T(8,128)(2,1)S(1)}, bf16[480,384]{1,0:T(8,128)(2,1)S(1)...) custom-call(s32[1,2,6]{2,1,0:T(2,128)S(1)} %copy-done.3, bf16[16,24,128]{2,1,0:T(8,128)(2,1)S(1)} %all-to-all-done.received_ref, ...), custom_call_target="tpu_custom_call" | custom-call | tf_op jit(solution)/shard_map/pallas_call | solution.py:372
  20.9 2.9 %collective-permute-start = (bf16[96,256]{1,0:T(8,128)(2,1)S(1)}, bf16[96,256]{1,0:T(8,128)(2,1)S(1)}, u32[]{:S(2)}, u32[]{:S(2)}) collective-permute-start(bf16[96,256]{1,0:T(8,128)(2,1)S(1)} %get-tuple-element.21.high_own), channel_id=1, source_target_pairs={{0,2},{2,4},{4,6},{6,8},{8,10},{10,12},{12,14},{14,16},{16,18},{18... | collective-permute-start | bytes 147464 | tf_op jit(solution)/shard_map/ppermute | solution.py:343
  23.7 1.3 %collective-permute-start.1 = (bf16[96,256]{1,0:T(8,128)(2,1)S(1)}, bf16[96,256]{1,0:T(8,128)(2,1)S(1)}, u32[]{:S(2)}, u32[]{:S(2)}) collective-permute-start(bf16[96,256]{1,0:T(8,128)(2,1)S(1)} %get-tuple-element.22.low_own), channel_id=1, source_target_pairs={{2,0},{4,2},{6,4},{8,6},{10,8},{12,10},{14,12},{16,14},{18,16},{20... | collective-permute-start | bytes 147464 | tf_op jit(solution)/shard_map/ppermute | solution.py:343
  25.0 0.0 copy-done.6
  25.0 1.0 %shard_map.94 = (bf16[9,384,256]{2,1,0:T(8,128)(2,1)S(1)}, bf16[9,384,256]{2,1,0:T(8,128)(2,1)S(1)}) custom-call(bf16[27,32,32]{2,1,0:T(8,128)(2,1)S(1)} %copy-done.6), custom_call_target="tpu_custom_call" | custom-call | flops 1000000000 | bytes 2000000 | tf_op jit(solution)/shard_map/pallas_call | solution.py:368
  26.0 0.0 collective-permute-done.high_left
  26.1 3.7 %collective-permute-done.1.low_right = bf16[96,256]{1,0:T(8,128)(2,1)S(1)} collective-permute-done((bf16[96,256]{1,0:T(8,128)(2,1)S(1)}, bf16[96,256]{1,0:T(8,128)(2,1)S(1)}, u32[]{:S(2)}, u32[]{:S(2)}) %collective-permute-start.1) | collective-permute-done | bytes 49184 | tf_op jit(solution)/shard_map/ppermute | solution.py:343
  29.7 3.2 %shard_map.98 = (bf16[1,2,8,8,256]{4,3,2,1,0:T(8,128)(2,1)}, bf16[32,16,128]{2,1,0:T(8,128)(2,1)S(1)}) custom-call(s32[1,2,6]{2,1,0:T(2,128)S(1)} %copy-done.3, bf16[1,2,8,8,256]{4,3,2,1,0:T(8,128)(2,1)S(1)} %copy-done, bf16[9,384,256]{2,1,0:T(8,128)(2,1)S(1)} %get-tuple-element.15.band_ref, bf16[9,384,256]{2,1,0:T(8,128)(2,1)S(1)} %get-tuple-element.16.back_ref, ...), custom_call_target="tpu_custom_call" | custom-call | tf_op jit(solution)/shard_map/pallas_call | solution.py:397
  33.0 12.7 %all_to_all.15.parts_ref = bf16[32,16,128]{2,1,0:T(8,128)(2,1)S(1)} all-to-all(bf16[32,16,128]{2,1,0:T(8,128)(2,1)S(1)} %get-tuple-element.24), channel_id=1, replica_groups=mesh['space'=16,'dp'=2] {'space','dp'}, dimensions={0} | all-to-all | bytes 262144 | tf_op jit(solution)/shard_map/all_to_all | solution.py:416
  45.7 10.0 %all_to_all.16.sums_ref = bf16[32,16,128]{2,1,0:T(8,128)(2,1)S(1)} all-to-all(bf16[32,16,128]{2,1,0:T(8,128)(2,1)S(1)} %shard_map.99), channel_id=1, replica_groups=mesh['space'=16,'dp'=2] {'space','dp'}, dimensions={0} | all-to-all | bytes 262144 | tf_op jit(solution)/shard_map/all_to_all | solution.py:419
  55.7 1.0 %shard_map.100 = (f32[27,32,32]{2,1,0:T(8,128)}, f32[27,32,32]{2,1,0:T(8,128)}) custom-call(bf16[32,16,128]{2,1,0:T(8,128)(2,1)S(1)} %all_to_all.16.sums_ref), custom_call_target="tpu_custom_call" | custom-call | tf_op jit(solution)/shard_map/pallas_call | solution.py:422
  (5 shorter events, 0.1 us)
Async XLA Ops:
  0.6 0.8 %copy-start.2 = (bf16[1,64,512]{2,1,0:T(8,128)(2,1)S(1)}, bf16[1,64,512]{2,1,0:T(8,128)(2,1)}, u32[]{:S(2)}) copy-start(bf16[1,64,512]{2,1,0:T(8,128)(2,1)} %latents_hbm.1) | copy-start | bytes 196612
  1.5 0.7 %copy-start.4 = (s32[1,32]{1,0:T(1,128)S(1)}, s32[1,32]{1,0:T(1,128)}, u32[]{:S(2)}) copy-start(s32[1,32]{1,0:T(1,128)} %ids_hbm.1) | copy-start | bytes 388
  3.1 16.0 %all-to-all-start = ((bf16[16,24,128]{2,1,0:T(8,128)(2,1)}), bf16[16,24,128]{2,1,0:T(8,128)(2,1)S(1)}, u32[]{:S(2)}, u32[]{:S(2)}) async-start(bf16[16,24,128]{2,1,0:T(8,128)(2,1)} %shard_map.95), calls=%async_computation | async-start | bytes 196608 | tf_op jit(solution)/shard_map/all_to_all | solution.py:364
  11.4 0.9 %copy-start.5 = (bf16[27,32,32]{2,1,0:T(8,128)(2,1)S(1)}, bf16[27,32,32]{2,1,0:T(8,128)(2,1)}, u32[]{:S(2)}) copy-start(bf16[27,32,32]{2,1,0:T(8,128)(2,1)} %weights_ref.3) | copy-start | bytes 165892
  12.3 6.7 %copy-start = (bf16[1,2,8,8,256]{4,3,2,1,0:T(8,128)(2,1)S(1)}, bf16[1,2,8,8,256]{4,3,2,1,0:T(8,128)(2,1)}, u32[]{:S(2)}) copy-start(bf16[1,2,8,8,256]{4,3,2,1,0:T(8,128)(2,1)} %cotangent_ref.3) | copy-start | bytes 196612
  12.3 6.7 %copy-start.1 = (bf16[64,2048]{1,0:T(8,128)(2,1)S(1)}, bf16[64,2048]{1,0:T(8,128)(2,1)}, u32[]{:S(2)}) copy-start(bf16[64,2048]{1,0:T(8,128)(2,1)} %up_ref.1) | copy-start | bytes 786436
  12.3 6.7 %copy-start.3 = (s32[1,2,6]{2,1,0:T(2,128)S(1)}, s32[1,2,6]{2,1,0:T(2,128)}, u32[]{:S(2)}) copy-start(s32[1,2,6]{2,1,0:T(2,128)} %links_ref.3) | copy-start | bytes 148
  12.9 12.1 %copy-start.6 = (bf16[27,32,32]{2,1,0:T(8,128)(2,1)S(1)}, bf16[27,32,32]{2,1,0:T(8,128)(2,1)}, u32[]{:S(2)}) copy-start(bf16[27,32,32]{2,1,0:T(8,128)(2,1)} %weights_ref.2) | copy-start | bytes 165892
  20.9 5.2 %collective-permute-start = (bf16[96,256]{1,0:T(8,128)(2,1)S(1)}, bf16[96,256]{1,0:T(8,128)(2,1)S(1)}, u32[]{:S(2)}, u32[]{:S(2)}) collective-permute-start(bf16[96,256]{1,0:T(8,128)(2,1)S(1)} %get-tuple-element.21.high_own), channel_id=1, source_target_pairs={{0,2},{2,4},{4,6},{6,8},{8,10},{10,12},{12,14},{14,16},{16,18},{18... | collective-permute-start | bytes 147464 | tf_op jit(solution)/shard_map/ppermute | solution.py:343
  23.7 6.0 %collective-permute-start.1 = (bf16[96,256]{1,0:T(8,128)(2,1)S(1)}, bf16[96,256]{1,0:T(8,128)(2,1)S(1)}, u32[]{:S(2)}, u32[]{:S(2)}) collective-permute-start(bf16[96,256]{1,0:T(8,128)(2,1)S(1)} %get-tuple-element.22.low_own), channel_id=1, source_target_pairs={{2,0},{4,2},{6,4},{8,6},{10,8},{12,10},{14,12},{16,14},{18,16},{20... | collective-permute-start | bytes 147464 | tf_op jit(solution)/shard_map/ppermute | solution.py:343

commit v3 on v2

--- a/solution.py
+++ b/solution.py
@@ -38,11 +38,7 @@
     return lax.broadcasted_iota(jnp.int32, shape, len(shape) - 1)
 
 
-def pick_kernel(devices, ids_hbm, latents_hbm, out_ref, ids_ref, latents_ref, rows_ref, sems):
-    ids_copy = pltpu.make_async_copy(ids_hbm, ids_ref, sems.at[0])
-    latents_copy = pltpu.make_async_copy(latents_hbm, latents_ref, sems.at[1])
-    ids_copy.start()
-    latents_copy.start()
+def pick_kernel(devices, ids_ref, latents_ref, out_ref, rows_ref):
     held, width = latents_ref.shape[1:]
     bricks = ids_ref.shape[1]
     margin = 8 * width // 128
@@ -51,9 +47,7 @@
     rows_ref[margin + bricks * tiles :] = jnp.zeros((margin, 128), F32)
     first = lax.axis_index("space") * held
     rows = lax.broadcasted_iota(jnp.int32, (held, bricks), 0) + first
-    ids_copy.wait()
     hot = jnp.where(rows == ids_ref[...], 1.0, 0.0).astype(BF16)
-    latents_copy.wait()
     picked = dot_rows(hot, latents_ref[0])
     for tile in range(tiles):
         rows_ref[pl.ds(margin + tile, bricks, stride=tiles), :] = picked[:, tile * 128 : tile * 128 + 128]
@@ -343,22 +337,22 @@
     return lax.ppermute(value, axis, [(source, source + steps) for source in range(first, last)])
 
 
+def swapped(value, groups):
+    return lax.all_to_all(
+        value, ("space", "dp"), split_axis=0, concat_axis=0, axis_index_groups=groups, tiled=True
+    )
+
+
 def body(coarse_latents, active_blocks, face_links, cotangent, up_weight, conv_one, conv_two):
     devices = lax.axis_size("space")
     everyone = devices * lax.axis_size("dp")
-    held, width = coarse_latents.shape[1:]
+    width = coarse_latents.shape[2]
     bricks = active_blocks.shape[1]
     tiles = width // 128
     packed = call(
         functools.partial(pick_kernel, devices),
         shape(devices, 3 * BRICKS * tiles, 128),
-        [
-            pltpu.VMEM((1, bricks), jnp.int32),
-            pltpu.VMEM((1, held, width), BF16),
-            pltpu.VMEM(((bricks + 16) * tiles, 128), F32),
-            pltpu.SemaphoreType.DMA((2,)),
-        ],
-        hbm=(0, 1),
+        [pltpu.VMEM(((bricks + 16) * tiles, 128), F32)],
         inputs=2,
     )(active_blocks, coarse_latents)
     received = lax.all_to_all(packed, "space", split_axis=0, concat_axis=0, tiled=True)
@@ -392,11 +386,12 @@
     )(face_links, received, up_weight, band_one, cotangent)
     high_left = passed_along(high, "space", 1)
     low_right = passed_along(low, "space", -1)
-    per = -(-BLOCKS // everyone)
-    per += per % 2
+    inner = math.gcd(everyone, 8)
+    outer = everyone // inner
+    rows = -(-BLOCKS // inner) * 8
     fine, sums = call(
         second_kernel,
-        (shape(*cotangent.shape), shape(everyone, per * 8, 128)),
+        (shape(*cotangent.shape), shape(inner, rows, 128)),
         [
             pltpu.VMEM((2 * packed_faces, LINE), F32),
             pltpu.VMEM((2 * packed_faces, LINE), F32),
@@ -404,7 +399,7 @@
             pad,
             pad,
             pltpu.VMEM((WIDE, LINE), F32),
-            pltpu.VMEM((everyone * per * 8, 128), F32),
+            pltpu.VMEM((inner * rows, 128), F32),
         ],
         smem=(0,),
         inputs=12,
@@ -412,14 +407,17 @@
         face_links, cotangent, band_two, band_back, lifted, pre, hidden, lifted_pad,
         high, low, high_left, low_right,
     )
-    axes = ("space", "dp")
-    parts = lax.all_to_all(sums, axes, split_axis=0, concat_axis=0, tiled=True)
+    near = [[first * inner + i for i in range(inner)] for first in range(outer)]
+    far = [[first * inner + i for first in range(outer)] for i in range(inner)]
     scale = 1.0 / math.sqrt(lax.axis_size("dp") * devices * BRICKS * EDGE**3)
-    total = call(functools.partial(sum_kernel, scale), shape(*sums.shape))(parts)
-    gathered = lax.all_to_all(total, axes, split_axis=0, concat_axis=0, tiled=True)
+    parts = swapped(sums, near)
+    plane = call(functools.partial(sum_kernel, 1.0), shape(outer, rows, 128))(parts)
+    planes = swapped(plane, far)
+    total = call(functools.partial(sum_kernel, scale), shape(inner, rows, 128))(planes)
+    gathered = swapped(total, near)
     grads = shape(27, CHANNELS, CHANNELS, dtype=F32)
-    rows = pltpu.VMEM((everyone * per * 8, 128), F32)
-    grad_one, grad_two = call(unpack_kernel, (grads, grads), [rows])(gathered)
+    scratch = [pltpu.VMEM((inner * rows, 128), F32)]
+    grad_one, grad_two = call(unpack_kernel, (grads, grads), scratch)(gathered)
     return (fine, grad_one, grad_two)
 
 

time: 57.1 us -> 60.5 us (1.060)
  blocking collectives: 22.7 us -> 26.1 us
    all_to_all x2 -> x3, blocking collectives: 22.7 us -> 26.1 us  [swapped(): lax.all_to_all(value, ('space', 'dp'), split_axis=0, concat_axis=0, axis_...]
    pallas_call x3 -> x4, Pallas kernels: 4.32 us -> 4.31 us  [the longest x1 3.23 us: body(): call(second_kernel, (shape(*cotangent.shape), shape(inner, rows, 128)), [...]
where the time goes in v3:
time: 60.5 us; the launch traced here: 60.1 us
  blocking collectives  26.1 us (43%)
  starting transfers between devices  12.5 us (21%)
  waiting for transfers between devices  9.76 us (16%)
  Pallas kernels  8.53 us (14%)
  local copies, waits for them, and re-layouts  2.44 us (4%)
  between operations  0.73 us (1%)
    all_to_all x3, blocking collectives, swapped(): lax.all_to_all(value, ('space', 'dp'), split_axis=0, concat_axis=0, axis_...  26.1 us
    all_to_all x1, starting transfers between devices, body(): lax.all_to_all(packed, 'space', split_axis=0, concat_axis=0, tiled=True)  8.31 us
    all_to_all x1, waiting for transfers between devices, body(): lax.all_to_all(packed, 'space', split_axis=0, concat_axis=0, tiled=True)  6.1 us
    ppermute x2, starting transfers between devices, passed_along(): lax.ppermute(value, axis, [(source, source + steps) for source in range(f...  4.16 us
    ppermute x2, waiting for transfers between devices, passed_along(): lax.ppermute(value, axis, [(source, source + steps) for source in range(f...  3.66 us
    pallas_call x1, Pallas kernels, body(): call(second_kernel, (shape(*cotangent.shape), shape(inner, rows, 128)), [...  3.23 us
    unnamed x14, local copies, waits for them, and re-layouts  2.44 us
    pallas_call x1, Pallas kernels, body(): call(first_kernel, (shape(LINES, LINE), shape(LINES, LINE, dtype=F32), sh...  1.79 us
  transfers between devices with their start and end apart: 3, of which 2 were waited for; matrix products, arithmetic and copies ran while one was open for 0% of the time, Pallas kernels for 3%

profile of v3, /device:TPU:0, one launch (start us, length us, event | category | flops | bytes accessed | tf_op | source)
XLA Modules:
  0.0 60.1 jit_solution(362055496784713593)
XLA Ops:
  0.6 0.0 copy-start.2
  0.6 0.8 %copy-done.2 = bf16[1,64,512]{2,1,0:T(8,128)(2,1)S(1)} copy-done((bf16[1,64,512]{2,1,0:T(8,128)(2,1)S(1)}, bf16[1,64,512]{2,1,0:T(8,128)(2,1)}, u32[]{:S(2)}) %copy-start.2) | copy-done | bytes 65560
  1.5 0.7 %copy-done.4 = s32[1,32]{1,0:T(1,128)S(1)} copy-done((s32[1,32]{1,0:T(1,128)S(1)}, s32[1,32]{1,0:T(1,128)}, u32[]{:S(2)}) %copy-start.4) | copy-done | bytes 152
  2.1 0.8 %shard_map.95 = bf16[16,24,128]{2,1,0:T(8,128)(2,1)} custom-call(s32[1,32]{1,0:T(1,128)S(1)} %copy-done.4, bf16[1,64,512]{2,1,0:T(8,128)(2,1)S(1)} %copy-done.2), custom_call_target="tpu_custom_call" | custom-call | tf_op jit(solution)/shard_map/pallas_call | solution.py:352
  3.0 8.3 %all-to-all-start = ((bf16[16,24,128]{2,1,0:T(8,128)(2,1)}), bf16[16,24,128]{2,1,0:T(8,128)(2,1)S(1)}, u32[]{:S(2)}, u32[]{:S(2)}) async-start(bf16[16,24,128]{2,1,0:T(8,128)(2,1)} %shard_map.95), calls=%async_computation | async-start | bytes 196608 | tf_op jit(solution)/shard_map/all_to_all | solution.py:358
  11.3 0.0 copy-start.5
  11.3 0.9 %copy-done.5 = bf16[27,32,32]{2,1,0:T(8,128)(2,1)S(1)} copy-done((bf16[27,32,32]{2,1,0:T(8,128)(2,1)S(1)}, bf16[27,32,32]{2,1,0:T(8,128)(2,1)}, u32[]{:S(2)}) %copy-start.5) | copy-done | bytes 55320
  12.2 0.6 shard_map.96.band_ref
  12.8 0.0 copy-start.6
  12.9 6.1 %all-to-all-done.received_ref = bf16[16,24,128]{2,1,0:T(8,128)(2,1)S(1)} async-done(((bf16[16,24,128]{2,1,0:T(8,128)(2,1)}), bf16[16,24,128]{2,1,0:T(8,128)(2,1)S(1)}, u32[]{:S(2)}, u32[]{:S(2)}) %all-to-all-start) | async-done | bytes 98336 | tf_op jit(solution)/shard_map/all_to_all | solution.py:358
  19.0 0.0 copy-done
  19.0 0.0 copy-done.1
  19.0 1.8 %shard_map.97 = (bf16[128,256]{1,0:T(8,128)(2,1)S(1)}, f32[128,256]{1,0:T(8,128)S(1)}, bf16[128,256]{1,0:T(8,128)(2,1)S(1)}, bf16[480,384]{1,0:T(8,128)(2,1)S(1)...) custom-call(s32[1,2,6]{2,1,0:T(2,128)S(1)} %copy-done.3, bf16[16,24,128]{2,1,0:T(8,128)(2,1)S(1)} %all-to-all-done.received_ref, ...), custom_call_target="tpu_custom_call" | custom-call | tf_op jit(solution)/shard_map/pallas_call | solution.py:366
  20.8 2.9 %collective-permute-start = (bf16[96,256]{1,0:T(8,128)(2,1)S(1)}, bf16[96,256]{1,0:T(8,128)(2,1)S(1)}, u32[]{:S(2)}, u32[]{:S(2)}) collective-permute-start(bf16[96,256]{1,0:T(8,128)(2,1)S(1)} %get-tuple-element.21.high_own), channel_id=1, source_target_pairs={{0,2},{2,4},{4,6},{6,8},{8,10},{10,12},{12,14},{14,16},{16,18},{18... | collective-permute-start | bytes 147464 | tf_op jit(solution)/shard_map/ppermute | solution.py:337
  23.6 1.3 %collective-permute-start.1 = (bf16[96,256]{1,0:T(8,128)(2,1)S(1)}, bf16[96,256]{1,0:T(8,128)(2,1)S(1)}, u32[]{:S(2)}, u32[]{:S(2)}) collective-permute-start(bf16[96,256]{1,0:T(8,128)(2,1)S(1)} %get-tuple-element.22.low_own), channel_id=1, source_target_pairs={{2,0},{4,2},{6,4},{8,6},{10,8},{12,10},{14,12},{16,14},{18,16},{20... | collective-permute-start | bytes 147464 | tf_op jit(solution)/shard_map/ppermute | solution.py:337
  24.9 0.0 copy-done.6
  24.9 1.0 %shard_map.94 = (bf16[9,384,256]{2,1,0:T(8,128)(2,1)S(1)}, bf16[9,384,256]{2,1,0:T(8,128)(2,1)S(1)}) custom-call(bf16[27,32,32]{2,1,0:T(8,128)(2,1)S(1)} %copy-done.6), custom_call_target="tpu_custom_call" | custom-call | flops 1000000000 | bytes 2000000 | tf_op jit(solution)/shard_map/pallas_call | solution.py:362
  25.9 0.0 collective-permute-done.high_left
  26.0 3.7 %collective-permute-done.1.low_right = bf16[96,256]{1,0:T(8,128)(2,1)S(1)} collective-permute-done((bf16[96,256]{1,0:T(8,128)(2,1)S(1)}, bf16[96,256]{1,0:T(8,128)(2,1)S(1)}, u32[]{:S(2)}, u32[]{:S(2)}) %collective-permute-start.1) | collective-permute-done | bytes 49184 | tf_op jit(solution)/shard_map/ppermute | solution.py:337
  29.6 3.2 %shard_map.98 = (bf16[1,2,8,8,256]{4,3,2,1,0:T(8,128)(2,1)}, bf16[8,56,128]{2,1,0:T(8,128)(2,1)S(1)}) custom-call(s32[1,2,6]{2,1,0:T(2,128)S(1)} %copy-done.3, bf16[1,2,8,8,256]{4,3,2,1,0:T(8,128)(2,1)S(1)} %copy-done, bf16[9,384,256]{2,1,0:T(8,128)(2,1)S(1)} %get-tuple-element.15.band_ref, bf16[9,384,256]{2,1,0:T(8,128)(2,1)S(1)} %get-tuple-element.16.back_ref, ...), custom_call_target="tpu_custom_call" | custom-call | tf_op jit(solution)/shard_map/pallas_call | solution.py:392
  32.8 10.3 %all_to_all.20.parts_ref = bf16[8,56,128]{2,1,0:T(8,128)(2,1)S(1)} all-to-all(bf16[8,56,128]{2,1,0:T(8,128)(2,1)S(1)} %get-tuple-element.24), channel_id=1, replica_groups={{0,1,2,3,4,5,6,7},{8,9,10,11,12,13,14,15},{16,17,18,19,20,21,22,23},{24..., dimensions={0} | all-to-all | bytes 229376 | tf_op jit(solution)/shard_map/all_to_all | solution.py:341
  43.2 8.1 %all_to_all.21.parts_ref = bf16[4,56,128]{2,1,0:T(8,128)(2,1)S(1)} all-to-all(bf16[4,56,128]{2,1,0:T(8,128)(2,1)S(1)} %shard_map.99), channel_id=1, replica_groups={{0,8,16,24},{1,9,17,25},{2,10,18,26},{3,11,19,27},{4,12,20,28},{5,13,21..., dimensions={0} | all-to-all | bytes 114688 | tf_op jit(solution)/shard_map/all_to_all | solution.py:341
  51.3 7.7 %all_to_all.22.sums_ref = bf16[8,56,128]{2,1,0:T(8,128)(2,1)S(1)} all-to-all(bf16[8,56,128]{2,1,0:T(8,128)(2,1)S(1)} %shard_map.100), channel_id=1, replica_groups={{0,1,2,3,4,5,6,7},{8,9,10,11,12,13,14,15},{16,17,18,19,20,21,22,23},{24..., dimensions={0} | all-to-all | bytes 229376 | tf_op jit(solution)/shard_map/all_to_all | solution.py:341
  59.0 1.0 %shard_map.101 = (f32[27,32,32]{2,1,0:T(8,128)}, f32[27,32,32]{2,1,0:T(8,128)}) custom-call(bf16[8,56,128]{2,1,0:T(8,128)(2,1)S(1)} %all_to_all.22.sums_ref), custom_call_target="tpu_custom_call" | custom-call | tf_op jit(solution)/shard_map/pallas_call | solution.py:420
  (7 shorter events, 0.0 us)
Async XLA Ops:
  0.6 0.8 %copy-start.2 = (bf16[1,64,512]{2,1,0:T(8,128)(2,1)S(1)}, bf16[1,64,512]{2,1,0:T(8,128)(2,1)}, u32[]{:S(2)}) copy-start(bf16[1,64,512]{2,1,0:T(8,128)(2,1)} %latents_ref.1) | copy-start | bytes 196612
  1.5 0.7 %copy-start.4 = (s32[1,32]{1,0:T(1,128)S(1)}, s32[1,32]{1,0:T(1,128)}, u32[]{:S(2)}) copy-start(s32[1,32]{1,0:T(1,128)} %ids_ref.1) | copy-start | bytes 388
  3.0 16.0 %all-to-all-start = ((bf16[16,24,128]{2,1,0:T(8,128)(2,1)}), bf16[16,24,128]{2,1,0:T(8,128)(2,1)S(1)}, u32[]{:S(2)}, u32[]{:S(2)}) async-start(bf16[16,24,128]{2,1,0:T(8,128)(2,1)} %shard_map.95), calls=%async_computation | async-start | bytes 196608 | tf_op jit(solution)/shard_map/all_to_all | solution.py:358
  11.3 0.9 %copy-start.5 = (bf16[27,32,32]{2,1,0:T(8,128)(2,1)S(1)}, bf16[27,32,32]{2,1,0:T(8,128)(2,1)}, u32[]{:S(2)}) copy-start(bf16[27,32,32]{2,1,0:T(8,128)(2,1)} %weights_ref.3) | copy-start | bytes 165892
  12.2 6.7 %copy-start = (bf16[1,2,8,8,256]{4,3,2,1,0:T(8,128)(2,1)S(1)}, bf16[1,2,8,8,256]{4,3,2,1,0:T(8,128)(2,1)}, u32[]{:S(2)}) copy-start(bf16[1,2,8,8,256]{4,3,2,1,0:T(8,128)(2,1)} %cotangent_ref.3) | copy-start | bytes 196612
  12.2 6.7 %copy-start.1 = (bf16[64,2048]{1,0:T(8,128)(2,1)S(1)}, bf16[64,2048]{1,0:T(8,128)(2,1)}, u32[]{:S(2)}) copy-start(bf16[64,2048]{1,0:T(8,128)(2,1)} %up_ref.1) | copy-start | bytes 786436
  12.2 6.7 %copy-start.3 = (s32[1,2,6]{2,1,0:T(2,128)S(1)}, s32[1,2,6]{2,1,0:T(2,128)}, u32[]{:S(2)}) copy-start(s32[1,2,6]{2,1,0:T(2,128)} %links_ref.3) | copy-start | bytes 148
  12.8 12.1 %copy-start.6 = (bf16[27,32,32]{2,1,0:T(8,128)(2,1)S(1)}, bf16[27,32,32]{2,1,0:T(8,128)(2,1)}, u32[]{:S(2)}) copy-start(bf16[27,32,32]{2,1,0:T(8,128)(2,1)} %weights_ref.2) | copy-start | bytes 165892
  20.8 5.2 %collective-permute-start = (bf16[96,256]{1,0:T(8,128)(2,1)S(1)}, bf16[96,256]{1,0:T(8,128)(2,1)S(1)}, u32[]{:S(2)}, u32[]{:S(2)}) collective-permute-start(bf16[96,256]{1,0:T(8,128)(2,1)S(1)} %get-tuple-element.21.high_own), channel_id=1, source_target_pairs={{0,2},{2,4},{4,6},{6,8},{8,10},{10,12},{12,14},{14,16},{16,18},{18... | collective-permute-start | bytes 147464 | tf_op jit(solution)/shard_map/ppermute | solution.py:337
  23.6 6.0 %collective-permute-start.1 = (bf16[96,256]{1,0:T(8,128)(2,1)S(1)}, bf16[96,256]{1,0:T(8,128)(2,1)S(1)}, u32[]{:S(2)}, u32[]{:S(2)}) collective-permute-start(bf16[96,256]{1,0:T(8,128)(2,1)S(1)} %get-tuple-element.22.low_own), channel_id=1, source_target_pairs={{2,0},{4,2},{6,4},{8,6},{10,8},{12,10},{14,12},{16,14},{18,16},{20... | collective-permute-start | bytes 147464 | tf_op jit(solution)/shard_map/ppermute | solution.py:337

commit v4 on v2

--- a/solution.py
+++ b/solution.py
@@ -38,11 +38,7 @@
     return lax.broadcasted_iota(jnp.int32, shape, len(shape) - 1)
 
 
-def pick_kernel(devices, ids_hbm, latents_hbm, out_ref, ids_ref, latents_ref, rows_ref, sems):
-    ids_copy = pltpu.make_async_copy(ids_hbm, ids_ref, sems.at[0])
-    latents_copy = pltpu.make_async_copy(latents_hbm, latents_ref, sems.at[1])
-    ids_copy.start()
-    latents_copy.start()
+def pick_kernel(devices, ids_ref, latents_ref, out_ref, rows_ref):
     held, width = latents_ref.shape[1:]
     bricks = ids_ref.shape[1]
     margin = 8 * width // 128
@@ -51,9 +47,7 @@
     rows_ref[margin + bricks * tiles :] = jnp.zeros((margin, 128), F32)
     first = lax.axis_index("space") * held
     rows = lax.broadcasted_iota(jnp.int32, (held, bricks), 0) + first
-    ids_copy.wait()
     hot = jnp.where(rows == ids_ref[...], 1.0, 0.0).astype(BF16)
-    latents_copy.wait()
     picked = dot_rows(hot, latents_ref[0])
     for tile in range(tiles):
         rows_ref[pl.ds(margin + tile, bricks, stride=tiles), :] = picked[:, tile * 128 : tile * 128 + 128]
@@ -88,14 +82,13 @@
     return jnp.concatenate(pieces, axis=0).astype(BF16)
 
 
-def band_kernel(weights_ref, band_ref):
-    build_band(band_ref, weight_rows(weights_ref[...].astype(F32)))
-
-
-def two_bands_kernel(weights_ref, band_ref, back_ref):
-    weights = weights_ref[...].astype(F32)
-    build_band(band_ref, weight_rows(weights))
-    build_band(back_ref, flipped_rows(weights))
+def first_bands_kernel(one_ref, two_ref, band_ref, back_ref):
+    build_band(band_ref, weight_rows(one_ref[...].astype(F32)))
+    build_band(back_ref, flipped_rows(two_ref[...].astype(F32)))
+
+
+def last_band_kernel(two_ref, band_ref):
+    build_band(band_ref, weight_rows(two_ref[...].astype(F32)))
 
 
 def put_padded(pad_ref, brick, volume, x_low, x_high, y_low, y_high, z_low, z_high):
@@ -153,10 +146,83 @@
     return jnp.concatenate(pieces, axis=0).reshape(EDGE, EDGE, 128)
 
 
+def put_lines(halves_ref, values):
+    for half in range(2):
+        halves_ref[half] = values[:, half * 128 : half * 128 + 128]
+
+
+def pack_both(halves_ref, high_ref, low_ref, high_out, low_out):
+    for brick in range(BRICKS):
+        pack_faces(high_ref, brick * FACE, halves_ref, brick * CUBE, True)
+        pack_faces(low_ref, brick * FACE, halves_ref, brick * CUBE, False)
+    high_out[...] = high_ref[...].astype(BF16)
+    low_out[...] = low_ref[...].astype(BF16)
+
+
+def fill_pools(high_ref, low_ref, high_own, low_own, high_left, low_right):
+    half = BRICKS * FACE
+    high_ref[0:half] = high_left[...].astype(F32)
+    high_ref[half:] = high_own[...].astype(F32)
+    low_ref[0:half] = low_own[...].astype(F32)
+    low_ref[half:] = low_right[...].astype(F32)
+
+
+def padded_brick(pad_ref, brick, values, links_ref, high_ref, low_ref):
+    position = lax.axis_index("space")
+
+    def rows(face, axis):
+        link = links_ref[0, brick, face]
+        high = face % 2 == 0
+        index = jnp.clip(link - BRICKS * (position - 1 if high else position), 0, 2 * BRICKS - 1)
+        pool = high_ref if high else low_ref
+        present = jnp.where(link >= 0, 1.0, 0.0).astype(F32)
+        return pool[pl.ds(pl.multiple_of(index * FACE + axis * EDGE, 8), EDGE), :] * present
+
+    volume = values[brick * CUBE : brick * CUBE + CUBE].reshape(EDGE, EDGE, LINE)
+    put_padded(
+        pad_ref, brick, volume, rows(0, 0), rows(1, 0), rows(2, 1), rows(3, 1),
+        unpack_depth(rows(4, 2), True), unpack_depth(rows(5, 2), False),
+    )
+
+
+def faces_kernel(cotangent_ref, high_out, low_out, halves_ref, high_ref, low_ref):
+    put_lines(halves_ref, cotangent_ref[...].astype(F32).reshape(LINES, LINE))
+    pack_both(halves_ref, high_ref, low_ref, high_out, low_out)
+
+
+def fold(outer_ref, places):
+    lane = lanes_of((CHANNELS, 128)) // CHANNELS
+    folded = None
+    for turn in range(2):
+        picked = None
+        for block in range(4):
+            start, tile = places[block][turn]
+            rows = outer_ref[start : start + CHANNELS, tile * 128 : tile * 128 + 128]
+            picked = rows if picked is None else jnp.where(lane == block, rows, picked)
+        folded = picked if folded is None else folded + picked
+    quarter = [folded[8 * q : 8 * q + 8] for q in range(4)]
+    small = lanes_of((8, 128)) // CHANNELS
+    total = None
+    for turn in range(4):
+        mixed = quarter[0]
+        for q in range(1, 4):
+            mixed = jnp.where(small == (q + turn) % 4, quarter[q], mixed)
+        if turn:
+            mixed = pltpu.roll(mixed, 128 - turn * CHANNELS, 1)
+        total = mixed if total is None else total + mixed
+    return total
+
+
+def wide_start(z):
+    return z * CHANNELS if 0 <= z < EDGE else (LINE if z == EDGE else WIDE - CHANNELS)
+
+
 def first_kernel(
-    links_ref, received_ref, up_ref, band_ref, cotangent_ref,
-    lifted_out, pre_out, hidden_out, pad_out, high_out, low_out,
-    volumes_ref, pad_ref, lines_ref, high_ref, low_ref, rows_ref,
+    links_ref, received_ref, up_ref, band_ref, back_ref, cotangent_ref,
+    high_own, low_own, high_left, low_right,
+    lifted_out, hidden_out, high_out, low_out, sums_out,
+    volumes_ref, lifted_pad, cotangent_pad, halves_ref, high_ref, low_ref, high_pool, low_pool,
+    rows_ref, wide_ref, tall_ref, sums_ref,
 ):
     position = lax.axis_index("space")
     tiles = received_ref.shape[1] // (3 * BRICKS)
@@ -200,109 +266,49 @@
         own = (BRICKS + brick) * CUBE
         volume = lines(volumes_ref, own, CUBE).reshape(EDGE, EDGE, LINE)
         put_padded(
-            pad_ref, brick, volume, x_face(0), x_face(1), y_face(2), y_face(3), z_face(4), z_face(5)
+            lifted_pad, brick, volume, x_face(0), x_face(1), y_face(2), y_face(3), z_face(4), z_face(5)
         )
-    pre = convolve(pad_ref, band_ref)
-    hidden = pre / (1.0 + jnp.exp(-pre))
-    hidden = hidden.astype(BF16)
+    pre = convolve(lifted_pad, band_ref)
+    sigmoid = 1.0 / (1.0 + jnp.exp(-pre))
+    hidden = (pre / (1.0 + jnp.exp(-pre))).astype(BF16)
     lifted_out[...] = lines(volumes_ref, BRICKS * CUBE, LINES).astype(BF16)
-    pre_out[...] = pre
     hidden_out[...] = hidden
-    pad_out[...] = pad_ref[...].reshape(pad_out.shape).astype(BF16)
-    sources = (hidden.astype(F32), cotangent_ref[...].astype(F32).reshape(LINES, LINE))
-    for which, values in enumerate(sources):
-        for half in range(2):
-            lines_ref[half, which * LINES : which * LINES + LINES] = values[:, half * 128 : half * 128 + 128]
-    for which in range(2):
-        for brick in range(BRICKS):
-            base = (which * BRICKS + brick) * FACE
-            start = which * LINES + brick * CUBE
-            pack_faces(high_ref, base, lines_ref, start, True)
-            pack_faces(low_ref, base, lines_ref, start, False)
-    high_out[...] = high_ref[...].astype(BF16)
-    low_out[...] = low_ref[...].astype(BF16)
-
-
-def fold_diagonals(outer_ref, part):
-    lane = lanes_of((CHANNELS, 128)) // CHANNELS
-    folded = None
-    for half in range(2):
-        picked = None
-        for block in range(4):
-            depth = 4 * half + block + part - 1
-            start = depth * CHANNELS if 0 <= depth < EDGE else (LINE if depth == EDGE else WIDE - CHANNELS)
-            rows = outer_ref[start : start + CHANNELS, half * 128 : half * 128 + 128]
-            picked = rows if picked is None else jnp.where(lane == block, rows, picked)
-        folded = picked if folded is None else folded + picked
-    quarter = [folded[8 * q : 8 * q + 8] for q in range(4)]
-    small = lanes_of((8, 128)) // CHANNELS
-    total = None
-    for turn in range(4):
-        mixed = quarter[0]
-        for q in range(1, 4):
-            mixed = jnp.where(small == (q + turn) % 4, quarter[q], mixed)
-        if turn:
-            mixed = pltpu.roll(mixed, 128 - turn * CHANNELS, 1)
-        total = mixed if total is None else total + mixed
-    return total
-
-
-def padded_brick(pad_ref, brick, which, values, links_ref, high_ref, low_ref):
-    position = lax.axis_index("space")
-    half = high_ref.shape[0] // 2
-
-    def rows(face, axis):
-        link = links_ref[0, brick, face]
-        high = face % 2 == 0
-        index = jnp.clip(link - BRICKS * (position - 1 if high else position), 0, 2 * BRICKS - 1)
-        start = (index // BRICKS) * half + (which * BRICKS + index % BRICKS) * FACE + axis * EDGE
-        pool = high_ref if high else low_ref
-        present = jnp.where(link >= 0, 1.0, 0.0).astype(F32)
-        return pool[pl.ds(pl.multiple_of(start, 8), EDGE), :] * present
-
-    volume = values[brick * CUBE : brick * CUBE + CUBE].reshape(EDGE, EDGE, LINE)
-    put_padded(
-        pad_ref, brick, volume, rows(0, 0), rows(1, 0), rows(2, 1), rows(3, 1),
-        unpack_depth(rows(4, 2), True), unpack_depth(rows(5, 2), False),
-    )
-
-
-def fill_pools(high_ref, low_ref, high_own, low_own, high_left, low_right):
-    half = 2 * BRICKS * FACE
-    high_ref[0:half] = high_left[...].astype(F32)
-    high_ref[half:] = high_own[...].astype(F32)
-    low_ref[0:half] = low_own[...].astype(F32)
-    low_ref[half:] = low_right[...].astype(F32)
-
-
-def second_kernel(
-    links_ref, cotangent_ref, band_ref, back_ref, lifted_ref, pre_ref, hidden_ref, pad_in,
-    high_own, low_own, high_left, low_right,
-    fine_out, sums_out,
-    high_ref, low_ref, hidden_pad, cotangent_pad, lifted_pad, outer_ref, sums_ref,
+    put_lines(halves_ref, hidden.astype(F32))
+    pack_both(halves_ref, high_ref, low_ref, high_out, low_out)
+    fill_pools(high_pool, low_pool, high_own, low_own, high_left, low_right)
+    cotangent = cotangent_ref[...].astype(F32).reshape(LINES, LINE)
+    for brick in range(BRICKS):
+        padded_brick(cotangent_pad, brick, cotangent, links_ref, high_pool, low_pool)
+    back = convolve(cotangent_pad, back_ref)
+    gradient = (back * sigmoid * (1.0 + pre * (1.0 - sigmoid))).astype(BF16)
+    sums_ref[8 * BLOCKS :] = jnp.zeros((sums_ref.shape[0] - 8 * BLOCKS, 128), F32)
+    for k in range(9):
+        tall_ref[...] = dot_rows(window(lifted_pad, k), gradient)
+        for part in range(3):
+            places = [[(wide_start(4 * t + b + part - 1), t) for t in range(2)] for b in range(4)]
+            start = 8 * (3 * k + part)
+            sums_ref[start : start + 8] = fold(tall_ref, places)
+        wide_ref[...] = dot_rows(hidden, window(cotangent_pad, 8 - k))
+        for part in range(3):
+            places = [[], [], [], []]
+            for z in range(EDGE):
+                other = z + 1 - part
+                places[other % 4].append((z * CHANNELS, wide_start(other) // 128))
+            start = 8 * (27 + 3 * k + part)
+            sums_ref[start : start + 8] = fold(wide_ref, places)
+    sums_out[...] = sums_ref[...].astype(BF16).reshape(sums_out.shape)
+
+
+def fine_kernel(
+    links_ref, band_ref, lifted_ref, hidden_ref, high_own, low_own, high_left, low_right,
+    fine_out, hidden_pad, high_pool, low_pool,
 ):
-    fill_pools(high_ref, low_ref, high_own, low_own, high_left, low_right)
-    lifted_pad[...] = pad_in[...].astype(F32).reshape(lifted_pad.shape)
-    cotangent = cotangent_ref[...].astype(F32).reshape(LINES, LINE)
+    fill_pools(high_pool, low_pool, high_own, low_own, high_left, low_right)
     hidden = hidden_ref[...].astype(F32)
-    for which, values, pad_ref in ((0, hidden, hidden_pad), (1, cotangent, cotangent_pad)):
-        for brick in range(BRICKS):
-            padded_brick(pad_ref, brick, which, values, links_ref, high_ref, low_ref)
+    for brick in range(BRICKS):
+        padded_brick(hidden_pad, brick, hidden, links_ref, high_pool, low_pool)
     fine = lifted_ref[...].astype(F32) + convolve(hidden_pad, band_ref)
     fine_out[...] = fine.astype(BF16).reshape(fine_out.shape)
-    back = convolve(cotangent_pad, back_ref)
-    pre = pre_ref[...]
-    sigmoid = 1.0 / (1.0 + jnp.exp(-pre))
-    gradient = (back * sigmoid * (1.0 + pre * (1.0 - sigmoid))).astype(BF16)
-    upstream = cotangent.astype(BF16)
-    sums_ref[8 * BLOCKS :] = jnp.zeros((sums_ref.shape[0] - 8 * BLOCKS, 128), F32)
-    for base, pad_ref, right in ((0, lifted_pad, gradient), (27, hidden_pad, upstream)):
-        for k in range(9):
-            outer_ref[...] = dot_rows(window(pad_ref, k), right)
-            for part in range(3):
-                start = 8 * (base + 3 * k + part)
-                sums_ref[start : start + 8] = fold_diagonals(outer_ref, part)
-    sums_out[...] = sums_ref[...].astype(BF16).reshape(sums_out.shape)
 
 
 def sum_kernel(scale, parts_ref, out_ref):
@@ -320,8 +326,8 @@
             out[index % 27, 8 * q : 8 * q + 8, :] = moved[:, :CHANNELS]
 
 
-def call(kernel, out_shape, scratch=(), smem=(), hbm=(), inputs=1, limit=24, cost=None):
-    spaces = [pltpu.SMEM if i in smem else pltpu.HBM if i in hbm else pltpu.VMEM for i in range(inputs)]
+def call(kernel, out_shape, scratch=(), smem=(), inputs=1, limit=24, cost=None):
+    spaces = [pltpu.SMEM if i in smem else pltpu.VMEM for i in range(inputs)]
     return pl.pallas_call(
         kernel,
         out_shape=out_shape,
@@ -346,71 +352,50 @@
 def body(coarse_latents, active_blocks, face_links, cotangent, up_weight, conv_one, conv_two):
     devices = lax.axis_size("space")
     everyone = devices * lax.axis_size("dp")
-    held, width = coarse_latents.shape[1:]
+    width = coarse_latents.shape[2]
     bricks = active_blocks.shape[1]
     tiles = width // 128
     packed = call(
         functools.partial(pick_kernel, devices),
         shape(devices, 3 * BRICKS * tiles, 128),
-        [
-            pltpu.VMEM((1, bricks), jnp.int32),
-            pltpu.VMEM((1, held, width), BF16),
-            pltpu.VMEM(((bricks + 16) * tiles, 128), F32),
-            pltpu.SemaphoreType.DMA((2,)),
-        ],
-        hbm=(0, 1),
+        [pltpu.VMEM(((bricks + 16) * tiles, 128), F32)],
         inputs=2,
     )(active_blocks, coarse_latents)
     received = lax.all_to_all(packed, "space", split_axis=0, concat_axis=0, tiled=True)
     band = shape(9, WIDE, LINE)
     cost = pl.CostEstimate(flops=10**9, bytes_accessed=2 * 10**6, transcendentals=0)
-    band_one = call(band_kernel, band, cost=cost)(conv_one)
-    band_two, band_back = call(two_bands_kernel, (band, band), cost=cost)(conv_two)
-    pad_shape = (3, BRICKS, EDGE + 2, EDGE, WIDE)
-    pad = pltpu.VMEM(pad_shape, F32)
-    packed_faces = 2 * BRICKS * FACE
-    lifted, pre, hidden, lifted_pad, high, low = call(
-        first_kernel,
-        (
-            shape(LINES, LINE),
-            shape(LINES, LINE, dtype=F32),
-            shape(LINES, LINE),
-            shape(math.prod(pad_shape[:-1]), WIDE),
-            shape(packed_faces, LINE),
-            shape(packed_faces, LINE),
-        ),
-        [
-            pltpu.VMEM((2, 8 * CUBE, 128), F32),
-            pad,
-            pltpu.VMEM((2, 2 * LINES, 128), F32),
-            pltpu.VMEM((packed_faces, LINE), F32),
-            pltpu.VMEM((packed_faces, LINE), F32),
-            pltpu.VMEM((8 * tiles, 128), F32),
-        ],
-        smem=(0,),
-        inputs=5,
-    )(face_links, received, up_weight, band_one, cotangent)
+    face = shape(BRICKS * FACE, LINE)
+    halves = pltpu.VMEM((2, LINES, 128), F32)
+    faces = pltpu.VMEM((BRICKS * FACE, LINE), F32)
+    pool = pltpu.VMEM((2 * BRICKS * FACE, LINE), F32)
+    pad = pltpu.VMEM((3, BRICKS, EDGE + 2, EDGE, WIDE), F32)
+    volume = shape(LINES, LINE)
+    per = -(-BLOCKS // everyone)
+    per += per % 2
+    high, low = call(faces_kernel, (face, face), [halves, faces, faces])(cotangent)
     high_left = passed_along(high, "space", 1)
     low_right = passed_along(low, "space", -1)
-    per = -(-BLOCKS // everyone)
-    per += per % 2
-    fine, sums = call(
-        second_kernel,
-        (shape(*cotangent.shape), shape(everyone, per * 8, 128)),
+    band_one, band_back = call(first_bands_kernel, (band, band), inputs=2, cost=cost)(conv_one, conv_two)
+    lifted, hidden, hidden_high, hidden_low, sums = call(
+        first_kernel,
+        (volume, volume, face, face, shape(everyone, per * 8, 128)),
         [
-            pltpu.VMEM((2 * packed_faces, LINE), F32),
-            pltpu.VMEM((2 * packed_faces, LINE), F32),
-            pad,
-            pad,
-            pad,
+            pltpu.VMEM((2, 8 * CUBE, 128), F32), pad, pad, halves, faces, faces, pool, pool,
+            pltpu.VMEM((8 * tiles, 128), F32),
+            pltpu.VMEM((LINE, WIDE), F32),
             pltpu.VMEM((WIDE, LINE), F32),
             pltpu.VMEM((everyone * per * 8, 128), F32),
         ],
         smem=(0,),
-        inputs=12,
+        inputs=10,
     )(
-        face_links, cotangent, band_two, band_back, lifted, pre, hidden, lifted_pad,
-        high, low, high_left, low_right,
+        face_links, received, up_weight, band_one, band_back, cotangent, high, low, high_left, low_right
+    )
+    hidden_left = passed_along(hidden_high, "space", 1)
+    hidden_right = passed_along(hidden_low, "space", -1)
+    band_two = call(last_band_kernel, band, cost=cost)(conv_two)
+    fine = call(fine_kernel, shape(*cotangent.shape), [pad, pool, pool], smem=(0,), inputs=8, cost=cost)(
+        face_links, band_two, lifted, hidden, hidden_high, hidden_low, hidden_left, hidden_right
     )
     axes = ("space", "dp")
     parts = lax.all_to_all(sums, axes, split_axis=0, concat_axis=0, tiled=True)

time: 57.1 us -> 61.9 us (1.084)
  the two profiles are of different devices: /device:TPU:0 before, /device:TPU:6 now
where the time goes in v4:
time: 61.9 us; the launch traced here: 61 us
  starting transfers between devices  23.2 us (37%)
  local copies, waits for them, and re-layouts  11.1 us (18%)
  blocking collectives  11.1 us (18%)
  Pallas kernels  9.54 us (15%)
  waiting for transfers between devices  5.24 us (8%)
  between operations  0.85 us (1%)
    ppermute x4, starting transfers between devices, passed_along(): lax.ppermute(value, axis, [(source, source + steps) for source in range(f...  11.7 us
    unnamed x50, local copies, waits for them, and re-layouts  11.1 us
    all_to_all x1, blocking collectives, body(): parts = lax.all_to_all(sums, axes, split_axis=0, concat_axis=0, tiled=True)  11.1 us
    all_to_all x1, starting transfers between devices, body(): lax.all_to_all(packed, 'space', split_axis=0, concat_axis=0, tiled=True)  7.25 us
    ppermute x4, waiting for transfers between devices, passed_along(): lax.ppermute(value, axis, [(source, source + steps) for source in range(f...  5.24 us
    all_to_all x1, starting transfers between devices, body(): lax.all_to_all(total, axes, split_axis=0, concat_axis=0, tiled=True)  4.27 us
    pallas_call x1, Pallas kernels, body(): call(first_kernel, (volume, volume, face, face, shape(everyone, per * 8,...  3.57 us
    pallas_call x1, Pallas kernels, body(): call(fine_kernel, shape(*cotangent.shape), [pad, pool, pool], smem=(0,),...  1.72 us
  transfers between devices with their start and end apart: 6, of which 2 were waited for; matrix products, arithmetic and copies ran while one was open for 0% of the time, Pallas kernels for 6%

profile of v4, /device:TPU:6, one launch (start us, length us, event | category | flops | bytes accessed | tf_op | source)
XLA Modules:
  0.0 61.0 jit_solution(17382549665886844114)
XLA Ops:
  0.6 0.8 %copy-done.3 = bf16[1,64,512]{2,1,0:T(8,128)(2,1)S(1)} copy-done((bf16[1,64,512]{2,1,0:T(8,128)(2,1)S(1)}, bf16[1,64,512]{2,1,0:T(8,128)(2,1)}, u32[]{:S(2)}) %copy-start.3) | copy-done | bytes 65560
  2.1 0.8 %shard_map.95 = bf16[16,24,128]{2,1,0:T(8,128)(2,1)} custom-call(s32[1,32]{1,0:T(1,128)S(1)} %copy-done.13, bf16[1,64,512]{2,1,0:T(8,128)(2,1)S(1)} %copy-done.3), custom_call_target="tpu_custom_call" | custom-call | tf_op jit(solution)/shard_map/pallas_call | solution.py:358
  3.0 7.3 %all-to-all-start = ((bf16[16,24,128]{2,1,0:T(8,128)(2,1)}), bf16[16,24,128]{2,1,0:T(8,128)(2,1)}, u32[]{:S(2)}, u32[]{:S(2)}) async-start(bf16[16,24,128]{2,1,0:T(8,128)(2,1)} %shard_map.95), calls=%async_computation | async-start | bytes 196608 | tf_op jit(solution)/shard_map/all_to_all | solution.py:364
  10.2 0.8 %copy-done = bf16[1,2,8,8,256]{4,3,2,1,0:T(8,128)(2,1)S(1)} copy-done((bf16[1,2,8,8,256]{4,3,2,1,0:T(8,128)(2,1)S(1)}, bf16[1,2,8,8,256]{4,3,2,1,0:T(8,128)(2,1)}, u32[]{:S(2)}) %copy-start) | copy-done | bytes 65560
  11.2 3.4 %collective-permute-start = (bf16[48,256]{1,0:T(8,128)(2,1)S(1)}, bf16[48,256]{1,0:T(8,128)(2,1)S(1)}, u32[]{:S(2)}, u32[]{:S(2)}) collective-permute-start(bf16[48,256]{1,0:T(8,128)(2,1)S(1)} %get-tuple-element.16.high_own), channel_id=1, source_target_pairs={{0,2},{2,4},{4,6},{6,8},{8,10},{10,12},{12,14},{14,16},{16,18},{18... | collective-permute-start | bytes 73736 | tf_op jit(solution)/shard_map/ppermute | solution.py:349
  14.6 2.5 %collective-permute-start.1 = (bf16[48,256]{1,0:T(8,128)(2,1)S(1)}, bf16[48,256]{1,0:T(8,128)(2,1)S(1)}, u32[]{:S(2)}, u32[]{:S(2)}) collective-permute-start(bf16[48,256]{1,0:T(8,128)(2,1)S(1)} %get-tuple-element.17.low_own), channel_id=1, source_target_pairs={{2,0},{4,2},{6,4},{8,6},{10,8},{12,10},{14,12},{16,14},{18,16},{20... | collective-permute-start | bytes 73736 | tf_op jit(solution)/shard_map/ppermute | solution.py:349
  17.1 0.9 %copy-done.14 = bf16[27,32,32]{2,1,0:T(8,128)(2,1)S(1)} copy-done((bf16[27,32,32]{2,1,0:T(8,128)(2,1)S(1)}, bf16[27,32,32]{2,1,0:T(8,128)(2,1)}, u32[]{:S(2)}) %copy-start.14) | copy-done | bytes 55320
  18.0 0.9 %copy-done.15 = bf16[27,32,32]{2,1,0:T(8,128)(2,1)S(1)} copy-done((bf16[27,32,32]{2,1,0:T(8,128)(2,1)S(1)}, bf16[27,32,32]{2,1,0:T(8,128)(2,1)}, u32[]{:S(2)}) %copy-start.15) | copy-done | bytes 55320
  18.9 1.0 %shard_map.96 = (bf16[9,384,256]{2,1,0:T(8,128)(2,1)S(1)}, bf16[9,384,256]{2,1,0:T(8,128)(2,1)S(1)}) custom-call(bf16[27,32,32]{2,1,0:T(8,128)(2,1)S(1)} %copy-done.14, bf16[27,32,32]{2,1,0:T(8,128)(2,1)S(1)} %copy-done.15), custom_call_target="tpu_custom_call" | custom-call | flops 1000000000 | bytes 2000000 | tf_op jit(solution)/shard_map/pallas_call | solution.py:378
  20.6 1.5 %collective-permute-done.1.low_right = bf16[48,256]{1,0:T(8,128)(2,1)S(1)} collective-permute-done((bf16[48,256]{1,0:T(8,128)(2,1)S(1)}, bf16[48,256]{1,0:T(8,128)(2,1)S(1)}, u32[]{:S(2)}, u32[]{:S(2)}) %collective-permute-start.1) | collective-permute-done | bytes 24608 | tf_op jit(solution)/shard_map/ppermute | solution.py:349
  22.7 0.8 %copy-done.1 = bf16[1,2,8,8,256]{4,3,2,1,0:T(8,128)(2,1)S(1)} copy-done((bf16[1,2,8,8,256]{4,3,2,1,0:T(8,128)(2,1)S(1)}, bf16[1,2,8,8,256]{4,3,2,1,0:T(8,128)(2,1)}, u32[]{:S(2)}) %copy-start.1) | copy-done | bytes 65560
  23.5 0.9 %copy-done.2 = bf16[64,2048]{1,0:T(8,128)(2,1)S(1)} copy-done((bf16[64,2048]{1,0:T(8,128)(2,1)S(1)}, bf16[64,2048]{1,0:T(8,128)(2,1)}, u32[]{:S(2)}) %copy-start.2) | copy-done | bytes 262168
  24.5 0.7 %copy-done.5 = bf16[48,256]{1,0:T(8,128)(2,1)S(1)} copy-done((bf16[48,256]{1,0:T(8,128)(2,1)S(1)}, bf16[48,256]{1,0:T(8,128)(2,1)}, u32[]{:S(2)}) %copy-start.5) | copy-done | bytes 24600
  25.2 0.7 %copy-done.7 = bf16[48,256]{1,0:T(8,128)(2,1)S(1)} copy-done((bf16[48,256]{1,0:T(8,128)(2,1)S(1)}, bf16[48,256]{1,0:T(8,128)(2,1)}, u32[]{:S(2)}) %copy-start.7) | copy-done | bytes 24600
  26.0 0.7 %copy-done.9 = bf16[48,256]{1,0:T(8,128)(2,1)S(1)} copy-done((bf16[48,256]{1,0:T(8,128)(2,1)S(1)}, bf16[48,256]{1,0:T(8,128)(2,1)}, u32[]{:S(2)}) %copy-start.9) | copy-done | bytes 24600
  27.4 3.6 %shard_map.98 = (bf16[128,256]{1,0:T(8,128)(2,1)S(1)}, bf16[128,256]{1,0:T(8,128)(2,1)S(1)}, bf16[48,256]{1,0:T(8,128)(2,1)S(1)}, bf16[48,256]{1,0:T(8,128)(2,1)S(1)}, bf16[32,16,128]{2,1,0:T(8,128)(2,1)S(1)}) custom-call(s32[1,2,6]{2,1,0:T(2,128)S(1)} %copy-done.12, bf16[16,24,128]{2,1,0:T(8,128)(2,1)} %all-to-all-done.received_ref, ...), custom_call_target="tpu_custom_call" | custom-call | tf_op jit(solution)/shard_map/pallas_call | solution.py:379
  31.0 11.1 %all_to_all.15.parts_ref = bf16[32,16,128]{2,1,0:T(8,128)(2,1)S(1)} all-to-all(bf16[32,16,128]{2,1,0:T(8,128)(2,1)S(1)} %get-tuple-element.22), channel_id=1, replica_groups=mesh['space'=16,'dp'=2] {'space','dp'}, dimensions={0} | all-to-all | bytes 262144 | tf_op jit(solution)/shard_map/all_to_all | solution.py:401
  42.8 4.3 %all-to-all-start.2 = ((bf16[32,16,128]{2,1,0:T(8,128)(2,1)}), bf16[32,16,128]{2,1,0:T(8,128)(2,1)S(1)}, u32[]{:S(2)}, u32[]{:S(2)}) async-start(bf16[32,16,128]{2,1,0:T(8,128)(2,1)} %shard_map.100), calls=%async_computation.2 | async-start | bytes 262144 | tf_op jit(solution)/shard_map/all_to_all | solution.py:404
  47.1 3.4 %collective-permute-start.2 = (bf16[48,256]{1,0:T(8,128)(2,1)}, bf16[48,256]{1,0:T(8,128)(2,1)S(1)}, u32[]{:S(2)}, u32[]{:S(2)}) collective-permute-start(bf16[48,256]{1,0:T(8,128)(2,1)} %copy-done.21), channel_id=1, source_target_pairs={{0,2},{2,4},{4,6},{6,8},{8,10},{10,12},{12,14},{14,16},{16,18},{18... | collective-permute-start | bytes 73736 | tf_op jit(solution)/shard_map/ppermute | solution.py:349
  50.5 2.5 %collective-permute-start.3 = (bf16[48,256]{1,0:T(8,128)(2,1)}, bf16[48,256]{1,0:T(8,128)(2,1)S(1)}, u32[]{:S(2)}, u32[]{:S(2)}) collective-permute-start(bf16[48,256]{1,0:T(8,128)(2,1)} %copy-done.23), channel_id=1, source_target_pairs={{2,0},{4,2},{6,4},{8,6},{10,8},{12,10},{14,12},{16,14},{18,16},{20... | collective-permute-start | bytes 73736 | tf_op jit(solution)/shard_map/ppermute | solution.py:349
  53.0 0.9 %copy-done.16 = bf16[27,32,32]{2,1,0:T(8,128)(2,1)S(1)} copy-done((bf16[27,32,32]{2,1,0:T(8,128)(2,1)S(1)}, bf16[27,32,32]{2,1,0:T(8,128)(2,1)}, u32[]{:S(2)}) %copy-start.16) | copy-done | bytes 55320
  54.5 3.7 %collective-permute-done.3.low_right = bf16[48,256]{1,0:T(8,128)(2,1)S(1)} collective-permute-done((bf16[48,256]{1,0:T(8,128)(2,1)}, bf16[48,256]{1,0:T(8,128)(2,1)S(1)}, u32[]{:S(2)}, u32[]{:S(2)}) %collective-permute-start.3) | collective-permute-done | bytes 24608 | tf_op jit(solution)/shard_map/ppermute | solution.py:349
  58.3 1.7 %shard_map.99 = bf16[1,2,8,8,256]{4,3,2,1,0:T(8,128)(2,1)} custom-call(s32[1,2,6]{2,1,0:T(2,128)S(1)} %copy-done.12, bf16[9,384,256]{2,1,0:T(8,128)(2,1)S(1)} %shard_map.94.band_ref, bf16[128,256]{1,0:T(8,128)(2,1)S(1)} %copy-done.18, bf16[128,256]{1,0:T(8,128)(2,1)S(1)} %copy-done.20, bf16[48,256]{1,0:T(8,128)(2,1)S(1)} %copy-done.22, ...), custom_call_target="tpu_custom_call" | custom-call | flops 1000000000 | bytes 2000000 | tf_op jit(solution)/shard_map/pallas_call | solution.py:397
  60.0 1.0 %shard_map.101 = (f32[27,32,32]{2,1,0:T(8,128)}, f32[27,32,32]{2,1,0:T(8,128)}) custom-call(bf16[32,16,128]{2,1,0:T(8,128)(2,1)S(1)} %all-to-all-done.2.sums_ref), custom_call_target="tpu_custom_call" | custom-call | tf_op jit(solution)/shard_map/pallas_call | solution.py:407
  (47 shorter events, 4.0 us)
Async XLA Ops:
  0.6 0.8 %copy-start.3 = (bf16[1,64,512]{2,1,0:T(8,128)(2,1)S(1)}, bf16[1,64,512]{2,1,0:T(8,128)(2,1)}, u32[]{:S(2)}) copy-start(bf16[1,64,512]{2,1,0:T(8,128)(2,1)} %latents_ref.1) | copy-start | bytes 196612
  3.0 19.7 %all-to-all-start = ((bf16[16,24,128]{2,1,0:T(8,128)(2,1)}), bf16[16,24,128]{2,1,0:T(8,128)(2,1)}, u32[]{:S(2)}, u32[]{:S(2)}) async-start(bf16[16,24,128]{2,1,0:T(8,128)(2,1)} %shard_map.95), calls=%async_computation | async-start | bytes 196608 | tf_op jit(solution)/shard_map/all_to_all | solution.py:364
  10.2 0.8 %copy-start = (bf16[1,2,8,8,256]{4,3,2,1,0:T(8,128)(2,1)S(1)}, bf16[1,2,8,8,256]{4,3,2,1,0:T(8,128)(2,1)}, u32[]{:S(2)}) copy-start(bf16[1,2,8,8,256]{4,3,2,1,0:T(8,128)(2,1)} %cotangent_ref.3) | copy-start | bytes 196612
  11.1 8.8 %copy-start.4 = (bf16[48,256]{1,0:T(8,128)(2,1)}, bf16[48,256]{1,0:T(8,128)(2,1)S(1)}, u32[]{:S(2)}) copy-start(bf16[48,256]{1,0:T(8,128)(2,1)S(1)} %get-tuple-element.16.high_own) | copy-start | bytes 73732
  11.2 8.8 %copy-start.6 = (bf16[48,256]{1,0:T(8,128)(2,1)}, bf16[48,256]{1,0:T(8,128)(2,1)S(1)}, u32[]{:S(2)}) copy-start(bf16[48,256]{1,0:T(8,128)(2,1)S(1)} %get-tuple-element.17.low_own) | copy-start | bytes 73732
  11.2 8.8 %collective-permute-start = (bf16[48,256]{1,0:T(8,128)(2,1)S(1)}, bf16[48,256]{1,0:T(8,128)(2,1)S(1)}, u32[]{:S(2)}, u32[]{:S(2)}) collective-permute-start(bf16[48,256]{1,0:T(8,128)(2,1)S(1)} %get-tuple-element.16.high_own), channel_id=1, source_target_pairs={{0,2},{2,4},{4,6},{6,8},{8,10},{10,12},{12,14},{14,16},{16,18},{18... | collective-permute-start | bytes 73736 | tf_op jit(solution)/shard_map/ppermute | solution.py:349
  14.6 8.1 %copy-start.12 = (s32[1,2,6]{2,1,0:T(2,128)S(1)}, s32[1,2,6]{2,1,0:T(2,128)}, u32[]{:S(2)}) copy-start(s32[1,2,6]{2,1,0:T(2,128)} %links_ref.3) | copy-start | bytes 148
  14.6 7.5 %collective-permute-start.1 = (bf16[48,256]{1,0:T(8,128)(2,1)S(1)}, bf16[48,256]{1,0:T(8,128)(2,1)S(1)}, u32[]{:S(2)}, u32[]{:S(2)}) collective-permute-start(bf16[48,256]{1,0:T(8,128)(2,1)S(1)} %get-tuple-element.17.low_own), channel_id=1, source_target_pairs={{2,0},{4,2},{6,4},{8,6},{10,8},{12,10},{14,12},{16,14},{18,16},{20... | collective-permute-start | bytes 73736 | tf_op jit(solution)/shard_map/ppermute | solution.py:349
  17.0 0.9 %copy-start.14 = (bf16[27,32,32]{2,1,0:T(8,128)(2,1)S(1)}, bf16[27,32,32]{2,1,0:T(8,128)(2,1)}, u32[]{:S(2)}) copy-start(bf16[27,32,32]{2,1,0:T(8,128)(2,1)} %one_ref.1) | copy-start | bytes 165892
  18.0 0.9 %copy-start.15 = (bf16[27,32,32]{2,1,0:T(8,128)(2,1)S(1)}, bf16[27,32,32]{2,1,0:T(8,128)(2,1)}, u32[]{:S(2)}) copy-start(bf16[27,32,32]{2,1,0:T(8,128)(2,1)} %two_ref.3) | copy-start | bytes 165892
  22.7 0.8 %copy-start.1 = (bf16[1,2,8,8,256]{4,3,2,1,0:T(8,128)(2,1)S(1)}, bf16[1,2,8,8,256]{4,3,2,1,0:T(8,128)(2,1)}, u32[]{:S(2)}) copy-start(bf16[1,2,8,8,256]{4,3,2,1,0:T(8,128)(2,1)} %cotangent_ref.3) | copy-start | bytes 196612
  23.5 0.9 %copy-start.2 = (bf16[64,2048]{1,0:T(8,128)(2,1)S(1)}, bf16[64,2048]{1,0:T(8,128)(2,1)}, u32[]{:S(2)}) copy-start(bf16[64,2048]{1,0:T(8,128)(2,1)} %up_ref.1) | copy-start | bytes 786436
  31.0 11.1 %copy-start.17 = (bf16[128,256]{1,0:T(8,128)(2,1)}, bf16[128,256]{1,0:T(8,128)(2,1)S(1)}, u32[]{:S(2)}) copy-start(bf16[128,256]{1,0:T(8,128)(2,1)S(1)} %get-tuple-element.18.lifted_ref) | copy-start | bytes 196612
  31.0 11.1 %copy-start.19 = (bf16[128,256]{1,0:T(8,128)(2,1)}, bf16[128,256]{1,0:T(8,128)(2,1)S(1)}, u32[]{:S(2)}) copy-start(bf16[128,256]{1,0:T(8,128)(2,1)S(1)} %get-tuple-element.19.hidden_ref) | copy-start | bytes 196612
  31.0 11.1 %copy-start.21 = (bf16[48,256]{1,0:T(8,128)(2,1)}, bf16[48,256]{1,0:T(8,128)(2,1)S(1)}, u32[]{:S(2)}) copy-start(bf16[48,256]{1,0:T(8,128)(2,1)S(1)} %get-tuple-element.20.high_own) | copy-start | bytes 73732
  31.0 11.1 %copy-start.23 = (bf16[48,256]{1,0:T(8,128)(2,1)}, bf16[48,256]{1,0:T(8,128)(2,1)S(1)}, u32[]{:S(2)}) copy-start(bf16[48,256]{1,0:T(8,128)(2,1)S(1)} %get-tuple-element.21.low_own) | copy-start | bytes 73732
  42.8 17.2 %all-to-all-start.2 = ((bf16[32,16,128]{2,1,0:T(8,128)(2,1)}), bf16[32,16,128]{2,1,0:T(8,128)(2,1)S(1)}, u32[]{:S(2)}, u32[]{:S(2)}) async-start(bf16[32,16,128]{2,1,0:T(8,128)(2,1)} %shard_map.100), calls=%async_computation.2 | async-start | bytes 262144 | tf_op jit(solution)/shard_map/all_to_all | solution.py:404
  47.1 7.4 %collective-permute-start.2 = (bf16[48,256]{1,0:T(8,128)(2,1)}, bf16[48,256]{1,0:T(8,128)(2,1)S(1)}, u32[]{:S(2)}, u32[]{:S(2)}) collective-permute-start(bf16[48,256]{1,0:T(8,128)(2,1)} %copy-done.21), channel_id=1, source_target_pairs={{0,2},{2,4},{4,6},{6,8},{8,10},{10,12},{12,14},{14,16},{16,18},{18... | collective-permute-start | bytes 73736 | tf_op jit(solution)/shard_map/ppermute | solution.py:349
  50.5 7.7 %collective-permute-start.3 = (bf16[48,256]{1,0:T(8,128)(2,1)}, bf16[48,256]{1,0:T(8,128)(2,1)S(1)}, u32[]{:S(2)}, u32[]{:S(2)}) collective-permute-start(bf16[48,256]{1,0:T(8,128)(2,1)} %copy-done.23), channel_id=1, source_target_pairs={{2,0},{4,2},{6,4},{8,6},{10,8},{12,10},{14,12},{16,14},{18,16},{20... | collective-permute-start | bytes 73736 | tf_op jit(solution)/shard_map/ppermute | solution.py:349
  53.0 0.9 %copy-start.16 = (bf16[27,32,32]{2,1,0:T(8,128)(2,1)S(1)}, bf16[27,32,32]{2,1,0:T(8,128)(2,1)}, u32[]{:S(2)}) copy-start(bf16[27,32,32]{2,1,0:T(8,128)(2,1)} %two_ref.3) | copy-start | bytes 165892
  53.9 4.3 %copy-start.18 = (bf16[128,256]{1,0:T(8,128)(2,1)S(1)}, bf16[128,256]{1,0:T(8,128)(2,1)}, u32[]{:S(2)}) copy-start(bf16[128,256]{1,0:T(8,128)(2,1)} %copy-done.17) | copy-start | bytes 196612
  53.9 4.3 %copy-start.20 = (bf16[128,256]{1,0:T(8,128)(2,1)S(1)}, bf16[128,256]{1,0:T(8,128)(2,1)}, u32[]{:S(2)}) copy-start(bf16[128,256]{1,0:T(8,128)(2,1)} %copy-done.19) | copy-start | bytes 196612
  53.9 4.3 %copy-start.22 = (bf16[48,256]{1,0:T(8,128)(2,1)S(1)}, bf16[48,256]{1,0:T(8,128)(2,1)}, u32[]{:S(2)}) copy-start(bf16[48,256]{1,0:T(8,128)(2,1)} %copy-done.21) | copy-start | bytes 73732
  53.9 4.3 %copy-start.24 = (bf16[48,256]{1,0:T(8,128)(2,1)S(1)}, bf16[48,256]{1,0:T(8,128)(2,1)}, u32[]{:S(2)}) copy-start(bf16[48,256]{1,0:T(8,128)(2,1)} %copy-done.23) | copy-start | bytes 73732
  (7 other events, 4.8 us)

commit v5 on v4

--- a/solution.py
+++ b/solution.py
@@ -80,15 +80,6 @@
     cube = jnp.swapaxes(weights, 1, 2).reshape(9, 3, CHANNELS, CHANNELS)
     pieces = [jnp.concatenate([cube[8 - k, 2], cube[8 - k, 1], cube[8 - k, 0]], axis=-1) for k in range(9)]
     return jnp.concatenate(pieces, axis=0).astype(BF16)
-
-
-def first_bands_kernel(one_ref, two_ref, band_ref, back_ref):
-    build_band(band_ref, weight_rows(one_ref[...].astype(F32)))
-    build_band(back_ref, flipped_rows(two_ref[...].astype(F32)))
-
-
-def last_band_kernel(two_ref, band_ref):
-    build_band(band_ref, weight_rows(two_ref[...].astype(F32)))
 
 
 def put_padded(pad_ref, brick, volume, x_low, x_high, y_low, y_high, z_low, z_high):
@@ -218,12 +209,14 @@
 
 
 def first_kernel(
-    links_ref, received_ref, up_ref, band_ref, back_ref, cotangent_ref,
+    links_ref, received_ref, up_ref, one_ref, two_ref, cotangent_ref,
     high_own, low_own, high_left, low_right,
     lifted_out, hidden_out, high_out, low_out, sums_out,
     volumes_ref, lifted_pad, cotangent_pad, halves_ref, high_ref, low_ref, high_pool, low_pool,
-    rows_ref, wide_ref, tall_ref, sums_ref,
+    rows_ref, wide_ref, tall_ref, sums_ref, band_ref, back_ref,
 ):
+    build_band(band_ref, weight_rows(one_ref[...].astype(F32)))
+    build_band(back_ref, flipped_rows(two_ref[...].astype(F32)))
     position = lax.axis_index("space")
     tiles = received_ref.shape[1] // (3 * BRICKS)
     rows_ref[0 : 3 * BRICKS * tiles] = jnp.sum(received_ref[...].astype(F32), axis=0)
@@ -300,9 +293,10 @@
 
 
 def fine_kernel(
-    links_ref, band_ref, lifted_ref, hidden_ref, high_own, low_own, high_left, low_right,
-    fine_out, hidden_pad, high_pool, low_pool,
+    links_ref, two_ref, lifted_ref, hidden_ref, high_own, low_own, high_left, low_right,
+    fine_out, hidden_pad, high_pool, low_pool, band_ref,
 ):
+    build_band(band_ref, weight_rows(two_ref[...].astype(F32)))
     fill_pools(high_pool, low_pool, high_own, low_own, high_left, low_right)
     hidden = hidden_ref[...].astype(F32)
     for brick in range(BRICKS):
@@ -311,7 +305,8 @@
     fine_out[...] = fine.astype(BF16).reshape(fine_out.shape)
 
 
-def sum_kernel(scale, parts_ref, out_ref):
+def sum_kernel(scale, parts_ref, *refs):
+    out_ref = refs[-1]
     total = jnp.sum(parts_ref[...].astype(F32), axis=0) * scale
     out_ref[...] = jnp.broadcast_to(total.astype(BF16)[None], out_ref.shape)
 
@@ -326,8 +321,8 @@
             out[index % 27, 8 * q : 8 * q + 8, :] = moved[:, :CHANNELS]
 
 
-def call(kernel, out_shape, scratch=(), smem=(), inputs=1, limit=24, cost=None):
-    spaces = [pltpu.SMEM if i in smem else pltpu.VMEM for i in range(inputs)]
+def call(kernel, out_shape, scratch=(), smem=(), unread=(), inputs=1, limit=24, cost=None):
+    spaces = [pltpu.SMEM if i in smem else pl.ANY if i in unread else pltpu.VMEM for i in range(inputs)]
     return pl.pallas_call(
         kernel,
         out_shape=out_shape,
@@ -362,7 +357,7 @@
         inputs=2,
     )(active_blocks, coarse_latents)
     received = lax.all_to_all(packed, "space", split_axis=0, concat_axis=0, tiled=True)
-    band = shape(9, WIDE, LINE)
+    band = pltpu.VMEM((9, WIDE, LINE), BF16)
     cost = pl.CostEstimate(flops=10**9, bytes_accessed=2 * 10**6, transcendentals=0)
     face = shape(BRICKS * FACE, LINE)
     halves = pltpu.VMEM((2, LINES, 128), F32)
@@ -375,7 +370,6 @@
     high, low = call(faces_kernel, (face, face), [halves, faces, faces])(cotangent)
     high_left = passed_along(high, "space", 1)
     low_right = passed_along(low, "space", -1)
-    band_one, band_back = call(first_bands_kernel, (band, band), inputs=2, cost=cost)(conv_one, conv_two)
     lifted, hidden, hidden_high, hidden_low, sums = call(
         first_kernel,
         (volume, volume, face, face, shape(everyone, per * 8, 128)),
@@ -385,22 +379,25 @@
             pltpu.VMEM((LINE, WIDE), F32),
             pltpu.VMEM((WIDE, LINE), F32),
             pltpu.VMEM((everyone * per * 8, 128), F32),
+            band,
+            band,
         ],
         smem=(0,),
         inputs=10,
     )(
-        face_links, received, up_weight, band_one, band_back, cotangent, high, low, high_left, low_right
+        face_links, received, up_weight, conv_one, conv_two, cotangent, high, low, high_left, low_right
     )
     hidden_left = passed_along(hidden_high, "space", 1)
     hidden_right = passed_along(hidden_low, "space", -1)
-    band_two = call(last_band_kernel, band, cost=cost)(conv_two)
-    fine = call(fine_kernel, shape(*cotangent.shape), [pad, pool, pool], smem=(0,), inputs=8, cost=cost)(
-        face_links, band_two, lifted, hidden, hidden_high, hidden_low, hidden_left, hidden_right
+    fine = call(fine_kernel, shape(*cotangent.shape), [pad, pool, pool, band], smem=(0,), inputs=8, cost=cost)(
+        face_links, conv_two, lifted, hidden, hidden_high, hidden_low, hidden_left, hidden_right
     )
     axes = ("space", "dp")
     parts = lax.all_to_all(sums, axes, split_axis=0, concat_axis=0, tiled=True)
     scale = 1.0 / math.sqrt(lax.axis_size("dp") * devices * BRICKS * EDGE**3)
-    total = call(functools.partial(sum_kernel, scale), shape(*sums.shape))(parts)
+    total = call(functools.partial(sum_kernel, scale), shape(*sums.shape), unread=(1, 2), inputs=3)(
+        parts, hidden_left, hidden_right
+    )
     gathered = lax.all_to_all(total, axes, split_axis=0, concat_axis=0, tiled=True)
     grads = shape(27, CHANNELS, CHANNELS, dtype=F32)
     rows = pltpu.VMEM((everyone * per * 8, 128), F32)

time: 61.9 us -> 60.4 us (0.976)
  the two profiles are of different devices: /device:TPU:6 before, /device:TPU:0 now
where the time goes in v5:
time: 60.4 us; the launch traced here: 59.9 us
  starting transfers between devices  31.4 us (52%)
  waiting for transfers between devices  14.4 us (24%)
  Pallas kernels  10 us (17%)
  local copies, waits for them, and re-layouts  3.37 us (6%)
  between operations  0.75 us (1%)
    ppermute x4, starting transfers between devices, passed_along(): lax.ppermute(value, axis, [(source, source + steps) for source in range(f...  10.2 us
    ppermute x4, waiting for transfers between devices, passed_along(): lax.ppermute(value, axis, [(source, source + steps) for source in range(f...  8.84 us
    all_to_all x1, starting transfers between devices, body(): lax.all_to_all(packed, 'space', split_axis=0, concat_axis=0, tiled=True)  8.44 us
    all_to_all x1, starting transfers between devices, body(): lax.all_to_all(total, axes, split_axis=0, concat_axis=0, tiled=True)  6.38 us
    all_to_all x1, starting transfers between devices, body(): parts = lax.all_to_all(sums, axes, split_axis=0, concat_axis=0, tiled=True)  6.33 us
    all_to_all x1, waiting for transfers between devices, body(): lax.all_to_all(total, axes, split_axis=0, concat_axis=0, tiled=True)  5.51 us
    pallas_call x1, Pallas kernels, body(): call(first_kernel, (volume, volume, face, face, shape(everyone, per * 8,...  4.67 us
    unnamed x16, local copies, waits for them, and re-layouts  3.37 us
  transfers between devices with their start and end apart: 7, of which 5 were waited for; matrix products, arithmetic and copies ran while one was open for 0% of the time, Pallas kernels for 5%

profile of v5, /device:TPU:0, one launch (start us, length us, event | category | flops | bytes accessed | tf_op | source)
XLA Modules:
  0.0 59.9 jit_solution(16979348602494287257)
XLA Ops:
  0.6 0.8 %copy-done.5 = bf16[1,64,512]{2,1,0:T(8,128)(2,1)S(1)} copy-done((bf16[1,64,512]{2,1,0:T(8,128)(2,1)S(1)}, bf16[1,64,512]{2,1,0:T(8,128)(2,1)}, u32[]{:S(2)}) %copy-start.5) | copy-done | bytes 65560
  1.5 0.7 %copy-done.7 = s32[1,32]{1,0:T(1,128)S(1)} copy-done((s32[1,32]{1,0:T(1,128)S(1)}, s32[1,32]{1,0:T(1,128)}, u32[]{:S(2)}) %copy-start.7) | copy-done | bytes 152
  2.1 0.8 %shard_map.94 = bf16[16,24,128]{2,1,0:T(8,128)(2,1)} custom-call(s32[1,32]{1,0:T(1,128)S(1)} %copy-done.7, bf16[1,64,512]{2,1,0:T(8,128)(2,1)S(1)} %copy-done.5), custom_call_target="tpu_custom_call" | custom-call | tf_op jit(solution)/shard_map/pallas_call | solution.py:353
  3.0 8.4 %all-to-all-start = ((bf16[16,24,128]{2,1,0:T(8,128)(2,1)}), bf16[16,24,128]{2,1,0:T(8,128)(2,1)S(1)}, u32[]{:S(2)}, u32[]{:S(2)}) async-start(bf16[16,24,128]{2,1,0:T(8,128)(2,1)} %shard_map.94), calls=%async_computation | async-start | bytes 196608 | tf_op jit(solution)/shard_map/all_to_all | solution.py:359
  11.4 0.1 shard_map.95
  11.5 0.0 copy-start.6
  11.5 3.8 %collective-permute-start = (bf16[48,256]{1,0:T(8,128)(2,1)S(1)}, bf16[48,256]{1,0:T(8,128)(2,1)S(1)}, u32[]{:S(2)}, u32[]{:S(2)}) collective-permute-start(bf16[48,256]{1,0:T(8,128)(2,1)S(1)} %get-tuple-element.12.high_own), channel_id=1, source_target_pairs={{0,2},{2,4},{4,6},{6,8},{8,10},{10,12},{12,14},{14,16},{16,18},{18... | collective-permute-start | bytes 73736 | tf_op jit(solution)/shard_map/ppermute | solution.py:344
  15.4 1.3 %collective-permute-start.1 = (bf16[48,256]{1,0:T(8,128)(2,1)S(1)}, bf16[48,256]{1,0:T(8,128)(2,1)S(1)}, u32[]{:S(2)}, u32[]{:S(2)}) collective-permute-start(bf16[48,256]{1,0:T(8,128)(2,1)S(1)} %get-tuple-element.13.low_own), channel_id=1, source_target_pairs={{2,0},{4,2},{6,4},{8,6},{10,8},{12,10},{14,12},{16,14},{18,16},{20... | collective-permute-start | bytes 73736 | tf_op jit(solution)/shard_map/ppermute | solution.py:344
  16.7 0.2 collective-permute-done.high_left
  16.9 4.2 %collective-permute-done.1.low_right = bf16[48,256]{1,0:T(8,128)(2,1)S(1)} collective-permute-done((bf16[48,256]{1,0:T(8,128)(2,1)S(1)}, bf16[48,256]{1,0:T(8,128)(2,1)S(1)}, u32[]{:S(2)}, u32[]{:S(2)}) %collective-permute-start.1) | collective-permute-done | bytes 24608 | tf_op jit(solution)/shard_map/ppermute | solution.py:344
  21.1 0.0 copy-start.2
  21.1 0.9 %copy-done.2 = bf16[27,32,32]{2,1,0:T(8,128)(2,1)S(1)} copy-done((bf16[27,32,32]{2,1,0:T(8,128)(2,1)S(1)}, bf16[27,32,32]{2,1,0:T(8,128)(2,1)}, u32[]{:S(2)}) %copy-start.2) | copy-done | bytes 55320
  22.0 0.9 %copy-done.3 = bf16[27,32,32]{2,1,0:T(8,128)(2,1)S(1)} copy-done((bf16[27,32,32]{2,1,0:T(8,128)(2,1)S(1)}, bf16[27,32,32]{2,1,0:T(8,128)(2,1)}, u32[]{:S(2)}) %copy-start.3) | copy-done | bytes 55320
  23.0 4.7 %shard_map.96 = (bf16[128,256]{1,0:T(8,128)(2,1)S(1)}, bf16[128,256]{1,0:T(8,128)(2,1)S(1)}, bf16[48,256]{1,0:T(8,128)(2,1)S(1)}, bf16[48,256]{1,0:T(8,128)(2,1)S(1)}, bf16[32,16,128]{2,1,0:T(8,128)(2,1)}) custom-call(s32[1,2,6]{2,1,0:T(2,128)S(1)} %copy-done.6, bf16[16,24,128]{2,1,0:T(8,128)(2,1)S(1)} %all-to-all-done.received_ref, ...), custom_call_target="tpu_custom_call" | custom-call | tf_op jit(solution)/shard_map/pallas_call | solution.py:373
  27.6 6.3 %all-to-all-start.1 = ((bf16[32,16,128]{2,1,0:T(8,128)(2,1)}), bf16[32,16,128]{2,1,0:T(8,128)(2,1)S(1)}, u32[]{:S(2)}, u32[]{:S(2)}) async-start(bf16[32,16,128]{2,1,0:T(8,128)(2,1)} %get-tuple-element.18), calls=%async_computation.1 | async-start | bytes 262144 | tf_op jit(solution)/shard_map/all_to_all | solution.py:396
  34.0 3.7 %collective-permute-start.2 = (bf16[48,256]{1,0:T(8,128)(2,1)S(1)}, bf16[48,256]{1,0:T(8,128)(2,1)S(1)}, u32[]{:S(2)}, u32[]{:S(2)}) collective-permute-start(bf16[48,256]{1,0:T(8,128)(2,1)S(1)} %get-tuple-element.16.high_own), channel_id=1, source_target_pairs={{0,2},{2,4},{4,6},{6,8},{8,10},{10,12},{12,14},{14,16},{16,18},{18... | collective-permute-start | bytes 73736 | tf_op jit(solution)/shard_map/ppermute | solution.py:344
  37.7 1.4 %collective-permute-start.3 = (bf16[48,256]{1,0:T(8,128)(2,1)S(1)}, bf16[48,256]{1,0:T(8,128)(2,1)S(1)}, u32[]{:S(2)}, u32[]{:S(2)}) collective-permute-start(bf16[48,256]{1,0:T(8,128)(2,1)S(1)} %get-tuple-element.17.low_own), channel_id=1, source_target_pairs={{2,0},{4,2},{6,4},{8,6},{10,8},{12,10},{14,12},{16,14},{18,16},{20... | collective-permute-start | bytes 73736 | tf_op jit(solution)/shard_map/ppermute | solution.py:344
  39.1 0.1 collective-permute-done.2.high_left.refs_0_
  39.2 4.4 %collective-permute-done.3.low_right.refs_1_ = bf16[48,256]{1,0:T(8,128)(2,1)S(1)} collective-permute-done((bf16[48,256]{1,0:T(8,128)(2,1)S(1)}, bf16[48,256]{1,0:T(8,128)(2,1)S(1)}, u32[]{:S(2)}, u32[]{:S(2)}) %collective-permute-start.3) | collective-permute-done | bytes 24608 | tf_op jit(solution)/shard_map/ppermute | solution.py:344
  43.5 0.7 %shard_map.98 = bf16[32,16,128]{2,1,0:T(8,128)(2,1)} custom-call(bf16[32,16,128]{2,1,0:T(8,128)(2,1)S(1)} %all-to-all-done.1.parts_ref, bf16[48,256]{1,0:T(8,128)(2,1)S(1)} %collective-permute-done.2.high_left.refs_0_, bf16[48,256]{1,0:T(8,128)(2,1)S(1)} %collective-permute-done.3.low_right.refs_1_), custom_call_target="tpu_custom_call" | custom-call | tf_op jit(solution)/shard_map/pallas_call | solution.py:398
  44.2 6.4 %all-to-all-start.2 = ((bf16[32,16,128]{2,1,0:T(8,128)(2,1)}), bf16[32,16,128]{2,1,0:T(8,128)(2,1)S(1)}, u32[]{:S(2)}, u32[]{:S(2)}) async-start(bf16[32,16,128]{2,1,0:T(8,128)(2,1)} %shard_map.98), calls=%async_computation.2 | async-start | bytes 262144 | tf_op jit(solution)/shard_map/all_to_all | solution.py:401
  50.6 2.7 %shard_map.97 = bf16[1,2,8,8,256]{4,3,2,1,0:T(8,128)(2,1)} custom-call(s32[1,2,6]{2,1,0:T(2,128)S(1)} %copy-done.6, bf16[27,32,32]{2,1,0:T(8,128)(2,1)S(1)} %copy-done.4, bf16[128,256]{1,0:T(8,128)(2,1)S(1)} %get-tuple-element.14.lifted_ref, bf16[128,256]{1,0:T(8,128)(2,1)S(1)} %get-tuple-element.15.hidden_ref, ...), custom_call_target="tpu_custom_call" | custom-call | flops 1000000000 | bytes 2000000 | tf_op jit(solution)/shard_map/pallas_call | solution.py:392
  53.3 5.5 %all-to-all-done.2.sums_ref = bf16[32,16,128]{2,1,0:T(8,128)(2,1)S(1)} async-done(((bf16[32,16,128]{2,1,0:T(8,128)(2,1)}), bf16[32,16,128]{2,1,0:T(8,128)(2,1)S(1)}, u32[]{:S(2)}, u32[]{:S(2)}) %all-to-all-start.2) | async-done | bytes 131104 | tf_op jit(solution)/shard_map/all_to_all | solution.py:401
  58.9 1.0 %shard_map.99 = (f32[27,32,32]{2,1,0:T(8,128)}, f32[27,32,32]{2,1,0:T(8,128)}) custom-call(bf16[32,16,128]{2,1,0:T(8,128)(2,1)S(1)} %all-to-all-done.2.sums_ref), custom_call_target="tpu_custom_call" | custom-call | tf_op jit(solution)/shard_map/pallas_call | solution.py:404
  (12 shorter events, 0.0 us)
Async XLA Ops:
  0.6 0.8 %copy-start.5 = (bf16[1,64,512]{2,1,0:T(8,128)(2,1)S(1)}, bf16[1,64,512]{2,1,0:T(8,128)(2,1)}, u32[]{:S(2)}) copy-start(bf16[1,64,512]{2,1,0:T(8,128)(2,1)} %latents_ref.1) | copy-start | bytes 196612
  1.5 0.7 %copy-start.7 = (s32[1,32]{1,0:T(1,128)S(1)}, s32[1,32]{1,0:T(1,128)}, u32[]{:S(2)}) copy-start(s32[1,32]{1,0:T(1,128)} %ids_ref.1) | copy-start | bytes 388
  2.1 19.0 %copy-start = (bf16[64,2048]{1,0:T(8,128)(2,1)S(1)}, bf16[64,2048]{1,0:T(8,128)(2,1)}, u32[]{:S(2)}) copy-start(bf16[64,2048]{1,0:T(8,128)(2,1)} %up_ref.1) | copy-start | bytes 786436
  3.0 8.5 %copy-start.1 = (bf16[1,2,8,8,256]{4,3,2,1,0:T(8,128)(2,1)S(1)}, bf16[1,2,8,8,256]{4,3,2,1,0:T(8,128)(2,1)}, u32[]{:S(2)}) copy-start(bf16[1,2,8,8,256]{4,3,2,1,0:T(8,128)(2,1)} %cotangent_ref.3) | copy-start | bytes 196612
  3.0 18.1 %all-to-all-start = ((bf16[16,24,128]{2,1,0:T(8,128)(2,1)}), bf16[16,24,128]{2,1,0:T(8,128)(2,1)S(1)}, u32[]{:S(2)}, u32[]{:S(2)}) async-start(bf16[16,24,128]{2,1,0:T(8,128)(2,1)} %shard_map.94), calls=%async_computation | async-start | bytes 196608 | tf_op jit(solution)/shard_map/all_to_all | solution.py:359
  11.5 9.6 %copy-start.6 = (s32[1,2,6]{2,1,0:T(2,128)S(1)}, s32[1,2,6]{2,1,0:T(2,128)}, u32[]{:S(2)}) copy-start(s32[1,2,6]{2,1,0:T(2,128)} %links_ref.3) | copy-start | bytes 148
  11.5 5.3 %collective-permute-start = (bf16[48,256]{1,0:T(8,128)(2,1)S(1)}, bf16[48,256]{1,0:T(8,128)(2,1)S(1)}, u32[]{:S(2)}, u32[]{:S(2)}) collective-permute-start(bf16[48,256]{1,0:T(8,128)(2,1)S(1)} %get-tuple-element.12.high_own), channel_id=1, source_target_pairs={{0,2},{2,4},{4,6},{6,8},{8,10},{10,12},{12,14},{14,16},{16,18},{18... | collective-permute-start | bytes 73736 | tf_op jit(solution)/shard_map/ppermute | solution.py:344
  15.4 5.7 %collective-permute-start.1 = (bf16[48,256]{1,0:T(8,128)(2,1)S(1)}, bf16[48,256]{1,0:T(8,128)(2,1)S(1)}, u32[]{:S(2)}, u32[]{:S(2)}) collective-permute-start(bf16[48,256]{1,0:T(8,128)(2,1)S(1)} %get-tuple-element.13.low_own), channel_id=1, source_target_pairs={{2,0},{4,2},{6,4},{8,6},{10,8},{12,10},{14,12},{16,14},{18,16},{20... | collective-permute-start | bytes 73736 | tf_op jit(solution)/shard_map/ppermute | solution.py:344
  21.1 0.9 %copy-start.2 = (bf16[27,32,32]{2,1,0:T(8,128)(2,1)S(1)}, bf16[27,32,32]{2,1,0:T(8,128)(2,1)}, u32[]{:S(2)}) copy-start(bf16[27,32,32]{2,1,0:T(8,128)(2,1)} %one_ref.1) | copy-start | bytes 165892
  22.0 0.9 %copy-start.3 = (bf16[27,32,32]{2,1,0:T(8,128)(2,1)S(1)}, bf16[27,32,32]{2,1,0:T(8,128)(2,1)}, u32[]{:S(2)}) copy-start(bf16[27,32,32]{2,1,0:T(8,128)(2,1)} %two_ref.3) | copy-start | bytes 165892
  27.6 15.9 %all-to-all-start.1 = ((bf16[32,16,128]{2,1,0:T(8,128)(2,1)}), bf16[32,16,128]{2,1,0:T(8,128)(2,1)S(1)}, u32[]{:S(2)}, u32[]{:S(2)}) async-start(bf16[32,16,128]{2,1,0:T(8,128)(2,1)} %get-tuple-element.18), calls=%async_computation.1 | async-start | bytes 262144 | tf_op jit(solution)/shard_map/all_to_all | solution.py:396
  34.0 5.2 %collective-permute-start.2 = (bf16[48,256]{1,0:T(8,128)(2,1)S(1)}, bf16[48,256]{1,0:T(8,128)(2,1)S(1)}, u32[]{:S(2)}, u32[]{:S(2)}) collective-permute-start(bf16[48,256]{1,0:T(8,128)(2,1)S(1)} %get-tuple-element.16.high_own), channel_id=1, source_target_pairs={{0,2},{2,4},{4,6},{6,8},{8,10},{10,12},{12,14},{14,16},{16,18},{18... | collective-permute-start | bytes 73736 | tf_op jit(solution)/shard_map/ppermute | solution.py:344
  37.7 13.0 %copy-start.4 = (bf16[27,32,32]{2,1,0:T(8,128)(2,1)S(1)}, bf16[27,32,32]{2,1,0:T(8,128)(2,1)}, u32[]{:S(2)}) copy-start(bf16[27,32,32]{2,1,0:T(8,128)(2,1)} %two_ref.3) | copy-start | bytes 165892
  37.7 5.9 %collective-permute-start.3 = (bf16[48,256]{1,0:T(8,128)(2,1)S(1)}, bf16[48,256]{1,0:T(8,128)(2,1)S(1)}, u32[]{:S(2)}, u32[]{:S(2)}) collective-permute-start(bf16[48,256]{1,0:T(8,128)(2,1)S(1)} %get-tuple-element.17.low_own), channel_id=1, source_target_pairs={{2,0},{4,2},{6,4},{8,6},{10,8},{12,10},{14,12},{16,14},{18,16},{20... | collective-permute-start | bytes 73736 | tf_op jit(solution)/shard_map/ppermute | solution.py:344
  44.2 14.6 %all-to-all-start.2 = ((bf16[32,16,128]{2,1,0:T(8,128)(2,1)}), bf16[32,16,128]{2,1,0:T(8,128)(2,1)S(1)}, u32[]{:S(2)}, u32[]{:S(2)}) async-start(bf16[32,16,128]{2,1,0:T(8,128)(2,1)} %shard_map.98), calls=%async_computation.2 | async-start | bytes 262144 | tf_op jit(solution)/shard_map/all_to_all | solution.py:401

commit v6 on v2

--- a/solution.py
+++ b/solution.py
@@ -38,22 +38,15 @@
     return lax.broadcasted_iota(jnp.int32, shape, len(shape) - 1)
 
 
-def pick_kernel(devices, ids_hbm, latents_hbm, out_ref, ids_ref, latents_ref, rows_ref, sems):
-    ids_copy = pltpu.make_async_copy(ids_hbm, ids_ref, sems.at[0])
-    latents_copy = pltpu.make_async_copy(latents_hbm, latents_ref, sems.at[1])
-    ids_copy.start()
-    latents_copy.start()
+def pick_kernel(devices, ids_ref, latents_ref, out_ref, rows_ref):
     held, width = latents_ref.shape[1:]
     bricks = ids_ref.shape[1]
     margin = 8 * width // 128
     tiles = width // 128
     rows_ref[0:margin] = jnp.zeros((margin, 128), F32)
     rows_ref[margin + bricks * tiles :] = jnp.zeros((margin, 128), F32)
-    first = lax.axis_index("space") * held
-    rows = lax.broadcasted_iota(jnp.int32, (held, bricks), 0) + first
-    ids_copy.wait()
+    rows = lax.broadcasted_iota(jnp.int32, (held, bricks), 0)
     hot = jnp.where(rows == ids_ref[...], 1.0, 0.0).astype(BF16)
-    latents_copy.wait()
     picked = dot_rows(hot, latents_ref[0])
     for tile in range(tiles):
         rows_ref[pl.ds(margin + tile, bricks, stride=tiles), :] = picked[:, tile * 128 : tile * 128 + 128]
@@ -155,7 +148,7 @@
 
 def first_kernel(
     links_ref, received_ref, up_ref, band_ref, cotangent_ref,
-    lifted_out, pre_out, hidden_out, pad_out, high_out, low_out,
+    lifted_out, pre_out, hidden_out, pad_out, high_out, low_out, far_out, near_out,
     volumes_ref, pad_ref, lines_ref, high_ref, low_ref, rows_ref,
 ):
     position = lax.axis_index("space")
@@ -219,8 +212,13 @@
             start = which * LINES + brick * CUBE
             pack_faces(high_ref, base, lines_ref, start, True)
             pack_faces(low_ref, base, lines_ref, start, False)
-    high_out[...] = high_ref[...].astype(BF16)
-    low_out[...] = low_ref[...].astype(BF16)
+    high = high_ref[...].astype(BF16)
+    low = low_ref[...].astype(BF16)
+    high_out[...] = high
+    low_out[...] = low
+    even = position % 2 == 0
+    far_out[...] = jnp.where(even, low, high)
+    near_out[...] = jnp.where(even, high, low)
 
 
 def fold_diagonals(outer_ref, part):
@@ -267,21 +265,22 @@
     )
 
 
-def fill_pools(high_ref, low_ref, high_own, low_own, high_left, low_right):
+def fill_pools(high_ref, low_ref, high_own, low_own, far, near):
     half = 2 * BRICKS * FACE
-    high_ref[0:half] = high_left[...].astype(F32)
+    even = lax.axis_index("space") % 2 == 0
+    high_ref[0:half] = jnp.where(even, far[...], near[...]).astype(F32)
     high_ref[half:] = high_own[...].astype(F32)
     low_ref[0:half] = low_own[...].astype(F32)
-    low_ref[half:] = low_right[...].astype(F32)
+    low_ref[half:] = jnp.where(even, near[...], far[...]).astype(F32)
 
 
 def second_kernel(
     links_ref, cotangent_ref, band_ref, back_ref, lifted_ref, pre_ref, hidden_ref, pad_in,
-    high_own, low_own, high_left, low_right,
+    high_own, low_own, far, near,
     fine_out, sums_out,
     high_ref, low_ref, hidden_pad, cotangent_pad, lifted_pad, outer_ref, sums_ref,
 ):
-    fill_pools(high_ref, low_ref, high_own, low_own, high_left, low_right)
+    fill_pools(high_ref, low_ref, high_own, low_own, far, near)
     lifted_pad[...] = pad_in[...].astype(F32).reshape(lifted_pad.shape)
     cotangent = cotangent_ref[...].astype(F32).reshape(LINES, LINE)
     hidden = hidden_ref[...].astype(F32)
@@ -320,8 +319,8 @@
             out[index % 27, 8 * q : 8 * q + 8, :] = moved[:, :CHANNELS]
 
 
-def call(kernel, out_shape, scratch=(), smem=(), hbm=(), inputs=1, limit=24, cost=None):
-    spaces = [pltpu.SMEM if i in smem else pltpu.HBM if i in hbm else pltpu.VMEM for i in range(inputs)]
+def call(kernel, out_shape, scratch=(), smem=(), inputs=1, limit=24, cost=None):
+    spaces = [pltpu.SMEM if i in smem else pltpu.VMEM for i in range(inputs)]
     return pl.pallas_call(
         kernel,
         out_shape=out_shape,
@@ -337,10 +336,9 @@
     return jax.ShapeDtypeStruct(dims, dtype)
 
 
-def passed_along(value, axis, steps):
-    count = lax.axis_size(axis)
-    first, last = (max(0, -steps), min(count, count - steps))
-    return lax.ppermute(value, axis, [(source, source + steps) for source in range(first, last)])
+def swapped(value, first):
+    pairs = [(i, i + 1) for i in range(first, lax.axis_size("space") - 1, 2)]
+    return lax.ppermute(value, "space", pairs + [(target, source) for source, target in pairs])
 
 
 def body(coarse_latents, active_blocks, face_links, cotangent, up_weight, conv_one, conv_two):
@@ -352,15 +350,9 @@
     packed = call(
         functools.partial(pick_kernel, devices),
         shape(devices, 3 * BRICKS * tiles, 128),
-        [
-            pltpu.VMEM((1, bricks), jnp.int32),
-            pltpu.VMEM((1, held, width), BF16),
-            pltpu.VMEM(((bricks + 16) * tiles, 128), F32),
-            pltpu.SemaphoreType.DMA((2,)),
-        ],
-        hbm=(0, 1),
+        [pltpu.VMEM(((bricks + 16) * tiles, 128), F32)],
         inputs=2,
-    )(active_blocks, coarse_latents)
+    )(active_blocks - lax.axis_index("space") * held, coarse_latents)
     received = lax.all_to_all(packed, "space", split_axis=0, concat_axis=0, tiled=True)
     band = shape(9, WIDE, LINE)
     cost = pl.CostEstimate(flops=10**9, bytes_accessed=2 * 10**6, transcendentals=0)
@@ -369,13 +361,15 @@
     pad_shape = (3, BRICKS, EDGE + 2, EDGE, WIDE)
     pad = pltpu.VMEM(pad_shape, F32)
     packed_faces = 2 * BRICKS * FACE
-    lifted, pre, hidden, lifted_pad, high, low = call(
+    lifted, pre, hidden, lifted_pad, high, low, far, near = call(
         first_kernel,
         (
             shape(LINES, LINE),
             shape(LINES, LINE, dtype=F32),
             shape(LINES, LINE),
             shape(math.prod(pad_shape[:-1]), WIDE),
+            shape(packed_faces, LINE),
+            shape(packed_faces, LINE),
             shape(packed_faces, LINE),
             shape(packed_faces, LINE),
         ),
@@ -390,8 +384,8 @@
         smem=(0,),
         inputs=5,
     )(face_links, received, up_weight, band_one, cotangent)
-    high_left = passed_along(high, "space", 1)
-    low_right = passed_along(low, "space", -1)
+    far = swapped(far, 1)
+    near = swapped(near, 0)
     per = -(-BLOCKS // everyone)
     per += per % 2
     fine, sums = call(
@@ -410,7 +404,7 @@
         inputs=12,
     )(
         face_links, cotangent, band_two, band_back, lifted, pre, hidden, lifted_pad,
-        high, low, high_left, low_right,
+        high, low, far, near,
     )
     axes = ("space", "dp")
     parts = lax.all_to_all(sums, axes, split_axis=0, concat_axis=0, tiled=True)

time: 57.1 us -> 53.3 us (0.933)
  waiting for transfers between devices: 9.76 us -> 7.58 us
  blocking collectives: 22.7 us -> 21.3 us
  other arithmetic: 0 us -> 0.66 us
  local copies, waits for them, and re-layouts: 2.44 us -> 1.79 us
    ppermute x2, waiting for transfers between devices: 3.66 us -> 1.48 us  [swapped(): lax.ppermute(value, 'space', pairs + [(target, source) for source, target...]
    all_to_all x1, blocking collectives: 12.7 us -> 11.3 us  [body(): parts = lax.all_to_all(sums, axes, split_axis=0, concat_axis=0, tiled=True)]
    sub x0 -> x1, other arithmetic: none -> 0.66 us  [body(): active_blocks - lax.axis_index('space') * held]
    unnamed x14 -> x12, local copies, waits for them, and re-layouts: 2.44 us -> 1.79 us
where the time goes in v6:
time: 53.3 us; the launch traced here: 53 us
  blocking collectives  21.3 us (40%)
  starting transfers between devices  12.4 us (23%)
  Pallas kernels  8.54 us (16%)
  waiting for transfers between devices  7.58 us (14%)
  local copies, waits for them, and re-layouts  1.79 us (3%)
  between operations  0.71 us (1%)
  other arithmetic  0.66 us (1%)
    all_to_all x1, blocking collectives, body(): parts = lax.all_to_all(sums, axes, split_axis=0, concat_axis=0, tiled=True)  11.3 us
    all_to_all x1, blocking collectives, body(): lax.all_to_all(total, axes, split_axis=0, concat_axis=0, tiled=True)  10 us
    all_to_all x1, starting transfers between devices, body(): lax.all_to_all(packed, 'space', split_axis=0, concat_axis=0, tiled=True)  8.31 us
    all_to_all x1, waiting for transfers between devices, body(): lax.all_to_all(packed, 'space', split_axis=0, concat_axis=0, tiled=True)  6.1 us
    ppermute x2, starting transfers between devices, swapped(): lax.ppermute(value, 'space', pairs + [(target, source) for source, target...  4.13 us
    pallas_call x1, Pallas kernels, body(): call(second_kernel, (shape(*cotangent.shape), shape(everyone, per * 8, 12...  3.23 us
    pallas_call x1, Pallas kernels, body(): call(first_kernel, (shape(LINES, LINE), shape(LINES, LINE, dtype=F32), sh...  1.79 us
    unnamed x12, local copies, waits for them, and re-layouts  1.79 us
  transfers between devices with their start and end apart: 3, of which 2 were waited for; matrix products, arithmetic and copies ran while one was open for 0% of the time, Pallas kernels for 3%

profile of v6, /device:TPU:0, one launch (start us, length us, event | category | flops | bytes accessed | tf_op | source)
XLA Modules:
  0.0 53.0 jit_solution(8674443179114513064)
XLA Ops:
  0.6 0.7 %broadcast_subtract_fusion.ids_ref = s32[1,32]{1,0:T(1,128)S(1)} fusion(s32[1,32]{1,0:T(1,128)} %param.8, s32[]{:T(128)S(6)} %mul.3), kind=kLoop, calls=%fused_computation | loop fusion | flops 32 | bytes 260 | tf_op jit(solution)/shard_map/sub | solution.py:355
  1.3 0.0 copy-start.2
  1.3 0.8 %copy-done.2 = bf16[1,64,512]{2,1,0:T(8,128)(2,1)S(1)} copy-done((bf16[1,64,512]{2,1,0:T(8,128)(2,1)S(1)}, bf16[1,64,512]{2,1,0:T(8,128)(2,1)}, u32[]{:S(2)}) %copy-start.2) | copy-done | bytes 65560
  2.1 0.8 %shard_map.95 = bf16[16,24,128]{2,1,0:T(8,128)(2,1)} custom-call(s32[1,32]{1,0:T(1,128)S(1)} %broadcast_subtract_fusion.ids_ref, bf16[1,64,512]{2,1,0:T(8,128)(2,1)S(1)} %copy-done.2), custom_call_target="tpu_custom_call" | custom-call | tf_op jit(solution)/shard_map/pallas_call | solution.py:350
  3.0 8.3 %all-to-all-start = ((bf16[16,24,128]{2,1,0:T(8,128)(2,1)}), bf16[16,24,128]{2,1,0:T(8,128)(2,1)S(1)}, u32[]{:S(2)}, u32[]{:S(2)}) async-start(bf16[16,24,128]{2,1,0:T(8,128)(2,1)} %shard_map.95), calls=%async_computation | async-start | bytes 196608 | tf_op jit(solution)/shard_map/all_to_all | solution.py:356
  11.3 0.0 copy-start.4
  11.3 0.9 %copy-done.4 = bf16[27,32,32]{2,1,0:T(8,128)(2,1)S(1)} copy-done((bf16[27,32,32]{2,1,0:T(8,128)(2,1)S(1)}, bf16[27,32,32]{2,1,0:T(8,128)(2,1)}, u32[]{:S(2)}) %copy-start.4) | copy-done | bytes 55320
  12.2 0.6 %shard_map.96.band_ref = bf16[9,384,256]{2,1,0:T(8,128)(2,1)S(1)} custom-call(bf16[27,32,32]{2,1,0:T(8,128)(2,1)S(1)} %copy-done.4), custom_call_target="tpu_custom_call" | custom-call | flops 1000000000 | bytes 2000000 | tf_op jit(solution)/shard_map/pallas_call | solution.py:359
  12.8 0.0 copy-start.5
  12.9 6.1 %all-to-all-done.received_ref = bf16[16,24,128]{2,1,0:T(8,128)(2,1)S(1)} async-done(((bf16[16,24,128]{2,1,0:T(8,128)(2,1)}), bf16[16,24,128]{2,1,0:T(8,128)(2,1)S(1)}, u32[]{:S(2)}, u32[]{:S(2)}) %all-to-all-start) | async-done | bytes 98336 | tf_op jit(solution)/shard_map/all_to_all | solution.py:356
  19.0 0.0 copy-done
  19.0 0.0 copy-done.1
  19.0 0.0 copy-done.3
  19.0 1.8 %shard_map.97 = (bf16[128,256]{1,0:T(8,128)(2,1)S(1)}, f32[128,256]{1,0:T(8,128)S(1)}, bf16[128,256]{1,0:T(8,128)(2,1)S(1)}, bf16[480,384]{1,0:T(8,128)(2,1)S(1)...) custom-call(s32[1,2,6]{2,1,0:T(2,128)S(1)} %copy-done.3, ...), custom_call_target="tpu_custom_call" | custom-call | tf_op jit(solution)/shard_map/pallas_call | solution.py:364
  20.8 0.7 %collective-permute-start = (bf16[96,256]{1,0:T(8,128)(2,1)S(1)}, bf16[96,256]{1,0:T(8,128)(2,1)S(1)}, u32[]{:S(2)}, u32[]{:S(2)}) collective-permute-start(bf16[96,256]{1,0:T(8,128)(2,1)S(1)} %get-tuple-element.25), channel_id=1, source_target_pairs={{2,4},{6,8},{10,12},{14,16},{18,20},{22,24},{26,28},{4,2},{8,6},{1... | collective-permute-start | bytes 147464 | tf_op jit(solution)/shard_map/ppermute | solution.py:341
  21.4 3.5 %collective-permute-start.1 = (bf16[96,256]{1,0:T(8,128)(2,1)S(1)}, bf16[96,256]{1,0:T(8,128)(2,1)S(1)}, u32[]{:S(2)}, u32[]{:S(2)}) collective-permute-start(bf16[96,256]{1,0:T(8,128)(2,1)S(1)} %get-tuple-element.26), channel_id=1, source_target_pairs={{0,2},{4,6},{8,10},{12,14},{16,18},{20,22},{24,26},{28,30},{2,0},{... | collective-permute-start | bytes 147464 | tf_op jit(solution)/shard_map/ppermute | solution.py:341
  24.9 0.0 copy-done.5
  24.9 1.0 %shard_map.94 = (bf16[9,384,256]{2,1,0:T(8,128)(2,1)S(1)}, bf16[9,384,256]{2,1,0:T(8,128)(2,1)S(1)}) custom-call(bf16[27,32,32]{2,1,0:T(8,128)(2,1)S(1)} %copy-done.5), custom_call_target="tpu_custom_call" | custom-call | flops 1000000000 | bytes 2000000 | tf_op jit(solution)/shard_map/pallas_call | solution.py:360
  25.9 0.0 collective-permute-done.far
  25.9 1.5 %collective-permute-done.1.near = bf16[96,256]{1,0:T(8,128)(2,1)S(1)} collective-permute-done((bf16[96,256]{1,0:T(8,128)(2,1)S(1)}, bf16[96,256]{1,0:T(8,128)(2,1)S(1)}, u32[]{:S(2)}, u32[]{:S(2)}) %collective-permute-start.1) | collective-permute-done | bytes 49184 | tf_op jit(solution)/shard_map/ppermute | solution.py:341
  27.4 3.2 %shard_map.98 = (bf16[1,2,8,8,256]{4,3,2,1,0:T(8,128)(2,1)}, bf16[32,16,128]{2,1,0:T(8,128)(2,1)S(1)}) custom-call(s32[1,2,6]{2,1,0:T(2,128)S(1)} %copy-done.3, bf16[1,2,8,8,256]{4,3,2,1,0:T(8,128)(2,1)S(1)} %copy-done, bf16[9,384,256]{2,1,0:T(8,128)(2,1)S(1)} %get-tuple-element.17.band_ref, bf16[9,384,256]{2,1,0:T(8,128)(2,1)S(1)} %get-tuple-element.18.back_ref, ...), custom_call_target="tpu_custom_call" | custom-call | tf_op jit(solution)/shard_map/pallas_call | solution.py:391
  30.6 11.3 %all_to_all.15.parts_ref = bf16[32,16,128]{2,1,0:T(8,128)(2,1)S(1)} all-to-all(bf16[32,16,128]{2,1,0:T(8,128)(2,1)S(1)} %get-tuple-element.28), channel_id=1, replica_groups=mesh['space'=16,'dp'=2] {'space','dp'}, dimensions={0} | all-to-all | bytes 262144 | tf_op jit(solution)/shard_map/all_to_all | solution.py:410
  42.0 10.0 %all_to_all.16.sums_ref = bf16[32,16,128]{2,1,0:T(8,128)(2,1)S(1)} all-to-all(bf16[32,16,128]{2,1,0:T(8,128)(2,1)S(1)} %shard_map.99), channel_id=1, replica_groups=mesh['space'=16,'dp'=2] {'space','dp'}, dimensions={0} | all-to-all | bytes 262144 | tf_op jit(solution)/shard_map/all_to_all | solution.py:413
  52.0 1.0 %shard_map.100 = (f32[27,32,32]{2,1,0:T(8,128)}, f32[27,32,32]{2,1,0:T(8,128)}) custom-call(bf16[32,16,128]{2,1,0:T(8,128)(2,1)S(1)} %all_to_all.16.sums_ref), custom_call_target="tpu_custom_call" | custom-call | tf_op jit(solution)/shard_map/pallas_call | solution.py:416
  (4 shorter events, 0.1 us)
Async XLA Ops:
  1.3 0.8 %copy-start.2 = (bf16[1,64,512]{2,1,0:T(8,128)(2,1)S(1)}, bf16[1,64,512]{2,1,0:T(8,128)(2,1)}, u32[]{:S(2)}) copy-start(bf16[1,64,512]{2,1,0:T(8,128)(2,1)} %latents_ref.1) | copy-start | bytes 196612
  3.0 16.0 %all-to-all-start = ((bf16[16,24,128]{2,1,0:T(8,128)(2,1)}), bf16[16,24,128]{2,1,0:T(8,128)(2,1)S(1)}, u32[]{:S(2)}, u32[]{:S(2)}) async-start(bf16[16,24,128]{2,1,0:T(8,128)(2,1)} %shard_map.95), calls=%async_computation | async-start | bytes 196608 | tf_op jit(solution)/shard_map/all_to_all | solution.py:356
  11.3 0.9 %copy-start.4 = (bf16[27,32,32]{2,1,0:T(8,128)(2,1)S(1)}, bf16[27,32,32]{2,1,0:T(8,128)(2,1)}, u32[]{:S(2)}) copy-start(bf16[27,32,32]{2,1,0:T(8,128)(2,1)} %weights_ref.3) | copy-start | bytes 165892
  12.2 6.7 %copy-start = (bf16[1,2,8,8,256]{4,3,2,1,0:T(8,128)(2,1)S(1)}, bf16[1,2,8,8,256]{4,3,2,1,0:T(8,128)(2,1)}, u32[]{:S(2)}) copy-start(bf16[1,2,8,8,256]{4,3,2,1,0:T(8,128)(2,1)} %cotangent_ref.3) | copy-start | bytes 196612
  12.2 6.7 %copy-start.1 = (bf16[64,2048]{1,0:T(8,128)(2,1)S(1)}, bf16[64,2048]{1,0:T(8,128)(2,1)}, u32[]{:S(2)}) copy-start(bf16[64,2048]{1,0:T(8,128)(2,1)} %up_ref.1) | copy-start | bytes 786436
  12.2 6.7 %copy-start.3 = (s32[1,2,6]{2,1,0:T(2,128)S(1)}, s32[1,2,6]{2,1,0:T(2,128)}, u32[]{:S(2)}) copy-start(s32[1,2,6]{2,1,0:T(2,128)} %links_ref.3) | copy-start | bytes 148
  12.8 12.1 %copy-start.5 = (bf16[27,32,32]{2,1,0:T(8,128)(2,1)S(1)}, bf16[27,32,32]{2,1,0:T(8,128)(2,1)}, u32[]{:S(2)}) copy-start(bf16[27,32,32]{2,1,0:T(8,128)(2,1)} %weights_ref.2) | copy-start | bytes 165892
  20.8 5.2 %collective-permute-start = (bf16[96,256]{1,0:T(8,128)(2,1)S(1)}, bf16[96,256]{1,0:T(8,128)(2,1)S(1)}, u32[]{:S(2)}, u32[]{:S(2)}) collective-permute-start(bf16[96,256]{1,0:T(8,128)(2,1)S(1)} %get-tuple-element.25), channel_id=1, source_target_pairs={{2,4},{6,8},{10,12},{14,16},{18,20},{22,24},{26,28},{4,2},{8,6},{1... | collective-permute-start | bytes 147464 | tf_op jit(solution)/shard_map/ppermute | solution.py:341
  21.4 6.0 %collective-permute-start.1 = (bf16[96,256]{1,0:T(8,128)(2,1)S(1)}, bf16[96,256]{1,0:T(8,128)(2,1)S(1)}, u32[]{:S(2)}, u32[]{:S(2)}) collective-permute-start(bf16[96,256]{1,0:T(8,128)(2,1)S(1)} %get-tuple-element.26), channel_id=1, source_target_pairs={{0,2},{4,6},{8,10},{12,14},{16,18},{20,22},{24,26},{28,30},{2,0},{... | collective-permute-start | bytes 147464 | tf_op jit(solution)/shard_map/ppermute | solution.py:341

commit v7 on v6

--- a/solution.py
+++ b/solution.py
@@ -13,10 +13,12 @@
 EDGE = 8
 CHANNELS = 32
 LINE = EDGE * CHANNELS
-WIDE = LINE + 128
+HALF = LINE // 2
+WIDE = 2 * HALF
 BRICKS = 2
 CUBE = EDGE * EDGE
 LINES = BRICKS * CUBE
+ROWS = 2 * LINES
 FACE = 3 * EDGE
 BLOCKS = 54
 
@@ -29,24 +31,31 @@
     return lax.dot_general(left, right, (((0,), (0,)), ((), ())), preferred_element_type=F32)
 
 
-def lines(halves_ref, start, count, stride=1):
+def pair(halves_ref, start, count, stride=1):
     index = pl.ds(start, count, stride=stride) if stride > 1 else pl.ds(start, count)
-    return jnp.concatenate([halves_ref[0, index, :], halves_ref[1, index, :]], axis=-1)
+    return halves_ref[0, index, :], halves_ref[1, index, :]
 
 
 def lanes_of(shape):
     return lax.broadcasted_iota(jnp.int32, shape, len(shape) - 1)
 
 
-def pick_kernel(devices, ids_ref, latents_ref, out_ref, rows_ref):
+def pick_kernel(devices, ids_hbm, latents_hbm, out_ref, ids_ref, latents_ref, rows_ref, sems):
+    ids_copy = pltpu.make_async_copy(ids_hbm, ids_ref, sems.at[0])
+    latents_copy = pltpu.make_async_copy(latents_hbm, latents_ref, sems.at[1])
+    ids_copy.start()
+    latents_copy.start()
     held, width = latents_ref.shape[1:]
     bricks = ids_ref.shape[1]
     margin = 8 * width // 128
     tiles = width // 128
     rows_ref[0:margin] = jnp.zeros((margin, 128), F32)
     rows_ref[margin + bricks * tiles :] = jnp.zeros((margin, 128), F32)
-    rows = lax.broadcasted_iota(jnp.int32, (held, bricks), 0)
+    first = lax.axis_index("space") * held
+    rows = lax.broadcasted_iota(jnp.int32, (held, bricks), 0) + first
+    ids_copy.wait()
     hot = jnp.where(rows == ids_ref[...], 1.0, 0.0).astype(BF16)
+    latents_copy.wait()
     picked = dot_rows(hot, latents_ref[0])
     for tile in range(tiles):
         rows_ref[pl.ds(margin + tile, bricks, stride=tiles), :] = picked[:, tile * 128 : tile * 128 + 128]
@@ -57,16 +66,16 @@
 
 
 def build_band(band_ref, rows):
-    shape = (3 * CHANNELS, LINE)
+    shape = (3 * CHANNELS, HALF)
     row = lax.broadcasted_iota(jnp.int32, shape, 0)
     target = CHANNELS - (row // CHANNELS) * CHANNELS + row % CHANNELS
     distance = lanes_of(shape) - target
-    band_ref[:, LINE:, :] = jnp.zeros((9, 128, LINE), BF16)
-    places = [(z, z * CHANNELS) for z in range(EDGE)] + [(EDGE, LINE), (-1, WIDE - CHANNELS)]
-    for z, start in places:
+    band_ref[:, HALF:, :] = jnp.zeros((9, HALF, HALF), BF16)
+    for z in range(-1, 5):
         select = jnp.where(distance == z * CHANNELS, 1.0, 0.0).astype(BF16)
         block = dot(rows, select).astype(BF16)
-        band_ref[:, start : start + CHANNELS, :] = block.reshape(9, CHANNELS, LINE)
+        start = z % 8 * CHANNELS
+        band_ref[:, start : start + CHANNELS, :] = block.reshape(9, CHANNELS, HALF)
 
 
 def weight_rows(weights):
@@ -91,26 +100,31 @@
     build_band(back_ref, flipped_rows(weights))
 
 
-def put_padded(pad_ref, brick, volume, x_low, x_high, y_low, y_high, z_low, z_high):
-    lane = lanes_of((EDGE, EDGE, 128))
-    tail = jnp.where(lane < CHANNELS, z_high, jnp.where(lane >= 128 - CHANNELS, z_low, 0.0))
-    full = jnp.concatenate([volume, tail], axis=-1)
-    zeros = jnp.zeros((EDGE, 128), F32)
-    first = jnp.concatenate([x_low, zeros], axis=-1)[None]
-    last = jnp.concatenate([x_high, zeros], axis=-1)[None]
-    slabs = jnp.concatenate([first, full, last], axis=0)
-    no_halo = jnp.zeros((1, WIDE), F32)
-    low = jnp.concatenate([no_halo, jnp.concatenate([y_low, zeros], axis=-1), no_halo], axis=0)
-    high = jnp.concatenate([no_halo, jnp.concatenate([y_high, zeros], axis=-1), no_halo], axis=0)
-    row = lax.broadcasted_iota(jnp.int32, slabs.shape, 1)
-    pad_ref[0, brick] = jnp.where(row == 0, low[:, None, :], pltpu.roll(slabs, 1, 1))
-    pad_ref[1, brick] = slabs
-    pad_ref[2, brick] = jnp.where(row == EDGE - 1, high[:, None, :], pltpu.roll(slabs, EDGE - 1, 1))
+def put_padded(pad_ref, brick, lines, x_low, x_high, y_low, y_high, z_low, z_high):
+    def joined(halves, before, after):
+        lane = lanes_of(halves[0].shape)
+        first = jnp.where(lane < CHANNELS, halves[1], before)
+        second = jnp.where(lane >= HALF - CHANNELS, halves[0], after)
+        return jnp.concatenate([halves[0], first], axis=-1), jnp.concatenate([halves[1], second], axis=-1)
+
+    inside = joined(lines, z_low, z_high)
+    x_low, x_high, y_low, y_high = [joined(face, 0.0, 0.0) for face in (x_low, x_high, y_low, y_high)]
+    none = jnp.zeros((1, WIDE), F32)
+    shifted = [[], [], []]
+    for half in range(2):
+        slabs = jnp.concatenate([x_low[half][None], inside[half], x_high[half][None]], axis=0)
+        row = lax.broadcasted_iota(jnp.int32, slabs.shape, 1)
+        low = jnp.concatenate([none, y_low[half], none], axis=0)[:, None, :]
+        high = jnp.concatenate([none, y_high[half], none], axis=0)[:, None, :]
+        shifted[0].append(jnp.where(row == 0, low, pltpu.roll(slabs, 1, 1)))
+        shifted[1].append(slabs)
+        shifted[2].append(jnp.where(row == EDGE - 1, high, pltpu.roll(slabs, EDGE - 1, 1)))
+    for dy in range(3):
+        pad_ref[dy, brick] = jnp.concatenate(shifted[dy], axis=1).astype(BF16)
 
 
 def window(pad_ref, k):
-    lines = pad_ref[k % 3, :, k // 3 : k // 3 + EDGE]
-    return lines.reshape(LINES, WIDE).astype(BF16)
+    return pad_ref[k % 3, :, k // 3 : k // 3 + EDGE].reshape(ROWS, WIDE)
 
 
 def convolve(pad_ref, band_ref):
@@ -121,11 +135,30 @@
     return total
 
 
+def half_lines(values):
+    cube = values.reshape(BRICKS, EDGE, 2, EDGE, HALF)
+    return [(cube[brick, :, 0], cube[brick, :, 1]) for brick in range(BRICKS)]
+
+
+def put_halves(halves_ref, start, bricks):
+    for brick, lines in enumerate(bricks):
+        for half in range(2):
+            first = start + brick * CUBE
+            halves_ref[half, first : first + CUBE, :] = lines[half].reshape(CUBE, HALF)
+
+
+def cotangent_lines(cotangent_ref):
+    cube = cotangent_ref[...].astype(F32).reshape(BRICKS, EDGE, EDGE, LINE)
+    return [(cube[brick, :, :, :HALF], cube[brick, :, :, HALF:]) for brick in range(BRICKS)]
+
+
 def pack_faces(faces_ref, base, halves_ref, start, high):
-    first = start + ((EDGE - 1) * EDGE if high else 0)
-    faces_ref[base : base + EDGE] = lines(halves_ref, first, EDGE)
-    first = start + (EDGE - 1 if high else 0)
-    faces_ref[base + EDGE : base + 2 * EDGE] = lines(halves_ref, first, EDGE, EDGE)
+    x_face = pair(halves_ref, start + ((EDGE - 1) * EDGE if high else 0), EDGE)
+    y_face = pair(halves_ref, start + (EDGE - 1 if high else 0), EDGE, EDGE)
+    for half in range(2):
+        lanes = slice(half * HALF, half * HALF + HALF)
+        faces_ref[base : base + EDGE, lanes] = x_face[half]
+        faces_ref[base + EDGE : base + 2 * EDGE, lanes] = y_face[half]
     tile = halves_ref[1 if high else 0, start : start + CUBE, :]
     lane = lanes_of((16, 128)) // CHANNELS
     packed = jnp.zeros((16, 128), F32)
@@ -148,8 +181,8 @@
 
 def first_kernel(
     links_ref, received_ref, up_ref, band_ref, cotangent_ref,
-    lifted_out, pre_out, hidden_out, pad_out, high_out, low_out, far_out, near_out,
-    volumes_ref, pad_ref, lines_ref, high_ref, low_ref, rows_ref,
+    pre_out, hidden_out, pad_out, high_out, low_out, far_out, near_out,
+    volumes_ref, lines_ref, high_ref, low_ref, rows_ref,
 ):
     position = lax.axis_index("space")
     tiles = received_ref.shape[1] // (3 * BRICKS)
@@ -178,34 +211,28 @@
         def x_face(face):
             start, present = near(face)
             offset = EDGE * (EDGE - 1) if face % 2 == 0 else 0
-            return lines(volumes_ref, pl.multiple_of(start + offset, 8), EDGE) * present
+            return [half * present for half in pair(volumes_ref, pl.multiple_of(start + offset, 8), EDGE)]
 
         def y_face(face):
             start, present = near(face)
             offset = EDGE - 1 if face % 2 == 0 else 0
-            return lines(volumes_ref, start + offset, EDGE, EDGE) * present
+            return [half * present for half in pair(volumes_ref, start + offset, EDGE, EDGE)]
 
         def z_face(face):
             start, present = near(face)
             tile = volumes_ref[1 if face % 2 == 0 else 0, pl.ds(start, CUBE), :] * present
-            return tile.reshape(EDGE, EDGE, 128)
-
-        own = (BRICKS + brick) * CUBE
-        volume = lines(volumes_ref, own, CUBE).reshape(EDGE, EDGE, LINE)
-        put_padded(
-            pad_ref, brick, volume, x_face(0), x_face(1), y_face(2), y_face(3), z_face(4), z_face(5)
-        )
-    pre = convolve(pad_ref, band_ref)
+            return tile.reshape(EDGE, EDGE, HALF)
+
+        own = pair(volumes_ref, (BRICKS + brick) * CUBE, CUBE)
+        own = [half.reshape(EDGE, EDGE, HALF) for half in own]
+        put_padded(pad_out, brick, own, x_face(0), x_face(1), y_face(2), y_face(3), z_face(4), z_face(5))
+    pre = convolve(pad_out, band_ref)
     hidden = pre / (1.0 + jnp.exp(-pre))
     hidden = hidden.astype(BF16)
-    lifted_out[...] = lines(volumes_ref, BRICKS * CUBE, LINES).astype(BF16)
     pre_out[...] = pre
     hidden_out[...] = hidden
-    pad_out[...] = pad_ref[...].reshape(pad_out.shape).astype(BF16)
-    sources = (hidden.astype(F32), cotangent_ref[...].astype(F32).reshape(LINES, LINE))
-    for which, values in enumerate(sources):
-        for half in range(2):
-            lines_ref[half, which * LINES : which * LINES + LINES] = values[:, half * 128 : half * 128 + 128]
+    put_halves(lines_ref, 0, half_lines(hidden.astype(F32)))
+    put_halves(lines_ref, LINES, cotangent_lines(cotangent_ref))
     for which in range(2):
         for brick in range(BRICKS):
             base = (which * BRICKS + brick) * FACE
@@ -221,17 +248,13 @@
     near_out[...] = jnp.where(even, high, low)
 
 
-def fold_diagonals(outer_ref, part):
+def fold(outer_ref, places):
     lane = lanes_of((CHANNELS, 128)) // CHANNELS
     folded = None
-    for half in range(2):
-        picked = None
-        for block in range(4):
-            depth = 4 * half + block + part - 1
-            start = depth * CHANNELS if 0 <= depth < EDGE else (LINE if depth == EDGE else WIDE - CHANNELS)
-            rows = outer_ref[start : start + CHANNELS, half * 128 : half * 128 + 128]
-            picked = rows if picked is None else jnp.where(lane == block, rows, picked)
-        folded = picked if folded is None else folded + picked
+    for block in range(4):
+        start, tile = places[block]
+        rows = outer_ref[start : start + CHANNELS, tile * 128 : tile * 128 + 128]
+        folded = rows if folded is None else jnp.where(lane == block, rows, folded)
     quarter = [folded[8 * q : 8 * q + 8] for q in range(4)]
     small = lanes_of((8, 128)) // CHANNELS
     total = None
@@ -245,7 +268,15 @@
     return total
 
 
-def padded_brick(pad_ref, brick, which, values, links_ref, high_ref, low_ref):
+def diagonal(shift):
+    places = [None] * 4
+    for z in range(4):
+        other = z + shift
+        places[other % 4] = (z * CHANNELS, 0 if 0 <= other < 4 else 1)
+    return places
+
+
+def padded_brick(pad_ref, brick, which, lines, links_ref, high_ref, low_ref):
     position = lax.axis_index("space")
     half = high_ref.shape[0] // 2
 
@@ -258,9 +289,12 @@
         present = jnp.where(link >= 0, 1.0, 0.0).astype(F32)
         return pool[pl.ds(pl.multiple_of(start, 8), EDGE), :] * present
 
-    volume = values[brick * CUBE : brick * CUBE + CUBE].reshape(EDGE, EDGE, LINE)
+    def face(number, axis):
+        found = rows(number, axis)
+        return found[:, :HALF], found[:, HALF:]
+
     put_padded(
-        pad_ref, brick, volume, rows(0, 0), rows(1, 0), rows(2, 1), rows(3, 1),
+        pad_ref, brick, lines, face(0, 0), face(1, 0), face(2, 1), face(3, 1),
         unpack_depth(rows(4, 2), True), unpack_depth(rows(5, 2), False),
     )
 
@@ -275,37 +309,55 @@
 
 
 def second_kernel(
-    links_ref, cotangent_ref, band_ref, back_ref, lifted_ref, pre_ref, hidden_ref, pad_in,
+    links_ref, cotangent_ref, band_ref, back_ref, pre_ref, hidden_ref, lifted_pad,
     high_own, low_own, far, near,
     fine_out, sums_out,
-    high_ref, low_ref, hidden_pad, cotangent_pad, lifted_pad, outer_ref, sums_ref,
+    high_ref, low_ref, hidden_pad, cotangent_pad, one_ref, two_ref, sums_ref,
 ):
     fill_pools(high_ref, low_ref, high_own, low_own, far, near)
-    lifted_pad[...] = pad_in[...].astype(F32).reshape(lifted_pad.shape)
-    cotangent = cotangent_ref[...].astype(F32).reshape(LINES, LINE)
     hidden = hidden_ref[...].astype(F32)
-    for which, values, pad_ref in ((0, hidden, hidden_pad), (1, cotangent, cotangent_pad)):
+    sources = (half_lines(hidden), cotangent_lines(cotangent_ref))
+    for which, pad_ref in ((0, hidden_pad), (1, cotangent_pad)):
         for brick in range(BRICKS):
-            padded_brick(pad_ref, brick, which, values, links_ref, high_ref, low_ref)
-    fine = lifted_ref[...].astype(F32) + convolve(hidden_pad, band_ref)
+            padded_brick(pad_ref, brick, which, sources[which][brick], links_ref, high_ref, low_ref)
+    lifted = window(lifted_pad, 4)[:, :HALF].astype(F32)
+    fine = (lifted + convolve(hidden_pad, band_ref)).reshape(LINES // EDGE, 2, EDGE, HALF)
+    fine = jnp.concatenate([fine[:, 0], fine[:, 1]], axis=-1)
     fine_out[...] = fine.astype(BF16).reshape(fine_out.shape)
     back = convolve(cotangent_pad, back_ref)
     pre = pre_ref[...]
     sigmoid = 1.0 / (1.0 + jnp.exp(-pre))
     gradient = (back * sigmoid * (1.0 + pre * (1.0 - sigmoid))).astype(BF16)
-    upstream = cotangent.astype(BF16)
+    gradient = jnp.transpose(gradient.astype(F32)).astype(BF16)
+    hidden = jnp.transpose(hidden).astype(BF16)
     sums_ref[8 * BLOCKS :] = jnp.zeros((sums_ref.shape[0] - 8 * BLOCKS, 128), F32)
-    for base, pad_ref, right in ((0, lifted_pad, gradient), (27, hidden_pad, upstream)):
-        for k in range(9):
-            outer_ref[...] = dot_rows(window(pad_ref, k), right)
-            for part in range(3):
-                start = 8 * (base + 3 * k + part)
-                sums_ref[start : start + 8] = fold_diagonals(outer_ref, part)
+    for k in range(9):
+        one_ref[...] = dot(gradient, window(lifted_pad, k))
+        two_ref[...] = dot(hidden, window(cotangent_pad, 8 - k))
+        for part in range(3):
+            start = 8 * (3 * k + part)
+            sums_ref[start : start + 8] = fold(one_ref, diagonal(part - 1))
+            start += 8 * 27
+            sums_ref[start : start + 8] = fold(two_ref, diagonal(1 - part))
     sums_out[...] = sums_ref[...].astype(BF16).reshape(sums_out.shape)
+
+
+def unpacked(tile):
+    pieces = [tile] + [pltpu.roll(tile, 128 - q * CHANNELS, 1) for q in range(1, 4)]
+    return jnp.concatenate(pieces, axis=0)[:, :CHANNELS]
 
 
 def sum_kernel(scale, parts_ref, out_ref):
     total = jnp.sum(parts_ref[...].astype(F32), axis=0) * scale
+    per = parts_ref.shape[1] // 8
+    device = lax.axis_index("space") * lax.axis_size("dp") + lax.axis_index("dp")
+    tiles = []
+    for j in range(per):
+        tile = total[8 * j : 8 * j + 8]
+        block = jnp.transpose(unpacked(tile))
+        turned = jnp.concatenate([block[8 * q : 8 * q + 8] for q in range(4)], axis=1)
+        tiles.append(jnp.where(device * per + j < 27, turned, tile))
+    total = jnp.concatenate(tiles, axis=0)
     out_ref[...] = jnp.broadcast_to(total.astype(BF16)[None], out_ref.shape)
 
 
@@ -319,8 +371,8 @@
             out[index % 27, 8 * q : 8 * q + 8, :] = moved[:, :CHANNELS]
 
 
-def call(kernel, out_shape, scratch=(), smem=(), inputs=1, limit=24, cost=None):
-    spaces = [pltpu.SMEM if i in smem else pltpu.VMEM for i in range(inputs)]
+def call(kernel, out_shape, scratch=(), smem=(), hbm=(), inputs=1, limit=24, cost=None):
+    spaces = [pltpu.SMEM if i in smem else pl.ANY if i in hbm else pltpu.VMEM for i in range(inputs)]
     return pl.pallas_call(
         kernel,
         out_shape=out_shape,
@@ -350,24 +402,30 @@
     packed = call(
         functools.partial(pick_kernel, devices),
         shape(devices, 3 * BRICKS * tiles, 128),
-        [pltpu.VMEM(((bricks + 16) * tiles, 128), F32)],
+        [
+            pltpu.VMEM((1, bricks), jnp.int32),
+            pltpu.VMEM((1, held, width), BF16),
+            pltpu.VMEM(((bricks + 16) * tiles, 128), F32),
+            pltpu.SemaphoreType.DMA((2,)),
+        ],
+        hbm=(0, 1),
         inputs=2,
-    )(active_blocks - lax.axis_index("space") * held, coarse_latents)
+        limit=60,
+    )(active_blocks, coarse_latents)
     received = lax.all_to_all(packed, "space", split_axis=0, concat_axis=0, tiled=True)
-    band = shape(9, WIDE, LINE)
+    band = shape(9, WIDE, HALF)
     cost = pl.CostEstimate(flops=10**9, bytes_accessed=2 * 10**6, transcendentals=0)
     band_one = call(band_kernel, band, cost=cost)(conv_one)
     band_two, band_back = call(two_bands_kernel, (band, band), cost=cost)(conv_two)
-    pad_shape = (3, BRICKS, EDGE + 2, EDGE, WIDE)
-    pad = pltpu.VMEM(pad_shape, F32)
+    pad_shape = (3, BRICKS, EDGE + 2, 2 * EDGE, WIDE)
+    pad = pltpu.VMEM(pad_shape, BF16)
     packed_faces = 2 * BRICKS * FACE
-    lifted, pre, hidden, lifted_pad, high, low, far, near = call(
+    pre, hidden, lifted_pad, high, low, far, near = call(
         first_kernel,
         (
-            shape(LINES, LINE),
-            shape(LINES, LINE, dtype=F32),
-            shape(LINES, LINE),
-            shape(math.prod(pad_shape[:-1]), WIDE),
+            shape(ROWS, HALF, dtype=F32),
+            shape(ROWS, HALF),
+            shape(*pad_shape),
             shape(packed_faces, LINE),
             shape(packed_faces, LINE),
             shape(packed_faces, LINE),
@@ -375,7 +433,6 @@
         ),
         [
             pltpu.VMEM((2, 8 * CUBE, 128), F32),
-            pad,
             pltpu.VMEM((2, 2 * LINES, 128), F32),
             pltpu.VMEM((packed_faces, LINE), F32),
             pltpu.VMEM((packed_faces, LINE), F32),
@@ -396,14 +453,14 @@
             pltpu.VMEM((2 * packed_faces, LINE), F32),
             pad,
             pad,
-            pad,
-            pltpu.VMEM((WIDE, LINE), F32),
+            pltpu.VMEM((HALF, WIDE), F32),
+            pltpu.VMEM((HALF, WIDE), F32),
             pltpu.VMEM((everyone * per * 8, 128), F32),
         ],
         smem=(0,),
-        inputs=12,
+        inputs=11,
     )(
-        face_links, cotangent, band_two, band_back, lifted, pre, hidden, lifted_pad,
+        face_links, cotangent, band_two, band_back, pre, hidden, lifted_pad,
         high, low, far, near,
     )
     axes = ("space", "dp")

time: 53.3 us -> 52.2 us (0.979)
  local copies, waits for them, and re-layouts: 1.79 us -> 0.03 us
  waiting for transfers between devices: 7.58 us -> 9.16 us
  other arithmetic: 0.66 us -> 0 us
    unnamed x12 -> x10, local copies, waits for them, and re-layouts: 1.79 us -> 0.03 us
    all_to_all x1, waiting for transfers between devices: 6.1 us -> 7.27 us  [body(): lax.all_to_all(packed, 'space', split_axis=0, concat_axis=0, tiled=True)]
    pallas_call x1, Pallas kernels: 0.83 us -> 1.74 us  [body(): call(functools.partial(pick_kernel, devices), shape(devices, 3 * BRICKS *...]
    sub x1 -> x0, other arithmetic: 0.66 us -> none  [body(): active_blocks - lax.axis_index('space') * held]
    pallas_call x1, Pallas kernels: 3.23 us -> 2.58 us  [body(): call(second_kernel, (shape(*cotangent.shape), shape(everyone, per * 8, 12...]
  transfers between devices with their start and end apart: 3 -> 3, of which waited for: 2 -> 2; matrix products, arithmetic and copies ran while one was open for 0% -> 0% of each run, Pallas kernels for 3% -> 2%
where the time goes in v7:
time: 52.2 us; the launch traced here: 52 us
  blocking collectives  21.3 us (41%)
  starting transfers between devices  12.5 us (24%)
  waiting for transfers between devices  9.16 us (18%)
  Pallas kernels  8.31 us (16%)
  between operations  0.75 us (1%)
    all_to_all x1, blocking collectives, body(): parts = lax.all_to_all(sums, axes, split_axis=0, concat_axis=0, tiled=True)  11.3 us
    all_to_all x1, blocking collectives, body(): lax.all_to_all(total, axes, split_axis=0, concat_axis=0, tiled=True)  10 us
    all_to_all x1, starting transfers between devices, body(): lax.all_to_all(packed, 'space', split_axis=0, concat_axis=0, tiled=True)  8.32 us
    all_to_all x1, waiting for transfers between devices, body(): lax.all_to_all(packed, 'space', split_axis=0, concat_axis=0, tiled=True)  7.27 us
    ppermute x2, starting transfers between devices, swapped(): lax.ppermute(value, 'space', pairs + [(target, source) for source, target...  4.13 us
    pallas_call x1, Pallas kernels, body(): call(second_kernel, (shape(*cotangent.shape), shape(everyone, per * 8, 12...  2.58 us
    ppermute x2, waiting for transfers between devices, swapped(): lax.ppermute(value, 'space', pairs + [(target, source) for source, target...  1.9 us
    pallas_call x1, Pallas kernels, body(): call(first_kernel, (shape(ROWS, HALF, dtype=F32), shape(ROWS, HALF), shap...  1.79 us
  transfers between devices with their start and end apart: 3, of which 2 were waited for; matrix products, arithmetic and copies ran while one was open for 0% of the time, Pallas kernels for 2%

profile of v7, /device:TPU:0, one launch (start us, length us, event | category | flops | bytes accessed | tf_op | source)
XLA Modules:
  0.0 52.0 jit_solution(9865239737362999769)
XLA Ops:
  0.6 0.0 copy-start.3
  0.6 1.7 %shard_map.95 = bf16[16,24,128]{2,1,0:T(8,128)(2,1)} custom-call(s32[1,32]{1,0:T(1,128)} %ids_hbm.1, bf16[1,64,512]{2,1,0:T(8,128)(2,1)} %latents_hbm.1), custom_call_target="tpu_custom_call" | custom-call | tf_op jit(solution)/shard_map/pallas_call | solution.py:402
  2.4 8.3 %all-to-all-start = ((bf16[16,24,128]{2,1,0:T(8,128)(2,1)}), bf16[16,24,128]{2,1,0:T(8,128)(2,1)S(1)}, u32[]{:S(2)}, u32[]{:S(2)}) async-start(bf16[16,24,128]{2,1,0:T(8,128)(2,1)} %shard_map.95), calls=%async_computation | async-start | bytes 196608 | tf_op jit(solution)/shard_map/all_to_all | solution.py:415
  10.7 0.0 copy-done.3
  10.7 0.0 copy-start
  10.7 0.0 copy-start.1
  10.8 0.0 copy-start.2
  10.8 0.3 shard_map.96.band_ref
  11.1 0.0 copy-start.4
  11.1 7.3 %all-to-all-done.received_ref = bf16[16,24,128]{2,1,0:T(8,128)(2,1)S(1)} async-done(((bf16[16,24,128]{2,1,0:T(8,128)(2,1)}), bf16[16,24,128]{2,1,0:T(8,128)(2,1)S(1)}, u32[]{:S(2)}, u32[]{:S(2)}) %all-to-all-start) | async-done | bytes 98336 | tf_op jit(solution)/shard_map/all_to_all | solution.py:415
  18.4 0.0 copy-done
  18.4 0.0 copy-done.1
  18.4 0.0 copy-done.2
  18.4 1.8 %shard_map.97 = (f32[256,128]{1,0:T(8,128)S(1)}, bf16[256,128]{1,0:T(8,128)(2,1)S(1)}, bf16[3,2,10,16,256]{4,3,2,1,0:T(8,128)(2,1)S(1)}, bf16[96,256]{1,0:T(8,12...) custom-call(s32[1,2,6]{2,1,0:T(2,128)S(1)} %copy-done.2, ...), custom_call_target="tpu_custom_call" | custom-call | tf_op jit(solution)/shard_map/pallas_call | solution.py:423
  20.2 0.7 %collective-permute-start = (bf16[96,256]{1,0:T(8,128)(2,1)S(1)}, bf16[96,256]{1,0:T(8,128)(2,1)S(1)}, u32[]{:S(2)}, u32[]{:S(2)}) collective-permute-start(bf16[96,256]{1,0:T(8,128)(2,1)S(1)} %get-tuple-element.23), channel_id=1, source_target_pairs={{2,4},{6,8},{10,12},{14,16},{18,20},{22,24},{26,28},{4,2},{8,6},{1... | collective-permute-start | bytes 147464 | tf_op jit(solution)/shard_map/ppermute | solution.py:393
  20.9 3.5 %collective-permute-start.1 = (bf16[96,256]{1,0:T(8,128)(2,1)S(1)}, bf16[96,256]{1,0:T(8,128)(2,1)S(1)}, u32[]{:S(2)}, u32[]{:S(2)}) collective-permute-start(bf16[96,256]{1,0:T(8,128)(2,1)S(1)} %get-tuple-element.24), channel_id=1, source_target_pairs={{0,2},{4,6},{8,10},{12,14},{16,18},{20,22},{24,26},{28,30},{2,0},{... | collective-permute-start | bytes 147464 | tf_op jit(solution)/shard_map/ppermute | solution.py:393
  24.3 0.6 %shard_map.94 = (bf16[9,256,128]{2,1,0:T(8,128)(2,1)S(1)}, bf16[9,256,128]{2,1,0:T(8,128)(2,1)S(1)}) custom-call(bf16[27,32,32]{2,1,0:T(8,128)(2,1)S(1)} %copy-done.4), custom_call_target="tpu_custom_call" | custom-call | flops 1000000000 | bytes 2000000 | tf_op jit(solution)/shard_map/pallas_call | solution.py:419
  24.9 0.0 collective-permute-done.far
  24.9 1.9 %collective-permute-done.1.near = bf16[96,256]{1,0:T(8,128)(2,1)S(1)} collective-permute-done((bf16[96,256]{1,0:T(8,128)(2,1)S(1)}, bf16[96,256]{1,0:T(8,128)(2,1)S(1)}, u32[]{:S(2)}, u32[]{:S(2)}) %collective-permute-start.1) | collective-permute-done | bytes 49184 | tf_op jit(solution)/shard_map/ppermute | solution.py:393
  26.8 2.6 %shard_map.98 = (bf16[1,2,8,8,256]{4,3,2,1,0:T(8,128)(2,1)}, bf16[32,16,128]{2,1,0:T(8,128)(2,1)S(1)}) custom-call(s32[1,2,6]{2,1,0:T(2,128)S(1)} %copy-done.2, bf16[1,2,8,8,256]{4,3,2,1,0:T(8,128)(2,1)S(1)} %copy-done.1, bf16[9,256,128]{2,1,0:T(8,128)(2,1)S(1)} %get-tuple-element.16.band_ref, bf16[9,256,128]{2,1,0:T(8,128)(2,1)S(1)} %get-tuple-element.17.back_ref, ...), custom_call_target="tpu_custom_call" | custom-call | tf_op jit(solution)/shard_map/pallas_call | solution.py:448
  29.4 11.3 %all_to_all.15.parts_ref = bf16[32,16,128]{2,1,0:T(8,128)(2,1)S(1)} all-to-all(bf16[32,16,128]{2,1,0:T(8,128)(2,1)S(1)} %get-tuple-element.26), channel_id=1, replica_groups=mesh['space'=16,'dp'=2] {'space','dp'}, dimensions={0} | all-to-all | bytes 262144 | tf_op jit(solution)/shard_map/all_to_all | solution.py:467
  40.7 0.3 shard_map.99
  40.9 10.0 %all_to_all.16.sums_ref = bf16[32,16,128]{2,1,0:T(8,128)(2,1)S(1)} all-to-all(bf16[32,16,128]{2,1,0:T(8,128)(2,1)S(1)} %shard_map.99), channel_id=1, replica_groups=mesh['space'=16,'dp'=2] {'space','dp'}, dimensions={0} | all-to-all | bytes 262144 | tf_op jit(solution)/shard_map/all_to_all | solution.py:470
  50.9 1.0 %shard_map.100 = (f32[27,32,32]{2,1,0:T(8,128)}, f32[27,32,32]{2,1,0:T(8,128)}) custom-call(bf16[32,16,128]{2,1,0:T(8,128)(2,1)S(1)} %all_to_all.16.sums_ref), custom_call_target="tpu_custom_call" | custom-call | tf_op jit(solution)/shard_map/pallas_call | solution.py:473
  (1 shorter events, 0.0 us)
Async XLA Ops:
  0.6 10.1 %copy-start.3 = (bf16[27,32,32]{2,1,0:T(8,128)(2,1)S(1)}, bf16[27,32,32]{2,1,0:T(8,128)(2,1)}, u32[]{:S(2)}) copy-start(bf16[27,32,32]{2,1,0:T(8,128)(2,1)} %weights_ref.3) | copy-start | bytes 165892
  2.4 16.0 %all-to-all-start = ((bf16[16,24,128]{2,1,0:T(8,128)(2,1)}), bf16[16,24,128]{2,1,0:T(8,128)(2,1)S(1)}, u32[]{:S(2)}, u32[]{:S(2)}) async-start(bf16[16,24,128]{2,1,0:T(8,128)(2,1)} %shard_map.95), calls=%async_computation | async-start | bytes 196608 | tf_op jit(solution)/shard_map/all_to_all | solution.py:415
  10.7 7.7 %copy-start = (bf16[64,2048]{1,0:T(8,128)(2,1)S(1)}, bf16[64,2048]{1,0:T(8,128)(2,1)}, u32[]{:S(2)}) copy-start(bf16[64,2048]{1,0:T(8,128)(2,1)} %up_ref.1) | copy-start | bytes 786436
  10.7 7.6 %copy-start.1 = (bf16[1,2,8,8,256]{4,3,2,1,0:T(8,128)(2,1)S(1)}, bf16[1,2,8,8,256]{4,3,2,1,0:T(8,128)(2,1)}, u32[]{:S(2)}) copy-start(bf16[1,2,8,8,256]{4,3,2,1,0:T(8,128)(2,1)} %cotangent_ref.3) | copy-start | bytes 196612
  10.8 7.6 %copy-start.2 = (s32[1,2,6]{2,1,0:T(2,128)S(1)}, s32[1,2,6]{2,1,0:T(2,128)}, u32[]{:S(2)}) copy-start(s32[1,2,6]{2,1,0:T(2,128)} %links_ref.3) | copy-start | bytes 148
  11.1 13.2 %copy-start.4 = (bf16[27,32,32]{2,1,0:T(8,128)(2,1)S(1)}, bf16[27,32,32]{2,1,0:T(8,128)(2,1)}, u32[]{:S(2)}) copy-start(bf16[27,32,32]{2,1,0:T(8,128)(2,1)} %weights_ref.2) | copy-start | bytes 165892
  20.2 4.7 %collective-permute-start = (bf16[96,256]{1,0:T(8,128)(2,1)S(1)}, bf16[96,256]{1,0:T(8,128)(2,1)S(1)}, u32[]{:S(2)}, u32[]{:S(2)}) collective-permute-start(bf16[96,256]{1,0:T(8,128)(2,1)S(1)} %get-tuple-element.23), channel_id=1, source_target_pairs={{2,4},{6,8},{10,12},{14,16},{18,20},{22,24},{26,28},{4,2},{8,6},{1... | collective-permute-start | bytes 147464 | tf_op jit(solution)/shard_map/ppermute | solution.py:393
  20.9 6.0 %collective-permute-start.1 = (bf16[96,256]{1,0:T(8,128)(2,1)S(1)}, bf16[96,256]{1,0:T(8,128)(2,1)S(1)}, u32[]{:S(2)}, u32[]{:S(2)}) collective-permute-start(bf16[96,256]{1,0:T(8,128)(2,1)S(1)} %get-tuple-element.24), channel_id=1, source_target_pairs={{0,2},{4,6},{8,10},{12,14},{16,18},{20,22},{24,26},{28,30},{2,0},{... | collective-permute-start | bytes 147464 | tf_op jit(solution)/shard_map/ppermute | solution.py:393

commit v8 on v7

--- a/solution.py
+++ b/solution.py
@@ -94,10 +94,9 @@
     build_band(band_ref, weight_rows(weights_ref[...].astype(F32)))
 
 
-def two_bands_kernel(weights_ref, band_ref, back_ref):
-    weights = weights_ref[...].astype(F32)
-    build_band(band_ref, weight_rows(weights))
-    build_band(back_ref, flipped_rows(weights))
+def bands_kernel(one_ref, two_ref, band_ref, back_ref):
+    build_band(band_ref, weight_rows(one_ref[...].astype(F32)))
+    build_band(back_ref, flipped_rows(two_ref[...].astype(F32)))
 
 
 def put_padded(pad_ref, brick, lines, x_low, x_high, y_low, y_high, z_low, z_high):
@@ -170,6 +169,25 @@
     faces_ref[base + 2 * EDGE : base + FACE, 128:] = packed[8:]
 
 
+def pack_all(bricks, halves_ref, faces_ref, high_out, low_out, far_out, near_out):
+    put_halves(halves_ref, 0, bricks)
+    packed = []
+    for high in (True, False):
+        for brick in range(BRICKS):
+            pack_faces(faces_ref, brick * FACE, halves_ref, brick * CUBE, high)
+        packed.append(faces_ref[...].astype(BF16))
+    high, low = packed
+    high_out[...] = high
+    low_out[...] = low
+    even = lax.axis_index("space") % 2 == 0
+    far_out[...] = jnp.where(even, low, high)
+    near_out[...] = jnp.where(even, high, low)
+
+
+def faces_kernel(cotangent_ref, high_out, low_out, far_out, near_out, halves_ref, faces_ref):
+    pack_all(cotangent_lines(cotangent_ref), halves_ref, faces_ref, high_out, low_out, far_out, near_out)
+
+
 def unpack_depth(rows, high):
     packed = jnp.concatenate([rows[:, :128], rows[:, 128:]], axis=0)
     pieces = []
@@ -180,9 +198,9 @@
 
 
 def first_kernel(
-    links_ref, received_ref, up_ref, band_ref, cotangent_ref,
-    pre_out, hidden_out, pad_out, high_out, low_out, far_out, near_out,
-    volumes_ref, lines_ref, high_ref, low_ref, rows_ref,
+    links_ref, received_ref, up_ref, band_ref,
+    pre_out, hidden_out, pad_out,
+    volumes_ref, rows_ref,
 ):
     position = lax.axis_index("space")
     tiles = received_ref.shape[1] // (3 * BRICKS)
@@ -231,21 +249,6 @@
     hidden = hidden.astype(BF16)
     pre_out[...] = pre
     hidden_out[...] = hidden
-    put_halves(lines_ref, 0, half_lines(hidden.astype(F32)))
-    put_halves(lines_ref, LINES, cotangent_lines(cotangent_ref))
-    for which in range(2):
-        for brick in range(BRICKS):
-            base = (which * BRICKS + brick) * FACE
-            start = which * LINES + brick * CUBE
-            pack_faces(high_ref, base, lines_ref, start, True)
-            pack_faces(low_ref, base, lines_ref, start, False)
-    high = high_ref[...].astype(BF16)
-    low = low_ref[...].astype(BF16)
-    high_out[...] = high
-    low_out[...] = low
-    even = position % 2 == 0
-    far_out[...] = jnp.where(even, low, high)
-    near_out[...] = jnp.where(even, high, low)
 
 
 def fold(outer_ref, places):
@@ -276,60 +279,50 @@
     return places
 
 
-def padded_brick(pad_ref, brick, which, lines, links_ref, high_ref, low_ref):
+def pad_all(pad_ref, bricks, links_ref, high_pool, low_pool, high_own, low_own, far, near):
     position = lax.axis_index("space")
-    half = high_ref.shape[0] // 2
-
-    def rows(face, axis):
-        link = links_ref[0, brick, face]
-        high = face % 2 == 0
-        index = jnp.clip(link - BRICKS * (position - 1 if high else position), 0, 2 * BRICKS - 1)
-        start = (index // BRICKS) * half + (which * BRICKS + index % BRICKS) * FACE + axis * EDGE
-        pool = high_ref if high else low_ref
-        present = jnp.where(link >= 0, 1.0, 0.0).astype(F32)
-        return pool[pl.ds(pl.multiple_of(start, 8), EDGE), :] * present
-
-    def face(number, axis):
-        found = rows(number, axis)
-        return found[:, :HALF], found[:, HALF:]
-
-    put_padded(
-        pad_ref, brick, lines, face(0, 0), face(1, 0), face(2, 1), face(3, 1),
-        unpack_depth(rows(4, 2), True), unpack_depth(rows(5, 2), False),
-    )
-
-
-def fill_pools(high_ref, low_ref, high_own, low_own, far, near):
-    half = 2 * BRICKS * FACE
-    even = lax.axis_index("space") % 2 == 0
-    high_ref[0:half] = jnp.where(even, far[...], near[...]).astype(F32)
-    high_ref[half:] = high_own[...].astype(F32)
-    low_ref[0:half] = low_own[...].astype(F32)
-    low_ref[half:] = jnp.where(even, near[...], far[...]).astype(F32)
+    half = BRICKS * FACE
+    even = position % 2 == 0
+    high_pool[0:half] = jnp.where(even, far[...], near[...]).astype(F32)
+    high_pool[half:] = high_own[...].astype(F32)
+    low_pool[0:half] = low_own[...].astype(F32)
+    low_pool[half:] = jnp.where(even, near[...], far[...]).astype(F32)
+    for brick, lines in enumerate(bricks):
+
+        def rows(face, axis):
+            link = links_ref[0, brick, face]
+            high = face % 2 == 0
+            index = jnp.clip(link - BRICKS * (position - 1 if high else position), 0, 2 * BRICKS - 1)
+            pool = high_pool if high else low_pool
+            present = jnp.where(link >= 0, 1.0, 0.0).astype(F32)
+            return pool[pl.ds(pl.multiple_of(index * FACE + axis * EDGE, 8), EDGE), :] * present
+
+        def face(number, axis):
+            found = rows(number, axis)
+            return found[:, :HALF], found[:, HALF:]
+
+        put_padded(
+            pad_ref, brick, lines, face(0, 0), face(1, 0), face(2, 1), face(3, 1),
+            unpack_depth(rows(4, 2), True), unpack_depth(rows(5, 2), False),
+        )
 
 
 def second_kernel(
-    links_ref, cotangent_ref, band_ref, back_ref, pre_ref, hidden_ref, lifted_pad,
-    high_own, low_own, far, near,
-    fine_out, sums_out,
-    high_ref, low_ref, hidden_pad, cotangent_pad, one_ref, two_ref, sums_ref,
+    links_ref, cotangent_ref, band_ref, pre_ref, hidden_ref, lifted_pad, high_own, low_own, far, near,
+    sums_out, lifted_out, high_out, low_out, far_out, near_out,
+    high_pool, low_pool, cotangent_pad, one_ref, two_ref, sums_ref, halves_ref, faces_ref,
 ):
-    fill_pools(high_ref, low_ref, high_own, low_own, far, near)
     hidden = hidden_ref[...].astype(F32)
-    sources = (half_lines(hidden), cotangent_lines(cotangent_ref))
-    for which, pad_ref in ((0, hidden_pad), (1, cotangent_pad)):
-        for brick in range(BRICKS):
-            padded_brick(pad_ref, brick, which, sources[which][brick], links_ref, high_ref, low_ref)
-    lifted = window(lifted_pad, 4)[:, :HALF].astype(F32)
-    fine = (lifted + convolve(hidden_pad, band_ref)).reshape(LINES // EDGE, 2, EDGE, HALF)
-    fine = jnp.concatenate([fine[:, 0], fine[:, 1]], axis=-1)
-    fine_out[...] = fine.astype(BF16).reshape(fine_out.shape)
-    back = convolve(cotangent_pad, back_ref)
+    pack_all(half_lines(hidden), halves_ref, faces_ref, high_out, low_out, far_out, near_out)
+    lifted_out[...] = window(lifted_pad, 4)[:, :HALF]
     pre = pre_ref[...]
     sigmoid = 1.0 / (1.0 + jnp.exp(-pre))
-    gradient = (back * sigmoid * (1.0 + pre * (1.0 - sigmoid))).astype(BF16)
+    slope = sigmoid * (1.0 + pre * (1.0 - sigmoid))
+    hidden = jnp.transpose(hidden).astype(BF16)
+    bricks = cotangent_lines(cotangent_ref)
+    pad_all(cotangent_pad, bricks, links_ref, high_pool, low_pool, high_own, low_own, far, near)
+    gradient = (convolve(cotangent_pad, band_ref) * slope).astype(BF16)
     gradient = jnp.transpose(gradient.astype(F32)).astype(BF16)
-    hidden = jnp.transpose(hidden).astype(BF16)
     sums_ref[8 * BLOCKS :] = jnp.zeros((sums_ref.shape[0] - 8 * BLOCKS, 128), F32)
     for k in range(9):
         one_ref[...] = dot(gradient, window(lifted_pad, k))
@@ -342,12 +335,24 @@
     sums_out[...] = sums_ref[...].astype(BF16).reshape(sums_out.shape)
 
 
+def fine_kernel(
+    links_ref, band_ref, lifted_ref, hidden_ref, high_own, low_own, far, near,
+    fine_out, high_pool, low_pool, hidden_pad,
+):
+    bricks = half_lines(hidden_ref[...].astype(F32))
+    pad_all(hidden_pad, bricks, links_ref, high_pool, low_pool, high_own, low_own, far, near)
+    fine = lifted_ref[...].astype(F32) + convolve(hidden_pad, band_ref)
+    fine = fine.reshape(LINES // EDGE, 2, EDGE, HALF)
+    fine = jnp.concatenate([fine[:, 0], fine[:, 1]], axis=-1)
+    fine_out[...] = fine.astype(BF16).reshape(fine_out.shape)
+
+
 def unpacked(tile):
     pieces = [tile] + [pltpu.roll(tile, 128 - q * CHANNELS, 1) for q in range(1, 4)]
     return jnp.concatenate(pieces, axis=0)[:, :CHANNELS]
 
 
-def sum_kernel(scale, parts_ref, out_ref):
+def sum_kernel(scale, parts_ref, _, out_ref):
     total = jnp.sum(parts_ref[...].astype(F32), axis=0) * scale
     per = parts_ref.shape[1] // 8
     device = lax.axis_index("space") * lax.axis_size("dp") + lax.axis_index("dp")
@@ -415,58 +420,44 @@
     received = lax.all_to_all(packed, "space", split_axis=0, concat_axis=0, tiled=True)
     band = shape(9, WIDE, HALF)
     cost = pl.CostEstimate(flops=10**9, bytes_accessed=2 * 10**6, transcendentals=0)
-    band_one = call(band_kernel, band, cost=cost)(conv_one)
-    band_two, band_back = call(two_bands_kernel, (band, band), cost=cost)(conv_two)
+    face = shape(BRICKS * FACE, LINE)
+    halves = pltpu.VMEM((2, LINES, HALF), F32)
+    faces = pltpu.VMEM((BRICKS * FACE, LINE), F32)
+    pool = pltpu.VMEM((2 * BRICKS * FACE, LINE), F32)
+    volume = shape(ROWS, HALF)
     pad_shape = (3, BRICKS, EDGE + 2, 2 * EDGE, WIDE)
     pad = pltpu.VMEM(pad_shape, BF16)
-    packed_faces = 2 * BRICKS * FACE
-    pre, hidden, lifted_pad, high, low, far, near = call(
-        first_kernel,
-        (
-            shape(ROWS, HALF, dtype=F32),
-            shape(ROWS, HALF),
-            shape(*pad_shape),
-            shape(packed_faces, LINE),
-            shape(packed_faces, LINE),
-            shape(packed_faces, LINE),
-            shape(packed_faces, LINE),
-        ),
-        [
-            pltpu.VMEM((2, 8 * CUBE, 128), F32),
-            pltpu.VMEM((2, 2 * LINES, 128), F32),
-            pltpu.VMEM((packed_faces, LINE), F32),
-            pltpu.VMEM((packed_faces, LINE), F32),
-            pltpu.VMEM((8 * tiles, 128), F32),
-        ],
-        smem=(0,),
-        inputs=5,
-    )(face_links, received, up_weight, band_one, cotangent)
+    high, low, far, near = call(faces_kernel, (face,) * 4, [halves, faces])(cotangent)
     far = swapped(far, 1)
     near = swapped(near, 0)
+    band_one, band_back = call(bands_kernel, (band, band), inputs=2, cost=cost)(conv_one, conv_two)
+    pre, hidden, lifted_pad = call(
+        first_kernel,
+        (shape(ROWS, HALF, dtype=F32), volume, shape(*pad_shape)),
+        [pltpu.VMEM((2, 8 * CUBE, 128), F32), pltpu.VMEM((8 * tiles, 128), F32)],
+        smem=(0,),
+        inputs=4,
+    )(face_links, received, up_weight, band_one)
     per = -(-BLOCKS // everyone)
     per += per % 2
-    fine, sums = call(
+    product = pltpu.VMEM((HALF, WIDE), F32)
+    sums, lifted, hidden_high, hidden_low, hidden_far, hidden_near = call(
         second_kernel,
-        (shape(*cotangent.shape), shape(everyone, per * 8, 128)),
-        [
-            pltpu.VMEM((2 * packed_faces, LINE), F32),
-            pltpu.VMEM((2 * packed_faces, LINE), F32),
-            pad,
-            pad,
-            pltpu.VMEM((HALF, WIDE), F32),
-            pltpu.VMEM((HALF, WIDE), F32),
-            pltpu.VMEM((everyone * per * 8, 128), F32),
-        ],
+        (shape(everyone, per * 8, 128), volume, face, face, face, face),
+        [pool, pool, pad, product, product, pltpu.VMEM((everyone * per * 8, 128), F32), halves, faces],
         smem=(0,),
-        inputs=11,
-    )(
-        face_links, cotangent, band_two, band_back, pre, hidden, lifted_pad,
-        high, low, far, near,
+        inputs=10,
+    )(face_links, cotangent, band_back, pre, hidden, lifted_pad, high, low, far, near)
+    hidden_far = swapped(hidden_far, 1)
+    hidden_near = swapped(hidden_near, 0)
+    band_two = call(band_kernel, band, cost=cost)(conv_two)
+    fine = call(fine_kernel, shape(*cotangent.shape), [pool, pool, pad], smem=(0,), inputs=8, cost=cost)(
+        face_links, band_two, lifted, hidden, hidden_high, hidden_low, hidden_far, hidden_near
     )
     axes = ("space", "dp")
     parts = lax.all_to_all(sums, axes, split_axis=0, concat_axis=0, tiled=True)
     scale = 1.0 / math.sqrt(lax.axis_size("dp") * devices * BRICKS * EDGE**3)
-    total = call(functools.partial(sum_kernel, scale), shape(*sums.shape))(parts)
+    total = call(functools.partial(sum_kernel, scale), shape(*sums.shape), hbm=(1,), inputs=2)(parts, hidden_far)
     gathered = lax.all_to_all(total, axes, split_axis=0, concat_axis=0, tiled=True)
     grads = shape(27, CHANNELS, CHANNELS, dtype=F32)
     rows = pltpu.VMEM((everyone * per * 8, 128), F32)

time: 52.2 us -> 50.4 us (0.966)
  blocking collectives: 21.3 us -> 0 us
  starting transfers between devices: 12.5 us -> 25.3 us
  waiting for transfers between devices: 9.16 us -> 12.4 us
  Pallas kernels: 8.31 us -> 10.5 us
  local copies, waits for them, and re-layouts: 0.03 us -> 0.99 us
    all_to_all x2 -> x0, blocking collectives: 21.3 us -> none  [the longest x1 11.3 us: body(): parts = lax.all_to_all(sums, axes, split_axis=0, concat_axis=0, tiled=True)]
    all_to_all x0 -> x2, waiting for transfers between devices: none -> 10 us  [the longest x1 7.4 us: body(): parts = lax.all_to_all(sums, axes, split_axis=0, concat_axis=0, tiled=True)]
    all_to_all x0 -> x2, starting transfers between devices: none -> 8.83 us  [the longest x1 4.52 us: body(): parts = lax.all_to_all(sums, axes, split_axis=0, concat_axis=0, tiled=True)]
    all_to_all x1, waiting for transfers between devices: 7.27 us -> 0.64 us  [body(): lax.all_to_all(packed, 'space', split_axis=0, concat_axis=0, tiled=True)]
    ppermute x2 -> x4, starting transfers between devices: 4.13 us -> 7.98 us  [swapped(): lax.ppermute(value, 'space', pairs + [(target, source) for source, target...]
    pallas_call x5 -> x7, Pallas kernels: 5.54 us -> 7.78 us  [the longest x1 2.43 us: body(): call(second_kernel, (shape(everyone, per * 8, 128), volume, face, face, f...]
    unnamed x10 -> x12, local copies, waits for them, and re-layouts: 0.03 us -> 0.99 us
    ppermute x2 -> x4, waiting for transfers between devices: 1.9 us -> 1.74 us  [swapped(): lax.ppermute(value, 'space', pairs + [(target, source) for source, target...]
  transfers between devices with their start and end apart: 3 -> 7, of which waited for: 2 -> 4; matrix products, arithmetic and copies ran while one was open for 0% -> 0% of each run, Pallas kernels for 2% -> 9%
where the time goes in v8:
time: 50.4 us; the launch traced here: 50 us
  starting transfers between devices  25.3 us (50%)
  waiting for transfers between devices  12.4 us (25%)
  Pallas kernels  10.5 us (21%)
  local copies, waits for them, and re-layouts  0.99 us (2%)
  between operations  0.78 us (2%)
    all_to_all x1, starting transfers between devices, body(): lax.all_to_all(packed, 'space', split_axis=0, concat_axis=0, tiled=True)  8.46 us
    ppermute x4, starting transfers between devices, swapped(): lax.ppermute(value, 'space', pairs + [(target, source) for source, target...  7.98 us
    all_to_all x1, waiting for transfers between devices, body(): parts = lax.all_to_all(sums, axes, split_axis=0, concat_axis=0, tiled=True)  7.4 us
    all_to_all x1, starting transfers between devices, body(): parts = lax.all_to_all(sums, axes, split_axis=0, concat_axis=0, tiled=True)  4.52 us
    all_to_all x1, starting transfers between devices, body(): lax.all_to_all(total, axes, split_axis=0, concat_axis=0, tiled=True)  4.3 us
    all_to_all x1, waiting for transfers between devices, body(): lax.all_to_all(total, axes, split_axis=0, concat_axis=0, tiled=True)  2.6 us
    pallas_call x1, Pallas kernels, body(): call(second_kernel, (shape(everyone, per * 8, 128), volume, face, face, f...  2.43 us
    ppermute x4, waiting for transfers between devices, swapped(): lax.ppermute(value, 'space', pairs + [(target, source) for source, target...  1.74 us
  transfers between devices with their start and end apart: 7, of which 4 were waited for; matrix products, arithmetic and copies ran while one was open for 0% of the time, Pallas kernels for 9%

profile of v8, /device:TPU:0, one launch (start us, length us, event | category | flops | bytes accessed | tf_op | source)
XLA Modules:
  0.0 50.0 jit_solution(7009541970105083268)
XLA Ops:
  0.6 1.7 %shard_map.96 = bf16[16,24,128]{2,1,0:T(8,128)(2,1)} custom-call(s32[1,32]{1,0:T(1,128)} %ids_hbm.1, bf16[1,64,512]{2,1,0:T(8,128)(2,1)} %latents_hbm.1), custom_call_target="tpu_custom_call" | custom-call | tf_op jit(solution)/shard_map/pallas_call | solution.py:407
  2.4 8.5 %all-to-all-start = ((bf16[16,24,128]{2,1,0:T(8,128)(2,1)}), bf16[16,24,128]{2,1,0:T(8,128)(2,1)S(1)}, u32[]{:S(2)}, u32[]{:S(2)}) async-start(bf16[16,24,128]{2,1,0:T(8,128)(2,1)} %shard_map.96), calls=%async_computation | async-start | bytes 196608 | tf_op jit(solution)/shard_map/all_to_all | solution.py:420
  10.9 0.1 shard_map.98
  11.0 0.7 %collective-permute-start = (bf16[48,256]{1,0:T(8,128)(2,1)S(1)}, bf16[48,256]{1,0:T(8,128)(2,1)S(1)}, u32[]{:S(2)}, u32[]{:S(2)}) collective-permute-start(bf16[48,256]{1,0:T(8,128)(2,1)S(1)} %get-tuple-element.27), channel_id=1, source_target_pairs={{2,4},{6,8},{10,12},{14,16},{18,20},{22,24},{26,28},{4,2},{8,6},{1... | collective-permute-start | bytes 73736 | tf_op jit(solution)/shard_map/ppermute | solution.py:398
  11.6 0.0 copy-start
  11.7 4.7 %collective-permute-start.1 = (bf16[48,256]{1,0:T(8,128)(2,1)S(1)}, bf16[48,256]{1,0:T(8,128)(2,1)S(1)}, u32[]{:S(2)}, u32[]{:S(2)}) collective-permute-start(bf16[48,256]{1,0:T(8,128)(2,1)S(1)} %get-tuple-element.28), channel_id=1, source_target_pairs={{0,2},{4,6},{8,10},{12,14},{16,18},{20,22},{24,26},{28,30},{2,0},{... | collective-permute-start | bytes 73736 | tf_op jit(solution)/shard_map/ppermute | solution.py:398
  16.4 0.9 %copy-done.4 = bf16[27,32,32]{2,1,0:T(8,128)(2,1)S(1)} copy-done((bf16[27,32,32]{2,1,0:T(8,128)(2,1)S(1)}, bf16[27,32,32]{2,1,0:T(8,128)(2,1)}, u32[]{:S(2)}) %copy-start.4) | copy-done | bytes 55320
  17.3 0.6 %shard_map.95 = (bf16[9,256,128]{2,1,0:T(8,128)(2,1)S(1)}, bf16[9,256,128]{2,1,0:T(8,128)(2,1)S(1)}) custom-call(bf16[27,32,32]{2,1,0:T(8,128)(2,1)S(1)} %copy-done.3, bf16[27,32,32]{2,1,0:T(8,128)(2,1)S(1)} %copy-done.4), custom_call_target="tpu_custom_call" | custom-call | flops 1000000000 | bytes 2000000 | tf_op jit(solution)/shard_map/pallas_call | solution.py:433
  17.9 0.0 copy-start.2
  17.9 0.6 %all-to-all-done.received_ref = bf16[16,24,128]{2,1,0:T(8,128)(2,1)S(1)} async-done(((bf16[16,24,128]{2,1,0:T(8,128)(2,1)}), bf16[16,24,128]{2,1,0:T(8,128)(2,1)S(1)}, u32[]{:S(2)}, u32[]{:S(2)}) %all-to-all-start) | async-done | bytes 98336 | tf_op jit(solution)/shard_map/all_to_all | solution.py:420
  18.5 0.0 copy-done.2
  18.6 1.7 %shard_map.97 = (f32[256,128]{1,0:T(8,128)S(1)}, bf16[256,128]{1,0:T(8,128)(2,1)S(1)}, bf16[3,2,10,16,256]{4,3,2,1,0:T(8,128)(2,1)S(1)}) custom-call(s32[1,2,6]{2,1,0:T(2,128)S(1)} %copy-done.2, bf16[16,24,128]{2,1,0:T(8,128)(2,1)S(1)} %all-to-all-done.received_ref, bf16[64,2048]{1,0:T(8,128)(2,1)S(1)} %copy-done, ...), custom_call_target="tpu_custom_call" | custom-call | tf_op jit(solution)/shard_map/pallas_call | solution.py:434
  20.3 2.4 %shard_map.99 = (bf16[32,16,128]{2,1,0:T(8,128)(2,1)}, bf16[256,128]{1,0:T(8,128)(2,1)S(1)}, bf16[48,256]{1,0:T(8,128)(2,1)S(1)}, bf16[48,256]{1,0:T(8,128)(2,1)...) custom-call(s32[1,2,6]{2,1,0:T(2,128)S(1)} %copy-done.2, bf16[1,2,8,8,256]{4,3,2,1,0:T(8,128)(2,1)S(1)} %copy-done.1, ...), custom_call_target="tpu_custom_call" | custom-call | tf_op jit(solution)/shard_map/pallas_call | solution.py:444
  22.7 4.5 %all-to-all-start.1 = ((bf16[32,16,128]{2,1,0:T(8,128)(2,1)}), bf16[32,16,128]{2,1,0:T(8,128)(2,1)S(1)}, u32[]{:S(2)}, u32[]{:S(2)}) async-start(bf16[32,16,128]{2,1,0:T(8,128)(2,1)} %get-tuple-element.34), calls=%async_computation.1 | async-start | bytes 262144 | tf_op jit(solution)/shard_map/all_to_all | solution.py:458
  27.3 0.8 %collective-permute-start.2 = (bf16[48,256]{1,0:T(8,128)(2,1)S(1)}, bf16[48,256]{1,0:T(8,128)(2,1)S(1)}, u32[]{:S(2)}, u32[]{:S(2)}) collective-permute-start(bf16[48,256]{1,0:T(8,128)(2,1)S(1)} %get-tuple-element.32), channel_id=1, source_target_pairs={{2,4},{6,8},{10,12},{14,16},{18,20},{22,24},{26,28},{4,2},{8,6},{1... | collective-permute-start | bytes 73736 | tf_op jit(solution)/shard_map/ppermute | solution.py:398
  28.1 7.4 %all-to-all-done.1.parts_ref = bf16[32,16,128]{2,1,0:T(8,128)(2,1)S(1)} async-done(((bf16[32,16,128]{2,1,0:T(8,128)(2,1)}), bf16[32,16,128]{2,1,0:T(8,128)(2,1)S(1)}, u32[]{:S(2)}, u32[]{:S(2)}) %all-to-all-start.1) | async-done | bytes 131104 | tf_op jit(solution)/shard_map/all_to_all | solution.py:458
  35.5 0.9 %shard_map.101 = bf16[32,16,128]{2,1,0:T(8,128)(2,1)} custom-call(bf16[32,16,128]{2,1,0:T(8,128)(2,1)S(1)} %all-to-all-done.1.parts_ref, bf16[48,256]{1,0:T(8,128)(2,1)S(1)} %collective-permute-done.2.far._), custom_call_target="tpu_custom_call" | custom-call | tf_op jit(solution)/shard_map/pallas_call | solution.py:460
  36.4 4.3 %all-to-all-start.2 = ((bf16[32,16,128]{2,1,0:T(8,128)(2,1)}), bf16[32,16,128]{2,1,0:T(8,128)(2,1)S(1)}, u32[]{:S(2)}, u32[]{:S(2)}) async-start(bf16[32,16,128]{2,1,0:T(8,128)(2,1)} %shard_map.101), calls=%async_computation.2 | async-start | bytes 262144 | tf_op jit(solution)/shard_map/all_to_all | solution.py:461
  40.7 1.8 %collective-permute-start.3 = (bf16[48,256]{1,0:T(8,128)(2,1)S(1)}, bf16[48,256]{1,0:T(8,128)(2,1)S(1)}, u32[]{:S(2)}, u32[]{:S(2)}) collective-permute-start(bf16[48,256]{1,0:T(8,128)(2,1)S(1)} %get-tuple-element.33), channel_id=1, source_target_pairs={{0,2},{4,6},{8,10},{12,14},{16,18},{20,22},{24,26},{28,30},{2,0},{... | collective-permute-start | bytes 73736 | tf_op jit(solution)/shard_map/ppermute | solution.py:398
  42.5 0.3 shard_map.94.band_ref
  42.9 1.7 %collective-permute-done.3.near = bf16[48,256]{1,0:T(8,128)(2,1)S(1)} collective-permute-done((bf16[48,256]{1,0:T(8,128)(2,1)S(1)}, bf16[48,256]{1,0:T(8,128)(2,1)S(1)}, u32[]{:S(2)}, u32[]{:S(2)}) %collective-permute-start.3) | collective-permute-done | bytes 24608 | tf_op jit(solution)/shard_map/ppermute | solution.py:398
  44.6 1.7 %shard_map.100 = bf16[1,2,8,8,256]{4,3,2,1,0:T(8,128)(2,1)} custom-call(s32[1,2,6]{2,1,0:T(2,128)S(1)} %copy-done.2, bf16[9,256,128]{2,1,0:T(8,128)(2,1)S(1)} %shard_map.94.band_ref, bf16[256,128]{1,0:T(8,128)(2,1)S(1)} %get-tuple-element.29.lifted_ref, bf16[256,128]{1,0:T(8,128)(2,1)S(1)} %get-tuple-element.23.hidden_ref, ...), custom_call_target="tpu_custom_call" | custom-call | flops 1000000000 | bytes 2000000 | tf_op jit(solution)/shard_map/pallas_call | solution.py:454
  46.3 2.6 %all-to-all-done.2.sums_ref = bf16[32,16,128]{2,1,0:T(8,128)(2,1)S(1)} async-done(((bf16[32,16,128]{2,1,0:T(8,128)(2,1)}), bf16[32,16,128]{2,1,0:T(8,128)(2,1)S(1)}, u32[]{:S(2)}, u32[]{:S(2)}) %all-to-all-start.2) | async-done | bytes 131104 | tf_op jit(solution)/shard_map/all_to_all | solution.py:461
  48.9 1.0 %shard_map.102 = (f32[27,32,32]{2,1,0:T(8,128)}, f32[27,32,32]{2,1,0:T(8,128)}) custom-call(bf16[32,16,128]{2,1,0:T(8,128)(2,1)S(1)} %all-to-all-done.2.sums_ref), custom_call_target="tpu_custom_call" | custom-call | tf_op jit(solution)/shard_map/pallas_call | solution.py:464
  (11 shorter events, 0.0 us)
Async XLA Ops:
  0.6 15.7 %copy-start.3 = (bf16[27,32,32]{2,1,0:T(8,128)(2,1)S(1)}, bf16[27,32,32]{2,1,0:T(8,128)(2,1)}, u32[]{:S(2)}) copy-start(bf16[27,32,32]{2,1,0:T(8,128)(2,1)} %one_ref.1) | copy-start | bytes 165892
  2.4 8.5 %copy-start.1 = (bf16[1,2,8,8,256]{4,3,2,1,0:T(8,128)(2,1)S(1)}, bf16[1,2,8,8,256]{4,3,2,1,0:T(8,128)(2,1)}, u32[]{:S(2)}) copy-start(bf16[1,2,8,8,256]{4,3,2,1,0:T(8,128)(2,1)} %cotangent_ref.3) | copy-start | bytes 196612
  2.4 16.1 %all-to-all-start = ((bf16[16,24,128]{2,1,0:T(8,128)(2,1)}), bf16[16,24,128]{2,1,0:T(8,128)(2,1)S(1)}, u32[]{:S(2)}, u32[]{:S(2)}) async-start(bf16[16,24,128]{2,1,0:T(8,128)(2,1)} %shard_map.96), calls=%async_computation | async-start | bytes 196608 | tf_op jit(solution)/shard_map/all_to_all | solution.py:420
  11.0 9.3 %collective-permute-start = (bf16[48,256]{1,0:T(8,128)(2,1)S(1)}, bf16[48,256]{1,0:T(8,128)(2,1)S(1)}, u32[]{:S(2)}, u32[]{:S(2)}) collective-permute-start(bf16[48,256]{1,0:T(8,128)(2,1)S(1)} %get-tuple-element.27), channel_id=1, source_target_pairs={{2,4},{6,8},{10,12},{14,16},{18,20},{22,24},{26,28},{4,2},{8,6},{1... | collective-permute-start | bytes 73736 | tf_op jit(solution)/shard_map/ppermute | solution.py:398
  11.6 6.9 %copy-start = (bf16[64,2048]{1,0:T(8,128)(2,1)S(1)}, bf16[64,2048]{1,0:T(8,128)(2,1)}, u32[]{:S(2)}) copy-start(bf16[64,2048]{1,0:T(8,128)(2,1)} %up_ref.1) | copy-start | bytes 786436
  11.7 8.6 %collective-permute-start.1 = (bf16[48,256]{1,0:T(8,128)(2,1)S(1)}, bf16[48,256]{1,0:T(8,128)(2,1)S(1)}, u32[]{:S(2)}, u32[]{:S(2)}) collective-permute-start(bf16[48,256]{1,0:T(8,128)(2,1)S(1)} %get-tuple-element.28), channel_id=1, source_target_pairs={{0,2},{4,6},{8,10},{12,14},{16,18},{20,22},{24,26},{28,30},{2,0},{... | collective-permute-start | bytes 73736 | tf_op jit(solution)/shard_map/ppermute | solution.py:398
  16.3 0.9 %copy-start.4 = (bf16[27,32,32]{2,1,0:T(8,128)(2,1)S(1)}, bf16[27,32,32]{2,1,0:T(8,128)(2,1)}, u32[]{:S(2)}) copy-start(bf16[27,32,32]{2,1,0:T(8,128)(2,1)} %two_ref.1) | copy-start | bytes 165892
  17.9 0.7 %copy-start.2 = (s32[1,2,6]{2,1,0:T(2,128)S(1)}, s32[1,2,6]{2,1,0:T(2,128)}, u32[]{:S(2)}) copy-start(s32[1,2,6]{2,1,0:T(2,128)} %links_ref.5) | copy-start | bytes 148
  22.7 12.8 %all-to-all-start.1 = ((bf16[32,16,128]{2,1,0:T(8,128)(2,1)}), bf16[32,16,128]{2,1,0:T(8,128)(2,1)S(1)}, u32[]{:S(2)}, u32[]{:S(2)}) async-start(bf16[32,16,128]{2,1,0:T(8,128)(2,1)} %get-tuple-element.34), calls=%async_computation.1 | async-start | bytes 262144 | tf_op jit(solution)/shard_map/all_to_all | solution.py:458
  27.3 15.3 %copy-start.5 = (bf16[27,32,32]{2,1,0:T(8,128)(2,1)S(1)}, bf16[27,32,32]{2,1,0:T(8,128)(2,1)}, u32[]{:S(2)}) copy-start(bf16[27,32,32]{2,1,0:T(8,128)(2,1)} %two_ref.1) | copy-start | bytes 165892
  27.3 0.8 %collective-permute-start.2 = (bf16[48,256]{1,0:T(8,128)(2,1)S(1)}, bf16[48,256]{1,0:T(8,128)(2,1)S(1)}, u32[]{:S(2)}, u32[]{:S(2)}) collective-permute-start(bf16[48,256]{1,0:T(8,128)(2,1)S(1)} %get-tuple-element.32), channel_id=1, source_target_pairs={{2,4},{6,8},{10,12},{14,16},{18,20},{22,24},{26,28},{4,2},{8,6},{1... | collective-permute-start | bytes 73736 | tf_op jit(solution)/shard_map/ppermute | solution.py:398
  36.4 12.5 %all-to-all-start.2 = ((bf16[32,16,128]{2,1,0:T(8,128)(2,1)}), bf16[32,16,128]{2,1,0:T(8,128)(2,1)S(1)}, u32[]{:S(2)}, u32[]{:S(2)}) async-start(bf16[32,16,128]{2,1,0:T(8,128)(2,1)} %shard_map.101), calls=%async_computation.2 | async-start | bytes 262144 | tf_op jit(solution)/shard_map/all_to_all | solution.py:461
  40.7 3.9 %collective-permute-start.3 = (bf16[48,256]{1,0:T(8,128)(2,1)S(1)}, bf16[48,256]{1,0:T(8,128)(2,1)S(1)}, u32[]{:S(2)}, u32[]{:S(2)}) collective-permute-start(bf16[48,256]{1,0:T(8,128)(2,1)S(1)} %get-tuple-element.33), channel_id=1, source_target_pairs={{0,2},{4,6},{8,10},{12,14},{16,18},{20,22},{24,26},{28,30},{2,0},{... | collective-permute-start | bytes 73736 | tf_op jit(solution)/shard_map/ppermute | solution.py:398

commit v9 on v8

--- a/solution.py
+++ b/solution.py
@@ -18,6 +18,7 @@
 BRICKS = 2
 CUBE = EDGE * EDGE
 LINES = BRICKS * CUBE
+BAND = (9, WIDE, HALF)
 ROWS = 2 * LINES
 FACE = 3 * EDGE
 BLOCKS = 54
@@ -94,11 +95,6 @@
     build_band(band_ref, weight_rows(weights_ref[...].astype(F32)))
 
 
-def bands_kernel(one_ref, two_ref, band_ref, back_ref):
-    build_band(band_ref, weight_rows(one_ref[...].astype(F32)))
-    build_band(back_ref, flipped_rows(two_ref[...].astype(F32)))
-
-
 def put_padded(pad_ref, brick, lines, x_low, x_high, y_low, y_high, z_low, z_high):
     def joined(halves, before, after):
         lane = lanes_of(halves[0].shape)
@@ -198,10 +194,12 @@
 
 
 def first_kernel(
-    links_ref, received_ref, up_ref, band_ref,
+    links_in, received_ref, up_ref, band_ref,
     pre_out, hidden_out, pad_out,
-    volumes_ref, rows_ref,
+    volumes_ref, rows_ref, links_ref, links_sem,
 ):
+    links_copy = pltpu.make_async_copy(links_in, links_ref, links_sem)
+    links_copy.start()
     position = lax.axis_index("space")
     tiles = received_ref.shape[1] // (3 * BRICKS)
     rows_ref[0 : 3 * BRICKS * tiles] = jnp.sum(received_ref[...].astype(F32), axis=0)
@@ -219,6 +217,7 @@
             volumes_ref[c, pl.ds(line, 8, stride=CUBE), :] = lifted[
                 cell * 8 : cell * 8 + 8, sub * 128 : sub * 128 + 128
             ]
+    links_copy.wait()
     for brick in range(BRICKS):
 
         def near(face):
@@ -308,10 +307,14 @@
 
 
 def second_kernel(
-    links_ref, cotangent_ref, band_ref, pre_ref, hidden_ref, lifted_pad, high_own, low_own, far, near,
+    links_in, cotangent_ref, weights_ref, pre_ref, hidden_ref, lifted_pad, high_own, low_own, far, near,
     sums_out, lifted_out, high_out, low_out, far_out, near_out,
-    high_pool, low_pool, cotangent_pad, one_ref, two_ref, sums_ref, halves_ref, faces_ref,
+    high_pool, low_pool, cotangent_pad, one_ref, two_ref, sums_ref, halves_ref, faces_ref, band_ref,
+    links_ref, links_sem,
 ):
+    links_copy = pltpu.make_async_copy(links_in, links_ref, links_sem)
+    links_copy.start()
+    build_band(band_ref, flipped_rows(weights_ref[...].astype(F32)))
     hidden = hidden_ref[...].astype(F32)
     pack_all(half_lines(hidden), halves_ref, faces_ref, high_out, low_out, far_out, near_out)
     lifted_out[...] = window(lifted_pad, 4)[:, :HALF]
@@ -320,6 +323,7 @@
     slope = sigmoid * (1.0 + pre * (1.0 - sigmoid))
     hidden = jnp.transpose(hidden).astype(BF16)
     bricks = cotangent_lines(cotangent_ref)
+    links_copy.wait()
     pad_all(cotangent_pad, bricks, links_ref, high_pool, low_pool, high_own, low_own, far, near)
     gradient = (convolve(cotangent_pad, band_ref) * slope).astype(BF16)
     gradient = jnp.transpose(gradient.astype(F32)).astype(BF16)
@@ -336,9 +340,13 @@
 
 
 def fine_kernel(
-    links_ref, band_ref, lifted_ref, hidden_ref, high_own, low_own, far, near,
-    fine_out, high_pool, low_pool, hidden_pad,
+    links_in, weights_ref, lifted_ref, hidden_ref, high_own, low_own, far, near,
+    fine_out, high_pool, low_pool, hidden_pad, band_ref, links_ref, links_sem,
 ):
+    links_copy = pltpu.make_async_copy(links_in, links_ref, links_sem)
+    links_copy.start()
+    build_band(band_ref, weight_rows(weights_ref[...].astype(F32)))
+    links_copy.wait()
     bricks = half_lines(hidden_ref[...].astype(F32))
     pad_all(hidden_pad, bricks, links_ref, high_pool, low_pool, high_own, low_own, far, near)
     fine = lifted_ref[...].astype(F32) + convolve(hidden_pad, band_ref)
@@ -352,7 +360,7 @@
     return jnp.concatenate(pieces, axis=0)[:, :CHANNELS]
 
 
-def sum_kernel(scale, parts_ref, _, out_ref):
+def sum_kernel(scale, parts_ref, _far, _near, out_ref):
     total = jnp.sum(parts_ref[...].astype(F32), axis=0) * scale
     per = parts_ref.shape[1] // 8
     device = lax.axis_index("space") * lax.axis_size("dp") + lax.axis_index("dp")
@@ -366,23 +374,29 @@
     out_ref[...] = jnp.broadcast_to(total.astype(BF16)[None], out_ref.shape)
 
 
-def unpack_kernel(sums_ref, one_out, two_out, rows_ref):
+def unpack_kernel(sums_ref, one_out, two_out, rows_ref, one_ref, two_ref, sems):
     rows_ref[...] = sums_ref[...].astype(F32).reshape(rows_ref.shape)
-    for index in range(BLOCKS):
-        block = rows_ref[8 * index : 8 * index + 8]
-        out = one_out if index < 27 else two_out
-        for q in range(4):
-            moved = pltpu.roll(block, 128 - q * CHANNELS, 1) if q else block
-            out[index % 27, 8 * q : 8 * q + 8, :] = moved[:, :CHANNELS]
-
-
-def call(kernel, out_shape, scratch=(), smem=(), hbm=(), inputs=1, limit=24, cost=None):
-    spaces = [pltpu.SMEM if i in smem else pl.ANY if i in hbm else pltpu.VMEM for i in range(inputs)]
+    copies = []
+    for which, (block_ref, out) in enumerate(((one_ref, one_out), (two_ref, two_out))):
+        for third in range(3):
+            first = 9 * third
+            for index in range(first, first + 9):
+                row = 8 * (27 * which + index)
+                block_ref[index] = unpacked(rows_ref[row : row + 8])
+            part = pl.ds(first, 9)
+            copies.append(pltpu.make_async_copy(block_ref.at[part], out.at[part], sems.at[which, third]))
+            copies[-1].start()
+    for copy in copies:
+        copy.wait()
+
+
+def call(kernel, out_shape, scratch=(), hbm=(), inputs=1, limit=24, cost=None, out=pltpu.VMEM):
+    spaces = [pl.ANY if i in hbm else pltpu.VMEM for i in range(inputs)]
     return pl.pallas_call(
         kernel,
         out_shape=out_shape,
         in_specs=[pl.BlockSpec(memory_space=space) for space in spaces],
-        out_specs=jax.tree.map(lambda _: pl.BlockSpec(memory_space=pltpu.VMEM), out_shape),
+        out_specs=jax.tree.map(lambda _: pl.BlockSpec(memory_space=out), out_shape),
         scratch_shapes=list(scratch),
         compiler_params=pltpu.CompilerParams(vmem_limit_bytes=limit * 2**20),
         cost_estimate=cost,
@@ -418,24 +432,25 @@
         limit=60,
     )(active_blocks, coarse_latents)
     received = lax.all_to_all(packed, "space", split_axis=0, concat_axis=0, tiled=True)
-    band = shape(9, WIDE, HALF)
+    band = pltpu.VMEM(BAND, BF16)
     cost = pl.CostEstimate(flops=10**9, bytes_accessed=2 * 10**6, transcendentals=0)
     face = shape(BRICKS * FACE, LINE)
     halves = pltpu.VMEM((2, LINES, HALF), F32)
     faces = pltpu.VMEM((BRICKS * FACE, LINE), F32)
     pool = pltpu.VMEM((2 * BRICKS * FACE, LINE), F32)
     volume = shape(ROWS, HALF)
+    links = [pltpu.SMEM(face_links.shape, jnp.int32), pltpu.SemaphoreType.DMA]
     pad_shape = (3, BRICKS, EDGE + 2, 2 * EDGE, WIDE)
     pad = pltpu.VMEM(pad_shape, BF16)
     high, low, far, near = call(faces_kernel, (face,) * 4, [halves, faces])(cotangent)
     far = swapped(far, 1)
     near = swapped(near, 0)
-    band_one, band_back = call(bands_kernel, (band, band), inputs=2, cost=cost)(conv_one, conv_two)
+    band_one = call(band_kernel, shape(*BAND), cost=cost)(conv_one)
     pre, hidden, lifted_pad = call(
         first_kernel,
         (shape(ROWS, HALF, dtype=F32), volume, shape(*pad_shape)),
-        [pltpu.VMEM((2, 8 * CUBE, 128), F32), pltpu.VMEM((8 * tiles, 128), F32)],
-        smem=(0,),
+        [pltpu.VMEM((2, 8 * CUBE, 128), F32), pltpu.VMEM((8 * tiles, 128), F32), *links],
+        hbm=(0,),
         inputs=4,
     )(face_links, received, up_weight, band_one)
     per = -(-BLOCKS // everyone)
@@ -444,24 +459,26 @@
     sums, lifted, hidden_high, hidden_low, hidden_far, hidden_near = call(
         second_kernel,
         (shape(everyone, per * 8, 128), volume, face, face, face, face),
-        [pool, pool, pad, product, product, pltpu.VMEM((everyone * per * 8, 128), F32), halves, faces],
-        smem=(0,),
+        [pool, pool, pad, product, product, pltpu.VMEM((everyone * per * 8, 128), F32), halves, faces, band, *links],
+        hbm=(0,),
         inputs=10,
-    )(face_links, cotangent, band_back, pre, hidden, lifted_pad, high, low, far, near)
+    )(face_links, cotangent, conv_two, pre, hidden, lifted_pad, high, low, far, near)
     hidden_far = swapped(hidden_far, 1)
     hidden_near = swapped(hidden_near, 0)
-    band_two = call(band_kernel, band, cost=cost)(conv_two)
-    fine = call(fine_kernel, shape(*cotangent.shape), [pool, pool, pad], smem=(0,), inputs=8, cost=cost)(
-        face_links, band_two, lifted, hidden, hidden_high, hidden_low, hidden_far, hidden_near
+    fine = call(fine_kernel, shape(*cotangent.shape), [pool, pool, pad, band, *links], hbm=(0,), inputs=8, cost=cost)(
+        face_links, conv_two, lifted, hidden, hidden_high, hidden_low, hidden_far, hidden_near
     )
     axes = ("space", "dp")
     parts = lax.all_to_all(sums, axes, split_axis=0, concat_axis=0, tiled=True)
     scale = 1.0 / math.sqrt(lax.axis_size("dp") * devices * BRICKS * EDGE**3)
-    total = call(functools.partial(sum_kernel, scale), shape(*sums.shape), hbm=(1,), inputs=2)(parts, hidden_far)
+    total = call(functools.partial(sum_kernel, scale), shape(*sums.shape), hbm=(1, 2), inputs=3)(
+        parts, hidden_far, hidden_near
+    )
     gathered = lax.all_to_all(total, axes, split_axis=0, concat_axis=0, tiled=True)
     grads = shape(27, CHANNELS, CHANNELS, dtype=F32)
-    rows = pltpu.VMEM((everyone * per * 8, 128), F32)
-    grad_one, grad_two = call(unpack_kernel, (grads, grads), [rows])(gathered)
+    block = pltpu.VMEM(grads.shape, F32)
+    scratch = [pltpu.VMEM((everyone * per * 8, 128), F32), block, block, pltpu.SemaphoreType.DMA((2, 3))]
+    grad_one, grad_two = call(unpack_kernel, (grads, grads), scratch, out=pl.ANY)(gathered)
     return (fine, grad_one, grad_two)
 
 

time: 50.4 us -> 48.9 us (0.970)
  starting transfers between devices: 25.3 us -> 27 us
  waiting for transfers between devices: 12.4 us -> 11.3 us
  Pallas kernels: 10.5 us -> 9.47 us
  local copies, waits for them, and re-layouts: 0.99 us -> 0.03 us
    all_to_all x1, waiting for transfers between devices: 7.4 us -> 0.96 us  [body(): parts = lax.all_to_all(sums, axes, split_axis=0, concat_axis=0, tiled=True)]
    all_to_all x1, waiting for transfers between devices: 2.6 us -> 6.48 us  [body(): lax.all_to_all(total, axes, split_axis=0, concat_axis=0, tiled=True)]
    ppermute x4, starting transfers between devices: 7.98 us -> 10.6 us  [swapped(): lax.ppermute(value, 'space', pairs + [(target, source) for source, target...]
    all_to_all x1, waiting for transfers between devices: 0.64 us -> 1.81 us  [body(): lax.all_to_all(packed, 'space', split_axis=0, concat_axis=0, tiled=True)]
    unnamed x12 -> x10, local copies, waits for them, and re-layouts: 0.99 us -> 0.03 us
    all_to_all x1, starting transfers between devices: 4.52 us -> 3.77 us  [body(): parts = lax.all_to_all(sums, axes, split_axis=0, concat_axis=0, tiled=True)]
    pallas_call x5 -> x4, Pallas kernels: 4.58 us -> 4.03 us  [the longest x1 1.74 us: body(): call(fine_kernel, shape(*cotangent.shape), [pool, pool, pad, band, *links...]
    pallas_call x1, Pallas kernels: 1.7 us -> 1.18 us  [body(): call(first_kernel, (shape(ROWS, HALF, dtype=F32), volume, shape(*pad_shap...]
  transfers between devices with their start and end apart: 7 -> 7, of which waited for: 4 -> 4; matrix products, arithmetic and copies ran while one was open for 0% -> 0% of each run, Pallas kernels for 9% -> 7%
where the time goes in v9:
time: 48.9 us; the launch traced here: 48.6 us
  starting transfers between devices  27 us (55%)
  waiting for transfers between devices  11.3 us (23%)
  Pallas kernels  9.47 us (19%)
  between operations  0.79 us (2%)
    ppermute x4, starting transfers between devices, swapped(): lax.ppermute(value, 'space', pairs + [(target, source) for source, target...  10.6 us
    all_to_all x1, starting transfers between devices, body(): lax.all_to_all(packed, 'space', split_axis=0, concat_axis=0, tiled=True)  8.46 us
    all_to_all x1, waiting for transfers between devices, body(): lax.all_to_all(total, axes, split_axis=0, concat_axis=0, tiled=True)  6.48 us
    all_to_all x1, starting transfers between devices, body(): lax.all_to_all(total, axes, split_axis=0, concat_axis=0, tiled=True)  4.16 us
    all_to_all x1, starting transfers between devices, body(): parts = lax.all_to_all(sums, axes, split_axis=0, concat_axis=0, tiled=True)  3.77 us
    pallas_call x1, Pallas kernels, body(): call(second_kernel, (shape(everyone, per * 8, 128), volume, face, face, f...  2.43 us
    ppermute x4, waiting for transfers between devices, swapped(): lax.ppermute(value, 'space', pairs + [(target, source) for source, target...  2.06 us
    all_to_all x1, waiting for transfers between devices, body(): lax.all_to_all(packed, 'space', split_axis=0, concat_axis=0, tiled=True)  1.81 us
  transfers between devices with their start and end apart: 7, of which 4 were waited for; matrix products, arithmetic and copies ran while one was open for 0% of the time, Pallas kernels for 7%

profile of v9, /device:TPU:0, one launch (start us, length us, event | category | flops | bytes accessed | tf_op | source)
XLA Modules:
  0.0 48.6 jit_solution(10578745178965574644)
XLA Ops:
  0.6 1.7 %shard_map.94 = bf16[16,24,128]{2,1,0:T(8,128)(2,1)} custom-call(s32[1,32]{1,0:T(1,128)} %ids_hbm.1, bf16[1,64,512]{2,1,0:T(8,128)(2,1)} %latents_hbm.1), custom_call_target="tpu_custom_call" | custom-call | tf_op jit(solution)/shard_map/pallas_call | solution.py:421
  2.4 0.0 copy-start.1
  2.4 8.5 %all-to-all-start = ((bf16[16,24,128]{2,1,0:T(8,128)(2,1)}), bf16[16,24,128]{2,1,0:T(8,128)(2,1)S(1)}, u32[]{:S(2)}, u32[]{:S(2)}) async-start(bf16[16,24,128]{2,1,0:T(8,128)(2,1)} %shard_map.94), calls=%async_computation | async-start | bytes 196608 | tf_op jit(solution)/shard_map/all_to_all | solution.py:434
  10.9 0.1 shard_map.97
  11.0 0.7 %collective-permute-start = (bf16[48,256]{1,0:T(8,128)(2,1)S(1)}, bf16[48,256]{1,0:T(8,128)(2,1)S(1)}, u32[]{:S(2)}, u32[]{:S(2)}) collective-permute-start(bf16[48,256]{1,0:T(8,128)(2,1)S(1)} %get-tuple-element.23), channel_id=1, source_target_pairs={{2,4},{6,8},{10,12},{14,16},{18,20},{22,24},{26,28},{4,2},{8,6},{1... | collective-permute-start | bytes 73736 | tf_op jit(solution)/shard_map/ppermute | solution.py:412
  11.6 0.0 copy-start
  11.7 0.0 copy-start.3
  11.7 4.7 %collective-permute-start.1 = (bf16[48,256]{1,0:T(8,128)(2,1)S(1)}, bf16[48,256]{1,0:T(8,128)(2,1)S(1)}, u32[]{:S(2)}, u32[]{:S(2)}) collective-permute-start(bf16[48,256]{1,0:T(8,128)(2,1)S(1)} %get-tuple-element.24), channel_id=1, source_target_pairs={{0,2},{4,6},{8,10},{12,14},{16,18},{20,22},{24,26},{28,30},{2,0},{... | collective-permute-start | bytes 73736 | tf_op jit(solution)/shard_map/ppermute | solution.py:412
  16.4 0.3 shard_map.95.band_ref
  16.7 0.0 copy-start.2
  16.7 1.8 %all-to-all-done.received_ref = bf16[16,24,128]{2,1,0:T(8,128)(2,1)S(1)} async-done(((bf16[16,24,128]{2,1,0:T(8,128)(2,1)}), bf16[16,24,128]{2,1,0:T(8,128)(2,1)S(1)}, u32[]{:S(2)}, u32[]{:S(2)}) %all-to-all-start) | async-done | bytes 98336 | tf_op jit(solution)/shard_map/all_to_all | solution.py:434
  18.5 1.2 %shard_map.96 = (f32[256,128]{1,0:T(8,128)S(1)}, bf16[256,128]{1,0:T(8,128)(2,1)S(1)}, bf16[3,2,10,16,256]{4,3,2,1,0:T(8,128)(2,1)S(1)}) custom-call(s32[1,2,6]{2,1,0:T(2,128)S(1)} %copy-done.3, bf16[16,24,128]{2,1,0:T(8,128)(2,1)S(1)} %all-to-all-done.received_ref, bf16[64,2048]{1,0:T(8,128)(2,1)S(1)} %copy-done, bf16[9,256,128]{2,1,0:T(8,128)(2,1)S(1)} %shard_map.95.band_ref), custom_call_target="tpu_custom_call" | custom-call | tf_op jit(solution)/shard_map/pallas_call | solution.py:449
  19.7 0.0 collective-permute-done.far
  19.8 2.4 %shard_map.98 = (bf16[32,16,128]{2,1,0:T(8,128)(2,1)}, bf16[256,128]{1,0:T(8,128)(2,1)S(1)}, bf16[48,256]{1,0:T(8,128)(2,1)S(1)}, bf16[48,256]{1,0:T(8,128)(2,1)...) custom-call(s32[1,2,6]{2,1,0:T(2,128)S(1)} %copy-done.3, bf16[1,2,8,8,256]{4,3,2,1,0:T(8,128)(2,1)S(1)} %copy-done.1, ...), custom_call_target="tpu_custom_call" | custom-call | tf_op jit(solution)/shard_map/pallas_call | solution.py:459
  22.2 3.8 %all-to-all-start.1 = ((bf16[32,16,128]{2,1,0:T(8,128)(2,1)}), bf16[32,16,128]{2,1,0:T(8,128)(2,1)S(1)}, u32[]{:S(2)}, u32[]{:S(2)}) async-start(bf16[32,16,128]{2,1,0:T(8,128)(2,1)} %get-tuple-element.30), calls=%async_computation.1 | async-start | bytes 262144 | tf_op jit(solution)/shard_map/all_to_all | solution.py:472
  26.0 0.7 %collective-permute-start.2 = (bf16[48,256]{1,0:T(8,128)(2,1)S(1)}, bf16[48,256]{1,0:T(8,128)(2,1)S(1)}, u32[]{:S(2)}, u32[]{:S(2)}) collective-permute-start(bf16[48,256]{1,0:T(8,128)(2,1)S(1)} %get-tuple-element.28), channel_id=1, source_target_pairs={{2,4},{6,8},{10,12},{14,16},{18,20},{22,24},{26,28},{4,2},{8,6},{1... | collective-permute-start | bytes 73736 | tf_op jit(solution)/shard_map/ppermute | solution.py:412
  26.6 4.5 %collective-permute-start.3 = (bf16[48,256]{1,0:T(8,128)(2,1)S(1)}, bf16[48,256]{1,0:T(8,128)(2,1)S(1)}, u32[]{:S(2)}, u32[]{:S(2)}) collective-permute-start(bf16[48,256]{1,0:T(8,128)(2,1)S(1)} %get-tuple-element.29), channel_id=1, source_target_pairs={{0,2},{4,6},{8,10},{12,14},{16,18},{20,22},{24,26},{28,30},{2,0},{... | collective-permute-start | bytes 73736 | tf_op jit(solution)/shard_map/ppermute | solution.py:412
  31.2 2.1 %collective-permute-done.3.near._near = bf16[48,256]{1,0:T(8,128)(2,1)S(1)} collective-permute-done((bf16[48,256]{1,0:T(8,128)(2,1)S(1)}, bf16[48,256]{1,0:T(8,128)(2,1)S(1)}, u32[]{:S(2)}, u32[]{:S(2)}) %collective-permute-start.3) | collective-permute-done | bytes 24608 | tf_op jit(solution)/shard_map/ppermute | solution.py:412
  33.2 1.0 %all-to-all-done.1.parts_ref = bf16[32,16,128]{2,1,0:T(8,128)(2,1)S(1)} async-done(((bf16[32,16,128]{2,1,0:T(8,128)(2,1)}), bf16[32,16,128]{2,1,0:T(8,128)(2,1)S(1)}, u32[]{:S(2)}, u32[]{:S(2)}) %all-to-all-start.1) | async-done | bytes 131104 | tf_op jit(solution)/shard_map/all_to_all | solution.py:472
  34.2 0.9 %shard_map.100 = bf16[32,16,128]{2,1,0:T(8,128)(2,1)} custom-call(bf16[32,16,128]{2,1,0:T(8,128)(2,1)S(1)} %all-to-all-done.1.parts_ref, bf16[48,256]{1,0:T(8,128)(2,1)S(1)} %collective-permute-done.2.far._far, bf16[48,256]{1,0:T(8,128)(2,1)S(1)} %collective-permute-done.3.near._near), custom_call_target="tpu_custom_call" | custom-call | tf_op jit(solution)/shard_map/pallas_call | solution.py:474
  35.1 4.2 %all-to-all-start.2 = ((bf16[32,16,128]{2,1,0:T(8,128)(2,1)}), bf16[32,16,128]{2,1,0:T(8,128)(2,1)S(1)}, u32[]{:S(2)}, u32[]{:S(2)}) async-start(bf16[32,16,128]{2,1,0:T(8,128)(2,1)} %shard_map.100), calls=%async_computation.2 | async-start | bytes 262144 | tf_op jit(solution)/shard_map/all_to_all | solution.py:477
  39.3 1.7 %shard_map.99 = bf16[1,2,8,8,256]{4,3,2,1,0:T(8,128)(2,1)} custom-call(s32[1,2,6]{2,1,0:T(2,128)S(1)} %copy-done.3, bf16[27,32,32]{2,1,0:T(8,128)(2,1)S(1)} %copy-done.2, bf16[256,128]{1,0:T(8,128)(2,1)S(1)} %get-tuple-element.25.lifted_ref, bf16[256,128]{1,0:T(8,128)(2,1)S(1)} %get-tuple-element.19.hidden_ref, ...), custom_call_target="tpu_custom_call" | custom-call | flops 1000000000 | bytes 2000000 | tf_op jit(solution)/shard_map/pallas_call | solution.py:468
  41.0 6.5 %all-to-all-done.2.sums_ref = bf16[32,16,128]{2,1,0:T(8,128)(2,1)S(1)} async-done(((bf16[32,16,128]{2,1,0:T(8,128)(2,1)}), bf16[32,16,128]{2,1,0:T(8,128)(2,1)S(1)}, u32[]{:S(2)}, u32[]{:S(2)}) %all-to-all-start.2) | async-done | bytes 131104 | tf_op jit(solution)/shard_map/all_to_all | solution.py:477
  47.5 1.0 %shard_map.101 = (f32[27,32,32]{2,1,0:T(8,128)}, f32[27,32,32]{2,1,0:T(8,128)}) custom-call(bf16[32,16,128]{2,1,0:T(8,128)(2,1)S(1)} %all-to-all-done.2.sums_ref), custom_call_target="tpu_custom_call" | custom-call | tf_op jit(solution)/shard_map/pallas_call | solution.py:481
  (8 shorter events, 0.0 us)
Async XLA Ops:
  0.6 15.7 %copy-start.4 = (bf16[27,32,32]{2,1,0:T(8,128)(2,1)S(1)}, bf16[27,32,32]{2,1,0:T(8,128)(2,1)}, u32[]{:S(2)}) copy-start(bf16[27,32,32]{2,1,0:T(8,128)(2,1)} %weights_ref.3) | copy-start | bytes 165892
  2.4 8.5 %copy-start.1 = (bf16[1,2,8,8,256]{4,3,2,1,0:T(8,128)(2,1)S(1)}, bf16[1,2,8,8,256]{4,3,2,1,0:T(8,128)(2,1)}, u32[]{:S(2)}) copy-start(bf16[1,2,8,8,256]{4,3,2,1,0:T(8,128)(2,1)} %cotangent_ref.3) | copy-start | bytes 196612
  2.4 16.1 %all-to-all-start = ((bf16[16,24,128]{2,1,0:T(8,128)(2,1)}), bf16[16,24,128]{2,1,0:T(8,128)(2,1)S(1)}, u32[]{:S(2)}, u32[]{:S(2)}) async-start(bf16[16,24,128]{2,1,0:T(8,128)(2,1)} %shard_map.94), calls=%async_computation | async-start | bytes 196608 | tf_op jit(solution)/shard_map/all_to_all | solution.py:434
  11.0 8.8 %collective-permute-start = (bf16[48,256]{1,0:T(8,128)(2,1)S(1)}, bf16[48,256]{1,0:T(8,128)(2,1)S(1)}, u32[]{:S(2)}, u32[]{:S(2)}) collective-permute-start(bf16[48,256]{1,0:T(8,128)(2,1)S(1)} %get-tuple-element.23), channel_id=1, source_target_pairs={{2,4},{6,8},{10,12},{14,16},{18,20},{22,24},{26,28},{4,2},{8,6},{1... | collective-permute-start | bytes 73736 | tf_op jit(solution)/shard_map/ppermute | solution.py:412
  11.6 6.9 %copy-start = (bf16[64,2048]{1,0:T(8,128)(2,1)S(1)}, bf16[64,2048]{1,0:T(8,128)(2,1)}, u32[]{:S(2)}) copy-start(bf16[64,2048]{1,0:T(8,128)(2,1)} %up_ref.1) | copy-start | bytes 786436
  11.7 6.9 %copy-start.3 = (s32[1,2,6]{2,1,0:T(2,128)S(1)}, s32[1,2,6]{2,1,0:T(2,128)}, u32[]{:S(2)}) copy-start(s32[1,2,6]{2,1,0:T(2,128)} %links_in.5) | copy-start | bytes 148
  11.7 8.1 %collective-permute-start.1 = (bf16[48,256]{1,0:T(8,128)(2,1)S(1)}, bf16[48,256]{1,0:T(8,128)(2,1)S(1)}, u32[]{:S(2)}, u32[]{:S(2)}) collective-permute-start(bf16[48,256]{1,0:T(8,128)(2,1)S(1)} %get-tuple-element.24), channel_id=1, source_target_pairs={{0,2},{4,6},{8,10},{12,14},{16,18},{20,22},{24,26},{28,30},{2,0},{... | collective-permute-start | bytes 73736 | tf_op jit(solution)/shard_map/ppermute | solution.py:412
  16.7 3.0 %copy-start.2 = (bf16[27,32,32]{2,1,0:T(8,128)(2,1)S(1)}, bf16[27,32,32]{2,1,0:T(8,128)(2,1)}, u32[]{:S(2)}) copy-start(bf16[27,32,32]{2,1,0:T(8,128)(2,1)} %weights_ref.5) | copy-start | bytes 165892
  22.2 12.0 %all-to-all-start.1 = ((bf16[32,16,128]{2,1,0:T(8,128)(2,1)}), bf16[32,16,128]{2,1,0:T(8,128)(2,1)S(1)}, u32[]{:S(2)}, u32[]{:S(2)}) async-start(bf16[32,16,128]{2,1,0:T(8,128)(2,1)} %get-tuple-element.30), calls=%async_computation.1 | async-start | bytes 262144 | tf_op jit(solution)/shard_map/all_to_all | solution.py:472
  26.0 5.2 %collective-permute-start.2 = (bf16[48,256]{1,0:T(8,128)(2,1)S(1)}, bf16[48,256]{1,0:T(8,128)(2,1)S(1)}, u32[]{:S(2)}, u32[]{:S(2)}) collective-permute-start(bf16[48,256]{1,0:T(8,128)(2,1)S(1)} %get-tuple-element.28), channel_id=1, source_target_pairs={{2,4},{6,8},{10,12},{14,16},{18,20},{22,24},{26,28},{4,2},{8,6},{1... | collective-permute-start | bytes 73736 | tf_op jit(solution)/shard_map/ppermute | solution.py:412
  26.6 6.6 %collective-permute-start.3 = (bf16[48,256]{1,0:T(8,128)(2,1)S(1)}, bf16[48,256]{1,0:T(8,128)(2,1)S(1)}, u32[]{:S(2)}, u32[]{:S(2)}) collective-permute-start(bf16[48,256]{1,0:T(8,128)(2,1)S(1)} %get-tuple-element.29), channel_id=1, source_target_pairs={{0,2},{4,6},{8,10},{12,14},{16,18},{20,22},{24,26},{28,30},{2,0},{... | collective-permute-start | bytes 73736 | tf_op jit(solution)/shard_map/ppermute | solution.py:412
  35.1 12.4 %all-to-all-start.2 = ((bf16[32,16,128]{2,1,0:T(8,128)(2,1)}), bf16[32,16,128]{2,1,0:T(8,128)(2,1)S(1)}, u32[]{:S(2)}, u32[]{:S(2)}) async-start(bf16[32,16,128]{2,1,0:T(8,128)(2,1)} %shard_map.100), calls=%async_computation.2 | async-start | bytes 262144 | tf_op jit(solution)/shard_map/all_to_all | solution.py:477

commit v10 on v9

--- a/solution.py
+++ b/solution.py
@@ -165,23 +165,23 @@
     faces_ref[base + 2 * EDGE : base + FACE, 128:] = packed[8:]
 
 
-def pack_all(bricks, halves_ref, faces_ref, high_out, low_out, far_out, near_out):
+def pack_all(bricks, halves_ref, faces_ref, high_out, low_out):
     put_halves(halves_ref, 0, bricks)
-    packed = []
-    for high in (True, False):
+    for high, out_ref in ((True, high_out), (False, low_out)):
         for brick in range(BRICKS):
             pack_faces(faces_ref, brick * FACE, halves_ref, brick * CUBE, high)
-        packed.append(faces_ref[...].astype(BF16))
-    high, low = packed
-    high_out[...] = high
-    low_out[...] = low
+        out_ref[...] = faces_ref[...].astype(BF16)
+
+
+def to_partners(high_ref, low_ref, far_out, near_out):
     even = lax.axis_index("space") % 2 == 0
-    far_out[...] = jnp.where(even, low, high)
-    near_out[...] = jnp.where(even, high, low)
+    far_out[...] = jnp.where(even, low_ref[...], high_ref[...])
+    near_out[...] = jnp.where(even, high_ref[...], low_ref[...])
 
 
 def faces_kernel(cotangent_ref, high_out, low_out, far_out, near_out, halves_ref, faces_ref):
-    pack_all(cotangent_lines(cotangent_ref), halves_ref, faces_ref, high_out, low_out, far_out, near_out)
+    pack_all(cotangent_lines(cotangent_ref), halves_ref, faces_ref, high_out, low_out)
+    to_partners(high_out, low_out, far_out, near_out)
 
 
 def unpack_depth(rows, high):
@@ -194,9 +194,9 @@
 
 
 def first_kernel(
-    links_in, received_ref, up_ref, band_ref,
-    pre_out, hidden_out, pad_out,
-    volumes_ref, rows_ref, links_ref, links_sem,
+    links_in, received_ref, up_ref, band_ref, weights_ref,
+    slope_out, hidden_out, turned_out, pad_out, back_out, high_out, low_out,
+    volumes_ref, rows_ref, halves_ref, faces_ref, links_ref, links_sem,
 ):
     links_copy = pltpu.make_async_copy(links_in, links_ref, links_sem)
     links_copy.start()
@@ -244,18 +244,22 @@
         own = [half.reshape(EDGE, EDGE, HALF) for half in own]
         put_padded(pad_out, brick, own, x_face(0), x_face(1), y_face(2), y_face(3), z_face(4), z_face(5))
     pre = convolve(pad_out, band_ref)
-    hidden = pre / (1.0 + jnp.exp(-pre))
-    hidden = hidden.astype(BF16)
-    pre_out[...] = pre
+    sigmoid = 1.0 / (1.0 + jnp.exp(-pre))
+    hidden = (pre / (1.0 + jnp.exp(-pre))).astype(BF16)
+    slope_out[...] = sigmoid * (1.0 + pre * (1.0 - sigmoid))
     hidden_out[...] = hidden
-
-
-def fold(outer_ref, places):
+    hidden = hidden.astype(F32)
+    turned_out[...] = jnp.transpose(hidden).astype(BF16)
+    pack_all(half_lines(hidden), halves_ref, faces_ref, high_out, low_out)
+    build_band(back_out, flipped_rows(weights_ref[...].astype(F32)))
+
+
+def fold(outer, places):
     lane = lanes_of((CHANNELS, 128)) // CHANNELS
     folded = None
     for block in range(4):
         start, tile = places[block]
-        rows = outer_ref[start : start + CHANNELS, tile * 128 : tile * 128 + 128]
+        rows = outer[start : start + CHANNELS, tile * 128 : tile * 128 + 128]
         folded = rows if folded is None else jnp.where(lane == block, rows, folded)
     quarter = [folded[8 * q : 8 * q + 8] for q in range(4)]
     small = lanes_of((8, 128)) // CHANNELS
@@ -307,35 +311,30 @@
 
 
 def second_kernel(
-    links_in, cotangent_ref, weights_ref, pre_ref, hidden_ref, lifted_pad, high_own, low_own, far, near,
-    sums_out, lifted_out, high_out, low_out, far_out, near_out,
-    high_pool, low_pool, cotangent_pad, one_ref, two_ref, sums_ref, halves_ref, faces_ref, band_ref,
-    links_ref, links_sem,
+    links_in, cotangent_ref, band_ref, slope_ref, hidden_ref, lifted_pad, high_own, low_own, far, near,
+    hidden_high, hidden_low,
+    sums_out, lifted_out, far_out, near_out,
+    high_pool, low_pool, cotangent_pad, sums_ref, links_ref, links_sem,
 ):
     links_copy = pltpu.make_async_copy(links_in, links_ref, links_sem)
     links_copy.start()
-    build_band(band_ref, flipped_rows(weights_ref[...].astype(F32)))
-    hidden = hidden_ref[...].astype(F32)
-    pack_all(half_lines(hidden), halves_ref, faces_ref, high_out, low_out, far_out, near_out)
+    to_partners(hidden_high, hidden_low, far_out, near_out)
     lifted_out[...] = window(lifted_pad, 4)[:, :HALF]
-    pre = pre_ref[...]
-    sigmoid = 1.0 / (1.0 + jnp.exp(-pre))
-    slope = sigmoid * (1.0 + pre * (1.0 - sigmoid))
-    hidden = jnp.transpose(hidden).astype(BF16)
     bricks = cotangent_lines(cotangent_ref)
     links_copy.wait()
     pad_all(cotangent_pad, bricks, links_ref, high_pool, low_pool, high_own, low_own, far, near)
-    gradient = (convolve(cotangent_pad, band_ref) * slope).astype(BF16)
+    gradient = (convolve(cotangent_pad, band_ref) * slope_ref[...]).astype(BF16)
     gradient = jnp.transpose(gradient.astype(F32)).astype(BF16)
+    hidden = hidden_ref[...]
     sums_ref[8 * BLOCKS :] = jnp.zeros((sums_ref.shape[0] - 8 * BLOCKS, 128), F32)
     for k in range(9):
-        one_ref[...] = dot(gradient, window(lifted_pad, k))
-        two_ref[...] = dot(hidden, window(cotangent_pad, 8 - k))
+        one = dot(gradient, window(lifted_pad, k))
+        two = dot(hidden, window(cotangent_pad, 8 - k))
         for part in range(3):
             start = 8 * (3 * k + part)
-            sums_ref[start : start + 8] = fold(one_ref, diagonal(part - 1))
+            sums_ref[start : start + 8] = fold(one, diagonal(part - 1))
             start += 8 * 27
-            sums_ref[start : start + 8] = fold(two_ref, diagonal(1 - part))
+            sums_ref[start : start + 8] = fold(two, diagonal(1 - part))
     sums_out[...] = sums_ref[...].astype(BF16).reshape(sums_out.shape)
 
 
@@ -446,23 +445,28 @@
     far = swapped(far, 1)
     near = swapped(near, 0)
     band_one = call(band_kernel, shape(*BAND), cost=cost)(conv_one)
-    pre, hidden, lifted_pad = call(
+    slope, hidden, turned, lifted_pad, band_back, hidden_high, hidden_low = call(
         first_kernel,
-        (shape(ROWS, HALF, dtype=F32), volume, shape(*pad_shape)),
-        [pltpu.VMEM((2, 8 * CUBE, 128), F32), pltpu.VMEM((8 * tiles, 128), F32), *links],
+        (
+            shape(ROWS, HALF, dtype=F32), volume, shape(HALF, ROWS), shape(*pad_shape), shape(*BAND),
+            face, face,
+        ),
+        [pltpu.VMEM((2, 8 * CUBE, 128), F32), pltpu.VMEM((8 * tiles, 128), F32), halves, faces, *links],
         hbm=(0,),
-        inputs=4,
-    )(face_links, received, up_weight, band_one)
+        inputs=5,
+    )(face_links, received, up_weight, band_one, conv_two)
     per = -(-BLOCKS // everyone)
     per += per % 2
-    product = pltpu.VMEM((HALF, WIDE), F32)
-    sums, lifted, hidden_high, hidden_low, hidden_far, hidden_near = call(
+    sums, lifted, hidden_far, hidden_near = call(
         second_kernel,
-        (shape(everyone, per * 8, 128), volume, face, face, face, face),
-        [pool, pool, pad, product, product, pltpu.VMEM((everyone * per * 8, 128), F32), halves, faces, band, *links],
+        (shape(everyone, per * 8, 128), volume, face, face),
+        [pool, pool, pad, pltpu.VMEM((everyone * per * 8, 128), F32), *links],
         hbm=(0,),
-        inputs=10,
-    )(face_links, cotangent, conv_two, pre, hidden, lifted_pad, high, low, far, near)
+        inputs=12,
+    )(
+        face_links, cotangent, band_back, slope, turned, lifted_pad, high, low, far, near,
+        hidden_high, hidden_low,
+    )
     hidden_far = swapped(hidden_far, 1)
     hidden_near = swapped(hidden_near, 0)
     fine = call(fine_kernel, shape(*cotangent.shape), [pool, pool, pad, band, *links], hbm=(0,), inputs=8, cost=cost)(

time: 48.9 us -> 48.9 us (level)
  no operation moved by 1% of the time
where the time goes in v10:
time: 48.9 us; the launch traced here: 48.5 us
  starting transfers between devices  26.8 us (55%)
  waiting for transfers between devices  11.3 us (23%)
  Pallas kernels  9.58 us (20%)
  between operations  0.79 us (2%)
    ppermute x4, starting transfers between devices, swapped(): lax.ppermute(value, 'space', pairs + [(target, source) for source, target...  10.6 us
    all_to_all x1, starting transfers between devices, body(): lax.all_to_all(packed, 'space', split_axis=0, concat_axis=0, tiled=True)  8.46 us
    all_to_all x1, waiting for transfers between devices, body(): lax.all_to_all(total, axes, split_axis=0, concat_axis=0, tiled=True)  6.48 us
    all_to_all x1, starting transfers between devices, body(): lax.all_to_all(total, axes, split_axis=0, concat_axis=0, tiled=True)  4.16 us
    all_to_all x1, starting transfers between devices, body(): parts = lax.all_to_all(sums, axes, split_axis=0, concat_axis=0, tiled=True)  3.63 us
    pallas_call x1, Pallas kernels, body(): call(second_kernel, (shape(everyone, per * 8, 128), volume, face, face),...  2.39 us
    ppermute x4, waiting for transfers between devices, swapped(): lax.ppermute(value, 'space', pairs + [(target, source) for source, target...  2.06 us
    all_to_all x1, waiting for transfers between devices, body(): lax.all_to_all(packed, 'space', split_axis=0, concat_axis=0, tiled=True)  1.82 us
  transfers between devices with their start and end apart: 7, of which 4 were waited for; matrix products, arithmetic and copies ran while one was open for 0% of the time, Pallas kernels for 7%

profile of v10, /device:TPU:0, one launch (start us, length us, event | category | flops | bytes accessed | tf_op | source)
XLA Modules:
  0.0 48.5 jit_solution(11962571737667115794)
XLA Ops:
  0.6 1.7 %shard_map.94 = bf16[16,24,128]{2,1,0:T(8,128)(2,1)} custom-call(s32[1,32]{1,0:T(1,128)} %ids_hbm.1, bf16[1,64,512]{2,1,0:T(8,128)(2,1)} %latents_hbm.1), custom_call_target="tpu_custom_call" | custom-call | tf_op jit(solution)/shard_map/pallas_call | solution.py:420
  2.4 0.0 copy-start
  2.4 8.5 %all-to-all-start = ((bf16[16,24,128]{2,1,0:T(8,128)(2,1)}), bf16[16,24,128]{2,1,0:T(8,128)(2,1)S(1)}, u32[]{:S(2)}, u32[]{:S(2)}) async-start(bf16[16,24,128]{2,1,0:T(8,128)(2,1)} %shard_map.94), calls=%async_computation | async-start | bytes 196608 | tf_op jit(solution)/shard_map/all_to_all | solution.py:433
  10.9 0.1 shard_map.97
  11.0 0.7 %collective-permute-start = (bf16[48,256]{1,0:T(8,128)(2,1)S(1)}, bf16[48,256]{1,0:T(8,128)(2,1)S(1)}, u32[]{:S(2)}, u32[]{:S(2)}) collective-permute-start(bf16[48,256]{1,0:T(8,128)(2,1)S(1)} %get-tuple-element.26), channel_id=1, source_target_pairs={{2,4},{6,8},{10,12},{14,16},{18,20},{22,24},{26,28},{4,2},{8,6},{1... | collective-permute-start | bytes 73736 | tf_op jit(solution)/shard_map/ppermute | solution.py:411
  11.6 0.0 copy-start.1
  11.6 0.0 copy-start.2
  11.7 0.0 copy-start.3
  11.7 4.7 %collective-permute-start.1 = (bf16[48,256]{1,0:T(8,128)(2,1)S(1)}, bf16[48,256]{1,0:T(8,128)(2,1)S(1)}, u32[]{:S(2)}, u32[]{:S(2)}) collective-permute-start(bf16[48,256]{1,0:T(8,128)(2,1)S(1)} %get-tuple-element.27), channel_id=1, source_target_pairs={{0,2},{4,6},{8,10},{12,14},{16,18},{20,22},{24,26},{28,30},{2,0},{... | collective-permute-start | bytes 73736 | tf_op jit(solution)/shard_map/ppermute | solution.py:411
  16.4 0.3 shard_map.95.band_ref
  16.7 1.8 %all-to-all-done.received_ref = bf16[16,24,128]{2,1,0:T(8,128)(2,1)S(1)} async-done(((bf16[16,24,128]{2,1,0:T(8,128)(2,1)}), bf16[16,24,128]{2,1,0:T(8,128)(2,1)S(1)}, u32[]{:S(2)}, u32[]{:S(2)}) %all-to-all-start) | async-done | bytes 98336 | tf_op jit(solution)/shard_map/all_to_all | solution.py:433
  18.5 1.3 %shard_map.96 = (f32[256,128]{1,0:T(8,128)S(1)}, bf16[256,128]{1,0:T(8,128)(2,1)S(1)}, bf16[128,256]{1,0:T(8,128)(2,1)S(1)}, bf16[3,2,10,16,256]{4,3,2,1,0:T(8,1...) custom-call(s32[1,2,6]{2,1,0:T(2,128)S(1)} %copy-done.3, ...), custom_call_target="tpu_custom_call" | custom-call | tf_op jit(solution)/shard_map/pallas_call | solution.py:448
  19.9 0.0 collective-permute-done.1.near
  19.9 2.4 %shard_map.98 = (bf16[32,16,128]{2,1,0:T(8,128)(2,1)}, bf16[256,128]{1,0:T(8,128)(2,1)S(1)}, bf16[48,256]{1,0:T(8,128)(2,1)S(1)}, bf16[48,256]{1,0:T(8,128)(2,1)S(1)}) custom-call(s32[1,2,6]{2,1,0:T(2,128)S(1)} %copy-done.3, bf16[1,2,8,8,256]{4,3,2,1,0:T(8,128)(2,1)S(1)} %copy-done, bf16[9,256,128]{2,1,0:T(8,128)(2,1)S(1)} %get-tuple-element.20.band_ref, ...), custom_call_target="tpu_custom_call" | custom-call | tf_op jit(solution)/shard_map/pallas_call | solution.py:460
  22.3 3.6 %all-to-all-start.1 = ((bf16[32,16,128]{2,1,0:T(8,128)(2,1)}), bf16[32,16,128]{2,1,0:T(8,128)(2,1)S(1)}, u32[]{:S(2)}, u32[]{:S(2)}) async-start(bf16[32,16,128]{2,1,0:T(8,128)(2,1)} %get-tuple-element.34), calls=%async_computation.1 | async-start | bytes 262144 | tf_op jit(solution)/shard_map/all_to_all | solution.py:476
  25.9 0.7 %collective-permute-start.2 = (bf16[48,256]{1,0:T(8,128)(2,1)S(1)}, bf16[48,256]{1,0:T(8,128)(2,1)S(1)}, u32[]{:S(2)}, u32[]{:S(2)}) collective-permute-start(bf16[48,256]{1,0:T(8,128)(2,1)S(1)} %get-tuple-element.32), channel_id=1, source_target_pairs={{2,4},{6,8},{10,12},{14,16},{18,20},{22,24},{26,28},{4,2},{8,6},{1... | collective-permute-start | bytes 73736 | tf_op jit(solution)/shard_map/ppermute | solution.py:411
  26.6 4.5 %collective-permute-start.3 = (bf16[48,256]{1,0:T(8,128)(2,1)S(1)}, bf16[48,256]{1,0:T(8,128)(2,1)S(1)}, u32[]{:S(2)}, u32[]{:S(2)}) collective-permute-start(bf16[48,256]{1,0:T(8,128)(2,1)S(1)} %get-tuple-element.33), channel_id=1, source_target_pairs={{0,2},{4,6},{8,10},{12,14},{16,18},{20,22},{24,26},{28,30},{2,0},{... | collective-permute-start | bytes 73736 | tf_op jit(solution)/shard_map/ppermute | solution.py:411
  31.2 2.1 %collective-permute-done.3.near._near = bf16[48,256]{1,0:T(8,128)(2,1)S(1)} collective-permute-done((bf16[48,256]{1,0:T(8,128)(2,1)S(1)}, bf16[48,256]{1,0:T(8,128)(2,1)S(1)}, u32[]{:S(2)}, u32[]{:S(2)}) %collective-permute-start.3) | collective-permute-done | bytes 24608 | tf_op jit(solution)/shard_map/ppermute | solution.py:411
  33.2 1.0 %all-to-all-done.1.parts_ref = bf16[32,16,128]{2,1,0:T(8,128)(2,1)S(1)} async-done(((bf16[32,16,128]{2,1,0:T(8,128)(2,1)}), bf16[32,16,128]{2,1,0:T(8,128)(2,1)S(1)}, u32[]{:S(2)}, u32[]{:S(2)}) %all-to-all-start.1) | async-done | bytes 131104 | tf_op jit(solution)/shard_map/all_to_all | solution.py:476
  34.2 0.9 %shard_map.100 = bf16[32,16,128]{2,1,0:T(8,128)(2,1)} custom-call(bf16[32,16,128]{2,1,0:T(8,128)(2,1)S(1)} %all-to-all-done.1.parts_ref, bf16[48,256]{1,0:T(8,128)(2,1)S(1)} %collective-permute-done.2.far._far, bf16[48,256]{1,0:T(8,128)(2,1)S(1)} %collective-permute-done.3.near._near), custom_call_target="tpu_custom_call" | custom-call | tf_op jit(solution)/shard_map/pallas_call | solution.py:478
  35.1 4.2 %all-to-all-start.2 = ((bf16[32,16,128]{2,1,0:T(8,128)(2,1)}), bf16[32,16,128]{2,1,0:T(8,128)(2,1)S(1)}, u32[]{:S(2)}, u32[]{:S(2)}) async-start(bf16[32,16,128]{2,1,0:T(8,128)(2,1)} %shard_map.100), calls=%async_computation.2 | async-start | bytes 262144 | tf_op jit(solution)/shard_map/all_to_all | solution.py:481
  39.2 1.7 %shard_map.99 = bf16[1,2,8,8,256]{4,3,2,1,0:T(8,128)(2,1)} custom-call(s32[1,2,6]{2,1,0:T(2,128)S(1)} %copy-done.3, bf16[27,32,32]{2,1,0:T(8,128)(2,1)S(1)} %copy-done.2, bf16[256,128]{1,0:T(8,128)(2,1)S(1)} %get-tuple-element.30.lifted_ref, bf16[256,128]{1,0:T(8,128)(2,1)S(1)} %get-tuple-element.31.hidden_ref, ...), custom_call_target="tpu_custom_call" | custom-call | flops 1000000000 | bytes 2000000 | tf_op jit(solution)/shard_map/pallas_call | solution.py:472
  41.0 6.5 %all-to-all-done.2.sums_ref = bf16[32,16,128]{2,1,0:T(8,128)(2,1)S(1)} async-done(((bf16[32,16,128]{2,1,0:T(8,128)(2,1)}), bf16[32,16,128]{2,1,0:T(8,128)(2,1)S(1)}, u32[]{:S(2)}, u32[]{:S(2)}) %all-to-all-start.2) | async-done | bytes 131104 | tf_op jit(solution)/shard_map/all_to_all | solution.py:481
  47.5 1.0 %shard_map.101 = (f32[27,32,32]{2,1,0:T(8,128)}, f32[27,32,32]{2,1,0:T(8,128)}) custom-call(bf16[32,16,128]{2,1,0:T(8,128)(2,1)S(1)} %all-to-all-done.2.sums_ref), custom_call_target="tpu_custom_call" | custom-call | tf_op jit(solution)/shard_map/pallas_call | solution.py:485
  (8 shorter events, 0.0 us)
Async XLA Ops:
  0.6 15.7 %copy-start.4 = (bf16[27,32,32]{2,1,0:T(8,128)(2,1)S(1)}, bf16[27,32,32]{2,1,0:T(8,128)(2,1)}, u32[]{:S(2)}) copy-start(bf16[27,32,32]{2,1,0:T(8,128)(2,1)} %weights_ref.3) | copy-start | bytes 165892
  2.4 8.5 %copy-start = (bf16[1,2,8,8,256]{4,3,2,1,0:T(8,128)(2,1)S(1)}, bf16[1,2,8,8,256]{4,3,2,1,0:T(8,128)(2,1)}, u32[]{:S(2)}) copy-start(bf16[1,2,8,8,256]{4,3,2,1,0:T(8,128)(2,1)} %cotangent_ref.3) | copy-start | bytes 196612
  2.4 16.1 %all-to-all-start = ((bf16[16,24,128]{2,1,0:T(8,128)(2,1)}), bf16[16,24,128]{2,1,0:T(8,128)(2,1)S(1)}, u32[]{:S(2)}, u32[]{:S(2)}) async-start(bf16[16,24,128]{2,1,0:T(8,128)(2,1)} %shard_map.94), calls=%async_computation | async-start | bytes 196608 | tf_op jit(solution)/shard_map/all_to_all | solution.py:433
  11.0 8.9 %collective-permute-start = (bf16[48,256]{1,0:T(8,128)(2,1)S(1)}, bf16[48,256]{1,0:T(8,128)(2,1)S(1)}, u32[]{:S(2)}, u32[]{:S(2)}) collective-permute-start(bf16[48,256]{1,0:T(8,128)(2,1)S(1)} %get-tuple-element.26), channel_id=1, source_target_pairs={{2,4},{6,8},{10,12},{14,16},{18,20},{22,24},{26,28},{4,2},{8,6},{1... | collective-permute-start | bytes 73736 | tf_op jit(solution)/shard_map/ppermute | solution.py:411
  11.6 6.9 %copy-start.1 = (bf16[64,2048]{1,0:T(8,128)(2,1)S(1)}, bf16[64,2048]{1,0:T(8,128)(2,1)}, u32[]{:S(2)}) copy-start(bf16[64,2048]{1,0:T(8,128)(2,1)} %up_ref.1) | copy-start | bytes 786436
  11.6 6.9 %copy-start.2 = (bf16[27,32,32]{2,1,0:T(8,128)(2,1)S(1)}, bf16[27,32,32]{2,1,0:T(8,128)(2,1)}, u32[]{:S(2)}) copy-start(bf16[27,32,32]{2,1,0:T(8,128)(2,1)} %weights_ref.5) | copy-start | bytes 165892
  11.7 6.9 %copy-start.3 = (s32[1,2,6]{2,1,0:T(2,128)S(1)}, s32[1,2,6]{2,1,0:T(2,128)}, u32[]{:S(2)}) copy-start(s32[1,2,6]{2,1,0:T(2,128)} %links_in.5) | copy-start | bytes 148
  11.7 8.2 %collective-permute-start.1 = (bf16[48,256]{1,0:T(8,128)(2,1)S(1)}, bf16[48,256]{1,0:T(8,128)(2,1)S(1)}, u32[]{:S(2)}, u32[]{:S(2)}) collective-permute-start(bf16[48,256]{1,0:T(8,128)(2,1)S(1)} %get-tuple-element.27), channel_id=1, source_target_pairs={{0,2},{4,6},{8,10},{12,14},{16,18},{20,22},{24,26},{28,30},{2,0},{... | collective-permute-start | bytes 73736 | tf_op jit(solution)/shard_map/ppermute | solution.py:411
  22.3 11.9 %all-to-all-start.1 = ((bf16[32,16,128]{2,1,0:T(8,128)(2,1)}), bf16[32,16,128]{2,1,0:T(8,128)(2,1)S(1)}, u32[]{:S(2)}, u32[]{:S(2)}) async-start(bf16[32,16,128]{2,1,0:T(8,128)(2,1)} %get-tuple-element.34), calls=%async_computation.1 | async-start | bytes 262144 | tf_op jit(solution)/shard_map/all_to_all | solution.py:476
  25.9 5.2 %collective-permute-start.2 = (bf16[48,256]{1,0:T(8,128)(2,1)S(1)}, bf16[48,256]{1,0:T(8,128)(2,1)S(1)}, u32[]{:S(2)}, u32[]{:S(2)}) collective-permute-start(bf16[48,256]{1,0:T(8,128)(2,1)S(1)} %get-tuple-element.32), channel_id=1, source_target_pairs={{2,4},{6,8},{10,12},{14,16},{18,20},{22,24},{26,28},{4,2},{8,6},{1... | collective-permute-start | bytes 73736 | tf_op jit(solution)/shard_map/ppermute | solution.py:411
  26.6 6.6 %collective-permute-start.3 = (bf16[48,256]{1,0:T(8,128)(2,1)S(1)}, bf16[48,256]{1,0:T(8,128)(2,1)S(1)}, u32[]{:S(2)}, u32[]{:S(2)}) collective-permute-start(bf16[48,256]{1,0:T(8,128)(2,1)S(1)} %get-tuple-element.33), channel_id=1, source_target_pairs={{0,2},{4,6},{8,10},{12,14},{16,18},{20,22},{24,26},{28,30},{2,0},{... | collective-permute-start | bytes 73736 | tf_op jit(solution)/shard_map/ppermute | solution.py:411
  35.1 12.4 %all-to-all-start.2 = ((bf16[32,16,128]{2,1,0:T(8,128)(2,1)}), bf16[32,16,128]{2,1,0:T(8,128)(2,1)S(1)}, u32[]{:S(2)}, u32[]{:S(2)}) async-start(bf16[32,16,128]{2,1,0:T(8,128)(2,1)} %shard_map.100), calls=%async_computation.2 | async-start | bytes 262144 | tf_op jit(solution)/shard_map/all_to_all | solution.py:481

commit v11 on v10

--- a/solution.py
+++ b/solution.py
@@ -41,7 +41,7 @@
     return lax.broadcasted_iota(jnp.int32, shape, len(shape) - 1)
 
 
-def pick_kernel(devices, ids_hbm, latents_hbm, out_ref, ids_ref, latents_ref, rows_ref, sems):
+def pick_kernel(scenes, ids_hbm, latents_hbm, out_ref, ids_ref, latents_ref, rows_ref, sems):
     ids_copy = pltpu.make_async_copy(ids_hbm, ids_ref, sems.at[0])
     latents_copy = pltpu.make_async_copy(latents_hbm, latents_ref, sems.at[1])
     ids_copy.start()
@@ -61,9 +61,13 @@
     for tile in range(tiles):
         rows_ref[pl.ds(margin + tile, bricks, stride=tiles), :] = picked[:, tile * 128 : tile * 128 + 128]
     count = out_ref.shape[1]
-    for receiver in range(devices):
+    wanted = [jnp.where(lax.axis_index("dp") == scene, 1.0, 0.0).astype(F32) for scene in range(scenes)]
+    for receiver in range(out_ref.shape[0] // scenes):
         start = margin + BRICKS * (receiver - 1) * tiles
-        out_ref[receiver] = rows_ref[start : start + count].astype(BF16)
+        found = rows_ref[start : start + count]
+        for scene in range(scenes):
+            kept = found * wanted[scene] if scenes > 1 else found
+            out_ref[receiver * scenes + scene] = kept.astype(BF16)
 
 
 def build_band(band_ref, rows):
@@ -184,8 +188,8 @@
     to_partners(high_out, low_out, far_out, near_out)
 
 
-def unpack_depth(rows, high):
-    packed = jnp.concatenate([rows[:, :128], rows[:, 128:]], axis=0)
+def unpack_depth(halves, high):
+    packed = jnp.concatenate(halves, axis=0)
     pieces = []
     for part in range(4):
         shift = ((3 - part) if high else (4 - part)) % 4 * CHANNELS
@@ -195,7 +199,7 @@
 
 def first_kernel(
     links_in, received_ref, up_ref, band_ref, weights_ref,
-    slope_out, hidden_out, turned_out, pad_out, back_out, high_out, low_out,
+    slope_out, hidden_out, turned_out, pad_out, back_out, high_out, low_out, masks_out,
     volumes_ref, rows_ref, halves_ref, faces_ref, links_ref, links_sem,
 ):
     links_copy = pltpu.make_async_copy(links_in, links_ref, links_sem)
@@ -218,6 +222,7 @@
                 cell * 8 : cell * 8 + 8, sub * 128 : sub * 128 + 128
             ]
     links_copy.wait()
+    put_masks(masks_out, links_ref)
     for brick in range(BRICKS):
 
         def near(face):
@@ -282,7 +287,17 @@
     return places
 
 
-def pad_all(pad_ref, bricks, links_ref, high_pool, low_pool, high_own, low_own, far, near):
+def put_masks(masks_ref, links_ref):
+    position = lax.axis_index("space")
+    for brick in range(BRICKS):
+        for face in range(6):
+            first = links_ref[0, brick, face] - BRICKS * (position - 1 if face % 2 == 0 else position)
+            for i in range(2 * BRICKS):
+                row = (brick * 6 + face) * 2 * BRICKS + i
+                masks_ref[row : row + 1, :] = jnp.full((1, 128), jnp.where(first == i, 1.0, 0.0).astype(F32))
+
+
+def pad_all(pad_ref, bricks, masks_ref, high_pool, low_pool, high_own, low_own, far, near):
     position = lax.axis_index("space")
     half = BRICKS * FACE
     even = position % 2 == 0
@@ -292,37 +307,34 @@
     low_pool[half:] = jnp.where(even, near[...], far[...]).astype(F32)
     for brick, lines in enumerate(bricks):
 
-        def rows(face, axis):
-            link = links_ref[0, brick, face]
-            high = face % 2 == 0
-            index = jnp.clip(link - BRICKS * (position - 1 if high else position), 0, 2 * BRICKS - 1)
-            pool = high_pool if high else low_pool
-            present = jnp.where(link >= 0, 1.0, 0.0).astype(F32)
-            return pool[pl.ds(pl.multiple_of(index * FACE + axis * EDGE, 8), EDGE), :] * present
-
         def face(number, axis):
-            found = rows(number, axis)
-            return found[:, :HALF], found[:, HALF:]
+            pool = high_pool if number % 2 == 0 else low_pool
+            total = [0.0, 0.0]
+            for i in range(2 * BRICKS):
+                row = (brick * 6 + number) * 2 * BRICKS + i
+                mask = masks_ref[row : row + 1, :]
+                start = i * FACE + axis * EDGE
+                for part in range(2):
+                    found = pool[start : start + EDGE, part * HALF : part * HALF + HALF]
+                    total[part] = total[part] + found * mask
+            return total
 
         put_padded(
             pad_ref, brick, lines, face(0, 0), face(1, 0), face(2, 1), face(3, 1),
-            unpack_depth(rows(4, 2), True), unpack_depth(rows(5, 2), False),
+            unpack_depth(face(4, 2), True), unpack_depth(face(5, 2), False),
         )
 
 
 def second_kernel(
-    links_in, cotangent_ref, band_ref, slope_ref, hidden_ref, lifted_pad, high_own, low_own, far, near,
+    masks_ref, cotangent_ref, band_ref, slope_ref, hidden_ref, lifted_pad, high_own, low_own, far, near,
     hidden_high, hidden_low,
     sums_out, lifted_out, far_out, near_out,
-    high_pool, low_pool, cotangent_pad, sums_ref, links_ref, links_sem,
+    high_pool, low_pool, cotangent_pad, sums_ref,
 ):
-    links_copy = pltpu.make_async_copy(links_in, links_ref, links_sem)
-    links_copy.start()
     to_partners(hidden_high, hidden_low, far_out, near_out)
     lifted_out[...] = window(lifted_pad, 4)[:, :HALF]
     bricks = cotangent_lines(cotangent_ref)
-    links_copy.wait()
-    pad_all(cotangent_pad, bricks, links_ref, high_pool, low_pool, high_own, low_own, far, near)
+    pad_all(cotangent_pad, bricks, masks_ref, high_pool, low_pool, high_own, low_own, far, near)
     gradient = (convolve(cotangent_pad, band_ref) * slope_ref[...]).astype(BF16)
     gradient = jnp.transpose(gradient.astype(F32)).astype(BF16)
     hidden = hidden_ref[...]
@@ -339,15 +351,12 @@
 
 
 def fine_kernel(
-    links_in, weights_ref, lifted_ref, hidden_ref, high_own, low_own, far, near,
-    fine_out, high_pool, low_pool, hidden_pad, band_ref, links_ref, links_sem,
+    masks_ref, weights_ref, lifted_ref, hidden_ref, high_own, low_own, far, near,
+    fine_out, high_pool, low_pool, hidden_pad, band_ref,
 ):
-    links_copy = pltpu.make_async_copy(links_in, links_ref, links_sem)
-    links_copy.start()
     build_band(band_ref, weight_rows(weights_ref[...].astype(F32)))
-    links_copy.wait()
     bricks = half_lines(hidden_ref[...].astype(F32))
-    pad_all(hidden_pad, bricks, links_ref, high_pool, low_pool, high_own, low_own, far, near)
+    pad_all(hidden_pad, bricks, masks_ref, high_pool, low_pool, high_own, low_own, far, near)
     fine = lifted_ref[...].astype(F32) + convolve(hidden_pad, band_ref)
     fine = fine.reshape(LINES // EDGE, 2, EDGE, HALF)
     fine = jnp.concatenate([fine[:, 0], fine[:, 1]], axis=-1)
@@ -417,9 +426,10 @@
     held, width = coarse_latents.shape[1:]
     bricks = active_blocks.shape[1]
     tiles = width // 128
+    scenes = 2 if lax.axis_size("dp") == 2 else 1
     packed = call(
-        functools.partial(pick_kernel, devices),
-        shape(devices, 3 * BRICKS * tiles, 128),
+        functools.partial(pick_kernel, scenes),
+        shape(devices * scenes, 3 * BRICKS * tiles, 128),
         [
             pltpu.VMEM((1, bricks), jnp.int32),
             pltpu.VMEM((1, held, width), BF16),
@@ -430,7 +440,8 @@
         inputs=2,
         limit=60,
     )(active_blocks, coarse_latents)
-    received = lax.all_to_all(packed, "space", split_axis=0, concat_axis=0, tiled=True)
+    axes = ("space", "dp")
+    received = lax.all_to_all(packed, axes if scenes == 2 else "space", split_axis=0, concat_axis=0, tiled=True)
     band = pltpu.VMEM(BAND, BF16)
     cost = pl.CostEstimate(flops=10**9, bytes_accessed=2 * 10**6, transcendentals=0)
     face = shape(BRICKS * FACE, LINE)
@@ -445,11 +456,11 @@
     far = swapped(far, 1)
     near = swapped(near, 0)
     band_one = call(band_kernel, shape(*BAND), cost=cost)(conv_one)
-    slope, hidden, turned, lifted_pad, band_back, hidden_high, hidden_low = call(
+    slope, hidden, turned, lifted_pad, band_back, hidden_high, hidden_low, masks = call(
         first_kernel,
         (
             shape(ROWS, HALF, dtype=F32), volume, shape(HALF, ROWS), shape(*pad_shape), shape(*BAND),
-            face, face,
+            face, face, shape(BRICKS * 6 * 2 * BRICKS, 128, dtype=F32),
         ),
         [pltpu.VMEM((2, 8 * CUBE, 128), F32), pltpu.VMEM((8 * tiles, 128), F32), halves, faces, *links],
         hbm=(0,),
@@ -460,19 +471,17 @@
     sums, lifted, hidden_far, hidden_near = call(
         second_kernel,
         (shape(everyone, per * 8, 128), volume, face, face),
-        [pool, pool, pad, pltpu.VMEM((everyone * per * 8, 128), F32), *links],
-        hbm=(0,),
+        [pool, pool, pad, pltpu.VMEM((everyone * per * 8, 128), F32)],
         inputs=12,
     )(
-        face_links, cotangent, band_back, slope, turned, lifted_pad, high, low, far, near,
+        masks, cotangent, band_back, slope, turned, lifted_pad, high, low, far, near,
         hidden_high, hidden_low,
     )
     hidden_far = swapped(hidden_far, 1)
     hidden_near = swapped(hidden_near, 0)
-    fine = call(fine_kernel, shape(*cotangent.shape), [pool, pool, pad, band, *links], hbm=(0,), inputs=8, cost=cost)(
-        face_links, conv_two, lifted, hidden, hidden_high, hidden_low, hidden_far, hidden_near
+    fine = call(fine_kernel, shape(*cotangent.shape), [pool, pool, pad, band], inputs=8, cost=cost)(
+        masks, conv_two, lifted, hidden, hidden_high, hidden_low, hidden_far, hidden_near
     )
-    axes = ("space", "dp")
     parts = lax.all_to_all(sums, axes, split_axis=0, concat_axis=0, tiled=True)
     scale = 1.0 / math.sqrt(lax.axis_size("dp") * devices * BRICKS * EDGE**3)
     total = call(functools.partial(sum_kernel, scale), shape(*sums.shape), hbm=(1, 2), inputs=3)(

time: 48.9 us -> 47.6 us (0.973)
  starting transfers between devices: 26.8 us -> 24.7 us
  waiting for transfers between devices: 11.3 us -> 13 us
  Pallas kernels: 9.58 us -> 8.76 us
    all_to_all x1, waiting for transfers between devices: 1.82 us -> 3.2 us  [body(): lax.all_to_all(packed, axes if scenes == 2 else 'space', split_axis=0, co...]
    all_to_all x1, starting transfers between devices: 8.46 us -> 7.3 us  [body(): lax.all_to_all(packed, axes if scenes == 2 else 'space', split_axis=0, co...]
    all_to_all x1, starting transfers between devices: 3.63 us -> 2.86 us  [body(): parts = lax.all_to_all(sums, axes, split_axis=0, concat_axis=0, tiled=True)]
    pallas_call x1, Pallas kernels: 2.39 us -> 1.85 us  [body(): call(second_kernel, (shape(everyone, per * 8, 128), volume, face, face),...]
where the time goes in v11:
time: 47.6 us; the launch traced here: 47.3 us
  starting transfers between devices  24.7 us (52%)
  waiting for transfers between devices  13 us (27%)
  Pallas kernels  8.76 us (18%)
  between operations  0.77 us (2%)
    ppermute x4, starting transfers between devices, swapped(): lax.ppermute(value, 'space', pairs + [(target, source) for source, target...  10.4 us
    all_to_all x1, starting transfers between devices, body(): lax.all_to_all(packed, axes if scenes == 2 else 'space', split_axis=0, co...  7.3 us
    all_to_all x1, waiting for transfers between devices, body(): lax.all_to_all(total, axes, split_axis=0, concat_axis=0, tiled=True)  6.8 us
    all_to_all x1, starting transfers between devices, body(): lax.all_to_all(total, axes, split_axis=0, concat_axis=0, tiled=True)  4.16 us
    all_to_all x1, waiting for transfers between devices, body(): lax.all_to_all(packed, axes if scenes == 2 else 'space', split_axis=0, co...  3.2 us
    all_to_all x1, starting transfers between devices, body(): parts = lax.all_to_all(sums, axes, split_axis=0, concat_axis=0, tiled=True)  2.86 us
    ppermute x4, waiting for transfers between devices, swapped(): lax.ppermute(value, 'space', pairs + [(target, source) for source, target...  2.06 us
    pallas_call x1, Pallas kernels, body(): call(second_kernel, (shape(everyone, per * 8, 128), volume, face, face),...  1.85 us
  transfers between devices with their start and end apart: 7, of which 4 were waited for; matrix products, arithmetic and copies ran while one was open for 0% of the time, Pallas kernels for 7%

profile of v11, /device:TPU:0, one launch (start us, length us, event | category | flops | bytes accessed | tf_op | source)
XLA Modules:
  0.0 47.3 jit_solution(3972140071673055431)
XLA Ops:
  0.6 1.7 %shard_map.94 = bf16[32,24,128]{2,1,0:T(8,128)(2,1)} custom-call(s32[1,32]{1,0:T(1,128)} %ids_hbm.1, bf16[1,64,512]{2,1,0:T(8,128)(2,1)} %latents_hbm.1), custom_call_target="tpu_custom_call" | custom-call | tf_op jit(solution)/shard_map/pallas_call | solution.py:430
  2.4 0.0 copy-start
  2.4 0.0 copy-start.4
  2.4 7.3 %all-to-all-start = ((bf16[32,24,128]{2,1,0:T(8,128)(2,1)}), bf16[32,24,128]{2,1,0:T(8,128)(2,1)S(1)}, u32[]{:S(2)}, u32[]{:S(2)}) async-start(bf16[32,24,128]{2,1,0:T(8,128)(2,1)} %shard_map.94), calls=%async_computation | async-start | bytes 393216 | tf_op jit(solution)/shard_map/all_to_all | solution.py:444
  9.7 0.1 shard_map.97
  9.8 0.7 %collective-permute-start = (bf16[48,256]{1,0:T(8,128)(2,1)S(1)}, bf16[48,256]{1,0:T(8,128)(2,1)S(1)}, u32[]{:S(2)}, u32[]{:S(2)}) collective-permute-start(bf16[48,256]{1,0:T(8,128)(2,1)S(1)} %get-tuple-element.28), channel_id=1, source_target_pairs={{2,4},{6,8},{10,12},{14,16},{18,20},{22,24},{26,28},{4,2},{8,6},{1... | collective-permute-start | bytes 73736 | tf_op jit(solution)/shard_map/ppermute | solution.py:420
  10.5 0.0 copy-start.1
  10.5 0.0 copy-start.2
  10.5 0.0 copy-start.3
  10.5 4.5 %collective-permute-start.1 = (bf16[48,256]{1,0:T(8,128)(2,1)S(1)}, bf16[48,256]{1,0:T(8,128)(2,1)S(1)}, u32[]{:S(2)}, u32[]{:S(2)}) collective-permute-start(bf16[48,256]{1,0:T(8,128)(2,1)S(1)} %get-tuple-element.29), channel_id=1, source_target_pairs={{0,2},{4,6},{8,10},{12,14},{16,18},{20,22},{24,26},{28,30},{2,0},{... | collective-permute-start | bytes 73736 | tf_op jit(solution)/shard_map/ppermute | solution.py:420
  15.1 0.3 shard_map.95.band_ref
  15.4 3.2 %all-to-all-done.received_ref = bf16[32,24,128]{2,1,0:T(8,128)(2,1)S(1)} async-done(((bf16[32,24,128]{2,1,0:T(8,128)(2,1)}), bf16[32,24,128]{2,1,0:T(8,128)(2,1)S(1)}, u32[]{:S(2)}, u32[]{:S(2)}) %all-to-all-start) | async-done | bytes 196640 | tf_op jit(solution)/shard_map/all_to_all | solution.py:444
  18.6 1.4 %shard_map.96 = (f32[256,128]{1,0:T(8,128)S(1)}, bf16[256,128]{1,0:T(8,128)(2,1)S(1)}, bf16[128,256]{1,0:T(8,128)(2,1)S(1)}, bf16[3,2,10,16,256]{4,3,2,1,0:T(8,1...) custom-call(s32[1,2,6]{2,1,0:T(2,128)S(1)} %copy-done.3, ...), custom_call_target="tpu_custom_call" | custom-call | tf_op jit(solution)/shard_map/pallas_call | solution.py:459
  20.0 1.9 %shard_map.98 = (bf16[32,16,128]{2,1,0:T(8,128)(2,1)}, bf16[256,128]{1,0:T(8,128)(2,1)S(1)}, bf16[48,256]{1,0:T(8,128)(2,1)S(1)}, bf16[48,256]{1,0:T(8,128)(2,1)S(1)}) custom-call(f32[48,128]{1,0:T(8,128)S(1)} %get-tuple-element.21.masks_ref, bf16[1,2,8,8,256]{4,3,2,1,0:T(8,128)(2,1)S(1)} %copy-done, bf16[9,256,128]{2,1,0:T(8,128)(2,1)S(1)} %get-tuple-element.22.band_ref, ...), custom_call_target="tpu_custom_call" | custom-call | tf_op jit(solution)/shard_map/pallas_call | solution.py:471
  21.9 2.9 %all-to-all-start.1 = ((bf16[32,16,128]{2,1,0:T(8,128)(2,1)}), bf16[32,16,128]{2,1,0:T(8,128)(2,1)S(1)}, u32[]{:S(2)}, u32[]{:S(2)}) async-start(bf16[32,16,128]{2,1,0:T(8,128)(2,1)} %get-tuple-element.36), calls=%async_computation.1 | async-start | bytes 262144 | tf_op jit(solution)/shard_map/all_to_all | solution.py:485
  24.7 0.7 %collective-permute-start.2 = (bf16[48,256]{1,0:T(8,128)(2,1)S(1)}, bf16[48,256]{1,0:T(8,128)(2,1)S(1)}, u32[]{:S(2)}, u32[]{:S(2)}) collective-permute-start(bf16[48,256]{1,0:T(8,128)(2,1)S(1)} %get-tuple-element.34), channel_id=1, source_target_pairs={{2,4},{6,8},{10,12},{14,16},{18,20},{22,24},{26,28},{4,2},{8,6},{1... | collective-permute-start | bytes 73736 | tf_op jit(solution)/shard_map/ppermute | solution.py:420
  25.4 4.5 %collective-permute-start.3 = (bf16[48,256]{1,0:T(8,128)(2,1)S(1)}, bf16[48,256]{1,0:T(8,128)(2,1)S(1)}, u32[]{:S(2)}, u32[]{:S(2)}) collective-permute-start(bf16[48,256]{1,0:T(8,128)(2,1)S(1)} %get-tuple-element.35), channel_id=1, source_target_pairs={{0,2},{4,6},{8,10},{12,14},{16,18},{20,22},{24,26},{28,30},{2,0},{... | collective-permute-start | bytes 73736 | tf_op jit(solution)/shard_map/ppermute | solution.py:420
  29.9 2.1 %collective-permute-done.3.near._near = bf16[48,256]{1,0:T(8,128)(2,1)S(1)} collective-permute-done((bf16[48,256]{1,0:T(8,128)(2,1)S(1)}, bf16[48,256]{1,0:T(8,128)(2,1)S(1)}, u32[]{:S(2)}, u32[]{:S(2)}) %collective-permute-start.3) | collective-permute-done | bytes 24608 | tf_op jit(solution)/shard_map/ppermute | solution.py:420
  32.0 1.0 %all-to-all-done.1.parts_ref = bf16[32,16,128]{2,1,0:T(8,128)(2,1)S(1)} async-done(((bf16[32,16,128]{2,1,0:T(8,128)(2,1)}), bf16[32,16,128]{2,1,0:T(8,128)(2,1)S(1)}, u32[]{:S(2)}, u32[]{:S(2)}) %all-to-all-start.1) | async-done | bytes 131104 | tf_op jit(solution)/shard_map/all_to_all | solution.py:485
  32.9 0.9 %shard_map.100 = bf16[32,16,128]{2,1,0:T(8,128)(2,1)} custom-call(bf16[32,16,128]{2,1,0:T(8,128)(2,1)S(1)} %all-to-all-done.1.parts_ref, bf16[48,256]{1,0:T(8,128)(2,1)S(1)} %collective-permute-done.2.far._far, bf16[48,256]{1,0:T(8,128)(2,1)S(1)} %collective-permute-done.3.near._near), custom_call_target="tpu_custom_call" | custom-call | tf_op jit(solution)/shard_map/pallas_call | solution.py:487
  33.9 4.2 %all-to-all-start.2 = ((bf16[32,16,128]{2,1,0:T(8,128)(2,1)}), bf16[32,16,128]{2,1,0:T(8,128)(2,1)S(1)}, u32[]{:S(2)}, u32[]{:S(2)}) async-start(bf16[32,16,128]{2,1,0:T(8,128)(2,1)} %shard_map.100), calls=%async_computation.2 | async-start | bytes 262144 | tf_op jit(solution)/shard_map/all_to_all | solution.py:490
  38.0 1.4 %shard_map.99 = bf16[1,2,8,8,256]{4,3,2,1,0:T(8,128)(2,1)} custom-call(f32[48,128]{1,0:T(8,128)S(1)} %get-tuple-element.21.masks_ref, bf16[27,32,32]{2,1,0:T(8,128)(2,1)S(1)} %copy-done.2, bf16[256,128]{1,0:T(8,128)(2,1)S(1)} %get-tuple-element.32.lifted_ref, bf16[256,128]{1,0:T(8,128)(2,1)S(1)} %get-tuple-element.33.hidden_ref, ...), custom_call_target="tpu_custom_call" | custom-call | flops 1000000000 | bytes 2000000 | tf_op jit(solution)/shard_map/pallas_call | solution.py:482
  39.5 6.8 %all-to-all-done.2.sums_ref = bf16[32,16,128]{2,1,0:T(8,128)(2,1)S(1)} async-done(((bf16[32,16,128]{2,1,0:T(8,128)(2,1)}), bf16[32,16,128]{2,1,0:T(8,128)(2,1)S(1)}, u32[]{:S(2)}, u32[]{:S(2)}) %all-to-all-start.2) | async-done | bytes 131104 | tf_op jit(solution)/shard_map/all_to_all | solution.py:490
  46.3 1.0 %shard_map.101 = (f32[27,32,32]{2,1,0:T(8,128)}, f32[27,32,32]{2,1,0:T(8,128)}) custom-call(bf16[32,16,128]{2,1,0:T(8,128)(2,1)S(1)} %all-to-all-done.2.sums_ref), custom_call_target="tpu_custom_call" | custom-call | tf_op jit(solution)/shard_map/pallas_call | solution.py:494
  (8 shorter events, 0.0 us)
Async XLA Ops:
  2.4 7.3 %copy-start = (bf16[1,2,8,8,256]{4,3,2,1,0:T(8,128)(2,1)S(1)}, bf16[1,2,8,8,256]{4,3,2,1,0:T(8,128)(2,1)}, u32[]{:S(2)}) copy-start(bf16[1,2,8,8,256]{4,3,2,1,0:T(8,128)(2,1)} %cotangent_ref.3) | copy-start | bytes 196612
  2.4 12.7 %copy-start.4 = (bf16[27,32,32]{2,1,0:T(8,128)(2,1)S(1)}, bf16[27,32,32]{2,1,0:T(8,128)(2,1)}, u32[]{:S(2)}) copy-start(bf16[27,32,32]{2,1,0:T(8,128)(2,1)} %weights_ref.3) | copy-start | bytes 165892
  2.4 16.2 %all-to-all-start = ((bf16[32,24,128]{2,1,0:T(8,128)(2,1)}), bf16[32,24,128]{2,1,0:T(8,128)(2,1)S(1)}, u32[]{:S(2)}, u32[]{:S(2)}) async-start(bf16[32,24,128]{2,1,0:T(8,128)(2,1)} %shard_map.94), calls=%async_computation | async-start | bytes 393216 | tf_op jit(solution)/shard_map/all_to_all | solution.py:444
  9.8 10.2 %collective-permute-start = (bf16[48,256]{1,0:T(8,128)(2,1)S(1)}, bf16[48,256]{1,0:T(8,128)(2,1)S(1)}, u32[]{:S(2)}, u32[]{:S(2)}) collective-permute-start(bf16[48,256]{1,0:T(8,128)(2,1)S(1)} %get-tuple-element.28), channel_id=1, source_target_pairs={{2,4},{6,8},{10,12},{14,16},{18,20},{22,24},{26,28},{4,2},{8,6},{1... | collective-permute-start | bytes 73736 | tf_op jit(solution)/shard_map/ppermute | solution.py:420
  10.5 8.1 %copy-start.1 = (bf16[64,2048]{1,0:T(8,128)(2,1)S(1)}, bf16[64,2048]{1,0:T(8,128)(2,1)}, u32[]{:S(2)}) copy-start(bf16[64,2048]{1,0:T(8,128)(2,1)} %up_ref.1) | copy-start | bytes 786436
  10.5 8.1 %copy-start.2 = (bf16[27,32,32]{2,1,0:T(8,128)(2,1)S(1)}, bf16[27,32,32]{2,1,0:T(8,128)(2,1)}, u32[]{:S(2)}) copy-start(bf16[27,32,32]{2,1,0:T(8,128)(2,1)} %weights_ref.5) | copy-start | bytes 165892
  10.5 8.1 %copy-start.3 = (s32[1,2,6]{2,1,0:T(2,128)S(1)}, s32[1,2,6]{2,1,0:T(2,128)}, u32[]{:S(2)}) copy-start(s32[1,2,6]{2,1,0:T(2,128)} %links_in.1) | copy-start | bytes 148
  10.5 9.5 %collective-permute-start.1 = (bf16[48,256]{1,0:T(8,128)(2,1)S(1)}, bf16[48,256]{1,0:T(8,128)(2,1)S(1)}, u32[]{:S(2)}, u32[]{:S(2)}) collective-permute-start(bf16[48,256]{1,0:T(8,128)(2,1)S(1)} %get-tuple-element.29), channel_id=1, source_target_pairs={{0,2},{4,6},{8,10},{12,14},{16,18},{20,22},{24,26},{28,30},{2,0},{... | collective-permute-start | bytes 73736 | tf_op jit(solution)/shard_map/ppermute | solution.py:420
  21.9 11.1 %all-to-all-start.1 = ((bf16[32,16,128]{2,1,0:T(8,128)(2,1)}), bf16[32,16,128]{2,1,0:T(8,128)(2,1)S(1)}, u32[]{:S(2)}, u32[]{:S(2)}) async-start(bf16[32,16,128]{2,1,0:T(8,128)(2,1)} %get-tuple-element.36), calls=%async_computation.1 | async-start | bytes 262144 | tf_op jit(solution)/shard_map/all_to_all | solution.py:485
  24.7 5.2 %collective-permute-start.2 = (bf16[48,256]{1,0:T(8,128)(2,1)S(1)}, bf16[48,256]{1,0:T(8,128)(2,1)S(1)}, u32[]{:S(2)}, u32[]{:S(2)}) collective-permute-start(bf16[48,256]{1,0:T(8,128)(2,1)S(1)} %get-tuple-element.34), channel_id=1, source_target_pairs={{2,4},{6,8},{10,12},{14,16},{18,20},{22,24},{26,28},{4,2},{8,6},{1... | collective-permute-start | bytes 73736 | tf_op jit(solution)/shard_map/ppermute | solution.py:420
  25.4 6.6 %collective-permute-start.3 = (bf16[48,256]{1,0:T(8,128)(2,1)S(1)}, bf16[48,256]{1,0:T(8,128)(2,1)S(1)}, u32[]{:S(2)}, u32[]{:S(2)}) collective-permute-start(bf16[48,256]{1,0:T(8,128)(2,1)S(1)} %get-tuple-element.35), channel_id=1, source_target_pairs={{0,2},{4,6},{8,10},{12,14},{16,18},{20,22},{24,26},{28,30},{2,0},{... | collective-permute-start | bytes 73736 | tf_op jit(solution)/shard_map/ppermute | solution.py:420
  33.9 12.4 %all-to-all-start.2 = ((bf16[32,16,128]{2,1,0:T(8,128)(2,1)}), bf16[32,16,128]{2,1,0:T(8,128)(2,1)S(1)}, u32[]{:S(2)}, u32[]{:S(2)}) async-start(bf16[32,16,128]{2,1,0:T(8,128)(2,1)} %shard_map.100), calls=%async_computation.2 | async-start | bytes 262144 | tf_op jit(solution)/shard_map/all_to_all | solution.py:490

commit v12 on v11

--- a/solution.py
+++ b/solution.py
@@ -411,6 +411,10 @@
     )
 
 
+def inner(*dims, dtype=BF16):
+    return pltpu.VMEM(dims, dtype)
+
+
 def shape(*dims, dtype=BF16):
     return jax.ShapeDtypeStruct(dims, dtype)
 
@@ -429,7 +433,7 @@
     scenes = 2 if lax.axis_size("dp") == 2 else 1
     packed = call(
         functools.partial(pick_kernel, scenes),
-        shape(devices * scenes, 3 * BRICKS * tiles, 128),
+        inner(devices * scenes, 3 * BRICKS * tiles, 128),
         [
             pltpu.VMEM((1, bricks), jnp.int32),
             pltpu.VMEM((1, held, width), BF16),
@@ -438,8 +442,7 @@
         ],
         hbm=(0, 1),
         inputs=2,
-        limit=60,
-    )(active_blocks, coarse_latents)
+    )(*[pltpu.with_memory_space_constraint(x, pltpu.HBM) for x in (active_blocks, coarse_latents)])
     axes = ("space", "dp")
     received = lax.all_to_all(packed, axes if scenes == 2 else "space", split_axis=0, concat_axis=0, tiled=True)
     band = pltpu.VMEM(BAND, BF16)
@@ -470,7 +473,7 @@
     per += per % 2
     sums, lifted, hidden_far, hidden_near = call(
         second_kernel,
-        (shape(everyone, per * 8, 128), volume, face, face),
+        (inner(everyone, per * 8, 128), volume, face, face),
         [pool, pool, pad, pltpu.VMEM((everyone * per * 8, 128), F32)],
         inputs=12,
     )(
@@ -484,7 +487,7 @@
     )
     parts = lax.all_to_all(sums, axes, split_axis=0, concat_axis=0, tiled=True)
     scale = 1.0 / math.sqrt(lax.axis_size("dp") * devices * BRICKS * EDGE**3)
-    total = call(functools.partial(sum_kernel, scale), shape(*sums.shape), hbm=(1, 2), inputs=3)(
+    total = call(functools.partial(sum_kernel, scale), inner(*sums.shape), hbm=(1, 2), inputs=3)(
         parts, hidden_far, hidden_near
     )
     gathered = lax.all_to_all(total, axes, split_axis=0, concat_axis=0, tiled=True)

time: 47.6 us -> 47.6 us (level)
  no operation moved by 1% of the time
where the time goes in v12:
time: 47.6 us; the launch traced here: 47.3 us
  starting transfers between devices  24.7 us (52%)
  waiting for transfers between devices  13 us (27%)
  Pallas kernels  8.77 us (18%)
  between operations  0.77 us (2%)
    ppermute x4, starting transfers between devices, swapped(): lax.ppermute(value, 'space', pairs + [(target, source) for source, target...  10.4 us
    all_to_all x1, starting transfers between devices, body(): lax.all_to_all(packed, axes if scenes == 2 else 'space', split_axis=0, co...  7.3 us
    all_to_all x1, waiting for transfers between devices, body(): lax.all_to_all(total, axes, split_axis=0, concat_axis=0, tiled=True)  6.79 us
    all_to_all x1, starting transfers between devices, body(): lax.all_to_all(total, axes, split_axis=0, concat_axis=0, tiled=True)  4.16 us
    all_to_all x1, waiting for transfers between devices, body(): lax.all_to_all(packed, axes if scenes == 2 else 'space', split_axis=0, co...  3.2 us
    all_to_all x1, starting transfers between devices, body(): parts = lax.all_to_all(sums, axes, split_axis=0, concat_axis=0, tiled=True)  2.85 us
    ppermute x4, waiting for transfers between devices, swapped(): lax.ppermute(value, 'space', pairs + [(target, source) for source, target...  2.06 us
    pallas_call x1, Pallas kernels, body(): call(second_kernel, (inner(everyone, per * 8, 128), volume, face, face),...  1.87 us
  transfers between devices with their start and end apart: 7, of which 4 were waited for; matrix products, arithmetic and copies ran while one was open for 0% of the time, Pallas kernels for 7%

profile of v12, /device:TPU:0, one launch (start us, length us, event | category | flops | bytes accessed | tf_op | source)
XLA Modules:
  0.0 47.3 jit_solution(11057657731021010571)
XLA Ops:
  0.6 1.7 %shard_map.94 = bf16[32,24,128]{2,1,0:T(8,128)(2,1)} custom-call(s32[1,32]{1,0:T(1,128)} %ids_hbm.1, bf16[1,64,512]{2,1,0:T(8,128)(2,1)} %latents_hbm.1), custom_call_target="tpu_custom_call" | custom-call | tf_op jit(solution)/shard_map/pallas_call | solution.py:434
  2.4 0.0 copy-start
  2.4 0.0 copy-start.4
  2.4 7.3 %all-to-all-start = ((bf16[32,24,128]{2,1,0:T(8,128)(2,1)}), bf16[32,24,128]{2,1,0:T(8,128)(2,1)S(1)}, u32[]{:S(2)}, u32[]{:S(2)}) async-start(bf16[32,24,128]{2,1,0:T(8,128)(2,1)} %shard_map.94), calls=%async_computation | async-start | bytes 393216 | tf_op jit(solution)/shard_map/all_to_all | solution.py:447
  9.7 0.1 shard_map.97
  9.8 0.7 %collective-permute-start = (bf16[48,256]{1,0:T(8,128)(2,1)S(1)}, bf16[48,256]{1,0:T(8,128)(2,1)S(1)}, u32[]{:S(2)}, u32[]{:S(2)}) collective-permute-start(bf16[48,256]{1,0:T(8,128)(2,1)S(1)} %get-tuple-element.28), channel_id=1, source_target_pairs={{2,4},{6,8},{10,12},{14,16},{18,20},{22,24},{26,28},{4,2},{8,6},{1... | collective-permute-start | bytes 73736 | tf_op jit(solution)/shard_map/ppermute | solution.py:424
  10.5 0.0 copy-start.1
  10.5 0.0 copy-start.2
  10.5 0.0 copy-start.3
  10.5 4.5 %collective-permute-start.1 = (bf16[48,256]{1,0:T(8,128)(2,1)S(1)}, bf16[48,256]{1,0:T(8,128)(2,1)S(1)}, u32[]{:S(2)}, u32[]{:S(2)}) collective-permute-start(bf16[48,256]{1,0:T(8,128)(2,1)S(1)} %get-tuple-element.29), channel_id=1, source_target_pairs={{0,2},{4,6},{8,10},{12,14},{16,18},{20,22},{24,26},{28,30},{2,0},{... | collective-permute-start | bytes 73736 | tf_op jit(solution)/shard_map/ppermute | solution.py:424
  15.1 0.3 shard_map.95.band_ref
  15.4 3.2 %all-to-all-done.received_ref = bf16[32,24,128]{2,1,0:T(8,128)(2,1)S(1)} async-done(((bf16[32,24,128]{2,1,0:T(8,128)(2,1)}), bf16[32,24,128]{2,1,0:T(8,128)(2,1)S(1)}, u32[]{:S(2)}, u32[]{:S(2)}) %all-to-all-start) | async-done | bytes 196640 | tf_op jit(solution)/shard_map/all_to_all | solution.py:447
  18.6 1.4 %shard_map.96 = (f32[256,128]{1,0:T(8,128)S(1)}, bf16[256,128]{1,0:T(8,128)(2,1)S(1)}, bf16[128,256]{1,0:T(8,128)(2,1)S(1)}, bf16[3,2,10,16,256]{4,3,2,1,0:T(8,1...) custom-call(s32[1,2,6]{2,1,0:T(2,128)S(1)} %copy-done.3, ...), custom_call_target="tpu_custom_call" | custom-call | tf_op jit(solution)/shard_map/pallas_call | solution.py:462
  20.0 1.9 %shard_map.98 = (bf16[32,16,128]{2,1,0:T(8,128)(2,1)}, bf16[256,128]{1,0:T(8,128)(2,1)S(1)}, bf16[48,256]{1,0:T(8,128)(2,1)S(1)}, bf16[48,256]{1,0:T(8,128)(2,1)S(1)}) custom-call(f32[48,128]{1,0:T(8,128)S(1)} %get-tuple-element.21.masks_ref, bf16[1,2,8,8,256]{4,3,2,1,0:T(8,128)(2,1)S(1)} %copy-done, bf16[9,256,128]{2,1,0:T(8,128)(2,1)S(1)} %get-tuple-element.22.band_ref, ...), custom_call_target="tpu_custom_call" | custom-call | tf_op jit(solution)/shard_map/pallas_call | solution.py:474
  21.9 2.9 %all-to-all-start.1 = ((bf16[32,16,128]{2,1,0:T(8,128)(2,1)}), bf16[32,16,128]{2,1,0:T(8,128)(2,1)S(1)}, u32[]{:S(2)}, u32[]{:S(2)}) async-start(bf16[32,16,128]{2,1,0:T(8,128)(2,1)} %get-tuple-element.36), calls=%async_computation.1 | async-start | bytes 262144 | tf_op jit(solution)/shard_map/all_to_all | solution.py:488
  24.7 0.7 %collective-permute-start.2 = (bf16[48,256]{1,0:T(8,128)(2,1)S(1)}, bf16[48,256]{1,0:T(8,128)(2,1)S(1)}, u32[]{:S(2)}, u32[]{:S(2)}) collective-permute-start(bf16[48,256]{1,0:T(8,128)(2,1)S(1)} %get-tuple-element.34), channel_id=1, source_target_pairs={{2,4},{6,8},{10,12},{14,16},{18,20},{22,24},{26,28},{4,2},{8,6},{1... | collective-permute-start | bytes 73736 | tf_op jit(solution)/shard_map/ppermute | solution.py:424
  25.4 4.5 %collective-permute-start.3 = (bf16[48,256]{1,0:T(8,128)(2,1)S(1)}, bf16[48,256]{1,0:T(8,128)(2,1)S(1)}, u32[]{:S(2)}, u32[]{:S(2)}) collective-permute-start(bf16[48,256]{1,0:T(8,128)(2,1)S(1)} %get-tuple-element.35), channel_id=1, source_target_pairs={{0,2},{4,6},{8,10},{12,14},{16,18},{20,22},{24,26},{28,30},{2,0},{... | collective-permute-start | bytes 73736 | tf_op jit(solution)/shard_map/ppermute | solution.py:424
  29.9 2.1 %collective-permute-done.3.near._near = bf16[48,256]{1,0:T(8,128)(2,1)S(1)} collective-permute-done((bf16[48,256]{1,0:T(8,128)(2,1)S(1)}, bf16[48,256]{1,0:T(8,128)(2,1)S(1)}, u32[]{:S(2)}, u32[]{:S(2)}) %collective-permute-start.3) | collective-permute-done | bytes 24608 | tf_op jit(solution)/shard_map/ppermute | solution.py:424
  32.0 1.0 %all-to-all-done.1.parts_ref = bf16[32,16,128]{2,1,0:T(8,128)(2,1)S(1)} async-done(((bf16[32,16,128]{2,1,0:T(8,128)(2,1)}), bf16[32,16,128]{2,1,0:T(8,128)(2,1)S(1)}, u32[]{:S(2)}, u32[]{:S(2)}) %all-to-all-start.1) | async-done | bytes 131104 | tf_op jit(solution)/shard_map/all_to_all | solution.py:488
  33.0 0.9 %shard_map.100 = bf16[32,16,128]{2,1,0:T(8,128)(2,1)} custom-call(bf16[32,16,128]{2,1,0:T(8,128)(2,1)S(1)} %all-to-all-done.1.parts_ref, bf16[48,256]{1,0:T(8,128)(2,1)S(1)} %collective-permute-done.2.far._far, bf16[48,256]{1,0:T(8,128)(2,1)S(1)} %collective-permute-done.3.near._near), custom_call_target="tpu_custom_call" | custom-call | tf_op jit(solution)/shard_map/pallas_call | solution.py:490
  33.9 4.2 %all-to-all-start.2 = ((bf16[32,16,128]{2,1,0:T(8,128)(2,1)}), bf16[32,16,128]{2,1,0:T(8,128)(2,1)S(1)}, u32[]{:S(2)}, u32[]{:S(2)}) async-start(bf16[32,16,128]{2,1,0:T(8,128)(2,1)} %shard_map.100), calls=%async_computation.2 | async-start | bytes 262144 | tf_op jit(solution)/shard_map/all_to_all | solution.py:493
  38.0 1.4 %shard_map.99 = bf16[1,2,8,8,256]{4,3,2,1,0:T(8,128)(2,1)} custom-call(f32[48,128]{1,0:T(8,128)S(1)} %get-tuple-element.21.masks_ref, bf16[27,32,32]{2,1,0:T(8,128)(2,1)S(1)} %copy-done.2, bf16[256,128]{1,0:T(8,128)(2,1)S(1)} %get-tuple-element.32.lifted_ref, bf16[256,128]{1,0:T(8,128)(2,1)S(1)} %get-tuple-element.33.hidden_ref, ...), custom_call_target="tpu_custom_call" | custom-call | flops 1000000000 | bytes 2000000 | tf_op jit(solution)/shard_map/pallas_call | solution.py:485
  39.5 6.8 %all-to-all-done.2.sums_ref = bf16[32,16,128]{2,1,0:T(8,128)(2,1)S(1)} async-done(((bf16[32,16,128]{2,1,0:T(8,128)(2,1)}), bf16[32,16,128]{2,1,0:T(8,128)(2,1)S(1)}, u32[]{:S(2)}, u32[]{:S(2)}) %all-to-all-start.2) | async-done | bytes 131104 | tf_op jit(solution)/shard_map/all_to_all | solution.py:493
  46.3 1.0 %shard_map.101 = (f32[27,32,32]{2,1,0:T(8,128)}, f32[27,32,32]{2,1,0:T(8,128)}) custom-call(bf16[32,16,128]{2,1,0:T(8,128)(2,1)S(1)} %all-to-all-done.2.sums_ref), custom_call_target="tpu_custom_call" | custom-call | tf_op jit(solution)/shard_map/pallas_call | solution.py:497
  (8 shorter events, 0.0 us)
Async XLA Ops:
  2.4 7.3 %copy-start = (bf16[1,2,8,8,256]{4,3,2,1,0:T(8,128)(2,1)S(1)}, bf16[1,2,8,8,256]{4,3,2,1,0:T(8,128)(2,1)}, u32[]{:S(2)}) copy-start(bf16[1,2,8,8,256]{4,3,2,1,0:T(8,128)(2,1)} %cotangent_ref.3) | copy-start | bytes 196612
  2.4 12.7 %copy-start.4 = (bf16[27,32,32]{2,1,0:T(8,128)(2,1)S(1)}, bf16[27,32,32]{2,1,0:T(8,128)(2,1)}, u32[]{:S(2)}) copy-start(bf16[27,32,32]{2,1,0:T(8,128)(2,1)} %weights_ref.3) | copy-start | bytes 165892
  2.4 16.2 %all-to-all-start = ((bf16[32,24,128]{2,1,0:T(8,128)(2,1)}), bf16[32,24,128]{2,1,0:T(8,128)(2,1)S(1)}, u32[]{:S(2)}, u32[]{:S(2)}) async-start(bf16[32,24,128]{2,1,0:T(8,128)(2,1)} %shard_map.94), calls=%async_computation | async-start | bytes 393216 | tf_op jit(solution)/shard_map/all_to_all | solution.py:447
  9.8 10.2 %collective-permute-start = (bf16[48,256]{1,0:T(8,128)(2,1)S(1)}, bf16[48,256]{1,0:T(8,128)(2,1)S(1)}, u32[]{:S(2)}, u32[]{:S(2)}) collective-permute-start(bf16[48,256]{1,0:T(8,128)(2,1)S(1)} %get-tuple-element.28), channel_id=1, source_target_pairs={{2,4},{6,8},{10,12},{14,16},{18,20},{22,24},{26,28},{4,2},{8,6},{1... | collective-permute-start | bytes 73736 | tf_op jit(solution)/shard_map/ppermute | solution.py:424
  10.5 8.1 %copy-start.1 = (bf16[64,2048]{1,0:T(8,128)(2,1)S(1)}, bf16[64,2048]{1,0:T(8,128)(2,1)}, u32[]{:S(2)}) copy-start(bf16[64,2048]{1,0:T(8,128)(2,1)} %up_ref.1) | copy-start | bytes 786436
  10.5 8.1 %copy-start.2 = (bf16[27,32,32]{2,1,0:T(8,128)(2,1)S(1)}, bf16[27,32,32]{2,1,0:T(8,128)(2,1)}, u32[]{:S(2)}) copy-start(bf16[27,32,32]{2,1,0:T(8,128)(2,1)} %weights_ref.5) | copy-start | bytes 165892
  10.5 8.1 %copy-start.3 = (s32[1,2,6]{2,1,0:T(2,128)S(1)}, s32[1,2,6]{2,1,0:T(2,128)}, u32[]{:S(2)}) copy-start(s32[1,2,6]{2,1,0:T(2,128)} %links_in.1) | copy-start | bytes 148
  10.5 9.5 %collective-permute-start.1 = (bf16[48,256]{1,0:T(8,128)(2,1)S(1)}, bf16[48,256]{1,0:T(8,128)(2,1)S(1)}, u32[]{:S(2)}, u32[]{:S(2)}) collective-permute-start(bf16[48,256]{1,0:T(8,128)(2,1)S(1)} %get-tuple-element.29), channel_id=1, source_target_pairs={{0,2},{4,6},{8,10},{12,14},{16,18},{20,22},{24,26},{28,30},{2,0},{... | collective-permute-start | bytes 73736 | tf_op jit(solution)/shard_map/ppermute | solution.py:424
  21.9 11.1 %all-to-all-start.1 = ((bf16[32,16,128]{2,1,0:T(8,128)(2,1)}), bf16[32,16,128]{2,1,0:T(8,128)(2,1)S(1)}, u32[]{:S(2)}, u32[]{:S(2)}) async-start(bf16[32,16,128]{2,1,0:T(8,128)(2,1)} %get-tuple-element.36), calls=%async_computation.1 | async-start | bytes 262144 | tf_op jit(solution)/shard_map/all_to_all | solution.py:488
  24.7 5.2 %collective-permute-start.2 = (bf16[48,256]{1,0:T(8,128)(2,1)S(1)}, bf16[48,256]{1,0:T(8,128)(2,1)S(1)}, u32[]{:S(2)}, u32[]{:S(2)}) collective-permute-start(bf16[48,256]{1,0:T(8,128)(2,1)S(1)} %get-tuple-element.34), channel_id=1, source_target_pairs={{2,4},{6,8},{10,12},{14,16},{18,20},{22,24},{26,28},{4,2},{8,6},{1... | collective-permute-start | bytes 73736 | tf_op jit(solution)/shard_map/ppermute | solution.py:424
  25.4 6.6 %collective-permute-start.3 = (bf16[48,256]{1,0:T(8,128)(2,1)S(1)}, bf16[48,256]{1,0:T(8,128)(2,1)S(1)}, u32[]{:S(2)}, u32[]{:S(2)}) collective-permute-start(bf16[48,256]{1,0:T(8,128)(2,1)S(1)} %get-tuple-element.35), channel_id=1, source_target_pairs={{0,2},{4,6},{8,10},{12,14},{16,18},{20,22},{24,26},{28,30},{2,0},{... | collective-permute-start | bytes 73736 | tf_op jit(solution)/shard_map/ppermute | solution.py:424
  33.9 12.4 %all-to-all-start.2 = ((bf16[32,16,128]{2,1,0:T(8,128)(2,1)}), bf16[32,16,128]{2,1,0:T(8,128)(2,1)S(1)}, u32[]{:S(2)}, u32[]{:S(2)}) async-start(bf16[32,16,128]{2,1,0:T(8,128)(2,1)} %shard_map.100), calls=%async_computation.2 | async-start | bytes 262144 | tf_op jit(solution)/shard_map/all_to_all | solution.py:493

commit v13 on v11

--- a/solution.py
+++ b/solution.py
@@ -350,25 +350,24 @@
     sums_out[...] = sums_ref[...].astype(BF16).reshape(sums_out.shape)
 
 
-def fine_kernel(
-    masks_ref, weights_ref, lifted_ref, hidden_ref, high_own, low_own, far, near,
-    fine_out, high_pool, low_pool, hidden_pad, band_ref,
+def unpacked(tile):
+    pieces = [tile] + [pltpu.roll(tile, 128 - q * CHANNELS, 1) for q in range(1, 4)]
+    return jnp.concatenate(pieces, axis=0)[:, :CHANNELS]
+
+
+def third_kernel(
+    scale, masks_ref, band_ref, lifted_ref, hidden_ref, high_own, low_own, far, near, parts_ref,
+    fine_out, sums_out,
+    high_pool, low_pool, hidden_pad, fine_ref, fine_sem,
 ):
-    build_band(band_ref, weight_rows(weights_ref[...].astype(F32)))
     bricks = half_lines(hidden_ref[...].astype(F32))
     pad_all(hidden_pad, bricks, masks_ref, high_pool, low_pool, high_own, low_own, far, near)
     fine = lifted_ref[...].astype(F32) + convolve(hidden_pad, band_ref)
     fine = fine.reshape(LINES // EDGE, 2, EDGE, HALF)
     fine = jnp.concatenate([fine[:, 0], fine[:, 1]], axis=-1)
-    fine_out[...] = fine.astype(BF16).reshape(fine_out.shape)
-
-
-def unpacked(tile):
-    pieces = [tile] + [pltpu.roll(tile, 128 - q * CHANNELS, 1) for q in range(1, 4)]
-    return jnp.concatenate(pieces, axis=0)[:, :CHANNELS]
-
-
-def sum_kernel(scale, parts_ref, _far, _near, out_ref):
+    fine_ref[...] = fine.astype(BF16).reshape(fine_ref.shape)
+    fine_copy = pltpu.make_async_copy(fine_ref, fine_out, fine_sem)
+    fine_copy.start()
     total = jnp.sum(parts_ref[...].astype(F32), axis=0) * scale
     per = parts_ref.shape[1] // 8
     device = lax.axis_index("space") * lax.axis_size("dp") + lax.axis_index("dp")
@@ -379,7 +378,8 @@
         turned = jnp.concatenate([block[8 * q : 8 * q + 8] for q in range(4)], axis=1)
         tiles.append(jnp.where(device * per + j < 27, turned, tile))
     total = jnp.concatenate(tiles, axis=0)
-    out_ref[...] = jnp.broadcast_to(total.astype(BF16)[None], out_ref.shape)
+    sums_out[...] = jnp.broadcast_to(total.astype(BF16)[None], sums_out.shape)
+    fine_copy.wait()
 
 
 def unpack_kernel(sums_ref, one_out, two_out, rows_ref, one_ref, two_ref, sems):
@@ -398,13 +398,14 @@
         copy.wait()
 
 
-def call(kernel, out_shape, scratch=(), hbm=(), inputs=1, limit=24, cost=None, out=pltpu.VMEM):
+def call(kernel, out_shape, scratch=(), hbm=(), inputs=1, limit=24, cost=None, out=None):
     spaces = [pl.ANY if i in hbm else pltpu.VMEM for i in range(inputs)]
+    out = out or jax.tree.map(lambda _: pltpu.VMEM, out_shape)
     return pl.pallas_call(
         kernel,
         out_shape=out_shape,
         in_specs=[pl.BlockSpec(memory_space=space) for space in spaces],
-        out_specs=jax.tree.map(lambda _: pl.BlockSpec(memory_space=out), out_shape),
+        out_specs=jax.tree.map(lambda space: pl.BlockSpec(memory_space=space), out),
         scratch_shapes=list(scratch),
         compiler_params=pltpu.CompilerParams(vmem_limit_bytes=limit * 2**20),
         cost_estimate=cost,
@@ -479,19 +480,21 @@
     )
     hidden_far = swapped(hidden_far, 1)
     hidden_near = swapped(hidden_near, 0)
-    fine = call(fine_kernel, shape(*cotangent.shape), [pool, pool, pad, band], inputs=8, cost=cost)(
-        masks, conv_two, lifted, hidden, hidden_high, hidden_low, hidden_far, hidden_near
-    )
+    band_two = call(band_kernel, shape(*BAND), cost=cost)(conv_two)
     parts = lax.all_to_all(sums, axes, split_axis=0, concat_axis=0, tiled=True)
     scale = 1.0 / math.sqrt(lax.axis_size("dp") * devices * BRICKS * EDGE**3)
-    total = call(functools.partial(sum_kernel, scale), shape(*sums.shape), hbm=(1, 2), inputs=3)(
-        parts, hidden_far, hidden_near
-    )
+    fine, total = call(
+        functools.partial(third_kernel, scale),
+        (shape(*cotangent.shape), shape(*sums.shape)),
+        [pool, pool, pad, pltpu.VMEM(cotangent.shape, BF16), pltpu.SemaphoreType.DMA],
+        inputs=9,
+        out=(pl.ANY, pltpu.VMEM),
+    )(masks, band_two, lifted, hidden, hidden_high, hidden_low, hidden_far, hidden_near, parts)
     gathered = lax.all_to_all(total, axes, split_axis=0, concat_axis=0, tiled=True)
     grads = shape(27, CHANNELS, CHANNELS, dtype=F32)
     block = pltpu.VMEM(grads.shape, F32)
     scratch = [pltpu.VMEM((everyone * per * 8, 128), F32), block, block, pltpu.SemaphoreType.DMA((2, 3))]
-    grad_one, grad_two = call(unpack_kernel, (grads, grads), scratch, out=pl.ANY)(gathered)
+    grad_one, grad_two = call(unpack_kernel, (grads, grads), scratch, out=(pl.ANY, pl.ANY))(gathered)
     return (fine, grad_one, grad_two)
 
 

time: 47.6 us -> 47.7 us (level)
  blocking collectives: 0 us -> 12.2 us
  waiting for transfers between devices: 13 us -> 5.87 us
  starting transfers between devices: 24.7 us -> 20.6 us
  Pallas kernels: 8.76 us -> 7.93 us
    all_to_all x0 -> x1, blocking collectives: none -> 12.2 us  [body(): lax.all_to_all(total, axes, split_axis=0, concat_axis=0, tiled=True)]
    all_to_all x1 -> x0, waiting for transfers between devices: 6.8 us -> none  [body(): lax.all_to_all(total, axes, split_axis=0, concat_axis=0, tiled=True)]
    all_to_all x1 -> x0, starting transfers between devices: 4.16 us -> none  [body(): lax.all_to_all(total, axes, split_axis=0, concat_axis=0, tiled=True)]
    pallas_call x3, Pallas kernels: 3.39 us -> 2.56 us  [the longest x1 1.19 us: body(): call(functools.partial(third_kernel, scale), (shape(*cotangent.shape), sh...]
  transfers between devices with their start and end apart: 7 -> 6, of which waited for: 4 -> 3; matrix products, arithmetic and copies ran while one was open for 0% -> 0% of each run, Pallas kernels for 7% -> 4%
where the time goes in v13:
time: 47.7 us; the launch traced here: 47.4 us
  starting transfers between devices  20.6 us (43%)
  blocking collectives  12.2 us (26%)
  Pallas kernels  7.93 us (17%)
  waiting for transfers between devices  5.87 us (12%)
  between operations  0.78 us (2%)
    all_to_all x1, blocking collectives, body(): lax.all_to_all(total, axes, split_axis=0, concat_axis=0, tiled=True)  12.2 us
    ppermute x4, starting transfers between devices, swapped(): lax.ppermute(value, 'space', pairs + [(target, source) for source, target...  10.4 us
    all_to_all x1, starting transfers between devices, body(): lax.all_to_all(packed, axes if scenes == 2 else 'space', split_axis=0, co...  7.3 us
    all_to_all x1, waiting for transfers between devices, body(): lax.all_to_all(packed, axes if scenes == 2 else 'space', split_axis=0, co...  3.2 us
    all_to_all x1, starting transfers between devices, body(): parts = lax.all_to_all(sums, axes, split_axis=0, concat_axis=0, tiled=True)  2.85 us
    pallas_call x1, Pallas kernels, body(): call(second_kernel, (shape(everyone, per * 8, 128), volume, face, face),...  1.85 us
    pallas_call x1, Pallas kernels, body(): call(functools.partial(pick_kernel, scenes), shape(devices * scenes, 3 *...  1.74 us
    ppermute x4, waiting for transfers between devices, swapped(): lax.ppermute(value, 'space', pairs + [(target, source) for source, target...  1.72 us
  transfers between devices with their start and end apart: 6, of which 3 were waited for; matrix products, arithmetic and copies ran while one was open for 0% of the time, Pallas kernels for 4%

profile of v13, /device:TPU:0, one launch (start us, length us, event | category | flops | bytes accessed | tf_op | source)
XLA Modules:
  0.0 47.4 jit_solution(17580328671915165965)
XLA Ops:
  0.6 1.7 %shard_map.94 = bf16[32,24,128]{2,1,0:T(8,128)(2,1)} custom-call(s32[1,32]{1,0:T(1,128)} %ids_hbm.1, bf16[1,64,512]{2,1,0:T(8,128)(2,1)} %latents_hbm.1), custom_call_target="tpu_custom_call" | custom-call | tf_op jit(solution)/shard_map/pallas_call | solution.py:431
  2.4 0.0 copy-start
  2.4 0.0 copy-start.4
  2.4 7.3 %all-to-all-start = ((bf16[32,24,128]{2,1,0:T(8,128)(2,1)}), bf16[32,24,128]{2,1,0:T(8,128)(2,1)S(1)}, u32[]{:S(2)}, u32[]{:S(2)}) async-start(bf16[32,24,128]{2,1,0:T(8,128)(2,1)} %shard_map.94), calls=%async_computation | async-start | bytes 393216 | tf_op jit(solution)/shard_map/all_to_all | solution.py:445
  9.7 0.1 shard_map.98
  9.8 0.7 %collective-permute-start = (bf16[48,256]{1,0:T(8,128)(2,1)S(1)}, bf16[48,256]{1,0:T(8,128)(2,1)S(1)}, u32[]{:S(2)}, u32[]{:S(2)}) collective-permute-start(bf16[48,256]{1,0:T(8,128)(2,1)S(1)} %get-tuple-element.30), channel_id=1, source_target_pairs={{2,4},{6,8},{10,12},{14,16},{18,20},{22,24},{26,28},{4,2},{8,6},{1... | collective-permute-start | bytes 73736 | tf_op jit(solution)/shard_map/ppermute | solution.py:421
  10.5 0.0 copy-start.1
  10.5 0.0 copy-start.2
  10.5 0.0 copy-start.3
  10.5 4.5 %collective-permute-start.1 = (bf16[48,256]{1,0:T(8,128)(2,1)S(1)}, bf16[48,256]{1,0:T(8,128)(2,1)S(1)}, u32[]{:S(2)}, u32[]{:S(2)}) collective-permute-start(bf16[48,256]{1,0:T(8,128)(2,1)S(1)} %get-tuple-element.31), channel_id=1, source_target_pairs={{0,2},{4,6},{8,10},{12,14},{16,18},{20,22},{24,26},{28,30},{2,0},{... | collective-permute-start | bytes 73736 | tf_op jit(solution)/shard_map/ppermute | solution.py:421
  15.1 0.3 shard_map.95.band_ref
  15.4 3.2 %all-to-all-done.received_ref = bf16[32,24,128]{2,1,0:T(8,128)(2,1)S(1)} async-done(((bf16[32,24,128]{2,1,0:T(8,128)(2,1)}), bf16[32,24,128]{2,1,0:T(8,128)(2,1)S(1)}, u32[]{:S(2)}, u32[]{:S(2)}) %all-to-all-start) | async-done | bytes 196640 | tf_op jit(solution)/shard_map/all_to_all | solution.py:445
  18.6 1.4 %shard_map.96 = (f32[256,128]{1,0:T(8,128)S(1)}, bf16[256,128]{1,0:T(8,128)(2,1)S(1)}, bf16[128,256]{1,0:T(8,128)(2,1)S(1)}, bf16[3,2,10,16,256]{4,3,2,1,0:T(8,1...) custom-call(s32[1,2,6]{2,1,0:T(2,128)S(1)} %copy-done.3, ...), custom_call_target="tpu_custom_call" | custom-call | tf_op jit(solution)/shard_map/pallas_call | solution.py:460
  20.0 0.0 collective-permute-done.far
  20.0 1.9 %shard_map.99 = (bf16[32,16,128]{2,1,0:T(8,128)(2,1)}, bf16[256,128]{1,0:T(8,128)(2,1)S(1)}, bf16[48,256]{1,0:T(8,128)(2,1)S(1)}, bf16[48,256]{1,0:T(8,128)(2,1)S(1)}) custom-call(f32[48,128]{1,0:T(8,128)S(1)} %get-tuple-element.23.masks_ref, bf16[1,2,8,8,256]{4,3,2,1,0:T(8,128)(2,1)S(1)} %copy-done, bf16[9,256,128]{2,1,0:T(8,128)(2,1)S(1)} %get-tuple-element.24.band_ref, ...), custom_call_target="tpu_custom_call" | custom-call | tf_op jit(solution)/shard_map/pallas_call | solution.py:472
  21.9 2.9 %all-to-all-start.1 = ((bf16[32,16,128]{2,1,0:T(8,128)(2,1)}), bf16[32,16,128]{2,1,0:T(8,128)(2,1)S(1)}, u32[]{:S(2)}, u32[]{:S(2)}) async-start(bf16[32,16,128]{2,1,0:T(8,128)(2,1)} %get-tuple-element.38), calls=%async_computation.1 | async-start | bytes 262144 | tf_op jit(solution)/shard_map/all_to_all | solution.py:484
  24.7 0.7 %collective-permute-start.2 = (bf16[48,256]{1,0:T(8,128)(2,1)S(1)}, bf16[48,256]{1,0:T(8,128)(2,1)S(1)}, u32[]{:S(2)}, u32[]{:S(2)}) collective-permute-start(bf16[48,256]{1,0:T(8,128)(2,1)S(1)} %get-tuple-element.36), channel_id=1, source_target_pairs={{2,4},{6,8},{10,12},{14,16},{18,20},{22,24},{26,28},{4,2},{8,6},{1... | collective-permute-start | bytes 73736 | tf_op jit(solution)/shard_map/ppermute | solution.py:421
  25.4 4.5 %collective-permute-start.3 = (bf16[48,256]{1,0:T(8,128)(2,1)S(1)}, bf16[48,256]{1,0:T(8,128)(2,1)S(1)}, u32[]{:S(2)}, u32[]{:S(2)}) collective-permute-start(bf16[48,256]{1,0:T(8,128)(2,1)S(1)} %get-tuple-element.37), channel_id=1, source_target_pairs={{0,2},{4,6},{8,10},{12,14},{16,18},{20,22},{24,26},{28,30},{2,0},{... | collective-permute-start | bytes 73736 | tf_op jit(solution)/shard_map/ppermute | solution.py:421
  29.9 0.3 shard_map.97.band_ref
  30.3 1.7 %collective-permute-done.3.near = bf16[48,256]{1,0:T(8,128)(2,1)S(1)} collective-permute-done((bf16[48,256]{1,0:T(8,128)(2,1)S(1)}, bf16[48,256]{1,0:T(8,128)(2,1)S(1)}, u32[]{:S(2)}, u32[]{:S(2)}) %collective-permute-start.3) | collective-permute-done | bytes 24608 | tf_op jit(solution)/shard_map/ppermute | solution.py:421
  32.0 1.0 %all-to-all-done.1.parts_ref = bf16[32,16,128]{2,1,0:T(8,128)(2,1)S(1)} async-done(((bf16[32,16,128]{2,1,0:T(8,128)(2,1)}), bf16[32,16,128]{2,1,0:T(8,128)(2,1)S(1)}, u32[]{:S(2)}, u32[]{:S(2)}) %all-to-all-start.1) | async-done | bytes 131104 | tf_op jit(solution)/shard_map/all_to_all | solution.py:484
  32.9 1.2 %shard_map.100 = (bf16[1,2,8,8,256]{4,3,2,1,0:T(8,128)(2,1)}, bf16[32,16,128]{2,1,0:T(8,128)(2,1)S(1)}) custom-call(f32[48,128]{1,0:T(8,128)S(1)} %get-tuple-element.23.masks_ref, bf16[9,256,128]{2,1,0:T(8,128)(2,1)S(1)} %shard_map.97.band_ref, bf16[256,128]{1,0:T(8,128)(2,1)S(1)} %get-tuple-element.34.lifted_ref, ...), custom_call_target="tpu_custom_call" | custom-call | tf_op jit(solution)/shard_map/pallas_call | solution.py:486
  34.1 12.2 %all_to_all.15.sums_ref = bf16[32,16,128]{2,1,0:T(8,128)(2,1)S(1)} all-to-all(bf16[32,16,128]{2,1,0:T(8,128)(2,1)S(1)} %get-tuple-element.40), channel_id=1, replica_groups=mesh['space'=16,'dp'=2] {'space','dp'}, dimensions={0} | all-to-all | bytes 262144 | tf_op jit(solution)/shard_map/all_to_all | solution.py:493
  46.3 1.0 %shard_map.101 = (f32[27,32,32]{2,1,0:T(8,128)}, f32[27,32,32]{2,1,0:T(8,128)}) custom-call(bf16[32,16,128]{2,1,0:T(8,128)(2,1)S(1)} %all_to_all.15.sums_ref), custom_call_target="tpu_custom_call" | custom-call | tf_op jit(solution)/shard_map/pallas_call | solution.py:497
  (7 shorter events, 0.0 us)
Async XLA Ops:
  2.4 7.3 %copy-start = (bf16[1,2,8,8,256]{4,3,2,1,0:T(8,128)(2,1)S(1)}, bf16[1,2,8,8,256]{4,3,2,1,0:T(8,128)(2,1)}, u32[]{:S(2)}) copy-start(bf16[1,2,8,8,256]{4,3,2,1,0:T(8,128)(2,1)} %cotangent_ref.3) | copy-start | bytes 196612
  2.4 12.7 %copy-start.4 = (bf16[27,32,32]{2,1,0:T(8,128)(2,1)S(1)}, bf16[27,32,32]{2,1,0:T(8,128)(2,1)}, u32[]{:S(2)}) copy-start(bf16[27,32,32]{2,1,0:T(8,128)(2,1)} %weights_ref.3) | copy-start | bytes 165892
  2.4 16.2 %all-to-all-start = ((bf16[32,24,128]{2,1,0:T(8,128)(2,1)}), bf16[32,24,128]{2,1,0:T(8,128)(2,1)S(1)}, u32[]{:S(2)}, u32[]{:S(2)}) async-start(bf16[32,24,128]{2,1,0:T(8,128)(2,1)} %shard_map.94), calls=%async_computation | async-start | bytes 393216 | tf_op jit(solution)/shard_map/all_to_all | solution.py:445
  9.8 10.2 %collective-permute-start = (bf16[48,256]{1,0:T(8,128)(2,1)S(1)}, bf16[48,256]{1,0:T(8,128)(2,1)S(1)}, u32[]{:S(2)}, u32[]{:S(2)}) collective-permute-start(bf16[48,256]{1,0:T(8,128)(2,1)S(1)} %get-tuple-element.30), channel_id=1, source_target_pairs={{2,4},{6,8},{10,12},{14,16},{18,20},{22,24},{26,28},{4,2},{8,6},{1... | collective-permute-start | bytes 73736 | tf_op jit(solution)/shard_map/ppermute | solution.py:421
  10.5 8.1 %copy-start.1 = (bf16[64,2048]{1,0:T(8,128)(2,1)S(1)}, bf16[64,2048]{1,0:T(8,128)(2,1)}, u32[]{:S(2)}) copy-start(bf16[64,2048]{1,0:T(8,128)(2,1)} %up_ref.1) | copy-start | bytes 786436
  10.5 8.1 %copy-start.2 = (bf16[27,32,32]{2,1,0:T(8,128)(2,1)S(1)}, bf16[27,32,32]{2,1,0:T(8,128)(2,1)}, u32[]{:S(2)}) copy-start(bf16[27,32,32]{2,1,0:T(8,128)(2,1)} %weights_ref.5) | copy-start | bytes 165892
  10.5 8.1 %copy-start.3 = (s32[1,2,6]{2,1,0:T(2,128)S(1)}, s32[1,2,6]{2,1,0:T(2,128)}, u32[]{:S(2)}) copy-start(s32[1,2,6]{2,1,0:T(2,128)} %links_in.1) | copy-start | bytes 148
  10.5 9.5 %collective-permute-start.1 = (bf16[48,256]{1,0:T(8,128)(2,1)S(1)}, bf16[48,256]{1,0:T(8,128)(2,1)S(1)}, u32[]{:S(2)}, u32[]{:S(2)}) collective-permute-start(bf16[48,256]{1,0:T(8,128)(2,1)S(1)} %get-tuple-element.31), channel_id=1, source_target_pairs={{0,2},{4,6},{8,10},{12,14},{16,18},{20,22},{24,26},{28,30},{2,0},{... | collective-permute-start | bytes 73736 | tf_op jit(solution)/shard_map/ppermute | solution.py:421
  21.9 11.1 %all-to-all-start.1 = ((bf16[32,16,128]{2,1,0:T(8,128)(2,1)}), bf16[32,16,128]{2,1,0:T(8,128)(2,1)S(1)}, u32[]{:S(2)}, u32[]{:S(2)}) async-start(bf16[32,16,128]{2,1,0:T(8,128)(2,1)} %get-tuple-element.38), calls=%async_computation.1 | async-start | bytes 262144 | tf_op jit(solution)/shard_map/all_to_all | solution.py:484
  24.7 5.6 %collective-permute-start.2 = (bf16[48,256]{1,0:T(8,128)(2,1)S(1)}, bf16[48,256]{1,0:T(8,128)(2,1)S(1)}, u32[]{:S(2)}, u32[]{:S(2)}) collective-permute-start(bf16[48,256]{1,0:T(8,128)(2,1)S(1)} %get-tuple-element.36), channel_id=1, source_target_pairs={{2,4},{6,8},{10,12},{14,16},{18,20},{22,24},{26,28},{4,2},{8,6},{1... | collective-permute-start | bytes 73736 | tf_op jit(solution)/shard_map/ppermute | solution.py:421
  25.4 6.6 %collective-permute-start.3 = (bf16[48,256]{1,0:T(8,128)(2,1)S(1)}, bf16[48,256]{1,0:T(8,128)(2,1)S(1)}, u32[]{:S(2)}, u32[]{:S(2)}) collective-permute-start(bf16[48,256]{1,0:T(8,128)(2,1)S(1)} %get-tuple-element.37), channel_id=1, source_target_pairs={{0,2},{4,6},{8,10},{12,14},{16,18},{20,22},{24,26},{28,30},{2,0},{... | collective-permute-start | bytes 73736 | tf_op jit(solution)/shard_map/ppermute | solution.py:421

commit v14 on v11

--- a/solution.py
+++ b/solution.py
@@ -351,10 +351,9 @@
 
 
 def fine_kernel(
-    masks_ref, weights_ref, lifted_ref, hidden_ref, high_own, low_own, far, near,
-    fine_out, high_pool, low_pool, hidden_pad, band_ref,
+    masks_ref, band_ref, lifted_ref, hidden_ref, high_own, low_own, far, near,
+    fine_out, high_pool, low_pool, hidden_pad,
 ):
-    build_band(band_ref, weight_rows(weights_ref[...].astype(F32)))
     bricks = half_lines(hidden_ref[...].astype(F32))
     pad_all(hidden_pad, bricks, masks_ref, high_pool, low_pool, high_own, low_own, far, near)
     fine = lifted_ref[...].astype(F32) + convolve(hidden_pad, band_ref)
@@ -368,7 +367,7 @@
     return jnp.concatenate(pieces, axis=0)[:, :CHANNELS]
 
 
-def sum_kernel(scale, parts_ref, _far, _near, out_ref):
+def sum_kernel(scale, parts_ref, out_ref):
     total = jnp.sum(parts_ref[...].astype(F32), axis=0) * scale
     per = parts_ref.shape[1] // 8
     device = lax.axis_index("space") * lax.axis_size("dp") + lax.axis_index("dp")
@@ -442,7 +441,6 @@
     )(active_blocks, coarse_latents)
     axes = ("space", "dp")
     received = lax.all_to_all(packed, axes if scenes == 2 else "space", split_axis=0, concat_axis=0, tiled=True)
-    band = pltpu.VMEM(BAND, BF16)
     cost = pl.CostEstimate(flops=10**9, bytes_accessed=2 * 10**6, transcendentals=0)
     face = shape(BRICKS * FACE, LINE)
     halves = pltpu.VMEM((2, LINES, HALF), F32)
@@ -479,14 +477,13 @@
     )
     hidden_far = swapped(hidden_far, 1)
     hidden_near = swapped(hidden_near, 0)
-    fine = call(fine_kernel, shape(*cotangent.shape), [pool, pool, pad, band], inputs=8, cost=cost)(
-        masks, conv_two, lifted, hidden, hidden_high, hidden_low, hidden_far, hidden_near
+    band_two = call(band_kernel, shape(*BAND), cost=cost)(conv_two)
+    fine = call(fine_kernel, shape(*cotangent.shape), [pool, pool, pad], inputs=8, cost=cost)(
+        masks, band_two, lifted, hidden, hidden_high, hidden_low, hidden_far, hidden_near
     )
     parts = lax.all_to_all(sums, axes, split_axis=0, concat_axis=0, tiled=True)
     scale = 1.0 / math.sqrt(lax.axis_size("dp") * devices * BRICKS * EDGE**3)
-    total = call(functools.partial(sum_kernel, scale), shape(*sums.shape), hbm=(1, 2), inputs=3)(
-        parts, hidden_far, hidden_near
-    )
+    total = call(functools.partial(sum_kernel, scale), shape(*sums.shape))(parts)
     gathered = lax.all_to_all(total, axes, split_axis=0, concat_axis=0, tiled=True)
     grads = shape(27, CHANNELS, CHANNELS, dtype=F32)
     block = pltpu.VMEM(grads.shape, F32)

time: 47.6 us -> 45.2 us (0.950)
  blocking collectives: 0 us -> 10.9 us
  waiting for transfers between devices: 13 us -> 4.89 us
  starting transfers between devices: 24.7 us -> 20.2 us
  Pallas kernels: 8.76 us -> 8.17 us
    all_to_all x0 -> x1, blocking collectives: none -> 10.9 us  [body(): parts = lax.all_to_all(sums, axes, split_axis=0, concat_axis=0, tiled=True)]
    all_to_all x1, waiting for transfers between devices: 6.8 us -> 0.01 us  [body(): lax.all_to_all(total, axes, split_axis=0, concat_axis=0, tiled=True)]
    all_to_all x1 -> x0, starting transfers between devices: 2.86 us -> none  [body(): parts = lax.all_to_all(sums, axes, split_axis=0, concat_axis=0, tiled=True)]
    all_to_all x1, starting transfers between devices: 4.16 us -> 2.58 us  [body(): lax.all_to_all(total, axes, split_axis=0, concat_axis=0, tiled=True)]
    all_to_all x1 -> x0, waiting for transfers between devices: 0.96 us -> none  [body(): parts = lax.all_to_all(sums, axes, split_axis=0, concat_axis=0, tiled=True)]
    pallas_call x1, Pallas kernels: 1.85 us -> 1.2 us  [body(): call(second_kernel, (shape(everyone, per * 8, 128), volume, face, face),...]
    pallas_call x2 -> x3, Pallas kernels: 2.34 us -> 2.41 us  [the longest x1 1.17 us: body(): call(fine_kernel, shape(*cotangent.shape), [pool, pool, pad], inputs=8, c...]
  transfers between devices with their start and end apart: 7 -> 6, of which waited for: 4 -> 2; matrix products, arithmetic and copies ran while one was open for 0% -> 0% of each run, Pallas kernels for 7% -> 7%
where the time goes in v14:
time: 45.2 us; the launch traced here: 44.9 us
  starting transfers between devices  20.2 us (45%)
  blocking collectives  10.9 us (24%)
  Pallas kernels  8.17 us (18%)
  waiting for transfers between devices  4.89 us (11%)
  between operations  0.78 us (2%)
    all_to_all x1, blocking collectives, body(): parts = lax.all_to_all(sums, axes, split_axis=0, concat_axis=0, tiled=True)  10.9 us
    ppermute x4, starting transfers between devices, swapped(): lax.ppermute(value, 'space', pairs + [(target, source) for source, target...  10.3 us
    all_to_all x1, starting transfers between devices, body(): lax.all_to_all(packed, axes if scenes == 2 else 'space', split_axis=0, co...  7.3 us
    all_to_all x1, waiting for transfers between devices, body(): lax.all_to_all(packed, axes if scenes == 2 else 'space', split_axis=0, co...  3.2 us
    all_to_all x1, starting transfers between devices, body(): lax.all_to_all(total, axes, split_axis=0, concat_axis=0, tiled=True)  2.58 us
    pallas_call x1, Pallas kernels, body(): call(functools.partial(pick_kernel, scenes), shape(devices * scenes, 3 *...  1.74 us
    ppermute x4, waiting for transfers between devices, swapped(): lax.ppermute(value, 'space', pairs + [(target, source) for source, target...  1.69 us
    pallas_call x1, Pallas kernels, body(): call(first_kernel, (shape(ROWS, HALF, dtype=F32), volume, shape(HALF, ROW...  1.36 us
  transfers between devices with their start and end apart: 6, of which 2 were waited for; matrix products, arithmetic and copies ran while one was open for 0% of the time, Pallas kernels for 7%

profile of v14, /device:TPU:0, one launch (start us, length us, event | category | flops | bytes accessed | tf_op | source)
XLA Modules:
  0.0 44.9 jit_solution(16781362043338687201)
XLA Ops:
  0.6 1.7 %shard_map.94 = bf16[32,24,128]{2,1,0:T(8,128)(2,1)} custom-call(s32[1,32]{1,0:T(1,128)} %ids_hbm.1, bf16[1,64,512]{2,1,0:T(8,128)(2,1)} %latents_hbm.1), custom_call_target="tpu_custom_call" | custom-call | tf_op jit(solution)/shard_map/pallas_call | solution.py:429
  2.4 0.0 copy-start
  2.4 0.0 copy-start.4
  2.4 7.3 %all-to-all-start = ((bf16[32,24,128]{2,1,0:T(8,128)(2,1)}), bf16[32,24,128]{2,1,0:T(8,128)(2,1)S(1)}, u32[]{:S(2)}, u32[]{:S(2)}) async-start(bf16[32,24,128]{2,1,0:T(8,128)(2,1)} %shard_map.94), calls=%async_computation | async-start | bytes 393216 | tf_op jit(solution)/shard_map/all_to_all | solution.py:443
  9.7 0.1 shard_map.98
  9.8 0.7 %collective-permute-start = (bf16[48,256]{1,0:T(8,128)(2,1)S(1)}, bf16[48,256]{1,0:T(8,128)(2,1)S(1)}, u32[]{:S(2)}, u32[]{:S(2)}) collective-permute-start(bf16[48,256]{1,0:T(8,128)(2,1)S(1)} %get-tuple-element.28), channel_id=1, source_target_pairs={{2,4},{6,8},{10,12},{14,16},{18,20},{22,24},{26,28},{4,2},{8,6},{1... | collective-permute-start | bytes 73736 | tf_op jit(solution)/shard_map/ppermute | solution.py:419
  10.5 0.0 copy-start.1
  10.5 0.0 copy-start.2
  10.5 0.0 copy-start.3
  10.5 4.5 %collective-permute-start.1 = (bf16[48,256]{1,0:T(8,128)(2,1)S(1)}, bf16[48,256]{1,0:T(8,128)(2,1)S(1)}, u32[]{:S(2)}, u32[]{:S(2)}) collective-permute-start(bf16[48,256]{1,0:T(8,128)(2,1)S(1)} %get-tuple-element.29), channel_id=1, source_target_pairs={{0,2},{4,6},{8,10},{12,14},{16,18},{20,22},{24,26},{28,30},{2,0},{... | collective-permute-start | bytes 73736 | tf_op jit(solution)/shard_map/ppermute | solution.py:419
  15.1 0.3 shard_map.95.band_ref
  15.4 3.2 %all-to-all-done.received_ref = bf16[32,24,128]{2,1,0:T(8,128)(2,1)S(1)} async-done(((bf16[32,24,128]{2,1,0:T(8,128)(2,1)}), bf16[32,24,128]{2,1,0:T(8,128)(2,1)S(1)}, u32[]{:S(2)}, u32[]{:S(2)}) %all-to-all-start) | async-done | bytes 196640 | tf_op jit(solution)/shard_map/all_to_all | solution.py:443
  18.6 1.4 %shard_map.96 = (f32[256,128]{1,0:T(8,128)S(1)}, bf16[256,128]{1,0:T(8,128)(2,1)S(1)}, bf16[128,256]{1,0:T(8,128)(2,1)S(1)}, bf16[3,2,10,16,256]{4,3,2,1,0:T(8,1...) custom-call(s32[1,2,6]{2,1,0:T(2,128)S(1)} %copy-done.3, ...), custom_call_target="tpu_custom_call" | custom-call | tf_op jit(solution)/shard_map/pallas_call | solution.py:457
  20.0 0.0 collective-permute-done.1.near
  20.0 1.2 %shard_map.99 = (bf16[32,16,128]{2,1,0:T(8,128)(2,1)S(1)}, bf16[256,128]{1,0:T(8,128)(2,1)S(1)}, bf16[48,256]{1,0:T(8,128)(2,1)S(1)}, bf16[48,256]{1,0:T(8,128)(2,1)S(1)}) custom-call(f32[48,128]{1,0:T(8,128)S(1)} %get-tuple-element.21.masks_ref, bf16[1,2,8,8,256]{4,3,2,1,0:T(8,128)(2,1)S(1)} %copy-done, ...), custom_call_target="tpu_custom_call" | custom-call | tf_op jit(solution)/shard_map/pallas_call | solution.py:469
  21.2 10.9 %all_to_all.15.parts_ref = bf16[32,16,128]{2,1,0:T(8,128)(2,1)S(1)} all-to-all(bf16[32,16,128]{2,1,0:T(8,128)(2,1)S(1)} %get-tuple-element.36), channel_id=1, replica_groups=mesh['space'=16,'dp'=2] {'space','dp'}, dimensions={0} | all-to-all | bytes 262144 | tf_op jit(solution)/shard_map/all_to_all | solution.py:484
  32.1 0.9 %shard_map.101 = bf16[32,16,128]{2,1,0:T(8,128)(2,1)} custom-call(bf16[32,16,128]{2,1,0:T(8,128)(2,1)S(1)} %all_to_all.15.parts_ref), custom_call_target="tpu_custom_call" | custom-call | tf_op jit(solution)/shard_map/pallas_call | solution.py:486
  33.0 2.6 %all-to-all-start.2 = ((bf16[32,16,128]{2,1,0:T(8,128)(2,1)}), bf16[32,16,128]{2,1,0:T(8,128)(2,1)S(1)}, u32[]{:S(2)}, u32[]{:S(2)}) async-start(bf16[32,16,128]{2,1,0:T(8,128)(2,1)} %shard_map.101), calls=%async_computation.2 | async-start | bytes 262144 | tf_op jit(solution)/shard_map/all_to_all | solution.py:487
  35.6 0.7 %collective-permute-start.2 = (bf16[48,256]{1,0:T(8,128)(2,1)S(1)}, bf16[48,256]{1,0:T(8,128)(2,1)S(1)}, u32[]{:S(2)}, u32[]{:S(2)}) collective-permute-start(bf16[48,256]{1,0:T(8,128)(2,1)S(1)} %get-tuple-element.34), channel_id=1, source_target_pairs={{2,4},{6,8},{10,12},{14,16},{18,20},{22,24},{26,28},{4,2},{8,6},{1... | collective-permute-start | bytes 73736 | tf_op jit(solution)/shard_map/ppermute | solution.py:419
  36.2 4.4 %collective-permute-start.3 = (bf16[48,256]{1,0:T(8,128)(2,1)S(1)}, bf16[48,256]{1,0:T(8,128)(2,1)S(1)}, u32[]{:S(2)}, u32[]{:S(2)}) collective-permute-start(bf16[48,256]{1,0:T(8,128)(2,1)S(1)} %get-tuple-element.35), channel_id=1, source_target_pairs={{0,2},{4,6},{8,10},{12,14},{16,18},{20,22},{24,26},{28,30},{2,0},{... | collective-permute-start | bytes 73736 | tf_op jit(solution)/shard_map/ppermute | solution.py:419
  40.7 0.3 shard_map.97.band_ref
  41.0 1.7 %collective-permute-done.3.near = bf16[48,256]{1,0:T(8,128)(2,1)S(1)} collective-permute-done((bf16[48,256]{1,0:T(8,128)(2,1)S(1)}, bf16[48,256]{1,0:T(8,128)(2,1)S(1)}, u32[]{:S(2)}, u32[]{:S(2)}) %collective-permute-start.3) | collective-permute-done | bytes 24608 | tf_op jit(solution)/shard_map/ppermute | solution.py:419
  42.7 1.2 %shard_map.100 = bf16[1,2,8,8,256]{4,3,2,1,0:T(8,128)(2,1)} custom-call(f32[48,128]{1,0:T(8,128)S(1)} %get-tuple-element.21.masks_ref, bf16[9,256,128]{2,1,0:T(8,128)(2,1)S(1)} %shard_map.97.band_ref, bf16[256,128]{1,0:T(8,128)(2,1)S(1)} %get-tuple-element.32.lifted_ref, bf16[256,128]{1,0:T(8,128)(2,1)S(1)} %get-tuple-element.33.hidden_ref, ...), custom_call_target="tpu_custom_call" | custom-call | flops 1000000000 | bytes 2000000 | tf_op jit(solution)/shard_map/pallas_call | solution.py:481
  43.9 1.0 %shard_map.102 = (f32[27,32,32]{2,1,0:T(8,128)}, f32[27,32,32]{2,1,0:T(8,128)}) custom-call(bf16[32,16,128]{2,1,0:T(8,128)(2,1)S(1)} %all-to-all-done.2.sums_ref), custom_call_target="tpu_custom_call" | custom-call | tf_op jit(solution)/shard_map/pallas_call | solution.py:491
  (8 shorter events, 0.0 us)
Async XLA Ops:
  2.4 7.3 %copy-start = (bf16[1,2,8,8,256]{4,3,2,1,0:T(8,128)(2,1)S(1)}, bf16[1,2,8,8,256]{4,3,2,1,0:T(8,128)(2,1)}, u32[]{:S(2)}) copy-start(bf16[1,2,8,8,256]{4,3,2,1,0:T(8,128)(2,1)} %cotangent_ref.3) | copy-start | bytes 196612
  2.4 12.7 %copy-start.4 = (bf16[27,32,32]{2,1,0:T(8,128)(2,1)S(1)}, bf16[27,32,32]{2,1,0:T(8,128)(2,1)}, u32[]{:S(2)}) copy-start(bf16[27,32,32]{2,1,0:T(8,128)(2,1)} %weights_ref.3) | copy-start | bytes 165892
  2.4 16.2 %all-to-all-start = ((bf16[32,24,128]{2,1,0:T(8,128)(2,1)}), bf16[32,24,128]{2,1,0:T(8,128)(2,1)S(1)}, u32[]{:S(2)}, u32[]{:S(2)}) async-start(bf16[32,24,128]{2,1,0:T(8,128)(2,1)} %shard_map.94), calls=%async_computation | async-start | bytes 393216 | tf_op jit(solution)/shard_map/all_to_all | solution.py:443
  9.8 10.2 %collective-permute-start = (bf16[48,256]{1,0:T(8,128)(2,1)S(1)}, bf16[48,256]{1,0:T(8,128)(2,1)S(1)}, u32[]{:S(2)}, u32[]{:S(2)}) collective-permute-start(bf16[48,256]{1,0:T(8,128)(2,1)S(1)} %get-tuple-element.28), channel_id=1, source_target_pairs={{2,4},{6,8},{10,12},{14,16},{18,20},{22,24},{26,28},{4,2},{8,6},{1... | collective-permute-start | bytes 73736 | tf_op jit(solution)/shard_map/ppermute | solution.py:419
  10.5 8.1 %copy-start.1 = (bf16[64,2048]{1,0:T(8,128)(2,1)S(1)}, bf16[64,2048]{1,0:T(8,128)(2,1)}, u32[]{:S(2)}) copy-start(bf16[64,2048]{1,0:T(8,128)(2,1)} %up_ref.1) | copy-start | bytes 786436
  10.5 8.1 %copy-start.2 = (bf16[27,32,32]{2,1,0:T(8,128)(2,1)S(1)}, bf16[27,32,32]{2,1,0:T(8,128)(2,1)}, u32[]{:S(2)}) copy-start(bf16[27,32,32]{2,1,0:T(8,128)(2,1)} %weights_ref.5) | copy-start | bytes 165892
  10.5 8.1 %copy-start.3 = (s32[1,2,6]{2,1,0:T(2,128)S(1)}, s32[1,2,6]{2,1,0:T(2,128)}, u32[]{:S(2)}) copy-start(s32[1,2,6]{2,1,0:T(2,128)} %links_in.1) | copy-start | bytes 148
  10.5 9.5 %collective-permute-start.1 = (bf16[48,256]{1,0:T(8,128)(2,1)S(1)}, bf16[48,256]{1,0:T(8,128)(2,1)S(1)}, u32[]{:S(2)}, u32[]{:S(2)}) collective-permute-start(bf16[48,256]{1,0:T(8,128)(2,1)S(1)} %get-tuple-element.29), channel_id=1, source_target_pairs={{0,2},{4,6},{8,10},{12,14},{16,18},{20,22},{24,26},{28,30},{2,0},{... | collective-permute-start | bytes 73736 | tf_op jit(solution)/shard_map/ppermute | solution.py:419
  33.0 10.9 %all-to-all-start.2 = ((bf16[32,16,128]{2,1,0:T(8,128)(2,1)}), bf16[32,16,128]{2,1,0:T(8,128)(2,1)S(1)}, u32[]{:S(2)}, u32[]{:S(2)}) async-start(bf16[32,16,128]{2,1,0:T(8,128)(2,1)} %shard_map.101), calls=%async_computation.2 | async-start | bytes 262144 | tf_op jit(solution)/shard_map/all_to_all | solution.py:487
  35.6 5.4 %collective-permute-start.2 = (bf16[48,256]{1,0:T(8,128)(2,1)S(1)}, bf16[48,256]{1,0:T(8,128)(2,1)S(1)}, u32[]{:S(2)}, u32[]{:S(2)}) collective-permute-start(bf16[48,256]{1,0:T(8,128)(2,1)S(1)} %get-tuple-element.34), channel_id=1, source_target_pairs={{2,4},{6,8},{10,12},{14,16},{18,20},{22,24},{26,28},{4,2},{8,6},{1... | collective-permute-start | bytes 73736 | tf_op jit(solution)/shard_map/ppermute | solution.py:419
  36.2 6.5 %collective-permute-start.3 = (bf16[48,256]{1,0:T(8,128)(2,1)S(1)}, bf16[48,256]{1,0:T(8,128)(2,1)S(1)}, u32[]{:S(2)}, u32[]{:S(2)}) collective-permute-start(bf16[48,256]{1,0:T(8,128)(2,1)S(1)} %get-tuple-element.35), channel_id=1, source_target_pairs={{0,2},{4,6},{8,10},{12,14},{16,18},{20,22},{24,26},{28,30},{2,0},{... | collective-permute-start | bytes 73736 | tf_op jit(solution)/shard_map/ppermute | solution.py:419

commit v15 on v14

--- a/solution.py
+++ b/solution.py
@@ -99,6 +99,17 @@
     build_band(band_ref, weight_rows(weights_ref[...].astype(F32)))
 
 
+def bands_kernel(one_hbm, two_hbm, band_ref, back_ref, one_ref, two_ref, sems):
+    one_copy = pltpu.make_async_copy(one_hbm, one_ref, sems.at[0])
+    two_copy = pltpu.make_async_copy(two_hbm, two_ref, sems.at[1])
+    one_copy.start()
+    two_copy.start()
+    one_copy.wait()
+    build_band(band_ref, weight_rows(one_ref[...].astype(F32)))
+    two_copy.wait()
+    build_band(back_ref, flipped_rows(two_ref[...].astype(F32)))
+
+
 def put_padded(pad_ref, brick, lines, x_low, x_high, y_low, y_high, z_low, z_high):
     def joined(halves, before, after):
         lane = lanes_of(halves[0].shape)
@@ -127,11 +138,8 @@
 
 
 def convolve(pad_ref, band_ref):
-    total = None
-    for k in range(9):
-        term = dot(window(pad_ref, k), band_ref[k])
-        total = term if total is None else total + term
-    return total
+    windows = jnp.concatenate([window(pad_ref, k) for k in range(9)], axis=1)
+    return dot(windows, band_ref[...].reshape(9 * WIDE, HALF))
 
 
 def half_lines(values):
@@ -198,8 +206,8 @@
 
 
 def first_kernel(
-    links_in, received_ref, up_ref, band_ref, weights_ref,
-    slope_out, hidden_out, turned_out, pad_out, back_out, high_out, low_out, masks_out,
+    links_in, received_ref, up_ref, band_ref,
+    slope_out, hidden_out, turned_out, pad_out, high_out, low_out, masks_out,
     volumes_ref, rows_ref, halves_ref, faces_ref, links_ref, links_sem,
 ):
     links_copy = pltpu.make_async_copy(links_in, links_ref, links_sem)
@@ -256,7 +264,6 @@
     hidden = hidden.astype(F32)
     turned_out[...] = jnp.transpose(hidden).astype(BF16)
     pack_all(half_lines(hidden), halves_ref, faces_ref, high_out, low_out)
-    build_band(back_out, flipped_rows(weights_ref[...].astype(F32)))
 
 
 def fold(outer, places):
@@ -381,7 +388,9 @@
     out_ref[...] = jnp.broadcast_to(total.astype(BF16)[None], out_ref.shape)
 
 
-def unpack_kernel(sums_ref, one_out, two_out, rows_ref, one_ref, two_ref, sems):
+def unpack_kernel(sums_ref, fine_ref, one_out, two_out, fine_out, rows_ref, one_ref, two_ref, sems, fine_sem):
+    fine_copy = pltpu.make_async_copy(fine_ref, fine_out, fine_sem)
+    fine_copy.start()
     rows_ref[...] = sums_ref[...].astype(F32).reshape(rows_ref.shape)
     copies = []
     for which, (block_ref, out) in enumerate(((one_ref, one_out), (two_ref, two_out))):
@@ -395,6 +404,7 @@
             copies[-1].start()
     for copy in copies:
         copy.wait()
+    fine_copy.wait()
 
 
 def call(kernel, out_shape, scratch=(), hbm=(), inputs=1, limit=24, cost=None, out=pltpu.VMEM):
@@ -412,6 +422,10 @@
 
 def shape(*dims, dtype=BF16):
     return jax.ShapeDtypeStruct(dims, dtype)
+
+
+def kept_in_hbm(value):
+    return pltpu.with_memory_space_constraint(value, pltpu.HBM)
 
 
 def swapped(value, first):
@@ -437,8 +451,7 @@
         ],
         hbm=(0, 1),
         inputs=2,
-        limit=60,
-    )(active_blocks, coarse_latents)
+    )(kept_in_hbm(active_blocks), kept_in_hbm(coarse_latents))
     axes = ("space", "dp")
     received = lax.all_to_all(packed, axes if scenes == 2 else "space", split_axis=0, concat_axis=0, tiled=True)
     cost = pl.CostEstimate(flops=10**9, bytes_accessed=2 * 10**6, transcendentals=0)
@@ -453,17 +466,25 @@
     high, low, far, near = call(faces_kernel, (face,) * 4, [halves, faces])(cotangent)
     far = swapped(far, 1)
     near = swapped(near, 0)
-    band_one = call(band_kernel, shape(*BAND), cost=cost)(conv_one)
-    slope, hidden, turned, lifted_pad, band_back, hidden_high, hidden_low, masks = call(
+    weights = pltpu.VMEM(conv_one.shape, BF16)
+    band_one, band_back = call(
+        bands_kernel,
+        (shape(*BAND), shape(*BAND)),
+        [weights, weights, pltpu.SemaphoreType.DMA((2,))],
+        hbm=(0, 1),
+        inputs=2,
+        cost=cost,
+    )(kept_in_hbm(conv_one), kept_in_hbm(conv_two))
+    slope, hidden, turned, lifted_pad, hidden_high, hidden_low, masks = call(
         first_kernel,
         (
-            shape(ROWS, HALF, dtype=F32), volume, shape(HALF, ROWS), shape(*pad_shape), shape(*BAND),
+            shape(ROWS, HALF, dtype=F32), volume, shape(HALF, ROWS), shape(*pad_shape),
             face, face, shape(BRICKS * 6 * 2 * BRICKS, 128, dtype=F32),
         ),
         [pltpu.VMEM((2, 8 * CUBE, 128), F32), pltpu.VMEM((8 * tiles, 128), F32), halves, faces, *links],
         hbm=(0,),
-        inputs=5,
-    )(face_links, received, up_weight, band_one, conv_two)
+        inputs=4,
+    )(face_links, received, up_weight, band_one)
     per = -(-BLOCKS // everyone)
     per += per % 2
     sums, lifted, hidden_far, hidden_near = call(
@@ -487,8 +508,11 @@
     gathered = lax.all_to_all(total, axes, split_axis=0, concat_axis=0, tiled=True)
     grads = shape(27, CHANNELS, CHANNELS, dtype=F32)
     block = pltpu.VMEM(grads.shape, F32)
-    scratch = [pltpu.VMEM((everyone * per * 8, 128), F32), block, block, pltpu.SemaphoreType.DMA((2, 3))]
-    grad_one, grad_two = call(unpack_kernel, (grads, grads), scratch, out=pl.ANY)(gathered)
+    scratch = [pltpu.VMEM((everyone * per * 8, 128), F32), block, block]
+    scratch += [pltpu.SemaphoreType.DMA((2, 3)), pltpu.SemaphoreType.DMA]
+    grad_one, grad_two, fine = call(
+        unpack_kernel, (grads, grads, shape(*fine.shape)), scratch, inputs=2, out=pl.ANY
+    )(gathered, fine)
     return (fine, grad_one, grad_two)
 
 

time: 45.2 us -> 45.8 us (1.013)
  waiting for transfers between devices: 4.89 us -> 4.03 us
  Pallas kernels: 8.17 us -> 8.94 us
  blocking collectives: 10.9 us -> 11.5 us
    pallas_call x2, Pallas kernels: 1.37 us -> 2.81 us  [the longest x1 1.75 us: body(): call(bands_kernel, (shape(*BAND), shape(*BAND)), [weights, weights, pltpu...]
    all_to_all x1, waiting for transfers between devices: 3.2 us -> 1.79 us  [body(): lax.all_to_all(packed, axes if scenes == 2 else 'space', split_axis=0, co...]
    all_to_all x1, blocking collectives: 10.9 us -> 11.5 us  [body(): parts = lax.all_to_all(sums, axes, split_axis=0, concat_axis=0, tiled=True)]
    pallas_call x1, Pallas kernels: 1.17 us -> 0.55 us  [body(): call(fine_kernel, shape(*cotangent.shape), [pool, pool, pad], inputs=8, c...]
    all_to_all x1, waiting for transfers between devices: 0.01 us -> 0.55 us  [body(): lax.all_to_all(total, axes, split_axis=0, concat_axis=0, tiled=True)]
  transfers between devices with their start and end apart: 6 -> 6, of which waited for: 2 -> 3; matrix products, arithmetic and copies ran while one was open for 0% -> 0% of each run, Pallas kernels for 7% -> 9%
where the time goes in v15:
time: 45.8 us; the launch traced here: 45.4 us
  starting transfers between devices  20.2 us (44%)
  blocking collectives  11.5 us (25%)
  Pallas kernels  8.94 us (20%)
  waiting for transfers between devices  4.03 us (9%)
  between operations  0.76 us (2%)
    all_to_all x1, blocking collectives, body(): parts = lax.all_to_all(sums, axes, split_axis=0, concat_axis=0, tiled=True)  11.5 us
    ppermute x4, starting transfers between devices, swapped(): lax.ppermute(value, 'space', pairs + [(target, source) for source, target...  10.3 us
    all_to_all x1, starting transfers between devices, body(): lax.all_to_all(packed, axes if scenes == 2 else 'space', split_axis=0, co...  7.3 us
    all_to_all x1, starting transfers between devices, body(): lax.all_to_all(total, axes, split_axis=0, concat_axis=0, tiled=True)  2.58 us
    all_to_all x1, waiting for transfers between devices, body(): lax.all_to_all(packed, axes if scenes == 2 else 'space', split_axis=0, co...  1.79 us
    pallas_call x1, Pallas kernels, body(): call(bands_kernel, (shape(*BAND), shape(*BAND)), [weights, weights, pltpu...  1.75 us
    pallas_call x1, Pallas kernels, body(): call(functools.partial(pick_kernel, scenes), shape(devices * scenes, 3 *...  1.74 us
    ppermute x4, waiting for transfers between devices, swapped(): lax.ppermute(value, 'space', pairs + [(target, source) for source, target...  1.69 us
  transfers between devices with their start and end apart: 6, of which 3 were waited for; matrix products, arithmetic and copies ran while one was open for 0% of the time, Pallas kernels for 9%

profile of v15, /device:TPU:0, one launch (start us, length us, event | category | flops | bytes accessed | tf_op | source)
XLA Modules:
  0.0 45.4 jit_solution(10884122226407838281)
XLA Ops:
  0.6 1.7 %shard_map.94 = bf16[32,24,128]{2,1,0:T(8,128)(2,1)} custom-call(s32[1,32]{1,0:T(1,128)} %ids_hbm.1, bf16[1,64,512]{2,1,0:T(8,128)(2,1)} %latents_hbm.1), custom_call_target="tpu_custom_call" | custom-call | tf_op jit(solution)/shard_map/pallas_call | solution.py:443
  2.4 0.0 copy-start.1
  2.4 7.3 %all-to-all-start = ((bf16[32,24,128]{2,1,0:T(8,128)(2,1)}), bf16[32,24,128]{2,1,0:T(8,128)(2,1)S(1)}, u32[]{:S(2)}, u32[]{:S(2)}) async-start(bf16[32,24,128]{2,1,0:T(8,128)(2,1)} %shard_map.94), calls=%async_computation | async-start | bytes 393216 | tf_op jit(solution)/shard_map/all_to_all | solution.py:456
  9.7 0.1 shard_map.97
  9.8 0.7 %collective-permute-start = (bf16[48,256]{1,0:T(8,128)(2,1)S(1)}, bf16[48,256]{1,0:T(8,128)(2,1)S(1)}, u32[]{:S(2)}, u32[]{:S(2)}) collective-permute-start(bf16[48,256]{1,0:T(8,128)(2,1)S(1)} %get-tuple-element.31), channel_id=1, source_target_pairs={{2,4},{6,8},{10,12},{14,16},{18,20},{22,24},{26,28},{4,2},{8,6},{1... | collective-permute-start | bytes 73736 | tf_op jit(solution)/shard_map/ppermute | solution.py:433
  10.5 0.0 copy-start
  10.5 4.5 %collective-permute-start.1 = (bf16[48,256]{1,0:T(8,128)(2,1)S(1)}, bf16[48,256]{1,0:T(8,128)(2,1)S(1)}, u32[]{:S(2)}, u32[]{:S(2)}) collective-permute-start(bf16[48,256]{1,0:T(8,128)(2,1)S(1)} %get-tuple-element.32), channel_id=1, source_target_pairs={{0,2},{4,6},{8,10},{12,14},{16,18},{20,22},{24,26},{28,30},{2,0},{... | collective-permute-start | bytes 73736 | tf_op jit(solution)/shard_map/ppermute | solution.py:433
  15.0 1.8 %shard_map.95 = (bf16[9,256,128]{2,1,0:T(8,128)(2,1)S(1)}, bf16[9,256,128]{2,1,0:T(8,128)(2,1)S(1)}) custom-call(bf16[27,32,32]{2,1,0:T(8,128)(2,1)} %one_hbm.1, bf16[27,32,32]{2,1,0:T(8,128)(2,1)} %weights_ref.1), custom_call_target="tpu_custom_call" | custom-call | flops 1000000000 | bytes 2000000 | tf_op jit(solution)/shard_map/pallas_call | solution.py:470
  16.8 0.0 copy-start.2
  16.8 1.8 %all-to-all-done.received_ref = bf16[32,24,128]{2,1,0:T(8,128)(2,1)S(1)} async-done(((bf16[32,24,128]{2,1,0:T(8,128)(2,1)}), bf16[32,24,128]{2,1,0:T(8,128)(2,1)S(1)}, u32[]{:S(2)}, u32[]{:S(2)}) %all-to-all-start) | async-done | bytes 196640 | tf_op jit(solution)/shard_map/all_to_all | solution.py:456
  18.6 1.3 %shard_map.96 = (f32[256,128]{1,0:T(8,128)S(1)}, bf16[256,128]{1,0:T(8,128)(2,1)S(1)}, bf16[128,256]{1,0:T(8,128)(2,1)S(1)}, bf16[3,2,10,16,256]{4,3,2,1,0:T(8,1...) custom-call(s32[1,2,6]{2,1,0:T(2,128)S(1)} %copy-done.2, ...), custom_call_target="tpu_custom_call" | custom-call | tf_op jit(solution)/shard_map/pallas_call | solution.py:478
  19.9 0.0 collective-permute-done.far
  19.9 1.2 %shard_map.98 = (bf16[32,16,128]{2,1,0:T(8,128)(2,1)S(1)}, bf16[256,128]{1,0:T(8,128)(2,1)S(1)}, bf16[48,256]{1,0:T(8,128)(2,1)S(1)}, bf16[48,256]{1,0:T(8,128)(2,1)S(1)}) custom-call(f32[48,128]{1,0:T(8,128)S(1)} %get-tuple-element.24.masks_ref, bf16[1,2,8,8,256]{4,3,2,1,0:T(8,128)(2,1)S(1)} %copy-done.1, ...), custom_call_target="tpu_custom_call" | custom-call | tf_op jit(solution)/shard_map/pallas_call | solution.py:490
  21.1 11.5 %all_to_all.15.parts_ref = bf16[32,16,128]{2,1,0:T(8,128)(2,1)S(1)} all-to-all(bf16[32,16,128]{2,1,0:T(8,128)(2,1)S(1)} %get-tuple-element.35), channel_id=1, replica_groups=mesh['space'=16,'dp'=2] {'space','dp'}, dimensions={0} | all-to-all | bytes 262144 | tf_op jit(solution)/shard_map/all_to_all | solution.py:505
  32.7 0.9 %shard_map.99 = bf16[32,16,128]{2,1,0:T(8,128)(2,1)} custom-call(bf16[32,16,128]{2,1,0:T(8,128)(2,1)S(1)} %all_to_all.15.parts_ref), custom_call_target="tpu_custom_call" | custom-call | tf_op jit(solution)/shard_map/pallas_call | solution.py:507
  33.6 2.6 %all-to-all-start.2 = ((bf16[32,16,128]{2,1,0:T(8,128)(2,1)}), bf16[32,16,128]{2,1,0:T(8,128)(2,1)S(1)}, u32[]{:S(2)}, u32[]{:S(2)}) async-start(bf16[32,16,128]{2,1,0:T(8,128)(2,1)} %shard_map.99), calls=%async_computation.2 | async-start | bytes 262144 | tf_op jit(solution)/shard_map/all_to_all | solution.py:508
  36.2 0.7 %collective-permute-start.2 = (bf16[48,256]{1,0:T(8,128)(2,1)S(1)}, bf16[48,256]{1,0:T(8,128)(2,1)S(1)}, u32[]{:S(2)}, u32[]{:S(2)}) collective-permute-start(bf16[48,256]{1,0:T(8,128)(2,1)S(1)} %get-tuple-element.38), channel_id=1, source_target_pairs={{2,4},{6,8},{10,12},{14,16},{18,20},{22,24},{26,28},{4,2},{8,6},{1... | collective-permute-start | bytes 73736 | tf_op jit(solution)/shard_map/ppermute | solution.py:433
  36.8 4.4 %collective-permute-start.3 = (bf16[48,256]{1,0:T(8,128)(2,1)S(1)}, bf16[48,256]{1,0:T(8,128)(2,1)S(1)}, u32[]{:S(2)}, u32[]{:S(2)}) collective-permute-start(bf16[48,256]{1,0:T(8,128)(2,1)S(1)} %get-tuple-element.39), channel_id=1, source_target_pairs={{0,2},{4,6},{8,10},{12,14},{16,18},{20,22},{24,26},{28,30},{2,0},{... | collective-permute-start | bytes 73736 | tf_op jit(solution)/shard_map/ppermute | solution.py:433
  41.3 0.3 shard_map.100.band_ref
  41.6 0.0 collective-permute-done.2.far
  41.6 1.7 %collective-permute-done.3.near = bf16[48,256]{1,0:T(8,128)(2,1)S(1)} collective-permute-done((bf16[48,256]{1,0:T(8,128)(2,1)S(1)}, bf16[48,256]{1,0:T(8,128)(2,1)S(1)}, u32[]{:S(2)}, u32[]{:S(2)}) %collective-permute-start.3) | collective-permute-done | bytes 24608 | tf_op jit(solution)/shard_map/ppermute | solution.py:433
  43.3 0.5 %shard_map.101.fine_ref = bf16[1,2,8,8,256]{4,3,2,1,0:T(8,128)(2,1)S(1)} custom-call(f32[48,128]{1,0:T(8,128)S(1)} %get-tuple-element.24.masks_ref, bf16[9,256,128]{2,1,0:T(8,128)(2,1)S(1)} %shard_map.100.band_ref, bf16[256,128]{1,0:T(8,128)(2,1)S(1)} %get-tuple-element.36.lifted_ref, bf16[256,128]{1,0:T(8,128)(2,1)S(1)} %get-tuple-element.37.hidden_ref, ...), custom_call_target="tpu_custom_call" | custom-call | flops 1000000000 | bytes 2000000 | tf_op jit(solution)/shard_map/pallas_call | solution.py:502
  43.8 0.6 %all-to-all-done.2.sums_ref = bf16[32,16,128]{2,1,0:T(8,128)(2,1)S(1)} async-done(((bf16[32,16,128]{2,1,0:T(8,128)(2,1)}), bf16[32,16,128]{2,1,0:T(8,128)(2,1)S(1)}, u32[]{:S(2)}, u32[]{:S(2)}) %all-to-all-start.2) | async-done | bytes 131104 | tf_op jit(solution)/shard_map/all_to_all | solution.py:508
  44.4 1.1 %shard_map.102 = (f32[27,32,32]{2,1,0:T(8,128)}, f32[27,32,32]{2,1,0:T(8,128)}, bf16[1,2,8,8,256]{4,3,2,1,0:T(8,128)(2,1)}) custom-call(bf16[32,16,128]{2,1,0:T(8,128)(2,1)S(1)} %all-to-all-done.2.sums_ref, bf16[1,2,8,8,256]{4,3,2,1,0:T(8,128)(2,1)S(1)} %shard_map.101.fine_ref), custom_call_target="tpu_custom_call" | custom-call | tf_op jit(solution)/shard_map/pallas_call | solution.py:513
  (6 shorter events, 0.0 us)
Async XLA Ops:
  2.4 7.3 %copy-start.1 = (bf16[1,2,8,8,256]{4,3,2,1,0:T(8,128)(2,1)S(1)}, bf16[1,2,8,8,256]{4,3,2,1,0:T(8,128)(2,1)}, u32[]{:S(2)}) copy-start(bf16[1,2,8,8,256]{4,3,2,1,0:T(8,128)(2,1)} %cotangent_ref.3) | copy-start | bytes 196612
  2.4 16.2 %all-to-all-start = ((bf16[32,24,128]{2,1,0:T(8,128)(2,1)}), bf16[32,24,128]{2,1,0:T(8,128)(2,1)S(1)}, u32[]{:S(2)}, u32[]{:S(2)}) async-start(bf16[32,24,128]{2,1,0:T(8,128)(2,1)} %shard_map.94), calls=%async_computation | async-start | bytes 393216 | tf_op jit(solution)/shard_map/all_to_all | solution.py:456
  9.8 10.1 %collective-permute-start = (bf16[48,256]{1,0:T(8,128)(2,1)S(1)}, bf16[48,256]{1,0:T(8,128)(2,1)S(1)}, u32[]{:S(2)}, u32[]{:S(2)}) collective-permute-start(bf16[48,256]{1,0:T(8,128)(2,1)S(1)} %get-tuple-element.31), channel_id=1, source_target_pairs={{2,4},{6,8},{10,12},{14,16},{18,20},{22,24},{26,28},{4,2},{8,6},{1... | collective-permute-start | bytes 73736 | tf_op jit(solution)/shard_map/ppermute | solution.py:433
  10.5 8.1 %copy-start = (bf16[64,2048]{1,0:T(8,128)(2,1)S(1)}, bf16[64,2048]{1,0:T(8,128)(2,1)}, u32[]{:S(2)}) copy-start(bf16[64,2048]{1,0:T(8,128)(2,1)} %up_ref.1) | copy-start | bytes 786436
  10.5 9.4 %collective-permute-start.1 = (bf16[48,256]{1,0:T(8,128)(2,1)S(1)}, bf16[48,256]{1,0:T(8,128)(2,1)S(1)}, u32[]{:S(2)}, u32[]{:S(2)}) collective-permute-start(bf16[48,256]{1,0:T(8,128)(2,1)S(1)} %get-tuple-element.32), channel_id=1, source_target_pairs={{0,2},{4,6},{8,10},{12,14},{16,18},{20,22},{24,26},{28,30},{2,0},{... | collective-permute-start | bytes 73736 | tf_op jit(solution)/shard_map/ppermute | solution.py:433
  16.8 1.8 %copy-start.2 = (s32[1,2,6]{2,1,0:T(2,128)S(1)}, s32[1,2,6]{2,1,0:T(2,128)}, u32[]{:S(2)}) copy-start(s32[1,2,6]{2,1,0:T(2,128)} %links_in.1) | copy-start | bytes 148
  32.7 8.6 %copy-start.3 = (bf16[27,32,32]{2,1,0:T(8,128)(2,1)S(1)}, bf16[27,32,32]{2,1,0:T(8,128)(2,1)}, u32[]{:S(2)}) copy-start(bf16[27,32,32]{2,1,0:T(8,128)(2,1)} %weights_ref.1) | copy-start | bytes 165892
  33.6 10.8 %all-to-all-start.2 = ((bf16[32,16,128]{2,1,0:T(8,128)(2,1)}), bf16[32,16,128]{2,1,0:T(8,128)(2,1)S(1)}, u32[]{:S(2)}, u32[]{:S(2)}) async-start(bf16[32,16,128]{2,1,0:T(8,128)(2,1)} %shard_map.99), calls=%async_computation.2 | async-start | bytes 262144 | tf_op jit(solution)/shard_map/all_to_all | solution.py:508
  36.2 5.4 %collective-permute-start.2 = (bf16[48,256]{1,0:T(8,128)(2,1)S(1)}, bf16[48,256]{1,0:T(8,128)(2,1)S(1)}, u32[]{:S(2)}, u32[]{:S(2)}) collective-permute-start(bf16[48,256]{1,0:T(8,128)(2,1)S(1)} %get-tuple-element.38), channel_id=1, source_target_pairs={{2,4},{6,8},{10,12},{14,16},{18,20},{22,24},{26,28},{4,2},{8,6},{1... | collective-permute-start | bytes 73736 | tf_op jit(solution)/shard_map/ppermute | solution.py:433
  36.8 6.5 %collective-permute-start.3 = (bf16[48,256]{1,0:T(8,128)(2,1)S(1)}, bf16[48,256]{1,0:T(8,128)(2,1)S(1)}, u32[]{:S(2)}, u32[]{:S(2)}) collective-permute-start(bf16[48,256]{1,0:T(8,128)(2,1)S(1)} %get-tuple-element.39), channel_id=1, source_target_pairs={{0,2},{4,6},{8,10},{12,14},{16,18},{20,22},{24,26},{28,30},{2,0},{... | collective-permute-start | bytes 73736 | tf_op jit(solution)/shard_map/ppermute | solution.py:433

commit v16 on v14

--- a/solution.py
+++ b/solution.py
@@ -99,6 +99,14 @@
     build_band(band_ref, weight_rows(weights_ref[...].astype(F32)))
 
 
+def masks_kernel(links_in, weights_ref, band_ref, masks_ref, links_ref, links_sem):
+    links_copy = pltpu.make_async_copy(links_in, links_ref, links_sem)
+    links_copy.start()
+    band_kernel(weights_ref, band_ref)
+    links_copy.wait()
+    put_masks(masks_ref, links_ref)
+
+
 def put_padded(pad_ref, brick, lines, x_low, x_high, y_low, y_high, z_low, z_high):
     def joined(halves, before, after):
         lane = lanes_of(halves[0].shape)
@@ -199,8 +207,8 @@
 
 def first_kernel(
     links_in, received_ref, up_ref, band_ref, weights_ref,
-    slope_out, hidden_out, turned_out, pad_out, back_out, high_out, low_out, masks_out,
-    volumes_ref, rows_ref, halves_ref, faces_ref, links_ref, links_sem,
+    slope_out, hidden_out, turned_out, pad_out, back_out,
+    volumes_ref, rows_ref, links_ref, links_sem,
 ):
     links_copy = pltpu.make_async_copy(links_in, links_ref, links_sem)
     links_copy.start()
@@ -218,35 +226,33 @@
         a, b, c = cell // 4, cell // 2 % 2, cell % 2
         for sub in range(16):
             line = (4 * a + sub // 4) * EDGE + 4 * b + sub % 4
-            volumes_ref[c, pl.ds(line, 8, stride=CUBE), :] = lifted[
+            volumes_ref[c, line * 8 : line * 8 + 8, :] = lifted[
                 cell * 8 : cell * 8 + 8, sub * 128 : sub * 128 + 128
             ]
     links_copy.wait()
-    put_masks(masks_out, links_ref)
     for brick in range(BRICKS):
 
         def near(face):
             link = links_ref[0, brick, face]
             index = jnp.clip(link - BRICKS * (position - 1), 0, 3 * BRICKS - 1)
-            return pl.multiple_of(index * CUBE, CUBE), jnp.where(link >= 0, 1.0, 0.0).astype(F32)
+            return index, jnp.where(link >= 0, 1.0, 0.0).astype(F32)
 
         def x_face(face):
-            start, present = near(face)
-            offset = EDGE * (EDGE - 1) if face % 2 == 0 else 0
-            return [half * present for half in pair(volumes_ref, pl.multiple_of(start + offset, 8), EDGE)]
+            index, present = near(face)
+            line = EDGE * (EDGE - 1) if face % 2 == 0 else 0
+            return [half * present for half in pair(volumes_ref, line * 8 + index, EDGE, 8)]
 
         def y_face(face):
-            start, present = near(face)
-            offset = EDGE - 1 if face % 2 == 0 else 0
-            return [half * present for half in pair(volumes_ref, start + offset, EDGE, EDGE)]
+            index, present = near(face)
+            line = EDGE - 1 if face % 2 == 0 else 0
+            return [half * present for half in pair(volumes_ref, line * 8 + index, EDGE, 8 * EDGE)]
 
         def z_face(face):
-            start, present = near(face)
-            tile = volumes_ref[1 if face % 2 == 0 else 0, pl.ds(start, CUBE), :] * present
+            index, present = near(face)
+            tile = volumes_ref[1 if face % 2 == 0 else 0, pl.ds(index, CUBE, stride=8), :] * present
             return tile.reshape(EDGE, EDGE, HALF)
 
-        own = pair(volumes_ref, (BRICKS + brick) * CUBE, CUBE)
-        own = [half.reshape(EDGE, EDGE, HALF) for half in own]
+        own = [half.reshape(EDGE, EDGE, HALF) for half in pair(volumes_ref, BRICKS + brick, CUBE, 8)]
         put_padded(pad_out, brick, own, x_face(0), x_face(1), y_face(2), y_face(3), z_face(4), z_face(5))
     pre = convolve(pad_out, band_ref)
     sigmoid = 1.0 / (1.0 + jnp.exp(-pre))
@@ -255,8 +261,12 @@
     hidden_out[...] = hidden
     hidden = hidden.astype(F32)
     turned_out[...] = jnp.transpose(hidden).astype(BF16)
-    pack_all(half_lines(hidden), halves_ref, faces_ref, high_out, low_out)
     build_band(back_out, flipped_rows(weights_ref[...].astype(F32)))
+
+
+def hidden_faces_kernel(hidden_ref, _parts, high_out, low_out, far_out, near_out, halves_ref, faces_ref):
+    pack_all(half_lines(hidden_ref[...].astype(F32)), halves_ref, faces_ref, high_out, low_out)
+    to_partners(high_out, low_out, far_out, near_out)
 
 
 def fold(outer, places):
@@ -327,11 +337,9 @@
 
 def second_kernel(
     masks_ref, cotangent_ref, band_ref, slope_ref, hidden_ref, lifted_pad, high_own, low_own, far, near,
-    hidden_high, hidden_low,
-    sums_out, lifted_out, far_out, near_out,
+    sums_out, lifted_out,
     high_pool, low_pool, cotangent_pad, sums_ref,
 ):
-    to_partners(hidden_high, hidden_low, far_out, near_out)
     lifted_out[...] = window(lifted_pad, 4)[:, :HALF]
     bricks = cotangent_lines(cotangent_ref)
     pad_all(cotangent_pad, bricks, masks_ref, high_pool, low_pool, high_own, low_own, far, near)
@@ -381,7 +389,9 @@
     out_ref[...] = jnp.broadcast_to(total.astype(BF16)[None], out_ref.shape)
 
 
-def unpack_kernel(sums_ref, one_out, two_out, rows_ref, one_ref, two_ref, sems):
+def unpack_kernel(sums_ref, fine_ref, one_out, two_out, fine_out, rows_ref, one_ref, two_ref, sems, fine_sem):
+    fine_copy = pltpu.make_async_copy(fine_ref, fine_out, fine_sem)
+    fine_copy.start()
     rows_ref[...] = sums_ref[...].astype(F32).reshape(rows_ref.shape)
     copies = []
     for which, (block_ref, out) in enumerate(((one_ref, one_out), (two_ref, two_out))):
@@ -395,6 +405,7 @@
             copies[-1].start()
     for copy in copies:
         copy.wait()
+    fine_copy.wait()
 
 
 def call(kernel, out_shape, scratch=(), hbm=(), inputs=1, limit=24, cost=None, out=pltpu.VMEM):
@@ -453,42 +464,47 @@
     high, low, far, near = call(faces_kernel, (face,) * 4, [halves, faces])(cotangent)
     far = swapped(far, 1)
     near = swapped(near, 0)
-    band_one = call(band_kernel, shape(*BAND), cost=cost)(conv_one)
-    slope, hidden, turned, lifted_pad, band_back, hidden_high, hidden_low, masks = call(
+    masks = shape(BRICKS * 6 * 2 * BRICKS, 128, dtype=F32)
+    band_one, masks = call(masks_kernel, (shape(*BAND), masks), links, hbm=(0,), inputs=2, cost=cost)(
+        face_links, conv_one
+    )
+    slope, hidden, turned, lifted_pad, band_back = call(
         first_kernel,
         (
             shape(ROWS, HALF, dtype=F32), volume, shape(HALF, ROWS), shape(*pad_shape), shape(*BAND),
-            face, face, shape(BRICKS * 6 * 2 * BRICKS, 128, dtype=F32),
         ),
-        [pltpu.VMEM((2, 8 * CUBE, 128), F32), pltpu.VMEM((8 * tiles, 128), F32), halves, faces, *links],
+        [pltpu.VMEM((2, 8 * CUBE, 128), F32), pltpu.VMEM((8 * tiles, 128), F32), *links],
         hbm=(0,),
         inputs=5,
     )(face_links, received, up_weight, band_one, conv_two)
     per = -(-BLOCKS // everyone)
     per += per % 2
-    sums, lifted, hidden_far, hidden_near = call(
+    sums, lifted = call(
         second_kernel,
-        (shape(everyone, per * 8, 128), volume, face, face),
+        (shape(everyone, per * 8, 128), volume),
         [pool, pool, pad, pltpu.VMEM((everyone * per * 8, 128), F32)],
-        inputs=12,
-    )(
-        masks, cotangent, band_back, slope, turned, lifted_pad, high, low, far, near,
-        hidden_high, hidden_low,
-    )
+        inputs=10,
+    )(masks, cotangent, band_back, slope, turned, lifted_pad, high, low, far, near)
+    parts = lax.all_to_all(sums, axes, split_axis=0, concat_axis=0, tiled=True)
+    hidden_high, hidden_low, hidden_far, hidden_near = call(
+        hidden_faces_kernel, (face,) * 4, [halves, faces], hbm=(1,), inputs=2
+    )(hidden, parts)
     hidden_far = swapped(hidden_far, 1)
     hidden_near = swapped(hidden_near, 0)
     band_two = call(band_kernel, shape(*BAND), cost=cost)(conv_two)
     fine = call(fine_kernel, shape(*cotangent.shape), [pool, pool, pad], inputs=8, cost=cost)(
         masks, band_two, lifted, hidden, hidden_high, hidden_low, hidden_far, hidden_near
     )
-    parts = lax.all_to_all(sums, axes, split_axis=0, concat_axis=0, tiled=True)
     scale = 1.0 / math.sqrt(lax.axis_size("dp") * devices * BRICKS * EDGE**3)
     total = call(functools.partial(sum_kernel, scale), shape(*sums.shape))(parts)
     gathered = lax.all_to_all(total, axes, split_axis=0, concat_axis=0, tiled=True)
     grads = shape(27, CHANNELS, CHANNELS, dtype=F32)
     block = pltpu.VMEM(grads.shape, F32)
-    scratch = [pltpu.VMEM((everyone * per * 8, 128), F32), block, block, pltpu.SemaphoreType.DMA((2, 3))]
-    grad_one, grad_two = call(unpack_kernel, (grads, grads), scratch, out=pl.ANY)(gathered)
+    scratch = [pltpu.VMEM((everyone * per * 8, 128), F32), block, block]
+    scratch += [pltpu.SemaphoreType.DMA((2, 3)), pltpu.SemaphoreType.DMA]
+    grad_one, grad_two, fine = call(
+        unpack_kernel, (grads, grads, shape(*fine.shape)), scratch, inputs=2, out=pl.ANY
+    )(gathered, fine)
     return (fine, grad_one, grad_two)
 
 

time: 45.2 us -> 45 us (level)
    pallas_call x1, Pallas kernels: 1.17 us -> 0.54 us  [body(): call(fine_kernel, shape(*cotangent.shape), [pool, pool, pad], inputs=8, c...]
    pallas_call x3 -> x4, Pallas kernels: 2.57 us -> 2.95 us  [the longest x1 1.19 us: body(): call(second_kernel, (shape(everyone, per * 8, 128), volume), [pool, pool,...]
  transfers between devices with their start and end apart: 6 -> 6, of which waited for: 2 -> 3; matrix products, arithmetic and copies ran while one was open for 0% -> 0% of each run, Pallas kernels for 7% -> 6%
where the time goes in v16:
time: 45 us; the launch traced here: 44.7 us
  starting transfers between devices  20.2 us (45%)
  blocking collectives  10.9 us (24%)
  Pallas kernels  7.78 us (17%)
  waiting for transfers between devices  5.07 us (11%)
  between operations  0.78 us (2%)
    all_to_all x1, blocking collectives, body(): parts = lax.all_to_all(sums, axes, split_axis=0, concat_axis=0, tiled=True)  10.9 us
    ppermute x4, starting transfers between devices, swapped(): lax.ppermute(value, 'space', pairs + [(target, source) for source, target...  10.3 us
    all_to_all x1, starting transfers between devices, body(): lax.all_to_all(packed, axes if scenes == 2 else 'space', split_axis=0, co...  7.3 us
    all_to_all x1, waiting for transfers between devices, body(): lax.all_to_all(packed, axes if scenes == 2 else 'space', split_axis=0, co...  2.91 us
    all_to_all x1, starting transfers between devices, body(): lax.all_to_all(total, axes, split_axis=0, concat_axis=0, tiled=True)  2.58 us
    pallas_call x1, Pallas kernels, body(): call(functools.partial(pick_kernel, scenes), shape(devices * scenes, 3 *...  1.74 us
    ppermute x4, waiting for transfers between devices, swapped(): lax.ppermute(value, 'space', pairs + [(target, source) for source, target...  1.73 us
    pallas_call x1, Pallas kernels, body(): call(first_kernel, (shape(ROWS, HALF, dtype=F32), volume, shape(HALF, ROW...  1.22 us
  transfers between devices with their start and end apart: 6, of which 3 were waited for; matrix products, arithmetic and copies ran while one was open for 0% of the time, Pallas kernels for 6%

profile of v16, /device:TPU:0, one launch (start us, length us, event | category | flops | bytes accessed | tf_op | source)
XLA Modules:
  0.0 44.7 jit_solution(12262634049251182701)
XLA Ops:
  0.6 1.7 %shard_map.95 = bf16[32,24,128]{2,1,0:T(8,128)(2,1)} custom-call(s32[1,32]{1,0:T(1,128)} %ids_hbm.1, bf16[1,64,512]{2,1,0:T(8,128)(2,1)} %latents_hbm.1), custom_call_target="tpu_custom_call" | custom-call | tf_op jit(solution)/shard_map/pallas_call | solution.py:440
  2.4 0.0 copy-start
  2.4 0.0 copy-start.4
  2.4 7.3 %all-to-all-start = ((bf16[32,24,128]{2,1,0:T(8,128)(2,1)}), bf16[32,24,128]{2,1,0:T(8,128)(2,1)S(1)}, u32[]{:S(2)}, u32[]{:S(2)}) async-start(bf16[32,24,128]{2,1,0:T(8,128)(2,1)} %shard_map.95), calls=%async_computation | async-start | bytes 393216 | tf_op jit(solution)/shard_map/all_to_all | solution.py:454
  9.7 0.1 shard_map.97
  9.8 0.7 %collective-permute-start = (bf16[48,256]{1,0:T(8,128)(2,1)S(1)}, bf16[48,256]{1,0:T(8,128)(2,1)S(1)}, u32[]{:S(2)}, u32[]{:S(2)}) collective-permute-start(bf16[48,256]{1,0:T(8,128)(2,1)S(1)} %get-tuple-element.31), channel_id=1, source_target_pairs={{2,4},{6,8},{10,12},{14,16},{18,20},{22,24},{26,28},{4,2},{8,6},{1... | collective-permute-start | bytes 73736 | tf_op jit(solution)/shard_map/ppermute | solution.py:430
  10.5 0.0 copy-start.1
  10.5 0.0 copy-start.2
  10.5 4.5 %collective-permute-start.1 = (bf16[48,256]{1,0:T(8,128)(2,1)S(1)}, bf16[48,256]{1,0:T(8,128)(2,1)S(1)}, u32[]{:S(2)}, u32[]{:S(2)}) collective-permute-start(bf16[48,256]{1,0:T(8,128)(2,1)S(1)} %get-tuple-element.32), channel_id=1, source_target_pairs={{0,2},{4,6},{8,10},{12,14},{16,18},{20,22},{24,26},{28,30},{2,0},{... | collective-permute-start | bytes 73736 | tf_op jit(solution)/shard_map/ppermute | solution.py:430
  15.1 0.6 %shard_map.94 = (bf16[9,256,128]{2,1,0:T(8,128)(2,1)S(1)}, f32[48,128]{1,0:T(8,128)S(1)}) custom-call(s32[1,2,6]{2,1,0:T(2,128)S(1)} %copy-done.3, bf16[27,32,32]{2,1,0:T(8,128)(2,1)S(1)} %copy-done.4), custom_call_target="tpu_custom_call" | custom-call | flops 1000000000 | bytes 2000000 | tf_op jit(solution)/shard_map/pallas_call | solution.py:468
  15.7 2.9 %all-to-all-done.received_ref = bf16[32,24,128]{2,1,0:T(8,128)(2,1)S(1)} async-done(((bf16[32,24,128]{2,1,0:T(8,128)(2,1)}), bf16[32,24,128]{2,1,0:T(8,128)(2,1)S(1)}, u32[]{:S(2)}, u32[]{:S(2)}) %all-to-all-start) | async-done | bytes 196640 | tf_op jit(solution)/shard_map/all_to_all | solution.py:454
  18.6 1.2 %shard_map.96 = (f32[256,128]{1,0:T(8,128)S(1)}, bf16[256,128]{1,0:T(8,128)(2,1)S(1)}, bf16[128,256]{1,0:T(8,128)(2,1)S(1)}, bf16[3,2,10,16,256]{4,3,2,1,0:T(8,128)(2,1)S(1)}, bf16[9,256,128]{2,1,0:T(8,128)(2,1)S(1)}) custom-call(s32[1,2,6]{2,1,0:T(2,128)S(1)} %copy-done.3, bf16[32,24,128]{2,1,0:T(8,128)(2,1)S(1)} %all-to-all-done.received_ref, ...), custom_call_target="tpu_custom_call" | custom-call | tf_op jit(solution)/shard_map/pallas_call | solution.py:471
  19.9 1.2 %shard_map.98 = (bf16[32,16,128]{2,1,0:T(8,128)(2,1)S(1)}, bf16[256,128]{1,0:T(8,128)(2,1)S(1)}) custom-call(f32[48,128]{1,0:T(8,128)S(1)} %get-tuple-element.23.masks_ref, bf16[1,2,8,8,256]{4,3,2,1,0:T(8,128)(2,1)S(1)} %copy-done, bf16[9,256,128]{2,1,0:T(8,128)(2,1)S(1)} %get-tuple-element.25.band_ref, f32[256,128]{1,0:T(8,128)S(1)} %get-tuple-element.26.slope_ref, ...), custom_call_target="tpu_custom_call" | custom-call | tf_op jit(solution)/shard_map/pallas_call | solution.py:482
  21.1 10.9 %all_to_all.15.parts_ref._parts = bf16[32,16,128]{2,1,0:T(8,128)(2,1)S(1)} all-to-all(bf16[32,16,128]{2,1,0:T(8,128)(2,1)S(1)} %get-tuple-element.33), channel_id=1, replica_groups=mesh['space'=16,'dp'=2] {'space','dp'}, dimensions={0} | all-to-all | bytes 262144 | tf_op jit(solution)/shard_map/all_to_all | solution.py:488
  31.9 0.9 %shard_map.99 = bf16[32,16,128]{2,1,0:T(8,128)(2,1)} custom-call(bf16[32,16,128]{2,1,0:T(8,128)(2,1)S(1)} %all_to_all.15.parts_ref._parts), custom_call_target="tpu_custom_call" | custom-call | tf_op jit(solution)/shard_map/pallas_call | solution.py:499
  32.8 2.6 %all-to-all-start.2 = ((bf16[32,16,128]{2,1,0:T(8,128)(2,1)}), bf16[32,16,128]{2,1,0:T(8,128)(2,1)S(1)}, u32[]{:S(2)}, u32[]{:S(2)}) async-start(bf16[32,16,128]{2,1,0:T(8,128)(2,1)} %shard_map.99), calls=%async_computation.2 | async-start | bytes 262144 | tf_op jit(solution)/shard_map/all_to_all | solution.py:500
  35.4 0.1 shard_map.101
  35.5 0.7 %collective-permute-start.2 = (bf16[48,256]{1,0:T(8,128)(2,1)S(1)}, bf16[48,256]{1,0:T(8,128)(2,1)S(1)}, u32[]{:S(2)}, u32[]{:S(2)}) collective-permute-start(bf16[48,256]{1,0:T(8,128)(2,1)S(1)} %get-tuple-element.38), channel_id=1, source_target_pairs={{2,4},{6,8},{10,12},{14,16},{18,20},{22,24},{26,28},{4,2},{8,6},{1... | collective-permute-start | bytes 73736 | tf_op jit(solution)/shard_map/ppermute | solution.py:430
  36.2 4.4 %collective-permute-start.3 = (bf16[48,256]{1,0:T(8,128)(2,1)S(1)}, bf16[48,256]{1,0:T(8,128)(2,1)S(1)}, u32[]{:S(2)}, u32[]{:S(2)}) collective-permute-start(bf16[48,256]{1,0:T(8,128)(2,1)S(1)} %get-tuple-element.39), channel_id=1, source_target_pairs={{0,2},{4,6},{8,10},{12,14},{16,18},{20,22},{24,26},{28,30},{2,0},{... | collective-permute-start | bytes 73736 | tf_op jit(solution)/shard_map/ppermute | solution.py:430
  40.6 0.3 shard_map.100.band_ref
  41.0 1.7 %collective-permute-done.3.near = bf16[48,256]{1,0:T(8,128)(2,1)S(1)} collective-permute-done((bf16[48,256]{1,0:T(8,128)(2,1)S(1)}, bf16[48,256]{1,0:T(8,128)(2,1)S(1)}, u32[]{:S(2)}, u32[]{:S(2)}) %collective-permute-start.3) | collective-permute-done | bytes 24608 | tf_op jit(solution)/shard_map/ppermute | solution.py:430
  42.7 0.5 %shard_map.102.fine_ref = bf16[1,2,8,8,256]{4,3,2,1,0:T(8,128)(2,1)S(1)} custom-call(f32[48,128]{1,0:T(8,128)S(1)} %get-tuple-element.23.masks_ref, bf16[9,256,128]{2,1,0:T(8,128)(2,1)S(1)} %shard_map.100.band_ref, bf16[256,128]{1,0:T(8,128)(2,1)S(1)} %get-tuple-element.34.lifted_ref, bf16[256,128]{1,0:T(8,128)(2,1)S(1)} %get-tuple-element.35.hidden_ref, ...), custom_call_target="tpu_custom_call" | custom-call | flops 1000000000 | bytes 2000000 | tf_op jit(solution)/shard_map/pallas_call | solution.py:495
  43.2 0.4 all-to-all-done.2.sums_ref
  43.7 1.1 %shard_map.103 = (f32[27,32,32]{2,1,0:T(8,128)}, f32[27,32,32]{2,1,0:T(8,128)}, bf16[1,2,8,8,256]{4,3,2,1,0:T(8,128)(2,1)}) custom-call(bf16[32,16,128]{2,1,0:T(8,128)(2,1)S(1)} %all-to-all-done.2.sums_ref, bf16[1,2,8,8,256]{4,3,2,1,0:T(8,128)(2,1)S(1)} %shard_map.102.fine_ref), custom_call_target="tpu_custom_call" | custom-call | tf_op jit(solution)/shard_map/pallas_call | solution.py:505
  (9 shorter events, 0.0 us)
Async XLA Ops:
  2.4 7.3 %copy-start = (bf16[1,2,8,8,256]{4,3,2,1,0:T(8,128)(2,1)S(1)}, bf16[1,2,8,8,256]{4,3,2,1,0:T(8,128)(2,1)}, u32[]{:S(2)}) copy-start(bf16[1,2,8,8,256]{4,3,2,1,0:T(8,128)(2,1)} %cotangent_ref.3) | copy-start | bytes 196612
  2.4 12.7 %copy-start.4 = (bf16[27,32,32]{2,1,0:T(8,128)(2,1)S(1)}, bf16[27,32,32]{2,1,0:T(8,128)(2,1)}, u32[]{:S(2)}) copy-start(bf16[27,32,32]{2,1,0:T(8,128)(2,1)} %weights_ref.3) | copy-start | bytes 165892
  2.4 16.2 %all-to-all-start = ((bf16[32,24,128]{2,1,0:T(8,128)(2,1)}), bf16[32,24,128]{2,1,0:T(8,128)(2,1)S(1)}, u32[]{:S(2)}, u32[]{:S(2)}) async-start(bf16[32,24,128]{2,1,0:T(8,128)(2,1)} %shard_map.95), calls=%async_computation | async-start | bytes 393216 | tf_op jit(solution)/shard_map/all_to_all | solution.py:454
  9.8 5.3 %copy-start.3 = (s32[1,2,6]{2,1,0:T(2,128)S(1)}, s32[1,2,6]{2,1,0:T(2,128)}, u32[]{:S(2)}) copy-start(s32[1,2,6]{2,1,0:T(2,128)} %links_in.3) | copy-start | bytes 148
  9.8 10.0 %collective-permute-start = (bf16[48,256]{1,0:T(8,128)(2,1)S(1)}, bf16[48,256]{1,0:T(8,128)(2,1)S(1)}, u32[]{:S(2)}, u32[]{:S(2)}) collective-permute-start(bf16[48,256]{1,0:T(8,128)(2,1)S(1)} %get-tuple-element.31), channel_id=1, source_target_pairs={{2,4},{6,8},{10,12},{14,16},{18,20},{22,24},{26,28},{4,2},{8,6},{1... | collective-permute-start | bytes 73736 | tf_op jit(solution)/shard_map/ppermute | solution.py:430
  10.5 8.1 %copy-start.1 = (bf16[64,2048]{1,0:T(8,128)(2,1)S(1)}, bf16[64,2048]{1,0:T(8,128)(2,1)}, u32[]{:S(2)}) copy-start(bf16[64,2048]{1,0:T(8,128)(2,1)} %up_ref.1) | copy-start | bytes 786436
  10.5 8.1 %copy-start.2 = (bf16[27,32,32]{2,1,0:T(8,128)(2,1)S(1)}, bf16[27,32,32]{2,1,0:T(8,128)(2,1)}, u32[]{:S(2)}) copy-start(bf16[27,32,32]{2,1,0:T(8,128)(2,1)} %weights_ref.5) | copy-start | bytes 165892
  10.5 9.3 %collective-permute-start.1 = (bf16[48,256]{1,0:T(8,128)(2,1)S(1)}, bf16[48,256]{1,0:T(8,128)(2,1)S(1)}, u32[]{:S(2)}, u32[]{:S(2)}) collective-permute-start(bf16[48,256]{1,0:T(8,128)(2,1)S(1)} %get-tuple-element.32), channel_id=1, source_target_pairs={{0,2},{4,6},{8,10},{12,14},{16,18},{20,22},{24,26},{28,30},{2,0},{... | collective-permute-start | bytes 73736 | tf_op jit(solution)/shard_map/ppermute | solution.py:430
  32.8 10.8 %all-to-all-start.2 = ((bf16[32,16,128]{2,1,0:T(8,128)(2,1)}), bf16[32,16,128]{2,1,0:T(8,128)(2,1)S(1)}, u32[]{:S(2)}, u32[]{:S(2)}) async-start(bf16[32,16,128]{2,1,0:T(8,128)(2,1)} %shard_map.99), calls=%async_computation.2 | async-start | bytes 262144 | tf_op jit(solution)/shard_map/all_to_all | solution.py:500
  35.5 5.4 %collective-permute-start.2 = (bf16[48,256]{1,0:T(8,128)(2,1)S(1)}, bf16[48,256]{1,0:T(8,128)(2,1)S(1)}, u32[]{:S(2)}, u32[]{:S(2)}) collective-permute-start(bf16[48,256]{1,0:T(8,128)(2,1)S(1)} %get-tuple-element.38), channel_id=1, source_target_pairs={{2,4},{6,8},{10,12},{14,16},{18,20},{22,24},{26,28},{4,2},{8,6},{1... | collective-permute-start | bytes 73736 | tf_op jit(solution)/shard_map/ppermute | solution.py:430
  36.2 6.5 %collective-permute-start.3 = (bf16[48,256]{1,0:T(8,128)(2,1)S(1)}, bf16[48,256]{1,0:T(8,128)(2,1)S(1)}, u32[]{:S(2)}, u32[]{:S(2)}) collective-permute-start(bf16[48,256]{1,0:T(8,128)(2,1)S(1)} %get-tuple-element.39), channel_id=1, source_target_pairs={{0,2},{4,6},{8,10},{12,14},{16,18},{20,22},{24,26},{28,30},{2,0},{... | collective-permute-start | bytes 73736 | tf_op jit(solution)/shard_map/ppermute | solution.py:430

commit v17 on v16

--- a/solution.py
+++ b/solution.py
@@ -355,7 +355,7 @@
             sums_ref[start : start + 8] = fold(one, diagonal(part - 1))
             start += 8 * 27
             sums_ref[start : start + 8] = fold(two, diagonal(1 - part))
-    sums_out[...] = sums_ref[...].astype(BF16).reshape(sums_out.shape)
+    sums_out[...] = sums_ref[...].astype(BF16)
 
 
 def fine_kernel(
@@ -370,38 +370,53 @@
     fine_out[...] = fine.astype(BF16).reshape(fine_out.shape)
 
 
+def sum_kernel(devices, scale, parts_ref, out_ref, rows_ref):
+    rows_ref[...] = parts_ref[...].astype(F32)
+    share = rows_ref.shape[0] // devices
+    pieces = [rows_ref[share * i : share * i + share] for i in range(devices)]
+    while len(pieces) > 1:
+        pairs = [a + b for a, b in zip(pieces[::2], pieces[1::2])]
+        pieces = pairs + pieces[len(pieces) - len(pieces) % 2 :]
+    total = pieces[0] * scale
+    for i in range(devices):
+        rows_ref[share * i : share * i + share] = total
+    out_ref[...] = rows_ref[...].astype(BF16)
+
+
 def unpacked(tile):
     pieces = [tile] + [pltpu.roll(tile, 128 - q * CHANNELS, 1) for q in range(1, 4)]
     return jnp.concatenate(pieces, axis=0)[:, :CHANNELS]
 
 
-def sum_kernel(scale, parts_ref, out_ref):
-    total = jnp.sum(parts_ref[...].astype(F32), axis=0) * scale
-    per = parts_ref.shape[1] // 8
-    device = lax.axis_index("space") * lax.axis_size("dp") + lax.axis_index("dp")
-    tiles = []
-    for j in range(per):
-        tile = total[8 * j : 8 * j + 8]
-        block = jnp.transpose(unpacked(tile))
-        turned = jnp.concatenate([block[8 * q : 8 * q + 8] for q in range(4)], axis=1)
-        tiles.append(jnp.where(device * per + j < 27, turned, tile))
-    total = jnp.concatenate(tiles, axis=0)
-    out_ref[...] = jnp.broadcast_to(total.astype(BF16)[None], out_ref.shape)
+def turned(tiles):
+    lane = lanes_of((8, 128)) // CHANNELS
+    rows = []
+    for q in range(4):
+        mixed = jnp.zeros((8, 128), F32)
+        for n, tile in enumerate(tiles):
+            shift = (n - q) % 4 * CHANNELS
+            mixed = jnp.where(lane == n, pltpu.roll(tile, shift, 1) if shift else tile, mixed)
+        rows.append(mixed)
+    return jnp.transpose(jnp.concatenate(rows, axis=0))
 
 
 def unpack_kernel(sums_ref, fine_ref, one_out, two_out, fine_out, rows_ref, one_ref, two_ref, sems, fine_sem):
     fine_copy = pltpu.make_async_copy(fine_ref, fine_out, fine_sem)
     fine_copy.start()
-    rows_ref[...] = sums_ref[...].astype(F32).reshape(rows_ref.shape)
+    rows_ref[...] = sums_ref[...].astype(F32)
+    tiles = [rows_ref[8 * index : 8 * index + 8] for index in range(BLOCKS)]
     copies = []
     for which, (block_ref, out) in enumerate(((one_ref, one_out), (two_ref, two_out))):
-        for third in range(3):
-            first = 9 * third
-            for index in range(first, first + 9):
-                row = 8 * (27 * which + index)
-                block_ref[index] = unpacked(rows_ref[row : row + 8])
-            part = pl.ds(first, 9)
-            copies.append(pltpu.make_async_copy(block_ref.at[part], out.at[part], sems.at[which, third]))
+        for part, (first, last) in enumerate(((0, 8), (8, 16), (16, 27))):
+            for index in range(first, last):
+                if which:
+                    block_ref[index] = unpacked(tiles[27 + index])
+                elif index % 4 == 0:
+                    blocks = turned(tiles[index : min(index + 4, 27)])
+                    for n in range(min(4, 27 - index)):
+                        block_ref[index + n] = blocks[CHANNELS * n : CHANNELS * n + CHANNELS]
+            span = pl.ds(first, last - first)
+            copies.append(pltpu.make_async_copy(block_ref.at[span], out.at[span], sems.at[which, part]))
             copies[-1].start()
     for copy in copies:
         copy.wait()
@@ -428,6 +443,13 @@
 def swapped(value, first):
     pairs = [(i, i + 1) for i in range(first, lax.axis_size("space") - 1, 2)]
     return lax.ppermute(value, "space", pairs + [(target, source) for source, target in pairs])
+
+
+def exchanged(rows):
+    everyone = lax.axis_size("space") * lax.axis_size("dp")
+    shares = rows.reshape(everyone, -1, 2, 128)
+    shares = lax.all_to_all(shares, ("space", "dp"), split_axis=0, concat_axis=0, tiled=True)
+    return shares.reshape(rows.shape)
 
 
 def body(coarse_latents, active_blocks, face_links, cotangent, up_weight, conv_one, conv_two):
@@ -477,15 +499,15 @@
         hbm=(0,),
         inputs=5,
     )(face_links, received, up_weight, band_one, conv_two)
-    per = -(-BLOCKS // everyone)
-    per += per % 2
+    share = 2 * -(-4 * BLOCKS // everyone)
+    packed_rows = (everyone * share, 128)
     sums, lifted = call(
         second_kernel,
-        (shape(everyone, per * 8, 128), volume),
-        [pool, pool, pad, pltpu.VMEM((everyone * per * 8, 128), F32)],
+        (shape(*packed_rows), volume),
+        [pool, pool, pad, pltpu.VMEM(packed_rows, F32)],
         inputs=10,
     )(masks, cotangent, band_back, slope, turned, lifted_pad, high, low, far, near)
-    parts = lax.all_to_all(sums, axes, split_axis=0, concat_axis=0, tiled=True)
+    parts = exchanged(sums)
     hidden_high, hidden_low, hidden_far, hidden_near = call(
         hidden_faces_kernel, (face,) * 4, [halves, faces], hbm=(1,), inputs=2
     )(hidden, parts)
@@ -496,11 +518,13 @@
         masks, band_two, lifted, hidden, hidden_high, hidden_low, hidden_far, hidden_near
     )
     scale = 1.0 / math.sqrt(lax.axis_size("dp") * devices * BRICKS * EDGE**3)
-    total = call(functools.partial(sum_kernel, scale), shape(*sums.shape))(parts)
-    gathered = lax.all_to_all(total, axes, split_axis=0, concat_axis=0, tiled=True)
+    total = call(
+        functools.partial(sum_kernel, everyone, scale), shape(*packed_rows), [pltpu.VMEM(packed_rows, F32)]
+    )(parts)
+    gathered = exchanged(total)
     grads = shape(27, CHANNELS, CHANNELS, dtype=F32)
     block = pltpu.VMEM(grads.shape, F32)
-    scratch = [pltpu.VMEM((everyone * per * 8, 128), F32), block, block]
+    scratch = [pltpu.VMEM(packed_rows, F32), block, block]
     scratch += [pltpu.SemaphoreType.DMA((2, 3)), pltpu.SemaphoreType.DMA]
     grad_one, grad_two, fine = call(
         unpack_kernel, (grads, grads, shape(*fine.shape)), scratch, inputs=2, out=pl.ANY

time: 45 us -> 44.6 us (level)
  transfers between devices with their start and end apart: 6 -> 6, of which waited for: 3 -> 3; matrix products, arithmetic and copies ran while one was open for 0% -> 0% of each run, Pallas kernels for 6% -> 7%
where the time goes in v17:
time: 44.6 us; the launch traced here: 44.3 us
  starting transfers between devices  20.2 us (45%)
  blocking collectives  10.7 us (24%)
  Pallas kernels  7.76 us (17%)
  waiting for transfers between devices  4.85 us (11%)
  between operations  0.78 us (2%)
    all_to_all x1, blocking collectives, exchanged(): lax.all_to_all(shares, ('space', 'dp'), split_axis=0, concat_axis=0, tile...  10.7 us
    ppermute x4, starting transfers between devices, swapped(): lax.ppermute(value, 'space', pairs + [(target, source) for source, target...  10.3 us
    all_to_all x1, starting transfers between devices, body(): lax.all_to_all(packed, axes if scenes == 2 else 'space', split_axis=0, co...  7.3 us
    all_to_all x1, waiting for transfers between devices, body(): lax.all_to_all(packed, axes if scenes == 2 else 'space', split_axis=0, co...  2.91 us
    all_to_all x1, starting transfers between devices, exchanged(): lax.all_to_all(shares, ('space', 'dp'), split_axis=0, concat_axis=0, tile...  2.57 us
    pallas_call x1, Pallas kernels, body(): call(functools.partial(pick_kernel, scenes), shape(devices * scenes, 3 *...  1.74 us
    ppermute x4, waiting for transfers between devices, swapped(): lax.ppermute(value, 'space', pairs + [(target, source) for source, target...  1.71 us
    pallas_call x1, Pallas kernels, body(): call(unpack_kernel, (grads, grads, shape(*fine.shape)), scratch, inputs=2...  1.24 us
  transfers between devices with their start and end apart: 6, of which 3 were waited for; matrix products, arithmetic and copies ran while one was open for 0% of the time, Pallas kernels for 7%

profile of v17, /device:TPU:0, one launch (start us, length us, event | category | flops | bytes accessed | tf_op | source)
XLA Modules:
  0.0 44.3 jit_solution(14766940531498516716)
XLA Ops:
  0.6 1.7 %shard_map.95 = bf16[32,24,128]{2,1,0:T(8,128)(2,1)} custom-call(s32[1,32]{1,0:T(1,128)} %ids_hbm.1, bf16[1,64,512]{2,1,0:T(8,128)(2,1)} %latents_hbm.1), custom_call_target="tpu_custom_call" | custom-call | tf_op jit(solution)/shard_map/pallas_call | solution.py:462
  2.4 0.0 copy-start
  2.4 0.0 copy-start.4
  2.4 7.3 %all-to-all-start = ((bf16[32,24,128]{2,1,0:T(8,128)(2,1)}), bf16[32,24,128]{2,1,0:T(8,128)(2,1)S(1)}, u32[]{:S(2)}, u32[]{:S(2)}) async-start(bf16[32,24,128]{2,1,0:T(8,128)(2,1)} %shard_map.95), calls=%async_computation | async-start | bytes 393216 | tf_op jit(solution)/shard_map/all_to_all | solution.py:476
  9.7 0.1 shard_map.97
  9.8 0.0 copy-start.3
  9.8 0.7 %collective-permute-start = (bf16[48,256]{1,0:T(8,128)(2,1)S(1)}, bf16[48,256]{1,0:T(8,128)(2,1)S(1)}, u32[]{:S(2)}, u32[]{:S(2)}) collective-permute-start(bf16[48,256]{1,0:T(8,128)(2,1)S(1)} %get-tuple-element.31), channel_id=1, source_target_pairs={{2,4},{6,8},{10,12},{14,16},{18,20},{22,24},{26,28},{4,2},{8,6},{1... | collective-permute-start | bytes 73736 | tf_op jit(solution)/shard_map/ppermute | solution.py:445
  10.5 0.0 copy-start.1
  10.5 4.5 %collective-permute-start.1 = (bf16[48,256]{1,0:T(8,128)(2,1)S(1)}, bf16[48,256]{1,0:T(8,128)(2,1)S(1)}, u32[]{:S(2)}, u32[]{:S(2)}) collective-permute-start(bf16[48,256]{1,0:T(8,128)(2,1)S(1)} %get-tuple-element.32), channel_id=1, source_target_pairs={{0,2},{4,6},{8,10},{12,14},{16,18},{20,22},{24,26},{28,30},{2,0},{... | collective-permute-start | bytes 73736 | tf_op jit(solution)/shard_map/ppermute | solution.py:445
  15.1 0.6 %shard_map.94 = (bf16[9,256,128]{2,1,0:T(8,128)(2,1)S(1)}, f32[48,128]{1,0:T(8,128)S(1)}) custom-call(s32[1,2,6]{2,1,0:T(2,128)S(1)} %copy-done.3, bf16[27,32,32]{2,1,0:T(8,128)(2,1)S(1)} %copy-done.4), custom_call_target="tpu_custom_call" | custom-call | flops 1000000000 | bytes 2000000 | tf_op jit(solution)/shard_map/pallas_call | solution.py:490
  15.7 2.9 %all-to-all-done.received_ref = bf16[32,24,128]{2,1,0:T(8,128)(2,1)S(1)} async-done(((bf16[32,24,128]{2,1,0:T(8,128)(2,1)}), bf16[32,24,128]{2,1,0:T(8,128)(2,1)S(1)}, u32[]{:S(2)}, u32[]{:S(2)}) %all-to-all-start) | async-done | bytes 196640 | tf_op jit(solution)/shard_map/all_to_all | solution.py:476
  18.6 1.2 %shard_map.96 = (f32[256,128]{1,0:T(8,128)S(1)}, bf16[256,128]{1,0:T(8,128)(2,1)S(1)}, bf16[128,256]{1,0:T(8,128)(2,1)S(1)}, bf16[3,2,10,16,256]{4,3,2,1,0:T(8,128)(2,1)S(1)}, bf16[9,256,128]{2,1,0:T(8,128)(2,1)S(1)}) custom-call(s32[1,2,6]{2,1,0:T(2,128)S(1)} %copy-done.3, bf16[32,24,128]{2,1,0:T(8,128)(2,1)S(1)} %all-to-all-done.received_ref, ...), custom_call_target="tpu_custom_call" | custom-call | tf_op jit(solution)/shard_map/pallas_call | solution.py:493
  19.9 1.2 %shard_map.98 = (bf16[448,128]{1,0:T(8,128)(2,1)S(1)}, bf16[256,128]{1,0:T(8,128)(2,1)S(1)}) custom-call(f32[48,128]{1,0:T(8,128)S(1)} %get-tuple-element.23.masks_ref, bf16[1,2,8,8,256]{4,3,2,1,0:T(8,128)(2,1)S(1)} %copy-done, bf16[9,256,128]{2,1,0:T(8,128)(2,1)S(1)} %get-tuple-element.25.band_ref, f32[256,128]{1,0:T(8,128)S(1)} %get-tuple-element.26.slope_ref, ...), custom_call_target="tpu_custom_call" | custom-call | tf_op jit(solution)/shard_map/pallas_call | solution.py:504
  21.1 10.7 %all_to_all.15 = bf16[32,7,2,128]{3,2,1,0:T(2,128)(2,1)S(1)} all-to-all(bf16[32,7,2,128]{3,2,1,0:T(2,128)(2,1)S(1)} %bitcast.7), channel_id=1, replica_groups=mesh['space'=16,'dp'=2] {'space','dp'}, dimensions={0} | all-to-all | bytes 229376 | tf_op jit(solution)/shard_map/all_to_all | solution.py:451
  31.7 0.7 %shard_map.99 = bf16[448,128]{1,0:T(8,128)(2,1)} custom-call(bf16[448,128]{1,0:T(8,128)(2,1)S(1)} %bitcast.4), custom_call_target="tpu_custom_call" | custom-call | tf_op jit(solution)/shard_map/pallas_call | solution.py:521
  32.4 2.6 %all-to-all-start.2 = ((bf16[32,7,2,128]{3,2,1,0:T(2,128)(2,1)}), bf16[32,7,2,128]{3,2,1,0:T(2,128)(2,1)S(1)}, u32[]{:S(2)}, u32[]{:S(2)}) async-start(bf16[32,7,2,128]{3,2,1,0:T(2,128)(2,1)} %bitcast.2), calls=%async_computation.2 | async-start | bytes 229376 | tf_op jit(solution)/shard_map/all_to_all | solution.py:451
  35.0 0.1 shard_map.101
  35.1 0.7 %collective-permute-start.2 = (bf16[48,256]{1,0:T(8,128)(2,1)S(1)}, bf16[48,256]{1,0:T(8,128)(2,1)S(1)}, u32[]{:S(2)}, u32[]{:S(2)}) collective-permute-start(bf16[48,256]{1,0:T(8,128)(2,1)S(1)} %get-tuple-element.38), channel_id=1, source_target_pairs={{2,4},{6,8},{10,12},{14,16},{18,20},{22,24},{26,28},{4,2},{8,6},{1... | collective-permute-start | bytes 73736 | tf_op jit(solution)/shard_map/ppermute | solution.py:445
  35.8 4.4 %collective-permute-start.3 = (bf16[48,256]{1,0:T(8,128)(2,1)S(1)}, bf16[48,256]{1,0:T(8,128)(2,1)S(1)}, u32[]{:S(2)}, u32[]{:S(2)}) collective-permute-start(bf16[48,256]{1,0:T(8,128)(2,1)S(1)} %get-tuple-element.39), channel_id=1, source_target_pairs={{0,2},{4,6},{8,10},{12,14},{16,18},{20,22},{24,26},{28,30},{2,0},{... | collective-permute-start | bytes 73736 | tf_op jit(solution)/shard_map/ppermute | solution.py:445
  40.2 0.3 shard_map.100.band_ref
  40.6 1.7 %collective-permute-done.3.near = bf16[48,256]{1,0:T(8,128)(2,1)S(1)} collective-permute-done((bf16[48,256]{1,0:T(8,128)(2,1)S(1)}, bf16[48,256]{1,0:T(8,128)(2,1)S(1)}, u32[]{:S(2)}, u32[]{:S(2)}) %collective-permute-start.3) | collective-permute-done | bytes 24608 | tf_op jit(solution)/shard_map/ppermute | solution.py:445
  42.3 0.5 %shard_map.102.fine_ref = bf16[1,2,8,8,256]{4,3,2,1,0:T(8,128)(2,1)S(1)} custom-call(f32[48,128]{1,0:T(8,128)S(1)} %get-tuple-element.23.masks_ref, bf16[9,256,128]{2,1,0:T(8,128)(2,1)S(1)} %shard_map.100.band_ref, bf16[256,128]{1,0:T(8,128)(2,1)S(1)} %get-tuple-element.34.lifted_ref, bf16[256,128]{1,0:T(8,128)(2,1)S(1)} %get-tuple-element.35.hidden_ref, ...), custom_call_target="tpu_custom_call" | custom-call | flops 1000000000 | bytes 2000000 | tf_op jit(solution)/shard_map/pallas_call | solution.py:517
  42.8 0.2 all-to-all-done.2
  43.0 1.2 %shard_map.103 = (f32[27,32,32]{2,1,0:T(8,128)}, f32[27,32,32]{2,1,0:T(8,128)}, bf16[1,2,8,8,256]{4,3,2,1,0:T(8,128)(2,1)}) custom-call(bf16[448,128]{1,0:T(8,128)(2,1)S(1)} %bitcast.6, bf16[1,2,8,8,256]{4,3,2,1,0:T(8,128)(2,1)S(1)} %shard_map.102.fine_ref), custom_call_target="tpu_custom_call" | custom-call | tf_op jit(solution)/shard_map/pallas_call | solution.py:529
  (9 shorter events, 0.0 us)
Async XLA Ops:
  2.4 7.3 %copy-start = (bf16[1,2,8,8,256]{4,3,2,1,0:T(8,128)(2,1)S(1)}, bf16[1,2,8,8,256]{4,3,2,1,0:T(8,128)(2,1)}, u32[]{:S(2)}) copy-start(bf16[1,2,8,8,256]{4,3,2,1,0:T(8,128)(2,1)} %cotangent_ref.3) | copy-start | bytes 196612
  2.4 12.7 %copy-start.4 = (bf16[27,32,32]{2,1,0:T(8,128)(2,1)S(1)}, bf16[27,32,32]{2,1,0:T(8,128)(2,1)}, u32[]{:S(2)}) copy-start(bf16[27,32,32]{2,1,0:T(8,128)(2,1)} %weights_ref.3) | copy-start | bytes 165892
  2.4 16.2 %all-to-all-start = ((bf16[32,24,128]{2,1,0:T(8,128)(2,1)}), bf16[32,24,128]{2,1,0:T(8,128)(2,1)S(1)}, u32[]{:S(2)}, u32[]{:S(2)}) async-start(bf16[32,24,128]{2,1,0:T(8,128)(2,1)} %shard_map.95), calls=%async_computation | async-start | bytes 393216 | tf_op jit(solution)/shard_map/all_to_all | solution.py:476
  9.8 5.3 %copy-start.3 = (s32[1,2,6]{2,1,0:T(2,128)S(1)}, s32[1,2,6]{2,1,0:T(2,128)}, u32[]{:S(2)}) copy-start(s32[1,2,6]{2,1,0:T(2,128)} %links_in.3) | copy-start | bytes 148
  9.8 10.0 %collective-permute-start = (bf16[48,256]{1,0:T(8,128)(2,1)S(1)}, bf16[48,256]{1,0:T(8,128)(2,1)S(1)}, u32[]{:S(2)}, u32[]{:S(2)}) collective-permute-start(bf16[48,256]{1,0:T(8,128)(2,1)S(1)} %get-tuple-element.31), channel_id=1, source_target_pairs={{2,4},{6,8},{10,12},{14,16},{18,20},{22,24},{26,28},{4,2},{8,6},{1... | collective-permute-start | bytes 73736 | tf_op jit(solution)/shard_map/ppermute | solution.py:445
  10.5 8.1 %copy-start.1 = (bf16[64,2048]{1,0:T(8,128)(2,1)S(1)}, bf16[64,2048]{1,0:T(8,128)(2,1)}, u32[]{:S(2)}) copy-start(bf16[64,2048]{1,0:T(8,128)(2,1)} %up_ref.1) | copy-start | bytes 786436
  10.5 8.1 %copy-start.2 = (bf16[27,32,32]{2,1,0:T(8,128)(2,1)S(1)}, bf16[27,32,32]{2,1,0:T(8,128)(2,1)}, u32[]{:S(2)}) copy-start(bf16[27,32,32]{2,1,0:T(8,128)(2,1)} %weights_ref.5) | copy-start | bytes 165892
  10.5 9.3 %collective-permute-start.1 = (bf16[48,256]{1,0:T(8,128)(2,1)S(1)}, bf16[48,256]{1,0:T(8,128)(2,1)S(1)}, u32[]{:S(2)}, u32[]{:S(2)}) collective-permute-start(bf16[48,256]{1,0:T(8,128)(2,1)S(1)} %get-tuple-element.32), channel_id=1, source_target_pairs={{0,2},{4,6},{8,10},{12,14},{16,18},{20,22},{24,26},{28,30},{2,0},{... | collective-permute-start | bytes 73736 | tf_op jit(solution)/shard_map/ppermute | solution.py:445
  32.4 10.6 %all-to-all-start.2 = ((bf16[32,7,2,128]{3,2,1,0:T(2,128)(2,1)}), bf16[32,7,2,128]{3,2,1,0:T(2,128)(2,1)S(1)}, u32[]{:S(2)}, u32[]{:S(2)}) async-start(bf16[32,7,2,128]{3,2,1,0:T(2,128)(2,1)} %bitcast.2), calls=%async_computation.2 | async-start | bytes 229376 | tf_op jit(solution)/shard_map/all_to_all | solution.py:451
  35.1 5.4 %collective-permute-start.2 = (bf16[48,256]{1,0:T(8,128)(2,1)S(1)}, bf16[48,256]{1,0:T(8,128)(2,1)S(1)}, u32[]{:S(2)}, u32[]{:S(2)}) collective-permute-start(bf16[48,256]{1,0:T(8,128)(2,1)S(1)} %get-tuple-element.38), channel_id=1, source_target_pairs={{2,4},{6,8},{10,12},{14,16},{18,20},{22,24},{26,28},{4,2},{8,6},{1... | collective-permute-start | bytes 73736 | tf_op jit(solution)/shard_map/ppermute | solution.py:445
  35.8 6.5 %collective-permute-start.3 = (bf16[48,256]{1,0:T(8,128)(2,1)S(1)}, bf16[48,256]{1,0:T(8,128)(2,1)S(1)}, u32[]{:S(2)}, u32[]{:S(2)}) collective-permute-start(bf16[48,256]{1,0:T(8,128)(2,1)S(1)} %get-tuple-element.39), channel_id=1, source_target_pairs={{0,2},{4,6},{8,10},{12,14},{16,18},{20,22},{24,26},{28,30},{2,0},{... | collective-permute-start | bytes 73736 | tf_op jit(solution)/shard_map/ppermute | solution.py:445

commit v18 on v17

--- a/solution.py
+++ b/solution.py
@@ -135,11 +135,16 @@
 
 
 def convolve(pad_ref, band_ref):
-    total = None
-    for k in range(9):
-        term = dot(window(pad_ref, k), band_ref[k])
-        total = term if total is None else total + term
-    return total
+    both, last = None, None
+    for dy in range(3):
+        slabs = pad_ref[dy, :, : EDGE + 1].reshape(-1, WIDE)
+        term = dot(slabs, jnp.concatenate([band_ref[dy], band_ref[3 + dy]], axis=1))
+        both = term if both is None else both + term
+        term = dot(window(pad_ref, 6 + dy), band_ref[6 + dy])
+        last = term if last is None else last + term
+    both = both.reshape(BRICKS, EDGE + 1, 2 * EDGE, 2 * HALF)
+    total = both[:, :EDGE, :, :HALF] + both[:, 1:, :, HALF:]
+    return total.reshape(ROWS, HALF) + last
 
 
 def half_lines(values):
@@ -406,7 +411,7 @@
     rows_ref[...] = sums_ref[...].astype(F32)
     tiles = [rows_ref[8 * index : 8 * index + 8] for index in range(BLOCKS)]
     copies = []
-    for which, (block_ref, out) in enumerate(((one_ref, one_out), (two_ref, two_out))):
+    for which, (block_ref, out) in ((1, (two_ref, two_out)), (0, (one_ref, one_out))):
         for part, (first, last) in enumerate(((0, 8), (8, 16), (16, 27))):
             for index in range(first, last):
                 if which:

time: 44.6 us -> 44.3 us (level)
  transfers between devices with their start and end apart: 6 -> 6, of which waited for: 3 -> 3; matrix products, arithmetic and copies ran while one was open for 0% -> 0% of each run, Pallas kernels for 7% -> 6%
where the time goes in v18:
time: 44.3 us; the launch traced here: 44 us
  starting transfers between devices  20.2 us (46%)
  blocking collectives  10.7 us (24%)
  Pallas kernels  7.39 us (17%)
  waiting for transfers between devices  4.93 us (11%)
  between operations  0.78 us (2%)
    all_to_all x1, blocking collectives, exchanged(): lax.all_to_all(shares, ('space', 'dp'), split_axis=0, concat_axis=0, tile...  10.7 us
    ppermute x4, starting transfers between devices, swapped(): lax.ppermute(value, 'space', pairs + [(target, source) for source, target...  10.3 us
    all_to_all x1, starting transfers between devices, body(): lax.all_to_all(packed, axes if scenes == 2 else 'space', split_axis=0, co...  7.3 us
    all_to_all x1, waiting for transfers between devices, body(): lax.all_to_all(packed, axes if scenes == 2 else 'space', split_axis=0, co...  2.91 us
    all_to_all x1, starting transfers between devices, exchanged(): lax.all_to_all(shares, ('space', 'dp'), split_axis=0, concat_axis=0, tile...  2.57 us
    pallas_call x1, Pallas kernels, body(): call(functools.partial(pick_kernel, scenes), shape(devices * scenes, 3 *...  1.74 us
    ppermute x4, waiting for transfers between devices, swapped(): lax.ppermute(value, 'space', pairs + [(target, source) for source, target...  1.71 us
    pallas_call x1, Pallas kernels, body(): call(first_kernel, (shape(ROWS, HALF, dtype=F32), volume, shape(HALF, ROW...  1.16 us
  transfers between devices with their start and end apart: 6, of which 3 were waited for; matrix products, arithmetic and copies ran while one was open for 0% of the time, Pallas kernels for 6%

profile of v18, /device:TPU:0, one launch (start us, length us, event | category | flops | bytes accessed | tf_op | source)
XLA Modules:
  0.0 44.0 jit_solution(4466565815086516003)
XLA Ops:
  0.6 1.7 %shard_map.95 = bf16[32,24,128]{2,1,0:T(8,128)(2,1)} custom-call(s32[1,32]{1,0:T(1,128)} %ids_hbm.1, bf16[1,64,512]{2,1,0:T(8,128)(2,1)} %latents_hbm.1), custom_call_target="tpu_custom_call" | custom-call | tf_op jit(solution)/shard_map/pallas_call | solution.py:467
  2.4 0.0 copy-start
  2.4 0.0 copy-start.4
  2.4 7.3 %all-to-all-start = ((bf16[32,24,128]{2,1,0:T(8,128)(2,1)}), bf16[32,24,128]{2,1,0:T(8,128)(2,1)S(1)}, u32[]{:S(2)}, u32[]{:S(2)}) async-start(bf16[32,24,128]{2,1,0:T(8,128)(2,1)} %shard_map.95), calls=%async_computation | async-start | bytes 393216 | tf_op jit(solution)/shard_map/all_to_all | solution.py:481
  9.7 0.1 shard_map.97
  9.8 0.7 %collective-permute-start = (bf16[48,256]{1,0:T(8,128)(2,1)S(1)}, bf16[48,256]{1,0:T(8,128)(2,1)S(1)}, u32[]{:S(2)}, u32[]{:S(2)}) collective-permute-start(bf16[48,256]{1,0:T(8,128)(2,1)S(1)} %get-tuple-element.31), channel_id=1, source_target_pairs={{2,4},{6,8},{10,12},{14,16},{18,20},{22,24},{26,28},{4,2},{8,6},{1... | collective-permute-start | bytes 73736 | tf_op jit(solution)/shard_map/ppermute | solution.py:450
  10.5 0.0 copy-start.1
  10.5 0.0 copy-start.2
  10.5 4.5 %collective-permute-start.1 = (bf16[48,256]{1,0:T(8,128)(2,1)S(1)}, bf16[48,256]{1,0:T(8,128)(2,1)S(1)}, u32[]{:S(2)}, u32[]{:S(2)}) collective-permute-start(bf16[48,256]{1,0:T(8,128)(2,1)S(1)} %get-tuple-element.32), channel_id=1, source_target_pairs={{0,2},{4,6},{8,10},{12,14},{16,18},{20,22},{24,26},{28,30},{2,0},{... | collective-permute-start | bytes 73736 | tf_op jit(solution)/shard_map/ppermute | solution.py:450
  15.1 0.6 %shard_map.94 = (bf16[9,256,128]{2,1,0:T(8,128)(2,1)S(1)}, f32[48,128]{1,0:T(8,128)S(1)}) custom-call(s32[1,2,6]{2,1,0:T(2,128)S(1)} %copy-done.3, bf16[27,32,32]{2,1,0:T(8,128)(2,1)S(1)} %copy-done.4), custom_call_target="tpu_custom_call" | custom-call | flops 1000000000 | bytes 2000000 | tf_op jit(solution)/shard_map/pallas_call | solution.py:495
  15.7 2.9 %all-to-all-done.received_ref = bf16[32,24,128]{2,1,0:T(8,128)(2,1)S(1)} async-done(((bf16[32,24,128]{2,1,0:T(8,128)(2,1)}), bf16[32,24,128]{2,1,0:T(8,128)(2,1)S(1)}, u32[]{:S(2)}, u32[]{:S(2)}) %all-to-all-start) | async-done | bytes 196640 | tf_op jit(solution)/shard_map/all_to_all | solution.py:481
  18.6 1.2 %shard_map.96 = (f32[256,128]{1,0:T(8,128)S(1)}, bf16[256,128]{1,0:T(8,128)(2,1)S(1)}, bf16[128,256]{1,0:T(8,128)(2,1)S(1)}, bf16[3,2,10,16,256]{4,3,2,1,0:T(8,128)(2,1)S(1)}, bf16[9,256,128]{2,1,0:T(8,128)(2,1)S(1)}) custom-call(s32[1,2,6]{2,1,0:T(2,128)S(1)} %copy-done.3, bf16[32,24,128]{2,1,0:T(8,128)(2,1)S(1)} %all-to-all-done.received_ref, ...), custom_call_target="tpu_custom_call" | custom-call | tf_op jit(solution)/shard_map/pallas_call | solution.py:498
  19.8 1.1 %shard_map.98 = (bf16[448,128]{1,0:T(8,128)(2,1)S(1)}, bf16[256,128]{1,0:T(8,128)(2,1)S(1)}) custom-call(f32[48,128]{1,0:T(8,128)S(1)} %get-tuple-element.23.masks_ref, bf16[1,2,8,8,256]{4,3,2,1,0:T(8,128)(2,1)S(1)} %copy-done, bf16[9,256,128]{2,1,0:T(8,128)(2,1)S(1)} %get-tuple-element.25.band_ref, f32[256,128]{1,0:T(8,128)S(1)} %get-tuple-element.26.slope_ref, ...), custom_call_target="tpu_custom_call" | custom-call | tf_op jit(solution)/shard_map/pallas_call | solution.py:509
  20.9 10.7 %all_to_all.15 = bf16[32,7,2,128]{3,2,1,0:T(2,128)(2,1)S(1)} all-to-all(bf16[32,7,2,128]{3,2,1,0:T(2,128)(2,1)S(1)} %bitcast.7), channel_id=1, replica_groups=mesh['space'=16,'dp'=2] {'space','dp'}, dimensions={0} | all-to-all | bytes 229376 | tf_op jit(solution)/shard_map/all_to_all | solution.py:456
  31.6 0.7 %shard_map.99 = bf16[448,128]{1,0:T(8,128)(2,1)} custom-call(bf16[448,128]{1,0:T(8,128)(2,1)S(1)} %bitcast.4), custom_call_target="tpu_custom_call" | custom-call | tf_op jit(solution)/shard_map/pallas_call | solution.py:526
  32.3 2.6 %all-to-all-start.2 = ((bf16[32,7,2,128]{3,2,1,0:T(2,128)(2,1)}), bf16[32,7,2,128]{3,2,1,0:T(2,128)(2,1)S(1)}, u32[]{:S(2)}, u32[]{:S(2)}) async-start(bf16[32,7,2,128]{3,2,1,0:T(2,128)(2,1)} %bitcast.2), calls=%async_computation.2 | async-start | bytes 229376 | tf_op jit(solution)/shard_map/all_to_all | solution.py:456
  34.8 0.1 shard_map.101
  34.9 0.7 %collective-permute-start.2 = (bf16[48,256]{1,0:T(8,128)(2,1)S(1)}, bf16[48,256]{1,0:T(8,128)(2,1)S(1)}, u32[]{:S(2)}, u32[]{:S(2)}) collective-permute-start(bf16[48,256]{1,0:T(8,128)(2,1)S(1)} %get-tuple-element.38), channel_id=1, source_target_pairs={{2,4},{6,8},{10,12},{14,16},{18,20},{22,24},{26,28},{4,2},{8,6},{1... | collective-permute-start | bytes 73736 | tf_op jit(solution)/shard_map/ppermute | solution.py:450
  35.6 4.4 %collective-permute-start.3 = (bf16[48,256]{1,0:T(8,128)(2,1)S(1)}, bf16[48,256]{1,0:T(8,128)(2,1)S(1)}, u32[]{:S(2)}, u32[]{:S(2)}) collective-permute-start(bf16[48,256]{1,0:T(8,128)(2,1)S(1)} %get-tuple-element.39), channel_id=1, source_target_pairs={{0,2},{4,6},{8,10},{12,14},{16,18},{20,22},{24,26},{28,30},{2,0},{... | collective-permute-start | bytes 73736 | tf_op jit(solution)/shard_map/ppermute | solution.py:450
  40.0 0.3 shard_map.100.band_ref
  40.4 1.7 %collective-permute-done.3.near = bf16[48,256]{1,0:T(8,128)(2,1)S(1)} collective-permute-done((bf16[48,256]{1,0:T(8,128)(2,1)S(1)}, bf16[48,256]{1,0:T(8,128)(2,1)S(1)}, u32[]{:S(2)}, u32[]{:S(2)}) %collective-permute-start.3) | collective-permute-done | bytes 24608 | tf_op jit(solution)/shard_map/ppermute | solution.py:450
  42.1 0.5 %shard_map.102.fine_ref = bf16[1,2,8,8,256]{4,3,2,1,0:T(8,128)(2,1)S(1)} custom-call(f32[48,128]{1,0:T(8,128)S(1)} %get-tuple-element.23.masks_ref, bf16[9,256,128]{2,1,0:T(8,128)(2,1)S(1)} %shard_map.100.band_ref, bf16[256,128]{1,0:T(8,128)(2,1)S(1)} %get-tuple-element.34.lifted_ref, bf16[256,128]{1,0:T(8,128)(2,1)S(1)} %get-tuple-element.35.hidden_ref, ...), custom_call_target="tpu_custom_call" | custom-call | flops 1000000000 | bytes 2000000 | tf_op jit(solution)/shard_map/pallas_call | solution.py:522
  42.5 0.3 all-to-all-done.2
  42.9 1.1 %shard_map.103 = (f32[27,32,32]{2,1,0:T(8,128)}, f32[27,32,32]{2,1,0:T(8,128)}, bf16[1,2,8,8,256]{4,3,2,1,0:T(8,128)(2,1)}) custom-call(bf16[448,128]{1,0:T(8,128)(2,1)S(1)} %bitcast.6, bf16[1,2,8,8,256]{4,3,2,1,0:T(8,128)(2,1)S(1)} %shard_map.102.fine_ref), custom_call_target="tpu_custom_call" | custom-call | tf_op jit(solution)/shard_map/pallas_call | solution.py:534
  (9 shorter events, 0.0 us)
Async XLA Ops:
  2.4 7.3 %copy-start = (bf16[1,2,8,8,256]{4,3,2,1,0:T(8,128)(2,1)S(1)}, bf16[1,2,8,8,256]{4,3,2,1,0:T(8,128)(2,1)}, u32[]{:S(2)}) copy-start(bf16[1,2,8,8,256]{4,3,2,1,0:T(8,128)(2,1)} %cotangent_ref.3) | copy-start | bytes 196612
  2.4 12.7 %copy-start.4 = (bf16[27,32,32]{2,1,0:T(8,128)(2,1)S(1)}, bf16[27,32,32]{2,1,0:T(8,128)(2,1)}, u32[]{:S(2)}) copy-start(bf16[27,32,32]{2,1,0:T(8,128)(2,1)} %weights_ref.3) | copy-start | bytes 165892
  2.4 16.2 %all-to-all-start = ((bf16[32,24,128]{2,1,0:T(8,128)(2,1)}), bf16[32,24,128]{2,1,0:T(8,128)(2,1)S(1)}, u32[]{:S(2)}, u32[]{:S(2)}) async-start(bf16[32,24,128]{2,1,0:T(8,128)(2,1)} %shard_map.95), calls=%async_computation | async-start | bytes 393216 | tf_op jit(solution)/shard_map/all_to_all | solution.py:481
  9.8 5.3 %copy-start.3 = (s32[1,2,6]{2,1,0:T(2,128)S(1)}, s32[1,2,6]{2,1,0:T(2,128)}, u32[]{:S(2)}) copy-start(s32[1,2,6]{2,1,0:T(2,128)} %links_in.3) | copy-start | bytes 148
  9.8 10.0 %collective-permute-start = (bf16[48,256]{1,0:T(8,128)(2,1)S(1)}, bf16[48,256]{1,0:T(8,128)(2,1)S(1)}, u32[]{:S(2)}, u32[]{:S(2)}) collective-permute-start(bf16[48,256]{1,0:T(8,128)(2,1)S(1)} %get-tuple-element.31), channel_id=1, source_target_pairs={{2,4},{6,8},{10,12},{14,16},{18,20},{22,24},{26,28},{4,2},{8,6},{1... | collective-permute-start | bytes 73736 | tf_op jit(solution)/shard_map/ppermute | solution.py:450
  10.5 8.1 %copy-start.1 = (bf16[64,2048]{1,0:T(8,128)(2,1)S(1)}, bf16[64,2048]{1,0:T(8,128)(2,1)}, u32[]{:S(2)}) copy-start(bf16[64,2048]{1,0:T(8,128)(2,1)} %up_ref.1) | copy-start | bytes 786436
  10.5 8.1 %copy-start.2 = (bf16[27,32,32]{2,1,0:T(8,128)(2,1)S(1)}, bf16[27,32,32]{2,1,0:T(8,128)(2,1)}, u32[]{:S(2)}) copy-start(bf16[27,32,32]{2,1,0:T(8,128)(2,1)} %weights_ref.5) | copy-start | bytes 165892
  10.5 9.3 %collective-permute-start.1 = (bf16[48,256]{1,0:T(8,128)(2,1)S(1)}, bf16[48,256]{1,0:T(8,128)(2,1)S(1)}, u32[]{:S(2)}, u32[]{:S(2)}) collective-permute-start(bf16[48,256]{1,0:T(8,128)(2,1)S(1)} %get-tuple-element.32), channel_id=1, source_target_pairs={{0,2},{4,6},{8,10},{12,14},{16,18},{20,22},{24,26},{28,30},{2,0},{... | collective-permute-start | bytes 73736 | tf_op jit(solution)/shard_map/ppermute | solution.py:450
  32.3 10.6 %all-to-all-start.2 = ((bf16[32,7,2,128]{3,2,1,0:T(2,128)(2,1)}), bf16[32,7,2,128]{3,2,1,0:T(2,128)(2,1)S(1)}, u32[]{:S(2)}, u32[]{:S(2)}) async-start(bf16[32,7,2,128]{3,2,1,0:T(2,128)(2,1)} %bitcast.2), calls=%async_computation.2 | async-start | bytes 229376 | tf_op jit(solution)/shard_map/all_to_all | solution.py:456
  34.9 5.4 %collective-permute-start.2 = (bf16[48,256]{1,0:T(8,128)(2,1)S(1)}, bf16[48,256]{1,0:T(8,128)(2,1)S(1)}, u32[]{:S(2)}, u32[]{:S(2)}) collective-permute-start(bf16[48,256]{1,0:T(8,128)(2,1)S(1)} %get-tuple-element.38), channel_id=1, source_target_pairs={{2,4},{6,8},{10,12},{14,16},{18,20},{22,24},{26,28},{4,2},{8,6},{1... | collective-permute-start | bytes 73736 | tf_op jit(solution)/shard_map/ppermute | solution.py:450
  35.6 6.5 %collective-permute-start.3 = (bf16[48,256]{1,0:T(8,128)(2,1)S(1)}, bf16[48,256]{1,0:T(8,128)(2,1)S(1)}, u32[]{:S(2)}, u32[]{:S(2)}) collective-permute-start(bf16[48,256]{1,0:T(8,128)(2,1)S(1)} %get-tuple-element.39), channel_id=1, source_target_pairs={{0,2},{4,6},{8,10},{12,14},{16,18},{20,22},{24,26},{28,30},{2,0},{... | collective-permute-start | bytes 73736 | tf_op jit(solution)/shard_map/ppermute | solution.py:450

commit v19 on v18

--- a/solution.py
+++ b/solution.py
@@ -41,12 +41,25 @@
     return lax.broadcasted_iota(jnp.int32, shape, len(shape) - 1)
 
 
-def pick_kernel(scenes, ids_hbm, latents_hbm, out_ref, ids_ref, latents_ref, rows_ref, sems):
+def scene_of(blocks_ref):
+    return lax.axis_index("dp") if blocks_ref.shape[1] > 1 else 0
+
+
+def pick_kernel(ids_hbm, latents_hbm, out_hbm, ids_ref, latents_ref, rows_ref, blocks_ref, zeros_ref, sems):
     ids_copy = pltpu.make_async_copy(ids_hbm, ids_ref, sems.at[0])
-    latents_copy = pltpu.make_async_copy(latents_hbm, latents_ref, sems.at[1])
     ids_copy.start()
-    latents_copy.start()
     held, width = latents_ref.shape[1:]
+    copies = []
+    for i in range(4):
+        part = pl.ds(i * held // 4, held // 4)
+        copies.append(pltpu.make_async_copy(latents_hbm.at[0, part], latents_ref.at[0, part], sems.at[1 + i]))
+        copies[-1].start()
+    scene = scene_of(out_hbm)
+    others = None
+    if out_hbm.shape[1] > 1:
+        zeros_ref[...] = jnp.zeros(zeros_ref.shape, BF16)
+        others = pltpu.make_async_copy(zeros_ref, out_hbm.at[:, 1 - scene], sems.at[5])
+        others.start()
     bricks = ids_ref.shape[1]
     margin = 8 * width // 128
     tiles = width // 128
@@ -56,18 +69,20 @@
     rows = lax.broadcasted_iota(jnp.int32, (held, bricks), 0) + first
     ids_copy.wait()
     hot = jnp.where(rows == ids_ref[...], 1.0, 0.0).astype(BF16)
-    latents_copy.wait()
+    for copy in copies:
+        copy.wait()
     picked = dot_rows(hot, latents_ref[0])
     for tile in range(tiles):
         rows_ref[pl.ds(margin + tile, bricks, stride=tiles), :] = picked[:, tile * 128 : tile * 128 + 128]
-    count = out_ref.shape[1]
-    wanted = [jnp.where(lax.axis_index("dp") == scene, 1.0, 0.0).astype(F32) for scene in range(scenes)]
-    for receiver in range(out_ref.shape[0] // scenes):
+    count = blocks_ref.shape[1]
+    for receiver in range(blocks_ref.shape[0]):
         start = margin + BRICKS * (receiver - 1) * tiles
-        found = rows_ref[start : start + count]
-        for scene in range(scenes):
-            kept = found * wanted[scene] if scenes > 1 else found
-            out_ref[receiver * scenes + scene] = kept.astype(BF16)
+        blocks_ref[receiver] = rows_ref[start : start + count].astype(BF16)
+    found = pltpu.make_async_copy(blocks_ref, out_hbm.at[:, scene], sems.at[6])
+    found.start()
+    found.wait()
+    if others is not None:
+        others.wait()
 
 
 def build_band(band_ref, rows):
@@ -99,10 +114,11 @@
     build_band(band_ref, weight_rows(weights_ref[...].astype(F32)))
 
 
-def masks_kernel(links_in, weights_ref, band_ref, masks_ref, links_ref, links_sem):
+def masks_kernel(links_in, one_ref, two_ref, band_ref, back_ref, masks_ref, links_ref, links_sem):
     links_copy = pltpu.make_async_copy(links_in, links_ref, links_sem)
     links_copy.start()
-    band_kernel(weights_ref, band_ref)
+    build_band(band_ref, weight_rows(one_ref[...].astype(F32)))
+    build_band(back_ref, flipped_rows(two_ref[...].astype(F32)))
     links_copy.wait()
     put_masks(masks_ref, links_ref)
 
@@ -211,15 +227,16 @@
 
 
 def first_kernel(
-    links_in, received_ref, up_ref, band_ref, weights_ref,
-    slope_out, hidden_out, turned_out, pad_out, back_out,
+    links_in, received_ref, up_ref, band_ref,
+    slope_out, hidden_out, turned_out, pad_out,
     volumes_ref, rows_ref, links_ref, links_sem,
 ):
     links_copy = pltpu.make_async_copy(links_in, links_ref, links_sem)
     links_copy.start()
     position = lax.axis_index("space")
-    tiles = received_ref.shape[1] // (3 * BRICKS)
-    rows_ref[0 : 3 * BRICKS * tiles] = jnp.sum(received_ref[...].astype(F32), axis=0)
+    tiles = received_ref.shape[2] // (3 * BRICKS)
+    received = received_ref[:, pl.ds(scene_of(received_ref), 1)]
+    rows_ref[0 : 3 * BRICKS * tiles] = jnp.sum(received.astype(F32), axis=(0, 1))
     rows_ref[3 * BRICKS * tiles :] = jnp.zeros((2 * tiles, 128), F32)
     cells = []
     for tile in range(tiles):
@@ -266,7 +283,6 @@
     hidden_out[...] = hidden
     hidden = hidden.astype(F32)
     turned_out[...] = jnp.transpose(hidden).astype(BF16)
-    build_band(back_out, flipped_rows(weights_ref[...].astype(F32)))
 
 
 def hidden_faces_kernel(hidden_ref, _parts, high_out, low_out, far_out, near_out, halves_ref, faces_ref):
@@ -375,7 +391,7 @@
     fine_out[...] = fine.astype(BF16).reshape(fine_out.shape)
 
 
-def sum_kernel(devices, scale, parts_ref, out_ref, rows_ref):
+def sum_kernel(devices, scale, parts_ref, out_hbm, rows_ref, shares_ref, sems):
     rows_ref[...] = parts_ref[...].astype(F32)
     share = rows_ref.shape[0] // devices
     pieces = [rows_ref[share * i : share * i + share] for i in range(devices)]
@@ -383,9 +399,16 @@
         pairs = [a + b for a, b in zip(pieces[::2], pieces[1::2])]
         pieces = pairs + pieces[len(pieces) - len(pieces) % 2 :]
     total = pieces[0] * scale
-    for i in range(devices):
+    some = shares_ref.shape[0]
+    for i in range(some // share):
         rows_ref[share * i : share * i + share] = total
-    out_ref[...] = rows_ref[...].astype(BF16)
+    shares_ref[...] = rows_ref[0:some].astype(BF16)
+    copies = []
+    for i in range(out_hbm.shape[0] // some):
+        copies.append(pltpu.make_async_copy(shares_ref, out_hbm.at[pl.ds(some * i, some)], sems.at[i]))
+        copies[-1].start()
+    for copy in copies:
+        copy.wait()
 
 
 def unpacked(tile):
@@ -464,21 +487,31 @@
     bricks = active_blocks.shape[1]
     tiles = width // 128
     scenes = 2 if lax.axis_size("dp") == 2 else 1
+    count = 3 * BRICKS * tiles
+    blocks = pltpu.VMEM((devices, count, 128), BF16)
     packed = call(
-        functools.partial(pick_kernel, scenes),
-        shape(devices * scenes, 3 * BRICKS * tiles, 128),
+        pick_kernel,
+        shape(devices, scenes, count, 128),
         [
             pltpu.VMEM((1, bricks), jnp.int32),
             pltpu.VMEM((1, held, width), BF16),
             pltpu.VMEM(((bricks + 16) * tiles, 128), F32),
-            pltpu.SemaphoreType.DMA((2,)),
+            blocks,
+            blocks,
+            pltpu.SemaphoreType.DMA((7,)),
         ],
         hbm=(0, 1),
         inputs=2,
         limit=60,
+        out=pl.ANY,
     )(active_blocks, coarse_latents)
-    axes = ("space", "dp")
-    received = lax.all_to_all(packed, axes if scenes == 2 else "space", split_axis=0, concat_axis=0, tiled=True)
+    received = lax.all_to_all(
+        packed.reshape(devices * scenes, count, 128),
+        ("space", "dp") if scenes == 2 else "space",
+        split_axis=0,
+        concat_axis=0,
+        tiled=True,
+    ).reshape(packed.shape)
     cost = pl.CostEstimate(flops=10**9, bytes_accessed=2 * 10**6, transcendentals=0)
     face = shape(BRICKS * FACE, LINE)
     halves = pltpu.VMEM((2, LINES, HALF), F32)
@@ -492,18 +525,18 @@
     far = swapped(far, 1)
     near = swapped(near, 0)
     masks = shape(BRICKS * 6 * 2 * BRICKS, 128, dtype=F32)
-    band_one, masks = call(masks_kernel, (shape(*BAND), masks), links, hbm=(0,), inputs=2, cost=cost)(
-        face_links, conv_one
-    )
-    slope, hidden, turned, lifted_pad, band_back = call(
+    band_one, band_back, masks = call(
+        masks_kernel, (shape(*BAND), shape(*BAND), masks), links, hbm=(0,), inputs=3, cost=cost
+    )(face_links, conv_one, conv_two)
+    slope, hidden, turned, lifted_pad = call(
         first_kernel,
         (
-            shape(ROWS, HALF, dtype=F32), volume, shape(HALF, ROWS), shape(*pad_shape), shape(*BAND),
+            shape(ROWS, HALF, dtype=F32), volume, shape(HALF, ROWS), shape(*pad_shape),
         ),
         [pltpu.VMEM((2, 8 * CUBE, 128), F32), pltpu.VMEM((8 * tiles, 128), F32), *links],
         hbm=(0,),
-        inputs=5,
-    )(face_links, received, up_weight, band_one, conv_two)
+        inputs=4,
+    )(face_links, received, up_weight, band_one)
     share = 2 * -(-4 * BLOCKS // everyone)
     packed_rows = (everyone * share, 128)
     sums, lifted = call(
@@ -523,8 +556,16 @@
         masks, band_two, lifted, hidden, hidden_high, hidden_low, hidden_far, hidden_near
     )
     scale = 1.0 / math.sqrt(lax.axis_size("dp") * devices * BRICKS * EDGE**3)
+    times = 4 if everyone % 32 == 0 else 1
     total = call(
-        functools.partial(sum_kernel, everyone, scale), shape(*packed_rows), [pltpu.VMEM(packed_rows, F32)]
+        functools.partial(sum_kernel, everyone, scale),
+        shape(*packed_rows),
+        [
+            pltpu.VMEM(packed_rows, F32),
+            pltpu.VMEM((packed_rows[0] // times, 128), BF16),
+            pltpu.SemaphoreType.DMA((times,)),
+        ],
+        out=pl.ANY,
     )(parts)
     gathered = exchanged(total)
     grads = shape(27, CHANNELS, CHANNELS, dtype=F32)

time: 44.3 us -> 44.3 us (level)
  no operation moved by 1% of the time
where the time goes in v19:
time: 44.3 us; the launch traced here: 44 us
  starting transfers between devices  20.2 us (46%)
  blocking collectives  10.7 us (24%)
  Pallas kernels  7.36 us (17%)
  waiting for transfers between devices  4.9 us (11%)
  between operations  0.79 us (2%)
    all_to_all x1, blocking collectives, exchanged(): lax.all_to_all(shares, ('space', 'dp'), split_axis=0, concat_axis=0, tile...  10.7 us
    ppermute x4, starting transfers between devices, swapped(): lax.ppermute(value, 'space', pairs + [(target, source) for source, target...  10.3 us
    all_to_all x1, starting transfers between devices, body(): lax.all_to_all(packed.reshape(devices * scenes, count, 128), ('space', 'd...  7.3 us
    all_to_all x1, waiting for transfers between devices, body(): lax.all_to_all(packed.reshape(devices * scenes, count, 128), ('space', 'd...  2.88 us
    all_to_all x1, starting transfers between devices, exchanged(): lax.all_to_all(shares, ('space', 'dp'), split_axis=0, concat_axis=0, tile...  2.59 us
    pallas_call x1, Pallas kernels, body(): call(pick_kernel, shape(devices, scenes, count, 128), [pltpu.VMEM((1, bri...  1.74 us
    ppermute x4, waiting for transfers between devices, swapped(): lax.ppermute(value, 'space', pairs + [(target, source) for source, target...  1.71 us
    pallas_call x1, Pallas kernels, body(): call(unpack_kernel, (grads, grads, shape(*fine.shape)), scratch, inputs=2...  1.13 us
  transfers between devices with their start and end apart: 6, of which 3 were waited for; matrix products, arithmetic and copies ran while one was open for 0% of the time, Pallas kernels for 6%

profile of v19, /device:TPU:0, one launch (start us, length us, event | category | flops | bytes accessed | tf_op | source)
XLA Modules:
  0.0 44.0 jit_solution(16846821787851575447)
XLA Ops:
  0.6 1.7 %shard_map.95 = bf16[16,2,24,128]{3,2,1,0:T(8,128)(2,1)} custom-call(s32[1,32]{1,0:T(1,128)} %ids_hbm.1, bf16[1,64,512]{2,1,0:T(8,128)(2,1)} %latents_hbm.1), custom_call_target="tpu_custom_call" | custom-call | tf_op jit(solution)/shard_map/pallas_call | solution.py:492
  2.4 0.0 copy-start.1
  2.4 0.0 copy-start.3
  2.4 7.3 %all-to-all-start = ((bf16[32,24,128]{2,1,0:T(8,128)(2,1)}), bf16[32,24,128]{2,1,0:T(8,128)(2,1)S(1)}, u32[]{:S(2)}, u32[]{:S(2)}) async-start(bf16[32,24,128]{2,1,0:T(8,128)(2,1)} %bitcast.11), calls=%async_computation | async-start | bytes 393216 | tf_op jit(solution)/shard_map/all_to_all | solution.py:508
  9.7 0.1 shard_map.97
  9.8 0.0 copy-start.2
  9.8 0.7 %collective-permute-start = (bf16[48,256]{1,0:T(8,128)(2,1)S(1)}, bf16[48,256]{1,0:T(8,128)(2,1)S(1)}, u32[]{:S(2)}, u32[]{:S(2)}) collective-permute-start(bf16[48,256]{1,0:T(8,128)(2,1)S(1)} %get-tuple-element.31), channel_id=1, source_target_pairs={{2,4},{6,8},{10,12},{14,16},{18,20},{22,24},{26,28},{4,2},{8,6},{1... | collective-permute-start | bytes 73736 | tf_op jit(solution)/shard_map/ppermute | solution.py:473
  10.5 0.0 copy-start
  10.5 4.5 %collective-permute-start.1 = (bf16[48,256]{1,0:T(8,128)(2,1)S(1)}, bf16[48,256]{1,0:T(8,128)(2,1)S(1)}, u32[]{:S(2)}, u32[]{:S(2)}) collective-permute-start(bf16[48,256]{1,0:T(8,128)(2,1)S(1)} %get-tuple-element.32), channel_id=1, source_target_pairs={{0,2},{4,6},{8,10},{12,14},{16,18},{20,22},{24,26},{28,30},{2,0},{... | collective-permute-start | bytes 73736 | tf_op jit(solution)/shard_map/ppermute | solution.py:473
  15.1 0.7 %shard_map.94 = (bf16[9,256,128]{2,1,0:T(8,128)(2,1)S(1)}, bf16[9,256,128]{2,1,0:T(8,128)(2,1)S(1)}, f32[48,128]{1,0:T(8,128)S(1)}) custom-call(s32[1,2,6]{2,1,0:T(2,128)S(1)} %copy-done.2, bf16[27,32,32]{2,1,0:T(8,128)(2,1)S(1)} %copy-done.3, bf16[27,32,32]{2,1,0:T(8,128)(2,1)S(1)} %copy-done.4), custom_call_target="tpu_custom_call" | custom-call | flops 1000000000 | bytes 2000000 | tf_op jit(solution)/shard_map/pallas_call | solution.py:528
  15.7 2.9 %all-to-all-done = bf16[32,24,128]{2,1,0:T(8,128)(2,1)S(1)} async-done(((bf16[32,24,128]{2,1,0:T(8,128)(2,1)}), bf16[32,24,128]{2,1,0:T(8,128)(2,1)S(1)}, u32[]{:S(2)}, u32[]{:S(2)}) %all-to-all-start) | async-done | bytes 196640 | tf_op jit(solution)/shard_map/all_to_all | solution.py:508
  18.6 1.1 %shard_map.96 = (f32[256,128]{1,0:T(8,128)S(1)}, bf16[256,128]{1,0:T(8,128)(2,1)S(1)}, bf16[128,256]{1,0:T(8,128)(2,1)S(1)}, bf16[3,2,10,16,256]{4,3,2,1,0:T(8,128)(2,1)S(1)}) custom-call(s32[1,2,6]{2,1,0:T(2,128)S(1)} %copy-done.2, bf16[16,2,24,128]{3,2,1,0:T(8,128)(2,1)S(1)} %bitcast.8, bf16[64,2048]{1,0:T(8,128)(2,1)S(1)} %copy-done, ...), custom_call_target="tpu_custom_call" | custom-call | tf_op jit(solution)/shard_map/pallas_call | solution.py:531
  19.7 1.1 %shard_map.98 = (bf16[448,128]{1,0:T(8,128)(2,1)S(1)}, bf16[256,128]{1,0:T(8,128)(2,1)S(1)}) custom-call(f32[48,128]{1,0:T(8,128)S(1)} %get-tuple-element.23.masks_ref, bf16[1,2,8,8,256]{4,3,2,1,0:T(8,128)(2,1)S(1)} %copy-done.1, bf16[9,256,128]{2,1,0:T(8,128)(2,1)S(1)} %get-tuple-element.24.band_ref, f32[256,128]{1,0:T(8,128)S(1)} %get-tuple-element.26.slope_ref, ...), custom_call_target="tpu_custom_call" | custom-call | tf_op jit(solution)/shard_map/pallas_call | solution.py:542
  20.8 10.7 %all_to_all.15 = bf16[32,7,2,128]{3,2,1,0:T(2,128)(2,1)S(1)} all-to-all(bf16[32,7,2,128]{3,2,1,0:T(2,128)(2,1)S(1)} %bitcast.10), channel_id=1, replica_groups=mesh['space'=16,'dp'=2] {'space','dp'}, dimensions={0} | all-to-all | bytes 229376 | tf_op jit(solution)/shard_map/all_to_all | solution.py:479
  31.5 0.7 %shard_map.99 = bf16[448,128]{1,0:T(8,128)(2,1)} custom-call(bf16[448,128]{1,0:T(8,128)(2,1)S(1)} %bitcast.6), custom_call_target="tpu_custom_call" | custom-call | tf_op jit(solution)/shard_map/pallas_call | solution.py:560
  32.2 2.6 %all-to-all-start.2 = ((bf16[32,7,2,128]{3,2,1,0:T(2,128)(2,1)}), bf16[32,7,2,128]{3,2,1,0:T(2,128)(2,1)S(1)}, u32[]{:S(2)}, u32[]{:S(2)}) async-start(bf16[32,7,2,128]{3,2,1,0:T(2,128)(2,1)} %bitcast.4), calls=%async_computation.2 | async-start | bytes 229376 | tf_op jit(solution)/shard_map/all_to_all | solution.py:479
  34.8 0.1 shard_map.101
  34.9 0.7 %collective-permute-start.2 = (bf16[48,256]{1,0:T(8,128)(2,1)S(1)}, bf16[48,256]{1,0:T(8,128)(2,1)S(1)}, u32[]{:S(2)}, u32[]{:S(2)}) collective-permute-start(bf16[48,256]{1,0:T(8,128)(2,1)S(1)} %get-tuple-element.38), channel_id=1, source_target_pairs={{2,4},{6,8},{10,12},{14,16},{18,20},{22,24},{26,28},{4,2},{8,6},{1... | collective-permute-start | bytes 73736 | tf_op jit(solution)/shard_map/ppermute | solution.py:473
  35.6 4.4 %collective-permute-start.3 = (bf16[48,256]{1,0:T(8,128)(2,1)S(1)}, bf16[48,256]{1,0:T(8,128)(2,1)S(1)}, u32[]{:S(2)}, u32[]{:S(2)}) collective-permute-start(bf16[48,256]{1,0:T(8,128)(2,1)S(1)} %get-tuple-element.39), channel_id=1, source_target_pairs={{0,2},{4,6},{8,10},{12,14},{16,18},{20,22},{24,26},{28,30},{2,0},{... | collective-permute-start | bytes 73736 | tf_op jit(solution)/shard_map/ppermute | solution.py:473
  40.0 0.3 shard_map.100.band_ref
  40.3 1.7 %collective-permute-done.3.near = bf16[48,256]{1,0:T(8,128)(2,1)S(1)} collective-permute-done((bf16[48,256]{1,0:T(8,128)(2,1)S(1)}, bf16[48,256]{1,0:T(8,128)(2,1)S(1)}, u32[]{:S(2)}, u32[]{:S(2)}) %collective-permute-start.3) | collective-permute-done | bytes 24608 | tf_op jit(solution)/shard_map/ppermute | solution.py:473
  42.0 0.5 %shard_map.102.fine_ref = bf16[1,2,8,8,256]{4,3,2,1,0:T(8,128)(2,1)S(1)} custom-call(f32[48,128]{1,0:T(8,128)S(1)} %get-tuple-element.23.masks_ref, bf16[9,256,128]{2,1,0:T(8,128)(2,1)S(1)} %shard_map.100.band_ref, bf16[256,128]{1,0:T(8,128)(2,1)S(1)} %get-tuple-element.34.lifted_ref, bf16[256,128]{1,0:T(8,128)(2,1)S(1)} %get-tuple-element.35.hidden_ref, ...), custom_call_target="tpu_custom_call" | custom-call | flops 1000000000 | bytes 2000000 | tf_op jit(solution)/shard_map/pallas_call | solution.py:555
  42.5 0.3 all-to-all-done.2
  42.8 1.1 %shard_map.103 = (f32[27,32,32]{2,1,0:T(8,128)}, f32[27,32,32]{2,1,0:T(8,128)}, bf16[1,2,8,8,256]{4,3,2,1,0:T(8,128)(2,1)}) custom-call(bf16[448,128]{1,0:T(8,128)(2,1)S(1)} %bitcast.9, bf16[1,2,8,8,256]{4,3,2,1,0:T(8,128)(2,1)S(1)} %shard_map.102.fine_ref), custom_call_target="tpu_custom_call" | custom-call | tf_op jit(solution)/shard_map/pallas_call | solution.py:575
  (9 shorter events, 0.0 us)
Async XLA Ops:
  0.6 14.4 %copy-start.4 = (bf16[27,32,32]{2,1,0:T(8,128)(2,1)S(1)}, bf16[27,32,32]{2,1,0:T(8,128)(2,1)}, u32[]{:S(2)}) copy-start(bf16[27,32,32]{2,1,0:T(8,128)(2,1)} %weights_ref.1) | copy-start | bytes 165892
  2.4 7.3 %copy-start.1 = (bf16[1,2,8,8,256]{4,3,2,1,0:T(8,128)(2,1)S(1)}, bf16[1,2,8,8,256]{4,3,2,1,0:T(8,128)(2,1)}, u32[]{:S(2)}) copy-start(bf16[1,2,8,8,256]{4,3,2,1,0:T(8,128)(2,1)} %cotangent_ref.3) | copy-start | bytes 196612
  2.4 12.7 %copy-start.3 = (bf16[27,32,32]{2,1,0:T(8,128)(2,1)S(1)}, bf16[27,32,32]{2,1,0:T(8,128)(2,1)}, u32[]{:S(2)}) copy-start(bf16[27,32,32]{2,1,0:T(8,128)(2,1)} %one_ref.1) | copy-start | bytes 165892
  2.4 16.2 %all-to-all-start = ((bf16[32,24,128]{2,1,0:T(8,128)(2,1)}), bf16[32,24,128]{2,1,0:T(8,128)(2,1)S(1)}, u32[]{:S(2)}, u32[]{:S(2)}) async-start(bf16[32,24,128]{2,1,0:T(8,128)(2,1)} %bitcast.11), calls=%async_computation | async-start | bytes 393216 | tf_op jit(solution)/shard_map/all_to_all | solution.py:508
  9.8 5.2 %copy-start.2 = (s32[1,2,6]{2,1,0:T(2,128)S(1)}, s32[1,2,6]{2,1,0:T(2,128)}, u32[]{:S(2)}) copy-start(s32[1,2,6]{2,1,0:T(2,128)} %links_in.3) | copy-start | bytes 148
  9.8 9.9 %collective-permute-start = (bf16[48,256]{1,0:T(8,128)(2,1)S(1)}, bf16[48,256]{1,0:T(8,128)(2,1)S(1)}, u32[]{:S(2)}, u32[]{:S(2)}) collective-permute-start(bf16[48,256]{1,0:T(8,128)(2,1)S(1)} %get-tuple-element.31), channel_id=1, source_target_pairs={{2,4},{6,8},{10,12},{14,16},{18,20},{22,24},{26,28},{4,2},{8,6},{1... | collective-permute-start | bytes 73736 | tf_op jit(solution)/shard_map/ppermute | solution.py:473
  10.5 8.1 %copy-start = (bf16[64,2048]{1,0:T(8,128)(2,1)S(1)}, bf16[64,2048]{1,0:T(8,128)(2,1)}, u32[]{:S(2)}) copy-start(bf16[64,2048]{1,0:T(8,128)(2,1)} %up_ref.1) | copy-start | bytes 786436
  10.5 9.2 %collective-permute-start.1 = (bf16[48,256]{1,0:T(8,128)(2,1)S(1)}, bf16[48,256]{1,0:T(8,128)(2,1)S(1)}, u32[]{:S(2)}, u32[]{:S(2)}) collective-permute-start(bf16[48,256]{1,0:T(8,128)(2,1)S(1)} %get-tuple-element.32), channel_id=1, source_target_pairs={{0,2},{4,6},{8,10},{12,14},{16,18},{20,22},{24,26},{28,30},{2,0},{... | collective-permute-start | bytes 73736 | tf_op jit(solution)/shard_map/ppermute | solution.py:473
  32.2 10.6 %all-to-all-start.2 = ((bf16[32,7,2,128]{3,2,1,0:T(2,128)(2,1)}), bf16[32,7,2,128]{3,2,1,0:T(2,128)(2,1)S(1)}, u32[]{:S(2)}, u32[]{:S(2)}) async-start(bf16[32,7,2,128]{3,2,1,0:T(2,128)(2,1)} %bitcast.4), calls=%async_computation.2 | async-start | bytes 229376 | tf_op jit(solution)/shard_map/all_to_all | solution.py:479
  34.9 5.4 %collective-permute-start.2 = (bf16[48,256]{1,0:T(8,128)(2,1)S(1)}, bf16[48,256]{1,0:T(8,128)(2,1)S(1)}, u32[]{:S(2)}, u32[]{:S(2)}) collective-permute-start(bf16[48,256]{1,0:T(8,128)(2,1)S(1)} %get-tuple-element.38), channel_id=1, source_target_pairs={{2,4},{6,8},{10,12},{14,16},{18,20},{22,24},{26,28},{4,2},{8,6},{1... | collective-permute-start | bytes 73736 | tf_op jit(solution)/shard_map/ppermute | solution.py:473
  35.6 6.5 %collective-permute-start.3 = (bf16[48,256]{1,0:T(8,128)(2,1)S(1)}, bf16[48,256]{1,0:T(8,128)(2,1)S(1)}, u32[]{:S(2)}, u32[]{:S(2)}) collective-permute-start(bf16[48,256]{1,0:T(8,128)(2,1)S(1)} %get-tuple-element.39), channel_id=1, source_target_pairs={{0,2},{4,6},{8,10},{12,14},{16,18},{20,22},{24,26},{28,30},{2,0},{... | collective-permute-start | bytes 73736 | tf_op jit(solution)/shard_map/ppermute | solution.py:473

commit v20 on v19

--- a/solution.py
+++ b/solution.py
@@ -74,10 +74,11 @@
     picked = dot_rows(hot, latents_ref[0])
     for tile in range(tiles):
         rows_ref[pl.ds(margin + tile, bricks, stride=tiles), :] = picked[:, tile * 128 : tile * 128 + 128]
-    count = blocks_ref.shape[1]
-    for receiver in range(blocks_ref.shape[0]):
-        start = margin + BRICKS * (receiver - 1) * tiles
-        blocks_ref[receiver] = rows_ref[start : start + count].astype(BF16)
+    some, quarters, count = blocks_ref.shape[:3]
+    for quarter in range(quarters):
+        for place in range(some):
+            start = margin + BRICKS * (quarter * some + place - 1) * tiles
+            blocks_ref[place, quarter] = rows_ref[start : start + count].astype(BF16)
     found = pltpu.make_async_copy(blocks_ref, out_hbm.at[:, scene], sems.at[6])
     found.start()
     found.wait()
@@ -234,9 +235,9 @@
     links_copy = pltpu.make_async_copy(links_in, links_ref, links_sem)
     links_copy.start()
     position = lax.axis_index("space")
-    tiles = received_ref.shape[2] // (3 * BRICKS)
+    tiles = received_ref.shape[3] // (3 * BRICKS)
     received = received_ref[:, pl.ds(scene_of(received_ref), 1)]
-    rows_ref[0 : 3 * BRICKS * tiles] = jnp.sum(received.astype(F32), axis=(0, 1))
+    rows_ref[0 : 3 * BRICKS * tiles] = jnp.sum(received.astype(F32), axis=(0, 1, 2))
     rows_ref[3 * BRICKS * tiles :] = jnp.zeros((2 * tiles, 128), F32)
     cells = []
     for tile in range(tiles):
@@ -473,10 +474,16 @@
     return lax.ppermute(value, "space", pairs + [(target, source) for source, target in pairs])
 
 
+def crosswise(count):
+    return [[i % 4 * (count // 4) + i // 4 for i in range(count)]]
+
+
 def exchanged(rows):
     everyone = lax.axis_size("space") * lax.axis_size("dp")
     shares = rows.reshape(everyone, -1, 2, 128)
-    shares = lax.all_to_all(shares, ("space", "dp"), split_axis=0, concat_axis=0, tiled=True)
+    shares = lax.all_to_all(
+        shares, ("space", "dp"), split_axis=0, concat_axis=0, axis_index_groups=crosswise(everyone), tiled=True
+    )
     return shares.reshape(rows.shape)
 
 
@@ -488,10 +495,10 @@
     tiles = width // 128
     scenes = 2 if lax.axis_size("dp") == 2 else 1
     count = 3 * BRICKS * tiles
-    blocks = pltpu.VMEM((devices, count, 128), BF16)
+    blocks = pltpu.VMEM((devices // 4, 4, count, 128), BF16)
     packed = call(
         pick_kernel,
-        shape(devices, scenes, count, 128),
+        shape(devices // 4, scenes, 4, count, 128),
         [
             pltpu.VMEM((1, bricks), jnp.int32),
             pltpu.VMEM((1, held, width), BF16),
@@ -510,6 +517,7 @@
         ("space", "dp") if scenes == 2 else "space",
         split_axis=0,
         concat_axis=0,
+        axis_index_groups=crosswise(devices * scenes),
         tiled=True,
     ).reshape(packed.shape)
     cost = pl.CostEstimate(flops=10**9, bytes_accessed=2 * 10**6, transcendentals=0)

time: 44.3 us -> 44.6 us (level)
  waiting for transfers between devices: 4.9 us -> 5.5 us
where the time goes in v20:
time: 44.6 us; the launch traced here: 44.2 us
  starting transfers between devices  20.2 us (45%)
  blocking collectives  10.3 us (23%)
  Pallas kernels  7.35 us (16%)
  waiting for transfers between devices  5.5 us (12%)
  between operations  0.79 us (2%)
    all_to_all x1, blocking collectives, exchanged(): lax.all_to_all(shares, ('space', 'dp'), split_axis=0, concat_axis=0, axis...  10.3 us
    ppermute x4, starting transfers between devices, swapped(): lax.ppermute(value, 'space', pairs + [(target, source) for source, target...  10.3 us
    all_to_all x1, starting transfers between devices, body(): lax.all_to_all(packed.reshape(devices * scenes, count, 128), ('space', 'd...  7.3 us
    all_to_all x1, waiting for transfers between devices, body(): lax.all_to_all(packed.reshape(devices * scenes, count, 128), ('space', 'd...  3.32 us
    all_to_all x1, starting transfers between devices, exchanged(): lax.all_to_all(shares, ('space', 'dp'), split_axis=0, concat_axis=0, axis...  2.59 us
    ppermute x4, waiting for transfers between devices, swapped(): lax.ppermute(value, 'space', pairs + [(target, source) for source, target...  1.79 us
    pallas_call x1, Pallas kernels, body(): call(pick_kernel, shape(devices // 4, scenes, 4, count, 128), [pltpu.VMEM...  1.74 us
    pallas_call x1, Pallas kernels, body(): call(unpack_kernel, (grads, grads, shape(*fine.shape)), scratch, inputs=2...  1.13 us
  transfers between devices with their start and end apart: 6, of which 3 were waited for; matrix products, arithmetic and copies ran while one was open for 0% of the time, Pallas kernels for 6%

profile of v20, /device:TPU:0, one launch (start us, length us, event | category | flops | bytes accessed | tf_op | source)
XLA Modules:
  0.0 44.2 jit_solution(17829255548787680991)
XLA Ops:
  0.6 1.7 %shard_map.95 = bf16[4,2,4,24,128]{4,3,2,1,0:T(8,128)(2,1)} custom-call(s32[1,32]{1,0:T(1,128)} %ids_hbm.1, bf16[1,64,512]{2,1,0:T(8,128)(2,1)} %latents_hbm.1), custom_call_target="tpu_custom_call" | custom-call | tf_op jit(solution)/shard_map/pallas_call | solution.py:499
  2.4 0.0 copy-start.1
  2.4 0.0 copy-start.3
  2.4 7.3 %all-to-all-start = ((bf16[32,24,128]{2,1,0:T(8,128)(2,1)}), bf16[32,24,128]{2,1,0:T(8,128)(2,1)S(1)}, u32[]{:S(2)}, u32[]{:S(2)}) async-start(bf16[32,24,128]{2,1,0:T(8,128)(2,1)} %bitcast.11), calls=%async_computation | async-start | bytes 393216 | tf_op jit(solution)/shard_map/all_to_all | solution.py:515
  9.7 0.1 shard_map.97
  9.8 0.0 copy-start.2
  9.8 0.7 %collective-permute-start = (bf16[48,256]{1,0:T(8,128)(2,1)S(1)}, bf16[48,256]{1,0:T(8,128)(2,1)S(1)}, u32[]{:S(2)}, u32[]{:S(2)}) collective-permute-start(bf16[48,256]{1,0:T(8,128)(2,1)S(1)} %get-tuple-element.31), channel_id=1, source_target_pairs={{2,4},{6,8},{10,12},{14,16},{18,20},{22,24},{26,28},{4,2},{8,6},{1... | collective-permute-start | bytes 73736 | tf_op jit(solution)/shard_map/ppermute | solution.py:474
  10.5 0.0 copy-start
  10.5 4.5 %collective-permute-start.1 = (bf16[48,256]{1,0:T(8,128)(2,1)S(1)}, bf16[48,256]{1,0:T(8,128)(2,1)S(1)}, u32[]{:S(2)}, u32[]{:S(2)}) collective-permute-start(bf16[48,256]{1,0:T(8,128)(2,1)S(1)} %get-tuple-element.32), channel_id=1, source_target_pairs={{0,2},{4,6},{8,10},{12,14},{16,18},{20,22},{24,26},{28,30},{2,0},{... | collective-permute-start | bytes 73736 | tf_op jit(solution)/shard_map/ppermute | solution.py:474
  15.1 0.7 %shard_map.94 = (bf16[9,256,128]{2,1,0:T(8,128)(2,1)S(1)}, bf16[9,256,128]{2,1,0:T(8,128)(2,1)S(1)}, f32[48,128]{1,0:T(8,128)S(1)}) custom-call(s32[1,2,6]{2,1,0:T(2,128)S(1)} %copy-done.2, bf16[27,32,32]{2,1,0:T(8,128)(2,1)S(1)} %copy-done.3, bf16[27,32,32]{2,1,0:T(8,128)(2,1)S(1)} %copy-done.4), custom_call_target="tpu_custom_call" | custom-call | flops 1000000000 | bytes 2000000 | tf_op jit(solution)/shard_map/pallas_call | solution.py:536
  15.7 3.3 %all-to-all-done = bf16[32,24,128]{2,1,0:T(8,128)(2,1)S(1)} async-done(((bf16[32,24,128]{2,1,0:T(8,128)(2,1)}), bf16[32,24,128]{2,1,0:T(8,128)(2,1)S(1)}, u32[]{:S(2)}, u32[]{:S(2)}) %all-to-all-start) | async-done | bytes 196640 | tf_op jit(solution)/shard_map/all_to_all | solution.py:515
  19.1 1.1 %shard_map.96 = (f32[256,128]{1,0:T(8,128)S(1)}, bf16[256,128]{1,0:T(8,128)(2,1)S(1)}, bf16[128,256]{1,0:T(8,128)(2,1)S(1)}, bf16[3,2,10,16,256]{4,3,2,1,0:T(8,128)(2,1)S(1)}) custom-call(s32[1,2,6]{2,1,0:T(2,128)S(1)} %copy-done.2, bf16[4,2,4,24,128]{4,3,2,1,0:T(8,128)(2,1)S(1)} %bitcast.8, bf16[64,2048]{1,0:T(8,128)(2,1)S(1)} %copy-done, ...), custom_call_target="tpu_custom_call" | custom-call | tf_op jit(solution)/shard_map/pallas_call | solution.py:539
  20.2 1.1 %shard_map.98 = (bf16[448,128]{1,0:T(8,128)(2,1)S(1)}, bf16[256,128]{1,0:T(8,128)(2,1)S(1)}) custom-call(f32[48,128]{1,0:T(8,128)S(1)} %get-tuple-element.23.masks_ref, bf16[1,2,8,8,256]{4,3,2,1,0:T(8,128)(2,1)S(1)} %copy-done.1, bf16[9,256,128]{2,1,0:T(8,128)(2,1)S(1)} %get-tuple-element.24.band_ref, f32[256,128]{1,0:T(8,128)S(1)} %get-tuple-element.26.slope_ref, ...), custom_call_target="tpu_custom_call" | custom-call | tf_op jit(solution)/shard_map/pallas_call | solution.py:550
  21.2 10.3 %all_to_all.15 = bf16[32,7,2,128]{3,2,1,0:T(2,128)(2,1)S(1)} all-to-all(bf16[32,7,2,128]{3,2,1,0:T(2,128)(2,1)S(1)} %bitcast.10), channel_id=1, replica_groups={{0,8,16,24,1,9,17,25,2,10,18,26,3,11,19,27,4,12,20,28,5,13,21,29,6,14,2..., dimensions={0} | all-to-all | bytes 229376 | tf_op jit(solution)/shard_map/all_to_all | solution.py:484
  31.6 0.7 %shard_map.99 = bf16[448,128]{1,0:T(8,128)(2,1)} custom-call(bf16[448,128]{1,0:T(8,128)(2,1)S(1)} %bitcast.6), custom_call_target="tpu_custom_call" | custom-call | tf_op jit(solution)/shard_map/pallas_call | solution.py:568
  32.3 2.6 %all-to-all-start.2 = ((bf16[32,7,2,128]{3,2,1,0:T(2,128)(2,1)}), bf16[32,7,2,128]{3,2,1,0:T(2,128)(2,1)S(1)}, u32[]{:S(2)}, u32[]{:S(2)}) async-start(bf16[32,7,2,128]{3,2,1,0:T(2,128)(2,1)} %bitcast.4), calls=%async_computation.2 | async-start | bytes 229376 | tf_op jit(solution)/shard_map/all_to_all | solution.py:484
  34.9 0.1 shard_map.101
  35.0 0.7 %collective-permute-start.2 = (bf16[48,256]{1,0:T(8,128)(2,1)S(1)}, bf16[48,256]{1,0:T(8,128)(2,1)S(1)}, u32[]{:S(2)}, u32[]{:S(2)}) collective-permute-start(bf16[48,256]{1,0:T(8,128)(2,1)S(1)} %get-tuple-element.38), channel_id=1, source_target_pairs={{2,4},{6,8},{10,12},{14,16},{18,20},{22,24},{26,28},{4,2},{8,6},{1... | collective-permute-start | bytes 73736 | tf_op jit(solution)/shard_map/ppermute | solution.py:474
  35.7 4.4 %collective-permute-start.3 = (bf16[48,256]{1,0:T(8,128)(2,1)S(1)}, bf16[48,256]{1,0:T(8,128)(2,1)S(1)}, u32[]{:S(2)}, u32[]{:S(2)}) collective-permute-start(bf16[48,256]{1,0:T(8,128)(2,1)S(1)} %get-tuple-element.39), channel_id=1, source_target_pairs={{0,2},{4,6},{8,10},{12,14},{16,18},{20,22},{24,26},{28,30},{2,0},{... | collective-permute-start | bytes 73736 | tf_op jit(solution)/shard_map/ppermute | solution.py:474
  40.1 0.3 shard_map.100.band_ref
  40.4 1.8 %collective-permute-done.3.near = bf16[48,256]{1,0:T(8,128)(2,1)S(1)} collective-permute-done((bf16[48,256]{1,0:T(8,128)(2,1)S(1)}, bf16[48,256]{1,0:T(8,128)(2,1)S(1)}, u32[]{:S(2)}, u32[]{:S(2)}) %collective-permute-start.3) | collective-permute-done | bytes 24608 | tf_op jit(solution)/shard_map/ppermute | solution.py:474
  42.2 0.5 %shard_map.102.fine_ref = bf16[1,2,8,8,256]{4,3,2,1,0:T(8,128)(2,1)S(1)} custom-call(f32[48,128]{1,0:T(8,128)S(1)} %get-tuple-element.23.masks_ref, bf16[9,256,128]{2,1,0:T(8,128)(2,1)S(1)} %shard_map.100.band_ref, bf16[256,128]{1,0:T(8,128)(2,1)S(1)} %get-tuple-element.34.lifted_ref, bf16[256,128]{1,0:T(8,128)(2,1)S(1)} %get-tuple-element.35.hidden_ref, ...), custom_call_target="tpu_custom_call" | custom-call | flops 1000000000 | bytes 2000000 | tf_op jit(solution)/shard_map/pallas_call | solution.py:563
  42.7 0.4 all-to-all-done.2
  43.1 1.1 %shard_map.103 = (f32[27,32,32]{2,1,0:T(8,128)}, f32[27,32,32]{2,1,0:T(8,128)}, bf16[1,2,8,8,256]{4,3,2,1,0:T(8,128)(2,1)}) custom-call(bf16[448,128]{1,0:T(8,128)(2,1)S(1)} %bitcast.9, bf16[1,2,8,8,256]{4,3,2,1,0:T(8,128)(2,1)S(1)} %shard_map.102.fine_ref), custom_call_target="tpu_custom_call" | custom-call | tf_op jit(solution)/shard_map/pallas_call | solution.py:583
  (9 shorter events, 0.0 us)
Async XLA Ops:
  0.6 14.4 %copy-start.4 = (bf16[27,32,32]{2,1,0:T(8,128)(2,1)S(1)}, bf16[27,32,32]{2,1,0:T(8,128)(2,1)}, u32[]{:S(2)}) copy-start(bf16[27,32,32]{2,1,0:T(8,128)(2,1)} %weights_ref.1) | copy-start | bytes 165892
  2.4 7.3 %copy-start.1 = (bf16[1,2,8,8,256]{4,3,2,1,0:T(8,128)(2,1)S(1)}, bf16[1,2,8,8,256]{4,3,2,1,0:T(8,128)(2,1)}, u32[]{:S(2)}) copy-start(bf16[1,2,8,8,256]{4,3,2,1,0:T(8,128)(2,1)} %cotangent_ref.3) | copy-start | bytes 196612
  2.4 12.7 %copy-start.3 = (bf16[27,32,32]{2,1,0:T(8,128)(2,1)S(1)}, bf16[27,32,32]{2,1,0:T(8,128)(2,1)}, u32[]{:S(2)}) copy-start(bf16[27,32,32]{2,1,0:T(8,128)(2,1)} %one_ref.1) | copy-start | bytes 165892
  2.4 16.6 %all-to-all-start = ((bf16[32,24,128]{2,1,0:T(8,128)(2,1)}), bf16[32,24,128]{2,1,0:T(8,128)(2,1)S(1)}, u32[]{:S(2)}, u32[]{:S(2)}) async-start(bf16[32,24,128]{2,1,0:T(8,128)(2,1)} %bitcast.11), calls=%async_computation | async-start | bytes 393216 | tf_op jit(solution)/shard_map/all_to_all | solution.py:515
  9.8 5.2 %copy-start.2 = (s32[1,2,6]{2,1,0:T(2,128)S(1)}, s32[1,2,6]{2,1,0:T(2,128)}, u32[]{:S(2)}) copy-start(s32[1,2,6]{2,1,0:T(2,128)} %links_in.3) | copy-start | bytes 148
  9.8 10.3 %collective-permute-start = (bf16[48,256]{1,0:T(8,128)(2,1)S(1)}, bf16[48,256]{1,0:T(8,128)(2,1)S(1)}, u32[]{:S(2)}, u32[]{:S(2)}) collective-permute-start(bf16[48,256]{1,0:T(8,128)(2,1)S(1)} %get-tuple-element.31), channel_id=1, source_target_pairs={{2,4},{6,8},{10,12},{14,16},{18,20},{22,24},{26,28},{4,2},{8,6},{1... | collective-permute-start | bytes 73736 | tf_op jit(solution)/shard_map/ppermute | solution.py:474
  10.5 8.5 %copy-start = (bf16[64,2048]{1,0:T(8,128)(2,1)S(1)}, bf16[64,2048]{1,0:T(8,128)(2,1)}, u32[]{:S(2)}) copy-start(bf16[64,2048]{1,0:T(8,128)(2,1)} %up_ref.1) | copy-start | bytes 786436
  10.5 9.6 %collective-permute-start.1 = (bf16[48,256]{1,0:T(8,128)(2,1)S(1)}, bf16[48,256]{1,0:T(8,128)(2,1)S(1)}, u32[]{:S(2)}, u32[]{:S(2)}) collective-permute-start(bf16[48,256]{1,0:T(8,128)(2,1)S(1)} %get-tuple-element.32), channel_id=1, source_target_pairs={{0,2},{4,6},{8,10},{12,14},{16,18},{20,22},{24,26},{28,30},{2,0},{... | collective-permute-start | bytes 73736 | tf_op jit(solution)/shard_map/ppermute | solution.py:474
  32.3 10.8 %all-to-all-start.2 = ((bf16[32,7,2,128]{3,2,1,0:T(2,128)(2,1)}), bf16[32,7,2,128]{3,2,1,0:T(2,128)(2,1)S(1)}, u32[]{:S(2)}, u32[]{:S(2)}) async-start(bf16[32,7,2,128]{3,2,1,0:T(2,128)(2,1)} %bitcast.4), calls=%async_computation.2 | async-start | bytes 229376 | tf_op jit(solution)/shard_map/all_to_all | solution.py:484
  35.0 5.4 %collective-permute-start.2 = (bf16[48,256]{1,0:T(8,128)(2,1)S(1)}, bf16[48,256]{1,0:T(8,128)(2,1)S(1)}, u32[]{:S(2)}, u32[]{:S(2)}) collective-permute-start(bf16[48,256]{1,0:T(8,128)(2,1)S(1)} %get-tuple-element.38), channel_id=1, source_target_pairs={{2,4},{6,8},{10,12},{14,16},{18,20},{22,24},{26,28},{4,2},{8,6},{1... | collective-permute-start | bytes 73736 | tf_op jit(solution)/shard_map/ppermute | solution.py:474
  35.7 6.6 %collective-permute-start.3 = (bf16[48,256]{1,0:T(8,128)(2,1)S(1)}, bf16[48,256]{1,0:T(8,128)(2,1)S(1)}, u32[]{:S(2)}, u32[]{:S(2)}) collective-permute-start(bf16[48,256]{1,0:T(8,128)(2,1)S(1)} %get-tuple-element.39), channel_id=1, source_target_pairs={{0,2},{4,6},{8,10},{12,14},{16,18},{20,22},{24,26},{28,30},{2,0},{... | collective-permute-start | bytes 73736 | tf_op jit(solution)/shard_map/ppermute | solution.py:474

commit v21 on v19

--- a/solution.py
+++ b/solution.py
@@ -21,7 +21,7 @@
 BAND = (9, WIDE, HALF)
 ROWS = 2 * LINES
 FACE = 3 * EDGE
-BLOCKS = 54
+GROUPS = 7
 
 
 def dot(left, right):
@@ -290,20 +290,23 @@
     to_partners(high_out, low_out, far_out, near_out)
 
 
-def fold(outer, places):
+def picked(outer, places):
     lane = lanes_of((CHANNELS, 128)) // CHANNELS
-    folded = None
+    found = None
     for block in range(4):
         start, tile = places[block]
         rows = outer[start : start + CHANNELS, tile * 128 : tile * 128 + 128]
-        folded = rows if folded is None else jnp.where(lane == block, rows, folded)
-    quarter = [folded[8 * q : 8 * q + 8] for q in range(4)]
-    small = lanes_of((8, 128)) // CHANNELS
+        found = rows if found is None else jnp.where(lane == block, rows, found)
+    return found
+
+
+def fold(four):
+    lane = lanes_of((CHANNELS, 128)) // CHANNELS
     total = None
     for turn in range(4):
-        mixed = quarter[0]
-        for q in range(1, 4):
-            mixed = jnp.where(small == (q + turn) % 4, quarter[q], mixed)
+        mixed = four[0]
+        for n in range(1, len(four)):
+            mixed = jnp.where(lane == (n + turn) % 4, four[n], mixed)
         if turn:
             mixed = pltpu.roll(mixed, 128 - turn * CHANNELS, 1)
         total = mixed if total is None else total + mixed
@@ -367,15 +370,21 @@
     gradient = (convolve(cotangent_pad, band_ref) * slope_ref[...]).astype(BF16)
     gradient = jnp.transpose(gradient.astype(F32)).astype(BF16)
     hidden = hidden_ref[...]
-    sums_ref[8 * BLOCKS :] = jnp.zeros((sums_ref.shape[0] - 8 * BLOCKS, 128), F32)
+    if sums_ref.shape[0] > 2 * GROUPS * CHANNELS:
+        rest = sums_ref.shape[0] - 2 * GROUPS * CHANNELS
+        sums_ref[2 * GROUPS * CHANNELS :] = jnp.zeros((rest, 128), F32)
+    ones, twos = [], []
     for k in range(9):
         one = dot(gradient, window(lifted_pad, k))
         two = dot(hidden, window(cotangent_pad, 8 - k))
-        for part in range(3):
-            start = 8 * (3 * k + part)
-            sums_ref[start : start + 8] = fold(one, diagonal(part - 1))
-            start += 8 * 27
-            sums_ref[start : start + 8] = fold(two, diagonal(1 - part))
+        ones += [picked(one, diagonal(part - 1)) for part in range(3)]
+        twos += [picked(two, diagonal(1 - part)) for part in range(3)]
+        while len(ones) >= 4 or (k == 8 and ones):
+            group = (3 * k + 3 - len(ones)) // 4
+            for first, blocks in ((0, ones), (GROUPS, twos)):
+                start = (first + group) * CHANNELS
+                sums_ref[start : start + CHANNELS] = fold(blocks[:4])
+            ones, twos = ones[4:], twos[4:]
     sums_out[...] = sums_ref[...].astype(BF16)
 
 
@@ -411,39 +420,24 @@
         copy.wait()
 
 
-def unpacked(tile):
-    pieces = [tile] + [pltpu.roll(tile, 128 - q * CHANNELS, 1) for q in range(1, 4)]
-    return jnp.concatenate(pieces, axis=0)[:, :CHANNELS]
-
-
-def turned(tiles):
-    lane = lanes_of((8, 128)) // CHANNELS
-    rows = []
-    for q in range(4):
-        mixed = jnp.zeros((8, 128), F32)
-        for n, tile in enumerate(tiles):
-            shift = (n - q) % 4 * CHANNELS
-            mixed = jnp.where(lane == n, pltpu.roll(tile, shift, 1) if shift else tile, mixed)
-        rows.append(mixed)
-    return jnp.transpose(jnp.concatenate(rows, axis=0))
-
-
 def unpack_kernel(sums_ref, fine_ref, one_out, two_out, fine_out, rows_ref, one_ref, two_ref, sems, fine_sem):
     fine_copy = pltpu.make_async_copy(fine_ref, fine_out, fine_sem)
     fine_copy.start()
     rows_ref[...] = sums_ref[...].astype(F32)
-    tiles = [rows_ref[8 * index : 8 * index + 8] for index in range(BLOCKS)]
     copies = []
     for which, (block_ref, out) in ((1, (two_ref, two_out)), (0, (one_ref, one_out))):
-        for part, (first, last) in enumerate(((0, 8), (8, 16), (16, 27))):
-            for index in range(first, last):
-                if which:
-                    block_ref[index] = unpacked(tiles[27 + index])
-                elif index % 4 == 0:
-                    blocks = turned(tiles[index : min(index + 4, 27)])
-                    for n in range(min(4, 27 - index)):
-                        block_ref[index + n] = blocks[CHANNELS * n : CHANNELS * n + CHANNELS]
-            span = pl.ds(first, last - first)
+        for part, (first, last) in enumerate(((0, 2), (2, 4), (4, GROUPS))):
+            for group in range(first, last):
+                start = (which * GROUPS + group) * CHANNELS
+                four = rows_ref[start : start + CHANNELS]
+                turned = None if which else jnp.transpose(four)
+                for n in range(min(4, 27 - 4 * group)):
+                    if which:
+                        block = pltpu.roll(four, 128 - n * CHANNELS, 1) if n else four
+                        block_ref[4 * group + n] = block[:, :CHANNELS]
+                    else:
+                        block_ref[4 * group + n] = turned[CHANNELS * n : CHANNELS * n + CHANNELS]
+            span = pl.ds(4 * first, min(4 * last, 27) - 4 * first)
             copies.append(pltpu.make_async_copy(block_ref.at[span], out.at[span], sems.at[which, part]))
             copies[-1].start()
     for copy in copies:
@@ -537,7 +531,7 @@
         hbm=(0,),
         inputs=4,
     )(face_links, received, up_weight, band_one)
-    share = 2 * -(-4 * BLOCKS // everyone)
+    share = 2 * -(-GROUPS * CHANNELS // everyone)
     packed_rows = (everyone * share, 128)
     sums, lifted = call(
         second_kernel,

time: 44.3 us -> 44.3 us (level)
  no operation moved by 1% of the time
where the time goes in v21:
time: 44.3 us; the launch traced here: 43.9 us
  starting transfers between devices  20.2 us (46%)
  blocking collectives  10.7 us (24%)
  Pallas kernels  7.3 us (16%)
  waiting for transfers between devices  4.9 us (11%)
  between operations  0.8 us (2%)
    all_to_all x1, blocking collectives, exchanged(): lax.all_to_all(shares, ('space', 'dp'), split_axis=0, concat_axis=0, tile...  10.7 us
    ppermute x4, starting transfers between devices, swapped(): lax.ppermute(value, 'space', pairs + [(target, source) for source, target...  10.3 us
    all_to_all x1, starting transfers between devices, body(): lax.all_to_all(packed.reshape(devices * scenes, count, 128), ('space', 'd...  7.3 us
    all_to_all x1, waiting for transfers between devices, body(): lax.all_to_all(packed.reshape(devices * scenes, count, 128), ('space', 'd...  2.88 us
    all_to_all x1, starting transfers between devices, exchanged(): lax.all_to_all(shares, ('space', 'dp'), split_axis=0, concat_axis=0, tile...  2.59 us
    pallas_call x1, Pallas kernels, body(): call(pick_kernel, shape(devices, scenes, count, 128), [pltpu.VMEM((1, bri...  1.74 us
    ppermute x4, waiting for transfers between devices, swapped(): lax.ppermute(value, 'space', pairs + [(target, source) for source, target...  1.71 us
    pallas_call x1, Pallas kernels, body(): call(first_kernel, (shape(ROWS, HALF, dtype=F32), volume, shape(HALF, ROW...  1.09 us
  transfers between devices with their start and end apart: 6, of which 3 were waited for; matrix products, arithmetic and copies ran while one was open for 0% of the time, Pallas kernels for 6%

profile of v21, /device:TPU:0, one launch (start us, length us, event | category | flops | bytes accessed | tf_op | source)
XLA Modules:
  0.0 43.9 jit_solution(9047757014053981337)
XLA Ops:
  0.6 1.7 %shard_map.95 = bf16[16,2,24,128]{3,2,1,0:T(8,128)(2,1)} custom-call(s32[1,32]{1,0:T(1,128)} %ids_hbm.1, bf16[1,64,512]{2,1,0:T(8,128)(2,1)} %latents_hbm.1), custom_call_target="tpu_custom_call" | custom-call | tf_op jit(solution)/shard_map/pallas_call | solution.py:486
  2.4 0.0 copy-start.1
  2.4 0.0 copy-start.3
  2.4 7.3 %all-to-all-start = ((bf16[32,24,128]{2,1,0:T(8,128)(2,1)}), bf16[32,24,128]{2,1,0:T(8,128)(2,1)S(1)}, u32[]{:S(2)}, u32[]{:S(2)}) async-start(bf16[32,24,128]{2,1,0:T(8,128)(2,1)} %bitcast.11), calls=%async_computation | async-start | bytes 393216 | tf_op jit(solution)/shard_map/all_to_all | solution.py:502
  9.7 0.1 shard_map.97
  9.8 0.0 copy-start.2
  9.8 0.7 %collective-permute-start = (bf16[48,256]{1,0:T(8,128)(2,1)S(1)}, bf16[48,256]{1,0:T(8,128)(2,1)S(1)}, u32[]{:S(2)}, u32[]{:S(2)}) collective-permute-start(bf16[48,256]{1,0:T(8,128)(2,1)S(1)} %get-tuple-element.31), channel_id=1, source_target_pairs={{2,4},{6,8},{10,12},{14,16},{18,20},{22,24},{26,28},{4,2},{8,6},{1... | collective-permute-start | bytes 73736 | tf_op jit(solution)/shard_map/ppermute | solution.py:467
  10.5 0.0 copy-start
  10.5 4.5 %collective-permute-start.1 = (bf16[48,256]{1,0:T(8,128)(2,1)S(1)}, bf16[48,256]{1,0:T(8,128)(2,1)S(1)}, u32[]{:S(2)}, u32[]{:S(2)}) collective-permute-start(bf16[48,256]{1,0:T(8,128)(2,1)S(1)} %get-tuple-element.32), channel_id=1, source_target_pairs={{0,2},{4,6},{8,10},{12,14},{16,18},{20,22},{24,26},{28,30},{2,0},{... | collective-permute-start | bytes 73736 | tf_op jit(solution)/shard_map/ppermute | solution.py:467
  15.1 0.7 %shard_map.94 = (bf16[9,256,128]{2,1,0:T(8,128)(2,1)S(1)}, bf16[9,256,128]{2,1,0:T(8,128)(2,1)S(1)}, f32[48,128]{1,0:T(8,128)S(1)}) custom-call(s32[1,2,6]{2,1,0:T(2,128)S(1)} %copy-done.2, bf16[27,32,32]{2,1,0:T(8,128)(2,1)S(1)} %copy-done.3, bf16[27,32,32]{2,1,0:T(8,128)(2,1)S(1)} %copy-done.4), custom_call_target="tpu_custom_call" | custom-call | flops 1000000000 | bytes 2000000 | tf_op jit(solution)/shard_map/pallas_call | solution.py:522
  15.7 2.9 %all-to-all-done = bf16[32,24,128]{2,1,0:T(8,128)(2,1)S(1)} async-done(((bf16[32,24,128]{2,1,0:T(8,128)(2,1)}), bf16[32,24,128]{2,1,0:T(8,128)(2,1)S(1)}, u32[]{:S(2)}, u32[]{:S(2)}) %all-to-all-start) | async-done | bytes 196640 | tf_op jit(solution)/shard_map/all_to_all | solution.py:502
  18.6 1.1 %shard_map.96 = (f32[256,128]{1,0:T(8,128)S(1)}, bf16[256,128]{1,0:T(8,128)(2,1)S(1)}, bf16[128,256]{1,0:T(8,128)(2,1)S(1)}, bf16[3,2,10,16,256]{4,3,2,1,0:T(8,128)(2,1)S(1)}) custom-call(s32[1,2,6]{2,1,0:T(2,128)S(1)} %copy-done.2, bf16[16,2,24,128]{3,2,1,0:T(8,128)(2,1)S(1)} %bitcast.8, bf16[64,2048]{1,0:T(8,128)(2,1)S(1)} %copy-done, ...), custom_call_target="tpu_custom_call" | custom-call | tf_op jit(solution)/shard_map/pallas_call | solution.py:525
  19.7 1.1 %shard_map.98 = (bf16[448,128]{1,0:T(8,128)(2,1)S(1)}, bf16[256,128]{1,0:T(8,128)(2,1)S(1)}) custom-call(f32[48,128]{1,0:T(8,128)S(1)} %get-tuple-element.23.masks_ref, bf16[1,2,8,8,256]{4,3,2,1,0:T(8,128)(2,1)S(1)} %copy-done.1, bf16[9,256,128]{2,1,0:T(8,128)(2,1)S(1)} %get-tuple-element.24.band_ref, f32[256,128]{1,0:T(8,128)S(1)} %get-tuple-element.26.slope_ref, ...), custom_call_target="tpu_custom_call" | custom-call | tf_op jit(solution)/shard_map/pallas_call | solution.py:536
  20.8 10.7 %all_to_all.15 = bf16[32,7,2,128]{3,2,1,0:T(2,128)(2,1)S(1)} all-to-all(bf16[32,7,2,128]{3,2,1,0:T(2,128)(2,1)S(1)} %bitcast.10), channel_id=1, replica_groups=mesh['space'=16,'dp'=2] {'space','dp'}, dimensions={0} | all-to-all | bytes 229376 | tf_op jit(solution)/shard_map/all_to_all | solution.py:473
  31.5 0.7 %shard_map.99 = bf16[448,128]{1,0:T(8,128)(2,1)} custom-call(bf16[448,128]{1,0:T(8,128)(2,1)S(1)} %bitcast.6), custom_call_target="tpu_custom_call" | custom-call | tf_op jit(solution)/shard_map/pallas_call | solution.py:554
  32.2 2.6 %all-to-all-start.2 = ((bf16[32,7,2,128]{3,2,1,0:T(2,128)(2,1)}), bf16[32,7,2,128]{3,2,1,0:T(2,128)(2,1)S(1)}, u32[]{:S(2)}, u32[]{:S(2)}) async-start(bf16[32,7,2,128]{3,2,1,0:T(2,128)(2,1)} %bitcast.4), calls=%async_computation.2 | async-start | bytes 229376 | tf_op jit(solution)/shard_map/all_to_all | solution.py:473
  34.8 0.1 shard_map.101
  34.9 0.7 %collective-permute-start.2 = (bf16[48,256]{1,0:T(8,128)(2,1)S(1)}, bf16[48,256]{1,0:T(8,128)(2,1)S(1)}, u32[]{:S(2)}, u32[]{:S(2)}) collective-permute-start(bf16[48,256]{1,0:T(8,128)(2,1)S(1)} %get-tuple-element.38), channel_id=1, source_target_pairs={{2,4},{6,8},{10,12},{14,16},{18,20},{22,24},{26,28},{4,2},{8,6},{1... | collective-permute-start | bytes 73736 | tf_op jit(solution)/shard_map/ppermute | solution.py:467
  35.6 4.4 %collective-permute-start.3 = (bf16[48,256]{1,0:T(8,128)(2,1)S(1)}, bf16[48,256]{1,0:T(8,128)(2,1)S(1)}, u32[]{:S(2)}, u32[]{:S(2)}) collective-permute-start(bf16[48,256]{1,0:T(8,128)(2,1)S(1)} %get-tuple-element.39), channel_id=1, source_target_pairs={{0,2},{4,6},{8,10},{12,14},{16,18},{20,22},{24,26},{28,30},{2,0},{... | collective-permute-start | bytes 73736 | tf_op jit(solution)/shard_map/ppermute | solution.py:467
  40.0 0.3 shard_map.100.band_ref
  40.3 1.7 %collective-permute-done.3.near = bf16[48,256]{1,0:T(8,128)(2,1)S(1)} collective-permute-done((bf16[48,256]{1,0:T(8,128)(2,1)S(1)}, bf16[48,256]{1,0:T(8,128)(2,1)S(1)}, u32[]{:S(2)}, u32[]{:S(2)}) %collective-permute-start.3) | collective-permute-done | bytes 24608 | tf_op jit(solution)/shard_map/ppermute | solution.py:467
  42.1 0.5 %shard_map.102.fine_ref = bf16[1,2,8,8,256]{4,3,2,1,0:T(8,128)(2,1)S(1)} custom-call(f32[48,128]{1,0:T(8,128)S(1)} %get-tuple-element.23.masks_ref, bf16[9,256,128]{2,1,0:T(8,128)(2,1)S(1)} %shard_map.100.band_ref, bf16[256,128]{1,0:T(8,128)(2,1)S(1)} %get-tuple-element.34.lifted_ref, bf16[256,128]{1,0:T(8,128)(2,1)S(1)} %get-tuple-element.35.hidden_ref, ...), custom_call_target="tpu_custom_call" | custom-call | flops 1000000000 | bytes 2000000 | tf_op jit(solution)/shard_map/pallas_call | solution.py:549
  42.5 0.3 all-to-all-done.2
  42.8 1.1 %shard_map.103 = (f32[27,32,32]{2,1,0:T(8,128)}, f32[27,32,32]{2,1,0:T(8,128)}, bf16[1,2,8,8,256]{4,3,2,1,0:T(8,128)(2,1)}) custom-call(bf16[448,128]{1,0:T(8,128)(2,1)S(1)} %bitcast.9, bf16[1,2,8,8,256]{4,3,2,1,0:T(8,128)(2,1)S(1)} %shard_map.102.fine_ref), custom_call_target="tpu_custom_call" | custom-call | tf_op jit(solution)/shard_map/pallas_call | solution.py:569
  (9 shorter events, 0.0 us)
Async XLA Ops:
  0.6 14.4 %copy-start.4 = (bf16[27,32,32]{2,1,0:T(8,128)(2,1)S(1)}, bf16[27,32,32]{2,1,0:T(8,128)(2,1)}, u32[]{:S(2)}) copy-start(bf16[27,32,32]{2,1,0:T(8,128)(2,1)} %weights_ref.1) | copy-start | bytes 165892
  2.4 7.3 %copy-start.1 = (bf16[1,2,8,8,256]{4,3,2,1,0:T(8,128)(2,1)S(1)}, bf16[1,2,8,8,256]{4,3,2,1,0:T(8,128)(2,1)}, u32[]{:S(2)}) copy-start(bf16[1,2,8,8,256]{4,3,2,1,0:T(8,128)(2,1)} %cotangent_ref.3) | copy-start | bytes 196612
  2.4 12.7 %copy-start.3 = (bf16[27,32,32]{2,1,0:T(8,128)(2,1)S(1)}, bf16[27,32,32]{2,1,0:T(8,128)(2,1)}, u32[]{:S(2)}) copy-start(bf16[27,32,32]{2,1,0:T(8,128)(2,1)} %one_ref.1) | copy-start | bytes 165892
  2.4 16.2 %all-to-all-start = ((bf16[32,24,128]{2,1,0:T(8,128)(2,1)}), bf16[32,24,128]{2,1,0:T(8,128)(2,1)S(1)}, u32[]{:S(2)}, u32[]{:S(2)}) async-start(bf16[32,24,128]{2,1,0:T(8,128)(2,1)} %bitcast.11), calls=%async_computation | async-start | bytes 393216 | tf_op jit(solution)/shard_map/all_to_all | solution.py:502
  9.8 5.2 %copy-start.2 = (s32[1,2,6]{2,1,0:T(2,128)S(1)}, s32[1,2,6]{2,1,0:T(2,128)}, u32[]{:S(2)}) copy-start(s32[1,2,6]{2,1,0:T(2,128)} %links_in.3) | copy-start | bytes 148
  9.8 9.9 %collective-permute-start = (bf16[48,256]{1,0:T(8,128)(2,1)S(1)}, bf16[48,256]{1,0:T(8,128)(2,1)S(1)}, u32[]{:S(2)}, u32[]{:S(2)}) collective-permute-start(bf16[48,256]{1,0:T(8,128)(2,1)S(1)} %get-tuple-element.31), channel_id=1, source_target_pairs={{2,4},{6,8},{10,12},{14,16},{18,20},{22,24},{26,28},{4,2},{8,6},{1... | collective-permute-start | bytes 73736 | tf_op jit(solution)/shard_map/ppermute | solution.py:467
  10.5 8.1 %copy-start = (bf16[64,2048]{1,0:T(8,128)(2,1)S(1)}, bf16[64,2048]{1,0:T(8,128)(2,1)}, u32[]{:S(2)}) copy-start(bf16[64,2048]{1,0:T(8,128)(2,1)} %up_ref.1) | copy-start | bytes 786436
  10.5 9.2 %collective-permute-start.1 = (bf16[48,256]{1,0:T(8,128)(2,1)S(1)}, bf16[48,256]{1,0:T(8,128)(2,1)S(1)}, u32[]{:S(2)}, u32[]{:S(2)}) collective-permute-start(bf16[48,256]{1,0:T(8,128)(2,1)S(1)} %get-tuple-element.32), channel_id=1, source_target_pairs={{0,2},{4,6},{8,10},{12,14},{16,18},{20,22},{24,26},{28,30},{2,0},{... | collective-permute-start | bytes 73736 | tf_op jit(solution)/shard_map/ppermute | solution.py:467
  32.2 10.6 %all-to-all-start.2 = ((bf16[32,7,2,128]{3,2,1,0:T(2,128)(2,1)}), bf16[32,7,2,128]{3,2,1,0:T(2,128)(2,1)S(1)}, u32[]{:S(2)}, u32[]{:S(2)}) async-start(bf16[32,7,2,128]{3,2,1,0:T(2,128)(2,1)} %bitcast.4), calls=%async_computation.2 | async-start | bytes 229376 | tf_op jit(solution)/shard_map/all_to_all | solution.py:473
  34.9 5.4 %collective-permute-start.2 = (bf16[48,256]{1,0:T(8,128)(2,1)S(1)}, bf16[48,256]{1,0:T(8,128)(2,1)S(1)}, u32[]{:S(2)}, u32[]{:S(2)}) collective-permute-start(bf16[48,256]{1,0:T(8,128)(2,1)S(1)} %get-tuple-element.38), channel_id=1, source_target_pairs={{2,4},{6,8},{10,12},{14,16},{18,20},{22,24},{26,28},{4,2},{8,6},{1... | collective-permute-start | bytes 73736 | tf_op jit(solution)/shard_map/ppermute | solution.py:467
  35.6 6.5 %collective-permute-start.3 = (bf16[48,256]{1,0:T(8,128)(2,1)S(1)}, bf16[48,256]{1,0:T(8,128)(2,1)S(1)}, u32[]{:S(2)}, u32[]{:S(2)}) collective-permute-start(bf16[48,256]{1,0:T(8,128)(2,1)S(1)} %get-tuple-element.39), channel_id=1, source_target_pairs={{0,2},{4,6},{8,10},{12,14},{16,18},{20,22},{24,26},{28,30},{2,0},{... | collective-permute-start | bytes 73736 | tf_op jit(solution)/shard_map/ppermute | solution.py:467

commit v22 on v21

--- a/solution.py
+++ b/solution.py
@@ -41,48 +41,57 @@
     return lax.broadcasted_iota(jnp.int32, shape, len(shape) - 1)
 
 
-def scene_of(blocks_ref):
-    return lax.axis_index("dp") if blocks_ref.shape[1] > 1 else 0
-
-
-def pick_kernel(ids_hbm, latents_hbm, out_hbm, ids_ref, latents_ref, rows_ref, blocks_ref, zeros_ref, sems):
+def first_half(split):
+    return lax.axis_index("dp") if split else 0
+
+
+def pick_kernel(split, ids_hbm, latents_hbm, out_ref, ids_ref, latents_ref, rows_ref, blocks_ref, sems):
     ids_copy = pltpu.make_async_copy(ids_hbm, ids_ref, sems.at[0])
+    latents_copy = pltpu.make_async_copy(latents_hbm, latents_ref, sems.at[1])
     ids_copy.start()
+    latents_copy.start()
     held, width = latents_ref.shape[1:]
-    copies = []
-    for i in range(4):
-        part = pl.ds(i * held // 4, held // 4)
-        copies.append(pltpu.make_async_copy(latents_hbm.at[0, part], latents_ref.at[0, part], sems.at[1 + i]))
-        copies[-1].start()
-    scene = scene_of(out_hbm)
-    others = None
-    if out_hbm.shape[1] > 1:
-        zeros_ref[...] = jnp.zeros(zeros_ref.shape, BF16)
-        others = pltpu.make_async_copy(zeros_ref, out_hbm.at[:, 1 - scene], sems.at[5])
-        others.start()
     bricks = ids_ref.shape[1]
-    margin = 8 * width // 128
-    tiles = width // 128
-    rows_ref[0:margin] = jnp.zeros((margin, 128), F32)
-    rows_ref[margin + bricks * tiles :] = jnp.zeros((margin, 128), F32)
+    tiles = width // 256
+    margin = 8 * tiles
+    empty = jnp.zeros((margin, 128), F32)
+    for half in range(2):
+        rows_ref[half, 0:margin] = empty
+        rows_ref[half, margin + bricks * tiles :] = empty
     first = lax.axis_index("space") * held
     rows = lax.broadcasted_iota(jnp.int32, (held, bricks), 0) + first
     ids_copy.wait()
     hot = jnp.where(rows == ids_ref[...], 1.0, 0.0).astype(BF16)
-    for copy in copies:
-        copy.wait()
+    latents_copy.wait()
     picked = dot_rows(hot, latents_ref[0])
-    for tile in range(tiles):
-        rows_ref[pl.ds(margin + tile, bricks, stride=tiles), :] = picked[:, tile * 128 : tile * 128 + 128]
-    count = blocks_ref.shape[1]
-    for receiver in range(blocks_ref.shape[0]):
+    for tile in range(2 * tiles):
+        place = pl.ds(margin + tile % tiles, bricks, stride=tiles)
+        rows_ref[tile // tiles, place, :] = picked[:, tile * 128 : tile * 128 + 128]
+    count = 3 * BRICKS * tiles
+    straight = first_half(split) == 0
+    for receiver in range(blocks_ref.shape[0] // (2 * count)):
         start = margin + BRICKS * (receiver - 1) * tiles
-        blocks_ref[receiver] = rows_ref[start : start + count].astype(BF16)
-    found = pltpu.make_async_copy(blocks_ref, out_hbm.at[:, scene], sems.at[6])
-    found.start()
-    found.wait()
-    if others is not None:
-        others.wait()
+        halves = [rows_ref[half, start : start + count] for half in range(2)]
+        for half in range(2):
+            block = jnp.where(straight, halves[half], halves[1 - half]) if split else halves[half]
+            place = (2 * receiver + half) * count
+            blocks_ref[place : place + count] = block
+    out_ref[...] = blocks_ref[...].astype(BF16)
+
+
+def relay_kernel(split, received_ref, own_out, other_out, rows_ref):
+    rows_ref[...] = received_ref[...].astype(F32)
+    count = own_out.shape[0] * 3 // 4
+    sums = []
+    for half in range(2):
+        total = None
+        for start in range(half * count, rows_ref.shape[0], 2 * count):
+            piece = rows_ref[start : start + count]
+            total = piece if total is None else total + piece
+        sums.append(jnp.concatenate([total, jnp.zeros((count // 3, 128), F32)], axis=0))
+    straight = first_half(split) == 0
+    own_out[...] = jnp.where(straight, sums[0], sums[1]).astype(BF16)
+    other_out[...] = jnp.where(straight, sums[1], sums[0]).astype(BF16)
 
 
 def build_band(band_ref, rows):
@@ -227,21 +236,20 @@
 
 
 def first_kernel(
-    links_in, received_ref, up_ref, band_ref,
+    links_in, own_ref, other_ref, up_ref, band_ref,
     slope_out, hidden_out, turned_out, pad_out,
     volumes_ref, rows_ref, links_ref, links_sem,
 ):
     links_copy = pltpu.make_async_copy(links_in, links_ref, links_sem)
     links_copy.start()
     position = lax.axis_index("space")
-    tiles = received_ref.shape[2] // (3 * BRICKS)
-    received = received_ref[:, pl.ds(scene_of(received_ref), 1)]
-    rows_ref[0 : 3 * BRICKS * tiles] = jnp.sum(received.astype(F32), axis=(0, 1))
-    rows_ref[3 * BRICKS * tiles :] = jnp.zeros((2 * tiles, 128), F32)
     cells = []
-    for tile in range(tiles):
-        rows = rows_ref[pl.ds(tile, 8, stride=tiles), :]
-        cells += [rows[:, :64], rows[:, 64:]]
+    for half, half_ref in enumerate((own_ref, other_ref)):
+        tiles = half_ref.shape[0] // 8
+        rows_ref[half] = half_ref[...].astype(F32)
+        for tile in range(tiles):
+            rows = rows_ref[half, pl.ds(tile, 8, stride=tiles), :]
+            cells += [rows[:, :64], rows[:, 64:]]
     lifted = dot(jnp.concatenate(cells, axis=0).astype(BF16), up_ref[...])
     lifted = lifted.astype(BF16).astype(F32)
     for cell in range(8):
@@ -467,10 +475,10 @@
     return lax.ppermute(value, "space", pairs + [(target, source) for source, target in pairs])
 
 
-def exchanged(rows):
-    everyone = lax.axis_size("space") * lax.axis_size("dp")
-    shares = rows.reshape(everyone, -1, 2, 128)
-    shares = lax.all_to_all(shares, ("space", "dp"), split_axis=0, concat_axis=0, tiled=True)
+def exchanged(rows, axes=("space", "dp")):
+    count = math.prod(lax.axis_size(axis) for axis in axes)
+    shares = rows.reshape(count, -1, 2, 128)
+    shares = lax.all_to_all(shares, axes, split_axis=0, concat_axis=0, tiled=True)
     return shares.reshape(rows.shape)
 
 
@@ -479,33 +487,31 @@
     everyone = devices * lax.axis_size("dp")
     held, width = coarse_latents.shape[1:]
     bricks = active_blocks.shape[1]
-    tiles = width // 128
-    scenes = 2 if lax.axis_size("dp") == 2 else 1
+    split = lax.axis_size("dp") == 2
+    tiles = width // 256
     count = 3 * BRICKS * tiles
-    blocks = pltpu.VMEM((devices, count, 128), BF16)
+    blocks = (2 * devices * count, 128)
     packed = call(
-        pick_kernel,
-        shape(devices, scenes, count, 128),
+        functools.partial(pick_kernel, split),
+        shape(*blocks),
         [
             pltpu.VMEM((1, bricks), jnp.int32),
             pltpu.VMEM((1, held, width), BF16),
-            pltpu.VMEM(((bricks + 16) * tiles, 128), F32),
-            blocks,
-            blocks,
-            pltpu.SemaphoreType.DMA((7,)),
+            pltpu.VMEM((2, (bricks + 16) * tiles, 128), F32),
+            pltpu.VMEM(blocks, F32),
+            pltpu.SemaphoreType.DMA((2,)),
         ],
         hbm=(0, 1),
         inputs=2,
         limit=60,
-        out=pl.ANY,
     )(active_blocks, coarse_latents)
-    received = lax.all_to_all(
-        packed.reshape(devices * scenes, count, 128),
-        ("space", "dp") if scenes == 2 else "space",
-        split_axis=0,
-        concat_axis=0,
-        tiled=True,
-    ).reshape(packed.shape)
+    received = exchanged(packed, ("space", "dp") if split else ("space",))
+    window_half = shape(8 * tiles, 128)
+    own, other = call(
+        functools.partial(relay_kernel, split), (window_half, window_half), [pltpu.VMEM(blocks, F32)]
+    )(received)
+    if split:
+        other = lax.ppermute(other, "dp", [(0, 1), (1, 0)])
     cost = pl.CostEstimate(flops=10**9, bytes_accessed=2 * 10**6, transcendentals=0)
     face = shape(BRICKS * FACE, LINE)
     halves = pltpu.VMEM((2, LINES, HALF), F32)
@@ -527,10 +533,10 @@
         (
             shape(ROWS, HALF, dtype=F32), volume, shape(HALF, ROWS), shape(*pad_shape),
         ),
-        [pltpu.VMEM((2, 8 * CUBE, 128), F32), pltpu.VMEM((8 * tiles, 128), F32), *links],
+        [pltpu.VMEM((2, 8 * CUBE, 128), F32), pltpu.VMEM((2, 8 * tiles, 128), F32), *links],
         hbm=(0,),
-        inputs=4,
-    )(face_links, received, up_weight, band_one)
+        inputs=5,
+    )(face_links, own, other, up_weight, band_one)
     share = 2 * -(-GROUPS * CHANNELS // everyone)
     packed_rows = (everyone * share, 128)
     sums, lifted = call(

time: 44.3 us -> 43.8 us (0.989)
  blocking collectives: 10.7 us -> 10 us
  local copies, waits for them, and re-layouts: 0.03 us -> 0.5 us
    all_to_all x1, blocking collectives: 10.7 us -> 10 us  [exchanged(): lax.all_to_all(shares, axes, split_axis=0, concat_axis=0, tiled=True)]
    unnamed x10, local copies, waits for them, and re-layouts: 0.03 us -> 0.5 us
    pallas_call x1 -> x2, Pallas kernels: 1.74 us -> 1.79 us  [the longest x1 1.76 us: body(): call(functools.partial(pick_kernel, split), shape(*blocks), [pltpu.VMEM((...]
  transfers between devices with their start and end apart: 6 -> 7, of which waited for: 3 -> 3; matrix products, arithmetic and copies ran while one was open for 0% -> 0% of each run, Pallas kernels for 6% -> 6%
where the time goes in v22:
time: 43.8 us; the launch traced here: 43.6 us
  starting transfers between devices  20.4 us (47%)
  blocking collectives  10 us (23%)
  Pallas kernels  7.34 us (17%)
  waiting for transfers between devices  4.53 us (10%)
  between operations  0.82 us (2%)
  local copies, waits for them, and re-layouts  0.5 us (1%)
    ppermute x4, starting transfers between devices, swapped(): lax.ppermute(value, 'space', pairs + [(target, source) for source, target...  10.3 us
    all_to_all x1, blocking collectives, exchanged(): lax.all_to_all(shares, axes, split_axis=0, concat_axis=0, tiled=True)  10 us
    all_to_all x2, starting transfers between devices, exchanged(): lax.all_to_all(shares, axes, split_axis=0, concat_axis=0, tiled=True)  9.89 us
    all_to_all x2, waiting for transfers between devices, exchanged(): lax.all_to_all(shares, axes, split_axis=0, concat_axis=0, tiled=True)  2.81 us
    pallas_call x1, Pallas kernels, body(): call(functools.partial(pick_kernel, split), shape(*blocks), [pltpu.VMEM((...  1.76 us
    ppermute x4, waiting for transfers between devices, swapped(): lax.ppermute(value, 'space', pairs + [(target, source) for source, target...  1.71 us
    pallas_call x1, Pallas kernels, body(): call(first_kernel, (shape(ROWS, HALF, dtype=F32), volume, shape(HALF, ROW...  1.09 us
    pallas_call x1, Pallas kernels, body(): call(second_kernel, (shape(*packed_rows), volume), [pool, pool, pad, pltp...  1.07 us
  transfers between devices with their start and end apart: 7, of which 3 were waited for; matrix products, arithmetic and copies ran while one was open for 0% of the time, Pallas kernels for 6%

profile of v22, /device:TPU:0, one launch (start us, length us, event | category | flops | bytes accessed | tf_op | source)
XLA Modules:
  0.0 43.6 jit_solution(12469480727018793914)
XLA Ops:
  0.6 1.8 %shard_map.95 = bf16[384,128]{1,0:T(8,128)(2,1)} custom-call(s32[1,32]{1,0:T(1,128)} %ids_hbm.1, bf16[1,64,512]{2,1,0:T(8,128)(2,1)} %latents_hbm.1), custom_call_target="tpu_custom_call" | custom-call | tf_op jit(solution)/shard_map/pallas_call | solution.py:494
  2.4 0.0 copy-start
  2.4 0.0 copy-start.3
  2.4 7.3 %all-to-all-start = ((bf16[32,6,2,128]{3,2,1,0:T(2,128)(2,1)}), bf16[32,6,2,128]{3,2,1,0:T(2,128)(2,1)S(1)}, u32[]{:S(2)}, u32[]{:S(2)}) async-start(bf16[32,6,2,128]{3,2,1,0:T(2,128)(2,1)} %bitcast.11), calls=%async_computation | async-start | bytes 196608 | tf_op jit(solution)/shard_map/all_to_all | solution.py:481
  9.8 0.1 shard_map.98
  9.8 0.7 %collective-permute-start.1 = (bf16[48,256]{1,0:T(8,128)(2,1)S(1)}, bf16[48,256]{1,0:T(8,128)(2,1)S(1)}, u32[]{:S(2)}, u32[]{:S(2)}) collective-permute-start(bf16[48,256]{1,0:T(8,128)(2,1)S(1)} %get-tuple-element.35), channel_id=1, source_target_pairs={{2,4},{6,8},{10,12},{14,16},{18,20},{22,24},{26,28},{4,2},{8,6},{1... | collective-permute-start | bytes 73736 | tf_op jit(solution)/shard_map/ppermute | solution.py:475
  10.5 4.5 %collective-permute-start.2 = (bf16[48,256]{1,0:T(8,128)(2,1)S(1)}, bf16[48,256]{1,0:T(8,128)(2,1)S(1)}, u32[]{:S(2)}, u32[]{:S(2)}) collective-permute-start(bf16[48,256]{1,0:T(8,128)(2,1)S(1)} %get-tuple-element.36), channel_id=1, source_target_pairs={{0,2},{4,6},{8,10},{12,14},{16,18},{20,22},{24,26},{28,30},{2,0},{... | collective-permute-start | bytes 73736 | tf_op jit(solution)/shard_map/ppermute | solution.py:475
  15.1 2.5 %all-to-all-done = bf16[32,6,2,128]{3,2,1,0:T(2,128)(2,1)S(1)} async-done(((bf16[32,6,2,128]{3,2,1,0:T(2,128)(2,1)}), bf16[32,6,2,128]{3,2,1,0:T(2,128)(2,1)S(1)}, u32[]{:S(2)}, u32[]{:S(2)}) %all-to-all-start) | async-done | bytes 98336 | tf_op jit(solution)/shard_map/all_to_all | solution.py:481
  17.6 0.2 collective-permute-start
  17.8 0.5 %copy-done.2 = s32[1,2,6]{2,1,0:T(2,128)S(1)} copy-done((s32[1,2,6]{2,1,0:T(2,128)S(1)}, s32[1,2,6]{2,1,0:T(2,128)}, u32[]{:S(2)}) %copy-start.2) | copy-done | bytes 72
  18.3 0.6 %shard_map.94 = (bf16[9,256,128]{2,1,0:T(8,128)(2,1)S(1)}, bf16[9,256,128]{2,1,0:T(8,128)(2,1)S(1)}, f32[48,128]{1,0:T(8,128)S(1)}) custom-call(s32[1,2,6]{2,1,0:T(2,128)S(1)} %copy-done.2, bf16[27,32,32]{2,1,0:T(8,128)(2,1)S(1)} %copy-done.3, bf16[27,32,32]{2,1,0:T(8,128)(2,1)S(1)} %copy-done.4), custom_call_target="tpu_custom_call" | custom-call | flops 1000000000 | bytes 2000000 | tf_op jit(solution)/shard_map/pallas_call | solution.py:528
  18.9 1.1 %shard_map.97 = (f32[256,128]{1,0:T(8,128)S(1)}, bf16[256,128]{1,0:T(8,128)(2,1)S(1)}, bf16[128,256]{1,0:T(8,128)(2,1)S(1)}, bf16[3,2,10,16,256]{4,3,2,1,0:T(8,128)(2,1)S(1)}) custom-call(s32[1,2,6]{2,1,0:T(2,128)S(1)} %copy-done.2, bf16[16,128]{1,0:T(8,128)(2,1)S(1)} %get-tuple-element.27.own_ref, bf16[16,128]{1,0:T(8,128)(2,1)S(1)} %collective-permute-done.other_ref, ...), custom_call_target="tpu_custom_call" | custom-call | tf_op jit(solution)/shard_map/pallas_call | solution.py:531
  20.1 1.1 %shard_map.99 = (bf16[448,128]{1,0:T(8,128)(2,1)S(1)}, bf16[256,128]{1,0:T(8,128)(2,1)S(1)}) custom-call(f32[48,128]{1,0:T(8,128)S(1)} %get-tuple-element.25.masks_ref, bf16[1,2,8,8,256]{4,3,2,1,0:T(8,128)(2,1)S(1)} %copy-done, bf16[9,256,128]{2,1,0:T(8,128)(2,1)S(1)} %get-tuple-element.26.band_ref, f32[256,128]{1,0:T(8,128)S(1)} %get-tuple-element.30.slope_ref, ...), custom_call_target="tpu_custom_call" | custom-call | tf_op jit(solution)/shard_map/pallas_call | solution.py:542
  21.1 10.0 %all_to_all.15 = bf16[32,7,2,128]{3,2,1,0:T(2,128)(2,1)S(1)} all-to-all(bf16[32,7,2,128]{3,2,1,0:T(2,128)(2,1)S(1)} %bitcast.10), channel_id=1, replica_groups=mesh['space'=16,'dp'=2] {'space','dp'}, dimensions={0} | all-to-all | bytes 229376 | tf_op jit(solution)/shard_map/all_to_all | solution.py:481
  31.1 0.7 %shard_map.100 = bf16[448,128]{1,0:T(8,128)(2,1)} custom-call(bf16[448,128]{1,0:T(8,128)(2,1)S(1)} %bitcast.6), custom_call_target="tpu_custom_call" | custom-call | tf_op jit(solution)/shard_map/pallas_call | solution.py:560
  31.9 2.6 %all-to-all-start.2 = ((bf16[32,7,2,128]{3,2,1,0:T(2,128)(2,1)}), bf16[32,7,2,128]{3,2,1,0:T(2,128)(2,1)S(1)}, u32[]{:S(2)}, u32[]{:S(2)}) async-start(bf16[32,7,2,128]{3,2,1,0:T(2,128)(2,1)} %bitcast.4), calls=%async_computation.2 | async-start | bytes 229376 | tf_op jit(solution)/shard_map/all_to_all | solution.py:481
  34.5 0.1 shard_map.102
  34.6 0.7 %collective-permute-start.3 = (bf16[48,256]{1,0:T(8,128)(2,1)S(1)}, bf16[48,256]{1,0:T(8,128)(2,1)S(1)}, u32[]{:S(2)}, u32[]{:S(2)}) collective-permute-start(bf16[48,256]{1,0:T(8,128)(2,1)S(1)} %get-tuple-element.42), channel_id=1, source_target_pairs={{2,4},{6,8},{10,12},{14,16},{18,20},{22,24},{26,28},{4,2},{8,6},{1... | collective-permute-start | bytes 73736 | tf_op jit(solution)/shard_map/ppermute | solution.py:475
  35.2 4.4 %collective-permute-start.4 = (bf16[48,256]{1,0:T(8,128)(2,1)S(1)}, bf16[48,256]{1,0:T(8,128)(2,1)S(1)}, u32[]{:S(2)}, u32[]{:S(2)}) collective-permute-start(bf16[48,256]{1,0:T(8,128)(2,1)S(1)} %get-tuple-element.43), channel_id=1, source_target_pairs={{0,2},{4,6},{8,10},{12,14},{16,18},{20,22},{24,26},{28,30},{2,0},{... | collective-permute-start | bytes 73736 | tf_op jit(solution)/shard_map/ppermute | solution.py:475
  39.7 0.3 shard_map.101.band_ref
  40.0 1.7 %collective-permute-done.4.near = bf16[48,256]{1,0:T(8,128)(2,1)S(1)} collective-permute-done((bf16[48,256]{1,0:T(8,128)(2,1)S(1)}, bf16[48,256]{1,0:T(8,128)(2,1)S(1)}, u32[]{:S(2)}, u32[]{:S(2)}) %collective-permute-start.4) | collective-permute-done | bytes 24608 | tf_op jit(solution)/shard_map/ppermute | solution.py:475
  41.7 0.5 %shard_map.103.fine_ref = bf16[1,2,8,8,256]{4,3,2,1,0:T(8,128)(2,1)S(1)} custom-call(f32[48,128]{1,0:T(8,128)S(1)} %get-tuple-element.25.masks_ref, bf16[9,256,128]{2,1,0:T(8,128)(2,1)S(1)} %shard_map.101.band_ref, bf16[256,128]{1,0:T(8,128)(2,1)S(1)} %get-tuple-element.38.lifted_ref, bf16[256,128]{1,0:T(8,128)(2,1)S(1)} %get-tuple-element.39.hidden_ref, ...), custom_call_target="tpu_custom_call" | custom-call | flops 1000000000 | bytes 2000000 | tf_op jit(solution)/shard_map/pallas_call | solution.py:555
  42.2 0.3 all-to-all-done.2
  42.5 1.1 %shard_map.104 = (f32[27,32,32]{2,1,0:T(8,128)}, f32[27,32,32]{2,1,0:T(8,128)}, bf16[1,2,8,8,256]{4,3,2,1,0:T(8,128)(2,1)}) custom-call(bf16[448,128]{1,0:T(8,128)(2,1)S(1)} %bitcast.8, bf16[1,2,8,8,256]{4,3,2,1,0:T(8,128)(2,1)S(1)} %shard_map.103.fine_ref), custom_call_target="tpu_custom_call" | custom-call | tf_op jit(solution)/shard_map/pallas_call | solution.py:575
  (12 shorter events, 0.1 us)
Async XLA Ops:
  0.6 17.2 %copy-start.4 = (bf16[27,32,32]{2,1,0:T(8,128)(2,1)S(1)}, bf16[27,32,32]{2,1,0:T(8,128)(2,1)}, u32[]{:S(2)}) copy-start(bf16[27,32,32]{2,1,0:T(8,128)(2,1)} %weights_ref.1) | copy-start | bytes 165892
  2.4 7.3 %copy-start = (bf16[1,2,8,8,256]{4,3,2,1,0:T(8,128)(2,1)S(1)}, bf16[1,2,8,8,256]{4,3,2,1,0:T(8,128)(2,1)}, u32[]{:S(2)}) copy-start(bf16[1,2,8,8,256]{4,3,2,1,0:T(8,128)(2,1)} %cotangent_ref.3) | copy-start | bytes 196612
  2.4 15.4 %copy-start.3 = (bf16[27,32,32]{2,1,0:T(8,128)(2,1)S(1)}, bf16[27,32,32]{2,1,0:T(8,128)(2,1)}, u32[]{:S(2)}) copy-start(bf16[27,32,32]{2,1,0:T(8,128)(2,1)} %one_ref.1) | copy-start | bytes 165892
  2.4 15.1 %all-to-all-start = ((bf16[32,6,2,128]{3,2,1,0:T(2,128)(2,1)}), bf16[32,6,2,128]{3,2,1,0:T(2,128)(2,1)S(1)}, u32[]{:S(2)}, u32[]{:S(2)}) async-start(bf16[32,6,2,128]{3,2,1,0:T(2,128)(2,1)} %bitcast.11), calls=%async_computation | async-start | bytes 196608 | tf_op jit(solution)/shard_map/all_to_all | solution.py:481
  9.8 10.2 %collective-permute-start.1 = (bf16[48,256]{1,0:T(8,128)(2,1)S(1)}, bf16[48,256]{1,0:T(8,128)(2,1)S(1)}, u32[]{:S(2)}, u32[]{:S(2)}) collective-permute-start(bf16[48,256]{1,0:T(8,128)(2,1)S(1)} %get-tuple-element.35), channel_id=1, source_target_pairs={{2,4},{6,8},{10,12},{14,16},{18,20},{22,24},{26,28},{4,2},{8,6},{1... | collective-permute-start | bytes 73736 | tf_op jit(solution)/shard_map/ppermute | solution.py:475
  10.5 9.5 %collective-permute-start.2 = (bf16[48,256]{1,0:T(8,128)(2,1)S(1)}, bf16[48,256]{1,0:T(8,128)(2,1)S(1)}, u32[]{:S(2)}, u32[]{:S(2)}) collective-permute-start(bf16[48,256]{1,0:T(8,128)(2,1)S(1)} %get-tuple-element.36), channel_id=1, source_target_pairs={{0,2},{4,6},{8,10},{12,14},{16,18},{20,22},{24,26},{28,30},{2,0},{... | collective-permute-start | bytes 73736 | tf_op jit(solution)/shard_map/ppermute | solution.py:475
  17.6 0.7 %copy-start.2 = (s32[1,2,6]{2,1,0:T(2,128)S(1)}, s32[1,2,6]{2,1,0:T(2,128)}, u32[]{:S(2)}) copy-start(s32[1,2,6]{2,1,0:T(2,128)} %links_in.3) | copy-start | bytes 148
  17.6 1.3 %copy-start.1 = (bf16[64,2048]{1,0:T(8,128)(2,1)S(1)}, bf16[64,2048]{1,0:T(8,128)(2,1)}, u32[]{:S(2)}) copy-start(bf16[64,2048]{1,0:T(8,128)(2,1)} %up_ref.1) | copy-start | bytes 786436
  17.6 1.3 %collective-permute-start = (bf16[16,128]{1,0:T(8,128)(2,1)S(1)}, bf16[16,128]{1,0:T(8,128)(2,1)S(1)}, u32[]{:S(2)}, u32[]{:S(2)}) collective-permute-start(bf16[16,128]{1,0:T(8,128)(2,1)S(1)} %get-tuple-element.28), channel_id=1, source_target_pairs={{0,1},{1,0},{2,3},{3,2},{4,5},{5,4},{6,7},{7,6},{8,9},{9,8},{10,11... | collective-permute-start | bytes 12296 | tf_op jit(solution)/shard_map/ppermute | solution.py:514
  31.9 10.6 %all-to-all-start.2 = ((bf16[32,7,2,128]{3,2,1,0:T(2,128)(2,1)}), bf16[32,7,2,128]{3,2,1,0:T(2,128)(2,1)S(1)}, u32[]{:S(2)}, u32[]{:S(2)}) async-start(bf16[32,7,2,128]{3,2,1,0:T(2,128)(2,1)} %bitcast.4), calls=%async_computation.2 | async-start | bytes 229376 | tf_op jit(solution)/shard_map/all_to_all | solution.py:481
  34.6 5.4 %collective-permute-start.3 = (bf16[48,256]{1,0:T(8,128)(2,1)S(1)}, bf16[48,256]{1,0:T(8,128)(2,1)S(1)}, u32[]{:S(2)}, u32[]{:S(2)}) collective-permute-start(bf16[48,256]{1,0:T(8,128)(2,1)S(1)} %get-tuple-element.42), channel_id=1, source_target_pairs={{2,4},{6,8},{10,12},{14,16},{18,20},{22,24},{26,28},{4,2},{8,6},{1... | collective-permute-start | bytes 73736 | tf_op jit(solution)/shard_map/ppermute | solution.py:475
  35.2 6.5 %collective-permute-start.4 = (bf16[48,256]{1,0:T(8,128)(2,1)S(1)}, bf16[48,256]{1,0:T(8,128)(2,1)S(1)}, u32[]{:S(2)}, u32[]{:S(2)}) collective-permute-start(bf16[48,256]{1,0:T(8,128)(2,1)S(1)} %get-tuple-element.43), channel_id=1, source_target_pairs={{0,2},{4,6},{8,10},{12,14},{16,18},{20,22},{24,26},{28,30},{2,0},{... | collective-permute-start | bytes 73736 | tf_op jit(solution)/shard_map/ppermute | solution.py:475

commit v23 on v22

--- a/solution.py
+++ b/solution.py
@@ -79,7 +79,7 @@
     out_ref[...] = blocks_ref[...].astype(BF16)
 
 
-def relay_kernel(split, received_ref, own_out, other_out, rows_ref):
+def relay_kernel(split, received_ref, _masks, own_out, other_out, rows_ref):
     rows_ref[...] = received_ref[...].astype(F32)
     count = own_out.shape[0] * 3 // 4
     sums = []
@@ -507,11 +507,6 @@
     )(active_blocks, coarse_latents)
     received = exchanged(packed, ("space", "dp") if split else ("space",))
     window_half = shape(8 * tiles, 128)
-    own, other = call(
-        functools.partial(relay_kernel, split), (window_half, window_half), [pltpu.VMEM(blocks, F32)]
-    )(received)
-    if split:
-        other = lax.ppermute(other, "dp", [(0, 1), (1, 0)])
     cost = pl.CostEstimate(flops=10**9, bytes_accessed=2 * 10**6, transcendentals=0)
     face = shape(BRICKS * FACE, LINE)
     halves = pltpu.VMEM((2, LINES, HALF), F32)
@@ -528,6 +523,15 @@
     band_one, band_back, masks = call(
         masks_kernel, (shape(*BAND), shape(*BAND), masks), links, hbm=(0,), inputs=3, cost=cost
     )(face_links, conv_one, conv_two)
+    own, other = call(
+        functools.partial(relay_kernel, split),
+        (window_half, window_half),
+        [pltpu.VMEM(blocks, F32)],
+        hbm=(1,),
+        inputs=2,
+    )(received, masks)
+    if split:
+        other = lax.ppermute(other, "dp", [(0, 1), (1, 0)])
     slope, hidden, turned, lifted_pad = call(
         first_kernel,
         (

time: 43.8 us -> 45.5 us (1.039)
  blocking collectives: 10 us -> 11.6 us
  waiting for transfers between devices: 4.53 us -> 3.95 us
  local copies, waits for them, and re-layouts: 0.5 us -> 0.96 us
    all_to_all x2, waiting for transfers between devices: 2.81 us -> 1.19 us  [exchanged(): lax.all_to_all(shares, axes, split_axis=0, concat_axis=0, tiled=True)]
    all_to_all x1, blocking collectives: 10 us -> 11.6 us  [exchanged(): lax.all_to_all(shares, axes, split_axis=0, concat_axis=0, tiled=True)]
    ppermute x1, waiting for transfers between devices: 0.01 us -> 1.05 us  [body(): other = lax.ppermute(other, 'dp', [(0, 1), (1, 0)])]
    unnamed x10 -> x12, local copies, waits for them, and re-layouts: 0.5 us -> 0.96 us
  transfers between devices with their start and end apart: 7 -> 7, of which waited for: 3 -> 4; matrix products, arithmetic and copies ran while one was open for 0% -> 0% of each run, Pallas kernels for 6% -> 6%
where the time goes in v23:
time: 45.5 us; the launch traced here: 45.1 us
  starting transfers between devices  20.5 us (45%)
  blocking collectives  11.6 us (25%)
  Pallas kernels  7.36 us (16%)
  waiting for transfers between devices  3.95 us (9%)
  local copies, waits for them, and re-layouts  0.96 us (2%)
  between operations  0.79 us (2%)
    all_to_all x1, blocking collectives, exchanged(): lax.all_to_all(shares, axes, split_axis=0, concat_axis=0, tiled=True)  11.6 us
    ppermute x4, starting transfers between devices, swapped(): lax.ppermute(value, 'space', pairs + [(target, source) for source, target...  10.3 us
    all_to_all x2, starting transfers between devices, exchanged(): lax.all_to_all(shares, axes, split_axis=0, concat_axis=0, tiled=True)  10 us
    pallas_call x1, Pallas kernels, body(): call(functools.partial(pick_kernel, split), shape(*blocks), [pltpu.VMEM((...  1.76 us
    ppermute x4, waiting for transfers between devices, swapped(): lax.ppermute(value, 'space', pairs + [(target, source) for source, target...  1.71 us
    all_to_all x2, waiting for transfers between devices, exchanged(): lax.all_to_all(shares, axes, split_axis=0, concat_axis=0, tiled=True)  1.19 us
    pallas_call x1, Pallas kernels, body(): call(second_kernel, (shape(*packed_rows), volume), [pool, pool, pad, pltp...  1.1 us
    pallas_call x1, Pallas kernels, body(): call(first_kernel, (shape(ROWS, HALF, dtype=F32), volume, shape(HALF, ROW...  1.09 us
  transfers between devices with their start and end apart: 7, of which 4 were waited for; matrix products, arithmetic and copies ran while one was open for 0% of the time, Pallas kernels for 6%

profile of v23, /device:TPU:0, one launch (start us, length us, event | category | flops | bytes accessed | tf_op | source)
XLA Modules:
  0.0 45.1 jit_solution(10371109919254107777)
XLA Ops:
  0.6 1.8 %shard_map.95 = bf16[384,128]{1,0:T(8,128)(2,1)} custom-call(s32[1,32]{1,0:T(1,128)} %ids_hbm.1, bf16[1,64,512]{2,1,0:T(8,128)(2,1)} %latents_hbm.1), custom_call_target="tpu_custom_call" | custom-call | tf_op jit(solution)/shard_map/pallas_call | solution.py:494
  2.4 7.3 %all-to-all-start = ((bf16[32,6,2,128]{3,2,1,0:T(2,128)(2,1)}), bf16[32,6,2,128]{3,2,1,0:T(2,128)(2,1)S(1)}, u32[]{:S(2)}, u32[]{:S(2)}) async-start(bf16[32,6,2,128]{3,2,1,0:T(2,128)(2,1)} %bitcast.11), calls=%async_computation | async-start | bytes 196608 | tf_op jit(solution)/shard_map/all_to_all | solution.py:481
  9.7 0.1 shard_map.98
  9.8 0.0 copy-start.2
  9.8 0.7 %collective-permute-start.1 = (bf16[48,256]{1,0:T(8,128)(2,1)S(1)}, bf16[48,256]{1,0:T(8,128)(2,1)S(1)}, u32[]{:S(2)}, u32[]{:S(2)}) collective-permute-start(bf16[48,256]{1,0:T(8,128)(2,1)S(1)} %get-tuple-element.35), channel_id=1, source_target_pairs={{2,4},{6,8},{10,12},{14,16},{18,20},{22,24},{26,28},{4,2},{8,6},{1... | collective-permute-start | bytes 73736 | tf_op jit(solution)/shard_map/ppermute | solution.py:475
  10.5 4.5 %collective-permute-start.2 = (bf16[48,256]{1,0:T(8,128)(2,1)S(1)}, bf16[48,256]{1,0:T(8,128)(2,1)S(1)}, u32[]{:S(2)}, u32[]{:S(2)}) collective-permute-start(bf16[48,256]{1,0:T(8,128)(2,1)S(1)} %get-tuple-element.36), channel_id=1, source_target_pairs={{0,2},{4,6},{8,10},{12,14},{16,18},{20,22},{24,26},{28,30},{2,0},{... | collective-permute-start | bytes 73736 | tf_op jit(solution)/shard_map/ppermute | solution.py:475
  15.1 0.9 %copy-done.4 = bf16[27,32,32]{2,1,0:T(8,128)(2,1)S(1)} copy-done((bf16[27,32,32]{2,1,0:T(8,128)(2,1)S(1)}, bf16[27,32,32]{2,1,0:T(8,128)(2,1)}, u32[]{:S(2)}) %copy-start.4) | copy-done | bytes 55320
  16.0 0.6 %shard_map.94 = (bf16[9,256,128]{2,1,0:T(8,128)(2,1)S(1)}, bf16[9,256,128]{2,1,0:T(8,128)(2,1)S(1)}, f32[48,128]{1,0:T(8,128)S(1)}) custom-call(s32[1,2,6]{2,1,0:T(2,128)S(1)} %copy-done.2, bf16[27,32,32]{2,1,0:T(8,128)(2,1)S(1)} %copy-done.3, bf16[27,32,32]{2,1,0:T(8,128)(2,1)S(1)} %copy-done.4), custom_call_target="tpu_custom_call" | custom-call | flops 1000000000 | bytes 2000000 | tf_op jit(solution)/shard_map/pallas_call | solution.py:523
  16.7 0.9 %all-to-all-done = bf16[32,6,2,128]{3,2,1,0:T(2,128)(2,1)S(1)} async-done(((bf16[32,6,2,128]{3,2,1,0:T(2,128)(2,1)}), bf16[32,6,2,128]{3,2,1,0:T(2,128)(2,1)S(1)}, u32[]{:S(2)}, u32[]{:S(2)}) %all-to-all-start) | async-done | bytes 98336 | tf_op jit(solution)/shard_map/all_to_all | solution.py:481
  17.6 0.2 collective-permute-start
  17.8 1.0 %collective-permute-done.other_ref = bf16[16,128]{1,0:T(8,128)(2,1)S(1)} collective-permute-done((bf16[16,128]{1,0:T(8,128)(2,1)S(1)}, bf16[16,128]{1,0:T(8,128)(2,1)S(1)}, u32[]{:S(2)}, u32[]{:S(2)}) %collective-permute-start) | collective-permute-done | bytes 4128 | tf_op jit(solution)/shard_map/ppermute | solution.py:534
  18.8 1.1 %shard_map.97 = (f32[256,128]{1,0:T(8,128)S(1)}, bf16[256,128]{1,0:T(8,128)(2,1)S(1)}, bf16[128,256]{1,0:T(8,128)(2,1)S(1)}, bf16[3,2,10,16,256]{4,3,2,1,0:T(8,128)(2,1)S(1)}) custom-call(s32[1,2,6]{2,1,0:T(2,128)S(1)} %copy-done.2, bf16[16,128]{1,0:T(8,128)(2,1)S(1)} %get-tuple-element.27.own_ref, bf16[16,128]{1,0:T(8,128)(2,1)S(1)} %collective-permute-done.other_ref, ...), custom_call_target="tpu_custom_call" | custom-call | tf_op jit(solution)/shard_map/pallas_call | solution.py:535
  19.9 1.1 %shard_map.99 = (bf16[448,128]{1,0:T(8,128)(2,1)S(1)}, bf16[256,128]{1,0:T(8,128)(2,1)S(1)}) custom-call(f32[48,128]{1,0:T(8,128)S(1)} %get-tuple-element.25._masks.masks_ref, bf16[1,2,8,8,256]{4,3,2,1,0:T(8,128)(2,1)S(1)} %copy-done, bf16[9,256,128]{2,1,0:T(8,128)(2,1)S(1)} %get-tuple-element.26.band_ref, f32[256,128]{1,0:T(8,128)S(1)} %get-tuple-element.30.slope_ref, ...), custom_call_target="tpu_custom_call" | custom-call | tf_op jit(solution)/shard_map/pallas_call | solution.py:546
  21.0 11.6 %all_to_all.15 = bf16[32,7,2,128]{3,2,1,0:T(2,128)(2,1)S(1)} all-to-all(bf16[32,7,2,128]{3,2,1,0:T(2,128)(2,1)S(1)} %bitcast.10), channel_id=1, replica_groups=mesh['space'=16,'dp'=2] {'space','dp'}, dimensions={0} | all-to-all | bytes 229376 | tf_op jit(solution)/shard_map/all_to_all | solution.py:481
  32.6 0.7 %shard_map.100 = bf16[448,128]{1,0:T(8,128)(2,1)} custom-call(bf16[448,128]{1,0:T(8,128)(2,1)S(1)} %bitcast.6), custom_call_target="tpu_custom_call" | custom-call | tf_op jit(solution)/shard_map/pallas_call | solution.py:564
  33.3 2.7 %all-to-all-start.2 = ((bf16[32,7,2,128]{3,2,1,0:T(2,128)(2,1)}), bf16[32,7,2,128]{3,2,1,0:T(2,128)(2,1)S(1)}, u32[]{:S(2)}, u32[]{:S(2)}) async-start(bf16[32,7,2,128]{3,2,1,0:T(2,128)(2,1)} %bitcast.4), calls=%async_computation.2 | async-start | bytes 229376 | tf_op jit(solution)/shard_map/all_to_all | solution.py:481
  36.0 0.1 shard_map.102
  36.1 0.7 %collective-permute-start.3 = (bf16[48,256]{1,0:T(8,128)(2,1)S(1)}, bf16[48,256]{1,0:T(8,128)(2,1)S(1)}, u32[]{:S(2)}, u32[]{:S(2)}) collective-permute-start(bf16[48,256]{1,0:T(8,128)(2,1)S(1)} %get-tuple-element.42), channel_id=1, source_target_pairs={{2,4},{6,8},{10,12},{14,16},{18,20},{22,24},{26,28},{4,2},{8,6},{1... | collective-permute-start | bytes 73736 | tf_op jit(solution)/shard_map/ppermute | solution.py:475
  36.8 4.4 %collective-permute-start.4 = (bf16[48,256]{1,0:T(8,128)(2,1)S(1)}, bf16[48,256]{1,0:T(8,128)(2,1)S(1)}, u32[]{:S(2)}, u32[]{:S(2)}) collective-permute-start(bf16[48,256]{1,0:T(8,128)(2,1)S(1)} %get-tuple-element.43), channel_id=1, source_target_pairs={{0,2},{4,6},{8,10},{12,14},{16,18},{20,22},{24,26},{28,30},{2,0},{... | collective-permute-start | bytes 73736 | tf_op jit(solution)/shard_map/ppermute | solution.py:475
  41.2 0.3 shard_map.101.band_ref
  41.6 1.7 %collective-permute-done.4.near = bf16[48,256]{1,0:T(8,128)(2,1)S(1)} collective-permute-done((bf16[48,256]{1,0:T(8,128)(2,1)S(1)}, bf16[48,256]{1,0:T(8,128)(2,1)S(1)}, u32[]{:S(2)}, u32[]{:S(2)}) %collective-permute-start.4) | collective-permute-done | bytes 24608 | tf_op jit(solution)/shard_map/ppermute | solution.py:475
  43.3 0.5 %shard_map.103.fine_ref = bf16[1,2,8,8,256]{4,3,2,1,0:T(8,128)(2,1)S(1)} custom-call(f32[48,128]{1,0:T(8,128)S(1)} %get-tuple-element.25._masks.masks_ref, bf16[9,256,128]{2,1,0:T(8,128)(2,1)S(1)} %shard_map.101.band_ref, bf16[256,128]{1,0:T(8,128)(2,1)S(1)} %get-tuple-element.38.lifted_ref, bf16[256,128]{1,0:T(8,128)(2,1)S(1)} %get-tuple-element.39.hidden_ref, ...), custom_call_target="tpu_custom_call" | custom-call | flops 1000000000 | bytes 2000000 | tf_op jit(solution)/shard_map/pallas_call | solution.py:559
  43.8 0.3 all-to-all-done.2
  44.1 1.1 %shard_map.104 = (f32[27,32,32]{2,1,0:T(8,128)}, f32[27,32,32]{2,1,0:T(8,128)}, bf16[1,2,8,8,256]{4,3,2,1,0:T(8,128)(2,1)}) custom-call(bf16[448,128]{1,0:T(8,128)(2,1)S(1)} %bitcast.8, bf16[1,2,8,8,256]{4,3,2,1,0:T(8,128)(2,1)S(1)} %shard_map.103.fine_ref), custom_call_target="tpu_custom_call" | custom-call | tf_op jit(solution)/shard_map/pallas_call | solution.py:579
  (14 shorter events, 0.1 us)
Async XLA Ops:
  0.6 14.4 %copy-start.3 = (bf16[27,32,32]{2,1,0:T(8,128)(2,1)S(1)}, bf16[27,32,32]{2,1,0:T(8,128)(2,1)}, u32[]{:S(2)}) copy-start(bf16[27,32,32]{2,1,0:T(8,128)(2,1)} %one_ref.1) | copy-start | bytes 165892
  2.4 7.3 %copy-start = (bf16[1,2,8,8,256]{4,3,2,1,0:T(8,128)(2,1)S(1)}, bf16[1,2,8,8,256]{4,3,2,1,0:T(8,128)(2,1)}, u32[]{:S(2)}) copy-start(bf16[1,2,8,8,256]{4,3,2,1,0:T(8,128)(2,1)} %cotangent_ref.3) | copy-start | bytes 196612
  2.4 15.1 %all-to-all-start = ((bf16[32,6,2,128]{3,2,1,0:T(2,128)(2,1)}), bf16[32,6,2,128]{3,2,1,0:T(2,128)(2,1)S(1)}, u32[]{:S(2)}, u32[]{:S(2)}) async-start(bf16[32,6,2,128]{3,2,1,0:T(2,128)(2,1)} %bitcast.11), calls=%async_computation | async-start | bytes 196608 | tf_op jit(solution)/shard_map/all_to_all | solution.py:481
  9.8 5.2 %copy-start.2 = (s32[1,2,6]{2,1,0:T(2,128)S(1)}, s32[1,2,6]{2,1,0:T(2,128)}, u32[]{:S(2)}) copy-start(s32[1,2,6]{2,1,0:T(2,128)} %links_in.3) | copy-start | bytes 148
  9.8 10.1 %collective-permute-start.1 = (bf16[48,256]{1,0:T(8,128)(2,1)S(1)}, bf16[48,256]{1,0:T(8,128)(2,1)S(1)}, u32[]{:S(2)}, u32[]{:S(2)}) collective-permute-start(bf16[48,256]{1,0:T(8,128)(2,1)S(1)} %get-tuple-element.35), channel_id=1, source_target_pairs={{2,4},{6,8},{10,12},{14,16},{18,20},{22,24},{26,28},{4,2},{8,6},{1... | collective-permute-start | bytes 73736 | tf_op jit(solution)/shard_map/ppermute | solution.py:475
  10.5 9.4 %collective-permute-start.2 = (bf16[48,256]{1,0:T(8,128)(2,1)S(1)}, bf16[48,256]{1,0:T(8,128)(2,1)S(1)}, u32[]{:S(2)}, u32[]{:S(2)}) collective-permute-start(bf16[48,256]{1,0:T(8,128)(2,1)S(1)} %get-tuple-element.36), channel_id=1, source_target_pairs={{0,2},{4,6},{8,10},{12,14},{16,18},{20,22},{24,26},{28,30},{2,0},{... | collective-permute-start | bytes 73736 | tf_op jit(solution)/shard_map/ppermute | solution.py:475
  15.1 0.9 %copy-start.4 = (bf16[27,32,32]{2,1,0:T(8,128)(2,1)S(1)}, bf16[27,32,32]{2,1,0:T(8,128)(2,1)}, u32[]{:S(2)}) copy-start(bf16[27,32,32]{2,1,0:T(8,128)(2,1)} %weights_ref.1) | copy-start | bytes 165892
  16.0 2.8 %copy-start.1 = (bf16[64,2048]{1,0:T(8,128)(2,1)S(1)}, bf16[64,2048]{1,0:T(8,128)(2,1)}, u32[]{:S(2)}) copy-start(bf16[64,2048]{1,0:T(8,128)(2,1)} %up_ref.1) | copy-start | bytes 786436
  17.6 1.2 %collective-permute-start = (bf16[16,128]{1,0:T(8,128)(2,1)S(1)}, bf16[16,128]{1,0:T(8,128)(2,1)S(1)}, u32[]{:S(2)}, u32[]{:S(2)}) collective-permute-start(bf16[16,128]{1,0:T(8,128)(2,1)S(1)} %get-tuple-element.28), channel_id=1, source_target_pairs={{0,1},{1,0},{2,3},{3,2},{4,5},{5,4},{6,7},{7,6},{8,9},{9,8},{10,11... | collective-permute-start | bytes 12296 | tf_op jit(solution)/shard_map/ppermute | solution.py:534
  33.3 7.9 %copy-start.5 = (bf16[27,32,32]{2,1,0:T(8,128)(2,1)S(1)}, bf16[27,32,32]{2,1,0:T(8,128)(2,1)}, u32[]{:S(2)}) copy-start(bf16[27,32,32]{2,1,0:T(8,128)(2,1)} %weights_ref.1) | copy-start | bytes 165892
  33.3 10.8 %all-to-all-start.2 = ((bf16[32,7,2,128]{3,2,1,0:T(2,128)(2,1)}), bf16[32,7,2,128]{3,2,1,0:T(2,128)(2,1)S(1)}, u32[]{:S(2)}, u32[]{:S(2)}) async-start(bf16[32,7,2,128]{3,2,1,0:T(2,128)(2,1)} %bitcast.4), calls=%async_computation.2 | async-start | bytes 229376 | tf_op jit(solution)/shard_map/all_to_all | solution.py:481
  36.1 5.4 %collective-permute-start.3 = (bf16[48,256]{1,0:T(8,128)(2,1)S(1)}, bf16[48,256]{1,0:T(8,128)(2,1)S(1)}, u32[]{:S(2)}, u32[]{:S(2)}) collective-permute-start(bf16[48,256]{1,0:T(8,128)(2,1)S(1)} %get-tuple-element.42), channel_id=1, source_target_pairs={{2,4},{6,8},{10,12},{14,16},{18,20},{22,24},{26,28},{4,2},{8,6},{1... | collective-permute-start | bytes 73736 | tf_op jit(solution)/shard_map/ppermute | solution.py:475
  36.8 6.5 %collective-permute-start.4 = (bf16[48,256]{1,0:T(8,128)(2,1)S(1)}, bf16[48,256]{1,0:T(8,128)(2,1)S(1)}, u32[]{:S(2)}, u32[]{:S(2)}) collective-permute-start(bf16[48,256]{1,0:T(8,128)(2,1)S(1)} %get-tuple-element.43), channel_id=1, source_target_pairs={{0,2},{4,6},{8,10},{12,14},{16,18},{20,22},{24,26},{28,30},{2,0},{... | collective-permute-start | bytes 73736 | tf_op jit(solution)/shard_map/ppermute | solution.py:475

commit v24 on v22

--- a/solution.py
+++ b/solution.py
@@ -123,11 +123,32 @@
     build_band(band_ref, weight_rows(weights_ref[...].astype(F32)))
 
 
-def masks_kernel(links_in, one_ref, two_ref, band_ref, back_ref, masks_ref, links_ref, links_sem):
+def lift(half_ref, up_ref, rows_ref, volumes_ref, half):
+    tiles = half_ref.shape[0] // 8
+    rows_ref[...] = half_ref[...].astype(F32)
+    cells = []
+    for tile in range(tiles):
+        rows = rows_ref[pl.ds(tile, 8, stride=tiles), :]
+        cells += [rows[:, :64], rows[:, 64:]]
+    lifted = dot(jnp.concatenate(cells, axis=0).astype(BF16), up_ref[...])
+    lifted = lifted.astype(BF16).astype(F32)
+    first = 4 * CUBE * half
+    for cell in range(4):
+        b, c = cell // 2, cell % 2
+        for sub in range(16):
+            line = first + 8 * (sub // 4 * EDGE + 4 * b + sub % 4)
+            volumes_ref[c, line : line + 8, :] = lifted[cell * 8 : cell * 8 + 8, sub * 128 : sub * 128 + 128]
+
+
+def early_kernel(
+    links_in, own_ref, up_ref, weights_ref,
+    band_ref, masks_ref, volumes_out,
+    rows_ref, links_ref, links_sem,
+):
     links_copy = pltpu.make_async_copy(links_in, links_ref, links_sem)
     links_copy.start()
-    build_band(band_ref, weight_rows(one_ref[...].astype(F32)))
-    build_band(back_ref, flipped_rows(two_ref[...].astype(F32)))
+    lift(own_ref, up_ref, rows_ref, volumes_out, 0)
+    build_band(band_ref, weight_rows(weights_ref[...].astype(F32)))
     links_copy.wait()
     put_masks(masks_ref, links_ref)
 
@@ -236,29 +257,15 @@
 
 
 def first_kernel(
-    links_in, own_ref, other_ref, up_ref, band_ref,
-    slope_out, hidden_out, turned_out, pad_out,
+    links_in, other_ref, up_ref, band_ref, lifted_half, weights_ref,
+    slope_out, hidden_out, turned_out, pad_out, back_out,
     volumes_ref, rows_ref, links_ref, links_sem,
 ):
     links_copy = pltpu.make_async_copy(links_in, links_ref, links_sem)
     links_copy.start()
     position = lax.axis_index("space")
-    cells = []
-    for half, half_ref in enumerate((own_ref, other_ref)):
-        tiles = half_ref.shape[0] // 8
-        rows_ref[half] = half_ref[...].astype(F32)
-        for tile in range(tiles):
-            rows = rows_ref[half, pl.ds(tile, 8, stride=tiles), :]
-            cells += [rows[:, :64], rows[:, 64:]]
-    lifted = dot(jnp.concatenate(cells, axis=0).astype(BF16), up_ref[...])
-    lifted = lifted.astype(BF16).astype(F32)
-    for cell in range(8):
-        a, b, c = cell // 4, cell // 2 % 2, cell % 2
-        for sub in range(16):
-            line = (4 * a + sub // 4) * EDGE + 4 * b + sub % 4
-            volumes_ref[c, line * 8 : line * 8 + 8, :] = lifted[
-                cell * 8 : cell * 8 + 8, sub * 128 : sub * 128 + 128
-            ]
+    volumes_ref[:, : 4 * CUBE] = lifted_half[...]
+    lift(other_ref, up_ref, rows_ref, volumes_ref, 1)
     links_copy.wait()
     for brick in range(BRICKS):
 
@@ -291,6 +298,7 @@
     hidden_out[...] = hidden
     hidden = hidden.astype(F32)
     turned_out[...] = jnp.transpose(hidden).astype(BF16)
+    build_band(back_out, flipped_rows(weights_ref[...].astype(F32)))
 
 
 def hidden_faces_kernel(hidden_ref, _parts, high_out, low_out, far_out, near_out, halves_ref, faces_ref):
@@ -525,18 +533,20 @@
     far = swapped(far, 1)
     near = swapped(near, 0)
     masks = shape(BRICKS * 6 * 2 * BRICKS, 128, dtype=F32)
-    band_one, band_back, masks = call(
-        masks_kernel, (shape(*BAND), shape(*BAND), masks), links, hbm=(0,), inputs=3, cost=cost
-    )(face_links, conv_one, conv_two)
-    slope, hidden, turned, lifted_pad = call(
+    lifted_half = shape(2, 4 * CUBE, 128, dtype=F32)
+    window_rows = pltpu.VMEM((8 * tiles, 128), F32)
+    band_one, masks, lifted_half = call(
+        early_kernel, (shape(*BAND), masks, lifted_half), [window_rows, *links], hbm=(0,), inputs=4, cost=cost
+    )(face_links, own, up_weight, conv_one)
+    slope, hidden, turned, lifted_pad, band_back = call(
         first_kernel,
         (
-            shape(ROWS, HALF, dtype=F32), volume, shape(HALF, ROWS), shape(*pad_shape),
+            shape(ROWS, HALF, dtype=F32), volume, shape(HALF, ROWS), shape(*pad_shape), shape(*BAND),
         ),
-        [pltpu.VMEM((2, 8 * CUBE, 128), F32), pltpu.VMEM((2, 8 * tiles, 128), F32), *links],
+        [pltpu.VMEM((2, 8 * CUBE, 128), F32), window_rows, *links],
         hbm=(0,),
-        inputs=5,
-    )(face_links, own, other, up_weight, band_one)
+        inputs=6,
+    )(face_links, other, up_weight, band_one, lifted_half, conv_two)
     share = 2 * -(-GROUPS * CHANNELS // everyone)
     packed_rows = (everyone * share, 128)
     sums, lifted = call(

time: 43.8 us -> 45.1 us (1.030)
  local copies, waits for them, and re-layouts: 0.5 us -> 1.63 us
    unnamed x10, local copies, waits for them, and re-layouts: 0.5 us -> 1.63 us
where the time goes in v24:
time: 45.1 us; the launch traced here: 44.8 us
  starting transfers between devices  20.4 us (45%)
  blocking collectives  9.93 us (22%)
  Pallas kernels  7.52 us (17%)
  waiting for transfers between devices  4.53 us (10%)
  local copies, waits for them, and re-layouts  1.63 us (4%)
  between operations  0.79 us (2%)
    ppermute x4, starting transfers between devices, swapped(): lax.ppermute(value, 'space', pairs + [(target, source) for source, target...  10.3 us
    all_to_all x1, blocking collectives, exchanged(): lax.all_to_all(shares, axes, split_axis=0, concat_axis=0, tiled=True)  9.93 us
    all_to_all x2, starting transfers between devices, exchanged(): lax.all_to_all(shares, axes, split_axis=0, concat_axis=0, tiled=True)  9.89 us
    all_to_all x2, waiting for transfers between devices, exchanged(): lax.all_to_all(shares, axes, split_axis=0, concat_axis=0, tiled=True)  2.81 us
    pallas_call x1, Pallas kernels, body(): call(functools.partial(pick_kernel, split), shape(*blocks), [pltpu.VMEM((...  1.76 us
    ppermute x4, waiting for transfers between devices, swapped(): lax.ppermute(value, 'space', pairs + [(target, source) for source, target...  1.71 us
    unnamed x10, local copies, waits for them, and re-layouts  1.63 us
    pallas_call x1, Pallas kernels, body(): call(first_kernel, (shape(ROWS, HALF, dtype=F32), volume, shape(HALF, ROW...  1.2 us
  transfers between devices with their start and end apart: 7, of which 3 were waited for; matrix products, arithmetic and copies ran while one was open for 0% of the time, Pallas kernels for 6%

profile of v24, /device:TPU:0, one launch (start us, length us, event | category | flops | bytes accessed | tf_op | source)
XLA Modules:
  0.0 44.8 jit_solution(9674843217621538924)
XLA Ops:
  0.6 1.8 %shard_map.94 = bf16[384,128]{1,0:T(8,128)(2,1)} custom-call(s32[1,32]{1,0:T(1,128)} %ids_hbm.1, bf16[1,64,512]{2,1,0:T(8,128)(2,1)} %latents_hbm.1), custom_call_target="tpu_custom_call" | custom-call | tf_op jit(solution)/shard_map/pallas_call | solution.py:502
  2.4 7.3 %all-to-all-start = ((bf16[32,6,2,128]{3,2,1,0:T(2,128)(2,1)}), bf16[32,6,2,128]{3,2,1,0:T(2,128)(2,1)S(1)}, u32[]{:S(2)}, u32[]{:S(2)}) async-start(bf16[32,6,2,128]{3,2,1,0:T(2,128)(2,1)} %bitcast.11), calls=%async_computation | async-start | bytes 196608 | tf_op jit(solution)/shard_map/all_to_all | solution.py:489
  9.7 0.1 shard_map.98
  9.8 0.7 %collective-permute-start.1 = (bf16[48,256]{1,0:T(8,128)(2,1)S(1)}, bf16[48,256]{1,0:T(8,128)(2,1)S(1)}, u32[]{:S(2)}, u32[]{:S(2)}) collective-permute-start(bf16[48,256]{1,0:T(8,128)(2,1)S(1)} %get-tuple-element.37), channel_id=1, source_target_pairs={{2,4},{6,8},{10,12},{14,16},{18,20},{22,24},{26,28},{4,2},{8,6},{1... | collective-permute-start | bytes 73736 | tf_op jit(solution)/shard_map/ppermute | solution.py:483
  10.5 4.5 %collective-permute-start.2 = (bf16[48,256]{1,0:T(8,128)(2,1)S(1)}, bf16[48,256]{1,0:T(8,128)(2,1)S(1)}, u32[]{:S(2)}, u32[]{:S(2)}) collective-permute-start(bf16[48,256]{1,0:T(8,128)(2,1)S(1)} %get-tuple-element.38), channel_id=1, source_target_pairs={{0,2},{4,6},{8,10},{12,14},{16,18},{20,22},{24,26},{28,30},{2,0},{... | collective-permute-start | bytes 73736 | tf_op jit(solution)/shard_map/ppermute | solution.py:483
  15.0 2.5 %all-to-all-done = bf16[32,6,2,128]{3,2,1,0:T(2,128)(2,1)S(1)} async-done(((bf16[32,6,2,128]{3,2,1,0:T(2,128)(2,1)}), bf16[32,6,2,128]{3,2,1,0:T(2,128)(2,1)S(1)}, u32[]{:S(2)}, u32[]{:S(2)}) %all-to-all-start) | async-done | bytes 98336 | tf_op jit(solution)/shard_map/all_to_all | solution.py:489
  17.6 0.2 collective-permute-start
  17.8 0.5 %copy-done.3 = s32[1,2,6]{2,1,0:T(2,128)S(1)} copy-done((s32[1,2,6]{2,1,0:T(2,128)S(1)}, s32[1,2,6]{2,1,0:T(2,128)}, u32[]{:S(2)}) %copy-start.3) | copy-done | bytes 72
  18.3 0.9 %copy-done.4 = bf16[27,32,32]{2,1,0:T(8,128)(2,1)S(1)} copy-done((bf16[27,32,32]{2,1,0:T(8,128)(2,1)S(1)}, bf16[27,32,32]{2,1,0:T(8,128)(2,1)}, u32[]{:S(2)}) %copy-start.4) | copy-done | bytes 55320
  19.2 0.7 %shard_map.96 = (bf16[9,256,128]{2,1,0:T(8,128)(2,1)S(1)}, f32[48,128]{1,0:T(8,128)S(1)}, f32[2,256,128]{2,1,0:T(8,128)S(1)}) custom-call(s32[1,2,6]{2,1,0:T(2,128)S(1)} %copy-done.3, bf16[16,128]{1,0:T(8,128)(2,1)S(1)} %get-tuple-element.26.own_ref, bf16[64,2048]{1,0:T(8,128)(2,1)S(1)} %copy-done.1, bf16[27,32,32]{2,1,0:T(8,128)(2,1)S(1)} %copy-done.4), custom_call_target="tpu_custom_call" | custom-call | flops 1000000000 | bytes 2000000 | tf_op jit(solution)/shard_map/pallas_call | solution.py:538
  19.9 0.2 copy-done.2
  20.1 1.2 %shard_map.97 = (f32[256,128]{1,0:T(8,128)S(1)}, bf16[256,128]{1,0:T(8,128)(2,1)S(1)}, bf16[128,256]{1,0:T(8,128)(2,1)S(1)}, bf16[3,2,10,16,256]{4,3,2,1,0:T(8,128)(2,1)S(1)}, bf16[9,256,128]{2,1,0:T(8,128)(2,1)S(1)}) custom-call(s32[1,2,6]{2,1,0:T(2,128)S(1)} %copy-done.3, bf16[16,128]{1,0:T(8,128)(2,1)S(1)} %collective-permute-done.other_ref, ...), custom_call_target="tpu_custom_call" | custom-call | tf_op jit(solution)/shard_map/pallas_call | solution.py:541
  21.4 1.1 %shard_map.99 = (bf16[448,128]{1,0:T(8,128)(2,1)S(1)}, bf16[256,128]{1,0:T(8,128)(2,1)S(1)}) custom-call(f32[48,128]{1,0:T(8,128)S(1)} %get-tuple-element.27.masks_ref, bf16[1,2,8,8,256]{4,3,2,1,0:T(8,128)(2,1)S(1)} %copy-done, bf16[9,256,128]{2,1,0:T(8,128)(2,1)S(1)} %get-tuple-element.31.band_ref, f32[256,128]{1,0:T(8,128)S(1)} %get-tuple-element.32.slope_ref, ...), custom_call_target="tpu_custom_call" | custom-call | tf_op jit(solution)/shard_map/pallas_call | solution.py:552
  22.4 9.9 %all_to_all.15 = bf16[32,7,2,128]{3,2,1,0:T(2,128)(2,1)S(1)} all-to-all(bf16[32,7,2,128]{3,2,1,0:T(2,128)(2,1)S(1)} %bitcast.10), channel_id=1, replica_groups=mesh['space'=16,'dp'=2] {'space','dp'}, dimensions={0} | all-to-all | bytes 229376 | tf_op jit(solution)/shard_map/all_to_all | solution.py:489
  32.4 0.7 %shard_map.100 = bf16[448,128]{1,0:T(8,128)(2,1)} custom-call(bf16[448,128]{1,0:T(8,128)(2,1)S(1)} %bitcast.6), custom_call_target="tpu_custom_call" | custom-call | tf_op jit(solution)/shard_map/pallas_call | solution.py:570
  33.1 2.6 %all-to-all-start.2 = ((bf16[32,7,2,128]{3,2,1,0:T(2,128)(2,1)}), bf16[32,7,2,128]{3,2,1,0:T(2,128)(2,1)S(1)}, u32[]{:S(2)}, u32[]{:S(2)}) async-start(bf16[32,7,2,128]{3,2,1,0:T(2,128)(2,1)} %bitcast.4), calls=%async_computation.2 | async-start | bytes 229376 | tf_op jit(solution)/shard_map/all_to_all | solution.py:489
  35.7 0.1 shard_map.102
  35.8 0.7 %collective-permute-start.3 = (bf16[48,256]{1,0:T(8,128)(2,1)S(1)}, bf16[48,256]{1,0:T(8,128)(2,1)S(1)}, u32[]{:S(2)}, u32[]{:S(2)}) collective-permute-start(bf16[48,256]{1,0:T(8,128)(2,1)S(1)} %get-tuple-element.44), channel_id=1, source_target_pairs={{2,4},{6,8},{10,12},{14,16},{18,20},{22,24},{26,28},{4,2},{8,6},{1... | collective-permute-start | bytes 73736 | tf_op jit(solution)/shard_map/ppermute | solution.py:483
  36.4 4.4 %collective-permute-start.4 = (bf16[48,256]{1,0:T(8,128)(2,1)S(1)}, bf16[48,256]{1,0:T(8,128)(2,1)S(1)}, u32[]{:S(2)}, u32[]{:S(2)}) collective-permute-start(bf16[48,256]{1,0:T(8,128)(2,1)S(1)} %get-tuple-element.45), channel_id=1, source_target_pairs={{0,2},{4,6},{8,10},{12,14},{16,18},{20,22},{24,26},{28,30},{2,0},{... | collective-permute-start | bytes 73736 | tf_op jit(solution)/shard_map/ppermute | solution.py:483
  40.9 0.3 shard_map.101.band_ref
  41.2 1.7 %collective-permute-done.4.near = bf16[48,256]{1,0:T(8,128)(2,1)S(1)} collective-permute-done((bf16[48,256]{1,0:T(8,128)(2,1)S(1)}, bf16[48,256]{1,0:T(8,128)(2,1)S(1)}, u32[]{:S(2)}, u32[]{:S(2)}) %collective-permute-start.4) | collective-permute-done | bytes 24608 | tf_op jit(solution)/shard_map/ppermute | solution.py:483
  42.9 0.5 %shard_map.103.fine_ref = bf16[1,2,8,8,256]{4,3,2,1,0:T(8,128)(2,1)S(1)} custom-call(f32[48,128]{1,0:T(8,128)S(1)} %get-tuple-element.27.masks_ref, bf16[9,256,128]{2,1,0:T(8,128)(2,1)S(1)} %shard_map.101.band_ref, bf16[256,128]{1,0:T(8,128)(2,1)S(1)} %get-tuple-element.40.lifted_ref, bf16[256,128]{1,0:T(8,128)(2,1)S(1)} %get-tuple-element.41.hidden_ref, ...), custom_call_target="tpu_custom_call" | custom-call | flops 1000000000 | bytes 2000000 | tf_op jit(solution)/shard_map/pallas_call | solution.py:565
  43.4 0.3 all-to-all-done.2
  43.7 1.1 %shard_map.104 = (f32[27,32,32]{2,1,0:T(8,128)}, f32[27,32,32]{2,1,0:T(8,128)}, bf16[1,2,8,8,256]{4,3,2,1,0:T(8,128)(2,1)}) custom-call(bf16[448,128]{1,0:T(8,128)(2,1)S(1)} %bitcast.8, bf16[1,2,8,8,256]{4,3,2,1,0:T(8,128)(2,1)S(1)} %shard_map.103.fine_ref), custom_call_target="tpu_custom_call" | custom-call | tf_op jit(solution)/shard_map/pallas_call | solution.py:585
  (12 shorter events, 0.1 us)
Async XLA Ops:
  0.6 17.1 %copy-start.1 = (bf16[64,2048]{1,0:T(8,128)(2,1)S(1)}, bf16[64,2048]{1,0:T(8,128)(2,1)}, u32[]{:S(2)}) copy-start(bf16[64,2048]{1,0:T(8,128)(2,1)} %up_ref.3) | copy-start | bytes 786436
  2.4 7.3 %copy-start = (bf16[1,2,8,8,256]{4,3,2,1,0:T(8,128)(2,1)S(1)}, bf16[1,2,8,8,256]{4,3,2,1,0:T(8,128)(2,1)}, u32[]{:S(2)}) copy-start(bf16[1,2,8,8,256]{4,3,2,1,0:T(8,128)(2,1)} %cotangent_ref.3) | copy-start | bytes 196612
  2.4 15.1 %all-to-all-start = ((bf16[32,6,2,128]{3,2,1,0:T(2,128)(2,1)}), bf16[32,6,2,128]{3,2,1,0:T(2,128)(2,1)S(1)}, u32[]{:S(2)}, u32[]{:S(2)}) async-start(bf16[32,6,2,128]{3,2,1,0:T(2,128)(2,1)} %bitcast.11), calls=%async_computation | async-start | bytes 196608 | tf_op jit(solution)/shard_map/all_to_all | solution.py:489
  9.8 11.5 %collective-permute-start.1 = (bf16[48,256]{1,0:T(8,128)(2,1)S(1)}, bf16[48,256]{1,0:T(8,128)(2,1)S(1)}, u32[]{:S(2)}, u32[]{:S(2)}) collective-permute-start(bf16[48,256]{1,0:T(8,128)(2,1)S(1)} %get-tuple-element.37), channel_id=1, source_target_pairs={{2,4},{6,8},{10,12},{14,16},{18,20},{22,24},{26,28},{4,2},{8,6},{1... | collective-permute-start | bytes 73736 | tf_op jit(solution)/shard_map/ppermute | solution.py:483
  10.5 10.8 %collective-permute-start.2 = (bf16[48,256]{1,0:T(8,128)(2,1)S(1)}, bf16[48,256]{1,0:T(8,128)(2,1)S(1)}, u32[]{:S(2)}, u32[]{:S(2)}) collective-permute-start(bf16[48,256]{1,0:T(8,128)(2,1)S(1)} %get-tuple-element.38), channel_id=1, source_target_pairs={{0,2},{4,6},{8,10},{12,14},{16,18},{20,22},{24,26},{28,30},{2,0},{... | collective-permute-start | bytes 73736 | tf_op jit(solution)/shard_map/ppermute | solution.py:483
  17.6 0.7 %copy-start.3 = (s32[1,2,6]{2,1,0:T(2,128)S(1)}, s32[1,2,6]{2,1,0:T(2,128)}, u32[]{:S(2)}) copy-start(s32[1,2,6]{2,1,0:T(2,128)} %links_in.3) | copy-start | bytes 148
  17.6 2.3 %collective-permute-start = (bf16[16,128]{1,0:T(8,128)(2,1)S(1)}, bf16[16,128]{1,0:T(8,128)(2,1)S(1)}, u32[]{:S(2)}, u32[]{:S(2)}) collective-permute-start(bf16[16,128]{1,0:T(8,128)(2,1)S(1)} %get-tuple-element.28), channel_id=1, source_target_pairs={{0,1},{1,0},{2,3},{3,2},{4,5},{5,4},{6,7},{7,6},{8,9},{9,8},{10,11... | collective-permute-start | bytes 12296 | tf_op jit(solution)/shard_map/ppermute | solution.py:522
  18.3 0.9 %copy-start.4 = (bf16[27,32,32]{2,1,0:T(8,128)(2,1)S(1)}, bf16[27,32,32]{2,1,0:T(8,128)(2,1)}, u32[]{:S(2)}) copy-start(bf16[27,32,32]{2,1,0:T(8,128)(2,1)} %weights_ref.3) | copy-start | bytes 165892
  19.2 0.9 %copy-start.2 = (bf16[27,32,32]{2,1,0:T(8,128)(2,1)S(1)}, bf16[27,32,32]{2,1,0:T(8,128)(2,1)}, u32[]{:S(2)}) copy-start(bf16[27,32,32]{2,1,0:T(8,128)(2,1)} %weights_ref.5) | copy-start | bytes 165892
  33.1 10.6 %all-to-all-start.2 = ((bf16[32,7,2,128]{3,2,1,0:T(2,128)(2,1)}), bf16[32,7,2,128]{3,2,1,0:T(2,128)(2,1)S(1)}, u32[]{:S(2)}, u32[]{:S(2)}) async-start(bf16[32,7,2,128]{3,2,1,0:T(2,128)(2,1)} %bitcast.4), calls=%async_computation.2 | async-start | bytes 229376 | tf_op jit(solution)/shard_map/all_to_all | solution.py:489
  35.8 5.4 %collective-permute-start.3 = (bf16[48,256]{1,0:T(8,128)(2,1)S(1)}, bf16[48,256]{1,0:T(8,128)(2,1)S(1)}, u32[]{:S(2)}, u32[]{:S(2)}) collective-permute-start(bf16[48,256]{1,0:T(8,128)(2,1)S(1)} %get-tuple-element.44), channel_id=1, source_target_pairs={{2,4},{6,8},{10,12},{14,16},{18,20},{22,24},{26,28},{4,2},{8,6},{1... | collective-permute-start | bytes 73736 | tf_op jit(solution)/shard_map/ppermute | solution.py:483
  36.4 6.5 %collective-permute-start.4 = (bf16[48,256]{1,0:T(8,128)(2,1)S(1)}, bf16[48,256]{1,0:T(8,128)(2,1)S(1)}, u32[]{:S(2)}, u32[]{:S(2)}) collective-permute-start(bf16[48,256]{1,0:T(8,128)(2,1)S(1)} %get-tuple-element.45), channel_id=1, source_target_pairs={{0,2},{4,6},{8,10},{12,14},{16,18},{20,22},{24,26},{28,30},{2,0},{... | collective-permute-start | bytes 73736 | tf_op jit(solution)/shard_map/ppermute | solution.py:483

commit v25 on v24

--- a/solution.py
+++ b/solution.py
@@ -45,11 +45,17 @@
     return lax.axis_index("dp") if split else 0
 
 
-def pick_kernel(split, ids_hbm, latents_hbm, out_ref, ids_ref, latents_ref, rows_ref, blocks_ref, sems):
+def pick_kernel(split, extras, ids_hbm, latents_hbm, *refs):
+    brought = zip(refs[:extras], refs[extras + 1 : 2 * extras + 1])
+    out_ref = refs[extras]
+    ids_ref, latents_ref, rows_ref, blocks_ref, sems = refs[2 * extras + 1 :]
     ids_copy = pltpu.make_async_copy(ids_hbm, ids_ref, sems.at[0])
     latents_copy = pltpu.make_async_copy(latents_hbm, latents_ref, sems.at[1])
     ids_copy.start()
     latents_copy.start()
+    others = [pltpu.make_async_copy(*pair, sems.at[2 + i]) for i, pair in enumerate(brought)]
+    for copy in others:
+        copy.start()
     held, width = latents_ref.shape[1:]
     bricks = ids_ref.shape[1]
     tiles = width // 256
@@ -77,6 +83,8 @@
             place = (2 * receiver + half) * count
             blocks_ref[place : place + count] = block
     out_ref[...] = blocks_ref[...].astype(BF16)
+    for copy in others:
+        copy.wait()
 
 
 def relay_kernel(split, received_ref, own_out, other_out, rows_ref):
@@ -478,6 +486,10 @@
     return jax.ShapeDtypeStruct(dims, dtype)
 
 
+def kept_in_hbm(value):
+    return pltpu.with_memory_space_constraint(value, pltpu.HBM)
+
+
 def swapped(value, first):
     pairs = [(i, i + 1) for i in range(first, lax.axis_size("space") - 1, 2)]
     return lax.ppermute(value, "space", pairs + [(target, source) for source, target in pairs])
@@ -499,20 +511,20 @@
     tiles = width // 256
     count = 3 * BRICKS * tiles
     blocks = (2 * devices * count, 128)
-    packed = call(
-        functools.partial(pick_kernel, split),
-        shape(*blocks),
+    extras = (up_weight, conv_one, conv_two, face_links)
+    packed, up_weight, conv_one, conv_two, face_links = call(
+        functools.partial(pick_kernel, split, len(extras)),
+        (shape(*blocks), *[shape(*extra.shape, dtype=extra.dtype) for extra in extras]),
         [
             pltpu.VMEM((1, bricks), jnp.int32),
             pltpu.VMEM((1, held, width), BF16),
             pltpu.VMEM((2, (bricks + 16) * tiles, 128), F32),
             pltpu.VMEM(blocks, F32),
-            pltpu.SemaphoreType.DMA((2,)),
+            pltpu.SemaphoreType.DMA((2 + len(extras),)),
         ],
-        hbm=(0, 1),
-        inputs=2,
-        limit=60,
-    )(active_blocks, coarse_latents)
+        hbm=range(2 + len(extras)),
+        inputs=2 + len(extras),
+    )(*[kept_in_hbm(operand) for operand in (active_blocks, coarse_latents, *extras)])
     received = exchanged(packed, ("space", "dp") if split else ("space",))
     window_half = shape(8 * tiles, 128)
     own, other = call(

time: 45.1 us -> 44 us (0.976)
  local copies, waits for them, and re-layouts: 1.63 us -> 0.01 us
    unnamed x10 -> x2, local copies, waits for them, and re-layouts: 1.63 us -> 0.01 us
  transfers between devices with their start and end apart: 7 -> 7, of which waited for: 3 -> 4; matrix products, arithmetic and copies ran while one was open for 0% -> 0% of each run, Pallas kernels for 6% -> 7%
where the time goes in v25:
time: 44 us; the launch traced here: 43.7 us
  starting transfers between devices  20.4 us (46%)
  blocking collectives  10 us (23%)
  Pallas kernels  7.66 us (17%)
  waiting for transfers between devices  4.84 us (11%)
  between operations  0.77 us (2%)
    ppermute x4, starting transfers between devices, swapped(): lax.ppermute(value, 'space', pairs + [(target, source) for source, target...  10.3 us
    all_to_all x1, blocking collectives, exchanged(): lax.all_to_all(shares, axes, split_axis=0, concat_axis=0, tiled=True)  10 us
    all_to_all x2, starting transfers between devices, exchanged(): lax.all_to_all(shares, axes, split_axis=0, concat_axis=0, tiled=True)  9.89 us
    all_to_all x2, waiting for transfers between devices, exchanged(): lax.all_to_all(shares, axes, split_axis=0, concat_axis=0, tiled=True)  2.8 us
    pallas_call x1, Pallas kernels, body(): call(functools.partial(pick_kernel, split, len(extras)), (shape(*blocks),...  1.87 us
    ppermute x4, waiting for transfers between devices, swapped(): lax.ppermute(value, 'space', pairs + [(target, source) for source, target...  1.71 us
    pallas_call x1, Pallas kernels, body(): call(first_kernel, (shape(ROWS, HALF, dtype=F32), volume, shape(HALF, ROW...  1.19 us
    pallas_call x1, Pallas kernels, body(): call(second_kernel, (shape(*packed_rows), volume), [pool, pool, pad, pltp...  1.1 us
  transfers between devices with their start and end apart: 7, of which 4 were waited for; matrix products, arithmetic and copies ran while one was open for 0% of the time, Pallas kernels for 7%

profile of v25, /device:TPU:0, one launch (start us, length us, event | category | flops | bytes accessed | tf_op | source)
XLA Modules:
  0.0 43.7 jit_solution(15074954392846250825)
XLA Ops:
  0.6 1.9 %shard_map.94 = (bf16[384,128]{1,0:T(8,128)(2,1)}, bf16[64,2048]{1,0:T(8,128)(2,1)S(1)}, bf16[27,32,32]{2,1,0:T(8,128)(2,1)S(1)}, bf16[27,32,32]{2,1,0:T(8,128)(2,1)S(1)}, s32[1,2,6]{2,1,0:T(2,128)S(1)}) custom-call(s32[1,32]{1,0:T(1,128)} %ids_hbm.1, bf16[1,64,512]{2,1,0:T(8,128)(2,1)} %latents_hbm.1, bf16[64,2048]{1,0:T(8,128)(2,1)} %refs_0_.1, ...), custom_call_target="tpu_custom_call" | custom-call | tf_op jit(solution)/shard_map/pallas_call | solution.py:515
  2.5 0.0 copy-start
  2.5 7.3 %all-to-all-start = ((bf16[32,6,2,128]{3,2,1,0:T(2,128)(2,1)}), bf16[32,6,2,128]{3,2,1,0:T(2,128)(2,1)S(1)}, u32[]{:S(2)}, u32[]{:S(2)}) async-start(bf16[32,6,2,128]{3,2,1,0:T(2,128)(2,1)} %bitcast), calls=%async_computation | async-start | bytes 196608 | tf_op jit(solution)/shard_map/all_to_all | solution.py:501
  9.8 0.1 shard_map.98
  9.9 0.7 %collective-permute-start.1 = (bf16[48,256]{1,0:T(8,128)(2,1)S(1)}, bf16[48,256]{1,0:T(8,128)(2,1)S(1)}, u32[]{:S(2)}, u32[]{:S(2)}) collective-permute-start(bf16[48,256]{1,0:T(8,128)(2,1)S(1)} %get-tuple-element.47), channel_id=1, source_target_pairs={{2,4},{6,8},{10,12},{14,16},{18,20},{22,24},{26,28},{4,2},{8,6},{1... | collective-permute-start | bytes 73736 | tf_op jit(solution)/shard_map/ppermute | solution.py:495
  10.6 4.5 %collective-permute-start.2 = (bf16[48,256]{1,0:T(8,128)(2,1)S(1)}, bf16[48,256]{1,0:T(8,128)(2,1)S(1)}, u32[]{:S(2)}, u32[]{:S(2)}) collective-permute-start(bf16[48,256]{1,0:T(8,128)(2,1)S(1)} %get-tuple-element.48), channel_id=1, source_target_pairs={{0,2},{4,6},{8,10},{12,14},{16,18},{20,22},{24,26},{28,30},{2,0},{... | collective-permute-start | bytes 73736 | tf_op jit(solution)/shard_map/ppermute | solution.py:495
  15.1 2.5 %all-to-all-done = bf16[32,6,2,128]{3,2,1,0:T(2,128)(2,1)S(1)} async-done(((bf16[32,6,2,128]{3,2,1,0:T(2,128)(2,1)}), bf16[32,6,2,128]{3,2,1,0:T(2,128)(2,1)S(1)}, u32[]{:S(2)}, u32[]{:S(2)}) %all-to-all-start) | async-done | bytes 98336 | tf_op jit(solution)/shard_map/all_to_all | solution.py:501
  17.7 0.2 collective-permute-start
  17.9 0.7 %shard_map.96 = (bf16[9,256,128]{2,1,0:T(8,128)(2,1)S(1)}, f32[48,128]{1,0:T(8,128)S(1)}, f32[2,256,128]{2,1,0:T(8,128)S(1)}) custom-call(s32[1,2,6]{2,1,0:T(2,128)S(1)} %get-tuple-element.31.links_in, bf16[16,128]{1,0:T(8,128)(2,1)S(1)} %get-tuple-element.33.own_ref, bf16[64,2048]{1,0:T(8,128)(2,1)S(1)} %get-tuple-element.34.up_ref, ...), custom_call_target="tpu_custom_call" | custom-call | flops 1000000000 | bytes 2000000 | tf_op jit(solution)/shard_map/pallas_call | solution.py:550
  18.6 0.3 collective-permute-done.other_ref
  18.9 1.2 %shard_map.97 = (f32[256,128]{1,0:T(8,128)S(1)}, bf16[256,128]{1,0:T(8,128)(2,1)S(1)}, bf16[128,256]{1,0:T(8,128)(2,1)S(1)}, bf16[3,2,10,16,256]{4,3,2,1,0:T(8,128)(2,1)S(1)}, bf16[9,256,128]{2,1,0:T(8,128)(2,1)S(1)}) custom-call(s32[1,2,6]{2,1,0:T(2,128)S(1)} %get-tuple-element.31.links_in, bf16[16,128]{1,0:T(8,128)(2,1)S(1)} %collective-permute-done.other_ref, ...), custom_call_target="tpu_custom_call" | custom-call | tf_op jit(solution)/shard_map/pallas_call | solution.py:553
  20.1 0.0 collective-permute-done.2.near
  20.1 1.1 %shard_map.99 = (bf16[448,128]{1,0:T(8,128)(2,1)S(1)}, bf16[256,128]{1,0:T(8,128)(2,1)S(1)}) custom-call(f32[48,128]{1,0:T(8,128)S(1)} %get-tuple-element.36.masks_ref, bf16[1,2,8,8,256]{4,3,2,1,0:T(8,128)(2,1)S(1)} %copy-done, bf16[9,256,128]{2,1,0:T(8,128)(2,1)S(1)} %get-tuple-element.41.band_ref, f32[256,128]{1,0:T(8,128)S(1)} %get-tuple-element.42.slope_ref, ...), custom_call_target="tpu_custom_call" | custom-call | tf_op jit(solution)/shard_map/pallas_call | solution.py:564
  21.2 10.0 %all_to_all.15 = bf16[32,7,2,128]{3,2,1,0:T(2,128)(2,1)S(1)} all-to-all(bf16[32,7,2,128]{3,2,1,0:T(2,128)(2,1)S(1)} %bitcast.10), channel_id=1, replica_groups=mesh['space'=16,'dp'=2] {'space','dp'}, dimensions={0} | all-to-all | bytes 229376 | tf_op jit(solution)/shard_map/all_to_all | solution.py:501
  31.3 0.7 %shard_map.100 = bf16[448,128]{1,0:T(8,128)(2,1)} custom-call(bf16[448,128]{1,0:T(8,128)(2,1)S(1)} %bitcast.6), custom_call_target="tpu_custom_call" | custom-call | tf_op jit(solution)/shard_map/pallas_call | solution.py:582
  32.0 2.6 %all-to-all-start.2 = ((bf16[32,7,2,128]{3,2,1,0:T(2,128)(2,1)}), bf16[32,7,2,128]{3,2,1,0:T(2,128)(2,1)S(1)}, u32[]{:S(2)}, u32[]{:S(2)}) async-start(bf16[32,7,2,128]{3,2,1,0:T(2,128)(2,1)} %bitcast.4), calls=%async_computation.2 | async-start | bytes 229376 | tf_op jit(solution)/shard_map/all_to_all | solution.py:501
  34.6 0.1 shard_map.102
  34.7 0.7 %collective-permute-start.3 = (bf16[48,256]{1,0:T(8,128)(2,1)S(1)}, bf16[48,256]{1,0:T(8,128)(2,1)S(1)}, u32[]{:S(2)}, u32[]{:S(2)}) collective-permute-start(bf16[48,256]{1,0:T(8,128)(2,1)S(1)} %get-tuple-element.54), channel_id=1, source_target_pairs={{2,4},{6,8},{10,12},{14,16},{18,20},{22,24},{26,28},{4,2},{8,6},{1... | collective-permute-start | bytes 73736 | tf_op jit(solution)/shard_map/ppermute | solution.py:495
  35.3 4.4 %collective-permute-start.4 = (bf16[48,256]{1,0:T(8,128)(2,1)S(1)}, bf16[48,256]{1,0:T(8,128)(2,1)S(1)}, u32[]{:S(2)}, u32[]{:S(2)}) collective-permute-start(bf16[48,256]{1,0:T(8,128)(2,1)S(1)} %get-tuple-element.55), channel_id=1, source_target_pairs={{0,2},{4,6},{8,10},{12,14},{16,18},{20,22},{24,26},{28,30},{2,0},{... | collective-permute-start | bytes 73736 | tf_op jit(solution)/shard_map/ppermute | solution.py:495
  39.8 0.3 shard_map.101.band_ref
  40.1 1.7 %collective-permute-done.4.near = bf16[48,256]{1,0:T(8,128)(2,1)S(1)} collective-permute-done((bf16[48,256]{1,0:T(8,128)(2,1)S(1)}, bf16[48,256]{1,0:T(8,128)(2,1)S(1)}, u32[]{:S(2)}, u32[]{:S(2)}) %collective-permute-start.4) | collective-permute-done | bytes 24608 | tf_op jit(solution)/shard_map/ppermute | solution.py:495
  41.8 0.5 %shard_map.103.fine_ref = bf16[1,2,8,8,256]{4,3,2,1,0:T(8,128)(2,1)S(1)} custom-call(f32[48,128]{1,0:T(8,128)S(1)} %get-tuple-element.36.masks_ref, bf16[9,256,128]{2,1,0:T(8,128)(2,1)S(1)} %shard_map.101.band_ref, bf16[256,128]{1,0:T(8,128)(2,1)S(1)} %get-tuple-element.50.lifted_ref, bf16[256,128]{1,0:T(8,128)(2,1)S(1)} %get-tuple-element.51.hidden_ref, ...), custom_call_target="tpu_custom_call" | custom-call | flops 1000000000 | bytes 2000000 | tf_op jit(solution)/shard_map/pallas_call | solution.py:577
  42.3 0.3 all-to-all-done.2
  42.6 1.1 %shard_map.104 = (f32[27,32,32]{2,1,0:T(8,128)}, f32[27,32,32]{2,1,0:T(8,128)}, bf16[1,2,8,8,256]{4,3,2,1,0:T(8,128)(2,1)}) custom-call(bf16[448,128]{1,0:T(8,128)(2,1)S(1)} %bitcast.8, bf16[1,2,8,8,256]{4,3,2,1,0:T(8,128)(2,1)S(1)} %shard_map.103.fine_ref), custom_call_target="tpu_custom_call" | custom-call | tf_op jit(solution)/shard_map/pallas_call | solution.py:597
  (4 shorter events, 0.0 us)
Async XLA Ops:
  2.5 7.3 %copy-start = (bf16[1,2,8,8,256]{4,3,2,1,0:T(8,128)(2,1)S(1)}, bf16[1,2,8,8,256]{4,3,2,1,0:T(8,128)(2,1)}, u32[]{:S(2)}) copy-start(bf16[1,2,8,8,256]{4,3,2,1,0:T(8,128)(2,1)} %cotangent_ref.3) | copy-start | bytes 196612
  2.5 15.1 %all-to-all-start = ((bf16[32,6,2,128]{3,2,1,0:T(2,128)(2,1)}), bf16[32,6,2,128]{3,2,1,0:T(2,128)(2,1)S(1)}, u32[]{:S(2)}, u32[]{:S(2)}) async-start(bf16[32,6,2,128]{3,2,1,0:T(2,128)(2,1)} %bitcast), calls=%async_computation | async-start | bytes 196608 | tf_op jit(solution)/shard_map/all_to_all | solution.py:501
  9.9 10.2 %collective-permute-start.1 = (bf16[48,256]{1,0:T(8,128)(2,1)S(1)}, bf16[48,256]{1,0:T(8,128)(2,1)S(1)}, u32[]{:S(2)}, u32[]{:S(2)}) collective-permute-start(bf16[48,256]{1,0:T(8,128)(2,1)S(1)} %get-tuple-element.47), channel_id=1, source_target_pairs={{2,4},{6,8},{10,12},{14,16},{18,20},{22,24},{26,28},{4,2},{8,6},{1... | collective-permute-start | bytes 73736 | tf_op jit(solution)/shard_map/ppermute | solution.py:495
  10.6 9.5 %collective-permute-start.2 = (bf16[48,256]{1,0:T(8,128)(2,1)S(1)}, bf16[48,256]{1,0:T(8,128)(2,1)S(1)}, u32[]{:S(2)}, u32[]{:S(2)}) collective-permute-start(bf16[48,256]{1,0:T(8,128)(2,1)S(1)} %get-tuple-element.48), channel_id=1, source_target_pairs={{0,2},{4,6},{8,10},{12,14},{16,18},{20,22},{24,26},{28,30},{2,0},{... | collective-permute-start | bytes 73736 | tf_op jit(solution)/shard_map/ppermute | solution.py:495
  17.7 1.2 %collective-permute-start = (bf16[16,128]{1,0:T(8,128)(2,1)S(1)}, bf16[16,128]{1,0:T(8,128)(2,1)S(1)}, u32[]{:S(2)}, u32[]{:S(2)}) collective-permute-start(bf16[16,128]{1,0:T(8,128)(2,1)S(1)} %get-tuple-element.37), channel_id=1, source_target_pairs={{0,1},{1,0},{2,3},{3,2},{4,5},{5,4},{6,7},{7,6},{8,9},{9,8},{10,11... | collective-permute-start | bytes 12296 | tf_op jit(solution)/shard_map/ppermute | solution.py:534
  32.0 10.6 %all-to-all-start.2 = ((bf16[32,7,2,128]{3,2,1,0:T(2,128)(2,1)}), bf16[32,7,2,128]{3,2,1,0:T(2,128)(2,1)S(1)}, u32[]{:S(2)}, u32[]{:S(2)}) async-start(bf16[32,7,2,128]{3,2,1,0:T(2,128)(2,1)} %bitcast.4), calls=%async_computation.2 | async-start | bytes 229376 | tf_op jit(solution)/shard_map/all_to_all | solution.py:501
  34.7 5.4 %collective-permute-start.3 = (bf16[48,256]{1,0:T(8,128)(2,1)S(1)}, bf16[48,256]{1,0:T(8,128)(2,1)S(1)}, u32[]{:S(2)}, u32[]{:S(2)}) collective-permute-start(bf16[48,256]{1,0:T(8,128)(2,1)S(1)} %get-tuple-element.54), channel_id=1, source_target_pairs={{2,4},{6,8},{10,12},{14,16},{18,20},{22,24},{26,28},{4,2},{8,6},{1... | collective-permute-start | bytes 73736 | tf_op jit(solution)/shard_map/ppermute | solution.py:495
  35.3 6.5 %collective-permute-start.4 = (bf16[48,256]{1,0:T(8,128)(2,1)S(1)}, bf16[48,256]{1,0:T(8,128)(2,1)S(1)}, u32[]{:S(2)}, u32[]{:S(2)}) collective-permute-start(bf16[48,256]{1,0:T(8,128)(2,1)S(1)} %get-tuple-element.55), channel_id=1, source_target_pairs={{0,2},{4,6},{8,10},{12,14},{16,18},{20,22},{24,26},{28,30},{2,0},{... | collective-permute-start | bytes 73736 | tf_op jit(solution)/shard_map/ppermute | solution.py:495

commit v26 on v25

--- a/solution.py
+++ b/solution.py
@@ -149,14 +149,15 @@
 
 
 def early_kernel(
-    links_in, own_ref, up_ref, weights_ref,
-    band_ref, masks_ref, volumes_out,
+    links_in, own_ref, up_ref, one_ref, two_ref,
+    band_ref, back_ref, masks_ref, volumes_out,
     rows_ref, links_ref, links_sem,
 ):
     links_copy = pltpu.make_async_copy(links_in, links_ref, links_sem)
     links_copy.start()
     lift(own_ref, up_ref, rows_ref, volumes_out, 0)
-    build_band(band_ref, weight_rows(weights_ref[...].astype(F32)))
+    build_band(band_ref, weight_rows(one_ref[...].astype(F32)))
+    build_band(back_ref, flipped_rows(two_ref[...].astype(F32)))
     links_copy.wait()
     put_masks(masks_ref, links_ref)
 
@@ -265,8 +266,8 @@
 
 
 def first_kernel(
-    links_in, other_ref, up_ref, band_ref, lifted_half, weights_ref,
-    slope_out, hidden_out, turned_out, pad_out, back_out,
+    links_in, other_ref, up_ref, band_ref, lifted_half,
+    slope_out, hidden_out, turned_out, pad_out,
     volumes_ref, rows_ref, links_ref, links_sem,
 ):
     links_copy = pltpu.make_async_copy(links_in, links_ref, links_sem)
@@ -301,12 +302,11 @@
         put_padded(pad_out, brick, own, x_face(0), x_face(1), y_face(2), y_face(3), z_face(4), z_face(5))
     pre = convolve(pad_out, band_ref)
     sigmoid = 1.0 / (1.0 + jnp.exp(-pre))
-    hidden = (pre / (1.0 + jnp.exp(-pre))).astype(BF16)
+    hidden = (pre * sigmoid).astype(BF16)
     slope_out[...] = sigmoid * (1.0 + pre * (1.0 - sigmoid))
     hidden_out[...] = hidden
     hidden = hidden.astype(F32)
     turned_out[...] = jnp.transpose(hidden).astype(BF16)
-    build_band(back_out, flipped_rows(weights_ref[...].astype(F32)))
 
 
 def hidden_faces_kernel(hidden_ref, _parts, high_out, low_out, far_out, near_out, halves_ref, faces_ref):
@@ -547,18 +547,23 @@
     masks = shape(BRICKS * 6 * 2 * BRICKS, 128, dtype=F32)
     lifted_half = shape(2, 4 * CUBE, 128, dtype=F32)
     window_rows = pltpu.VMEM((8 * tiles, 128), F32)
-    band_one, masks, lifted_half = call(
-        early_kernel, (shape(*BAND), masks, lifted_half), [window_rows, *links], hbm=(0,), inputs=4, cost=cost
-    )(face_links, own, up_weight, conv_one)
-    slope, hidden, turned, lifted_pad, band_back = call(
+    band_one, band_back, masks, lifted_half = call(
+        early_kernel,
+        (shape(*BAND), shape(*BAND), masks, lifted_half),
+        [window_rows, *links],
+        hbm=(0,),
+        inputs=5,
+        cost=cost,
+    )(face_links, own, up_weight, conv_one, conv_two)
+    slope, hidden, turned, lifted_pad = call(
         first_kernel,
         (
-            shape(ROWS, HALF, dtype=F32), volume, shape(HALF, ROWS), shape(*pad_shape), shape(*BAND),
+            shape(ROWS, HALF, dtype=F32), volume, shape(HALF, ROWS), shape(*pad_shape),
         ),
         [pltpu.VMEM((2, 8 * CUBE, 128), F32), window_rows, *links],
         hbm=(0,),
-        inputs=6,
-    )(face_links, other, up_weight, band_one, lifted_half, conv_two)
+        inputs=5,
+    )(face_links, other, up_weight, band_one, lifted_half)
     share = 2 * -(-GROUPS * CHANNELS // everyone)
     packed_rows = (everyone * share, 128)
     sums, lifted = call(

time: 44 us -> 44 us (level)
  transfers between devices with their start and end apart: 7 -> 7, of which waited for: 4 -> 4; matrix products, arithmetic and copies ran while one was open for 0% -> 0% of each run, Pallas kernels for 7% -> 6%
where the time goes in v26:
time: 44 us; the launch traced here: 43.7 us
  starting transfers between devices  20.4 us (46%)
  blocking collectives  10.1 us (23%)
  Pallas kernels  7.44 us (17%)
  waiting for transfers between devices  4.96 us (11%)
  between operations  0.77 us (2%)
    ppermute x4, starting transfers between devices, swapped(): lax.ppermute(value, 'space', pairs + [(target, source) for source, target...  10.3 us
    all_to_all x1, blocking collectives, exchanged(): lax.all_to_all(shares, axes, split_axis=0, concat_axis=0, tiled=True)  10.1 us
    all_to_all x2, starting transfers between devices, exchanged(): lax.all_to_all(shares, axes, split_axis=0, concat_axis=0, tiled=True)  9.89 us
    all_to_all x2, waiting for transfers between devices, exchanged(): lax.all_to_all(shares, axes, split_axis=0, concat_axis=0, tiled=True)  2.81 us
    pallas_call x1, Pallas kernels, body(): call(functools.partial(pick_kernel, split, len(extras)), (shape(*blocks),...  1.87 us
    ppermute x4, waiting for transfers between devices, swapped(): lax.ppermute(value, 'space', pairs + [(target, source) for source, target...  1.71 us
    pallas_call x1, Pallas kernels, body(): call(second_kernel, (shape(*packed_rows), volume), [pool, pool, pad, pltp...  1.11 us
    pallas_call x1, Pallas kernels, body(): call(first_kernel, (shape(ROWS, HALF, dtype=F32), volume, shape(HALF, ROW...  1.09 us
  transfers between devices with their start and end apart: 7, of which 4 were waited for; matrix products, arithmetic and copies ran while one was open for 0% of the time, Pallas kernels for 6%

profile of v26, /device:TPU:0, one launch (start us, length us, event | category | flops | bytes accessed | tf_op | source)
XLA Modules:
  0.0 43.7 jit_solution(8053621757477566439)
XLA Ops:
  0.6 1.9 %shard_map.94 = (bf16[384,128]{1,0:T(8,128)(2,1)}, bf16[64,2048]{1,0:T(8,128)(2,1)S(1)}, bf16[27,32,32]{2,1,0:T(8,128)(2,1)S(1)}, bf16[27,32,32]{2,1,0:T(8,128)(2,1)S(1)}, s32[1,2,6]{2,1,0:T(2,128)S(1)}) custom-call(s32[1,32]{1,0:T(1,128)} %ids_hbm.1, bf16[1,64,512]{2,1,0:T(8,128)(2,1)} %latents_hbm.1, bf16[64,2048]{1,0:T(8,128)(2,1)} %refs_0_.1, ...), custom_call_target="tpu_custom_call" | custom-call | tf_op jit(solution)/shard_map/pallas_call | solution.py:515
  2.5 0.0 copy-start
  2.5 7.3 %all-to-all-start = ((bf16[32,6,2,128]{3,2,1,0:T(2,128)(2,1)}), bf16[32,6,2,128]{3,2,1,0:T(2,128)(2,1)S(1)}, u32[]{:S(2)}, u32[]{:S(2)}) async-start(bf16[32,6,2,128]{3,2,1,0:T(2,128)(2,1)} %bitcast), calls=%async_computation | async-start | bytes 196608 | tf_op jit(solution)/shard_map/all_to_all | solution.py:501
  9.8 0.1 shard_map.98
  9.9 0.7 %collective-permute-start.1 = (bf16[48,256]{1,0:T(8,128)(2,1)S(1)}, bf16[48,256]{1,0:T(8,128)(2,1)S(1)}, u32[]{:S(2)}, u32[]{:S(2)}) collective-permute-start(bf16[48,256]{1,0:T(8,128)(2,1)S(1)} %get-tuple-element.47), channel_id=1, source_target_pairs={{2,4},{6,8},{10,12},{14,16},{18,20},{22,24},{26,28},{4,2},{8,6},{1... | collective-permute-start | bytes 73736 | tf_op jit(solution)/shard_map/ppermute | solution.py:495
  10.6 4.5 %collective-permute-start.2 = (bf16[48,256]{1,0:T(8,128)(2,1)S(1)}, bf16[48,256]{1,0:T(8,128)(2,1)S(1)}, u32[]{:S(2)}, u32[]{:S(2)}) collective-permute-start(bf16[48,256]{1,0:T(8,128)(2,1)S(1)} %get-tuple-element.48), channel_id=1, source_target_pairs={{0,2},{4,6},{8,10},{12,14},{16,18},{20,22},{24,26},{28,30},{2,0},{... | collective-permute-start | bytes 73736 | tf_op jit(solution)/shard_map/ppermute | solution.py:495
  15.1 2.5 %all-to-all-done = bf16[32,6,2,128]{3,2,1,0:T(2,128)(2,1)S(1)} async-done(((bf16[32,6,2,128]{3,2,1,0:T(2,128)(2,1)}), bf16[32,6,2,128]{3,2,1,0:T(2,128)(2,1)S(1)}, u32[]{:S(2)}, u32[]{:S(2)}) %all-to-all-start) | async-done | bytes 98336 | tf_op jit(solution)/shard_map/all_to_all | solution.py:501
  17.7 0.2 collective-permute-start
  17.9 0.6 %shard_map.96 = (bf16[9,256,128]{2,1,0:T(8,128)(2,1)S(1)}, bf16[9,256,128]{2,1,0:T(8,128)(2,1)S(1)}, f32[48,128]{1,0:T(8,128)S(1)}, f32[2,256,128]{2,1,0:T(8,128)S(1)}) custom-call(s32[1,2,6]{2,1,0:T(2,128)S(1)} %get-tuple-element.31.links_in, bf16[16,128]{1,0:T(8,128)(2,1)S(1)} %get-tuple-element.33.own_ref, bf16[64,2048]{1,0:T(8,128)(2,1)S(1)} %get-tuple-element.34.up_ref, ...), custom_call_target="tpu_custom_call" | custom-call | flops 1000000000 | bytes 2000000 | tf_op jit(solution)/shard_map/pallas_call | solution.py:550
  18.5 0.4 collective-permute-done.other_ref
  18.9 1.1 %shard_map.97 = (f32[256,128]{1,0:T(8,128)S(1)}, bf16[256,128]{1,0:T(8,128)(2,1)S(1)}, bf16[128,256]{1,0:T(8,128)(2,1)S(1)}, bf16[3,2,10,16,256]{4,3,2,1,0:T(8,128)(2,1)S(1)}) custom-call(s32[1,2,6]{2,1,0:T(2,128)S(1)} %get-tuple-element.31.links_in, bf16[16,128]{1,0:T(8,128)(2,1)S(1)} %collective-permute-done.other_ref, ...), custom_call_target="tpu_custom_call" | custom-call | tf_op jit(solution)/shard_map/pallas_call | solution.py:558
  20.0 0.0 collective-permute-done.1.far
  20.0 1.1 %shard_map.99 = (bf16[448,128]{1,0:T(8,128)(2,1)S(1)}, bf16[256,128]{1,0:T(8,128)(2,1)S(1)}) custom-call(f32[48,128]{1,0:T(8,128)S(1)} %get-tuple-element.37.masks_ref, bf16[1,2,8,8,256]{4,3,2,1,0:T(8,128)(2,1)S(1)} %copy-done, bf16[9,256,128]{2,1,0:T(8,128)(2,1)S(1)} %get-tuple-element.38.band_ref, f32[256,128]{1,0:T(8,128)S(1)} %get-tuple-element.42.slope_ref, ...), custom_call_target="tpu_custom_call" | custom-call | tf_op jit(solution)/shard_map/pallas_call | solution.py:569
  21.1 10.1 %all_to_all.15 = bf16[32,7,2,128]{3,2,1,0:T(2,128)(2,1)S(1)} all-to-all(bf16[32,7,2,128]{3,2,1,0:T(2,128)(2,1)S(1)} %bitcast.10), channel_id=1, replica_groups=mesh['space'=16,'dp'=2] {'space','dp'}, dimensions={0} | all-to-all | bytes 229376 | tf_op jit(solution)/shard_map/all_to_all | solution.py:501
  31.3 0.7 %shard_map.100 = bf16[448,128]{1,0:T(8,128)(2,1)} custom-call(bf16[448,128]{1,0:T(8,128)(2,1)S(1)} %bitcast.6), custom_call_target="tpu_custom_call" | custom-call | tf_op jit(solution)/shard_map/pallas_call | solution.py:587
  32.0 2.6 %all-to-all-start.2 = ((bf16[32,7,2,128]{3,2,1,0:T(2,128)(2,1)}), bf16[32,7,2,128]{3,2,1,0:T(2,128)(2,1)S(1)}, u32[]{:S(2)}, u32[]{:S(2)}) async-start(bf16[32,7,2,128]{3,2,1,0:T(2,128)(2,1)} %bitcast.4), calls=%async_computation.2 | async-start | bytes 229376 | tf_op jit(solution)/shard_map/all_to_all | solution.py:501
  34.6 0.1 shard_map.102
  34.7 0.7 %collective-permute-start.3 = (bf16[48,256]{1,0:T(8,128)(2,1)S(1)}, bf16[48,256]{1,0:T(8,128)(2,1)S(1)}, u32[]{:S(2)}, u32[]{:S(2)}) collective-permute-start(bf16[48,256]{1,0:T(8,128)(2,1)S(1)} %get-tuple-element.54), channel_id=1, source_target_pairs={{2,4},{6,8},{10,12},{14,16},{18,20},{22,24},{26,28},{4,2},{8,6},{1... | collective-permute-start | bytes 73736 | tf_op jit(solution)/shard_map/ppermute | solution.py:495
  35.3 4.4 %collective-permute-start.4 = (bf16[48,256]{1,0:T(8,128)(2,1)S(1)}, bf16[48,256]{1,0:T(8,128)(2,1)S(1)}, u32[]{:S(2)}, u32[]{:S(2)}) collective-permute-start(bf16[48,256]{1,0:T(8,128)(2,1)S(1)} %get-tuple-element.55), channel_id=1, source_target_pairs={{0,2},{4,6},{8,10},{12,14},{16,18},{20,22},{24,26},{28,30},{2,0},{... | collective-permute-start | bytes 73736 | tf_op jit(solution)/shard_map/ppermute | solution.py:495
  39.8 0.3 shard_map.101.band_ref
  40.1 1.7 %collective-permute-done.4.near = bf16[48,256]{1,0:T(8,128)(2,1)S(1)} collective-permute-done((bf16[48,256]{1,0:T(8,128)(2,1)S(1)}, bf16[48,256]{1,0:T(8,128)(2,1)S(1)}, u32[]{:S(2)}, u32[]{:S(2)}) %collective-permute-start.4) | collective-permute-done | bytes 24608 | tf_op jit(solution)/shard_map/ppermute | solution.py:495
  41.8 0.5 %shard_map.103.fine_ref = bf16[1,2,8,8,256]{4,3,2,1,0:T(8,128)(2,1)S(1)} custom-call(f32[48,128]{1,0:T(8,128)S(1)} %get-tuple-element.37.masks_ref, bf16[9,256,128]{2,1,0:T(8,128)(2,1)S(1)} %shard_map.101.band_ref, bf16[256,128]{1,0:T(8,128)(2,1)S(1)} %get-tuple-element.50.lifted_ref, bf16[256,128]{1,0:T(8,128)(2,1)S(1)} %get-tuple-element.51.hidden_ref, ...), custom_call_target="tpu_custom_call" | custom-call | flops 1000000000 | bytes 2000000 | tf_op jit(solution)/shard_map/pallas_call | solution.py:582
  42.3 0.3 all-to-all-done.2
  42.6 1.1 %shard_map.104 = (f32[27,32,32]{2,1,0:T(8,128)}, f32[27,32,32]{2,1,0:T(8,128)}, bf16[1,2,8,8,256]{4,3,2,1,0:T(8,128)(2,1)}) custom-call(bf16[448,128]{1,0:T(8,128)(2,1)S(1)} %bitcast.8, bf16[1,2,8,8,256]{4,3,2,1,0:T(8,128)(2,1)S(1)} %shard_map.103.fine_ref), custom_call_target="tpu_custom_call" | custom-call | tf_op jit(solution)/shard_map/pallas_call | solution.py:602
  (4 shorter events, 0.0 us)
Async XLA Ops:
  2.5 7.3 %copy-start = (bf16[1,2,8,8,256]{4,3,2,1,0:T(8,128)(2,1)S(1)}, bf16[1,2,8,8,256]{4,3,2,1,0:T(8,128)(2,1)}, u32[]{:S(2)}) copy-start(bf16[1,2,8,8,256]{4,3,2,1,0:T(8,128)(2,1)} %cotangent_ref.3) | copy-start | bytes 196612
  2.5 15.1 %all-to-all-start = ((bf16[32,6,2,128]{3,2,1,0:T(2,128)(2,1)}), bf16[32,6,2,128]{3,2,1,0:T(2,128)(2,1)S(1)}, u32[]{:S(2)}, u32[]{:S(2)}) async-start(bf16[32,6,2,128]{3,2,1,0:T(2,128)(2,1)} %bitcast), calls=%async_computation | async-start | bytes 196608 | tf_op jit(solution)/shard_map/all_to_all | solution.py:501
  9.9 10.1 %collective-permute-start.1 = (bf16[48,256]{1,0:T(8,128)(2,1)S(1)}, bf16[48,256]{1,0:T(8,128)(2,1)S(1)}, u32[]{:S(2)}, u32[]{:S(2)}) collective-permute-start(bf16[48,256]{1,0:T(8,128)(2,1)S(1)} %get-tuple-element.47), channel_id=1, source_target_pairs={{2,4},{6,8},{10,12},{14,16},{18,20},{22,24},{26,28},{4,2},{8,6},{1... | collective-permute-start | bytes 73736 | tf_op jit(solution)/shard_map/ppermute | solution.py:495
  10.6 9.4 %collective-permute-start.2 = (bf16[48,256]{1,0:T(8,128)(2,1)S(1)}, bf16[48,256]{1,0:T(8,128)(2,1)S(1)}, u32[]{:S(2)}, u32[]{:S(2)}) collective-permute-start(bf16[48,256]{1,0:T(8,128)(2,1)S(1)} %get-tuple-element.48), channel_id=1, source_target_pairs={{0,2},{4,6},{8,10},{12,14},{16,18},{20,22},{24,26},{28,30},{2,0},{... | collective-permute-start | bytes 73736 | tf_op jit(solution)/shard_map/ppermute | solution.py:495
  17.7 1.2 %collective-permute-start = (bf16[16,128]{1,0:T(8,128)(2,1)S(1)}, bf16[16,128]{1,0:T(8,128)(2,1)S(1)}, u32[]{:S(2)}, u32[]{:S(2)}) collective-permute-start(bf16[16,128]{1,0:T(8,128)(2,1)S(1)} %get-tuple-element.39), channel_id=1, source_target_pairs={{0,1},{1,0},{2,3},{3,2},{4,5},{5,4},{6,7},{7,6},{8,9},{9,8},{10,11... | collective-permute-start | bytes 12296 | tf_op jit(solution)/shard_map/ppermute | solution.py:534
  32.0 10.6 %all-to-all-start.2 = ((bf16[32,7,2,128]{3,2,1,0:T(2,128)(2,1)}), bf16[32,7,2,128]{3,2,1,0:T(2,128)(2,1)S(1)}, u32[]{:S(2)}, u32[]{:S(2)}) async-start(bf16[32,7,2,128]{3,2,1,0:T(2,128)(2,1)} %bitcast.4), calls=%async_computation.2 | async-start | bytes 229376 | tf_op jit(solution)/shard_map/all_to_all | solution.py:501
  34.7 5.4 %collective-permute-start.3 = (bf16[48,256]{1,0:T(8,128)(2,1)S(1)}, bf16[48,256]{1,0:T(8,128)(2,1)S(1)}, u32[]{:S(2)}, u32[]{:S(2)}) collective-permute-start(bf16[48,256]{1,0:T(8,128)(2,1)S(1)} %get-tuple-element.54), channel_id=1, source_target_pairs={{2,4},{6,8},{10,12},{14,16},{18,20},{22,24},{26,28},{4,2},{8,6},{1... | collective-permute-start | bytes 73736 | tf_op jit(solution)/shard_map/ppermute | solution.py:495
  35.3 6.5 %collective-permute-start.4 = (bf16[48,256]{1,0:T(8,128)(2,1)S(1)}, bf16[48,256]{1,0:T(8,128)(2,1)S(1)}, u32[]{:S(2)}, u32[]{:S(2)}) collective-permute-start(bf16[48,256]{1,0:T(8,128)(2,1)S(1)} %get-tuple-element.55), channel_id=1, source_target_pairs={{0,2},{4,6},{8,10},{12,14},{16,18},{20,22},{24,26},{28,30},{2,0},{... | collective-permute-start | bytes 73736 | tf_op jit(solution)/shard_map/ppermute | solution.py:495

commit v27 on v26

--- a/solution.py
+++ b/solution.py
@@ -424,24 +424,14 @@
     fine_out[...] = fine.astype(BF16).reshape(fine_out.shape)
 
 
-def sum_kernel(devices, scale, parts_ref, out_hbm, rows_ref, shares_ref, sems):
+def sum_kernel(devices, scale, parts_ref, out_ref, rows_ref):
     rows_ref[...] = parts_ref[...].astype(F32)
     share = rows_ref.shape[0] // devices
     pieces = [rows_ref[share * i : share * i + share] for i in range(devices)]
     while len(pieces) > 1:
         pairs = [a + b for a, b in zip(pieces[::2], pieces[1::2])]
         pieces = pairs + pieces[len(pieces) - len(pieces) % 2 :]
-    total = pieces[0] * scale
-    some = shares_ref.shape[0]
-    for i in range(some // share):
-        rows_ref[share * i : share * i + share] = total
-    shares_ref[...] = rows_ref[0:some].astype(BF16)
-    copies = []
-    for i in range(out_hbm.shape[0] // some):
-        copies.append(pltpu.make_async_copy(shares_ref, out_hbm.at[pl.ds(some * i, some)], sems.at[i]))
-        copies[-1].start()
-    for copy in copies:
-        copy.wait()
+    out_ref[...] = (pieces[0] * scale).astype(BF16)
 
 
 def unpack_kernel(sums_ref, fine_ref, one_out, two_out, fine_out, rows_ref, one_ref, two_ref, sems, fine_sem):
@@ -583,18 +573,10 @@
         masks, band_two, lifted, hidden, hidden_high, hidden_low, hidden_far, hidden_near
     )
     scale = 1.0 / math.sqrt(lax.axis_size("dp") * devices * BRICKS * EDGE**3)
-    times = 4 if everyone % 32 == 0 else 1
     total = call(
-        functools.partial(sum_kernel, everyone, scale),
-        shape(*packed_rows),
-        [
-            pltpu.VMEM(packed_rows, F32),
-            pltpu.VMEM((packed_rows[0] // times, 128), BF16),
-            pltpu.SemaphoreType.DMA((times,)),
-        ],
-        out=pl.ANY,
+        functools.partial(sum_kernel, everyone, scale), shape(share, 128), [pltpu.VMEM(packed_rows, F32)]
     )(parts)
-    gathered = exchanged(total)
+    gathered = lax.all_gather(total.reshape(-1, 2, 128), ("space", "dp"), tiled=True).reshape(packed_rows)
     grads = shape(27, CHANNELS, CHANNELS, dtype=F32)
     block = pltpu.VMEM(grads.shape, F32)
     scratch = [pltpu.VMEM(packed_rows, F32), block, block]

time: 44 us -> 76.8 us (1.75)
  blocking collectives: 10.1 us -> 38.3 us
  waiting for transfers between devices: 4.96 us -> 10.6 us
  starting transfers between devices: 20.4 us -> 19.3 us
    all_gather x0 -> x1, blocking collectives: none -> 38.3 us  [body(): lax.all_gather(total.reshape(-1, 2, 128), ('space', 'dp'), tiled=True)]
    all_to_all x1 -> x0, blocking collectives: 10.1 us -> none  [exchanged(): lax.all_to_all(shares, axes, split_axis=0, concat_axis=0, tiled=True)]
    all_to_all x2, waiting for transfers between devices: 2.81 us -> 10.2 us  [exchanged(): lax.all_to_all(shares, axes, split_axis=0, concat_axis=0, tiled=True)]
    ppermute x4, waiting for transfers between devices: 1.71 us -> 0.01 us  [swapped(): lax.ppermute(value, 'space', pairs + [(target, source) for source, target...]
    ppermute x4, starting transfers between devices: 10.3 us -> 9.29 us  [swapped(): lax.ppermute(value, 'space', pairs + [(target, source) for source, target...]
  transfers between devices with their start and end apart: 7 -> 7, of which waited for: 4 -> 3; matrix products, arithmetic and copies ran while one was open for 0% -> 0% of each run, Pallas kernels for 6% -> 3%
where the time goes in v27:
time: 76.8 us; the launch traced here: 76.5 us
  blocking collectives  38.3 us (50%)
  starting transfers between devices  19.3 us (25%)
  waiting for transfers between devices  10.6 us (14%)
  Pallas kernels  7.42 us (10%)
    all_gather x1, blocking collectives, body(): lax.all_gather(total.reshape(-1, 2, 128), ('space', 'dp'), tiled=True)  38.3 us
    all_to_all x2, waiting for transfers between devices, exchanged(): lax.all_to_all(shares, axes, split_axis=0, concat_axis=0, tiled=True)  10.2 us
    all_to_all x2, starting transfers between devices, exchanged(): lax.all_to_all(shares, axes, split_axis=0, concat_axis=0, tiled=True)  9.88 us
    ppermute x4, starting transfers between devices, swapped(): lax.ppermute(value, 'space', pairs + [(target, source) for source, target...  9.29 us
    pallas_call x1, Pallas kernels, body(): call(functools.partial(pick_kernel, split, len(extras)), (shape(*blocks),...  1.87 us
    pallas_call x1, Pallas kernels, body(): call(second_kernel, (shape(*packed_rows), volume), [pool, pool, pad, pltp...  1.76 us
  transfers between devices with their start and end apart: 7, of which 3 were waited for; matrix products, arithmetic and copies ran while one was open for 0% of the time, Pallas kernels for 3%

profile of v27, /device:TPU:0, one launch (start us, length us, event | category | flops | bytes accessed | tf_op | source)
XLA Modules:
  0.0 76.5 jit_solution(8824305292535858936)
XLA Ops:
  0.6 1.9 %shard_map.94 = (bf16[384,128]{1,0:T(8,128)(2,1)}, bf16[64,2048]{1,0:T(8,128)(2,1)S(1)}, bf16[27,32,32]{2,1,0:T(8,128)(2,1)S(1)}, bf16[27,32,32]{2,1,0:T(8,128)(2,1)S(1)}, s32[1,2,6]{2,1,0:T(2,128)S(1)}) custom-call(s32[1,32]{1,0:T(1,128)} %ids_hbm.1, bf16[1,64,512]{2,1,0:T(8,128)(2,1)} %latents_hbm.1, bf16[64,2048]{1,0:T(8,128)(2,1)} %refs_0_.1, ...), custom_call_target="tpu_custom_call" | custom-call | tf_op jit(solution)/shard_map/pallas_call | solution.py:505
  2.5 0.0 copy-start
  2.5 7.3 %all-to-all-start = ((bf16[32,6,2,128]{3,2,1,0:T(2,128)(2,1)}), bf16[32,6,2,128]{3,2,1,0:T(2,128)(2,1)S(1)}, u32[]{:S(2)}, u32[]{:S(2)}) async-start(bf16[32,6,2,128]{3,2,1,0:T(2,128)(2,1)} %bitcast), calls=%async_computation | async-start | bytes 196608 | tf_op jit(solution)/shard_map/all_to_all | solution.py:491
  9.8 0.1 shard_map.98
  9.9 0.7 collective-permute-start.1
  10.6 4.5 %collective-permute-start.2 = (bf16[48,256]{1,0:T(8,128)(2,1)S(1)}, bf16[48,256]{1,0:T(8,128)(2,1)S(1)}, u32[]{:S(2)}, u32[]{:S(2)}) collective-permute-start(bf16[48,256]{1,0:T(8,128)(2,1)S(1)} %get-tuple-element.48), channel_id=1, source_target_pairs={{0,2},{4,6},{8,10},{12,14},{16,18},{20,22},{24,26},{28,30},{2,0},{... | collective-permute-start | bytes 73736 | tf_op jit(solution)/shard_map/ppermute | solution.py:485
  15.1 2.5 %all-to-all-done = bf16[32,6,2,128]{3,2,1,0:T(2,128)(2,1)S(1)} async-done(((bf16[32,6,2,128]{3,2,1,0:T(2,128)(2,1)}), bf16[32,6,2,128]{3,2,1,0:T(2,128)(2,1)S(1)}, u32[]{:S(2)}, u32[]{:S(2)}) %all-to-all-start) | async-done | bytes 98336 | tf_op jit(solution)/shard_map/all_to_all | solution.py:491
  17.7 0.2 collective-permute-start
  17.9 0.6 shard_map.96
  18.5 0.4 collective-permute-done.other_ref
  18.9 1.1 %shard_map.97 = (f32[256,128]{1,0:T(8,128)S(1)}, bf16[256,128]{1,0:T(8,128)(2,1)S(1)}, bf16[128,256]{1,0:T(8,128)(2,1)S(1)}, bf16[3,2,10,16,256]{4,3,2,1,0:T(8,128)(2,1)S(1)}) custom-call(s32[1,2,6]{2,1,0:T(2,128)S(1)} %get-tuple-element.31.links_in, bf16[16,128]{1,0:T(8,128)(2,1)S(1)} %collective-permute-done.other_ref, ...), custom_call_target="tpu_custom_call" | custom-call | tf_op jit(solution)/shard_map/pallas_call | solution.py:548
  20.0 0.0 collective-permute-done.1.far
  20.0 0.0 collective-permute-done.2.near
  20.0 1.8 %shard_map.99 = (bf16[448,128]{1,0:T(8,128)(2,1)}, bf16[256,128]{1,0:T(8,128)(2,1)S(1)}) custom-call(f32[48,128]{1,0:T(8,128)S(1)} %get-tuple-element.37.masks_ref, bf16[1,2,8,8,256]{4,3,2,1,0:T(8,128)(2,1)S(1)} %copy-done, bf16[9,256,128]{2,1,0:T(8,128)(2,1)S(1)} %get-tuple-element.38.band_ref, f32[256,128]{1,0:T(8,128)S(1)} %get-tuple-element.42.slope_ref, ...), custom_call_target="tpu_custom_call" | custom-call | tf_op jit(solution)/shard_map/pallas_call | solution.py:559
  21.8 2.6 %all-to-all-start.1 = ((bf16[32,7,2,128]{3,2,1,0:T(2,128)(2,1)}), bf16[32,7,2,128]{3,2,1,0:T(2,128)(2,1)S(1)}, u32[]{:S(2)}, u32[]{:S(2)}) async-start(bf16[32,7,2,128]{3,2,1,0:T(2,128)(2,1)} %bitcast.2), calls=%async_computation.1 | async-start | bytes 229376 | tf_op jit(solution)/shard_map/all_to_all | solution.py:491
  24.4 0.3 shard_map.101.band_ref
  24.7 7.7 %all-to-all-done.1 = bf16[32,7,2,128]{3,2,1,0:T(2,128)(2,1)S(1)} async-done(((bf16[32,7,2,128]{3,2,1,0:T(2,128)(2,1)}), bf16[32,7,2,128]{3,2,1,0:T(2,128)(2,1)S(1)}, u32[]{:S(2)}, u32[]{:S(2)}) %all-to-all-start.1) | async-done | bytes 114720 | tf_op jit(solution)/shard_map/all_to_all | solution.py:491
  32.4 0.1 shard_map.102
  32.5 0.7 collective-permute-start.3
  33.2 3.4 %collective-permute-start.4 = (bf16[48,256]{1,0:T(8,128)(2,1)S(1)}, bf16[48,256]{1,0:T(8,128)(2,1)S(1)}, u32[]{:S(2)}, u32[]{:S(2)}) collective-permute-start(bf16[48,256]{1,0:T(8,128)(2,1)S(1)} %get-tuple-element.55), channel_id=1, source_target_pairs={{0,2},{4,6},{8,10},{12,14},{16,18},{20,22},{24,26},{28,30},{2,0},{... | collective-permute-start | bytes 73736 | tf_op jit(solution)/shard_map/ppermute | solution.py:485
  36.6 38.3 %all_gather.3 = bf16[224,2,128]{2,1,0:T(2,128)(2,1)S(1)} all-gather(bf16[7,2,128]{2,1,0:T(2,128)(2,1)S(1)} %reshape.28), channel_id=1, replica_groups=mesh['space'=16,'dp'=2] {'space','dp'}, dimensions={0}, use_global_device_ids=true | all-gather | bytes 118272 | tf_op jit(solution)/shard_map/all_gather | solution.py:579
  74.9 0.0 collective-permute-done.3.far
  74.9 0.5 shard_map.103.fine_ref
  75.4 1.1 %shard_map.104 = (f32[27,32,32]{2,1,0:T(8,128)}, f32[27,32,32]{2,1,0:T(8,128)}, bf16[1,2,8,8,256]{4,3,2,1,0:T(8,128)(2,1)}) custom-call(bf16[448,128]{1,0:T(8,128)(2,1)S(1)} %bitcast.7, bf16[1,2,8,8,256]{4,3,2,1,0:T(8,128)(2,1)S(1)} %shard_map.103.fine_ref), custom_call_target="tpu_custom_call" | custom-call | tf_op jit(solution)/shard_map/pallas_call | solution.py:584
  (5 shorter events, 0.1 us)
Async XLA Ops:
  2.5 7.3 %copy-start = (bf16[1,2,8,8,256]{4,3,2,1,0:T(8,128)(2,1)S(1)}, bf16[1,2,8,8,256]{4,3,2,1,0:T(8,128)(2,1)}, u32[]{:S(2)}) copy-start(bf16[1,2,8,8,256]{4,3,2,1,0:T(8,128)(2,1)} %cotangent_ref.3) | copy-start | bytes 196612
  2.5 15.1 %all-to-all-start = ((bf16[32,6,2,128]{3,2,1,0:T(2,128)(2,1)}), bf16[32,6,2,128]{3,2,1,0:T(2,128)(2,1)S(1)}, u32[]{:S(2)}, u32[]{:S(2)}) async-start(bf16[32,6,2,128]{3,2,1,0:T(2,128)(2,1)} %bitcast), calls=%async_computation | async-start | bytes 196608 | tf_op jit(solution)/shard_map/all_to_all | solution.py:491
  9.9 10.1 %collective-permute-start.1 = (bf16[48,256]{1,0:T(8,128)(2,1)S(1)}, bf16[48,256]{1,0:T(8,128)(2,1)S(1)}, u32[]{:S(2)}, u32[]{:S(2)}) collective-permute-start(bf16[48,256]{1,0:T(8,128)(2,1)S(1)} %get-tuple-element.47), channel_id=1, source_target_pairs={{2,4},{6,8},{10,12},{14,16},{18,20},{22,24},{26,28},{4,2},{8,6},{1... | collective-permute-start | bytes 73736 | tf_op jit(solution)/shard_map/ppermute | solution.py:485
  10.6 9.4 %collective-permute-start.2 = (bf16[48,256]{1,0:T(8,128)(2,1)S(1)}, bf16[48,256]{1,0:T(8,128)(2,1)S(1)}, u32[]{:S(2)}, u32[]{:S(2)}) collective-permute-start(bf16[48,256]{1,0:T(8,128)(2,1)S(1)} %get-tuple-element.48), channel_id=1, source_target_pairs={{0,2},{4,6},{8,10},{12,14},{16,18},{20,22},{24,26},{28,30},{2,0},{... | collective-permute-start | bytes 73736 | tf_op jit(solution)/shard_map/ppermute | solution.py:485
  17.7 1.2 %collective-permute-start = (bf16[16,128]{1,0:T(8,128)(2,1)S(1)}, bf16[16,128]{1,0:T(8,128)(2,1)S(1)}, u32[]{:S(2)}, u32[]{:S(2)}) collective-permute-start(bf16[16,128]{1,0:T(8,128)(2,1)S(1)} %get-tuple-element.39), channel_id=1, source_target_pairs={{0,1},{1,0},{2,3},{3,2},{4,5},{5,4},{6,7},{7,6},{8,9},{9,8},{10,11... | collective-permute-start | bytes 12296 | tf_op jit(solution)/shard_map/ppermute | solution.py:524
  21.8 10.6 %all-to-all-start.1 = ((bf16[32,7,2,128]{3,2,1,0:T(2,128)(2,1)}), bf16[32,7,2,128]{3,2,1,0:T(2,128)(2,1)S(1)}, u32[]{:S(2)}, u32[]{:S(2)}) async-start(bf16[32,7,2,128]{3,2,1,0:T(2,128)(2,1)} %bitcast.2), calls=%async_computation.1 | async-start | bytes 229376 | tf_op jit(solution)/shard_map/all_to_all | solution.py:491
  32.5 42.4 %collective-permute-start.3 = (bf16[48,256]{1,0:T(8,128)(2,1)S(1)}, bf16[48,256]{1,0:T(8,128)(2,1)S(1)}, u32[]{:S(2)}, u32[]{:S(2)}) collective-permute-start(bf16[48,256]{1,0:T(8,128)(2,1)S(1)} %get-tuple-element.54), channel_id=1, source_target_pairs={{2,4},{6,8},{10,12},{14,16},{18,20},{22,24},{26,28},{4,2},{8,6},{1... | collective-permute-start | bytes 73736 | tf_op jit(solution)/shard_map/ppermute | solution.py:485
  33.2 41.7 %collective-permute-start.4 = (bf16[48,256]{1,0:T(8,128)(2,1)S(1)}, bf16[48,256]{1,0:T(8,128)(2,1)S(1)}, u32[]{:S(2)}, u32[]{:S(2)}) collective-permute-start(bf16[48,256]{1,0:T(8,128)(2,1)S(1)} %get-tuple-element.55), channel_id=1, source_target_pairs={{0,2},{4,6},{8,10},{12,14},{16,18},{20,22},{24,26},{28,30},{2,0},{... | collective-permute-start | bytes 73736 | tf_op jit(solution)/shard_map/ppermute | solution.py:485

commit v28 on v26

--- a/solution.py
+++ b/solution.py
@@ -305,8 +305,7 @@
     hidden = (pre * sigmoid).astype(BF16)
     slope_out[...] = sigmoid * (1.0 + pre * (1.0 - sigmoid))
     hidden_out[...] = hidden
-    hidden = hidden.astype(F32)
-    turned_out[...] = jnp.transpose(hidden).astype(BF16)
+    turned_out[...] = jnp.transpose(hidden)
 
 
 def hidden_faces_kernel(hidden_ref, _parts, high_out, low_out, far_out, near_out, halves_ref, faces_ref):
@@ -392,7 +391,7 @@
     bricks = cotangent_lines(cotangent_ref)
     pad_all(cotangent_pad, bricks, masks_ref, high_pool, low_pool, high_own, low_own, far, near)
     gradient = (convolve(cotangent_pad, band_ref) * slope_ref[...]).astype(BF16)
-    gradient = jnp.transpose(gradient.astype(F32)).astype(BF16)
+    gradient = jnp.transpose(gradient)
     hidden = hidden_ref[...]
     if sums_ref.shape[0] > 2 * GROUPS * CHANNELS:
         rest = sums_ref.shape[0] - 2 * GROUPS * CHANNELS
@@ -450,19 +449,19 @@
     rows_ref[...] = sums_ref[...].astype(F32)
     copies = []
     for which, (block_ref, out) in ((1, (two_ref, two_out)), (0, (one_ref, one_out))):
-        for part, (first, last) in enumerate(((0, 2), (2, 4), (4, GROUPS))):
-            for group in range(first, last):
-                start = (which * GROUPS + group) * CHANNELS
-                four = rows_ref[start : start + CHANNELS]
-                turned = None if which else jnp.transpose(four)
-                for n in range(min(4, 27 - 4 * group)):
-                    if which:
-                        block = pltpu.roll(four, 128 - n * CHANNELS, 1) if n else four
-                        block_ref[4 * group + n] = block[:, :CHANNELS]
-                    else:
-                        block_ref[4 * group + n] = turned[CHANNELS * n : CHANNELS * n + CHANNELS]
-            span = pl.ds(4 * first, min(4 * last, 27) - 4 * first)
-            copies.append(pltpu.make_async_copy(block_ref.at[span], out.at[span], sems.at[which, part]))
+        for group in range(GROUPS):
+            start = (which * GROUPS + group) * CHANNELS
+            four = rows_ref[start : start + CHANNELS]
+            turned = None if which else jnp.transpose(four)
+            count = min(4, 27 - 4 * group)
+            for n in range(count):
+                if which:
+                    block = pltpu.roll(four, 128 - n * CHANNELS, 1) if n else four
+                    block_ref[4 * group + n] = block[:, :CHANNELS]
+                else:
+                    block_ref[4 * group + n] = turned[CHANNELS * n : CHANNELS * n + CHANNELS]
+            span = pl.ds(4 * group, count)
+            copies.append(pltpu.make_async_copy(block_ref.at[span], out.at[span], sems.at[which, group]))
             copies[-1].start()
     for copy in copies:
         copy.wait()
@@ -598,7 +597,7 @@
     grads = shape(27, CHANNELS, CHANNELS, dtype=F32)
     block = pltpu.VMEM(grads.shape, F32)
     scratch = [pltpu.VMEM(packed_rows, F32), block, block]
-    scratch += [pltpu.SemaphoreType.DMA((2, 3)), pltpu.SemaphoreType.DMA]
+    scratch += [pltpu.SemaphoreType.DMA((2, GROUPS)), pltpu.SemaphoreType.DMA]
     grad_one, grad_two, fine = call(
         unpack_kernel, (grads, grads, shape(*fine.shape)), scratch, inputs=2, out=pl.ANY
     )(gathered, fine)

time: 44 us -> 44 us (level)
  no operation moved by 1% of the time
where the time goes in v28:
time: 44 us; the launch traced here: 43.7 us
  starting transfers between devices  20.4 us (46%)
  blocking collectives  10.2 us (23%)
  Pallas kernels  7.45 us (17%)
  waiting for transfers between devices  4.96 us (11%)
  between operations  0.77 us (2%)
    ppermute x4, starting transfers between devices, swapped(): lax.ppermute(value, 'space', pairs + [(target, source) for source, target...  10.3 us
    all_to_all x1, blocking collectives, exchanged(): lax.all_to_all(shares, axes, split_axis=0, concat_axis=0, tiled=True)  10.2 us
    all_to_all x2, starting transfers between devices, exchanged(): lax.all_to_all(shares, axes, split_axis=0, concat_axis=0, tiled=True)  9.89 us
    all_to_all x2, waiting for transfers between devices, exchanged(): lax.all_to_all(shares, axes, split_axis=0, concat_axis=0, tiled=True)  2.81 us
    pallas_call x1, Pallas kernels, body(): call(functools.partial(pick_kernel, split, len(extras)), (shape(*blocks),...  1.87 us
    ppermute x4, waiting for transfers between devices, swapped(): lax.ppermute(value, 'space', pairs + [(target, source) for source, target...  1.71 us
    pallas_call x1, Pallas kernels, body(): call(second_kernel, (shape(*packed_rows), volume), [pool, pool, pad, pltp...  1.11 us
    pallas_call x1, Pallas kernels, body(): call(unpack_kernel, (grads, grads, shape(*fine.shape)), scratch, inputs=2...  1.1 us
  transfers between devices with their start and end apart: 7, of which 4 were waited for; matrix products, arithmetic and copies ran while one was open for 0% of the time, Pallas kernels for 6%

profile of v28, /device:TPU:0, one launch (start us, length us, event | category | flops | bytes accessed | tf_op | source)
XLA Modules:
  0.0 43.7 jit_solution(14908547361017950732)
XLA Ops:
  0.6 1.9 %shard_map.94 = (bf16[384,128]{1,0:T(8,128)(2,1)}, bf16[64,2048]{1,0:T(8,128)(2,1)S(1)}, bf16[27,32,32]{2,1,0:T(8,128)(2,1)S(1)}, bf16[27,32,32]{2,1,0:T(8,128)(2,1)S(1)}, s32[1,2,6]{2,1,0:T(2,128)S(1)}) custom-call(s32[1,32]{1,0:T(1,128)} %ids_hbm.1, bf16[1,64,512]{2,1,0:T(8,128)(2,1)} %latents_hbm.1, bf16[64,2048]{1,0:T(8,128)(2,1)} %refs_0_.1, ...), custom_call_target="tpu_custom_call" | custom-call | tf_op jit(solution)/shard_map/pallas_call | solution.py:514
  2.5 0.0 copy-start
  2.5 7.3 %all-to-all-start = ((bf16[32,6,2,128]{3,2,1,0:T(2,128)(2,1)}), bf16[32,6,2,128]{3,2,1,0:T(2,128)(2,1)S(1)}, u32[]{:S(2)}, u32[]{:S(2)}) async-start(bf16[32,6,2,128]{3,2,1,0:T(2,128)(2,1)} %bitcast), calls=%async_computation | async-start | bytes 196608 | tf_op jit(solution)/shard_map/all_to_all | solution.py:500
  9.8 0.1 shard_map.98
  9.9 0.7 %collective-permute-start.1 = (bf16[48,256]{1,0:T(8,128)(2,1)S(1)}, bf16[48,256]{1,0:T(8,128)(2,1)S(1)}, u32[]{:S(2)}, u32[]{:S(2)}) collective-permute-start(bf16[48,256]{1,0:T(8,128)(2,1)S(1)} %get-tuple-element.47), channel_id=1, source_target_pairs={{2,4},{6,8},{10,12},{14,16},{18,20},{22,24},{26,28},{4,2},{8,6},{1... | collective-permute-start | bytes 73736 | tf_op jit(solution)/shard_map/ppermute | solution.py:494
  10.6 4.5 %collective-permute-start.2 = (bf16[48,256]{1,0:T(8,128)(2,1)S(1)}, bf16[48,256]{1,0:T(8,128)(2,1)S(1)}, u32[]{:S(2)}, u32[]{:S(2)}) collective-permute-start(bf16[48,256]{1,0:T(8,128)(2,1)S(1)} %get-tuple-element.48), channel_id=1, source_target_pairs={{0,2},{4,6},{8,10},{12,14},{16,18},{20,22},{24,26},{28,30},{2,0},{... | collective-permute-start | bytes 73736 | tf_op jit(solution)/shard_map/ppermute | solution.py:494
  15.1 2.5 %all-to-all-done = bf16[32,6,2,128]{3,2,1,0:T(2,128)(2,1)S(1)} async-done(((bf16[32,6,2,128]{3,2,1,0:T(2,128)(2,1)}), bf16[32,6,2,128]{3,2,1,0:T(2,128)(2,1)S(1)}, u32[]{:S(2)}, u32[]{:S(2)}) %all-to-all-start) | async-done | bytes 98336 | tf_op jit(solution)/shard_map/all_to_all | solution.py:500
  17.7 0.2 collective-permute-start
  17.9 0.6 %shard_map.96 = (bf16[9,256,128]{2,1,0:T(8,128)(2,1)S(1)}, bf16[9,256,128]{2,1,0:T(8,128)(2,1)S(1)}, f32[48,128]{1,0:T(8,128)S(1)}, f32[2,256,128]{2,1,0:T(8,128)S(1)}) custom-call(s32[1,2,6]{2,1,0:T(2,128)S(1)} %get-tuple-element.31.links_in, bf16[16,128]{1,0:T(8,128)(2,1)S(1)} %get-tuple-element.33.own_ref, bf16[64,2048]{1,0:T(8,128)(2,1)S(1)} %get-tuple-element.34.up_ref, ...), custom_call_target="tpu_custom_call" | custom-call | flops 1000000000 | bytes 2000000 | tf_op jit(solution)/shard_map/pallas_call | solution.py:549
  18.5 0.4 collective-permute-done.other_ref
  18.9 1.1 %shard_map.97 = (f32[256,128]{1,0:T(8,128)S(1)}, bf16[256,128]{1,0:T(8,128)(2,1)S(1)}, bf16[128,256]{1,0:T(8,128)(2,1)S(1)}, bf16[3,2,10,16,256]{4,3,2,1,0:T(8,128)(2,1)S(1)}) custom-call(s32[1,2,6]{2,1,0:T(2,128)S(1)} %get-tuple-element.31.links_in, bf16[16,128]{1,0:T(8,128)(2,1)S(1)} %collective-permute-done.other_ref, ...), custom_call_target="tpu_custom_call" | custom-call | tf_op jit(solution)/shard_map/pallas_call | solution.py:557
  20.0 0.0 collective-permute-done.1.far
  20.0 1.1 %shard_map.99 = (bf16[448,128]{1,0:T(8,128)(2,1)S(1)}, bf16[256,128]{1,0:T(8,128)(2,1)S(1)}) custom-call(f32[48,128]{1,0:T(8,128)S(1)} %get-tuple-element.37.masks_ref, bf16[1,2,8,8,256]{4,3,2,1,0:T(8,128)(2,1)S(1)} %copy-done, bf16[9,256,128]{2,1,0:T(8,128)(2,1)S(1)} %get-tuple-element.38.band_ref, f32[256,128]{1,0:T(8,128)S(1)} %get-tuple-element.42.slope_ref, ...), custom_call_target="tpu_custom_call" | custom-call | tf_op jit(solution)/shard_map/pallas_call | solution.py:568
  21.1 10.2 %all_to_all.15 = bf16[32,7,2,128]{3,2,1,0:T(2,128)(2,1)S(1)} all-to-all(bf16[32,7,2,128]{3,2,1,0:T(2,128)(2,1)S(1)} %bitcast.10), channel_id=1, replica_groups=mesh['space'=16,'dp'=2] {'space','dp'}, dimensions={0} | all-to-all | bytes 229376 | tf_op jit(solution)/shard_map/all_to_all | solution.py:500
  31.3 0.7 %shard_map.100 = bf16[448,128]{1,0:T(8,128)(2,1)} custom-call(bf16[448,128]{1,0:T(8,128)(2,1)S(1)} %bitcast.6), custom_call_target="tpu_custom_call" | custom-call | tf_op jit(solution)/shard_map/pallas_call | solution.py:586
  32.0 2.6 %all-to-all-start.2 = ((bf16[32,7,2,128]{3,2,1,0:T(2,128)(2,1)}), bf16[32,7,2,128]{3,2,1,0:T(2,128)(2,1)S(1)}, u32[]{:S(2)}, u32[]{:S(2)}) async-start(bf16[32,7,2,128]{3,2,1,0:T(2,128)(2,1)} %bitcast.4), calls=%async_computation.2 | async-start | bytes 229376 | tf_op jit(solution)/shard_map/all_to_all | solution.py:500
  34.6 0.1 shard_map.102
  34.7 0.7 %collective-permute-start.3 = (bf16[48,256]{1,0:T(8,128)(2,1)S(1)}, bf16[48,256]{1,0:T(8,128)(2,1)S(1)}, u32[]{:S(2)}, u32[]{:S(2)}) collective-permute-start(bf16[48,256]{1,0:T(8,128)(2,1)S(1)} %get-tuple-element.54), channel_id=1, source_target_pairs={{2,4},{6,8},{10,12},{14,16},{18,20},{22,24},{26,28},{4,2},{8,6},{1... | collective-permute-start | bytes 73736 | tf_op jit(solution)/shard_map/ppermute | solution.py:494
  35.3 4.4 %collective-permute-start.4 = (bf16[48,256]{1,0:T(8,128)(2,1)S(1)}, bf16[48,256]{1,0:T(8,128)(2,1)S(1)}, u32[]{:S(2)}, u32[]{:S(2)}) collective-permute-start(bf16[48,256]{1,0:T(8,128)(2,1)S(1)} %get-tuple-element.55), channel_id=1, source_target_pairs={{0,2},{4,6},{8,10},{12,14},{16,18},{20,22},{24,26},{28,30},{2,0},{... | collective-permute-start | bytes 73736 | tf_op jit(solution)/shard_map/ppermute | solution.py:494
  39.8 0.3 shard_map.101.band_ref
  40.1 1.7 %collective-permute-done.4.near = bf16[48,256]{1,0:T(8,128)(2,1)S(1)} collective-permute-done((bf16[48,256]{1,0:T(8,128)(2,1)S(1)}, bf16[48,256]{1,0:T(8,128)(2,1)S(1)}, u32[]{:S(2)}, u32[]{:S(2)}) %collective-permute-start.4) | collective-permute-done | bytes 24608 | tf_op jit(solution)/shard_map/ppermute | solution.py:494
  41.8 0.5 %shard_map.103.fine_ref = bf16[1,2,8,8,256]{4,3,2,1,0:T(8,128)(2,1)S(1)} custom-call(f32[48,128]{1,0:T(8,128)S(1)} %get-tuple-element.37.masks_ref, bf16[9,256,128]{2,1,0:T(8,128)(2,1)S(1)} %shard_map.101.band_ref, bf16[256,128]{1,0:T(8,128)(2,1)S(1)} %get-tuple-element.50.lifted_ref, bf16[256,128]{1,0:T(8,128)(2,1)S(1)} %get-tuple-element.51.hidden_ref, ...), custom_call_target="tpu_custom_call" | custom-call | flops 1000000000 | bytes 2000000 | tf_op jit(solution)/shard_map/pallas_call | solution.py:581
  42.3 0.3 all-to-all-done.2
  42.6 1.1 %shard_map.104 = (f32[27,32,32]{2,1,0:T(8,128)}, f32[27,32,32]{2,1,0:T(8,128)}, bf16[1,2,8,8,256]{4,3,2,1,0:T(8,128)(2,1)}) custom-call(bf16[448,128]{1,0:T(8,128)(2,1)S(1)} %bitcast.8, bf16[1,2,8,8,256]{4,3,2,1,0:T(8,128)(2,1)S(1)} %shard_map.103.fine_ref), custom_call_target="tpu_custom_call" | custom-call | tf_op jit(solution)/shard_map/pallas_call | solution.py:601
  (4 shorter events, 0.0 us)
Async XLA Ops:
  2.5 7.3 %copy-start = (bf16[1,2,8,8,256]{4,3,2,1,0:T(8,128)(2,1)S(1)}, bf16[1,2,8,8,256]{4,3,2,1,0:T(8,128)(2,1)}, u32[]{:S(2)}) copy-start(bf16[1,2,8,8,256]{4,3,2,1,0:T(8,128)(2,1)} %cotangent_ref.3) | copy-start | bytes 196612
  2.5 15.1 %all-to-all-start = ((bf16[32,6,2,128]{3,2,1,0:T(2,128)(2,1)}), bf16[32,6,2,128]{3,2,1,0:T(2,128)(2,1)S(1)}, u32[]{:S(2)}, u32[]{:S(2)}) async-start(bf16[32,6,2,128]{3,2,1,0:T(2,128)(2,1)} %bitcast), calls=%async_computation | async-start | bytes 196608 | tf_op jit(solution)/shard_map/all_to_all | solution.py:500
  9.9 10.0 %collective-permute-start.1 = (bf16[48,256]{1,0:T(8,128)(2,1)S(1)}, bf16[48,256]{1,0:T(8,128)(2,1)S(1)}, u32[]{:S(2)}, u32[]{:S(2)}) collective-permute-start(bf16[48,256]{1,0:T(8,128)(2,1)S(1)} %get-tuple-element.47), channel_id=1, source_target_pairs={{2,4},{6,8},{10,12},{14,16},{18,20},{22,24},{26,28},{4,2},{8,6},{1... | collective-permute-start | bytes 73736 | tf_op jit(solution)/shard_map/ppermute | solution.py:494
  10.6 9.4 %collective-permute-start.2 = (bf16[48,256]{1,0:T(8,128)(2,1)S(1)}, bf16[48,256]{1,0:T(8,128)(2,1)S(1)}, u32[]{:S(2)}, u32[]{:S(2)}) collective-permute-start(bf16[48,256]{1,0:T(8,128)(2,1)S(1)} %get-tuple-element.48), channel_id=1, source_target_pairs={{0,2},{4,6},{8,10},{12,14},{16,18},{20,22},{24,26},{28,30},{2,0},{... | collective-permute-start | bytes 73736 | tf_op jit(solution)/shard_map/ppermute | solution.py:494
  17.7 1.2 %collective-permute-start = (bf16[16,128]{1,0:T(8,128)(2,1)S(1)}, bf16[16,128]{1,0:T(8,128)(2,1)S(1)}, u32[]{:S(2)}, u32[]{:S(2)}) collective-permute-start(bf16[16,128]{1,0:T(8,128)(2,1)S(1)} %get-tuple-element.39), channel_id=1, source_target_pairs={{0,1},{1,0},{2,3},{3,2},{4,5},{5,4},{6,7},{7,6},{8,9},{9,8},{10,11... | collective-permute-start | bytes 12296 | tf_op jit(solution)/shard_map/ppermute | solution.py:533
  32.0 10.6 %all-to-all-start.2 = ((bf16[32,7,2,128]{3,2,1,0:T(2,128)(2,1)}), bf16[32,7,2,128]{3,2,1,0:T(2,128)(2,1)S(1)}, u32[]{:S(2)}, u32[]{:S(2)}) async-start(bf16[32,7,2,128]{3,2,1,0:T(2,128)(2,1)} %bitcast.4), calls=%async_computation.2 | async-start | bytes 229376 | tf_op jit(solution)/shard_map/all_to_all | solution.py:500
  34.7 5.4 %collective-permute-start.3 = (bf16[48,256]{1,0:T(8,128)(2,1)S(1)}, bf16[48,256]{1,0:T(8,128)(2,1)S(1)}, u32[]{:S(2)}, u32[]{:S(2)}) collective-permute-start(bf16[48,256]{1,0:T(8,128)(2,1)S(1)} %get-tuple-element.54), channel_id=1, source_target_pairs={{2,4},{6,8},{10,12},{14,16},{18,20},{22,24},{26,28},{4,2},{8,6},{1... | collective-permute-start | bytes 73736 | tf_op jit(solution)/shard_map/ppermute | solution.py:494
  35.3 6.5 %collective-permute-start.4 = (bf16[48,256]{1,0:T(8,128)(2,1)S(1)}, bf16[48,256]{1,0:T(8,128)(2,1)S(1)}, u32[]{:S(2)}, u32[]{:S(2)}) collective-permute-start(bf16[48,256]{1,0:T(8,128)(2,1)S(1)} %get-tuple-element.55), channel_id=1, source_target_pairs={{0,2},{4,6},{8,10},{12,14},{16,18},{20,22},{24,26},{28,30},{2,0},{... | collective-permute-start | bytes 73736 | tf_op jit(solution)/shard_map/ppermute | solution.py:494

commit v29 on v26

--- a/solution.py
+++ b/solution.py
@@ -133,7 +133,7 @@
 
 def lift(half_ref, up_ref, rows_ref, volumes_ref, half):
     tiles = half_ref.shape[0] // 8
-    rows_ref[...] = half_ref[...].astype(F32)
+    rows_ref[: 8 * tiles] = half_ref[...].astype(F32)
     cells = []
     for tile in range(tiles):
         rows = rows_ref[pl.ds(tile, 8, stride=tiles), :]
@@ -305,8 +305,7 @@
     hidden = (pre * sigmoid).astype(BF16)
     slope_out[...] = sigmoid * (1.0 + pre * (1.0 - sigmoid))
     hidden_out[...] = hidden
-    hidden = hidden.astype(F32)
-    turned_out[...] = jnp.transpose(hidden).astype(BF16)
+    turned_out[...] = jnp.transpose(hidden)
 
 
 def hidden_faces_kernel(hidden_ref, _parts, high_out, low_out, far_out, near_out, halves_ref, faces_ref):
@@ -392,7 +391,7 @@
     bricks = cotangent_lines(cotangent_ref)
     pad_all(cotangent_pad, bricks, masks_ref, high_pool, low_pool, high_own, low_own, far, near)
     gradient = (convolve(cotangent_pad, band_ref) * slope_ref[...]).astype(BF16)
-    gradient = jnp.transpose(gradient.astype(F32)).astype(BF16)
+    gradient = jnp.transpose(gradient)
     hidden = hidden_ref[...]
     if sums_ref.shape[0] > 2 * GROUPS * CHANNELS:
         rest = sums_ref.shape[0] - 2 * GROUPS * CHANNELS
@@ -534,7 +533,7 @@
         other = lax.ppermute(other, "dp", [(0, 1), (1, 0)])
     cost = pl.CostEstimate(flops=10**9, bytes_accessed=2 * 10**6, transcendentals=0)
     face = shape(BRICKS * FACE, LINE)
-    halves = pltpu.VMEM((2, LINES, HALF), F32)
+    halves = pltpu.VMEM((2, LINES + 8, HALF), F32)
     faces = pltpu.VMEM((BRICKS * FACE, LINE), F32)
     pool = pltpu.VMEM((2 * BRICKS * FACE, LINE), F32)
     volume = shape(ROWS, HALF)
@@ -546,7 +545,7 @@
     near = swapped(near, 0)
     masks = shape(BRICKS * 6 * 2 * BRICKS, 128, dtype=F32)
     lifted_half = shape(2, 4 * CUBE, 128, dtype=F32)
-    window_rows = pltpu.VMEM((8 * tiles, 128), F32)
+    window_rows = pltpu.VMEM((8 * tiles + 8, 128), F32)
     band_one, band_back, masks, lifted_half = call(
         early_kernel,
         (shape(*BAND), shape(*BAND), masks, lifted_half),
@@ -560,7 +559,7 @@
         (
             shape(ROWS, HALF, dtype=F32), volume, shape(HALF, ROWS), shape(*pad_shape),
         ),
-        [pltpu.VMEM((2, 8 * CUBE, 128), F32), window_rows, *links],
+        [pltpu.VMEM((2, 9 * CUBE, 128), F32), window_rows, *links],
         hbm=(0,),
         inputs=5,
     )(face_links, other, up_weight, band_one, lifted_half)

time: 44 us -> 44 us (level)
  no operation moved by 1% of the time
where the time goes in v29:
time: 44 us; the launch traced here: 43.7 us
  starting transfers between devices  20.4 us (46%)
  blocking collectives  10.2 us (23%)
  Pallas kernels  7.42 us (17%)
  waiting for transfers between devices  4.95 us (11%)
  between operations  0.77 us (2%)
    ppermute x4, starting transfers between devices, swapped(): lax.ppermute(value, 'space', pairs + [(target, source) for source, target...  10.3 us
    all_to_all x1, blocking collectives, exchanged(): lax.all_to_all(shares, axes, split_axis=0, concat_axis=0, tiled=True)  10.2 us
    all_to_all x2, starting transfers between devices, exchanged(): lax.all_to_all(shares, axes, split_axis=0, concat_axis=0, tiled=True)  9.89 us
    all_to_all x2, waiting for transfers between devices, exchanged(): lax.all_to_all(shares, axes, split_axis=0, concat_axis=0, tiled=True)  2.81 us
    pallas_call x1, Pallas kernels, body(): call(functools.partial(pick_kernel, split, len(extras)), (shape(*blocks),...  1.87 us
    ppermute x4, waiting for transfers between devices, swapped(): lax.ppermute(value, 'space', pairs + [(target, source) for source, target...  1.71 us
    pallas_call x1, Pallas kernels, body(): call(second_kernel, (shape(*packed_rows), volume), [pool, pool, pad, pltp...  1.11 us
    pallas_call x1, Pallas kernels, body(): call(unpack_kernel, (grads, grads, shape(*fine.shape)), scratch, inputs=2...  1.07 us
  transfers between devices with their start and end apart: 7, of which 4 were waited for; matrix products, arithmetic and copies ran while one was open for 0% of the time, Pallas kernels for 6%

profile of v29, /device:TPU:0, one launch (start us, length us, event | category | flops | bytes accessed | tf_op | source)
XLA Modules:
  0.0 43.7 jit_solution(1890689988695937586)
XLA Ops:
  0.6 1.9 %shard_map.94 = (bf16[384,128]{1,0:T(8,128)(2,1)}, bf16[64,2048]{1,0:T(8,128)(2,1)S(1)}, bf16[27,32,32]{2,1,0:T(8,128)(2,1)S(1)}, bf16[27,32,32]{2,1,0:T(8,128)(2,1)S(1)}, s32[1,2,6]{2,1,0:T(2,128)S(1)}) custom-call(s32[1,32]{1,0:T(1,128)} %ids_hbm.1, bf16[1,64,512]{2,1,0:T(8,128)(2,1)} %latents_hbm.1, bf16[64,2048]{1,0:T(8,128)(2,1)} %refs_0_.1, ...), custom_call_target="tpu_custom_call" | custom-call | tf_op jit(solution)/shard_map/pallas_call | solution.py:514
  2.5 0.0 copy-start
  2.5 7.3 %all-to-all-start = ((bf16[32,6,2,128]{3,2,1,0:T(2,128)(2,1)}), bf16[32,6,2,128]{3,2,1,0:T(2,128)(2,1)S(1)}, u32[]{:S(2)}, u32[]{:S(2)}) async-start(bf16[32,6,2,128]{3,2,1,0:T(2,128)(2,1)} %bitcast), calls=%async_computation | async-start | bytes 196608 | tf_op jit(solution)/shard_map/all_to_all | solution.py:500
  9.8 0.1 shard_map.98
  9.9 0.7 %collective-permute-start.1 = (bf16[48,256]{1,0:T(8,128)(2,1)S(1)}, bf16[48,256]{1,0:T(8,128)(2,1)S(1)}, u32[]{:S(2)}, u32[]{:S(2)}) collective-permute-start(bf16[48,256]{1,0:T(8,128)(2,1)S(1)} %get-tuple-element.47), channel_id=1, source_target_pairs={{2,4},{6,8},{10,12},{14,16},{18,20},{22,24},{26,28},{4,2},{8,6},{1... | collective-permute-start | bytes 73736 | tf_op jit(solution)/shard_map/ppermute | solution.py:494
  10.6 4.5 %collective-permute-start.2 = (bf16[48,256]{1,0:T(8,128)(2,1)S(1)}, bf16[48,256]{1,0:T(8,128)(2,1)S(1)}, u32[]{:S(2)}, u32[]{:S(2)}) collective-permute-start(bf16[48,256]{1,0:T(8,128)(2,1)S(1)} %get-tuple-element.48), channel_id=1, source_target_pairs={{0,2},{4,6},{8,10},{12,14},{16,18},{20,22},{24,26},{28,30},{2,0},{... | collective-permute-start | bytes 73736 | tf_op jit(solution)/shard_map/ppermute | solution.py:494
  15.1 2.5 %all-to-all-done = bf16[32,6,2,128]{3,2,1,0:T(2,128)(2,1)S(1)} async-done(((bf16[32,6,2,128]{3,2,1,0:T(2,128)(2,1)}), bf16[32,6,2,128]{3,2,1,0:T(2,128)(2,1)S(1)}, u32[]{:S(2)}, u32[]{:S(2)}) %all-to-all-start) | async-done | bytes 98336 | tf_op jit(solution)/shard_map/all_to_all | solution.py:500
  17.7 0.2 collective-permute-start
  17.9 0.6 %shard_map.96 = (bf16[9,256,128]{2,1,0:T(8,128)(2,1)S(1)}, bf16[9,256,128]{2,1,0:T(8,128)(2,1)S(1)}, f32[48,128]{1,0:T(8,128)S(1)}, f32[2,256,128]{2,1,0:T(8,128)S(1)}) custom-call(s32[1,2,6]{2,1,0:T(2,128)S(1)} %get-tuple-element.31.links_in, bf16[16,128]{1,0:T(8,128)(2,1)S(1)} %get-tuple-element.33.own_ref, bf16[64,2048]{1,0:T(8,128)(2,1)S(1)} %get-tuple-element.34.up_ref, ...), custom_call_target="tpu_custom_call" | custom-call | flops 1000000000 | bytes 2000000 | tf_op jit(solution)/shard_map/pallas_call | solution.py:549
  18.5 0.4 collective-permute-done.other_ref
  18.9 1.1 %shard_map.97 = (f32[256,128]{1,0:T(8,128)S(1)}, bf16[256,128]{1,0:T(8,128)(2,1)S(1)}, bf16[128,256]{1,0:T(8,128)(2,1)S(1)}, bf16[3,2,10,16,256]{4,3,2,1,0:T(8,128)(2,1)S(1)}) custom-call(s32[1,2,6]{2,1,0:T(2,128)S(1)} %get-tuple-element.31.links_in, bf16[16,128]{1,0:T(8,128)(2,1)S(1)} %collective-permute-done.other_ref, ...), custom_call_target="tpu_custom_call" | custom-call | tf_op jit(solution)/shard_map/pallas_call | solution.py:557
  20.0 0.0 collective-permute-done.1.far
  20.0 1.1 %shard_map.99 = (bf16[448,128]{1,0:T(8,128)(2,1)S(1)}, bf16[256,128]{1,0:T(8,128)(2,1)S(1)}) custom-call(f32[48,128]{1,0:T(8,128)S(1)} %get-tuple-element.37.masks_ref, bf16[1,2,8,8,256]{4,3,2,1,0:T(8,128)(2,1)S(1)} %copy-done, bf16[9,256,128]{2,1,0:T(8,128)(2,1)S(1)} %get-tuple-element.38.band_ref, f32[256,128]{1,0:T(8,128)S(1)} %get-tuple-element.42.slope_ref, ...), custom_call_target="tpu_custom_call" | custom-call | tf_op jit(solution)/shard_map/pallas_call | solution.py:568
  21.1 10.2 %all_to_all.15 = bf16[32,7,2,128]{3,2,1,0:T(2,128)(2,1)S(1)} all-to-all(bf16[32,7,2,128]{3,2,1,0:T(2,128)(2,1)S(1)} %bitcast.10), channel_id=1, replica_groups=mesh['space'=16,'dp'=2] {'space','dp'}, dimensions={0} | all-to-all | bytes 229376 | tf_op jit(solution)/shard_map/all_to_all | solution.py:500
  31.3 0.7 %shard_map.100 = bf16[448,128]{1,0:T(8,128)(2,1)} custom-call(bf16[448,128]{1,0:T(8,128)(2,1)S(1)} %bitcast.6), custom_call_target="tpu_custom_call" | custom-call | tf_op jit(solution)/shard_map/pallas_call | solution.py:586
  32.0 2.6 %all-to-all-start.2 = ((bf16[32,7,2,128]{3,2,1,0:T(2,128)(2,1)}), bf16[32,7,2,128]{3,2,1,0:T(2,128)(2,1)S(1)}, u32[]{:S(2)}, u32[]{:S(2)}) async-start(bf16[32,7,2,128]{3,2,1,0:T(2,128)(2,1)} %bitcast.4), calls=%async_computation.2 | async-start | bytes 229376 | tf_op jit(solution)/shard_map/all_to_all | solution.py:500
  34.6 0.1 shard_map.102
  34.7 0.7 %collective-permute-start.3 = (bf16[48,256]{1,0:T(8,128)(2,1)S(1)}, bf16[48,256]{1,0:T(8,128)(2,1)S(1)}, u32[]{:S(2)}, u32[]{:S(2)}) collective-permute-start(bf16[48,256]{1,0:T(8,128)(2,1)S(1)} %get-tuple-element.54), channel_id=1, source_target_pairs={{2,4},{6,8},{10,12},{14,16},{18,20},{22,24},{26,28},{4,2},{8,6},{1... | collective-permute-start | bytes 73736 | tf_op jit(solution)/shard_map/ppermute | solution.py:494
  35.3 4.4 %collective-permute-start.4 = (bf16[48,256]{1,0:T(8,128)(2,1)S(1)}, bf16[48,256]{1,0:T(8,128)(2,1)S(1)}, u32[]{:S(2)}, u32[]{:S(2)}) collective-permute-start(bf16[48,256]{1,0:T(8,128)(2,1)S(1)} %get-tuple-element.55), channel_id=1, source_target_pairs={{0,2},{4,6},{8,10},{12,14},{16,18},{20,22},{24,26},{28,30},{2,0},{... | collective-permute-start | bytes 73736 | tf_op jit(solution)/shard_map/ppermute | solution.py:494
  39.8 0.3 shard_map.101.band_ref
  40.1 1.7 %collective-permute-done.4.near = bf16[48,256]{1,0:T(8,128)(2,1)S(1)} collective-permute-done((bf16[48,256]{1,0:T(8,128)(2,1)S(1)}, bf16[48,256]{1,0:T(8,128)(2,1)S(1)}, u32[]{:S(2)}, u32[]{:S(2)}) %collective-permute-start.4) | collective-permute-done | bytes 24608 | tf_op jit(solution)/shard_map/ppermute | solution.py:494
  41.8 0.5 %shard_map.103.fine_ref = bf16[1,2,8,8,256]{4,3,2,1,0:T(8,128)(2,1)S(1)} custom-call(f32[48,128]{1,0:T(8,128)S(1)} %get-tuple-element.37.masks_ref, bf16[9,256,128]{2,1,0:T(8,128)(2,1)S(1)} %shard_map.101.band_ref, bf16[256,128]{1,0:T(8,128)(2,1)S(1)} %get-tuple-element.50.lifted_ref, bf16[256,128]{1,0:T(8,128)(2,1)S(1)} %get-tuple-element.51.hidden_ref, ...), custom_call_target="tpu_custom_call" | custom-call | flops 1000000000 | bytes 2000000 | tf_op jit(solution)/shard_map/pallas_call | solution.py:581
  42.3 0.3 all-to-all-done.2
  42.6 1.1 %shard_map.104 = (f32[27,32,32]{2,1,0:T(8,128)}, f32[27,32,32]{2,1,0:T(8,128)}, bf16[1,2,8,8,256]{4,3,2,1,0:T(8,128)(2,1)}) custom-call(bf16[448,128]{1,0:T(8,128)(2,1)S(1)} %bitcast.8, bf16[1,2,8,8,256]{4,3,2,1,0:T(8,128)(2,1)S(1)} %shard_map.103.fine_ref), custom_call_target="tpu_custom_call" | custom-call | tf_op jit(solution)/shard_map/pallas_call | solution.py:601
  (4 shorter events, 0.0 us)
Async XLA Ops:
  2.5 7.3 %copy-start = (bf16[1,2,8,8,256]{4,3,2,1,0:T(8,128)(2,1)S(1)}, bf16[1,2,8,8,256]{4,3,2,1,0:T(8,128)(2,1)}, u32[]{:S(2)}) copy-start(bf16[1,2,8,8,256]{4,3,2,1,0:T(8,128)(2,1)} %cotangent_ref.3) | copy-start | bytes 196612
  2.5 15.1 %all-to-all-start = ((bf16[32,6,2,128]{3,2,1,0:T(2,128)(2,1)}), bf16[32,6,2,128]{3,2,1,0:T(2,128)(2,1)S(1)}, u32[]{:S(2)}, u32[]{:S(2)}) async-start(bf16[32,6,2,128]{3,2,1,0:T(2,128)(2,1)} %bitcast), calls=%async_computation | async-start | bytes 196608 | tf_op jit(solution)/shard_map/all_to_all | solution.py:500
  9.9 10.0 %collective-permute-start.1 = (bf16[48,256]{1,0:T(8,128)(2,1)S(1)}, bf16[48,256]{1,0:T(8,128)(2,1)S(1)}, u32[]{:S(2)}, u32[]{:S(2)}) collective-permute-start(bf16[48,256]{1,0:T(8,128)(2,1)S(1)} %get-tuple-element.47), channel_id=1, source_target_pairs={{2,4},{6,8},{10,12},{14,16},{18,20},{22,24},{26,28},{4,2},{8,6},{1... | collective-permute-start | bytes 73736 | tf_op jit(solution)/shard_map/ppermute | solution.py:494
  10.6 9.4 %collective-permute-start.2 = (bf16[48,256]{1,0:T(8,128)(2,1)S(1)}, bf16[48,256]{1,0:T(8,128)(2,1)S(1)}, u32[]{:S(2)}, u32[]{:S(2)}) collective-permute-start(bf16[48,256]{1,0:T(8,128)(2,1)S(1)} %get-tuple-element.48), channel_id=1, source_target_pairs={{0,2},{4,6},{8,10},{12,14},{16,18},{20,22},{24,26},{28,30},{2,0},{... | collective-permute-start | bytes 73736 | tf_op jit(solution)/shard_map/ppermute | solution.py:494
  17.7 1.2 %collective-permute-start = (bf16[16,128]{1,0:T(8,128)(2,1)S(1)}, bf16[16,128]{1,0:T(8,128)(2,1)S(1)}, u32[]{:S(2)}, u32[]{:S(2)}) collective-permute-start(bf16[16,128]{1,0:T(8,128)(2,1)S(1)} %get-tuple-element.39), channel_id=1, source_target_pairs={{0,1},{1,0},{2,3},{3,2},{4,5},{5,4},{6,7},{7,6},{8,9},{9,8},{10,11... | collective-permute-start | bytes 12296 | tf_op jit(solution)/shard_map/ppermute | solution.py:533
  32.0 10.6 %all-to-all-start.2 = ((bf16[32,7,2,128]{3,2,1,0:T(2,128)(2,1)}), bf16[32,7,2,128]{3,2,1,0:T(2,128)(2,1)S(1)}, u32[]{:S(2)}, u32[]{:S(2)}) async-start(bf16[32,7,2,128]{3,2,1,0:T(2,128)(2,1)} %bitcast.4), calls=%async_computation.2 | async-start | bytes 229376 | tf_op jit(solution)/shard_map/all_to_all | solution.py:500
  34.7 5.4 %collective-permute-start.3 = (bf16[48,256]{1,0:T(8,128)(2,1)S(1)}, bf16[48,256]{1,0:T(8,128)(2,1)S(1)}, u32[]{:S(2)}, u32[]{:S(2)}) collective-permute-start(bf16[48,256]{1,0:T(8,128)(2,1)S(1)} %get-tuple-element.54), channel_id=1, source_target_pairs={{2,4},{6,8},{10,12},{14,16},{18,20},{22,24},{26,28},{4,2},{8,6},{1... | collective-permute-start | bytes 73736 | tf_op jit(solution)/shard_map/ppermute | solution.py:494
  35.3 6.5 %collective-permute-start.4 = (bf16[48,256]{1,0:T(8,128)(2,1)S(1)}, bf16[48,256]{1,0:T(8,128)(2,1)S(1)}, u32[]{:S(2)}, u32[]{:S(2)}) collective-permute-start(bf16[48,256]{1,0:T(8,128)(2,1)S(1)} %get-tuple-element.55), channel_id=1, source_target_pairs={{0,2},{4,6},{8,10},{12,14},{16,18},{20,22},{24,26},{28,30},{2,0},{... | collective-permute-start | bytes 73736 | tf_op jit(solution)/shard_map/ppermute | solution.py:494

commit v30 on v29

--- a/solution.py
+++ b/solution.py
@@ -510,8 +510,8 @@
     tiles = width // 256
     count = 3 * BRICKS * tiles
     blocks = (2 * devices * count, 128)
-    extras = (up_weight, conv_one, conv_two, face_links)
-    packed, up_weight, conv_one, conv_two, face_links = call(
+    extras = (conv_one, conv_two, face_links)
+    packed, conv_one, conv_two, face_links = call(
         functools.partial(pick_kernel, split, len(extras)),
         (shape(*blocks), *[shape(*extra.shape, dtype=extra.dtype) for extra in extras]),
         [

time: 44 us -> 43.9 us (level)
  no operation moved by 1% of the time
where the time goes in v30:
time: 43.9 us; the launch traced here: 43.6 us
  starting transfers between devices  20.4 us (46%)
  blocking collectives  10.1 us (23%)
  Pallas kernels  7.38 us (17%)
  waiting for transfers between devices  4.94 us (11%)
  between operations  0.77 us (2%)
    ppermute x4, starting transfers between devices, swapped(): lax.ppermute(value, 'space', pairs + [(target, source) for source, target...  10.3 us
    all_to_all x1, blocking collectives, exchanged(): lax.all_to_all(shares, axes, split_axis=0, concat_axis=0, tiled=True)  10.1 us
    all_to_all x2, starting transfers between devices, exchanged(): lax.all_to_all(shares, axes, split_axis=0, concat_axis=0, tiled=True)  9.89 us
    all_to_all x2, waiting for transfers between devices, exchanged(): lax.all_to_all(shares, axes, split_axis=0, concat_axis=0, tiled=True)  2.81 us
    pallas_call x1, Pallas kernels, body(): call(functools.partial(pick_kernel, split, len(extras)), (shape(*blocks),...  1.81 us
    ppermute x4, waiting for transfers between devices, swapped(): lax.ppermute(value, 'space', pairs + [(target, source) for source, target...  1.71 us
    pallas_call x1, Pallas kernels, body(): call(second_kernel, (shape(*packed_rows), volume), [pool, pool, pad, pltp...  1.13 us
    pallas_call x1, Pallas kernels, body(): call(unpack_kernel, (grads, grads, shape(*fine.shape)), scratch, inputs=2...  1.07 us
  transfers between devices with their start and end apart: 7, of which 4 were waited for; matrix products, arithmetic and copies ran while one was open for 0% of the time, Pallas kernels for 6%

profile of v30, /device:TPU:0, one launch (start us, length us, event | category | flops | bytes accessed | tf_op | source)
XLA Modules:
  0.0 43.6 jit_solution(11070652735891630680)
XLA Ops:
  0.6 1.8 %shard_map.94 = (bf16[384,128]{1,0:T(8,128)(2,1)}, bf16[27,32,32]{2,1,0:T(8,128)(2,1)S(1)}, bf16[27,32,32]{2,1,0:T(8,128)(2,1)S(1)}, s32[1,2,6]{2,1,0:T(2,128)S(1)}) custom-call(s32[1,32]{1,0:T(1,128)} %ids_hbm.1, bf16[1,64,512]{2,1,0:T(8,128)(2,1)} %latents_hbm.1, bf16[27,32,32]{2,1,0:T(8,128)(2,1)} %refs_0_.1, bf16[27,32,32]{2,1,0:T(8,128)(2,1)} %refs_1_.1, ...), custom_call_target="tpu_custom_call" | custom-call | tf_op jit(solution)/shard_map/pallas_call | solution.py:514
  2.5 0.0 copy-start
  2.5 7.3 %all-to-all-start = ((bf16[32,6,2,128]{3,2,1,0:T(2,128)(2,1)}), bf16[32,6,2,128]{3,2,1,0:T(2,128)(2,1)S(1)}, u32[]{:S(2)}, u32[]{:S(2)}) async-start(bf16[32,6,2,128]{3,2,1,0:T(2,128)(2,1)} %bitcast), calls=%async_computation | async-start | bytes 196608 | tf_op jit(solution)/shard_map/all_to_all | solution.py:500
  9.8 0.1 shard_map.98
  9.9 0.7 %collective-permute-start.1 = (bf16[48,256]{1,0:T(8,128)(2,1)S(1)}, bf16[48,256]{1,0:T(8,128)(2,1)S(1)}, u32[]{:S(2)}, u32[]{:S(2)}) collective-permute-start(bf16[48,256]{1,0:T(8,128)(2,1)S(1)} %get-tuple-element.45), channel_id=1, source_target_pairs={{2,4},{6,8},{10,12},{14,16},{18,20},{22,24},{26,28},{4,2},{8,6},{1... | collective-permute-start | bytes 73736 | tf_op jit(solution)/shard_map/ppermute | solution.py:494
  10.6 4.5 %collective-permute-start.2 = (bf16[48,256]{1,0:T(8,128)(2,1)S(1)}, bf16[48,256]{1,0:T(8,128)(2,1)S(1)}, u32[]{:S(2)}, u32[]{:S(2)}) collective-permute-start(bf16[48,256]{1,0:T(8,128)(2,1)S(1)} %get-tuple-element.46), channel_id=1, source_target_pairs={{0,2},{4,6},{8,10},{12,14},{16,18},{20,22},{24,26},{28,30},{2,0},{... | collective-permute-start | bytes 73736 | tf_op jit(solution)/shard_map/ppermute | solution.py:494
  15.1 2.5 %all-to-all-done = bf16[32,6,2,128]{3,2,1,0:T(2,128)(2,1)S(1)} async-done(((bf16[32,6,2,128]{3,2,1,0:T(2,128)(2,1)}), bf16[32,6,2,128]{3,2,1,0:T(2,128)(2,1)S(1)}, u32[]{:S(2)}, u32[]{:S(2)}) %all-to-all-start) | async-done | bytes 98336 | tf_op jit(solution)/shard_map/all_to_all | solution.py:500
  17.6 0.2 collective-permute-start
  17.8 0.6 %shard_map.96 = (bf16[9,256,128]{2,1,0:T(8,128)(2,1)S(1)}, bf16[9,256,128]{2,1,0:T(8,128)(2,1)S(1)}, f32[48,128]{1,0:T(8,128)S(1)}, f32[2,256,128]{2,1,0:T(8,128)S(1)}) custom-call(s32[1,2,6]{2,1,0:T(2,128)S(1)} %get-tuple-element.30.links_in, bf16[16,128]{1,0:T(8,128)(2,1)S(1)} %get-tuple-element.32.own_ref, bf16[64,2048]{1,0:T(8,128)(2,1)S(1)} %copy-done, ...), custom_call_target="tpu_custom_call" | custom-call | flops 1000000000 | bytes 2000000 | tf_op jit(solution)/shard_map/pallas_call | solution.py:549
  18.4 0.4 collective-permute-done.other_ref
  18.9 1.1 %shard_map.97 = (f32[256,128]{1,0:T(8,128)S(1)}, bf16[256,128]{1,0:T(8,128)(2,1)S(1)}, bf16[128,256]{1,0:T(8,128)(2,1)S(1)}, bf16[3,2,10,16,256]{4,3,2,1,0:T(8,128)(2,1)S(1)}) custom-call(s32[1,2,6]{2,1,0:T(2,128)S(1)} %get-tuple-element.30.links_in, bf16[16,128]{1,0:T(8,128)(2,1)S(1)} %collective-permute-done.other_ref, bf16[64,2048]{1,0:T(8,128)(2,1)S(1)} %copy-done, ...), custom_call_target="tpu_custom_call" | custom-call | tf_op jit(solution)/shard_map/pallas_call | solution.py:557
  19.9 0.0 collective-permute-done.1.far
  19.9 1.1 %shard_map.99 = (bf16[448,128]{1,0:T(8,128)(2,1)S(1)}, bf16[256,128]{1,0:T(8,128)(2,1)S(1)}) custom-call(f32[48,128]{1,0:T(8,128)S(1)} %get-tuple-element.35.masks_ref, bf16[1,2,8,8,256]{4,3,2,1,0:T(8,128)(2,1)S(1)} %copy-done.1, bf16[9,256,128]{2,1,0:T(8,128)(2,1)S(1)} %get-tuple-element.36.band_ref, f32[256,128]{1,0:T(8,128)S(1)} %get-tuple-element.40.slope_ref, ...), custom_call_target="tpu_custom_call" | custom-call | tf_op jit(solution)/shard_map/pallas_call | solution.py:568
  21.1 10.1 %all_to_all.15 = bf16[32,7,2,128]{3,2,1,0:T(2,128)(2,1)S(1)} all-to-all(bf16[32,7,2,128]{3,2,1,0:T(2,128)(2,1)S(1)} %bitcast.10), channel_id=1, replica_groups=mesh['space'=16,'dp'=2] {'space','dp'}, dimensions={0} | all-to-all | bytes 229376 | tf_op jit(solution)/shard_map/all_to_all | solution.py:500
  31.2 0.7 %shard_map.100 = bf16[448,128]{1,0:T(8,128)(2,1)} custom-call(bf16[448,128]{1,0:T(8,128)(2,1)S(1)} %bitcast.6), custom_call_target="tpu_custom_call" | custom-call | tf_op jit(solution)/shard_map/pallas_call | solution.py:586
  31.9 2.6 %all-to-all-start.2 = ((bf16[32,7,2,128]{3,2,1,0:T(2,128)(2,1)}), bf16[32,7,2,128]{3,2,1,0:T(2,128)(2,1)S(1)}, u32[]{:S(2)}, u32[]{:S(2)}) async-start(bf16[32,7,2,128]{3,2,1,0:T(2,128)(2,1)} %bitcast.4), calls=%async_computation.2 | async-start | bytes 229376 | tf_op jit(solution)/shard_map/all_to_all | solution.py:500
  34.5 0.1 shard_map.102
  34.6 0.7 %collective-permute-start.3 = (bf16[48,256]{1,0:T(8,128)(2,1)S(1)}, bf16[48,256]{1,0:T(8,128)(2,1)S(1)}, u32[]{:S(2)}, u32[]{:S(2)}) collective-permute-start(bf16[48,256]{1,0:T(8,128)(2,1)S(1)} %get-tuple-element.52), channel_id=1, source_target_pairs={{2,4},{6,8},{10,12},{14,16},{18,20},{22,24},{26,28},{4,2},{8,6},{1... | collective-permute-start | bytes 73736 | tf_op jit(solution)/shard_map/ppermute | solution.py:494
  35.3 4.4 %collective-permute-start.4 = (bf16[48,256]{1,0:T(8,128)(2,1)S(1)}, bf16[48,256]{1,0:T(8,128)(2,1)S(1)}, u32[]{:S(2)}, u32[]{:S(2)}) collective-permute-start(bf16[48,256]{1,0:T(8,128)(2,1)S(1)} %get-tuple-element.53), channel_id=1, source_target_pairs={{0,2},{4,6},{8,10},{12,14},{16,18},{20,22},{24,26},{28,30},{2,0},{... | collective-permute-start | bytes 73736 | tf_op jit(solution)/shard_map/ppermute | solution.py:494
  39.7 0.3 shard_map.101.band_ref
  40.1 1.7 %collective-permute-done.4.near = bf16[48,256]{1,0:T(8,128)(2,1)S(1)} collective-permute-done((bf16[48,256]{1,0:T(8,128)(2,1)S(1)}, bf16[48,256]{1,0:T(8,128)(2,1)S(1)}, u32[]{:S(2)}, u32[]{:S(2)}) %collective-permute-start.4) | collective-permute-done | bytes 24608 | tf_op jit(solution)/shard_map/ppermute | solution.py:494
  41.8 0.5 %shard_map.103.fine_ref = bf16[1,2,8,8,256]{4,3,2,1,0:T(8,128)(2,1)S(1)} custom-call(f32[48,128]{1,0:T(8,128)S(1)} %get-tuple-element.35.masks_ref, bf16[9,256,128]{2,1,0:T(8,128)(2,1)S(1)} %shard_map.101.band_ref, bf16[256,128]{1,0:T(8,128)(2,1)S(1)} %get-tuple-element.48.lifted_ref, bf16[256,128]{1,0:T(8,128)(2,1)S(1)} %get-tuple-element.49.hidden_ref, ...), custom_call_target="tpu_custom_call" | custom-call | flops 1000000000 | bytes 2000000 | tf_op jit(solution)/shard_map/pallas_call | solution.py:581
  42.2 0.3 all-to-all-done.2
  42.6 1.1 %shard_map.104 = (f32[27,32,32]{2,1,0:T(8,128)}, f32[27,32,32]{2,1,0:T(8,128)}, bf16[1,2,8,8,256]{4,3,2,1,0:T(8,128)(2,1)}) custom-call(bf16[448,128]{1,0:T(8,128)(2,1)S(1)} %bitcast.8, bf16[1,2,8,8,256]{4,3,2,1,0:T(8,128)(2,1)S(1)} %shard_map.103.fine_ref), custom_call_target="tpu_custom_call" | custom-call | tf_op jit(solution)/shard_map/pallas_call | solution.py:601
  (6 shorter events, 0.0 us)
Async XLA Ops:
  0.6 9.1 %copy-start.1 = (bf16[1,2,8,8,256]{4,3,2,1,0:T(8,128)(2,1)S(1)}, bf16[1,2,8,8,256]{4,3,2,1,0:T(8,128)(2,1)}, u32[]{:S(2)}) copy-start(bf16[1,2,8,8,256]{4,3,2,1,0:T(8,128)(2,1)} %cotangent_ref.3) | copy-start | bytes 196612
  2.5 15.4 %copy-start = (bf16[64,2048]{1,0:T(8,128)(2,1)S(1)}, bf16[64,2048]{1,0:T(8,128)(2,1)}, u32[]{:S(2)}) copy-start(bf16[64,2048]{1,0:T(8,128)(2,1)} %up_ref.3) | copy-start | bytes 786436
  2.5 15.1 %all-to-all-start = ((bf16[32,6,2,128]{3,2,1,0:T(2,128)(2,1)}), bf16[32,6,2,128]{3,2,1,0:T(2,128)(2,1)S(1)}, u32[]{:S(2)}, u32[]{:S(2)}) async-start(bf16[32,6,2,128]{3,2,1,0:T(2,128)(2,1)} %bitcast), calls=%async_computation | async-start | bytes 196608 | tf_op jit(solution)/shard_map/all_to_all | solution.py:500
  9.9 10.0 %collective-permute-start.1 = (bf16[48,256]{1,0:T(8,128)(2,1)S(1)}, bf16[48,256]{1,0:T(8,128)(2,1)S(1)}, u32[]{:S(2)}, u32[]{:S(2)}) collective-permute-start(bf16[48,256]{1,0:T(8,128)(2,1)S(1)} %get-tuple-element.45), channel_id=1, source_target_pairs={{2,4},{6,8},{10,12},{14,16},{18,20},{22,24},{26,28},{4,2},{8,6},{1... | collective-permute-start | bytes 73736 | tf_op jit(solution)/shard_map/ppermute | solution.py:494
  10.6 9.4 %collective-permute-start.2 = (bf16[48,256]{1,0:T(8,128)(2,1)S(1)}, bf16[48,256]{1,0:T(8,128)(2,1)S(1)}, u32[]{:S(2)}, u32[]{:S(2)}) collective-permute-start(bf16[48,256]{1,0:T(8,128)(2,1)S(1)} %get-tuple-element.46), channel_id=1, source_target_pairs={{0,2},{4,6},{8,10},{12,14},{16,18},{20,22},{24,26},{28,30},{2,0},{... | collective-permute-start | bytes 73736 | tf_op jit(solution)/shard_map/ppermute | solution.py:494
  17.6 1.2 %collective-permute-start = (bf16[16,128]{1,0:T(8,128)(2,1)S(1)}, bf16[16,128]{1,0:T(8,128)(2,1)S(1)}, u32[]{:S(2)}, u32[]{:S(2)}) collective-permute-start(bf16[16,128]{1,0:T(8,128)(2,1)S(1)} %get-tuple-element.37), channel_id=1, source_target_pairs={{0,1},{1,0},{2,3},{3,2},{4,5},{5,4},{6,7},{7,6},{8,9},{9,8},{10,11... | collective-permute-start | bytes 12296 | tf_op jit(solution)/shard_map/ppermute | solution.py:533
  31.9 10.6 %all-to-all-start.2 = ((bf16[32,7,2,128]{3,2,1,0:T(2,128)(2,1)}), bf16[32,7,2,128]{3,2,1,0:T(2,128)(2,1)S(1)}, u32[]{:S(2)}, u32[]{:S(2)}) async-start(bf16[32,7,2,128]{3,2,1,0:T(2,128)(2,1)} %bitcast.4), calls=%async_computation.2 | async-start | bytes 229376 | tf_op jit(solution)/shard_map/all_to_all | solution.py:500
  34.6 5.4 %collective-permute-start.3 = (bf16[48,256]{1,0:T(8,128)(2,1)S(1)}, bf16[48,256]{1,0:T(8,128)(2,1)S(1)}, u32[]{:S(2)}, u32[]{:S(2)}) collective-permute-start(bf16[48,256]{1,0:T(8,128)(2,1)S(1)} %get-tuple-element.52), channel_id=1, source_target_pairs={{2,4},{6,8},{10,12},{14,16},{18,20},{22,24},{26,28},{4,2},{8,6},{1... | collective-permute-start | bytes 73736 | tf_op jit(solution)/shard_map/ppermute | solution.py:494
  35.3 6.5 %collective-permute-start.4 = (bf16[48,256]{1,0:T(8,128)(2,1)S(1)}, bf16[48,256]{1,0:T(8,128)(2,1)S(1)}, u32[]{:S(2)}, u32[]{:S(2)}) collective-permute-start(bf16[48,256]{1,0:T(8,128)(2,1)S(1)} %get-tuple-element.53), channel_id=1, source_target_pairs={{0,2},{4,6},{8,10},{12,14},{16,18},{20,22},{24,26},{28,30},{2,0},{... | collective-permute-start | bytes 73736 | tf_op jit(solution)/shard_map/ppermute | solution.py:494

commit v31 on v29

--- a/solution.py
+++ b/solution.py
@@ -55,7 +55,7 @@
     latents_copy.start()
     others = [pltpu.make_async_copy(*pair, sems.at[2 + i]) for i, pair in enumerate(brought)]
     for copy in others:
-        copy.start()
+        copy.start(priority=1)
     held, width = latents_ref.shape[1:]
     bricks = ids_ref.shape[1]
     tiles = width // 256

time: 44 us -> 44 us (level)
  no operation moved by 1% of the time
where the time goes in v31:
time: 44 us; the launch traced here: 43.7 us
  starting transfers between devices  20.4 us (46%)
  blocking collectives  10.2 us (23%)
  Pallas kernels  7.41 us (17%)
  waiting for transfers between devices  4.96 us (11%)
  between operations  0.77 us (2%)
    ppermute x4, starting transfers between devices, swapped(): lax.ppermute(value, 'space', pairs + [(target, source) for source, target...  10.3 us
    all_to_all x1, blocking collectives, exchanged(): lax.all_to_all(shares, axes, split_axis=0, concat_axis=0, tiled=True)  10.2 us
    all_to_all x2, starting transfers between devices, exchanged(): lax.all_to_all(shares, axes, split_axis=0, concat_axis=0, tiled=True)  9.89 us
    all_to_all x2, waiting for transfers between devices, exchanged(): lax.all_to_all(shares, axes, split_axis=0, concat_axis=0, tiled=True)  2.81 us
    pallas_call x1, Pallas kernels, body(): call(functools.partial(pick_kernel, split, len(extras)), (shape(*blocks),...  1.86 us
    ppermute x4, waiting for transfers between devices, swapped(): lax.ppermute(value, 'space', pairs + [(target, source) for source, target...  1.71 us
    pallas_call x1, Pallas kernels, body(): call(second_kernel, (shape(*packed_rows), volume), [pool, pool, pad, pltp...  1.11 us
    pallas_call x1, Pallas kernels, body(): call(unpack_kernel, (grads, grads, shape(*fine.shape)), scratch, inputs=2...  1.07 us
  transfers between devices with their start and end apart: 7, of which 4 were waited for; matrix products, arithmetic and copies ran while one was open for 0% of the time, Pallas kernels for 6%

profile of v31, /device:TPU:0, one launch (start us, length us, event | category | flops | bytes accessed | tf_op | source)
XLA Modules:
  0.0 43.7 jit_solution(360687496220254501)
XLA Ops:
  0.6 1.9 %shard_map.94 = (bf16[384,128]{1,0:T(8,128)(2,1)}, bf16[64,2048]{1,0:T(8,128)(2,1)S(1)}, bf16[27,32,32]{2,1,0:T(8,128)(2,1)S(1)}, bf16[27,32,32]{2,1,0:T(8,128)(2,1)S(1)}, s32[1,2,6]{2,1,0:T(2,128)S(1)}) custom-call(s32[1,32]{1,0:T(1,128)} %ids_hbm.1, bf16[1,64,512]{2,1,0:T(8,128)(2,1)} %latents_hbm.1, bf16[64,2048]{1,0:T(8,128)(2,1)} %refs_0_.1, ...), custom_call_target="tpu_custom_call" | custom-call | tf_op jit(solution)/shard_map/pallas_call | solution.py:514
  2.5 0.0 copy-start
  2.5 7.3 %all-to-all-start = ((bf16[32,6,2,128]{3,2,1,0:T(2,128)(2,1)}), bf16[32,6,2,128]{3,2,1,0:T(2,128)(2,1)S(1)}, u32[]{:S(2)}, u32[]{:S(2)}) async-start(bf16[32,6,2,128]{3,2,1,0:T(2,128)(2,1)} %bitcast), calls=%async_computation | async-start | bytes 196608 | tf_op jit(solution)/shard_map/all_to_all | solution.py:500
  9.8 0.1 shard_map.98
  9.9 0.7 %collective-permute-start.1 = (bf16[48,256]{1,0:T(8,128)(2,1)S(1)}, bf16[48,256]{1,0:T(8,128)(2,1)S(1)}, u32[]{:S(2)}, u32[]{:S(2)}) collective-permute-start(bf16[48,256]{1,0:T(8,128)(2,1)S(1)} %get-tuple-element.47), channel_id=1, source_target_pairs={{2,4},{6,8},{10,12},{14,16},{18,20},{22,24},{26,28},{4,2},{8,6},{1... | collective-permute-start | bytes 73736 | tf_op jit(solution)/shard_map/ppermute | solution.py:494
  10.6 4.5 %collective-permute-start.2 = (bf16[48,256]{1,0:T(8,128)(2,1)S(1)}, bf16[48,256]{1,0:T(8,128)(2,1)S(1)}, u32[]{:S(2)}, u32[]{:S(2)}) collective-permute-start(bf16[48,256]{1,0:T(8,128)(2,1)S(1)} %get-tuple-element.48), channel_id=1, source_target_pairs={{0,2},{4,6},{8,10},{12,14},{16,18},{20,22},{24,26},{28,30},{2,0},{... | collective-permute-start | bytes 73736 | tf_op jit(solution)/shard_map/ppermute | solution.py:494
  15.1 2.5 %all-to-all-done = bf16[32,6,2,128]{3,2,1,0:T(2,128)(2,1)S(1)} async-done(((bf16[32,6,2,128]{3,2,1,0:T(2,128)(2,1)}), bf16[32,6,2,128]{3,2,1,0:T(2,128)(2,1)S(1)}, u32[]{:S(2)}, u32[]{:S(2)}) %all-to-all-start) | async-done | bytes 98336 | tf_op jit(solution)/shard_map/all_to_all | solution.py:500
  17.7 0.2 collective-permute-start
  17.9 0.6 %shard_map.96 = (bf16[9,256,128]{2,1,0:T(8,128)(2,1)S(1)}, bf16[9,256,128]{2,1,0:T(8,128)(2,1)S(1)}, f32[48,128]{1,0:T(8,128)S(1)}, f32[2,256,128]{2,1,0:T(8,128)S(1)}) custom-call(s32[1,2,6]{2,1,0:T(2,128)S(1)} %get-tuple-element.31.links_in, bf16[16,128]{1,0:T(8,128)(2,1)S(1)} %get-tuple-element.33.own_ref, bf16[64,2048]{1,0:T(8,128)(2,1)S(1)} %get-tuple-element.34.up_ref, ...), custom_call_target="tpu_custom_call" | custom-call | flops 1000000000 | bytes 2000000 | tf_op jit(solution)/shard_map/pallas_call | solution.py:549
  18.5 0.4 collective-permute-done.other_ref
  18.9 1.1 %shard_map.97 = (f32[256,128]{1,0:T(8,128)S(1)}, bf16[256,128]{1,0:T(8,128)(2,1)S(1)}, bf16[128,256]{1,0:T(8,128)(2,1)S(1)}, bf16[3,2,10,16,256]{4,3,2,1,0:T(8,128)(2,1)S(1)}) custom-call(s32[1,2,6]{2,1,0:T(2,128)S(1)} %get-tuple-element.31.links_in, bf16[16,128]{1,0:T(8,128)(2,1)S(1)} %collective-permute-done.other_ref, ...), custom_call_target="tpu_custom_call" | custom-call | tf_op jit(solution)/shard_map/pallas_call | solution.py:557
  20.0 0.0 collective-permute-done.1.far
  20.0 1.1 %shard_map.99 = (bf16[448,128]{1,0:T(8,128)(2,1)S(1)}, bf16[256,128]{1,0:T(8,128)(2,1)S(1)}) custom-call(f32[48,128]{1,0:T(8,128)S(1)} %get-tuple-element.37.masks_ref, bf16[1,2,8,8,256]{4,3,2,1,0:T(8,128)(2,1)S(1)} %copy-done, bf16[9,256,128]{2,1,0:T(8,128)(2,1)S(1)} %get-tuple-element.38.band_ref, f32[256,128]{1,0:T(8,128)S(1)} %get-tuple-element.42.slope_ref, ...), custom_call_target="tpu_custom_call" | custom-call | tf_op jit(solution)/shard_map/pallas_call | solution.py:568
  21.1 10.2 %all_to_all.15 = bf16[32,7,2,128]{3,2,1,0:T(2,128)(2,1)S(1)} all-to-all(bf16[32,7,2,128]{3,2,1,0:T(2,128)(2,1)S(1)} %bitcast.10), channel_id=1, replica_groups=mesh['space'=16,'dp'=2] {'space','dp'}, dimensions={0} | all-to-all | bytes 229376 | tf_op jit(solution)/shard_map/all_to_all | solution.py:500
  31.3 0.7 %shard_map.100 = bf16[448,128]{1,0:T(8,128)(2,1)} custom-call(bf16[448,128]{1,0:T(8,128)(2,1)S(1)} %bitcast.6), custom_call_target="tpu_custom_call" | custom-call | tf_op jit(solution)/shard_map/pallas_call | solution.py:586
  32.0 2.6 %all-to-all-start.2 = ((bf16[32,7,2,128]{3,2,1,0:T(2,128)(2,1)}), bf16[32,7,2,128]{3,2,1,0:T(2,128)(2,1)S(1)}, u32[]{:S(2)}, u32[]{:S(2)}) async-start(bf16[32,7,2,128]{3,2,1,0:T(2,128)(2,1)} %bitcast.4), calls=%async_computation.2 | async-start | bytes 229376 | tf_op jit(solution)/shard_map/all_to_all | solution.py:500
  34.6 0.1 shard_map.102
  34.7 0.7 %collective-permute-start.3 = (bf16[48,256]{1,0:T(8,128)(2,1)S(1)}, bf16[48,256]{1,0:T(8,128)(2,1)S(1)}, u32[]{:S(2)}, u32[]{:S(2)}) collective-permute-start(bf16[48,256]{1,0:T(8,128)(2,1)S(1)} %get-tuple-element.54), channel_id=1, source_target_pairs={{2,4},{6,8},{10,12},{14,16},{18,20},{22,24},{26,28},{4,2},{8,6},{1... | collective-permute-start | bytes 73736 | tf_op jit(solution)/shard_map/ppermute | solution.py:494
  35.3 4.4 %collective-permute-start.4 = (bf16[48,256]{1,0:T(8,128)(2,1)S(1)}, bf16[48,256]{1,0:T(8,128)(2,1)S(1)}, u32[]{:S(2)}, u32[]{:S(2)}) collective-permute-start(bf16[48,256]{1,0:T(8,128)(2,1)S(1)} %get-tuple-element.55), channel_id=1, source_target_pairs={{0,2},{4,6},{8,10},{12,14},{16,18},{20,22},{24,26},{28,30},{2,0},{... | collective-permute-start | bytes 73736 | tf_op jit(solution)/shard_map/ppermute | solution.py:494
  39.8 0.3 shard_map.101.band_ref
  40.1 1.7 %collective-permute-done.4.near = bf16[48,256]{1,0:T(8,128)(2,1)S(1)} collective-permute-done((bf16[48,256]{1,0:T(8,128)(2,1)S(1)}, bf16[48,256]{1,0:T(8,128)(2,1)S(1)}, u32[]{:S(2)}, u32[]{:S(2)}) %collective-permute-start.4) | collective-permute-done | bytes 24608 | tf_op jit(solution)/shard_map/ppermute | solution.py:494
  41.8 0.5 %shard_map.103.fine_ref = bf16[1,2,8,8,256]{4,3,2,1,0:T(8,128)(2,1)S(1)} custom-call(f32[48,128]{1,0:T(8,128)S(1)} %get-tuple-element.37.masks_ref, bf16[9,256,128]{2,1,0:T(8,128)(2,1)S(1)} %shard_map.101.band_ref, bf16[256,128]{1,0:T(8,128)(2,1)S(1)} %get-tuple-element.50.lifted_ref, bf16[256,128]{1,0:T(8,128)(2,1)S(1)} %get-tuple-element.51.hidden_ref, ...), custom_call_target="tpu_custom_call" | custom-call | flops 1000000000 | bytes 2000000 | tf_op jit(solution)/shard_map/pallas_call | solution.py:581
  42.3 0.3 all-to-all-done.2
  42.6 1.1 %shard_map.104 = (f32[27,32,32]{2,1,0:T(8,128)}, f32[27,32,32]{2,1,0:T(8,128)}, bf16[1,2,8,8,256]{4,3,2,1,0:T(8,128)(2,1)}) custom-call(bf16[448,128]{1,0:T(8,128)(2,1)S(1)} %bitcast.8, bf16[1,2,8,8,256]{4,3,2,1,0:T(8,128)(2,1)S(1)} %shard_map.103.fine_ref), custom_call_target="tpu_custom_call" | custom-call | tf_op jit(solution)/shard_map/pallas_call | solution.py:601
  (4 shorter events, 0.0 us)
Async XLA Ops:
  2.5 7.3 %copy-start = (bf16[1,2,8,8,256]{4,3,2,1,0:T(8,128)(2,1)S(1)}, bf16[1,2,8,8,256]{4,3,2,1,0:T(8,128)(2,1)}, u32[]{:S(2)}) copy-start(bf16[1,2,8,8,256]{4,3,2,1,0:T(8,128)(2,1)} %cotangent_ref.3) | copy-start | bytes 196612
  2.5 15.1 %all-to-all-start = ((bf16[32,6,2,128]{3,2,1,0:T(2,128)(2,1)}), bf16[32,6,2,128]{3,2,1,0:T(2,128)(2,1)S(1)}, u32[]{:S(2)}, u32[]{:S(2)}) async-start(bf16[32,6,2,128]{3,2,1,0:T(2,128)(2,1)} %bitcast), calls=%async_computation | async-start | bytes 196608 | tf_op jit(solution)/shard_map/all_to_all | solution.py:500
  9.9 10.0 %collective-permute-start.1 = (bf16[48,256]{1,0:T(8,128)(2,1)S(1)}, bf16[48,256]{1,0:T(8,128)(2,1)S(1)}, u32[]{:S(2)}, u32[]{:S(2)}) collective-permute-start(bf16[48,256]{1,0:T(8,128)(2,1)S(1)} %get-tuple-element.47), channel_id=1, source_target_pairs={{2,4},{6,8},{10,12},{14,16},{18,20},{22,24},{26,28},{4,2},{8,6},{1... | collective-permute-start | bytes 73736 | tf_op jit(solution)/shard_map/ppermute | solution.py:494
  10.6 9.4 %collective-permute-start.2 = (bf16[48,256]{1,0:T(8,128)(2,1)S(1)}, bf16[48,256]{1,0:T(8,128)(2,1)S(1)}, u32[]{:S(2)}, u32[]{:S(2)}) collective-permute-start(bf16[48,256]{1,0:T(8,128)(2,1)S(1)} %get-tuple-element.48), channel_id=1, source_target_pairs={{0,2},{4,6},{8,10},{12,14},{16,18},{20,22},{24,26},{28,30},{2,0},{... | collective-permute-start | bytes 73736 | tf_op jit(solution)/shard_map/ppermute | solution.py:494
  17.7 1.2 %collective-permute-start = (bf16[16,128]{1,0:T(8,128)(2,1)S(1)}, bf16[16,128]{1,0:T(8,128)(2,1)S(1)}, u32[]{:S(2)}, u32[]{:S(2)}) collective-permute-start(bf16[16,128]{1,0:T(8,128)(2,1)S(1)} %get-tuple-element.39), channel_id=1, source_target_pairs={{0,1},{1,0},{2,3},{3,2},{4,5},{5,4},{6,7},{7,6},{8,9},{9,8},{10,11... | collective-permute-start | bytes 12296 | tf_op jit(solution)/shard_map/ppermute | solution.py:533
  32.0 10.6 %all-to-all-start.2 = ((bf16[32,7,2,128]{3,2,1,0:T(2,128)(2,1)}), bf16[32,7,2,128]{3,2,1,0:T(2,128)(2,1)S(1)}, u32[]{:S(2)}, u32[]{:S(2)}) async-start(bf16[32,7,2,128]{3,2,1,0:T(2,128)(2,1)} %bitcast.4), calls=%async_computation.2 | async-start | bytes 229376 | tf_op jit(solution)/shard_map/all_to_all | solution.py:500
  34.7 5.4 %collective-permute-start.3 = (bf16[48,256]{1,0:T(8,128)(2,1)S(1)}, bf16[48,256]{1,0:T(8,128)(2,1)S(1)}, u32[]{:S(2)}, u32[]{:S(2)}) collective-permute-start(bf16[48,256]{1,0:T(8,128)(2,1)S(1)} %get-tuple-element.54), channel_id=1, source_target_pairs={{2,4},{6,8},{10,12},{14,16},{18,20},{22,24},{26,28},{4,2},{8,6},{1... | collective-permute-start | bytes 73736 | tf_op jit(solution)/shard_map/ppermute | solution.py:494
  35.3 6.5 %collective-permute-start.4 = (bf16[48,256]{1,0:T(8,128)(2,1)S(1)}, bf16[48,256]{1,0:T(8,128)(2,1)S(1)}, u32[]{:S(2)}, u32[]{:S(2)}) collective-permute-start(bf16[48,256]{1,0:T(8,128)(2,1)S(1)} %get-tuple-element.55), channel_id=1, source_target_pairs={{0,2},{4,6},{8,10},{12,14},{16,18},{20,22},{24,26},{28,30},{2,0},{... | collective-permute-start | bytes 73736 | tf_op jit(solution)/shard_map/ppermute | solution.py:494

commit v32 on v31

--- a/solution.py
+++ b/solution.py
@@ -445,7 +445,7 @@
 
 def unpack_kernel(sums_ref, fine_ref, one_out, two_out, fine_out, rows_ref, one_ref, two_ref, sems, fine_sem):
     fine_copy = pltpu.make_async_copy(fine_ref, fine_out, fine_sem)
-    fine_copy.start()
+    fine_copy.start(priority=1)
     rows_ref[...] = sums_ref[...].astype(F32)
     copies = []
     for which, (block_ref, out) in ((1, (two_ref, two_out)), (0, (one_ref, one_out))):

time: 44 us -> 44 us (level)
  no operation moved by 1% of the time
where the time goes in v32:
time: 44 us; the launch traced here: 43.7 us
  starting transfers between devices  20.4 us (46%)
  blocking collectives  10.2 us (23%)
  Pallas kernels  7.4 us (17%)
  waiting for transfers between devices  4.96 us (11%)
  between operations  0.77 us (2%)
    ppermute x4, starting transfers between devices, swapped(): lax.ppermute(value, 'space', pairs + [(target, source) for source, target...  10.3 us
    all_to_all x1, blocking collectives, exchanged(): lax.all_to_all(shares, axes, split_axis=0, concat_axis=0, tiled=True)  10.2 us
    all_to_all x2, starting transfers between devices, exchanged(): lax.all_to_all(shares, axes, split_axis=0, concat_axis=0, tiled=True)  9.89 us
    all_to_all x2, waiting for transfers between devices, exchanged(): lax.all_to_all(shares, axes, split_axis=0, concat_axis=0, tiled=True)  2.81 us
    pallas_call x1, Pallas kernels, body(): call(functools.partial(pick_kernel, split, len(extras)), (shape(*blocks),...  1.86 us
    ppermute x4, waiting for transfers between devices, swapped(): lax.ppermute(value, 'space', pairs + [(target, source) for source, target...  1.71 us
    pallas_call x1, Pallas kernels, body(): call(second_kernel, (shape(*packed_rows), volume), [pool, pool, pad, pltp...  1.11 us
    pallas_call x1, Pallas kernels, body(): call(unpack_kernel, (grads, grads, shape(*fine.shape)), scratch, inputs=2...  1.06 us
  transfers between devices with their start and end apart: 7, of which 4 were waited for; matrix products, arithmetic and copies ran while one was open for 0% of the time, Pallas kernels for 6%

profile of v32, /device:TPU:0, one launch (start us, length us, event | category | flops | bytes accessed | tf_op | source)
XLA Modules:
  0.0 43.7 jit_solution(11082361599006550372)
XLA Ops:
  0.6 1.9 %shard_map.94 = (bf16[384,128]{1,0:T(8,128)(2,1)}, bf16[64,2048]{1,0:T(8,128)(2,1)S(1)}, bf16[27,32,32]{2,1,0:T(8,128)(2,1)S(1)}, bf16[27,32,32]{2,1,0:T(8,128)(2,1)S(1)}, s32[1,2,6]{2,1,0:T(2,128)S(1)}) custom-call(s32[1,32]{1,0:T(1,128)} %ids_hbm.1, bf16[1,64,512]{2,1,0:T(8,128)(2,1)} %latents_hbm.1, bf16[64,2048]{1,0:T(8,128)(2,1)} %refs_0_.1, ...), custom_call_target="tpu_custom_call" | custom-call | tf_op jit(solution)/shard_map/pallas_call | solution.py:514
  2.5 0.0 copy-start
  2.5 7.3 %all-to-all-start = ((bf16[32,6,2,128]{3,2,1,0:T(2,128)(2,1)}), bf16[32,6,2,128]{3,2,1,0:T(2,128)(2,1)S(1)}, u32[]{:S(2)}, u32[]{:S(2)}) async-start(bf16[32,6,2,128]{3,2,1,0:T(2,128)(2,1)} %bitcast), calls=%async_computation | async-start | bytes 196608 | tf_op jit(solution)/shard_map/all_to_all | solution.py:500
  9.8 0.1 shard_map.98
  9.9 0.7 %collective-permute-start.1 = (bf16[48,256]{1,0:T(8,128)(2,1)S(1)}, bf16[48,256]{1,0:T(8,128)(2,1)S(1)}, u32[]{:S(2)}, u32[]{:S(2)}) collective-permute-start(bf16[48,256]{1,0:T(8,128)(2,1)S(1)} %get-tuple-element.47), channel_id=1, source_target_pairs={{2,4},{6,8},{10,12},{14,16},{18,20},{22,24},{26,28},{4,2},{8,6},{1... | collective-permute-start | bytes 73736 | tf_op jit(solution)/shard_map/ppermute | solution.py:494
  10.6 4.5 %collective-permute-start.2 = (bf16[48,256]{1,0:T(8,128)(2,1)S(1)}, bf16[48,256]{1,0:T(8,128)(2,1)S(1)}, u32[]{:S(2)}, u32[]{:S(2)}) collective-permute-start(bf16[48,256]{1,0:T(8,128)(2,1)S(1)} %get-tuple-element.48), channel_id=1, source_target_pairs={{0,2},{4,6},{8,10},{12,14},{16,18},{20,22},{24,26},{28,30},{2,0},{... | collective-permute-start | bytes 73736 | tf_op jit(solution)/shard_map/ppermute | solution.py:494
  15.1 2.5 %all-to-all-done = bf16[32,6,2,128]{3,2,1,0:T(2,128)(2,1)S(1)} async-done(((bf16[32,6,2,128]{3,2,1,0:T(2,128)(2,1)}), bf16[32,6,2,128]{3,2,1,0:T(2,128)(2,1)S(1)}, u32[]{:S(2)}, u32[]{:S(2)}) %all-to-all-start) | async-done | bytes 98336 | tf_op jit(solution)/shard_map/all_to_all | solution.py:500
  17.7 0.2 collective-permute-start
  17.9 0.6 %shard_map.96 = (bf16[9,256,128]{2,1,0:T(8,128)(2,1)S(1)}, bf16[9,256,128]{2,1,0:T(8,128)(2,1)S(1)}, f32[48,128]{1,0:T(8,128)S(1)}, f32[2,256,128]{2,1,0:T(8,128)S(1)}) custom-call(s32[1,2,6]{2,1,0:T(2,128)S(1)} %get-tuple-element.31.links_in, bf16[16,128]{1,0:T(8,128)(2,1)S(1)} %get-tuple-element.33.own_ref, bf16[64,2048]{1,0:T(8,128)(2,1)S(1)} %get-tuple-element.34.up_ref, ...), custom_call_target="tpu_custom_call" | custom-call | flops 1000000000 | bytes 2000000 | tf_op jit(solution)/shard_map/pallas_call | solution.py:549
  18.5 0.4 collective-permute-done.other_ref
  18.9 1.1 %shard_map.97 = (f32[256,128]{1,0:T(8,128)S(1)}, bf16[256,128]{1,0:T(8,128)(2,1)S(1)}, bf16[128,256]{1,0:T(8,128)(2,1)S(1)}, bf16[3,2,10,16,256]{4,3,2,1,0:T(8,128)(2,1)S(1)}) custom-call(s32[1,2,6]{2,1,0:T(2,128)S(1)} %get-tuple-element.31.links_in, bf16[16,128]{1,0:T(8,128)(2,1)S(1)} %collective-permute-done.other_ref, ...), custom_call_target="tpu_custom_call" | custom-call | tf_op jit(solution)/shard_map/pallas_call | solution.py:557
  20.0 0.0 collective-permute-done.1.far
  20.0 1.1 %shard_map.99 = (bf16[448,128]{1,0:T(8,128)(2,1)S(1)}, bf16[256,128]{1,0:T(8,128)(2,1)S(1)}) custom-call(f32[48,128]{1,0:T(8,128)S(1)} %get-tuple-element.37.masks_ref, bf16[1,2,8,8,256]{4,3,2,1,0:T(8,128)(2,1)S(1)} %copy-done, bf16[9,256,128]{2,1,0:T(8,128)(2,1)S(1)} %get-tuple-element.38.band_ref, f32[256,128]{1,0:T(8,128)S(1)} %get-tuple-element.42.slope_ref, ...), custom_call_target="tpu_custom_call" | custom-call | tf_op jit(solution)/shard_map/pallas_call | solution.py:568
  21.1 10.2 %all_to_all.15 = bf16[32,7,2,128]{3,2,1,0:T(2,128)(2,1)S(1)} all-to-all(bf16[32,7,2,128]{3,2,1,0:T(2,128)(2,1)S(1)} %bitcast.10), channel_id=1, replica_groups=mesh['space'=16,'dp'=2] {'space','dp'}, dimensions={0} | all-to-all | bytes 229376 | tf_op jit(solution)/shard_map/all_to_all | solution.py:500
  31.3 0.7 %shard_map.100 = bf16[448,128]{1,0:T(8,128)(2,1)} custom-call(bf16[448,128]{1,0:T(8,128)(2,1)S(1)} %bitcast.6), custom_call_target="tpu_custom_call" | custom-call | tf_op jit(solution)/shard_map/pallas_call | solution.py:586
  32.0 2.6 %all-to-all-start.2 = ((bf16[32,7,2,128]{3,2,1,0:T(2,128)(2,1)}), bf16[32,7,2,128]{3,2,1,0:T(2,128)(2,1)S(1)}, u32[]{:S(2)}, u32[]{:S(2)}) async-start(bf16[32,7,2,128]{3,2,1,0:T(2,128)(2,1)} %bitcast.4), calls=%async_computation.2 | async-start | bytes 229376 | tf_op jit(solution)/shard_map/all_to_all | solution.py:500
  34.6 0.1 shard_map.102
  34.7 0.7 %collective-permute-start.3 = (bf16[48,256]{1,0:T(8,128)(2,1)S(1)}, bf16[48,256]{1,0:T(8,128)(2,1)S(1)}, u32[]{:S(2)}, u32[]{:S(2)}) collective-permute-start(bf16[48,256]{1,0:T(8,128)(2,1)S(1)} %get-tuple-element.54), channel_id=1, source_target_pairs={{2,4},{6,8},{10,12},{14,16},{18,20},{22,24},{26,28},{4,2},{8,6},{1... | collective-permute-start | bytes 73736 | tf_op jit(solution)/shard_map/ppermute | solution.py:494
  35.3 4.4 %collective-permute-start.4 = (bf16[48,256]{1,0:T(8,128)(2,1)S(1)}, bf16[48,256]{1,0:T(8,128)(2,1)S(1)}, u32[]{:S(2)}, u32[]{:S(2)}) collective-permute-start(bf16[48,256]{1,0:T(8,128)(2,1)S(1)} %get-tuple-element.55), channel_id=1, source_target_pairs={{0,2},{4,6},{8,10},{12,14},{16,18},{20,22},{24,26},{28,30},{2,0},{... | collective-permute-start | bytes 73736 | tf_op jit(solution)/shard_map/ppermute | solution.py:494
  39.8 0.3 shard_map.101.band_ref
  40.1 1.7 %collective-permute-done.4.near = bf16[48,256]{1,0:T(8,128)(2,1)S(1)} collective-permute-done((bf16[48,256]{1,0:T(8,128)(2,1)S(1)}, bf16[48,256]{1,0:T(8,128)(2,1)S(1)}, u32[]{:S(2)}, u32[]{:S(2)}) %collective-permute-start.4) | collective-permute-done | bytes 24608 | tf_op jit(solution)/shard_map/ppermute | solution.py:494
  41.8 0.5 %shard_map.103.fine_ref = bf16[1,2,8,8,256]{4,3,2,1,0:T(8,128)(2,1)S(1)} custom-call(f32[48,128]{1,0:T(8,128)S(1)} %get-tuple-element.37.masks_ref, bf16[9,256,128]{2,1,0:T(8,128)(2,1)S(1)} %shard_map.101.band_ref, bf16[256,128]{1,0:T(8,128)(2,1)S(1)} %get-tuple-element.50.lifted_ref, bf16[256,128]{1,0:T(8,128)(2,1)S(1)} %get-tuple-element.51.hidden_ref, ...), custom_call_target="tpu_custom_call" | custom-call | flops 1000000000 | bytes 2000000 | tf_op jit(solution)/shard_map/pallas_call | solution.py:581
  42.3 0.3 all-to-all-done.2
  42.6 1.1 %shard_map.104 = (f32[27,32,32]{2,1,0:T(8,128)}, f32[27,32,32]{2,1,0:T(8,128)}, bf16[1,2,8,8,256]{4,3,2,1,0:T(8,128)(2,1)}) custom-call(bf16[448,128]{1,0:T(8,128)(2,1)S(1)} %bitcast.8, bf16[1,2,8,8,256]{4,3,2,1,0:T(8,128)(2,1)S(1)} %shard_map.103.fine_ref), custom_call_target="tpu_custom_call" | custom-call | tf_op jit(solution)/shard_map/pallas_call | solution.py:601
  (4 shorter events, 0.0 us)
Async XLA Ops:
  2.5 7.3 %copy-start = (bf16[1,2,8,8,256]{4,3,2,1,0:T(8,128)(2,1)S(1)}, bf16[1,2,8,8,256]{4,3,2,1,0:T(8,128)(2,1)}, u32[]{:S(2)}) copy-start(bf16[1,2,8,8,256]{4,3,2,1,0:T(8,128)(2,1)} %cotangent_ref.3) | copy-start | bytes 196612
  2.5 15.1 %all-to-all-start = ((bf16[32,6,2,128]{3,2,1,0:T(2,128)(2,1)}), bf16[32,6,2,128]{3,2,1,0:T(2,128)(2,1)S(1)}, u32[]{:S(2)}, u32[]{:S(2)}) async-start(bf16[32,6,2,128]{3,2,1,0:T(2,128)(2,1)} %bitcast), calls=%async_computation | async-start | bytes 196608 | tf_op jit(solution)/shard_map/all_to_all | solution.py:500
  9.9 10.0 %collective-permute-start.1 = (bf16[48,256]{1,0:T(8,128)(2,1)S(1)}, bf16[48,256]{1,0:T(8,128)(2,1)S(1)}, u32[]{:S(2)}, u32[]{:S(2)}) collective-permute-start(bf16[48,256]{1,0:T(8,128)(2,1)S(1)} %get-tuple-element.47), channel_id=1, source_target_pairs={{2,4},{6,8},{10,12},{14,16},{18,20},{22,24},{26,28},{4,2},{8,6},{1... | collective-permute-start | bytes 73736 | tf_op jit(solution)/shard_map/ppermute | solution.py:494
  10.6 9.4 %collective-permute-start.2 = (bf16[48,256]{1,0:T(8,128)(2,1)S(1)}, bf16[48,256]{1,0:T(8,128)(2,1)S(1)}, u32[]{:S(2)}, u32[]{:S(2)}) collective-permute-start(bf16[48,256]{1,0:T(8,128)(2,1)S(1)} %get-tuple-element.48), channel_id=1, source_target_pairs={{0,2},{4,6},{8,10},{12,14},{16,18},{20,22},{24,26},{28,30},{2,0},{... | collective-permute-start | bytes 73736 | tf_op jit(solution)/shard_map/ppermute | solution.py:494
  17.7 1.2 %collective-permute-start = (bf16[16,128]{1,0:T(8,128)(2,1)S(1)}, bf16[16,128]{1,0:T(8,128)(2,1)S(1)}, u32[]{:S(2)}, u32[]{:S(2)}) collective-permute-start(bf16[16,128]{1,0:T(8,128)(2,1)S(1)} %get-tuple-element.39), channel_id=1, source_target_pairs={{0,1},{1,0},{2,3},{3,2},{4,5},{5,4},{6,7},{7,6},{8,9},{9,8},{10,11... | collective-permute-start | bytes 12296 | tf_op jit(solution)/shard_map/ppermute | solution.py:533
  32.0 10.6 %all-to-all-start.2 = ((bf16[32,7,2,128]{3,2,1,0:T(2,128)(2,1)}), bf16[32,7,2,128]{3,2,1,0:T(2,128)(2,1)S(1)}, u32[]{:S(2)}, u32[]{:S(2)}) async-start(bf16[32,7,2,128]{3,2,1,0:T(2,128)(2,1)} %bitcast.4), calls=%async_computation.2 | async-start | bytes 229376 | tf_op jit(solution)/shard_map/all_to_all | solution.py:500
  34.7 5.4 %collective-permute-start.3 = (bf16[48,256]{1,0:T(8,128)(2,1)S(1)}, bf16[48,256]{1,0:T(8,128)(2,1)S(1)}, u32[]{:S(2)}, u32[]{:S(2)}) collective-permute-start(bf16[48,256]{1,0:T(8,128)(2,1)S(1)} %get-tuple-element.54), channel_id=1, source_target_pairs={{2,4},{6,8},{10,12},{14,16},{18,20},{22,24},{26,28},{4,2},{8,6},{1... | collective-permute-start | bytes 73736 | tf_op jit(solution)/shard_map/ppermute | solution.py:494
  35.3 6.5 %collective-permute-start.4 = (bf16[48,256]{1,0:T(8,128)(2,1)S(1)}, bf16[48,256]{1,0:T(8,128)(2,1)S(1)}, u32[]{:S(2)}, u32[]{:S(2)}) collective-permute-start(bf16[48,256]{1,0:T(8,128)(2,1)S(1)} %get-tuple-element.55), channel_id=1, source_target_pairs={{0,2},{4,6},{8,10},{12,14},{16,18},{20,22},{24,26},{28,30},{2,0},{... | collective-permute-start | bytes 73736 | tf_op jit(solution)/shard_map/ppermute | solution.py:494
